TPU v7x, 512 devices: a whole 4x4x16 slice. The times are simulated.
512 devices in a mesh: seq: 128 (over y, z, core), head: 4 (over x).
Axes of the slice: x: 4, y: 4, z: 16, core: 2. Of those that a mesh axis runs over, the one named last changes fastest.
Arguments:
- values: bfloat16 [32768, 4096], P('seq', 'head'), may hold values from -6 to 6
- keys: bfloat16 [32768, 4096], P('seq', 'head'), may hold values from -0.59765625 to 0.59765625
- queries: bfloat16 [32768, 4096], P('seq', 'head'), may hold values from -6 to 6
- gates: bfloat16 [32768, 4096], P('seq', 'head'), may hold values from -6 to 6
- log_decay: float32 [32, 32768], P('head', 'seq'), may hold values from -1 to 0, as said below
- level_mix: float32 [8, 32, 32768], P(None, 'head', 'seq'), may hold values from 0.25 to 2
- norm_gain: bfloat16 [4096], P('head'), may hold values from 0.25 to 1.75
- out_weight_t: bfloat16 [4096, 4096], P('seq', 'head'), may hold values from -0.09375 to 0.09375
Outputs:
- mixed: bfloat16 [32768, 4096], P('seq', 'head')
Inputs may be any that keep to these rules, and one draw needn't show every extreme that they name: `log_decay`: log decays are never positive; rates differ strongly between heads.
All inputs are finite; a program needn't handle non-finite values.
Results may differ from a plain program's by a relative error of at most 0.015.
Values may be sent and summed in bfloat16 or wider, within the bound.
No kernel may reach another device: no remote copies, remote signals or barrier semaphores. Data moves between devices by JAX's collectives and lax.ppermute only.
A program may use at most 64 MiB of HBM per device.

v0:
```python
import jax
import jax.numpy as jnp
from jax import lax
from jax.sharding import PartitionSpec as P


def swapped(value, axis, bit):
    mask = 2**bit
    pairs = [(source, source ^ mask) for source in range(lax.axis_size(axis))]
    return lax.ppermute(value, axis, pairs)


def shards(values, keys, queries, gates, log_decay, level_mix, norm_gain, out_weight_t):
    rows = values.shape[0]
    heads = log_decay.shape[0]
    width = values.shape[1] // heads
    state = keys.shape[1] // heads
    xv = values.reshape(rows, heads, width)
    kb = keys.reshape(rows, heads, state)
    qc = queries.reshape(rows, heads, state)
    local = jnp.cumsum(log_decay, axis=1)
    total = local[:, -1]
    scores = jnp.einsum("lhn,mhn->hlm", qc, kb, preferred_element_type=jnp.float32)
    lower = jnp.arange(rows)[:, None] >= jnp.arange(rows)[None, :]
    gap = jnp.where(lower[None], local[:, :, None] - local[:, None, :], -jnp.inf)
    weights = (scores * jnp.exp(gap)).astype(jnp.bfloat16)
    own = jnp.einsum("hlm,mhp->lhp", weights, xv, preferred_element_type=jnp.float32)
    mixture = own * level_mix[0].T[:, :, None]
    scaled = (kb.astype(jnp.float32) * jnp.exp(total[:, None] - local).T[:, :, None]).astype(
        jnp.bfloat16
    )
    aggregate = jnp.einsum("lhn,lhp->hnp", scaled, xv, preferred_element_type=jnp.float32)
    running = total
    before = jnp.zeros_like(total)
    start_scale = jnp.exp(local).T
    nbits = lax.axis_size("seq").bit_length() - 1
    myself = lax.axis_index("seq")
    for level_bit in range(nbits):
        partner, partner_total = swapped((aggregate, running), "seq", level_bit)
        upper = myself >> level_bit & 1 == 1
        bucket = jnp.where(upper, partner * jnp.exp(before)[:, None, None], 0.0).astype(
            jnp.bfloat16
        )
        read = jnp.einsum("lhn,hnp->lhp", qc, bucket, preferred_element_type=jnp.float32)
        mixture = mixture + read * (start_scale * level_mix[level_bit + 1].T)[:, :, None]
        aggregate = jnp.where(
            upper,
            partner * jnp.exp(running)[:, None, None] + aggregate,
            aggregate * jnp.exp(partner_total)[:, None, None] + partner,
        )
        before = jnp.where(upper, before + partner_total, before)
        running = running + partner_total
    gated = mixture * jax.nn.silu(gates.reshape(rows, heads, width).astype(jnp.float32))
    rms = jnp.sqrt(jnp.mean(gated * gated, axis=2, keepdims=True) + 1e-05)
    gain = norm_gain.reshape(heads, width).astype(jnp.float32)
    normed = (gated / rms * gain[None]).astype(jnp.bfloat16).reshape(rows, heads * width)
    terms = lax.dot_general(
        normed,
        lax.all_gather(out_weight_t, "seq", axis=0, tiled=True),
        (((1,), (1,)), ((), ())),
        preferred_element_type=jnp.float32,
    )
    summed = lax.psum(terms.astype(jnp.bfloat16), "head").astype(jnp.float32)
    share = summed.shape[1] // lax.axis_size("head")
    mine = lax.dynamic_slice_in_dim(summed, lax.axis_index("head") * share, share, 1)
    return mine.astype(jnp.bfloat16)


def solution(mesh):
    return jax.shard_map(
        shards,
        mesh=mesh,
        in_specs=(
            P("seq", "head"),
            P("seq", "head"),
            P("seq", "head"),
            P("seq", "head"),
            P("head", "seq"),
            P(None, "head", "seq"),
            P("head"),
            P("seq", "head"),
        ),
        out_specs=P("seq", "head"),
        check_vma=False,
    )
```

profile of v0, /device:TPU:1, one launch (start us, length us, event | category | flops | bytes accessed | tf_op | source)
XLA Modules:
  0.0 338.7 jit_solution(12284078144844199591)
XLA Ops:
  9.7 8.8 %collective-permute-start.1 = (f32[8]{0:T(128)S(1)}, f32[8]{0:T(128)S(1)}, u32[]{:S(2)}, u32[]{:S(2)}) collective-permute-start(f32[8]{0:T(128)S(1)} %slice_reduce_fusion.1), channel_id=1, source_target_pairs={{0,4},{4,0},{8,12},{12,8},{16,20},{20,16},{24,28},{28,24},{32,36},... | collective-permute-start | bytes 104 | tf_op jit(solution)/shard_map/ppermute | solution.py:10
  22.0 1.9 collective-permute-start
  23.9 1.9 collective-permute-start.3
  25.9 2.4 collective-permute-done.3
  30.1 3.3 collective-permute-done.5
  33.4 4.3 %collective-permute-start.7 = (f32[8]{0:T(128)S(1)}, f32[8]{0:T(128)S(1)}, u32[]{:S(2)}, u32[]{:S(2)}) collective-permute-start(f32[8]{0:T(128)S(1)} %get-tuple-element.15), channel_id=1, source_target_pairs={{0,32},{4,36},{8,40},{12,44},{16,48},{20,52},{24,56},{28,60},{32,0... | collective-permute-start | bytes 104 | tf_op jit(solution)/shard_map/ppermute | solution.py:10
  37.7 3.9 %collective-permute-done.7 = f32[8]{0:T(128)S(1)} collective-permute-done((f32[8]{0:T(128)S(1)}, f32[8]{0:T(128)S(1)}, u32[]{:S(2)}, u32[]{:S(2)}) %collective-permute-start.7) | collective-permute-done | bytes 64 | tf_op jit(solution)/shard_map/ppermute | solution.py:10
  41.6 10.1 %collective-permute-start.9 = (f32[8]{0:T(128)S(1)}, f32[8]{0:T(128)S(1)}, u32[]{:S(2)}, u32[]{:S(2)}) collective-permute-start(f32[8]{0:T(128)S(1)} %get-tuple-element.13), channel_id=1, source_target_pairs={{0,64},{4,68},{8,72},{12,76},{16,80},{20,84},{24,88},{28,92},{32,9... | collective-permute-start | bytes 104 | tf_op jit(solution)/shard_map/ppermute | solution.py:10
  51.7 2.9 collective-permute-done.9
  56.5 2.8 collective-permute-done.11
  61.4 9.1 %collective-permute-done.2 = f32[8,128,128]{2,1,0:T(8,128)S(1)} collective-permute-done((f32[8,128,128]{2,1,0:T(8,128)S(1)}, f32[8,128,128]{2,1,0:T(8,128)S(1)}, u32[]{:S(2)}, u32[]{:S(2)}) %collective-permute-start.2) | collective-permute-done | bytes 524320 | tf_op jit(solution)/shard_map/ppermute | solution.py:10
  73.4 3.0 fusion.2
  76.4 22.0 %collective-permute-done.4 = f32[8,128,128]{2,1,0:T(8,128)S(1)} collective-permute-done((f32[8,128,128]{2,1,0:T(8,128)S(1)}, f32[8,128,128]{2,1,0:T(8,128)S(1)}, u32[]{:S(2)}, u32[]{:S(2)}) %collective-permute-start.4) | collective-permute-done | bytes 524320 | tf_op jit(solution)/shard_map/ppermute | solution.py:10
  98.6 3.4 %collective-permute-start.6 = (f32[8,128,128]{2,1,0:T(8,128)S(1)}, f32[8,128,128]{2,1,0:T(8,128)S(1)}, u32[]{:S(2)}, u32[]{:S(2)}) collective-permute-start(f32[8,128,128]{2,1,0:T(8,128)S(1)} %add_select_fusion.3), channel_id=1, source_target_pairs={{0,32},{4,36},{8,40},{12,44},{16,48},{20,52},{24,56},{28,60},{32,0... | collective-permute-start | bytes 1572872 | tf_op jit(solution)/shard_map/ppermute | solution.py:10
  102.0 2.3 copy.44
  104.3 66.3 %collective-permute-done.6 = f32[8,128,128]{2,1,0:T(8,128)S(1)} collective-permute-done((f32[8,128,128]{2,1,0:T(8,128)S(1)}, f32[8,128,128]{2,1,0:T(8,128)S(1)}, u32[]{:S(2)}, u32[]{:S(2)}) %collective-permute-start.6) | collective-permute-done | bytes 524320 | tf_op jit(solution)/shard_map/ppermute | solution.py:10
  170.8 11.4 %collective-permute-start.8 = (f32[8,128,128]{2,1,0:T(8,128)S(1)}, f32[8,128,128]{2,1,0:T(8,128)S(1)}, u32[]{:S(2)}, u32[]{:S(2)}) collective-permute-start(f32[8,128,128]{2,1,0:T(8,128)S(1)} %add_select_fusion.2), channel_id=1, source_target_pairs={{0,64},{4,68},{8,72},{12,76},{16,80},{20,84},{24,88},{28,92},{32,9... | collective-permute-start | bytes 1572872 | tf_op jit(solution)/shard_map/ppermute | solution.py:10
  183.0 37.7 %collective-permute-done.8 = f32[8,128,128]{2,1,0:T(8,128)S(1)} collective-permute-done((f32[8,128,128]{2,1,0:T(8,128)S(1)}, f32[8,128,128]{2,1,0:T(8,128)S(1)}, u32[]{:S(2)}, u32[]{:S(2)}) %collective-permute-start.8) | collective-permute-done | bytes 524320 | tf_op jit(solution)/shard_map/ppermute | solution.py:10
  220.9 3.4 collective-permute-start.10
  225.2 10.6 %collective-permute-done.10 = f32[8,128,128]{2,1,0:T(8,128)S(1)} collective-permute-done((f32[8,128,128]{2,1,0:T(8,128)S(1)}, f32[8,128,128]{2,1,0:T(8,128)S(1)}, u32[]{:S(2)}, u32[]{:S(2)}) %collective-permute-start.10) | collective-permute-done | bytes 524320 | tf_op jit(solution)/shard_map/ppermute | solution.py:10
  236.0 3.7 %collective-permute-start.12 = (f32[8,128,128]{2,1,0:T(8,128)S(1)}, f32[8,128,128]{2,1,0:T(8,128)S(1)}, u32[]{:S(2)}, u32[]{:S(2)}) collective-permute-start(f32[8,128,128]{2,1,0:T(8,128)S(1)} %add_select_fusion), channel_id=1, source_target_pairs={{0,256},{4,260},{8,264},{12,268},{16,272},{20,276},{24,280},{28,28... | collective-permute-start | bytes 1572872 | tf_op jit(solution)/shard_map/ppermute | solution.py:10
  240.7 10.8 %collective-permute-done.12 = f32[8,128,128]{2,1,0:T(8,128)S(1)} collective-permute-done((f32[8,128,128]{2,1,0:T(8,128)S(1)}, f32[8,128,128]{2,1,0:T(8,128)S(1)}, u32[]{:S(2)}, u32[]{:S(2)}) %collective-permute-start.12) | collective-permute-done | bytes 524320 | tf_op jit(solution)/shard_map/ppermute | solution.py:10
  252.4 7.3 %convolution_convert_fusion = bf16[256,4096]{1,0:T(8,128)(2,1)} fusion(bf16[256,1024]{0,1:T(8,128)(2,1)S(1)} %bitcast.170, bf16[4096,1024]{1,0:T(8,128)(2,1)} %all-gather.2.cloned.1.call-done), kind=kOutput, calls=%fused_computation | convolution fusion | flops 2148532224 | bytes 11010048 | tf_op jit(solution)/shard_map/dot_general | solution.py:57
  259.7 70.3 %all-reduce.2.cloned.1.call-done = bf16[256,4096]{1,0:T(8,128)(2,1)} async-done(((bf16[256,4096]{1,0:T(8,128)(2,1)}), bf16[256,4096]{1,0:T(8,128)(2,1)}) %all-reduce.2.cloned.1.call-update) | async-done | bytes 2097168 | tf_op jit(solution)/shard_map/psum | solution.py:63
  (59 shorter events, 21.4 us)
Async XLA Ops:
  6.5 66.8 %copy-start = (bf16[256,1024]{1,0:T(8,128)(2,1)S(1)}, bf16[256,1024]{1,0:T(8,128)(2,1)}, u32[]{:S(2)}) copy-start(bf16[256,1024]{1,0:T(8,128)(2,1)} %param.10) | copy-start | bytes 1572868
  6.5 245.9 %all-gather.2.cloned.1.call-start = ((), (), s32[]{:S(2)}) async-start(), calls=%async_computation | async-start | bytes 8454144 | tf_op jit(solution)/shard_map/all_gather | solution.py:59
  7.3 322.7 %all-reduce.2.cloned.1.call-start = ((), (), s32[]{:S(2)}) async-start(), calls=%async_computation.1 | async-start | bytes 4194304 | tf_op jit(solution)/shard_map/psum | solution.py:63
  9.7 14.2 %collective-permute-start.1 = (f32[8]{0:T(128)S(1)}, f32[8]{0:T(128)S(1)}, u32[]{:S(2)}, u32[]{:S(2)}) collective-permute-start(f32[8]{0:T(128)S(1)} %slice_reduce_fusion.1), channel_id=1, source_target_pairs={{0,4},{4,0},{8,12},{12,8},{16,20},{20,16},{24,28},{28,24},{32,36},... | collective-permute-start | bytes 104 | tf_op jit(solution)/shard_map/ppermute | solution.py:10
  22.0 37.3 %collective-permute-start = (f32[8,128,128]{2,1,0:T(8,128)S(1)}, f32[8,128,128]{2,1,0:T(8,128)S(1)}, u32[]{:S(2)}, u32[]{:S(2)}) collective-permute-start(f32[8,128,128]{2,1,0:T(8,128)S(1)} %fusion.22), channel_id=1, source_target_pairs={{0,4},{4,0},{8,12},{12,8},{16,20},{20,16},{24,28},{28,24},{32,36},... | collective-permute-start | bytes 1572872 | tf_op jit(solution)/shard_map/ppermute | solution.py:10
  23.9 4.3 %collective-permute-start.3 = (f32[8]{0:T(128)S(1)}, f32[8]{0:T(128)S(1)}, u32[]{:S(2)}, u32[]{:S(2)}) collective-permute-start(f32[8]{0:T(128)S(1)} %get-tuple-element.19), channel_id=1, source_target_pairs={{0,8},{4,12},{8,0},{12,4},{16,24},{20,28},{24,16},{28,20},{32,40},... | collective-permute-start | bytes 104 | tf_op jit(solution)/shard_map/ppermute | solution.py:10
  28.2 5.2 %collective-permute-start.5 = (f32[8]{0:T(128)S(1)}, f32[8]{0:T(128)S(1)}, u32[]{:S(2)}, u32[]{:S(2)}) collective-permute-start(f32[8]{0:T(128)S(1)} %get-tuple-element.17), channel_id=1, source_target_pairs={{0,16},{4,20},{8,24},{12,28},{16,0},{20,4},{24,8},{28,12},{32,48},... | collective-permute-start | bytes 104 | tf_op jit(solution)/shard_map/ppermute | solution.py:10
  33.4 8.2 %collective-permute-start.7 = (f32[8]{0:T(128)S(1)}, f32[8]{0:T(128)S(1)}, u32[]{:S(2)}, u32[]{:S(2)}) collective-permute-start(f32[8]{0:T(128)S(1)} %get-tuple-element.15), channel_id=1, source_target_pairs={{0,32},{4,36},{8,40},{12,44},{16,48},{20,52},{24,56},{28,60},{32,0... | collective-permute-start | bytes 104 | tf_op jit(solution)/shard_map/ppermute | solution.py:10
  41.6 13.0 %collective-permute-start.9 = (f32[8]{0:T(128)S(1)}, f32[8]{0:T(128)S(1)}, u32[]{:S(2)}, u32[]{:S(2)}) collective-permute-start(f32[8]{0:T(128)S(1)} %get-tuple-element.13), channel_id=1, source_target_pairs={{0,64},{4,68},{8,72},{12,76},{16,80},{20,84},{24,88},{28,92},{32,9... | collective-permute-start | bytes 104 | tf_op jit(solution)/shard_map/ppermute | solution.py:10
  54.6 4.7 %collective-permute-start.11 = (f32[8]{0:T(128)S(1)}, f32[8]{0:T(128)S(1)}, u32[]{:S(2)}, u32[]{:S(2)}) collective-permute-start(f32[8]{0:T(128)S(1)} %get-tuple-element.9), channel_id=1, source_target_pairs={{0,128},{4,132},{8,136},{12,140},{16,144},{20,148},{24,152},{28,15... | collective-permute-start | bytes 104 | tf_op jit(solution)/shard_map/ppermute | solution.py:10
  59.5 11.0 %collective-permute-start.2 = (f32[8,128,128]{2,1,0:T(8,128)S(1)}, f32[8,128,128]{2,1,0:T(8,128)S(1)}, u32[]{:S(2)}, u32[]{:S(2)}) collective-permute-start(f32[8,128,128]{2,1,0:T(8,128)S(1)} %add_select_fusion.5), channel_id=1, source_target_pairs={{0,8},{4,12},{8,0},{12,4},{16,24},{20,28},{24,16},{28,20},{32,40},... | collective-permute-start | bytes 1572872 | tf_op jit(solution)/shard_map/ppermute | solution.py:10
  70.5 5.9 %copy-start.1 = (f32[8,128,128]{2,1,0:T(8,128)}, f32[8,128,128]{2,1,0:T(8,128)S(1)}, u32[]{:S(2)}) copy-start(f32[8,128,128]{2,1,0:T(8,128)S(1)} %collective-permute-done.2) | copy-start | bytes 1572868
  70.7 27.7 %collective-permute-start.4 = (f32[8,128,128]{2,1,0:T(8,128)S(1)}, f32[8,128,128]{2,1,0:T(8,128)S(1)}, u32[]{:S(2)}, u32[]{:S(2)}) collective-permute-start(f32[8,128,128]{2,1,0:T(8,128)S(1)} %add_select_fusion.4), channel_id=1, source_target_pairs={{0,16},{4,20},{8,24},{12,28},{16,0},{20,4},{24,8},{28,12},{32,48},... | collective-permute-start | bytes 1572872 | tf_op jit(solution)/shard_map/ppermute | solution.py:10
  73.4 28.6 %copy-start.5 = (bf16[1024]{0:T(1024)(128)(2,1)S(1)}, bf16[1024]{0:T(1024)(128)(2,1)}, u32[]{:S(2)}) copy-start(bf16[1024]{0:T(1024)(128)(2,1)} %param.14) | copy-start | bytes 6148
  98.6 72.1 %collective-permute-start.6 = (f32[8,128,128]{2,1,0:T(8,128)S(1)}, f32[8,128,128]{2,1,0:T(8,128)S(1)}, u32[]{:S(2)}, u32[]{:S(2)}) collective-permute-start(f32[8,128,128]{2,1,0:T(8,128)S(1)} %add_select_fusion.3), channel_id=1, source_target_pairs={{0,32},{4,36},{8,40},{12,44},{16,48},{20,52},{24,56},{28,60},{32,0... | collective-permute-start | bytes 1572872 | tf_op jit(solution)/shard_map/ppermute | solution.py:10
  104.3 77.9 %copy-start.4 = (f32[256,8,128]{0,2,1:T(8,128)S(1)}, f32[256,8,128]{0,2,1:T(8,128)}, u32[]{:S(2)}) copy-start(f32[256,8,128]{0,2,1:T(8,128)} %fusion.2) | copy-start | bytes 3145732
  170.6 11.9 %copy-start.2 = (f32[8,128,128]{2,1,0:T(8,128)S(1)}, f32[8,128,128]{2,1,0:T(8,128)}, u32[]{:S(2)}) copy-start(f32[8,128,128]{2,1,0:T(8,128)} %copy-done.1) | copy-start | bytes 1572868
  170.8 50.0 %collective-permute-start.8 = (f32[8,128,128]{2,1,0:T(8,128)S(1)}, f32[8,128,128]{2,1,0:T(8,128)S(1)}, u32[]{:S(2)}, u32[]{:S(2)}) collective-permute-start(f32[8,128,128]{2,1,0:T(8,128)S(1)} %add_select_fusion.2), channel_id=1, source_target_pairs={{0,64},{4,68},{8,72},{12,76},{16,80},{20,84},{24,88},{28,92},{32,9... | collective-permute-start | bytes 1572872 | tf_op jit(solution)/shard_map/ppermute | solution.py:10
  220.9 14.9 %collective-permute-start.10 = (f32[8,128,128]{2,1,0:T(8,128)S(1)}, f32[8,128,128]{2,1,0:T(8,128)S(1)}, u32[]{:S(2)}, u32[]{:S(2)}) collective-permute-start(f32[8,128,128]{2,1,0:T(8,128)S(1)} %add_select_fusion.1), channel_id=1, source_target_pairs={{0,128},{4,132},{8,136},{12,140},{16,144},{20,148},{24,152},{28,15... | collective-permute-start | bytes 1572872 | tf_op jit(solution)/shard_map/ppermute | solution.py:10
  236.0 15.5 %collective-permute-start.12 = (f32[8,128,128]{2,1,0:T(8,128)S(1)}, f32[8,128,128]{2,1,0:T(8,128)S(1)}, u32[]{:S(2)}, u32[]{:S(2)}) collective-permute-start(f32[8,128,128]{2,1,0:T(8,128)S(1)} %add_select_fusion), channel_id=1, source_target_pairs={{0,256},{4,260},{8,264},{12,268},{16,272},{20,276},{24,280},{28,28... | collective-permute-start | bytes 1572872 | tf_op jit(solution)/shard_map/ppermute | solution.py:10
  240.2 11.3 %copy-start.3 = (f32[256,1024]{0,1:T(8,128)S(1)}, f32[256,1024]{0,1:T(8,128)}, u32[]{:S(2)}) copy-start(f32[256,1024]{0,1:T(8,128)} %copy.44) | copy-start | bytes 3145732
Sparse Core Ops, SparseCore 0:
  10.5 210.7 all-gather.1
  259.8 70.0 all-reduce.1
where the time goes:
time: 340 us; the launch traced here: 339 us
  waiting for transfers between devices  243 us (71%)
  starting transfers between devices  56.6 us (17%)
  matrix products  14.9 us (4%)
  between operations  13.8 us (4%)
  other arithmetic  6.08 us (2%)
  local copies, waits for them, and re-layouts  4.61 us (1%)
    ppermute x13, waiting for transfers between devices, swapped(): return lax.ppermute(value, axis, pairs)  172 us
    psum x1, waiting for transfers between devices, shards(): summed = lax.psum(terms.astype(jnp.bfloat16), 'head').astype(jnp.float32)  70.3 us
    ppermute x13, starting transfers between devices, swapped(): return lax.ppermute(value, axis, pairs)  56.5 us
    dot_general x1, matrix products, shards(): lax.dot_general(normed, lax.all_gather(out_weight_t, 'seq', axis=0, tiled...  7.26 us
  transfers between devices with their start and end apart: 15, of which 12 were waited for; matrix products, arithmetic and copies ran while one was open for 5% of the time, Pallas kernels for 0%

commit v1 on v0

v1 whole, which is shorter than its diff:
```python
import jax
import jax.numpy as jnp
from jax import lax
from jax.sharding import Mesh, PartitionSpec as P

BF = jnp.bfloat16
F32 = jnp.float32
SEQ = ("y", "a", "b", "c")


def swap(value):
    return lax.ppermute(value, "c", [(0, 1), (1, 0)])


def flip(value, axis, mask):
    return lax.ppermute(value, axis, [(i, i ^ mask) for i in range(4)])


def halves(value, axis, core):
    size = value.shape[axis] // 2
    kept = lax.dynamic_slice_in_dim(value, core * size, size, axis)
    sent = lax.dynamic_slice_in_dim(value, (1 - core) * size, size, axis)
    return kept, sent


def in_order(kept, got, core):
    first = core == 0
    return jnp.stack([jnp.where(first, kept, got), jnp.where(first, got, kept)])


def tail(log):
    high = lax.reduce_precision(log, 8, 7)
    middle = lax.reduce_precision(log - high, 8, 7)
    terms = jnp.stack([high, middle, log - high - middle], axis=-1)
    rows = jnp.pad(terms, [(0, 0)] * log.ndim + [(0, 13)])
    return jnp.broadcast_to(rows[..., None], rows.shape + (128,)).astype(BF)


def untail(rows):
    return jnp.sum(rows[..., :3, 0].astype(F32), axis=-1)


def with_tail(state, log):
    return jnp.concatenate([state.astype(BF), tail(log)], axis=-2)


def split_tail(block):
    return block[..., :128, :], untail(block[..., 128:, :])


def exchange(block, axis):
    return lax.all_to_all(
        jnp.broadcast_to(block[None], (4,) + block.shape), axis, 0, 0, tiled=True
    )


def merge(state, log):
    state = state.astype(F32)
    e = jnp.exp
    pair = state[0] * e(log[1]) + state[1]
    whole = pair * e(log[2] + log[3]) + state[2] * e(log[3]) + state[3]
    return pair, whole


def shards(values, keys, queries, gates, log_decay, level_mix, norm_gain, weight):
    y, a, b, c, x = (lax.axis_index(n) for n in ("y", "a", "b", "c", "x"))
    kept, sent = halves(weight, 1, c)
    both = in_order(kept, swap(sent), c).reshape(64, 512)
    spread = []
    for k in range(4):
        perm = [(s * 4 + f, ((f + k) % 4) * 4 + s) for s in range(4) for f in range(4)]
        spread.append(lax.ppermute(both, ("y", "x"), perm))
    ring = jnp.concatenate(spread + spread[:3], axis=1)
    mine = lax.dynamic_slice_in_dim(ring, ((y - x) % 4) * 512, 2048, 1)
    gathered = lax.all_gather(mine, ("a", "b"), axis=0, tiled=True)

    small = jnp.concatenate([log_decay[None], level_mix])
    kept, sent = halves(small, 1, c)
    small = in_order(kept, swap(sent), c)
    kv = jnp.stack([keys, values])
    kept, sent = halves(kv, 2, c)
    kv = in_order(kept, swap(sent), c)
    qg = jnp.stack([queries, gates])
    kept, sent = halves(qg, 2, c)
    qg = in_order(kept, swap(sent), c)
    kb = kv[:, 0].reshape(2, 256, 4, 128)
    xv = kv[:, 1].reshape(2, 256, 4, 128)
    qc = qg[:, 0].reshape(2, 256, 4, 128)
    z = qg[:, 1].reshape(2, 256, 4, 128)
    gain = lax.dynamic_slice_in_dim(norm_gain, c * 512, 512, 0).reshape(4, 128)
    decay = small[:, 0]
    mix = small[:, 1:]

    local = jnp.cumsum(decay, axis=2)
    total = local[:, :, -1]
    scaled = (
        kb.astype(F32) * jnp.exp(total[:, :, None] - local).transpose(0, 2, 1)[..., None]
    ).astype(BF)
    ends = jnp.einsum("slhn,slhp->shnp", scaled, xv, preferred_element_type=F32)
    chip = ends[0] * jnp.exp(total[1])[:, None, None] + ends[1]
    chip_log = total[0] + total[1]

    got = lax.all_to_all(with_tail(chip, chip_log), "b", 0, 0, tiled=True)
    near, near_log = split_tail(got)
    pair, group = merge(near, near_log)
    group_log = jnp.sum(near_log)

    def near_message(target):
        odd = target % 2 == 1
        upper = target >= 2
        e0 = jnp.where(upper, near[2], near[0])
        l2 = jnp.where(odd, e0, jnp.zeros_like(e0))
        step = jnp.where(odd, jnp.where(upper, near_log[2], near_log[0]), 0.0)
        l3 = jnp.where(upper, pair * jnp.exp(step), 0.0).astype(BF)
        before = jnp.sum(jnp.where(jnp.arange(4) < target, near_log, 0.0))
        return jnp.concatenate([l2, l3, tail(before)], axis=0)

    near_got = [near_message(b)] + [flip(near_message(b ^ k), "b", k) for k in (1, 2, 3)]

    def by_head(blocks):
        stacked = jnp.stack(blocks)
        return jnp.stack([lax.dynamic_index_in_dim(stacked, b ^ h, 0, False) for h in range(4)])

    got = exchange(with_tail(group, group_log[None][0]), "a")
    far, far_log = split_tail(got)
    far_pair, row = merge(far, far_log)
    row_log = jnp.sum(far_log)
    odd, upper = a % 2 == 1, a >= 2
    l4 = jnp.where(odd, jnp.where(upper, far[2], far[0]), jnp.zeros_like(far[0]))
    step = jnp.where(odd, jnp.where(upper, far_log[2], far_log[0]), 0.0)
    l5 = jnp.where(upper, far_pair * jnp.exp(step), 0.0).astype(BF)
    far_before = jnp.sum(jnp.where(jnp.arange(4) < a, far_log, 0.0))
    far_message = jnp.concatenate([l4, l5], axis=0)
    far_got = [far_message] + [flip(far_message, "b", k) for k in (1, 2, 3)]

    got = exchange(with_tail(row, row_log), "y")
    rows, rows_log = split_tail(got)
    rows_pair = rows[0].astype(F32) * jnp.exp(rows_log[1]) + rows[1].astype(F32)
    odd, upper = y % 2 == 1, y >= 2
    l6 = jnp.where(odd, jnp.where(upper, rows[2], rows[0]).astype(F32) * jnp.exp(far_before), 0.0)
    step = jnp.where(odd, jnp.where(upper, rows_log[2], rows_log[0]), 0.0)
    l7 = jnp.where(upper, rows_pair * jnp.exp(step + far_before), 0.0)
    last_message = jnp.concatenate([l6.astype(BF), l7.astype(BF)], axis=0)
    last_got = exchange(last_message, "b")

    lower = jnp.arange(256)[:, None] >= jnp.arange(256)[None, :]
    scores = jnp.einsum("slhn,smhn->shlm", qc, kb, preferred_element_type=F32)
    gap = jnp.where(lower, local[..., :, None] - local[..., None, :], -jnp.inf)
    weights = (scores * jnp.exp(gap)).astype(BF)
    own = jnp.einsum("shlm,smhp->shlp", weights, xv, preferred_element_type=F32)
    mixture = own * mix[:, 0][..., None]
    start = jnp.exp(local)
    read1 = jnp.einsum("lhn,hnp->hlp", qc[1], ends[0].astype(BF), preferred_element_type=F32)
    read1 = read1 * (start[1] * mix[1, 1])[..., None]
    mixture = mixture + jnp.stack([jnp.zeros_like(read1), read1])
    chip_start = jnp.stack([start[0], jnp.exp(local[1] + total[0][:, None])])

    near_all = by_head(near_got)
    far_all = by_head(far_got)
    b_start = chip_start * jnp.exp(untail(near_all[:, 256:]))[None, :, None]
    for level, block, scale in (
        (2, near_all[:, :128], chip_start),
        (3, near_all[:, 128:256], chip_start),
        (4, far_all[:, :128], b_start),
        (5, far_all[:, 128:], b_start),
        (6, last_got[:, :128], b_start),
        (7, last_got[:, 128:], b_start),
    ):
        read = jnp.einsum("slhn,hnp->shlp", qc, block, preferred_element_type=F32)
        mixture = mixture + read * (scale * mix[:, level])[..., None]

    gated = mixture * jax.nn.silu(z.transpose(0, 2, 1, 3).astype(F32))
    rms = jnp.sqrt(jnp.mean(gated * gated, axis=3, keepdims=True) + 1e-05)
    normed = (gated / rms * gain[None, :, None].astype(F32)).astype(BF)
    normed = normed.transpose(0, 2, 1, 3).reshape(512, 512)

    blocks = [normed] + [
        lax.ppermute(normed, "x", [(i, (i + j) % 4) for i in range(4)]) for j in (1, 2, 3)
    ]
    out = 0.0
    for j in range(4):
        out = out + lax.dot_general(
            blocks[j],
            gathered[:, j * 512 : (j + 1) * 512],
            (((1,), (1,)), ((), ())),
            preferred_element_type=F32,
        )
    kept, sent = halves(out, 0, c)
    return (kept + swap(sent.astype(BF)).astype(F32)).astype(BF)


def solution(mesh):
    fine = Mesh(mesh.devices.reshape(4, 4, 4, 2, 4), SEQ + ("x",))
    return jax.shard_map(
        shards,
        mesh=fine,
        in_specs=(
            P(SEQ, "x"),
            P(SEQ, "x"),
            P(SEQ, "x"),
            P(SEQ, "x"),
            P("x", SEQ),
            P(None, "x", SEQ),
            P("x"),
            P(SEQ, "x"),
        ),
        out_specs=P(SEQ, "x"),
        check_vma=False,
    )
```

time: 340 us -> 224 us (0.66)
  waiting for transfers between devices: 243 us -> 36.3 us
  between operations: 13.8 us -> 58.7 us
  starting transfers between devices: 56.6 us -> 88.1 us
  other arithmetic: 6.08 us -> 17.4 us
  local copies, waits for them, and re-layouts: 4.61 us -> 10.4 us
  matrix products: 14.9 us -> 11.1 us
    ppermute x13 -> x18, waiting for transfers between devices: 172 us -> 25.7 us  [the longest x3 13.2 us: shards(): lax.ppermute(normed, 'x', [(i, (i + j) % 4) for i in range(4)])]
    psum x1 -> x0, waiting for transfers between devices: 70.3 us -> none  [shards(): summed = lax.psum(terms.astype(jnp.bfloat16), 'head').astype(jnp.float32)]
    all_to_all x0 -> x4, starting transfers between devices: none -> 28.9 us  [the longest x3 23.3 us: exchange(): lax.all_to_all(jnp.broadcast_to(block[None], (4,) + block.shape), axis, 0...]
    all_to_all x0 -> x4, waiting for transfers between devices: none -> 10.5 us  [the longest x3 9.64 us: exchange(): lax.all_to_all(jnp.broadcast_to(block[None], (4,) + block.shape), axis, 0...]
    another operation x2 -> x27, other arithmetic: 1.29 us -> 7.69 us  [the longest x8 3.53 us: in_order(): return jnp.stack([jnp.where(first, kept, got), jnp.where(first, got, kept)])]
    dot_general x10 -> x13, matrix products: 14.9 us -> 11.1 us  [the longest x4 5.6 us: shards(): lax.dot_general(blocks[j], gathered[:, j * 512:(j + 1) * 512], (((1,), (1...]
    unnamed x12 -> x54, local copies, waits for them, and re-layouts: 0.02 us -> 3.55 us
    ppermute x13 -> x18, starting transfers between devices: 56.5 us -> 59.2 us  [the longest x5 21.7 us: swap(): return lax.ppermute(value, 'c', [(0, 1), (1, 0)])]
  transfers between devices with their start and end apart: 15 -> 23, of which waited for: 12 -> 10; matrix products, arithmetic and copies ran while one was open for 5% -> 16% of each run, Pallas kernels for 0% -> 0%
where the time goes in v1:
time: 224 us; the launch traced here: 222 us
  starting transfers between devices  88.1 us (39%)
  between operations  58.7 us (26%)
  waiting for transfers between devices  36.3 us (16%)
  other arithmetic  17.4 us (8%)
  matrix products  11.1 us (5%)
  local copies, waits for them, and re-layouts  10.4 us (5%)
    all_to_all x3, starting transfers between devices, exchange(): lax.all_to_all(jnp.broadcast_to(block[None], (4,) + block.shape), axis, 0...  23.3 us
    ppermute x5, starting transfers between devices, swap(): return lax.ppermute(value, 'c', [(0, 1), (1, 0)])  21.7 us
    ppermute x6, starting transfers between devices, flip(): return lax.ppermute(value, axis, [(i, i ^ mask) for i in range(4)])  18.5 us
    ppermute x3, waiting for transfers between devices, shards(): lax.ppermute(normed, 'x', [(i, (i + j) % 4) for i in range(4)])  13.2 us
    ppermute x4, starting transfers between devices, shards(): spread.append(lax.ppermute(both, ('y', 'x'), perm))  10.3 us
    all_to_all x3, waiting for transfers between devices, exchange(): lax.all_to_all(jnp.broadcast_to(block[None], (4,) + block.shape), axis, 0...  9.64 us
    ppermute x6, waiting for transfers between devices, flip(): return lax.ppermute(value, axis, [(i, i ^ mask) for i in range(4)])  9.08 us
    ppermute x3, starting transfers between devices, shards(): lax.ppermute(normed, 'x', [(i, (i + j) % 4) for i in range(4)])  8.62 us
  transfers between devices with their start and end apart: 23, of which 10 were waited for; matrix products, arithmetic and copies ran while one was open for 16% of the time, Pallas kernels for 0%

profile of v1, /device:TPU:1, one launch (start us, length us, event | category | flops | bytes accessed | tf_op | source)
XLA Modules:
  0.0 222.0 jit_solution(288984395341669945)
XLA Ops:
  7.4 8.8 %collective-permute-start.9 = (bf16[32,512]{1,0:T(8,128)(2,1)S(1)}, bf16[32,512]{1,0:T(8,128)(2,1)S(1)}, u32[]{:S(2)}, u32[]{:S(2)}) collective-permute-start(bf16[32,512]{1,0:T(8,128)(2,1)S(1)} %constant_dynamic-slice_fusion.1), channel_id=1, source_target_pairs={{0,4},{4,0},{1,5},{5,1},{2,6},{6,2},{3,7},{7,3},{8,12},{12,8},{9,1... | collective-permute-start | bytes 98312 | tf_op jit(solution)/shard_map/ppermute | solution.py:12
  21.6 2.5 %collective-permute-start = (bf16[2,256,512]{1,2,0:T(8,128)(2,1)S(1)}, bf16[2,256,512]{1,2,0:T(8,128)(2,1)}, u32[]{:S(2)}, u32[]{:S(2)}) collective-permute-start(bf16[2,256,512]{1,2,0:T(8,128)(2,1)S(1)} %fusion.41), channel_id=1, source_target_pairs={{0,4},{4,0},{1,5},{5,1},{2,6},{6,2},{3,7},{7,3},{8,12},{12,8},{9,1... | collective-permute-start | bytes 1572872 | tf_op jit(solution)/shard_map/ppermute | solution.py:12
  30.6 2.9 %collective-permute-start.12 = (bf16[64,512]{1,0:T(8,128)(2,1)S(1)}, bf16[64,512]{1,0:T(8,128)(2,1)S(1)}, u32[]{:S(2)}, u32[]{:S(2)}) collective-permute-start(bf16[64,512]{1,0:T(8,128)(2,1)S(1)} %bitcast.290), channel_id=1, source_target_pairs={{0,256},{1,384},{2,0},{3,128},{128,257},{129,385},{130,1},{131,129... | collective-permute-start | bytes 196616 | tf_op jit(solution)/shard_map/ppermute | solution.py:72
  34.9 2.4 %reduce-window.6 = f32[2,4,2,128]{3,2,1,0:T(2,128)S(1)} reduce-window(f32[2,4,2,128]{3,2,1,0:T(2,128)S(1)} %reshape.386, f32[]{:T(128)} %constant.103.clone.1), window={size=1x1x1x128 pad=0_0x0_0x0_0x127_0}, to_apply=%region_0.1 | reduce-window | flops 260096 | bytes 16388 | tf_op jit(solution)/shard_map/reduce-window
  39.7 4.8 %collective-permute-start.11 = (bf16[64,512]{1,0:T(8,128)(2,1)S(1)}, bf16[64,512]{1,0:T(8,128)(2,1)S(1)}, u32[]{:S(2)}, u32[]{:S(2)}) collective-permute-start(bf16[64,512]{1,0:T(8,128)(2,1)S(1)} %bitcast.292), channel_id=1, source_target_pairs={{0,128},{1,256},{2,384},{3,0},{128,129},{129,257},{130,385},{131,1... | collective-permute-start | bytes 196616 | tf_op jit(solution)/shard_map/ppermute | solution.py:72
  51.2 5.6 %all-to-all-start = ((bf16[4,144,128]{2,1,0:T(8,128)(2,1)}), bf16[4,144,128]{2,1,0:T(8,128)(2,1)S(1)}, u32[]{:S(2)}, u32[]{:S(2)}) async-start(bf16[4,144,128]{2,1,0:T(8,128)(2,1)} %pad_maximum_fusion.6), calls=%async_computation | async-start | bytes 294912 | tf_op jit(solution)/shard_map/all_to_all | solution.py:103
  97.1 12.5 %all-to-all-start.1 = ((bf16[4,144,128]{2,1,0:T(8,128)(2,1)}), bf16[4,144,128]{2,1,0:T(8,128)(2,1)S(1)}, u32[]{:S(2)}, u32[]{:S(2)}) async-start(bf16[4,144,128]{2,1,0:T(8,128)(2,1)} %broadcast_in_dim.61), calls=%async_computation.1 | async-start | bytes 294912 | tf_op jit(solution)/shard_map/all_to_all | solution.py:52
  109.8 3.0 %collective-permute-start.3 = (bf16[272,128]{1,0:T(8,128)(2,1)S(1)}, bf16[272,128]{1,0:T(8,128)(2,1)S(1)}, u32[]{:S(2)}, u32[]{:S(2)}) collective-permute-start(bf16[272,128]{1,0:T(8,128)(2,1)S(1)} %maximum_maximum_fusion), channel_id=1, source_target_pairs={{0,8},{8,0},{16,24},{24,16},{1,9},{9,1},{17,25},{25,17},{2,10},{10... | collective-permute-start | bytes 208904 | tf_op jit(solution)/shard_map/ppermute | solution.py:16
  112.9 3.5 %collective-permute-start.4 = (bf16[272,128]{1,0:T(8,128)(2,1)S(1)}, bf16[272,128]{1,0:T(8,128)(2,1)S(1)}, u32[]{:S(2)}, u32[]{:S(2)}) collective-permute-start(bf16[272,128]{1,0:T(8,128)(2,1)S(1)} %maximum_maximum_fusion.1), channel_id=1, source_target_pairs={{0,16},{8,24},{16,0},{24,8},{1,17},{9,25},{17,1},{25,9},{2,18},{10... | collective-permute-start | bytes 208904 | tf_op jit(solution)/shard_map/ppermute | solution.py:16
  116.5 2.8 %collective-permute-start.5 = (bf16[272,128]{1,0:T(8,128)(2,1)S(1)}, bf16[272,128]{1,0:T(8,128)(2,1)S(1)}, u32[]{:S(2)}, u32[]{:S(2)}) collective-permute-start(bf16[272,128]{1,0:T(8,128)(2,1)S(1)} %maximum_maximum_fusion.2), channel_id=1, source_target_pairs={{0,24},{8,16},{16,8},{24,0},{1,25},{9,17},{17,9},{25,1},{2,26},{10... | collective-permute-start | bytes 208904 | tf_op jit(solution)/shard_map/ppermute | solution.py:16
  121.1 2.1 collective-permute-done.4
  123.2 5.3 %collective-permute-done.5 = bf16[272,128]{1,0:T(8,128)(2,1)S(1)} collective-permute-done((bf16[272,128]{1,0:T(8,128)(2,1)S(1)}, bf16[272,128]{1,0:T(8,128)(2,1)S(1)}, u32[]{:S(2)}, u32[]{:S(2)}) %collective-permute-start.5) | collective-permute-done | bytes 69664 | tf_op jit(solution)/shard_map/ppermute | solution.py:16
  140.1 4.0 %collective-permute-start.7 = (bf16[256,128]{1,0:T(8,128)(2,1)S(1)}, bf16[256,128]{1,0:T(8,128)(2,1)S(1)}, u32[]{:S(2)}, u32[]{:S(2)}) collective-permute-start(bf16[256,128]{1,0:T(8,128)(2,1)S(1)} %get-tuple-element.57), channel_id=1, source_target_pairs={{0,16},{8,24},{16,0},{24,8},{1,17},{9,25},{17,1},{25,9},{2,18},{10... | collective-permute-start | bytes 196616 | tf_op jit(solution)/shard_map/ppermute | solution.py:16
  146.0 3.3 %collective-permute-start.8 = (bf16[256,128]{1,0:T(8,128)(2,1)S(1)}, bf16[256,128]{1,0:T(8,128)(2,1)S(1)}, u32[]{:S(2)}, u32[]{:S(2)}) collective-permute-start(bf16[256,128]{1,0:T(8,128)(2,1)S(1)} %get-tuple-element.57), channel_id=1, source_target_pairs={{0,24},{8,16},{16,8},{24,0},{1,25},{9,17},{17,9},{25,1},{2,26},{10... | collective-permute-start | bytes 196616 | tf_op jit(solution)/shard_map/ppermute | solution.py:16
  151.5 7.4 %all-to-all-start.2 = ((bf16[4,144,128]{2,1,0:T(8,128)(2,1)}), bf16[4,144,128]{2,1,0:T(8,128)(2,1)S(1)}, u32[]{:S(2)}, u32[]{:S(2)}) async-start(bf16[4,144,128]{2,1,0:T(8,128)(2,1)} %broadcast_in_dim.63), calls=%async_computation.2 | async-start | bytes 294912 | tf_op jit(solution)/shard_map/all_to_all | solution.py:52
  158.9 4.9 %all-to-all-done.2 = bf16[4,144,128]{2,1,0:T(8,128)(2,1)S(1)} async-done(((bf16[4,144,128]{2,1,0:T(8,128)(2,1)}), bf16[4,144,128]{2,1,0:T(8,128)(2,1)S(1)}, u32[]{:S(2)}, u32[]{:S(2)}) %all-to-all-start.2) | async-done | bytes 147488 | tf_op jit(solution)/shard_map/all_to_all | solution.py:52
  168.0 3.4 %all-to-all-start.3 = ((bf16[4,256,128]{1,2,0:T(8,128)(2,1)}), bf16[4,256,128]{1,2,0:T(8,128)(2,1)S(1)}, u32[]{:S(2)}, u32[]{:S(2)}) async-start(bf16[4,256,128]{1,2,0:T(8,128)(2,1)} %broadcast_in_dim.121), calls=%async_computation.3 | async-start | bytes 524288 | tf_op jit(solution)/shard_map/all_to_all | solution.py:52
  172.2 4.8 %all-to-all-done.3 = bf16[4,256,128]{1,2,0:T(8,128)(2,1)S(1)} async-done(((bf16[4,256,128]{1,2,0:T(8,128)(2,1)}), bf16[4,256,128]{1,2,0:T(8,128)(2,1)S(1)}, u32[]{:S(2)}, u32[]{:S(2)}) %all-to-all-start.3) | async-done | bytes 262176 | tf_op jit(solution)/shard_map/all_to_all | solution.py:52
  180.4 3.0 %collective-permute-start.15 = (bf16[512,512]{1,0:T(8,128)(2,1)S(1)}, bf16[512,512]{1,0:T(8,128)(2,1)S(1)}, u32[]{:S(2)}, u32[]{:S(2)}) collective-permute-start(bf16[512,512]{1,0:T(8,128)(2,1)S(1)} %bitcast.283), channel_id=1, source_target_pairs={{0,2},{1,3},{2,0},{3,1},{4,6},{5,7},{6,4},{7,5},{8,10},{9,11},{10,... | collective-permute-start | bytes 1572872 | tf_op jit(solution)/shard_map/ppermute | solution.py:178
  183.4 3.7 %collective-permute-start.16 = (bf16[512,512]{1,0:T(8,128)(2,1)S(1)}, bf16[512,512]{1,0:T(8,128)(2,1)S(1)}, u32[]{:S(2)}, u32[]{:S(2)}) collective-permute-start(bf16[512,512]{1,0:T(8,128)(2,1)S(1)} %bitcast.284), channel_id=1, source_target_pairs={{0,3},{1,0},{2,1},{3,2},{4,7},{5,4},{6,5},{7,6},{8,11},{9,8},{10,9... | collective-permute-start | bytes 1572872 | tf_op jit(solution)/shard_map/ppermute | solution.py:178
  187.2 2.1 fusion.25
  189.3 6.4 %collective-permute-done.14 = bf16[512,512]{1,0:T(8,128)(2,1)S(1)} collective-permute-done((bf16[512,512]{1,0:T(8,128)(2,1)S(1)}, bf16[512,512]{1,0:T(8,128)(2,1)S(1)}, u32[]{:S(2)}, u32[]{:S(2)}) %collective-permute-start.14) | collective-permute-done | bytes 524320 | tf_op jit(solution)/shard_map/ppermute | solution.py:178
  198.5 6.8 %collective-permute-done.16 = bf16[512,512]{1,0:T(8,128)(2,1)S(1)} collective-permute-done((bf16[512,512]{1,0:T(8,128)(2,1)S(1)}, bf16[512,512]{1,0:T(8,128)(2,1)S(1)}, u32[]{:S(2)}, u32[]{:S(2)}) %collective-permute-start.16) | collective-permute-done | bytes 524320 | tf_op jit(solution)/shard_map/ppermute | solution.py:178
  206.1 6.6 %collective-permute-start.17 = (bf16[256,1024]{1,0:T(8,128)(2,1)S(1)}, bf16[256,1024]{1,0:T(8,128)(2,1)S(1)}, u32[]{:S(2)}, u32[]{:S(2)}) collective-permute-start(bf16[256,1024]{1,0:T(8,128)(2,1)S(1)} %dynamic-slice_convert_fusion), channel_id=1, source_target_pairs={{0,4},{4,0},{1,5},{5,1},{2,6},{6,2},{3,7},{7,3},{8,12},{12,8},{9,1... | collective-permute-start | bytes 1572872 | tf_op jit(solution)/shard_map/ppermute | solution.py:12
  (186 shorter events, 50.8 us)
Async XLA Ops:
  6.5 180.6 %all-gather.2.cloned.1.call-start = ((), (), s32[]{:S(2)}) async-start(), calls=%async_computation.4 | async-start | bytes 4456448 | tf_op jit(solution)/shard_map/all_gather | solution.py:75
  7.4 21.3 %collective-permute-start.9 = (bf16[32,512]{1,0:T(8,128)(2,1)S(1)}, bf16[32,512]{1,0:T(8,128)(2,1)S(1)}, u32[]{:S(2)}, u32[]{:S(2)}) collective-permute-start(bf16[32,512]{1,0:T(8,128)(2,1)S(1)} %constant_dynamic-slice_fusion.1), channel_id=1, source_target_pairs={{0,4},{4,0},{1,5},{5,1},{2,6},{6,2},{3,7},{7,3},{8,12},{12,8},{9,1... | collective-permute-start | bytes 98312 | tf_op jit(solution)/shard_map/ppermute | solution.py:12
  17.0 16.5 %collective-permute-start.2 = (f32[9,4,256]{2,1,0:T(4,128)S(1)}, f32[9,4,256]{2,1,0:T(4,128)S(1)}, u32[]{:S(2)}, u32[]{:S(2)}) collective-permute-start(f32[9,4,256]{2,1,0:T(4,128)S(1)} %fusion.53), channel_id=1, source_target_pairs={{0,4},{4,0},{1,5},{5,1},{2,6},{6,2},{3,7},{7,3},{8,12},{12,8},{9,1... | collective-permute-start | bytes 110600 | tf_op jit(solution)/shard_map/ppermute | solution.py:12
  21.6 25.8 %collective-permute-start = (bf16[2,256,512]{1,2,0:T(8,128)(2,1)S(1)}, bf16[2,256,512]{1,2,0:T(8,128)(2,1)}, u32[]{:S(2)}, u32[]{:S(2)}) collective-permute-start(bf16[2,256,512]{1,2,0:T(8,128)(2,1)S(1)} %fusion.41), channel_id=1, source_target_pairs={{0,4},{4,0},{1,5},{5,1},{2,6},{6,2},{3,7},{7,3},{8,12},{12,8},{9,1... | collective-permute-start | bytes 1572872 | tf_op jit(solution)/shard_map/ppermute | solution.py:12
  25.4 23.2 %collective-permute-start.1 = (bf16[2,256,512]{1,2,0:T(8,128)(2,1)}, bf16[2,256,512]{1,2,0:T(8,128)(2,1)}, u32[]{:S(2)}, u32[]{:S(2)}) collective-permute-start(bf16[2,256,512]{1,2,0:T(8,128)(2,1)} %fusion.39), channel_id=1, source_target_pairs={{0,4},{4,0},{1,5},{5,1},{2,6},{6,2},{3,7},{7,3},{8,12},{12,8},{9,1... | collective-permute-start | bytes 1572872 | tf_op jit(solution)/shard_map/ppermute | solution.py:12
  28.7 17.8 %collective-permute-start.13 = (bf16[64,512]{1,0:T(8,128)(2,1)S(1)}, bf16[64,512]{1,0:T(8,128)(2,1)S(1)}, u32[]{:S(2)}, u32[]{:S(2)}) collective-permute-start(bf16[64,512]{1,0:T(8,128)(2,1)S(1)} %bitcast.289), channel_id=1, source_target_pairs={{0,384},{1,0},{2,128},{3,256},{128,385},{129,1},{130,129},{131,257... | collective-permute-start | bytes 196616 | tf_op jit(solution)/shard_map/ppermute | solution.py:72
  30.6 15.9 %collective-permute-start.12 = (bf16[64,512]{1,0:T(8,128)(2,1)S(1)}, bf16[64,512]{1,0:T(8,128)(2,1)S(1)}, u32[]{:S(2)}, u32[]{:S(2)}) collective-permute-start(bf16[64,512]{1,0:T(8,128)(2,1)S(1)} %bitcast.290), channel_id=1, source_target_pairs={{0,256},{1,384},{2,0},{3,128},{128,257},{129,385},{130,1},{131,129... | collective-permute-start | bytes 196616 | tf_op jit(solution)/shard_map/ppermute | solution.py:72
  33.5 6.2 %collective-permute-start.10 = (bf16[64,512]{1,0:T(8,128)(2,1)S(1)}, bf16[64,512]{1,0:T(8,128)(2,1)S(1)}, u32[]{:S(2)}, u32[]{:S(2)}) collective-permute-start(bf16[64,512]{1,0:T(8,128)(2,1)S(1)} %bitcast.291), channel_id=1, source_target_pairs={{0,0},{1,128},{2,256},{3,384},{128,1},{129,129},{130,257},{131,385... | collective-permute-start | bytes 196616 | tf_op jit(solution)/shard_map/ppermute | solution.py:72
  39.7 6.8 %collective-permute-start.11 = (bf16[64,512]{1,0:T(8,128)(2,1)S(1)}, bf16[64,512]{1,0:T(8,128)(2,1)S(1)}, u32[]{:S(2)}, u32[]{:S(2)}) collective-permute-start(bf16[64,512]{1,0:T(8,128)(2,1)S(1)} %bitcast.292), channel_id=1, source_target_pairs={{0,128},{1,256},{2,384},{3,0},{128,129},{129,257},{130,385},{131,1... | collective-permute-start | bytes 196616 | tf_op jit(solution)/shard_map/ppermute | solution.py:72
  51.2 10.4 %all-to-all-start = ((bf16[4,144,128]{2,1,0:T(8,128)(2,1)}), bf16[4,144,128]{2,1,0:T(8,128)(2,1)S(1)}, u32[]{:S(2)}, u32[]{:S(2)}) async-start(bf16[4,144,128]{2,1,0:T(8,128)(2,1)} %pad_maximum_fusion.6), calls=%async_computation | async-start | bytes 294912 | tf_op jit(solution)/shard_map/all_to_all | solution.py:103
  96.3 32.5 %copy-start.16 = (f32[2,4,256]{2,1,0:T(4,128)S(1)}, f32[2,4,256]{2,1,0:T(4,128)}, u32[]{:S(2)}) copy-start(f32[2,4,256]{2,1,0:T(4,128)} %get-tuple-element.51) | copy-start | bytes 24580
  97.1 32.6 %all-to-all-start.1 = ((bf16[4,144,128]{2,1,0:T(8,128)(2,1)}), bf16[4,144,128]{2,1,0:T(8,128)(2,1)S(1)}, u32[]{:S(2)}, u32[]{:S(2)}) async-start(bf16[4,144,128]{2,1,0:T(8,128)(2,1)} %broadcast_in_dim.61), calls=%async_computation.1 | async-start | bytes 294912 | tf_op jit(solution)/shard_map/all_to_all | solution.py:52
  109.8 11.3 %collective-permute-start.3 = (bf16[272,128]{1,0:T(8,128)(2,1)S(1)}, bf16[272,128]{1,0:T(8,128)(2,1)S(1)}, u32[]{:S(2)}, u32[]{:S(2)}) collective-permute-start(bf16[272,128]{1,0:T(8,128)(2,1)S(1)} %maximum_maximum_fusion), channel_id=1, source_target_pairs={{0,8},{8,0},{16,24},{24,16},{1,9},{9,1},{17,25},{25,17},{2,10},{10... | collective-permute-start | bytes 208904 | tf_op jit(solution)/shard_map/ppermute | solution.py:16
  112.9 10.3 %collective-permute-start.4 = (bf16[272,128]{1,0:T(8,128)(2,1)S(1)}, bf16[272,128]{1,0:T(8,128)(2,1)S(1)}, u32[]{:S(2)}, u32[]{:S(2)}) collective-permute-start(bf16[272,128]{1,0:T(8,128)(2,1)S(1)} %maximum_maximum_fusion.1), channel_id=1, source_target_pairs={{0,16},{8,24},{16,0},{24,8},{1,17},{9,25},{17,1},{25,9},{2,18},{10... | collective-permute-start | bytes 208904 | tf_op jit(solution)/shard_map/ppermute | solution.py:16
  116.5 12.0 %collective-permute-start.5 = (bf16[272,128]{1,0:T(8,128)(2,1)S(1)}, bf16[272,128]{1,0:T(8,128)(2,1)S(1)}, u32[]{:S(2)}, u32[]{:S(2)}) collective-permute-start(bf16[272,128]{1,0:T(8,128)(2,1)S(1)} %maximum_maximum_fusion.2), channel_id=1, source_target_pairs={{0,24},{8,16},{16,8},{24,0},{1,25},{9,17},{17,9},{25,1},{2,26},{10... | collective-permute-start | bytes 208904 | tf_op jit(solution)/shard_map/ppermute | solution.py:16
  140.1 18.8 %collective-permute-start.7 = (bf16[256,128]{1,0:T(8,128)(2,1)S(1)}, bf16[256,128]{1,0:T(8,128)(2,1)S(1)}, u32[]{:S(2)}, u32[]{:S(2)}) collective-permute-start(bf16[256,128]{1,0:T(8,128)(2,1)S(1)} %get-tuple-element.57), channel_id=1, source_target_pairs={{0,16},{8,24},{16,0},{24,8},{1,17},{9,25},{17,1},{25,9},{2,18},{10... | collective-permute-start | bytes 196616 | tf_op jit(solution)/shard_map/ppermute | solution.py:16
  144.1 14.7 %collective-permute-start.6 = (bf16[256,128]{1,0:T(8,128)(2,1)S(1)}, bf16[256,128]{1,0:T(8,128)(2,1)S(1)}, u32[]{:S(2)}, u32[]{:S(2)}) collective-permute-start(bf16[256,128]{1,0:T(8,128)(2,1)S(1)} %get-tuple-element.57), channel_id=1, source_target_pairs={{0,8},{8,0},{16,24},{24,16},{1,9},{9,1},{17,25},{25,17},{2,10},{10... | collective-permute-start | bytes 196616 | tf_op jit(solution)/shard_map/ppermute | solution.py:16
  146.0 12.8 %collective-permute-start.8 = (bf16[256,128]{1,0:T(8,128)(2,1)S(1)}, bf16[256,128]{1,0:T(8,128)(2,1)S(1)}, u32[]{:S(2)}, u32[]{:S(2)}) collective-permute-start(bf16[256,128]{1,0:T(8,128)(2,1)S(1)} %get-tuple-element.57), channel_id=1, source_target_pairs={{0,24},{8,16},{16,8},{24,0},{1,25},{9,17},{17,9},{25,1},{2,26},{10... | collective-permute-start | bytes 196616 | tf_op jit(solution)/shard_map/ppermute | solution.py:16
  151.5 12.3 %all-to-all-start.2 = ((bf16[4,144,128]{2,1,0:T(8,128)(2,1)}), bf16[4,144,128]{2,1,0:T(8,128)(2,1)S(1)}, u32[]{:S(2)}, u32[]{:S(2)}) async-start(bf16[4,144,128]{2,1,0:T(8,128)(2,1)} %broadcast_in_dim.63), calls=%async_computation.2 | async-start | bytes 294912 | tf_op jit(solution)/shard_map/all_to_all | solution.py:52
  168.0 9.0 %all-to-all-start.3 = ((bf16[4,256,128]{1,2,0:T(8,128)(2,1)}), bf16[4,256,128]{1,2,0:T(8,128)(2,1)S(1)}, u32[]{:S(2)}, u32[]{:S(2)}) async-start(bf16[4,256,128]{1,2,0:T(8,128)(2,1)} %broadcast_in_dim.121), calls=%async_computation.3 | async-start | bytes 524288 | tf_op jit(solution)/shard_map/all_to_all | solution.py:52
  178.5 17.2 %collective-permute-start.14 = (bf16[512,512]{1,0:T(8,128)(2,1)S(1)}, bf16[512,512]{1,0:T(8,128)(2,1)S(1)}, u32[]{:S(2)}, u32[]{:S(2)}) collective-permute-start(bf16[512,512]{1,0:T(8,128)(2,1)S(1)} %bitcast.282), channel_id=1, source_target_pairs={{0,1},{1,2},{2,3},{3,0},{4,5},{5,6},{6,7},{7,4},{8,9},{9,10},{10,1... | collective-permute-start | bytes 1572872 | tf_op jit(solution)/shard_map/ppermute | solution.py:178
  180.4 17.3 %collective-permute-start.15 = (bf16[512,512]{1,0:T(8,128)(2,1)S(1)}, bf16[512,512]{1,0:T(8,128)(2,1)S(1)}, u32[]{:S(2)}, u32[]{:S(2)}) collective-permute-start(bf16[512,512]{1,0:T(8,128)(2,1)S(1)} %bitcast.283), channel_id=1, source_target_pairs={{0,2},{1,3},{2,0},{3,1},{4,6},{5,7},{6,4},{7,5},{8,10},{9,11},{10,... | collective-permute-start | bytes 1572872 | tf_op jit(solution)/shard_map/ppermute | solution.py:178
  183.4 21.9 %collective-permute-start.16 = (bf16[512,512]{1,0:T(8,128)(2,1)S(1)}, bf16[512,512]{1,0:T(8,128)(2,1)S(1)}, u32[]{:S(2)}, u32[]{:S(2)}) collective-permute-start(bf16[512,512]{1,0:T(8,128)(2,1)S(1)} %bitcast.284), channel_id=1, source_target_pairs={{0,3},{1,0},{2,1},{3,2},{4,7},{5,4},{6,5},{7,6},{8,11},{9,8},{10,9... | collective-permute-start | bytes 1572872 | tf_op jit(solution)/shard_map/ppermute | solution.py:178
  206.1 8.1 %collective-permute-start.17 = (bf16[256,1024]{1,0:T(8,128)(2,1)S(1)}, bf16[256,1024]{1,0:T(8,128)(2,1)S(1)}, u32[]{:S(2)}, u32[]{:S(2)}) collective-permute-start(bf16[256,1024]{1,0:T(8,128)(2,1)S(1)} %dynamic-slice_convert_fusion), channel_id=1, source_target_pairs={{0,4},{4,0},{1,5},{5,1},{2,6},{6,2},{3,7},{7,3},{8,12},{12,8},{9,1... | collective-permute-start | bytes 1572872 | tf_op jit(solution)/shard_map/ppermute | solution.py:12
  (20 other events, 118.1 us)
Sparse Core Ops, SparseCore 0:
  47.5 87.9 all-gather.1

commit v2 on v0

v2 whole, which is shorter than its diff:
```python
import jax
import jax.numpy as jnp
from jax import lax
from jax.experimental import pallas as pl
from jax.experimental.pallas import tpu as pltpu
from jax.sharding import Mesh, PartitionSpec as P

BF = jnp.bfloat16
F32 = jnp.float32
SEQ = ("y", "a", "b", "c")
NT = (((1,), (1,)), ((), ()))
TN = (((0,), (0,)), ((), ()))


def swap(value):
    return lax.ppermute(value, "c", [(0, 1), (1, 0)])


def flip(value, axis, mask):
    return lax.ppermute(value, axis, [(i, i ^ mask) for i in range(4)])


def halves(value, axis, core):
    size = value.shape[axis] // 2
    kept = lax.dynamic_slice_in_dim(value, core * size, size, axis)
    sent = lax.dynamic_slice_in_dim(value, (1 - core) * size, size, axis)
    return kept, sent


def dot(left, right, dims=(((1,), (0,)), ((), ()))):
    return lax.dot_general(left, right, dims, preferred_element_type=F32)


def exact(left, right, dims):
    return lax.dot_general(
        left, right, dims, precision=lax.Precision.HIGHEST, preferred_element_type=F32
    )


def tail(log):
    high = log.astype(BF).astype(F32)
    middle = (log - high).astype(BF).astype(F32)
    low = log - high - middle
    row = lax.broadcasted_iota(jnp.int32, (16, 128), 0)
    return jnp.where(
        row == 0, high, jnp.where(row == 1, middle, jnp.where(row == 2, low, 0.0))
    ).astype(BF)


def untail(tile):
    return jnp.sum(tile.astype(F32), axis=0, keepdims=True)


def call(body, outs, args, scratch=(), flops=10**6):
    specs = [pl.BlockSpec(memory_space=pltpu.SMEM)]
    specs += [pl.BlockSpec(memory_space=pltpu.VMEM)] * (len(args) - 1)
    return pl.pallas_call(
        body,
        out_shape=[jax.ShapeDtypeStruct(*o) for o in outs],
        in_specs=specs,
        out_specs=[pl.BlockSpec(memory_space=pltpu.VMEM)] * len(outs),
        scratch_shapes=list(scratch),
        compiler_params=pltpu.CompilerParams(vmem_limit_bytes=32 * 2**20),
        cost_estimate=pl.CostEstimate(flops=flops, bytes_accessed=10**6, transcendentals=0),
    )(*args)


def four(ref, core):
    return jnp.where(core == 0, ref[0:4], ref[4:8])


def ends_body(at, keys, values, got, decay, got_small, pay, first):
    core = at[0]
    base = core * 512
    logs = jnp.concatenate([four(decay, core), got_small[0]], axis=0)
    after = (
        lax.broadcasted_iota(jnp.int32, (256, 256), 1)
        > lax.broadcasted_iota(jnp.int32, (256, 256), 0)
    ).astype(F32)
    scale = jnp.exp(exact(after, logs, NT))
    total = jnp.sum(logs, axis=1, keepdims=True)
    for h in range(4):
        mine = pl.ds(pl.multiple_of(base + h * 128, 128), 128)
        cols = slice(h * 128, h * 128 + 128)
        scaled = (keys[:, mine].astype(F32) * scale[:, h : h + 1]).astype(BF)
        own_end = dot(scaled, values[:, mine], TN)
        scaled = (got[0:256, cols].astype(F32) * scale[:, 4 + h : 5 + h]).astype(BF)
        got_end = dot(scaled, got[256:512, cols], TN)
        own_log, got_log = total[h : h + 1], total[4 + h : 5 + h]
        own_later = jnp.exp(jnp.where(core == 0, got_log, 0.0))
        got_later = jnp.exp(jnp.where(core == 0, 0.0, own_log))
        pay[h, 0:128, :] = (own_end * own_later + got_end * got_later).astype(BF)
        pay[h, 128:144, :] = tail(own_log + got_log)
        first[h, :, :] = jnp.where(core == 0, own_end, got_end).astype(BF)


def merge(got):
    s = [got[i, 0:128, :].astype(F32) for i in range(4)]
    t = [untail(got[i, 128:144, :]) for i in range(4)]
    pair = s[0] * jnp.exp(t[1]) + s[1]
    return s, t, pair


def whole(s, t, pair):
    return pair * jnp.exp(t[2] + t[3]) + s[2] * jnp.exp(t[3]) + s[3]


def lower_states(s, t, pair, at):
    odd, upper = at % 2 == 1, at >= 2
    one = jnp.where(odd, jnp.where(upper, s[2], s[0]), 0.0)
    step = jnp.where(odd, jnp.where(upper, t[2], t[0]), 0.0)
    two = jnp.where(upper, pair * jnp.exp(step), 0.0)
    before = sum(jnp.where(at > i, t[i], 0.0) for i in range(3))
    return one, two, before


def near_body(at, got, pay, *messages):
    s, t, pair = merge(got)
    group = whole(s, t, pair).astype(BF)
    log = tail(t[0] + t[1] + t[2] + t[3])
    for i in range(4):
        pay[i, 0:128, :] = group
        pay[i, 128:144, :] = log
    for k in range(4):
        one, two, before = lower_states(s, t, pair, at[1] ^ k)
        messages[k][0:128, 0:128] = one.astype(BF)
        messages[k][0:128, 128:256] = two.astype(BF)
        messages[k][128:144, 0:128] = tail(before)
        messages[k][128:144, 128:256] = jnp.zeros((16, 128), BF)


def far_body(at, got, pay, message, before_out):
    s, t, pair = merge(got)
    row = whole(s, t, pair).astype(BF)
    log = tail(t[0] + t[1] + t[2] + t[3])
    for i in range(4):
        pay[i, 0:128, :] = row
        pay[i, 128:144, :] = log
    one, two, before = lower_states(s, t, pair, at[2])
    message[:, 0:128] = one.astype(BF)
    message[:, 128:256] = two.astype(BF)
    before_out[...] = jnp.broadcast_to(before, (8, 128))


def last_body(at, got, before, message):
    s, t, pair = merge(got)
    one, two, _ = lower_states(s, t, pair, at[3])
    earlier = jnp.exp(before[0:1, :])
    one, two = (one * earlier).astype(BF), (two * earlier).astype(BF)
    for i in range(4):
        message[i, :, 0:128] = one
        message[i, :, 128:256] = two


def mix_body(
    at, keys, values, queries, got_kv, got_qg, decay, mix, got_small, first,
    n0, n1, n2, n3, f0, f1, f2, f3, mixture, coef, near, far,
):
    core, place = at[0], at[1]
    base = core * 512
    for k, (n, f) in enumerate(((n0, f0), (n1, f1), (n2, f2), (n3, f3))):
        near[place ^ k] = n[...]
        far[place ^ k] = f[...]
    rows = lax.broadcasted_iota(jnp.int32, (256, 256), 0)
    cols = lax.broadcasted_iota(jnp.int32, (256, 256), 1)
    lower = rows >= cols
    upto = lower.astype(F32)
    own_mix = jnp.where(core == 0, mix[:, 0:4, :], mix[:, 4:8, :])
    for s in range(2):
        logs = four(decay, core) if s == 0 else got_small[0]
        logs = jnp.concatenate([logs, logs], axis=0)
        other = four(decay, core) if s == 1 else got_small[0]
        levels = own_mix if s == 0 else got_small[1:9]
        second = (core if s == 0 else 1 - core) == 1
        at_row = exact(logs, upto, NT)
        at_col = exact(upto, logs, NT)
        flat = [levels[l] for l in range(8)]
        flat = [jnp.concatenate(flat[l : l + 2], axis=0) for l in range(0, 8, 2)]
        level = [f.T for f in flat]
        first_log = jnp.where(second, jnp.sum(other, axis=1, keepdims=True), 0.0)
        here = slice(s * 256, s * 256 + 256)
        for h in range(4):
            mine = pl.ds(pl.multiple_of(base + h * 128, 128), 128)
            hc = slice(h * 128, h * 128 + 128)
            if s == 0:
                q, kb, v = queries[:, mine], keys[:, mine], values[:, mine]
            else:
                q, kb, v = got_qg[0:256, hc], got_kv[0:256, hc], got_kv[256:512, hc]
            local = at_col[:, h : h + 1]
            gap = jnp.where(lower, local - at_row[h : h + 1, :], -1e30)
            weights = (dot(q, kb, NT) * jnp.exp(gap)).astype(BF)
            m = [level[l // 2][:, 4 * (l % 2) + h : 4 * (l % 2) + h + 1] for l in range(8)]
            total = dot(weights, v) * m[0]
            start = jnp.exp(local)
            total += dot(q, first[h]) * jnp.where(second, start * m[1], 0.0)
            start = start * jnp.exp(first_log[h : h + 1])
            read = dot(q, near[h, 0:128, :])
            total += read[:, 0:128] * (start * m[2]) + read[:, 128:256] * (start * m[3])
            start = start * jnp.exp(untail(near[h, 128:144, 0:128])[:, 0:1])
            read = dot(q, far[h])
            total += read[:, 0:128] * (start * m[4]) + read[:, 128:256] * (start * m[5])
            mixture[here, hc] = total
            coef[here, 2 * h : 2 * h + 1] = start * m[6]
            coef[here, 2 * h + 1 : 2 * h + 2] = start * m[7]


def norm_body(at, queries, gates, got_qg, gain, mixture, coef, last, normed):
    base = at[0] * 512
    for s in range(2):
        here = slice(s * 256, s * 256 + 256)
        for h in range(4):
            mine = pl.ds(pl.multiple_of(base + h * 128, 128), 128)
            hc = slice(h * 128, h * 128 + 128)
            if s == 0:
                q, z = queries[:, mine], gates[:, mine]
            else:
                q, z = got_qg[0:256, hc], got_qg[256:512, hc]
            read = dot(q, last[h])
            total = mixture[here, hc]
            total += read[:, 0:128] * coef[here, 2 * h : 2 * h + 1]
            total += read[:, 128:256] * coef[here, 2 * h + 1 : 2 * h + 2]
            z = z.astype(F32)
            gated = total * (z / (1.0 + jnp.exp(-z)))
            scale = lax.rsqrt(jnp.mean(gated * gated, axis=1, keepdims=True) + 1e-05)
            normed[here, hc] = (gated * scale * gain[:, mine].astype(F32)).astype(BF)


def shards(values, keys, queries, gates, log_decay, level_mix, norm_gain, weight):
    y, a, b, c, x = (lax.axis_index(n) for n in ("y", "a", "b", "c", "x"))
    at = jnp.stack([c, b, a, y]).astype(jnp.int32)
    kept, sent = halves(weight, 1, c)
    got = swap(sent)
    both = jnp.concatenate([jnp.where(c == 0, kept, got), jnp.where(c == 0, got, kept)])
    spread = []
    for k in range(4):
        perm = [(s * 4 + f, ((f + k) % 4) * 4 + s) for s in range(4) for f in range(4)]
        spread.append(lax.ppermute(both, ("y", "x"), perm))
    ring = jnp.concatenate(spread + spread[:3], axis=1)
    mine = lax.dynamic_slice_in_dim(ring, ((y - x) % 4) * 512, 2048, 1)
    gathered = lax.all_gather(mine, ("a", "b"), axis=0, tiled=True)

    away = (1 - c) * 512
    half = lambda v: lax.dynamic_slice_in_dim(v, away, 512, 1)
    got_kv = swap(jnp.concatenate([half(keys), half(values)]))
    small = jnp.concatenate([log_decay[None], level_mix])
    got_small = swap(lax.dynamic_slice_in_dim(small, (1 - c) * 4, 4, 1))
    got_qg = swap(jnp.concatenate([half(queries), half(gates)]))

    pay, first = call(
        ends_body,
        [((4, 144, 128), BF), ((4, 128, 128), BF)],
        (at, keys, values, got_kv, log_decay, got_small),
    )
    got = lax.all_to_all(pay, "b", 0, 0, tiled=True)
    pay, *near = call(near_body, [((4, 144, 128), BF)] + [((144, 256), BF)] * 4, (at, got))
    near = near[:1] + [flip(near[k], "b", k) for k in (1, 2, 3)]
    got = lax.all_to_all(pay, "a", 0, 0, tiled=True)
    pay, far, before = call(
        far_body, [((4, 144, 128), BF), ((128, 256), BF), ((8, 128), F32)], (at, got)
    )
    far = [far] + [flip(far, "b", k) for k in (1, 2, 3)]
    got = lax.all_to_all(pay, "y", 0, 0, tiled=True)
    (last,) = call(last_body, [((4, 128, 256), BF)], (at, got, before))
    last = lax.all_to_all(last, "b", 0, 0, tiled=True)
    mixture, coef = call(
        mix_body,
        [((512, 512), F32), ((512, 8), F32)],
        (at, keys, values, queries, got_kv, got_qg, log_decay, level_mix, got_small, first)
        + tuple(near) + tuple(far),
        [pltpu.VMEM((4, 144, 256), BF), pltpu.VMEM((4, 128, 256), BF)],
    )
    (normed,) = call(
        norm_body,
        [((512, 512), BF)],
        (at, queries, gates, got_qg, norm_gain[None], mixture, coef, last),
    )

    blocks = [normed] + [
        lax.ppermute(normed, "x", [(i, (i + j) % 4) for i in range(4)]) for j in (1, 2, 3)
    ]
    out = 0.0
    for j in range(4):
        out = out + dot(blocks[j], gathered[:, j * 512 : (j + 1) * 512], NT)
    return (out[:256] + swap(out[256:].astype(BF)).astype(F32)).astype(BF)


def solution(mesh):
    fine = Mesh(mesh.devices.reshape(4, 4, 4, 2, 4), SEQ + ("x",))
    return jax.shard_map(
        shards,
        mesh=fine,
        in_specs=(
            P(SEQ, "x"),
            P(SEQ, "x"),
            P(SEQ, "x"),
            P(SEQ, "x"),
            P("x", SEQ),
            P(None, "x", SEQ),
            P("x"),
            P(SEQ, "x"),
        ),
        out_specs=P(SEQ, "x"),
        check_vma=False,
    )
```

time: 340 us -> 185 us (0.54)
  waiting for transfers between devices: 243 us -> 29.4 us
  blocking collectives: 0 us -> 48.8 us
  Pallas kernels: 0 us -> 11.5 us
  matrix products: 14.9 us -> 5.6 us
  starting transfers between devices: 56.6 us -> 64.6 us
  other arithmetic: 6.08 us -> 1.88 us
    ppermute x13 -> x18, waiting for transfers between devices: 172 us -> 29.3 us  [the longest x3 13.7 us: shards(): lax.ppermute(normed, 'x', [(i, (i + j) % 4) for i in range(4)])]
    psum x1 -> x0, waiting for transfers between devices: 70.3 us -> none  [shards(): summed = lax.psum(terms.astype(jnp.bfloat16), 'head').astype(jnp.float32)]
    all_to_all x0 -> x3, blocking collectives: none -> 48.8 us  [the longest x1 28.8 us: shards(): got = lax.all_to_all(pay, 'a', 0, 0, tiled=True)]
    pallas_call x0 -> x6, Pallas kernels: none -> 11.5 us  [call(): pl.pallas_call(body, out_shape=[jax.ShapeDtypeStruct(*o) for o in outs],...]
    dot_general x10 -> x4, matrix products: 14.9 us -> 5.6 us  [dot(): return lax.dot_general(left, right, dims, preferred_element_type=F32)]
    unnamed x12 -> x50, local copies, waits for them, and re-layouts: 0.02 us -> 5.22 us
    ppermute x13 -> x18, starting transfers between devices: 56.5 us -> 61.2 us  [the longest x5 22.9 us: swap(): return lax.ppermute(value, 'c', [(0, 1), (1, 0)])]
    all_to_all x0 -> x1, starting transfers between devices: none -> 3.41 us  [shards(): last = lax.all_to_all(last, 'b', 0, 0, tiled=True)]
  transfers between devices with their start and end apart: 15 -> 20, of which waited for: 12 -> 7; matrix products, arithmetic and copies ran while one was open for 5% -> 3% of each run, Pallas kernels for 0% -> 6%
where the time goes in v2:
time: 185 us; the launch traced here: 183 us
  starting transfers between devices  64.6 us (35%)
  blocking collectives  48.8 us (26%)
  waiting for transfers between devices  29.4 us (16%)
  between operations  14 us (8%)
  Pallas kernels  11.5 us (6%)
  local copies, waits for them, and re-layouts  6.97 us (4%)
  matrix products  5.6 us (3%)
  other arithmetic  1.88 us (1%)
    all_to_all x1, blocking collectives, shards(): got = lax.all_to_all(pay, 'a', 0, 0, tiled=True)  28.8 us
    ppermute x5, starting transfers between devices, swap(): return lax.ppermute(value, 'c', [(0, 1), (1, 0)])  22.9 us
    ppermute x6, starting transfers between devices, flip(): return lax.ppermute(value, axis, [(i, i ^ mask) for i in range(4)])  18.9 us
    ppermute x3, waiting for transfers between devices, shards(): lax.ppermute(normed, 'x', [(i, (i + j) % 4) for i in range(4)])  13.7 us
    all_to_all x1, blocking collectives, shards(): got = lax.all_to_all(pay, 'b', 0, 0, tiled=True)  11.6 us
    pallas_call x6, Pallas kernels, call(): pl.pallas_call(body, out_shape=[jax.ShapeDtypeStruct(*o) for o in outs],...  11.5 us
    ppermute x4, starting transfers between devices, shards(): spread.append(lax.ppermute(both, ('y', 'x'), perm))  9.75 us
    ppermute x3, starting transfers between devices, shards(): lax.ppermute(normed, 'x', [(i, (i + j) % 4) for i in range(4)])  9.63 us
  transfers between devices with their start and end apart: 20, of which 7 were waited for; matrix products, arithmetic and copies ran while one was open for 3% of the time, Pallas kernels for 6%

profile of v2, /device:TPU:1, one launch (start us, length us, event | category | flops | bytes accessed | tf_op | source)
XLA Modules:
  0.0 182.8 jit_solution(5892831847921076871)
XLA Ops:
  7.4 8.8 %collective-permute-start.9 = (bf16[32,512]{1,0:T(8,128)(2,1)S(1)}, bf16[32,512]{1,0:T(8,128)(2,1)S(1)}, u32[]{:S(2)}, u32[]{:S(2)}) collective-permute-start(bf16[32,512]{1,0:T(8,128)(2,1)S(1)} %constant_dynamic-slice_fusion.1), channel_id=1, source_target_pairs={{0,4},{4,0},{1,5},{5,1},{2,6},{6,2},{3,7},{7,3},{8,12},{12,8},{9,1... | collective-permute-start | bytes 98312 | tf_op jit(solution)/shard_map/ppermute | solution.py:16
  18.5 2.6 %collective-permute-start.13 = (bf16[64,512]{1,0:T(8,128)(2,1)S(1)}, bf16[64,512]{1,0:T(8,128)(2,1)S(1)}, u32[]{:S(2)}, u32[]{:S(2)}) collective-permute-start(bf16[64,512]{1,0:T(8,128)(2,1)S(1)} %pad_maximum_fusion.2), channel_id=1, source_target_pairs={{0,384},{1,0},{2,128},{3,256},{128,385},{129,1},{130,129},{131,257... | collective-permute-start | bytes 196616 | tf_op jit(solution)/shard_map/ppermute | solution.py:237
  21.2 4.5 %collective-permute-start.12 = (bf16[64,512]{1,0:T(8,128)(2,1)S(1)}, bf16[64,512]{1,0:T(8,128)(2,1)S(1)}, u32[]{:S(2)}, u32[]{:S(2)}) collective-permute-start(bf16[64,512]{1,0:T(8,128)(2,1)S(1)} %pad_maximum_fusion.2), channel_id=1, source_target_pairs={{0,256},{1,384},{2,0},{3,128},{128,257},{129,385},{130,1},{131,129... | collective-permute-start | bytes 196616 | tf_op jit(solution)/shard_map/ppermute | solution.py:237
  27.6 5.0 %collective-permute-done.11 = bf16[64,512]{1,0:T(8,128)(2,1)S(1)} collective-permute-done((bf16[64,512]{1,0:T(8,128)(2,1)S(1)}, bf16[64,512]{1,0:T(8,128)(2,1)S(1)}, u32[]{:S(2)}, u32[]{:S(2)}) %collective-permute-start.11) | collective-permute-done | bytes 65568 | tf_op jit(solution)/shard_map/ppermute | solution.py:237
  33.6 3.7 %collective-permute-start.1 = (bf16[512,512]{1,0:T(8,128)(2,1)S(1)}, bf16[512,512]{1,0:T(8,128)(2,1)S(1)}, u32[]{:S(2)}, u32[]{:S(2)}) collective-permute-start(bf16[512,512]{1,0:T(8,128)(2,1)S(1)} %pad_maximum_fusion.1), channel_id=1, source_target_pairs={{0,4},{4,0},{1,5},{5,1},{2,6},{6,2},{3,7},{7,3},{8,12},{12,8},{9,1... | collective-permute-start | bytes 1572872 | tf_op jit(solution)/shard_map/ppermute | solution.py:16
  42.3 11.6 %all_to_all.20.got = bf16[4,144,128]{2,1,0:T(8,128)(2,1)S(1)} all-to-all(bf16[4,144,128]{2,1,0:T(8,128)(2,1)S(1)} %get-tuple-element.18), channel_id=1, replica_groups=mesh['y'=4,'a'=4,'b'=4,'c'=2,'x'=4] {'b'}, dimensions={0} | all-to-all | bytes 294912 | tf_op jit(solution)/shard_map/all_to_all | solution.py:254
  55.7 28.8 %all_to_all.21.got = bf16[4,144,128]{2,1,0:T(8,128)(2,1)S(1)} all-to-all(bf16[4,144,128]{2,1,0:T(8,128)(2,1)S(1)} %get-tuple-element.23), channel_id=1, replica_groups=mesh['y'=4,'a'=4,'b'=4,'c'=2,'x'=4] {'a'}, dimensions={0} | all-to-all | bytes 294912 | tf_op jit(solution)/shard_map/all_to_all | solution.py:257
  85.1 8.5 %all_to_all.22.got = bf16[4,144,128]{2,1,0:T(8,128)(2,1)S(1)} all-to-all(bf16[4,144,128]{2,1,0:T(8,128)(2,1)S(1)} %get-tuple-element.27), channel_id=1, replica_groups=mesh['y'=4,'a'=4,'b'=4,'c'=2,'x'=4] {'y'}, dimensions={0} | all-to-all | bytes 294912 | tf_op jit(solution)/shard_map/all_to_all | solution.py:262
  94.9 3.4 %all-to-all-start.3 = ((bf16[4,128,256]{2,1,0:T(8,128)(2,1)}), bf16[4,128,256]{2,1,0:T(8,128)(2,1)S(1)}, u32[]{:S(2)}, u32[]{:S(2)}) async-start(bf16[4,128,256]{2,1,0:T(8,128)(2,1)} %shard_map.86), calls=%async_computation.3 | async-start | bytes 524288 | tf_op jit(solution)/shard_map/all_to_all | solution.py:264
  98.5 4.9 %collective-permute-start = (bf16[512,512]{1,0:T(8,128)(2,1)S(1)}, bf16[512,512]{1,0:T(8,128)(2,1)S(1)}, u32[]{:S(2)}, u32[]{:S(2)}) collective-permute-start(bf16[512,512]{1,0:T(8,128)(2,1)S(1)} %pad_maximum_fusion), channel_id=1, source_target_pairs={{0,4},{4,0},{1,5},{5,1},{2,6},{6,2},{3,7},{7,3},{8,12},{12,8},{9,1... | collective-permute-start | bytes 1572872 | tf_op jit(solution)/shard_map/ppermute | solution.py:16
  103.5 3.6 %collective-permute-start.3 = (bf16[144,256]{1,0:T(8,128)(2,1)}, bf16[144,256]{1,0:T(8,128)(2,1)S(1)}, u32[]{:S(2)}, u32[]{:S(2)}) collective-permute-start(bf16[144,256]{1,0:T(8,128)(2,1)} %copy-done.19), channel_id=1, source_target_pairs={{0,8},{8,0},{16,24},{24,16},{1,9},{9,1},{17,25},{25,17},{2,10},{10... | collective-permute-start | bytes 221192 | tf_op jit(solution)/shard_map/ppermute | solution.py:20
  107.1 4.0 %collective-permute-start.4 = (bf16[144,256]{1,0:T(8,128)(2,1)}, bf16[144,256]{1,0:T(8,128)(2,1)S(1)}, u32[]{:S(2)}, u32[]{:S(2)}) collective-permute-start(bf16[144,256]{1,0:T(8,128)(2,1)} %copy-done.18), channel_id=1, source_target_pairs={{0,16},{8,24},{16,0},{24,8},{1,17},{9,25},{17,1},{25,9},{2,18},{10... | collective-permute-start | bytes 221192 | tf_op jit(solution)/shard_map/ppermute | solution.py:20
  113.2 5.0 %collective-permute-start.8 = (bf16[128,256]{1,0:T(8,128)(2,1)S(1)}, bf16[128,256]{1,0:T(8,128)(2,1)S(1)}, u32[]{:S(2)}, u32[]{:S(2)}) collective-permute-start(bf16[128,256]{1,0:T(8,128)(2,1)S(1)} %copy-done.15), channel_id=1, source_target_pairs={{0,24},{8,16},{16,8},{24,0},{1,25},{9,17},{17,9},{25,1},{2,26},{10... | collective-permute-start | bytes 196616 | tf_op jit(solution)/shard_map/ppermute | solution.py:20
  120.1 2.3 %collective-permute-start.6 = (bf16[128,256]{1,0:T(8,128)(2,1)S(1)}, bf16[128,256]{1,0:T(8,128)(2,1)S(1)}, u32[]{:S(2)}, u32[]{:S(2)}) collective-permute-start(bf16[128,256]{1,0:T(8,128)(2,1)S(1)} %copy-done.15), channel_id=1, source_target_pairs={{0,8},{8,0},{16,24},{24,16},{1,9},{9,1},{17,25},{25,17},{2,10},{10... | collective-permute-start | bytes 196616 | tf_op jit(solution)/shard_map/ppermute | solution.py:20
  122.5 7.2 %collective-permute-done.7.f2 = bf16[128,256]{1,0:T(8,128)(2,1)S(1)} collective-permute-done((bf16[128,256]{1,0:T(8,128)(2,1)S(1)}, bf16[128,256]{1,0:T(8,128)(2,1)S(1)}, u32[]{:S(2)}, u32[]{:S(2)}) %collective-permute-start.7) | collective-permute-done | bytes 65568 | tf_op jit(solution)/shard_map/ppermute | solution.py:20
  129.7 5.0 %shard_map.85 = (f32[512,512]{1,0:T(8,128)S(1)}, f32[512,8]{1,0:T(8,128)S(1)}) custom-call(s32[4]{0:T(128)S(1)} %pad_add_fusion.at, bf16[256,1024]{1,0:T(8,128)(2,1)S(1)} %copy-done.1, bf16[256,1024]{1,0:T(8,128)(2,1)S(1)} %copy-done.2, bf16[256,1024]{1,0:T(8,128)(2,1)S(1)} %copy-done, bf16[512,512]{1,0:T(8,128)(2,1)S(1)} %collective-permute-done.1.got.got_kv, ...), custom_call_target="tpu_custom_call" | custom-call | flops 1000000 | bytes 1000000 | tf_op jit(solution)/shard_map/pallas_call | solution.py:57
  138.6 2.2 %shard_map.87 = bf16[512,512]{1,0:T(8,128)(2,1)S(1)} custom-call(s32[4]{0:T(128)S(1)} %pad_add_fusion.at, bf16[256,1024]{1,0:T(8,128)(2,1)S(1)} %copy-done, bf16[256,1024]{1,0:T(8,128)(2,1)S(1)} %copy-done.3, bf16[512,512]{1,0:T(8,128)(2,1)S(1)} %collective-permute-done.got_qg, bf16[1,1024]{1,0:T(2,128)(2,1)S(1)} %broadcast_in_dim.6.gain, ...), custom_call_target="tpu_custom_call" | custom-call | flops 1000000 | bytes 1000000 | tf_op jit(solution)/shard_map/pallas_call | solution.py:57
  140.8 3.1 %collective-permute-start.14 = (bf16[512,512]{1,0:T(8,128)(2,1)S(1)}, bf16[512,512]{1,0:T(8,128)(2,1)S(1)}, u32[]{:S(2)}, u32[]{:S(2)}) collective-permute-start(bf16[512,512]{1,0:T(8,128)(2,1)S(1)} %shard_map.87), channel_id=1, source_target_pairs={{0,1},{1,2},{2,3},{3,0},{4,5},{5,6},{6,7},{7,4},{8,9},{9,10},{10,1... | collective-permute-start | bytes 1572872 | tf_op jit(solution)/shard_map/ppermute | solution.py:279
  143.9 3.4 %collective-permute-start.16 = (bf16[512,512]{1,0:T(8,128)(2,1)S(1)}, bf16[512,512]{1,0:T(8,128)(2,1)S(1)}, u32[]{:S(2)}, u32[]{:S(2)}) collective-permute-start(bf16[512,512]{1,0:T(8,128)(2,1)S(1)} %shard_map.87), channel_id=1, source_target_pairs={{0,3},{1,0},{2,1},{3,2},{4,7},{5,4},{6,5},{7,6},{8,11},{9,8},{10,9... | collective-permute-start | bytes 1572872 | tf_op jit(solution)/shard_map/ppermute | solution.py:279
  147.3 3.1 %collective-permute-start.15 = (bf16[512,512]{1,0:T(8,128)(2,1)S(1)}, bf16[512,512]{1,0:T(8,128)(2,1)S(1)}, u32[]{:S(2)}, u32[]{:S(2)}) collective-permute-start(bf16[512,512]{1,0:T(8,128)(2,1)S(1)} %shard_map.87), channel_id=1, source_target_pairs={{0,2},{1,3},{2,0},{3,1},{4,6},{5,7},{6,4},{7,5},{8,10},{9,11},{10,... | collective-permute-start | bytes 1572872 | tf_op jit(solution)/shard_map/ppermute | solution.py:279
  150.5 2.1 %fusion.9 = f32[512,1024]{1,0:T(8,128)S(1)} fusion(bf16[512,512]{1,0:T(8,128)(2,1)S(1)} %shard_map.87, bf16[1024,2048]{1,0:T(8,128)(2,1)} %all-gather.2.cloned.1.call-done), kind=kOutput, calls=%fused_computation.10 | convolution fusion | flops 536870912 | bytes 3670016 | tf_op jit(solution)/shard_map/dot_general | solution.py:31
  152.6 4.0 %collective-permute-done.14 = bf16[512,512]{1,0:T(8,128)(2,1)S(1)} collective-permute-done((bf16[512,512]{1,0:T(8,128)(2,1)S(1)}, bf16[512,512]{1,0:T(8,128)(2,1)S(1)}, u32[]{:S(2)}, u32[]{:S(2)}) %collective-permute-start.14) | collective-permute-done | bytes 524320 | tf_op jit(solution)/shard_map/ppermute | solution.py:279
  158.6 9.7 %collective-permute-done.15 = bf16[512,512]{1,0:T(8,128)(2,1)S(1)} collective-permute-done((bf16[512,512]{1,0:T(8,128)(2,1)S(1)}, bf16[512,512]{1,0:T(8,128)(2,1)S(1)}, u32[]{:S(2)}, u32[]{:S(2)}) %collective-permute-start.15) | collective-permute-done | bytes 524320 | tf_op jit(solution)/shard_map/ppermute | solution.py:279
  169.9 3.6 %collective-permute-start.17 = (bf16[256,1024]{1,0:T(8,128)(2,1)S(1)}, bf16[256,1024]{1,0:T(8,128)(2,1)S(1)}, u32[]{:S(2)}, u32[]{:S(2)}) collective-permute-start(bf16[256,1024]{1,0:T(8,128)(2,1)S(1)} %slice.45), channel_id=1, source_target_pairs={{0,4},{4,0},{1,5},{5,1},{2,6},{6,2},{3,7},{7,3},{8,12},{12,8},{9,1... | collective-permute-start | bytes 1572872 | tf_op jit(solution)/shard_map/ppermute | solution.py:16
  (94 shorter events, 28.7 us)
Async XLA Ops:
  6.5 144.0 %all-gather.2.cloned.1.call-start = ((), (), s32[]{:S(2)}) async-start(), calls=%async_computation.4 | async-start | bytes 4456448 | tf_op jit(solution)/shard_map/all_gather | solution.py:240
  7.4 9.6 %collective-permute-start.9 = (bf16[32,512]{1,0:T(8,128)(2,1)S(1)}, bf16[32,512]{1,0:T(8,128)(2,1)S(1)}, u32[]{:S(2)}, u32[]{:S(2)}) collective-permute-start(bf16[32,512]{1,0:T(8,128)(2,1)S(1)} %constant_dynamic-slice_fusion.1), channel_id=1, source_target_pairs={{0,4},{4,0},{1,5},{5,1},{2,6},{6,2},{3,7},{7,3},{8,12},{12,8},{9,1... | collective-permute-start | bytes 98312 | tf_op jit(solution)/shard_map/ppermute | solution.py:16
  17.8 9.8 %collective-permute-start.10 = (bf16[64,512]{1,0:T(8,128)(2,1)S(1)}, bf16[64,512]{1,0:T(8,128)(2,1)S(1)}, u32[]{:S(2)}, u32[]{:S(2)}) collective-permute-start(bf16[64,512]{1,0:T(8,128)(2,1)S(1)} %pad_maximum_fusion.2), channel_id=1, source_target_pairs={{0,0},{1,128},{2,256},{3,384},{128,1},{129,129},{130,257},{131,385... | collective-permute-start | bytes 196616 | tf_op jit(solution)/shard_map/ppermute | solution.py:237
  18.5 14.1 %collective-permute-start.13 = (bf16[64,512]{1,0:T(8,128)(2,1)S(1)}, bf16[64,512]{1,0:T(8,128)(2,1)S(1)}, u32[]{:S(2)}, u32[]{:S(2)}) collective-permute-start(bf16[64,512]{1,0:T(8,128)(2,1)S(1)} %pad_maximum_fusion.2), channel_id=1, source_target_pairs={{0,384},{1,0},{2,128},{3,256},{128,385},{129,1},{130,129},{131,257... | collective-permute-start | bytes 196616 | tf_op jit(solution)/shard_map/ppermute | solution.py:237
  21.2 11.5 %collective-permute-start.12 = (bf16[64,512]{1,0:T(8,128)(2,1)S(1)}, bf16[64,512]{1,0:T(8,128)(2,1)S(1)}, u32[]{:S(2)}, u32[]{:S(2)}) collective-permute-start(bf16[64,512]{1,0:T(8,128)(2,1)S(1)} %pad_maximum_fusion.2), channel_id=1, source_target_pairs={{0,256},{1,384},{2,0},{3,128},{128,257},{129,385},{130,1},{131,129... | collective-permute-start | bytes 196616 | tf_op jit(solution)/shard_map/ppermute | solution.py:237
  25.7 6.9 %collective-permute-start.11 = (bf16[64,512]{1,0:T(8,128)(2,1)S(1)}, bf16[64,512]{1,0:T(8,128)(2,1)S(1)}, u32[]{:S(2)}, u32[]{:S(2)}) collective-permute-start(bf16[64,512]{1,0:T(8,128)(2,1)S(1)} %pad_maximum_fusion.2), channel_id=1, source_target_pairs={{0,128},{1,256},{2,384},{3,0},{128,129},{129,257},{130,385},{131,1... | collective-permute-start | bytes 196616 | tf_op jit(solution)/shard_map/ppermute | solution.py:237
  33.6 64.8 %copy-start = (bf16[256,1024]{1,0:T(8,128)(2,1)S(1)}, bf16[256,1024]{1,0:T(8,128)(2,1)}, u32[]{:S(2)}) copy-start(bf16[256,1024]{1,0:T(8,128)(2,1)} %queries.3) | copy-start | bytes 1572868
  33.6 64.8 %copy-start.3 = (bf16[256,1024]{1,0:T(8,128)(2,1)S(1)}, bf16[256,1024]{1,0:T(8,128)(2,1)}, u32[]{:S(2)}) copy-start(bf16[256,1024]{1,0:T(8,128)(2,1)} %gates.1) | copy-start | bytes 1572868
  33.6 6.8 %collective-permute-start.1 = (bf16[512,512]{1,0:T(8,128)(2,1)S(1)}, bf16[512,512]{1,0:T(8,128)(2,1)S(1)}, u32[]{:S(2)}, u32[]{:S(2)}) collective-permute-start(bf16[512,512]{1,0:T(8,128)(2,1)S(1)} %pad_maximum_fusion.1), channel_id=1, source_target_pairs={{0,4},{4,0},{1,5},{5,1},{2,6},{6,2},{3,7},{7,3},{8,12},{12,8},{9,1... | collective-permute-start | bytes 1572872 | tf_op jit(solution)/shard_map/ppermute | solution.py:16
  37.3 3.1 %collective-permute-start.2 = (f32[9,4,256]{2,1,0:T(4,128)S(1)}, f32[9,4,256]{2,1,0:T(4,128)S(1)}, u32[]{:S(2)}, u32[]{:S(2)}) collective-permute-start(f32[9,4,256]{2,1,0:T(4,128)S(1)} %fusion.11), channel_id=1, source_target_pairs={{0,4},{4,0},{1,5},{5,1},{2,6},{6,2},{3,7},{7,3},{8,12},{12,8},{9,1... | collective-permute-start | bytes 110600 | tf_op jit(solution)/shard_map/ppermute | solution.py:16
  42.2 80.2 %copy-start.21 = (bf16[1024]{0:T(1024)(128)(2,1)S(1)}, bf16[1024]{0:T(1024)(128)(2,1)}, u32[]{:S(2)}) copy-start(bf16[1024]{0:T(1024)(128)(2,1)} %param.14) | copy-start | bytes 6148
  55.7 42.7 %copy-start.19 = (bf16[144,256]{1,0:T(8,128)(2,1)}, bf16[144,256]{1,0:T(8,128)(2,1)S(1)}, u32[]{:S(2)}) copy-start(bf16[144,256]{1,0:T(8,128)(2,1)S(1)} %get-tuple-element.20) | copy-start | bytes 221188
  94.9 41.5 %all-to-all-start.3 = ((bf16[4,128,256]{2,1,0:T(8,128)(2,1)}), bf16[4,128,256]{2,1,0:T(8,128)(2,1)S(1)}, u32[]{:S(2)}, u32[]{:S(2)}) async-start(bf16[4,128,256]{2,1,0:T(8,128)(2,1)} %shard_map.86), calls=%async_computation.3 | async-start | bytes 524288 | tf_op jit(solution)/shard_map/all_to_all | solution.py:264
  98.5 19.7 %collective-permute-start = (bf16[512,512]{1,0:T(8,128)(2,1)S(1)}, bf16[512,512]{1,0:T(8,128)(2,1)S(1)}, u32[]{:S(2)}, u32[]{:S(2)}) collective-permute-start(bf16[512,512]{1,0:T(8,128)(2,1)S(1)} %pad_maximum_fusion), channel_id=1, source_target_pairs={{0,4},{4,0},{1,5},{5,1},{2,6},{6,2},{3,7},{7,3},{8,12},{12,8},{9,1... | collective-permute-start | bytes 1572872 | tf_op jit(solution)/shard_map/ppermute | solution.py:16
  103.5 16.7 %collective-permute-start.3 = (bf16[144,256]{1,0:T(8,128)(2,1)}, bf16[144,256]{1,0:T(8,128)(2,1)S(1)}, u32[]{:S(2)}, u32[]{:S(2)}) collective-permute-start(bf16[144,256]{1,0:T(8,128)(2,1)} %copy-done.19), channel_id=1, source_target_pairs={{0,8},{8,0},{16,24},{24,16},{1,9},{9,1},{17,25},{25,17},{2,10},{10... | collective-permute-start | bytes 221192 | tf_op jit(solution)/shard_map/ppermute | solution.py:20
  107.1 15.4 %collective-permute-start.4 = (bf16[144,256]{1,0:T(8,128)(2,1)}, bf16[144,256]{1,0:T(8,128)(2,1)S(1)}, u32[]{:S(2)}, u32[]{:S(2)}) collective-permute-start(bf16[144,256]{1,0:T(8,128)(2,1)} %copy-done.18), channel_id=1, source_target_pairs={{0,16},{8,24},{16,0},{24,8},{1,17},{9,25},{17,1},{25,9},{2,18},{10... | collective-permute-start | bytes 221192 | tf_op jit(solution)/shard_map/ppermute | solution.py:20
  111.1 11.4 %collective-permute-start.5 = (bf16[144,256]{1,0:T(8,128)(2,1)S(1)}, bf16[144,256]{1,0:T(8,128)(2,1)S(1)}, u32[]{:S(2)}, u32[]{:S(2)}) collective-permute-start(bf16[144,256]{1,0:T(8,128)(2,1)S(1)} %copy-done.17), channel_id=1, source_target_pairs={{0,24},{8,16},{16,8},{24,0},{1,25},{9,17},{17,9},{25,1},{2,26},{10... | collective-permute-start | bytes 221192 | tf_op jit(solution)/shard_map/ppermute | solution.py:20
  113.2 9.4 %collective-permute-start.8 = (bf16[128,256]{1,0:T(8,128)(2,1)S(1)}, bf16[128,256]{1,0:T(8,128)(2,1)S(1)}, u32[]{:S(2)}, u32[]{:S(2)}) collective-permute-start(bf16[128,256]{1,0:T(8,128)(2,1)S(1)} %copy-done.15), channel_id=1, source_target_pairs={{0,24},{8,16},{16,8},{24,0},{1,25},{9,17},{17,9},{25,1},{2,26},{10... | collective-permute-start | bytes 196616 | tf_op jit(solution)/shard_map/ppermute | solution.py:20
  118.2 11.5 %collective-permute-start.7 = (bf16[128,256]{1,0:T(8,128)(2,1)S(1)}, bf16[128,256]{1,0:T(8,128)(2,1)S(1)}, u32[]{:S(2)}, u32[]{:S(2)}) collective-permute-start(bf16[128,256]{1,0:T(8,128)(2,1)S(1)} %copy-done.15), channel_id=1, source_target_pairs={{0,16},{8,24},{16,0},{24,8},{1,17},{9,25},{17,1},{25,9},{2,18},{10... | collective-permute-start | bytes 196616 | tf_op jit(solution)/shard_map/ppermute | solution.py:20
  120.1 9.6 %collective-permute-start.6 = (bf16[128,256]{1,0:T(8,128)(2,1)S(1)}, bf16[128,256]{1,0:T(8,128)(2,1)S(1)}, u32[]{:S(2)}, u32[]{:S(2)}) collective-permute-start(bf16[128,256]{1,0:T(8,128)(2,1)S(1)} %copy-done.15), channel_id=1, source_target_pairs={{0,8},{8,0},{16,24},{24,16},{1,9},{9,1},{17,25},{25,17},{2,10},{10... | collective-permute-start | bytes 196616 | tf_op jit(solution)/shard_map/ppermute | solution.py:20
  140.8 15.8 %collective-permute-start.14 = (bf16[512,512]{1,0:T(8,128)(2,1)S(1)}, bf16[512,512]{1,0:T(8,128)(2,1)S(1)}, u32[]{:S(2)}, u32[]{:S(2)}) collective-permute-start(bf16[512,512]{1,0:T(8,128)(2,1)S(1)} %shard_map.87), channel_id=1, source_target_pairs={{0,1},{1,2},{2,3},{3,0},{4,5},{5,6},{6,7},{7,4},{8,9},{9,10},{10,1... | collective-permute-start | bytes 1572872 | tf_op jit(solution)/shard_map/ppermute | solution.py:279
  143.9 25.1 %collective-permute-start.16 = (bf16[512,512]{1,0:T(8,128)(2,1)S(1)}, bf16[512,512]{1,0:T(8,128)(2,1)S(1)}, u32[]{:S(2)}, u32[]{:S(2)}) collective-permute-start(bf16[512,512]{1,0:T(8,128)(2,1)S(1)} %shard_map.87), channel_id=1, source_target_pairs={{0,3},{1,0},{2,1},{3,2},{4,7},{5,4},{6,5},{7,6},{8,11},{9,8},{10,9... | collective-permute-start | bytes 1572872 | tf_op jit(solution)/shard_map/ppermute | solution.py:279
  147.3 21.0 %collective-permute-start.15 = (bf16[512,512]{1,0:T(8,128)(2,1)S(1)}, bf16[512,512]{1,0:T(8,128)(2,1)S(1)}, u32[]{:S(2)}, u32[]{:S(2)}) collective-permute-start(bf16[512,512]{1,0:T(8,128)(2,1)S(1)} %shard_map.87), channel_id=1, source_target_pairs={{0,2},{1,3},{2,0},{3,1},{4,6},{5,7},{6,4},{7,5},{8,10},{9,11},{10,... | collective-permute-start | bytes 1572872 | tf_op jit(solution)/shard_map/ppermute | solution.py:279
  169.9 5.1 %collective-permute-start.17 = (bf16[256,1024]{1,0:T(8,128)(2,1)S(1)}, bf16[256,1024]{1,0:T(8,128)(2,1)S(1)}, u32[]{:S(2)}, u32[]{:S(2)}) collective-permute-start(bf16[256,1024]{1,0:T(8,128)(2,1)S(1)} %slice.45), channel_id=1, source_target_pairs={{0,4},{4,0},{1,5},{5,1},{2,6},{6,2},{3,7},{7,3},{8,12},{12,8},{9,1... | collective-permute-start | bytes 1572872 | tf_op jit(solution)/shard_map/ppermute | solution.py:16
  (18 other events, 294.5 us)
Sparse Core Ops, SparseCore 0:
  33.6 84.9 all-gather.1

commit v3 on v2

v3 whole, which is shorter than its diff:
```python
import jax
import jax.numpy as jnp
from jax import lax
from jax.experimental import pallas as pl
from jax.experimental.pallas import tpu as pltpu
from jax.sharding import Mesh, PartitionSpec as P

BF = jnp.bfloat16
F32 = jnp.float32
SEQ = ("y", "a", "b", "c")
NT = (((1,), (1,)), ((), ()))
TN = (((0,), (0,)), ((), ()))
LOGS = 1024


def swap(value):
    return lax.ppermute(value, "c", [(0, 1), (1, 0)])


def dot(left, right, dims=(((1,), (0,)), ((), ()))):
    return lax.dot_general(left, right, dims, preferred_element_type=F32)


def exact(left, right, dims):
    return lax.dot_general(
        left, right, dims, precision=lax.Precision.HIGHEST, preferred_element_type=F32
    )


def tail(log):
    high = log.astype(BF).astype(F32)
    middle = (log - high).astype(BF).astype(F32)
    low = log - high - middle
    row = lax.broadcasted_iota(jnp.int32, (16, 128), 0)
    return jnp.where(
        row == 0, high, jnp.where(row == 1, middle, jnp.where(row == 2, low, 0.0))
    ).astype(BF)


def untail(tile):
    return jnp.sum(tile.astype(F32), axis=0, keepdims=True)


def call(body, outs, args, unread=(), flops=10**6):
    specs = [pl.BlockSpec(memory_space=pltpu.SMEM)]
    specs += [pl.BlockSpec(memory_space=pltpu.VMEM)] * (len(args) - 1)
    specs += [pl.BlockSpec(memory_space=pl.ANY)] * len(unread)

    def run(*refs):
        body(*refs[: len(args)], *refs[len(args) + len(unread) :])

    return pl.pallas_call(
        run,
        out_shape=[jax.ShapeDtypeStruct(*o) for o in outs],
        in_specs=specs,
        out_specs=[pl.BlockSpec(memory_space=pltpu.VMEM)] * len(outs),
        compiler_params=pltpu.CompilerParams(vmem_limit_bytes=32 * 2**20),
        cost_estimate=pl.CostEstimate(flops=flops, bytes_accessed=10**6, transcendentals=0),
    )(*args, *unread)


def pack_body(at, keys, values, queries, gates, decay, mix, out):
    core = at[0]
    theirs = pl.ds(pl.multiple_of((1 - core) * 512, 512), 512)
    for i, ref in enumerate((keys, values, queries, gates)):
        out[i * 256 : i * 256 + 256, :] = ref[:, theirs]
    logs = [jnp.where(core == 0, decay[4:8], decay[0:4])]
    logs += [jnp.where(core == 0, mix[l, 4:8], mix[l, 0:4]) for l in range(8)]
    logs = jnp.concatenate(logs + [jnp.zeros((12, 256), F32)], axis=0)
    high = logs.astype(BF)
    out[LOGS:, 0:256] = high
    out[LOGS:, 256:512] = (logs - high.astype(F32)).astype(BF)


def own_half(ref, core):
    return jnp.where(core == 0, ref[0:4], ref[4:8])


def got_logs(got):
    tile = got[LOGS:, :].astype(F32)
    return tile[:, 0:256] + tile[:, 256:512]


def ends_body(at, keys, values, got, decay, pay, first):
    core = at[0]
    logs = jnp.concatenate([own_half(decay, core), got_logs(got)[0:4]], axis=0)
    after = (
        lax.broadcasted_iota(jnp.int32, (256, 256), 1)
        > lax.broadcasted_iota(jnp.int32, (256, 256), 0)
    ).astype(F32)
    scale = jnp.exp(exact(after, logs, NT))
    total = jnp.sum(logs, axis=1, keepdims=True)
    for h in range(4):
        mine = pl.ds(pl.multiple_of(core * 512 + h * 128, 128), 128)
        cols = slice(h * 128, h * 128 + 128)
        scaled = (keys[:, mine].astype(F32) * scale[:, h : h + 1]).astype(BF)
        own_end = dot(scaled, values[:, mine], TN)
        scaled = (got[0:256, cols].astype(F32) * scale[:, 4 + h : 5 + h]).astype(BF)
        got_end = dot(scaled, got[256:512, cols], TN)
        own_log, got_log = total[h : h + 1], total[4 + h : 5 + h]
        own_later = jnp.exp(jnp.where(core == 0, got_log, 0.0))
        got_later = jnp.exp(jnp.where(core == 0, 0.0, own_log))
        pay[h, 0:128, :] = (own_end * own_later + got_end * got_later).astype(BF)
        pay[h, 128:144, :] = tail(own_log + got_log)
        first[h, :, :] = jnp.where(core == 0, own_end, got_end).astype(BF)


def merge(got):
    s = [got[i, 0:128, :].astype(F32) for i in range(4)]
    t = [untail(got[i, 128:144, :]) for i in range(4)]
    pair = s[0] * jnp.exp(t[1]) + s[1]
    return s, t, pair


def send_whole(s, t, pair, pay):
    state = (pair * jnp.exp(t[2] + t[3]) + s[2] * jnp.exp(t[3]) + s[3]).astype(BF)
    log = tail(t[0] + t[1] + t[2] + t[3])
    for i in range(4):
        pay[i, 0:128, :] = state
        pay[i, 128:144, :] = log


def lower_states(s, t, pair, at):
    odd, upper = at % 2 == 1, at >= 2
    one = jnp.where(odd, jnp.where(upper, s[2], s[0]), 0.0)
    step = jnp.where(odd, jnp.where(upper, t[2], t[0]), 0.0)
    two = jnp.where(upper, pair * jnp.exp(step), 0.0)
    before = sum(jnp.where(at > i, t[i], 0.0) for i in range(3))
    return one, two, before


def near_body(at, got, pay, message):
    s, t, pair = merge(got)
    send_whole(s, t, pair, pay)
    for i in range(4):
        one, two, before = lower_states(s, t, pair, jnp.int32(i))
        message[i, 0:128, 0:128] = one.astype(BF)
        message[i, 0:128, 128:256] = two.astype(BF)
        message[i, 128:144, 0:128] = tail(before)
        message[i, 128:144, 128:256] = jnp.zeros((16, 128), BF)


def far_body(at, got, pay, message, before_out):
    s, t, pair = merge(got)
    send_whole(s, t, pair, pay)
    one, two, before = lower_states(s, t, pair, at[2])
    for i in range(4):
        message[i, :, 0:128] = one.astype(BF)
        message[i, :, 128:256] = two.astype(BF)
    before_out[...] = jnp.broadcast_to(before, (8, 128))


def last_body(at, got, before, message):
    s, t, pair = merge(got)
    one, two, _ = lower_states(s, t, pair, at[3])
    earlier = jnp.exp(before[0:1, :])
    one, two = (one * earlier).astype(BF), (two * earlier).astype(BF)
    for i in range(4):
        message[i, :, 0:128] = one
        message[i, :, 128:256] = two


def place(s, core):
    at = core if s == 0 else 1 - core
    return at, pl.ds(pl.multiple_of(at * 256, 256), 256)


def own_body(at, keys, values, queries, got, decay, mix, first, mixture, coef):
    core = at[0]
    rows = lax.broadcasted_iota(jnp.int32, (256, 256), 0)
    cols = lax.broadcasted_iota(jnp.int32, (256, 256), 1)
    lower = rows >= cols
    upto = lower.astype(F32)
    own_logs = [own_half(decay, core)]
    own_logs += [jnp.where(core == 0, mix[l, 0:4], mix[l, 4:8]) for l in range(8)]
    own_logs = jnp.concatenate(own_logs + [jnp.zeros((12, 256), F32)], axis=0)
    both = (own_logs, got_logs(got))
    for s in range(2):
        second, here = place(s, core)
        logs = both[s]
        at_row = exact(logs[0:8], upto, NT)
        at_col = exact(upto, logs[0:8], NT)
        level = logs.T
        first_log = jnp.sum(both[1 - s][0:4], axis=1, keepdims=True)
        first_log = jnp.where(second == 1, first_log, 0.0)
        for h in range(4):
            mine = pl.ds(pl.multiple_of(core * 512 + h * 128, 128), 128)
            hc = slice(h * 128, h * 128 + 128)
            if s == 0:
                q, kb, v = queries[:, mine], keys[:, mine], values[:, mine]
            else:
                q, kb, v = got[512:768, hc], got[0:256, hc], got[256:512, hc]
            local = at_col[:, h : h + 1]
            gap = jnp.where(lower, local - at_row[h : h + 1, :], -1e30)
            weights = (dot(q, kb, NT) * jnp.exp(gap)).astype(BF)
            m = [level[:, 4 + 4 * l + h : 5 + 4 * l + h] for l in range(8)]
            total = dot(weights, v) * m[0]
            start = jnp.exp(local)
            total += dot(q, first[h]) * jnp.where(second == 1, start * m[1], 0.0)
            start = start * jnp.exp(first_log[h : h + 1])
            mixture[here, hc] = total
            for l in range(2, 8):
                coef[here, 6 * h + l - 2 : 6 * h + l - 1] = start * m[l]


def norm_body(at, queries, gates, got, gain, mixture, coef, near, far, last, normed):
    core = at[0]
    for s in range(2):
        _, here = place(s, core)
        for h in range(4):
            mine = pl.ds(pl.multiple_of(core * 512 + h * 128, 128), 128)
            hc = slice(h * 128, h * 128 + 128)
            if s == 0:
                q, z = queries[:, mine], gates[:, mine]
            else:
                q, z = got[512:768, hc], got[768:1024, hc]
            scale = [coef[here, 6 * h + l : 6 * h + l + 1] for l in range(6)]
            later = jnp.exp(untail(near[h, 128:144, 0:128])[:, 0:1])
            total = mixture[here, hc]
            read = dot(q, near[h, 0:128, :])
            total += read[:, 0:128] * scale[0] + read[:, 128:256] * scale[1]
            read = dot(q, far[h])
            total += read[:, 0:128] * (scale[2] * later) + read[:, 128:256] * (scale[3] * later)
            read = dot(q, last[h])
            total += read[:, 0:128] * (scale[4] * later) + read[:, 128:256] * (scale[5] * later)
            z = z.astype(F32)
            gated = total * (z / (1.0 + jnp.exp(-z)))
            size = lax.rsqrt(jnp.mean(gated * gated, axis=1, keepdims=True) + 1e-05)
            normed[here, hc] = (gated * size * gain[:, mine].astype(F32)).astype(BF)


def project_body(at, left, right, out, total):
    step = pl.program_id(0)
    part = dot(left[...], right[...], NT)

    @pl.when(step == 0)
    def _():
        total[...] = part

    @pl.when(step > 0)
    def _():
        total[...] += part

    @pl.when(step == pl.num_programs(0) - 1)
    def _():
        out[...] = total[...].astype(BF)


def project(at, left, right, other):
    row = (lambda k, at: (1 - at[0], k)) if other else (lambda k, at: (at[0], k))
    return pl.pallas_call(
        project_body,
        out_shape=jax.ShapeDtypeStruct((256, 512), BF),
        grid_spec=pltpu.PrefetchScalarGridSpec(
            num_scalar_prefetch=1,
            grid=(4,),
            in_specs=[
                pl.BlockSpec((256, 1024), row),
                pl.BlockSpec((512, 1024), lambda k, at: (0, k)),
            ],
            out_specs=pl.BlockSpec((256, 512), lambda k, at: (0, 0)),
            scratch_shapes=[pltpu.VMEM((256, 512), F32)],
        ),
        compiler_params=pltpu.CompilerParams(vmem_limit_bytes=32 * 2**20),
        cost_estimate=pl.CostEstimate(
            flops=2**30, bytes_accessed=6 * 2**20, transcendentals=0
        ),
    )(at, left, right)


def weave_body(at, own, got, out):
    core = at[0]
    i = lax.broadcasted_iota(jnp.int32, (128, 256), 0)
    j = lax.broadcasted_iota(jnp.int32, (128, 256), 1)
    spot = (i >> 5) * 64 + (i & 31)
    mine = (j == spot + core * 32).astype(BF)
    theirs = (j == spot + (1 - core) * 32).astype(BF)
    for m in range(4):
        cols = slice(m * 128, m * 128 + 128)
        both = dot(own[:, cols], mine) + dot(got[:, cols], theirs)
        out[:, m * 256 : m * 256 + 256] = both.astype(BF)


def shards(values, keys, queries, gates, log_decay, level_mix, norm_gain, weight):
    y, a, b, c, x = (lax.axis_index(n) for n in ("y", "a", "b", "c", "x"))
    at = jnp.stack([c, b, a, y]).astype(jnp.int32)
    spread = []
    for k in range(4):
        perm = [(s * 4 + f, ((f + k) % 4) * 4 + s) for s in range(4) for f in range(4)]
        spread.append(lax.ppermute(weight, ("y", "x"), perm))
    ring = jnp.concatenate(spread + spread[:3], axis=1)
    mine = lax.dynamic_slice_in_dim(ring, ((y - x) % 4) * 1024, 4096, 1)
    (pack,) = call(
        pack_body,
        [((LOGS + 48, 512), BF)],
        (at, keys, values, queries, gates, log_decay, level_mix),
    )
    got = swap(pack)
    mine, got = lax.optimization_barrier((mine, got))
    gathered = lax.all_gather(mine, ("a", "b"), axis=0, tiled=True)

    pay, first = call(
        ends_body,
        [((4, 144, 128), BF), ((4, 128, 128), BF)],
        (at, keys, values, got, log_decay),
    )
    mixture, coef = call(
        own_body,
        [((512, 512), F32), ((512, 24), F32)],
        (at, keys, values, queries, got, log_decay, level_mix, first),
    )
    near = lax.all_to_all(pay, "b", 0, 0, tiled=True)
    pay, near = call(near_body, [((4, 144, 128), BF), ((4, 144, 256), BF)], (at, near))
    near = lax.all_to_all(near, "b", 0, 0, tiled=True)
    far = lax.all_to_all(pay, "a", 0, 0, tiled=True)
    pay, far, before = call(
        far_body,
        [((4, 144, 128), BF), ((4, 128, 256), BF), ((8, 128), F32)],
        (at, far),
        (near, mixture),
    )
    far = lax.all_to_all(far, "b", 0, 0, tiled=True)
    last = lax.all_to_all(pay, "y", 0, 0, tiled=True)
    (last,) = call(last_body, [((4, 128, 256), BF)], (at, last, before), (far,))
    last = lax.all_to_all(last, "b", 0, 0, tiled=True)
    (normed,) = call(
        norm_body,
        [((512, 512), BF)],
        (at, queries, gates, got, norm_gain[None], mixture, coef, near, far, last),
    )

    blocks = [normed] + [
        lax.ppermute(normed, "x", [(i, (i + j) % 4) for i in range(4)]) for j in (1, 2, 3)
    ]
    pairs = []
    for block in blocks:
        theirs = swap(block)
        pairs += [jnp.where(c == 0, block, theirs), jnp.where(c == 0, theirs, block)]
    left = jnp.concatenate(pairs, axis=1)
    theirs = swap(project(at, left, gathered, True))
    own = project(at, left, gathered, False)
    return call(weave_body, [((256, 1024), BF)], (at, own, theirs))[0]


def solution(mesh):
    fine = Mesh(mesh.devices.reshape(4, 4, 4, 2, 4), SEQ + ("x",))
    return jax.shard_map(
        shards,
        mesh=fine,
        in_specs=(
            P(SEQ, "x"),
            P(SEQ, "x"),
            P(SEQ, "x"),
            P(SEQ, "x"),
            P("x", SEQ),
            P(None, "x", SEQ),
            P("x"),
            P(SEQ, "x"),
        ),
        out_specs=P(SEQ, "x"),
        check_vma=False,
    )
```

time: 185 us -> 201 us (1.086)
  waiting for transfers between devices: 29.4 us -> 12 us
  local copies, waits for them, and re-layouts: 6.97 us -> 23 us
  Pallas kernels: 11.5 us -> 23.5 us
  blocking collectives: 48.8 us -> 60.2 us
  matrix products: 5.6 us -> 0 us
    unnamed x50 -> x66, local copies, waits for them, and re-layouts: 5.22 us -> 21.6 us
    ppermute x3, waiting for transfers between devices: 13.7 us -> 0.01 us  [shards(): lax.ppermute(normed, 'x', [(i, (i + j) % 4) for i in range(4)])]
    ppermute x10 -> x4, waiting for transfers between devices: 12.2 us -> 0.01 us  [shards(): spread.append(lax.ppermute(weight, ('y', 'x'), perm))]
    pallas_call x6 -> x10, Pallas kernels: 11.5 us -> 23.5 us  [the longest x8 17.3 us: call(): pl.pallas_call(run, out_shape=[jax.ShapeDtypeStruct(*o) for o in outs], i...]
    all_to_all x3 -> x4, blocking collectives: 48.8 us -> 60.2 us  [the longest x1 30.1 us: shards(): far = lax.all_to_all(pay, 'a', 0, 0, tiled=True)]
    ppermute x10 -> x4, starting transfers between devices: 28.7 us -> 17.3 us  [shards(): spread.append(lax.ppermute(weight, ('y', 'x'), perm))]
    ppermute x5 -> x6, starting transfers between devices: 22.9 us -> 31.6 us  [swap(): return lax.ppermute(value, 'c', [(0, 1), (1, 0)])]
    all_to_all x1, waiting for transfers between devices: 0.01 us -> 7.2 us  [shards(): last = lax.all_to_all(last, 'b', 0, 0, tiled=True)]
  transfers between devices with their start and end apart: 20 -> 16, of which waited for: 7 -> 4; matrix products, arithmetic and copies ran while one was open for 3% -> 1% of each run, Pallas kernels for 6% -> 9%
where the time goes in v3:
time: 201 us; the launch traced here: 199 us
  starting transfers between devices  65.2 us (32%)
  blocking collectives  60.2 us (30%)
  Pallas kernels  23.5 us (12%)
  local copies, waits for them, and re-layouts  23 us (11%)
  between operations  13.9 us (7%)
  waiting for transfers between devices  12 us (6%)
    ppermute x6, starting transfers between devices, swap(): return lax.ppermute(value, 'c', [(0, 1), (1, 0)])  31.6 us
    all_to_all x1, blocking collectives, shards(): far = lax.all_to_all(pay, 'a', 0, 0, tiled=True)  30.1 us
    unnamed x66, local copies, waits for them, and re-layouts  21.6 us
    ppermute x4, starting transfers between devices, shards(): spread.append(lax.ppermute(weight, ('y', 'x'), perm))  17.3 us
    pallas_call x8, Pallas kernels, call(): pl.pallas_call(run, out_shape=[jax.ShapeDtypeStruct(*o) for o in outs], i...  17.3 us
    all_to_all x1, blocking collectives, shards(): far = lax.all_to_all(far, 'b', 0, 0, tiled=True)  11.8 us
    all_to_all x1, blocking collectives, shards(): near = lax.all_to_all(pay, 'b', 0, 0, tiled=True)  11.1 us
    ppermute x3, starting transfers between devices, shards(): lax.ppermute(normed, 'x', [(i, (i + j) % 4) for i in range(4)])  9.22 us
  transfers between devices with their start and end apart: 16, of which 4 were waited for; matrix products, arithmetic and copies ran while one was open for 1% of the time, Pallas kernels for 9%

profile of v3, /device:TPU:1, one launch (start us, length us, event | category | flops | bytes accessed | tf_op | source)
XLA Modules:
  0.0 199.1 jit_solution(6915094395319790535)
XLA Ops:
  8.2 5.5 %collective-permute-start.1 = (bf16[32,1024]{1,0:T(8,128)(2,1)}, bf16[32,1024]{1,0:T(8,128)(2,1)S(1)}, u32[]{:S(2)}, u32[]{:S(2)}) collective-permute-start(bf16[32,1024]{1,0:T(8,128)(2,1)} %param.15), channel_id=1, source_target_pairs={{0,128},{1,256},{2,384},{3,0},{128,129},{129,257},{130,385},{131,1... | collective-permute-start | bytes 196616 | tf_op jit(solution)/shard_map/ppermute | solution.py:290
  13.7 6.3 %collective-permute-start.2 = (bf16[32,1024]{1,0:T(8,128)(2,1)}, bf16[32,1024]{1,0:T(8,128)(2,1)S(1)}, u32[]{:S(2)}, u32[]{:S(2)}) collective-permute-start(bf16[32,1024]{1,0:T(8,128)(2,1)} %param.15), channel_id=1, source_target_pairs={{0,256},{1,384},{2,0},{3,128},{128,257},{129,385},{130,1},{131,129... | collective-permute-start | bytes 196616 | tf_op jit(solution)/shard_map/ppermute | solution.py:290
  20.0 3.8 %collective-permute-start.3 = (bf16[32,1024]{1,0:T(8,128)(2,1)}, bf16[32,1024]{1,0:T(8,128)(2,1)S(1)}, u32[]{:S(2)}, u32[]{:S(2)}) collective-permute-start(bf16[32,1024]{1,0:T(8,128)(2,1)} %param.15), channel_id=1, source_target_pairs={{0,384},{1,0},{2,128},{3,256},{128,385},{129,1},{130,129},{131,257... | collective-permute-start | bytes 196616 | tf_op jit(solution)/shard_map/ppermute | solution.py:290
  31.4 3.5 %collective-permute-start.4 = (bf16[1072,512]{1,0:T(8,128)(2,1)}, bf16[1072,512]{1,0:T(8,128)(2,1)S(1)}, u32[]{:S(2)}, u32[]{:S(2)}) collective-permute-start(bf16[1072,512]{1,0:T(8,128)(2,1)} %shard_map.82), channel_id=1, source_target_pairs={{0,4},{4,0},{1,5},{5,1},{2,6},{6,2},{3,7},{7,3},{8,12},{12,8},{9,1... | collective-permute-start | bytes 3293192 | tf_op jit(solution)/shard_map/ppermute | solution.py:17
  39.3 11.1 %all_to_all.30.refs_1_ = bf16[4,144,128]{2,1,0:T(8,128)(2,1)S(1)} all-to-all(bf16[4,144,128]{2,1,0:T(8,128)(2,1)S(1)} %get-tuple-element.20), channel_id=1, replica_groups=mesh['y'=4,'a'=4,'b'=4,'c'=2,'x'=4] {'b'}, dimensions={0} | all-to-all | bytes 294912 | tf_op jit(solution)/shard_map/all_to_all | solution.py:312
  51.0 30.1 %all_to_all.31.refs_1_ = bf16[4,144,128]{2,1,0:T(8,128)(2,1)} all-to-all(bf16[4,144,128]{2,1,0:T(8,128)(2,1)S(1)} %get-tuple-element.22), channel_id=1, replica_groups=mesh['y'=4,'a'=4,'b'=4,'c'=2,'x'=4] {'a'}, dimensions={0} | all-to-all | bytes 294912 | tf_op jit(solution)/shard_map/all_to_all | solution.py:315
  81.1 3.5 %all-to-all-start.1 = ((bf16[4,144,256]{2,1,0:T(8,128)(2,1)}), bf16[4,144,256]{2,1,0:T(8,128)(2,1)S(1)}, u32[]{:S(2)}, u32[]{:S(2)}) async-start(bf16[4,144,256]{2,1,0:T(8,128)(2,1)} %copy-done.15), calls=%async_computation.1 | async-start | bytes 589824 | tf_op jit(solution)/shard_map/all_to_all | solution.py:314
  86.8 4.4 %shard_map.84 = (f32[512,512]{1,0:T(8,128)S(1)}, f32[512,24]{1,0:T(8,128)S(1)}) custom-call(s32[4]{0:T(128)S(1)} %copy-done.26, bf16[256,1024]{1,0:T(8,128)(2,1)S(1)} %copy-done.4, bf16[256,1024]{1,0:T(8,128)(2,1)S(1)} %copy-done.6, bf16[256,1024]{1,0:T(8,128)(2,1)S(1)} %copy-done.8, bf16[1072,512]{1,0:T(8,128)(2,1)S(1)} %collective-permute-done.4.refs_3_.refs_4_, ...), custom_call_target="tpu_custom_call" | custom-call | flops 1000000 | bytes 1000000 | tf_op jit(solution)/shard_map/pallas_call | solution.py:52
  92.9 2.8 %all-to-all-done.1.refs_2_.refs_7_ = bf16[4,144,256]{2,1,0:T(8,128)(2,1)S(1)} async-done(((bf16[4,144,256]{2,1,0:T(8,128)(2,1)}), bf16[4,144,256]{2,1,0:T(8,128)(2,1)S(1)}, u32[]{:S(2)}, u32[]{:S(2)}) %all-to-all-start.1) | async-done | bytes 294944 | tf_op jit(solution)/shard_map/all_to_all | solution.py:314
  99.0 7.3 %all_to_all.32.refs_1_ = bf16[4,144,128]{2,1,0:T(8,128)(2,1)S(1)} all-to-all(bf16[4,144,128]{2,1,0:T(8,128)(2,1)S(1)} %get-tuple-element.24), channel_id=1, replica_groups=mesh['y'=4,'a'=4,'b'=4,'c'=2,'x'=4] {'y'}, dimensions={0} | all-to-all | bytes 294912 | tf_op jit(solution)/shard_map/all_to_all | solution.py:323
  106.3 11.8 %all_to_all.33.refs_3_.refs_8_ = bf16[4,128,256]{2,1,0:T(8,128)(2,1)S(1)} all-to-all(bf16[4,128,256]{2,1,0:T(8,128)(2,1)S(1)} %get-tuple-element.23), channel_id=1, replica_groups=mesh['y'=4,'a'=4,'b'=4,'c'=2,'x'=4] {'b'}, dimensions={0} | all-to-all | bytes 524288 | tf_op jit(solution)/shard_map/all_to_all | solution.py:322
  119.4 3.5 %all-to-all-start.5 = ((bf16[4,128,256]{2,1,0:T(8,128)(2,1)}), bf16[4,128,256]{2,1,0:T(8,128)(2,1)S(1)}, u32[]{:S(2)}, u32[]{:S(2)}) async-start(bf16[4,128,256]{2,1,0:T(8,128)(2,1)} %shard_map.87), calls=%async_computation.5 | async-start | bytes 524288 | tf_op jit(solution)/shard_map/all_to_all | solution.py:325
  123.6 7.2 %all-to-all-done.5.refs_9_ = bf16[4,128,256]{2,1,0:T(8,128)(2,1)S(1)} async-done(((bf16[4,128,256]{2,1,0:T(8,128)(2,1)}), bf16[4,128,256]{2,1,0:T(8,128)(2,1)S(1)}, u32[]{:S(2)}, u32[]{:S(2)}) %all-to-all-start.5) | async-done | bytes 262176 | tf_op jit(solution)/shard_map/all_to_all | solution.py:325
  133.6 5.2 %shard_map.88 = bf16[512,512]{1,0:T(8,128)(2,1)S(1)} custom-call(s32[4]{0:T(128)S(1)} %copy-done.28, bf16[256,1024]{1,0:T(8,128)(2,1)S(1)} %copy-done.8, bf16[256,1024]{1,0:T(8,128)(2,1)S(1)} %copy-done.13, bf16[1072,512]{1,0:T(8,128)(2,1)S(1)} %collective-permute-done.4.refs_3_.refs_4_, bf16[1,1024]{1,0:T(2,128)(2,1)S(1)} %broadcast_in_dim.3.refs_4_, ...), custom_call_target="tpu_custom_call" | custom-call | flops 1000000 | bytes 1000000 | tf_op jit(solution)/shard_map/pallas_call | solution.py:52
  138.8 3.0 %collective-permute-start.6 = (bf16[512,512]{1,0:T(8,128)(2,1)S(1)}, bf16[512,512]{1,0:T(8,128)(2,1)S(1)}, u32[]{:S(2)}, u32[]{:S(2)}) collective-permute-start(bf16[512,512]{1,0:T(8,128)(2,1)S(1)} %shard_map.88), channel_id=1, source_target_pairs={{0,1},{1,2},{2,3},{3,0},{4,5},{5,6},{6,7},{7,4},{8,9},{9,10},{10,1... | collective-permute-start | bytes 1572872 | tf_op jit(solution)/shard_map/ppermute | solution.py:333
  143.7 4.3 %collective-permute-start.10 = (bf16[512,512]{1,0:T(8,128)(2,1)S(1)}, bf16[512,512]{1,0:T(8,128)(2,1)S(1)}, u32[]{:S(2)}, u32[]{:S(2)}) collective-permute-start(bf16[512,512]{1,0:T(8,128)(2,1)S(1)} %shard_map.88), channel_id=1, source_target_pairs={{0,3},{1,0},{2,1},{3,2},{4,7},{5,4},{6,5},{7,6},{8,11},{9,8},{10,9... | collective-permute-start | bytes 1572872 | tf_op jit(solution)/shard_map/ppermute | solution.py:333
  148.0 7.9 %collective-permute-start.5 = (bf16[512,512]{1,0:T(8,128)(2,1)S(1)}, bf16[512,512]{1,0:T(8,128)(2,1)S(1)}, u32[]{:S(2)}, u32[]{:S(2)}) collective-permute-start(bf16[512,512]{1,0:T(8,128)(2,1)S(1)} %shard_map.88), channel_id=1, source_target_pairs={{0,4},{4,0},{1,5},{5,1},{2,6},{6,2},{3,7},{7,3},{8,12},{12,8},{9,1... | collective-permute-start | bytes 1572872 | tf_op jit(solution)/shard_map/ppermute | solution.py:17
  155.9 13.4 %collective-permute-start.7 = (bf16[512,512]{1,0:T(8,128)(2,1)S(1)}, bf16[512,512]{1,0:T(8,128)(2,1)S(1)}, u32[]{:S(2)}, u32[]{:S(2)}) collective-permute-start(bf16[512,512]{1,0:T(8,128)(2,1)S(1)} %collective-permute-done.6), channel_id=1, source_target_pairs={{0,4},{4,0},{1,5},{5,1},{2,6},{6,2},{3,7},{7,3},{8,12},{12,8},{9,1... | collective-permute-start | bytes 1572872 | tf_op jit(solution)/shard_map/ppermute | solution.py:17
  171.3 2.6 %collective-permute-start.11 = (bf16[512,512]{1,0:T(8,128)(2,1)S(1)}, bf16[512,512]{1,0:T(8,128)(2,1)S(1)}, u32[]{:S(2)}, u32[]{:S(2)}) collective-permute-start(bf16[512,512]{1,0:T(8,128)(2,1)S(1)} %collective-permute-done.10), channel_id=1, source_target_pairs={{0,4},{4,0},{1,5},{5,1},{2,6},{6,2},{3,7},{7,3},{8,12},{12,8},{9,1... | collective-permute-start | bytes 1572872 | tf_op jit(solution)/shard_map/ppermute | solution.py:17
  177.6 2.2 %copy-done.1 = bf16[512,4096]{1,0:T(8,128)(2,1)S(1)} copy-done((bf16[512,4096]{1,0:T(8,128)(2,1)S(1)}, bf16[512,4096]{1,0:T(8,128)(2,1)}, u32[]{:S(2)}) %copy-start.1) | copy-done | bytes 4194328
  179.8 2.2 %copy-done.2 = bf16[512,4096]{1,0:T(8,128)(2,1)S(1)} copy-done((bf16[512,4096]{1,0:T(8,128)(2,1)S(1)}, bf16[512,4096]{1,0:T(8,128)(2,1)}, u32[]{:S(2)}) %copy-start.2) | copy-done | bytes 4194328
  181.9 3.1 %shard_map.90 = bf16[256,512]{1,0:T(8,128)(2,1)S(1)} custom-call(s32[4]{0:T(128)S(1)} %copy-done.29, bf16[512,4096]{1,0:T(8,128)(2,1)S(1)} %copy-done.1, bf16[512,4096]{1,0:T(8,128)(2,1)S(1)} %copy-done.2), custom_call_target="tpu_custom_call" | custom-call | flops 1073741824 | bytes 6291456 | tf_op jit(solution)/shard_map/pallas_call | solution.py:251
  185.1 2.3 %collective-permute-start.12 = (bf16[256,512]{1,0:T(8,128)(2,1)S(1)}, bf16[256,512]{1,0:T(8,128)(2,1)S(1)}, u32[]{:S(2)}, u32[]{:S(2)}) collective-permute-start(bf16[256,512]{1,0:T(8,128)(2,1)S(1)} %shard_map.90), channel_id=1, source_target_pairs={{0,4},{4,0},{1,5},{5,1},{2,6},{6,2},{3,7},{7,3},{8,12},{12,8},{9,1... | collective-permute-start | bytes 786440 | tf_op jit(solution)/shard_map/ppermute | solution.py:17
  187.4 3.1 %shard_map.89.refs_1_ = bf16[256,512]{1,0:T(8,128)(2,1)S(1)} custom-call(s32[4]{0:T(128)S(1)} %copy-done.29, bf16[512,4096]{1,0:T(8,128)(2,1)S(1)} %copy-done.1, bf16[512,4096]{1,0:T(8,128)(2,1)S(1)} %copy-done.2), custom_call_target="tpu_custom_call" | custom-call | flops 1073741824 | bytes 6291456 | tf_op jit(solution)/shard_map/pallas_call | solution.py:251
  (101 shorter events, 35.1 us)
Async XLA Ops:
  6.5 30.9 %copy-start.23 = (f32[8,256]{1,0:T(8,128)S(1)}, f32[8,256]{1,0:T(8,128)}, u32[]{:S(2)}) copy-start(f32[8,256]{1,0:T(8,128)} %refs_5_.3) | copy-start | bytes 24580
  6.5 171.0 %all-gather.2.cloned.1.call-start = ((), (), s32[]{:S(2)}) async-start(), calls=%async_computation.6 | async-start | bytes 4456448 | tf_op jit(solution)/shard_map/all_gather | solution.py:300
  6.5 28.4 %collective-permute-start = (bf16[32,1024]{1,0:T(8,128)(2,1)}, bf16[32,1024]{1,0:T(8,128)(2,1)S(1)}, u32[]{:S(2)}, u32[]{:S(2)}) collective-permute-start(bf16[32,1024]{1,0:T(8,128)(2,1)} %param.15), channel_id=1, source_target_pairs={{0,0},{1,128},{2,256},{3,384},{128,1},{129,129},{130,257},{131,385... | collective-permute-start | bytes 196616 | tf_op jit(solution)/shard_map/ppermute | solution.py:290
  8.2 26.8 %collective-permute-start.1 = (bf16[32,1024]{1,0:T(8,128)(2,1)}, bf16[32,1024]{1,0:T(8,128)(2,1)S(1)}, u32[]{:S(2)}, u32[]{:S(2)}) collective-permute-start(bf16[32,1024]{1,0:T(8,128)(2,1)} %param.15), channel_id=1, source_target_pairs={{0,128},{1,256},{2,384},{3,0},{128,129},{129,257},{130,385},{131,1... | collective-permute-start | bytes 196616 | tf_op jit(solution)/shard_map/ppermute | solution.py:290
  13.7 21.3 %collective-permute-start.2 = (bf16[32,1024]{1,0:T(8,128)(2,1)}, bf16[32,1024]{1,0:T(8,128)(2,1)S(1)}, u32[]{:S(2)}, u32[]{:S(2)}) collective-permute-start(bf16[32,1024]{1,0:T(8,128)(2,1)} %param.15), channel_id=1, source_target_pairs={{0,256},{1,384},{2,0},{3,128},{128,257},{129,385},{130,1},{131,129... | collective-permute-start | bytes 196616 | tf_op jit(solution)/shard_map/ppermute | solution.py:290
  20.0 14.9 %collective-permute-start.3 = (bf16[32,1024]{1,0:T(8,128)(2,1)}, bf16[32,1024]{1,0:T(8,128)(2,1)S(1)}, u32[]{:S(2)}, u32[]{:S(2)}) collective-permute-start(bf16[32,1024]{1,0:T(8,128)(2,1)} %param.15), channel_id=1, source_target_pairs={{0,384},{1,0},{2,128},{3,256},{128,385},{129,1},{130,129},{131,257... | collective-permute-start | bytes 196616 | tf_op jit(solution)/shard_map/ppermute | solution.py:290
  29.7 51.4 %copy-start.25 = (s32[4]{0:T(128)}, s32[4]{0:T(128)S(1)}, u32[]{:S(2)}) copy-start(s32[4]{0:T(128)S(1)} %pad_add_fusion.refs_0_.at) | copy-start | bytes 52
  29.7 7.8 %copy-start.6 = (bf16[256,1024]{1,0:T(8,128)(2,1)S(1)}, bf16[256,1024]{1,0:T(8,128)(2,1)}, u32[]{:S(2)}) copy-start(bf16[256,1024]{1,0:T(8,128)(2,1)} %refs_2_.6) | copy-start | bytes 1572868
  29.7 54.9 %copy-start.8 = (bf16[256,1024]{1,0:T(8,128)(2,1)S(1)}, bf16[256,1024]{1,0:T(8,128)(2,1)}, u32[]{:S(2)}) copy-start(bf16[256,1024]{1,0:T(8,128)(2,1)} %refs_1_.7) | copy-start | bytes 1572868
  29.7 54.9 %copy-start.19 = (f32[8,8,256]{2,1,0:T(8,128)S(1)}, f32[8,8,256]{2,1,0:T(8,128)}, u32[]{:S(2)}) copy-start(f32[8,8,256]{2,1,0:T(8,128)} %refs_6_.3) | copy-start | bytes 196612
  31.4 6.1 %collective-permute-start.4 = (bf16[1072,512]{1,0:T(8,128)(2,1)}, bf16[1072,512]{1,0:T(8,128)(2,1)S(1)}, u32[]{:S(2)}, u32[]{:S(2)}) collective-permute-start(bf16[1072,512]{1,0:T(8,128)(2,1)} %shard_map.82), channel_id=1, source_target_pairs={{0,4},{4,0},{1,5},{5,1},{2,6},{6,2},{3,7},{7,3},{8,12},{12,8},{9,1... | collective-permute-start | bytes 3293192 | tf_op jit(solution)/shard_map/ppermute | solution.py:17
  39.3 41.8 %copy-start.20 = (bf16[4,128,128]{2,1,0:T(8,128)(2,1)}, bf16[4,128,128]{2,1,0:T(8,128)(2,1)S(1)}, u32[]{:S(2)}) copy-start(bf16[4,128,128]{2,1,0:T(8,128)(2,1)S(1)} %get-tuple-element.17.refs_7_) | copy-start | bytes 393220
  39.3 91.5 %copy-start.13 = (bf16[256,1024]{1,0:T(8,128)(2,1)S(1)}, bf16[256,1024]{1,0:T(8,128)(2,1)}, u32[]{:S(2)}) copy-start(bf16[256,1024]{1,0:T(8,128)(2,1)} %refs_2_.7) | copy-start | bytes 1572868
  51.0 30.1 %copy-start.15 = (bf16[4,144,256]{2,1,0:T(8,128)(2,1)}, bf16[4,144,256]{2,1,0:T(8,128)(2,1)S(1)}, u32[]{:S(2)}) copy-start(bf16[4,144,256]{2,1,0:T(8,128)(2,1)S(1)} %get-tuple-element.21) | copy-start | bytes 884740
  81.1 14.6 %all-to-all-start.1 = ((bf16[4,144,256]{2,1,0:T(8,128)(2,1)}), bf16[4,144,256]{2,1,0:T(8,128)(2,1)S(1)}, u32[]{:S(2)}, u32[]{:S(2)}) async-start(bf16[4,144,256]{2,1,0:T(8,128)(2,1)} %copy-done.15), calls=%async_computation.1 | async-start | bytes 589824 | tf_op jit(solution)/shard_map/all_to_all | solution.py:314
  119.4 11.4 %all-to-all-start.5 = ((bf16[4,128,256]{2,1,0:T(8,128)(2,1)}), bf16[4,128,256]{2,1,0:T(8,128)(2,1)S(1)}, u32[]{:S(2)}, u32[]{:S(2)}) async-start(bf16[4,128,256]{2,1,0:T(8,128)(2,1)} %shard_map.87), calls=%async_computation.5 | async-start | bytes 524288 | tf_op jit(solution)/shard_map/all_to_all | solution.py:325
  138.8 17.2 %collective-permute-start.6 = (bf16[512,512]{1,0:T(8,128)(2,1)S(1)}, bf16[512,512]{1,0:T(8,128)(2,1)S(1)}, u32[]{:S(2)}, u32[]{:S(2)}) collective-permute-start(bf16[512,512]{1,0:T(8,128)(2,1)S(1)} %shard_map.88), channel_id=1, source_target_pairs={{0,1},{1,2},{2,3},{3,0},{4,5},{5,6},{6,7},{7,4},{8,9},{9,10},{10,1... | collective-permute-start | bytes 1572872 | tf_op jit(solution)/shard_map/ppermute | solution.py:333
  141.8 27.6 %collective-permute-start.8 = (bf16[512,512]{1,0:T(8,128)(2,1)S(1)}, bf16[512,512]{1,0:T(8,128)(2,1)S(1)}, u32[]{:S(2)}, u32[]{:S(2)}) collective-permute-start(bf16[512,512]{1,0:T(8,128)(2,1)S(1)} %shard_map.88), channel_id=1, source_target_pairs={{0,2},{1,3},{2,0},{3,1},{4,6},{5,7},{6,4},{7,5},{8,10},{9,11},{10,... | collective-permute-start | bytes 1572872 | tf_op jit(solution)/shard_map/ppermute | solution.py:333
  143.7 27.6 %collective-permute-start.10 = (bf16[512,512]{1,0:T(8,128)(2,1)S(1)}, bf16[512,512]{1,0:T(8,128)(2,1)S(1)}, u32[]{:S(2)}, u32[]{:S(2)}) collective-permute-start(bf16[512,512]{1,0:T(8,128)(2,1)S(1)} %shard_map.88), channel_id=1, source_target_pairs={{0,3},{1,0},{2,1},{3,2},{4,7},{5,4},{6,5},{7,6},{8,11},{9,8},{10,9... | collective-permute-start | bytes 1572872 | tf_op jit(solution)/shard_map/ppermute | solution.py:333
  148.0 25.9 %collective-permute-start.5 = (bf16[512,512]{1,0:T(8,128)(2,1)S(1)}, bf16[512,512]{1,0:T(8,128)(2,1)S(1)}, u32[]{:S(2)}, u32[]{:S(2)}) collective-permute-start(bf16[512,512]{1,0:T(8,128)(2,1)S(1)} %shard_map.88), channel_id=1, source_target_pairs={{0,4},{4,0},{1,5},{5,1},{2,6},{6,2},{3,7},{7,3},{8,12},{12,8},{9,1... | collective-permute-start | bytes 1572872 | tf_op jit(solution)/shard_map/ppermute | solution.py:17
  155.9 18.3 %collective-permute-start.7 = (bf16[512,512]{1,0:T(8,128)(2,1)S(1)}, bf16[512,512]{1,0:T(8,128)(2,1)S(1)}, u32[]{:S(2)}, u32[]{:S(2)}) collective-permute-start(bf16[512,512]{1,0:T(8,128)(2,1)S(1)} %collective-permute-done.6), channel_id=1, source_target_pairs={{0,4},{4,0},{1,5},{5,1},{2,6},{6,2},{3,7},{7,3},{8,12},{12,8},{9,1... | collective-permute-start | bytes 1572872 | tf_op jit(solution)/shard_map/ppermute | solution.py:17
  169.4 5.2 %collective-permute-start.9 = (bf16[512,512]{1,0:T(8,128)(2,1)S(1)}, bf16[512,512]{1,0:T(8,128)(2,1)S(1)}, u32[]{:S(2)}, u32[]{:S(2)}) collective-permute-start(bf16[512,512]{1,0:T(8,128)(2,1)S(1)} %collective-permute-done.8), channel_id=1, source_target_pairs={{0,4},{4,0},{1,5},{5,1},{2,6},{6,2},{3,7},{7,3},{8,12},{12,8},{9,1... | collective-permute-start | bytes 1572872 | tf_op jit(solution)/shard_map/ppermute | solution.py:17
  171.3 3.9 %collective-permute-start.11 = (bf16[512,512]{1,0:T(8,128)(2,1)S(1)}, bf16[512,512]{1,0:T(8,128)(2,1)S(1)}, u32[]{:S(2)}, u32[]{:S(2)}) collective-permute-start(bf16[512,512]{1,0:T(8,128)(2,1)S(1)} %collective-permute-done.10), channel_id=1, source_target_pairs={{0,4},{4,0},{1,5},{5,1},{2,6},{6,2},{3,7},{7,3},{8,12},{12,8},{9,1... | collective-permute-start | bytes 1572872 | tf_op jit(solution)/shard_map/ppermute | solution.py:17
  185.1 5.4 %collective-permute-start.12 = (bf16[256,512]{1,0:T(8,128)(2,1)S(1)}, bf16[256,512]{1,0:T(8,128)(2,1)S(1)}, u32[]{:S(2)}, u32[]{:S(2)}) collective-permute-start(bf16[256,512]{1,0:T(8,128)(2,1)S(1)} %shard_map.90), channel_id=1, source_target_pairs={{0,4},{4,0},{1,5},{5,1},{2,6},{6,2},{3,7},{7,3},{8,12},{12,8},{9,1... | collective-permute-start | bytes 786440 | tf_op jit(solution)/shard_map/ppermute | solution.py:17
  (22 other events, 32.5 us)
Sparse Core Ops, SparseCore 0:
  37.6 86.9 all-gather.1

commit v4 on v3

v4 whole, which is shorter than its diff:
```python
import functools

import jax
import jax.numpy as jnp
from jax import lax
from jax.experimental import pallas as pl
from jax.experimental.pallas import tpu as pltpu
from jax.sharding import Mesh, PartitionSpec as P

BF = jnp.bfloat16
F32 = jnp.float32
SEQ = ("y", "a", "b", "c")
NT = (((1,), (1,)), ((), ()))
TN = (((0,), (0,)), ((), ()))
LOGS = 1024


def swap(value):
    return lax.ppermute(value, "c", [(0, 1), (1, 0)])


def flip(value, axis, mask):
    return lax.ppermute(value, axis, [(i, i ^ mask) for i in range(4)])


def flat(place):
    y, x, core = place // 8, place // 2 % 4, place % 2
    return (y * 2 + core) * 4 + x


def dot(left, right, dims=(((1,), (0,)), ((), ()))):
    return lax.dot_general(left, right, dims, preferred_element_type=F32)


def exact(left, right, dims):
    return lax.dot_general(
        left, right, dims, precision=lax.Precision.HIGHEST, preferred_element_type=F32
    )


def tail(log):
    high = log.astype(BF).astype(F32)
    middle = (log - high).astype(BF).astype(F32)
    low = log - high - middle
    row = lax.broadcasted_iota(jnp.int32, (16, 128), 0)
    return jnp.where(
        row == 0, high, jnp.where(row == 1, middle, jnp.where(row == 2, low, 0.0))
    ).astype(BF)


def untail(tile):
    return jnp.sum(tile.astype(F32), axis=0, keepdims=True)


def call(body, outs, args, unread=(), scratch=(), hbm=()):
    specs = [pl.BlockSpec(memory_space=pltpu.SMEM)]
    specs += [
        pl.BlockSpec(memory_space=pl.ANY if i in hbm else pltpu.VMEM)
        for i in range(1, len(args))
    ]
    specs += [pl.BlockSpec(memory_space=pl.ANY)] * len(unread)

    def run(*refs):
        body(*refs[: len(args)], *refs[len(args) + len(unread) :])

    return pl.pallas_call(
        run,
        out_shape=[jax.ShapeDtypeStruct(*o) for o in outs],
        in_specs=specs,
        out_specs=[pl.BlockSpec(memory_space=pltpu.VMEM)] * len(outs),
        scratch_shapes=list(scratch),
        compiler_params=pltpu.CompilerParams(vmem_limit_bytes=32 * 2**20),
        cost_estimate=pl.CostEstimate(flops=10**6, bytes_accessed=10**6, transcendentals=0),
    )(*args, *unread)


def pack_body(
    at, keys, values, queries, gates, decay, mix, weight,
    keep, send, w_same, w_other, small, levels, wide, sems,
):
    core = at[0]
    mine = pl.ds(pl.multiple_of(core * 512, 512), 512)
    theirs = pl.ds(pl.multiple_of((1 - core) * 512, 512), 512)
    copies = [
        pltpu.make_async_copy(decay, small, sems.at[0]),
        pltpu.make_async_copy(mix, levels, sems.at[1]),
        pltpu.make_async_copy(weight, wide, sems.at[2]),
    ]
    for i, ref in enumerate((keys, values, queries, gates)):
        rows = pl.ds(i * 256, 256)
        for out, cols, n in ((send, theirs, 3), (keep, mine, 7)):
            copies.append(pltpu.make_async_copy(ref.at[:, cols], out.at[rows, :], sems.at[n + i]))
    for copy in copies:
        copy.start()
    for copy in copies[:3]:
        copy.wait()
    w_same[...] = wide[:, mine]
    w_other[...] = wide[:, theirs]
    for out, low in ((keep, core == 0), (send, core == 1)):
        logs = [jnp.where(low, small[0:4], small[4:8])]
        logs += [jnp.where(low, levels[l, 0:4], levels[l, 4:8]) for l in range(8)]
        logs = jnp.concatenate(logs + [jnp.zeros((12, 256), F32)], axis=0)
        high = logs.astype(BF)
        out[LOGS:, 0:256] = high
        out[LOGS:, 256:512] = (logs - high.astype(F32)).astype(BF)
    for copy in copies[3:]:
        copy.wait()


def logs_of(block):
    tile = block[LOGS:, :].astype(F32)
    return tile[:, 0:256] + tile[:, 256:512]


def ends_body(at, keep, got, pay, first):
    core = at[0]
    logs = jnp.concatenate([logs_of(keep)[0:4], logs_of(got)[0:4]], axis=0)
    after = (
        lax.broadcasted_iota(jnp.int32, (256, 256), 1)
        > lax.broadcasted_iota(jnp.int32, (256, 256), 0)
    ).astype(F32)
    scale = jnp.exp(exact(after, logs, NT))
    total = jnp.sum(logs, axis=1, keepdims=True)
    for h in range(4):
        cols = slice(h * 128, h * 128 + 128)
        end = []
        for i, ref in enumerate((keep, got)):
            scaled = ref[0:256, cols].astype(F32) * scale[:, 4 * i + h : 4 * i + h + 1]
            end.append(dot(scaled.astype(BF), ref[256:512, cols], TN))
        own_log, got_log = total[h : h + 1], total[4 + h : 5 + h]
        own_later = jnp.exp(jnp.where(core == 0, got_log, 0.0))
        got_later = jnp.exp(jnp.where(core == 0, 0.0, own_log))
        pay[h, 0:128, :] = (end[0] * own_later + end[1] * got_later).astype(BF)
        pay[h, 128:144, :] = tail(own_log + got_log)
        first[h, :, :] = jnp.where(core == 0, end[0], end[1]).astype(BF)


def merge(got):
    s = [got[i, 0:128, :].astype(F32) for i in range(4)]
    t = [untail(got[i, 128:144, :]) for i in range(4)]
    pair = s[0] * jnp.exp(t[1]) + s[1]
    return s, t, pair


def send_whole(s, t, pair, pay):
    state = (pair * jnp.exp(t[2] + t[3]) + s[2] * jnp.exp(t[3]) + s[3]).astype(BF)
    log = tail(t[0] + t[1] + t[2] + t[3])
    for i in range(4):
        pay[i, 0:128, :] = state
        pay[i, 128:144, :] = log


def lower_states(s, t, pair, at):
    odd, upper = at % 2 == 1, at >= 2
    one = jnp.where(odd, jnp.where(upper, s[2], s[0]), 0.0)
    step = jnp.where(odd, jnp.where(upper, t[2], t[0]), 0.0)
    two = jnp.where(upper, pair * jnp.exp(step), 0.0)
    before = sum(jnp.where(at > i, t[i], 0.0) for i in range(3))
    return one, two, before


def near_body(at, got, pay, *messages):
    s, t, pair = merge(got)
    send_whole(s, t, pair, pay)
    for k in range(4):
        one, two, before = lower_states(s, t, pair, at[1] ^ k)
        messages[k][0:128, 0:128] = one.astype(BF)
        messages[k][0:128, 128:256] = two.astype(BF)
        messages[k][128:144, 0:128] = tail(before)
        messages[k][128:144, 128:256] = jnp.zeros((16, 128), BF)


def far_body(at, got, pay, message, before_out):
    s, t, pair = merge(got)
    send_whole(s, t, pair, pay)
    one, two, before = lower_states(s, t, pair, at[2])
    message[:, 0:128] = one.astype(BF)
    message[:, 128:256] = two.astype(BF)
    before_out[...] = jnp.broadcast_to(before, (8, 128))


def last_body(at, got, far, before, message):
    s, t, pair = merge(got)
    one, two, _ = lower_states(s, t, pair, at[3])
    earlier = jnp.exp(before[0:1, :])
    one, two = (one * earlier).astype(BF), (two * earlier).astype(BF)
    for i in range(4):
        message[i, :, 0:256] = far[...]
        message[i, :, 256:384] = one
        message[i, :, 384:512] = two


def place(s, core):
    at = core if s == 0 else 1 - core
    return at, pl.ds(pl.multiple_of(at * 256, 256), 256)


def own_body(at, keep, got, first, n0, n1, n2, n3, mixture, coef, near):
    core = at[0]
    for k, n in enumerate((n0, n1, n2, n3)):
        near[at[1] ^ k] = n[...]
    rows = lax.broadcasted_iota(jnp.int32, (256, 256), 0)
    cols = lax.broadcasted_iota(jnp.int32, (256, 256), 1)
    lower = rows >= cols
    upto = lower.astype(F32)
    both = (logs_of(keep), logs_of(got))
    for s, ref in enumerate((keep, got)):
        second, here = place(s, core)
        logs = both[s]
        at_row = exact(logs[0:8], upto, NT)
        at_col = exact(upto, logs[0:8], NT)
        level = logs.T
        first_log = jnp.sum(both[1 - s][0:4], axis=1, keepdims=True)
        first_log = jnp.where(second == 1, first_log, 0.0)
        for h in range(4):
            hc = slice(h * 128, h * 128 + 128)
            q, kb, v = ref[512:768, hc], ref[0:256, hc], ref[256:512, hc]
            local = at_col[:, h : h + 1]
            gap = jnp.where(lower, local - at_row[h : h + 1, :], -1e30)
            weights = (dot(q, kb, NT) * jnp.exp(gap)).astype(BF)
            m = [level[:, 4 + 4 * l + h : 5 + 4 * l + h] for l in range(8)]
            total = dot(weights, v) * m[0]
            start = jnp.exp(local)
            total += dot(q, first[h]) * jnp.where(second == 1, start * m[1], 0.0)
            start = start * jnp.exp(first_log[h : h + 1])
            read = dot(q, near[h, 0:128, :])
            total += read[:, 0:128] * (start * m[2]) + read[:, 128:256] * (start * m[3])
            mixture[here, hc] = total
            start = start * jnp.exp(untail(near[h, 128:144, 0:128])[:, 0:1])
            for l in range(4, 8):
                coef[here, 4 * h + l - 4 : 4 * h + l - 3] = start * m[l]


def norm_body(at, keep, got, gain, mixture, coef, last, normed):
    core = at[0]
    for s, ref in enumerate((keep, got)):
        _, here = place(s, core)
        for h in range(4):
            mine = pl.ds(pl.multiple_of(core * 512 + h * 128, 128), 128)
            hc = slice(h * 128, h * 128 + 128)
            q, z = ref[512:768, hc], ref[768:1024, hc].astype(F32)
            total = mixture[here, hc]
            for l in range(0, 4, 2):
                read = dot(q, last[h, :, l * 128 : l * 128 + 256])
                total += read[:, 0:128] * coef[here, 4 * h + l : 4 * h + l + 1]
                total += read[:, 128:256] * coef[here, 4 * h + l + 1 : 4 * h + l + 2]
            gated = total * (z / (1.0 + jnp.exp(-z)))
            size = lax.rsqrt(jnp.mean(gated * gated, axis=1, keepdims=True) + 1e-05)
            normed[here, hc] = (gated * size * gain[:, mine].astype(F32)).astype(BF)


def project_body(other, at, b0, b1, b2, b3, right, out, total):
    step = pl.program_id(0)
    row = (1 - at[0]) if other else at[0]
    rows = pl.ds(pl.multiple_of(row * 256, 256), 256)
    for j, block in enumerate((b0, b1, b2, b3)):

        @pl.when(step == j)
        def _():
            part = dot(block[rows, :], right[...].reshape(1024, 512), NT)
            if j == 0:
                total[...] = part
            elif j < 3:
                total[...] += part
            else:
                out[...] = (total[...] + part).astype(out.dtype)


def project(at, blocks, right, other):
    whole_block = pl.BlockSpec((512, 512), lambda k, at: (0, 0))
    return pl.pallas_call(
        functools.partial(project_body, other),
        out_shape=jax.ShapeDtypeStruct((256, 1024), BF if other else F32),
        grid_spec=pltpu.PrefetchScalarGridSpec(
            num_scalar_prefetch=1,
            grid=(4,),
            in_specs=[whole_block] * 4
            + [pl.BlockSpec((16, 1, 64, 512), lambda k, at: (0, (at[4] + 4 - k) % 4, 0, 0))],
            out_specs=pl.BlockSpec((256, 1024), lambda k, at: (0, 0)),
            scratch_shapes=[pltpu.VMEM((256, 1024), F32)],
        ),
        compiler_params=pltpu.CompilerParams(vmem_limit_bytes=32 * 2**20),
        cost_estimate=pl.CostEstimate(
            flops=2**30, bytes_accessed=6 * 2**20, transcendentals=0
        ),
    )(at, *blocks, right)


def shards(values, keys, queries, gates, log_decay, level_mix, norm_gain, weight):
    y, a, b, c, x = (lax.axis_index(n) for n in ("y", "a", "b", "c", "x"))
    at = jnp.stack([c, b, a, y, x]).astype(jnp.int32)
    block = ((LOGS + 48, 512), BF)
    keep, send, w_same, w_other = call(
        pack_body,
        [block, block, ((32, 512), BF), ((32, 512), BF)],
        (at, keys, values, queries, gates, log_decay, level_mix, weight),
        scratch=[
            pltpu.VMEM((8, 256), F32),
            pltpu.VMEM((8, 8, 256), F32),
            pltpu.VMEM((32, 1024), BF),
            pltpu.SemaphoreType.DMA((11,)),
        ],
        hbm=range(1, 8),
    )
    turned = []
    for other, part in ((0, w_same), (1, w_other)):
        perm = [
            ((s * 4 + f) * 2 + k, (f * 4 + s) * 2 + (k ^ other))
            for s in range(4)
            for f in range(4)
            for k in range(2)
        ]
        perm = [(flat(p), flat(q)) for p, q in perm]
        turned.append(lax.ppermute(part, ("y", "c", "x"), perm))
    got = swap(send)
    first_rows = jnp.where(c == 0, turned[0], turned[1])
    later_rows = jnp.where(c == 0, turned[1], turned[0])
    mine = jnp.concatenate([first_rows, later_rows])
    mine = jnp.broadcast_to(mine[None], (4, 64, 512))
    mine = lax.all_to_all(mine, "y", 0, 0, tiled=True)
    gathered = lax.all_gather(mine, ("a", "b"))

    pay, first = call(
        ends_body, [((4, 144, 128), BF), ((4, 128, 128), BF)], (at, keep, got)
    )
    near = lax.all_to_all(pay, "b", 0, 0, tiled=True)
    pay, *near = call(near_body, [((4, 144, 128), BF)] + [((144, 256), BF)] * 4, (at, near))
    far = lax.all_to_all(pay, "a", 0, 0, tiled=True)
    near = near[:1] + [flip(near[k], "b", k) for k in (1, 2, 3)]
    mixture, coef = call(
        own_body,
        [((512, 512), F32), ((512, 16), F32)],
        (at, keep, got, first, *near),
        scratch=[pltpu.VMEM((4, 144, 256), BF)],
    )
    pay, far, before = call(
        far_body,
        [((4, 144, 128), BF), ((128, 256), BF), ((8, 128), F32)],
        (at, far),
        unread=(mixture,),
    )
    last = lax.all_to_all(pay, "y", 0, 0, tiled=True)
    (last,) = call(last_body, [((4, 128, 512), BF)], (at, last, far, before))
    last = lax.all_to_all(last, "b", 0, 0, tiled=True)
    (normed,) = call(
        norm_body,
        [((512, 512), BF)],
        (at, keep, got, norm_gain[None], mixture, coef, last),
    )

    blocks = [normed] + [
        lax.ppermute(normed, "x", [(i, (i + j) % 4) for i in range(4)]) for j in (1, 2, 3)
    ]
    theirs = swap(project(at, blocks, gathered, True))
    own = project(at, blocks, gathered, False)
    return (own + theirs.astype(F32)).astype(BF)


def solution(mesh):
    fine = Mesh(mesh.devices.reshape(4, 4, 4, 2, 4), SEQ + ("x",))
    return jax.shard_map(
        shards,
        mesh=fine,
        in_specs=(
            P(SEQ, "x"),
            P(SEQ, "x"),
            P(SEQ, "x"),
            P(SEQ, "x"),
            P("x", SEQ),
            P(None, "x", SEQ),
            P("x"),
            P(SEQ, "x"),
        ),
        out_specs=P(SEQ, "x"),
        check_vma=False,
    )
```

time: 201 us -> 183 us (0.910)
  waiting for transfers between devices: 12 us -> 50.8 us
  blocking collectives: 60.2 us -> 32.5 us
  starting transfers between devices: 65.2 us -> 52.2 us
  local copies, waits for them, and re-layouts: 23 us -> 13.1 us
  Pallas kernels: 23.5 us -> 18.8 us
    all_to_all x2 -> x1, blocking collectives: 41.8 us -> 14.1 us  [shards(): mine = lax.all_to_all(mine, 'y', 0, 0, tiled=True)]
    ppermute x6 -> x2, starting transfers between devices: 31.6 us -> 9.02 us  [swap(): return lax.ppermute(value, 'c', [(0, 1), (1, 0)])]
    ppermute x3, waiting for transfers between devices: 0.01 us -> 19.2 us  [shards(): lax.ppermute(normed, 'x', [(i, (i + j) % 4) for i in range(4)])]
    ppermute x4 -> x5, waiting for transfers between devices: 0.01 us -> 11.5 us  [the longest x3 10.7 us: flip(): return lax.ppermute(value, axis, [(i, i ^ mask) for i in range(4)])]
    all_to_all x1, waiting for transfers between devices: 7.2 us -> 17.7 us  [shards(): last = lax.all_to_all(last, 'b', 0, 0, tiled=True)]
    all_to_all x1, starting transfers between devices: 3.47 us -> 12.1 us  [shards(): far = lax.all_to_all(pay, 'a', 0, 0, tiled=True)]
    unnamed x66 -> x32, local copies, waits for them, and re-layouts: 21.6 us -> 13 us
    pallas_call x8 -> x7, Pallas kernels: 17.3 us -> 13 us  [call(): pl.pallas_call(run, out_shape=[jax.ShapeDtypeStruct(*o) for o in outs], i...]
  transfers between devices with their start and end apart: 16 -> 13, of which waited for: 4 -> 9; matrix products, arithmetic and copies ran while one was open for 1% -> 0% of each run, Pallas kernels for 9% -> 8%
where the time goes in v4:
time: 183 us; the launch traced here: 182 us
  starting transfers between devices  52.2 us (29%)
  waiting for transfers between devices  50.8 us (28%)
  blocking collectives  32.5 us (18%)
  Pallas kernels  18.8 us (10%)
  between operations  13.7 us (7%)
  local copies, waits for them, and re-layouts  13.1 us (7%)
    ppermute x3, waiting for transfers between devices, shards(): lax.ppermute(normed, 'x', [(i, (i + j) % 4) for i in range(4)])  19.2 us
    all_to_all x1, waiting for transfers between devices, shards(): last = lax.all_to_all(last, 'b', 0, 0, tiled=True)  17.7 us
    all_to_all x1, blocking collectives, shards(): mine = lax.all_to_all(mine, 'y', 0, 0, tiled=True)  14.1 us
    pallas_call x7, Pallas kernels, call(): pl.pallas_call(run, out_shape=[jax.ShapeDtypeStruct(*o) for o in outs], i...  13 us
    unnamed x32, local copies, waits for them, and re-layouts  13 us
    all_to_all x1, starting transfers between devices, shards(): far = lax.all_to_all(pay, 'a', 0, 0, tiled=True)  12.1 us
    all_to_all x1, blocking collectives, shards(): near = lax.all_to_all(pay, 'b', 0, 0, tiled=True)  10.9 us
    ppermute x3, waiting for transfers between devices, flip(): return lax.ppermute(value, axis, [(i, i ^ mask) for i in range(4)])  10.7 us
  transfers between devices with their start and end apart: 13, of which 9 were waited for; matrix products, arithmetic and copies ran while one was open for 0% of the time, Pallas kernels for 8%

profile of v4, /device:TPU:1, one launch (start us, length us, event | category | flops | bytes accessed | tf_op | source)
XLA Modules:
  0.0 181.9 jit_solution(2718653815522476210)
XLA Ops:
  14.9 8.8 %collective-permute-start.8 = (bf16[32,512]{1,0:T(8,128)(2,1)S(1)}, bf16[32,512]{1,0:T(8,128)(2,1)S(1)}, u32[]{:S(2)}, u32[]{:S(2)}) collective-permute-start(bf16[32,512]{1,0:T(8,128)(2,1)S(1)} %get-tuple-element.36), channel_id=1, source_target_pairs={{0,4},{4,0},{1,132},{5,128},{2,260},{6,256},{3,388},{7,384},{128,5... | collective-permute-start | bytes 98312 | tf_op jit(solution)/shard_map/ppermute | solution.py:314
  24.6 14.1 %all_to_all.25 = bf16[4,64,512]{2,1,0:T(8,128)(2,1)} all-to-all(bf16[4,64,512]{2,1,0:T(8,128)(2,1)S(1)} %broadcast_in_dim.10), channel_id=1, replica_groups=mesh['y'=4,'a'=4,'b'=4,'c'=2,'x'=4] {'y'}, dimensions={0} | all-to-all | bytes 524288 | tf_op jit(solution)/shard_map/all_to_all | solution.py:320
  38.7 4.0 %collective-permute-start = (bf16[1072,512]{1,0:T(8,128)(2,1)S(1)}, bf16[1072,512]{1,0:T(8,128)(2,1)S(1)}, u32[]{:S(2)}, u32[]{:S(2)}) collective-permute-start(bf16[1072,512]{1,0:T(8,128)(2,1)S(1)} %get-tuple-element.22), channel_id=1, source_target_pairs={{0,4},{4,0},{1,5},{5,1},{2,6},{6,2},{3,7},{7,3},{8,12},{12,8},{9,1... | collective-permute-start | bytes 3293192 | tf_op jit(solution)/shard_map/ppermute | solution.py:19
  42.7 2.3 %collective-permute-done.refs_2_ = bf16[1072,512]{1,0:T(8,128)(2,1)S(1)} collective-permute-done((bf16[1072,512]{1,0:T(8,128)(2,1)S(1)}, bf16[1072,512]{1,0:T(8,128)(2,1)S(1)}, u32[]{:S(2)}, u32[]{:S(2)}) %collective-permute-start) | collective-permute-done | bytes 1097760 | tf_op jit(solution)/shard_map/ppermute | solution.py:19
  46.8 10.9 %all_to_all.26.refs_1_ = bf16[4,144,128]{2,1,0:T(8,128)(2,1)S(1)} all-to-all(bf16[4,144,128]{2,1,0:T(8,128)(2,1)S(1)} %get-tuple-element.24), channel_id=1, replica_groups=mesh['y'=4,'a'=4,'b'=4,'c'=2,'x'=4] {'b'}, dimensions={0} | all-to-all | bytes 294912 | tf_op jit(solution)/shard_map/all_to_all | solution.py:326
  59.6 12.1 %all-to-all-start.1 = ((bf16[4,144,128]{2,1,0:T(8,128)(2,1)}), bf16[4,144,128]{2,1,0:T(8,128)(2,1)S(1)}, u32[]{:S(2)}, u32[]{:S(2)}) async-start(bf16[4,144,128]{2,1,0:T(8,128)(2,1)} %get-tuple-element.31), calls=%async_computation.1 | async-start | bytes 294912 | tf_op jit(solution)/shard_map/all_to_all | solution.py:328
  71.7 2.3 %collective-permute-start.1 = (bf16[144,256]{1,0:T(8,128)(2,1)S(1)}, bf16[144,256]{1,0:T(8,128)(2,1)S(1)}, u32[]{:S(2)}, u32[]{:S(2)}) collective-permute-start(bf16[144,256]{1,0:T(8,128)(2,1)S(1)} %get-tuple-element.26), channel_id=1, source_target_pairs={{0,8},{8,0},{16,24},{24,16},{1,9},{9,1},{17,25},{25,17},{2,10},{10... | collective-permute-start | bytes 221192 | tf_op jit(solution)/shard_map/ppermute | solution.py:23
  74.1 4.0 %collective-permute-start.2 = (bf16[144,256]{1,0:T(8,128)(2,1)S(1)}, bf16[144,256]{1,0:T(8,128)(2,1)S(1)}, u32[]{:S(2)}, u32[]{:S(2)}) collective-permute-start(bf16[144,256]{1,0:T(8,128)(2,1)S(1)} %get-tuple-element.27), channel_id=1, source_target_pairs={{0,16},{8,24},{16,0},{24,8},{1,17},{9,25},{17,1},{25,9},{2,18},{10... | collective-permute-start | bytes 221192 | tf_op jit(solution)/shard_map/ppermute | solution.py:23
  78.0 3.0 %collective-permute-start.3 = (bf16[144,256]{1,0:T(8,128)(2,1)S(1)}, bf16[144,256]{1,0:T(8,128)(2,1)S(1)}, u32[]{:S(2)}, u32[]{:S(2)}) collective-permute-start(bf16[144,256]{1,0:T(8,128)(2,1)S(1)} %get-tuple-element.28), channel_id=1, source_target_pairs={{0,24},{8,16},{16,8},{24,0},{1,25},{9,17},{17,9},{25,1},{2,26},{10... | collective-permute-start | bytes 221192 | tf_op jit(solution)/shard_map/ppermute | solution.py:23
  84.2 7.4 %collective-permute-done.3.refs_7_ = bf16[144,256]{1,0:T(8,128)(2,1)S(1)} collective-permute-done((bf16[144,256]{1,0:T(8,128)(2,1)S(1)}, bf16[144,256]{1,0:T(8,128)(2,1)S(1)}, u32[]{:S(2)}, u32[]{:S(2)}) %collective-permute-start.3) | collective-permute-done | bytes 73760 | tf_op jit(solution)/shard_map/ppermute | solution.py:23
  92.6 5.3 %shard_map.85 = (f32[512,512]{1,0:T(8,128)S(1)}, f32[512,16]{1,0:T(8,128)S(1)}) custom-call(s32[5]{0:T(128)S(1)} %stack.23.refs_0_.at, bf16[1072,512]{1,0:T(8,128)(2,1)S(1)} %get-tuple-element.21.refs_1_, bf16[1072,512]{1,0:T(8,128)(2,1)S(1)} %collective-permute-done.refs_2_, bf16[4,128,128]{2,1,0:T(8,128)(2,1)S(1)} %get-tuple-element.23.refs_3_, ...), custom_call_target="tpu_custom_call" | custom-call | flops 1000000 | bytes 1000000 | tf_op jit(solution)/shard_map/pallas_call | solution.py:66
  99.2 7.4 %all_to_all.27.refs_1_ = bf16[4,144,128]{2,1,0:T(8,128)(2,1)S(1)} all-to-all(bf16[4,144,128]{2,1,0:T(8,128)(2,1)S(1)} %get-tuple-element.32), channel_id=1, replica_groups=mesh['y'=4,'a'=4,'b'=4,'c'=2,'x'=4] {'y'}, dimensions={0} | all-to-all | bytes 294912 | tf_op jit(solution)/shard_map/all_to_all | solution.py:342
  108.1 3.5 %all-to-all-start.3 = ((bf16[4,128,512]{2,1,0:T(8,128)(2,1)}), bf16[4,128,512]{2,1,0:T(8,128)(2,1)S(1)}, u32[]{:S(2)}, u32[]{:S(2)}) async-start(bf16[4,128,512]{2,1,0:T(8,128)(2,1)} %copy-done.3), calls=%async_computation.3 | async-start | bytes 1048576 | tf_op jit(solution)/shard_map/all_to_all | solution.py:344
  111.6 17.7 %all-to-all-done.3.refs_6_ = bf16[4,128,512]{2,1,0:T(8,128)(2,1)S(1)} async-done(((bf16[4,128,512]{2,1,0:T(8,128)(2,1)}), bf16[4,128,512]{2,1,0:T(8,128)(2,1)S(1)}, u32[]{:S(2)}, u32[]{:S(2)}) %all-to-all-start.3) | async-done | bytes 524320 | tf_op jit(solution)/shard_map/all_to_all | solution.py:344
  130.5 2.5 %shard_map.88.b0 = bf16[512,512]{1,0:T(8,128)(2,1)S(1)} custom-call(s32[5]{0:T(128)S(1)} %stack.23.refs_0_.at, bf16[1072,512]{1,0:T(8,128)(2,1)S(1)} %get-tuple-element.21.refs_1_, bf16[1072,512]{1,0:T(8,128)(2,1)S(1)} %collective-permute-done.refs_2_, bf16[1,1024]{1,0:T(2,128)(2,1)S(1)} %broadcast_in_dim.4.refs_3_, f32[512,512]{1,0:T(8,128)S(1)} %copy-done.2, ...), custom_call_target="tpu_custom_call" | custom-call | flops 1000000 | bytes 1000000 | tf_op jit(solution)/shard_map/pallas_call | solution.py:66
  135.1 3.6 %collective-permute-start.5 = (bf16[512,512]{1,0:T(8,128)(2,1)S(1)}, bf16[512,512]{1,0:T(8,128)(2,1)S(1)}, u32[]{:S(2)}, u32[]{:S(2)}) collective-permute-start(bf16[512,512]{1,0:T(8,128)(2,1)S(1)} %shard_map.88.b0), channel_id=1, source_target_pairs={{0,2},{1,3},{2,0},{3,1},{4,6},{5,7},{6,4},{7,5},{8,10},{9,11},{10,... | collective-permute-start | bytes 1572872 | tf_op jit(solution)/shard_map/ppermute | solution.py:352
  138.7 3.1 %collective-permute-start.6 = (bf16[512,512]{1,0:T(8,128)(2,1)S(1)}, bf16[512,512]{1,0:T(8,128)(2,1)S(1)}, u32[]{:S(2)}, u32[]{:S(2)}) collective-permute-start(bf16[512,512]{1,0:T(8,128)(2,1)S(1)} %shard_map.88.b0), channel_id=1, source_target_pairs={{0,3},{1,0},{2,1},{3,2},{4,7},{5,4},{6,5},{7,6},{8,11},{9,8},{10,9... | collective-permute-start | bytes 1572872 | tf_op jit(solution)/shard_map/ppermute | solution.py:352
  141.9 4.3 %collective-permute-done.4.b1 = bf16[512,512]{1,0:T(8,128)(2,1)S(1)} collective-permute-done((bf16[512,512]{1,0:T(8,128)(2,1)S(1)}, bf16[512,512]{1,0:T(8,128)(2,1)S(1)}, u32[]{:S(2)}, u32[]{:S(2)}) %collective-permute-start.4) | collective-permute-done | bytes 524320 | tf_op jit(solution)/shard_map/ppermute | solution.py:352
  146.2 8.4 %collective-permute-done.5.b2 = bf16[512,512]{1,0:T(8,128)(2,1)S(1)} collective-permute-done((bf16[512,512]{1,0:T(8,128)(2,1)S(1)}, bf16[512,512]{1,0:T(8,128)(2,1)S(1)}, u32[]{:S(2)}, u32[]{:S(2)}) %collective-permute-start.5) | collective-permute-done | bytes 524320 | tf_op jit(solution)/shard_map/ppermute | solution.py:352
  154.6 6.5 %collective-permute-done.6.b3 = bf16[512,512]{1,0:T(8,128)(2,1)S(1)} collective-permute-done((bf16[512,512]{1,0:T(8,128)(2,1)S(1)}, bf16[512,512]{1,0:T(8,128)(2,1)S(1)}, u32[]{:S(2)}, u32[]{:S(2)}) %collective-permute-start.6) | collective-permute-done | bytes 524320 | tf_op jit(solution)/shard_map/ppermute | solution.py:352
  161.1 2.2 %copy-done = bf16[64,64,512]{2,1,0:T(8,128)(2,1)S(1)} copy-done((bf16[64,64,512]{2,1,0:T(8,128)(2,1)S(1)}, bf16[64,64,512]{2,1,0:T(8,128)(2,1)}, u32[]{:S(2)}) %copy-start) | copy-done | bytes 4194328
  163.3 2.9 %shard_map.90 = bf16[256,1024]{1,0:T(8,128)(2,1)S(1)} custom-call(s32[5]{0:T(128)S(1)} %stack.23.refs_0_.at, bf16[512,512]{1,0:T(8,128)(2,1)S(1)} %shard_map.88.b0, bf16[512,512]{1,0:T(8,128)(2,1)S(1)} %collective-permute-done.4.b1, bf16[512,512]{1,0:T(8,128)(2,1)S(1)} %collective-permute-done.5.b2, bf16[512,512]{1,0:T(8,128)(2,1)S(1)} %collective-permute-done.6.b3, ...), custom_call_target="tpu_custom_call" | custom-call | flops 1073741824 | bytes 6291456 | tf_op jit(solution)/shard_map/pallas_call | solution.py:271
  166.2 5.0 %collective-permute-start.9 = (bf16[256,1024]{1,0:T(8,128)(2,1)S(1)}, bf16[256,1024]{1,0:T(8,128)(2,1)S(1)}, u32[]{:S(2)}, u32[]{:S(2)}) collective-permute-start(bf16[256,1024]{1,0:T(8,128)(2,1)S(1)} %shard_map.90), channel_id=1, source_target_pairs={{0,4},{4,0},{1,5},{5,1},{2,6},{6,2},{3,7},{7,3},{8,12},{12,8},{9,1... | collective-permute-start | bytes 1572872 | tf_op jit(solution)/shard_map/ppermute | solution.py:19
  171.2 2.9 %shard_map.89 = f32[256,1024]{1,0:T(8,128)S(1)} custom-call(s32[5]{0:T(128)S(1)} %stack.23.refs_0_.at, bf16[512,512]{1,0:T(8,128)(2,1)S(1)} %shard_map.88.b0, bf16[512,512]{1,0:T(8,128)(2,1)S(1)} %collective-permute-done.4.b1, bf16[512,512]{1,0:T(8,128)(2,1)S(1)} %collective-permute-done.5.b2, bf16[512,512]{1,0:T(8,128)(2,1)S(1)} %collective-permute-done.6.b3, ...), custom_call_target="tpu_custom_call" | custom-call | flops 1073741824 | bytes 6291456 | tf_op jit(solution)/shard_map/pallas_call | solution.py:271
  (53 shorter events, 23.9 us)
Async XLA Ops:
  6.5 154.5 %all-gather.3.cloned.1.call-start = ((), (), s32[]{:S(2)}) async-start(), calls=%async_computation.5 | async-start | bytes 4456448 | tf_op jit(solution)/shard_map/all_gather | solution.py:321
  6.6 1.0 copy-start.4
  7.7 1.0 copy-start.5
  8.7 1.0 copy-start.6
  9.7 1.0 copy-start.7
  10.8 0.8 copy-start.12
  14.2 9.5 %collective-permute-start.7 = (bf16[32,512]{1,0:T(8,128)(2,1)S(1)}, bf16[32,512]{1,0:T(8,128)(2,1)S(1)}, u32[]{:S(2)}, u32[]{:S(2)}) collective-permute-start(bf16[32,512]{1,0:T(8,128)(2,1)S(1)} %get-tuple-element.35), channel_id=1, source_target_pairs={{0,0},{4,4},{1,128},{5,132},{2,256},{6,260},{3,384},{7,388},{128,1... | collective-permute-start | bytes 98312 | tf_op jit(solution)/shard_map/ppermute | solution.py:314
  14.9 9.6 %collective-permute-start.8 = (bf16[32,512]{1,0:T(8,128)(2,1)S(1)}, bf16[32,512]{1,0:T(8,128)(2,1)S(1)}, u32[]{:S(2)}, u32[]{:S(2)}) collective-permute-start(bf16[32,512]{1,0:T(8,128)(2,1)S(1)} %get-tuple-element.36), channel_id=1, source_target_pairs={{0,4},{4,0},{1,132},{5,128},{2,260},{6,256},{3,388},{7,384},{128,5... | collective-permute-start | bytes 98312 | tf_op jit(solution)/shard_map/ppermute | solution.py:314
  38.7 6.3 %collective-permute-start = (bf16[1072,512]{1,0:T(8,128)(2,1)S(1)}, bf16[1072,512]{1,0:T(8,128)(2,1)S(1)}, u32[]{:S(2)}, u32[]{:S(2)}) collective-permute-start(bf16[1072,512]{1,0:T(8,128)(2,1)S(1)} %get-tuple-element.22), channel_id=1, source_target_pairs={{0,4},{4,0},{1,5},{5,1},{2,6},{6,2},{3,7},{7,3},{8,12},{12,8},{9,1... | collective-permute-start | bytes 3293192 | tf_op jit(solution)/shard_map/ppermute | solution.py:19
  59.6 39.0 %all-to-all-start.1 = ((bf16[4,144,128]{2,1,0:T(8,128)(2,1)}), bf16[4,144,128]{2,1,0:T(8,128)(2,1)S(1)}, u32[]{:S(2)}, u32[]{:S(2)}) async-start(bf16[4,144,128]{2,1,0:T(8,128)(2,1)} %get-tuple-element.31), calls=%async_computation.1 | async-start | bytes 294912 | tf_op jit(solution)/shard_map/all_to_all | solution.py:328
  71.7 11.4 %collective-permute-start.1 = (bf16[144,256]{1,0:T(8,128)(2,1)S(1)}, bf16[144,256]{1,0:T(8,128)(2,1)S(1)}, u32[]{:S(2)}, u32[]{:S(2)}) collective-permute-start(bf16[144,256]{1,0:T(8,128)(2,1)S(1)} %get-tuple-element.26), channel_id=1, source_target_pairs={{0,8},{8,0},{16,24},{24,16},{1,9},{9,1},{17,25},{25,17},{2,10},{10... | collective-permute-start | bytes 221192 | tf_op jit(solution)/shard_map/ppermute | solution.py:23
  74.1 10.2 %collective-permute-start.2 = (bf16[144,256]{1,0:T(8,128)(2,1)S(1)}, bf16[144,256]{1,0:T(8,128)(2,1)S(1)}, u32[]{:S(2)}, u32[]{:S(2)}) collective-permute-start(bf16[144,256]{1,0:T(8,128)(2,1)S(1)} %get-tuple-element.27), channel_id=1, source_target_pairs={{0,16},{8,24},{16,0},{24,8},{1,17},{9,25},{17,1},{25,9},{2,18},{10... | collective-permute-start | bytes 221192 | tf_op jit(solution)/shard_map/ppermute | solution.py:23
  78.0 13.6 %collective-permute-start.3 = (bf16[144,256]{1,0:T(8,128)(2,1)S(1)}, bf16[144,256]{1,0:T(8,128)(2,1)S(1)}, u32[]{:S(2)}, u32[]{:S(2)}) collective-permute-start(bf16[144,256]{1,0:T(8,128)(2,1)S(1)} %get-tuple-element.28), channel_id=1, source_target_pairs={{0,24},{8,16},{16,8},{24,0},{1,25},{9,17},{17,9},{25,1},{2,26},{10... | collective-permute-start | bytes 221192 | tf_op jit(solution)/shard_map/ppermute | solution.py:23
  91.7 0.9 copy-start.11
  98.6 8.7 %copy-start.1 = (f32[512,512]{1,0:T(8,128)}, f32[512,512]{1,0:T(8,128)S(1)}, u32[]{:S(2)}) copy-start(f32[512,512]{1,0:T(8,128)S(1)} %get-tuple-element.29.refs_2_.refs_4_) | copy-start | bytes 3145732
  99.2 12.4 %copy-start.15 = (bf16[1024]{0:T(1024)(128)(2,1)S(1)}, bf16[1024]{0:T(1024)(128)(2,1)}, u32[]{:S(2)}) copy-start(bf16[1024]{0:T(1024)(128)(2,1)} %param.14) | copy-start | bytes 6148
  99.2 30.1 %copy-start.9 = (f32[512,16]{1,0:T(8,128)S(1)}, f32[512,16]{1,0:T(8,128)}, u32[]{:S(2)}) copy-start(f32[512,16]{1,0:T(8,128)} %copy-done.8) | copy-start | bytes 98308
  108.1 21.2 %all-to-all-start.3 = ((bf16[4,128,512]{2,1,0:T(8,128)(2,1)}), bf16[4,128,512]{2,1,0:T(8,128)(2,1)S(1)}, u32[]{:S(2)}, u32[]{:S(2)}) async-start(bf16[4,128,512]{2,1,0:T(8,128)(2,1)} %copy-done.3), calls=%async_computation.3 | async-start | bytes 1048576 | tf_op jit(solution)/shard_map/all_to_all | solution.py:344
  129.3 1.2 copy-start.2
  133.0 13.2 %collective-permute-start.4 = (bf16[512,512]{1,0:T(8,128)(2,1)S(1)}, bf16[512,512]{1,0:T(8,128)(2,1)S(1)}, u32[]{:S(2)}, u32[]{:S(2)}) collective-permute-start(bf16[512,512]{1,0:T(8,128)(2,1)S(1)} %shard_map.88.b0), channel_id=1, source_target_pairs={{0,1},{1,2},{2,3},{3,0},{4,5},{5,6},{6,7},{7,4},{8,9},{9,10},{10,1... | collective-permute-start | bytes 1572872 | tf_op jit(solution)/shard_map/ppermute | solution.py:352
  135.1 19.5 %collective-permute-start.5 = (bf16[512,512]{1,0:T(8,128)(2,1)S(1)}, bf16[512,512]{1,0:T(8,128)(2,1)S(1)}, u32[]{:S(2)}, u32[]{:S(2)}) collective-permute-start(bf16[512,512]{1,0:T(8,128)(2,1)S(1)} %shard_map.88.b0), channel_id=1, source_target_pairs={{0,2},{1,3},{2,0},{3,1},{4,6},{5,7},{6,4},{7,5},{8,10},{9,11},{10,... | collective-permute-start | bytes 1572872 | tf_op jit(solution)/shard_map/ppermute | solution.py:352
  138.7 22.3 %collective-permute-start.6 = (bf16[512,512]{1,0:T(8,128)(2,1)S(1)}, bf16[512,512]{1,0:T(8,128)(2,1)S(1)}, u32[]{:S(2)}, u32[]{:S(2)}) collective-permute-start(bf16[512,512]{1,0:T(8,128)(2,1)S(1)} %shard_map.88.b0), channel_id=1, source_target_pairs={{0,3},{1,0},{2,1},{3,2},{4,7},{5,4},{6,5},{7,6},{8,11},{9,8},{10,9... | collective-permute-start | bytes 1572872 | tf_op jit(solution)/shard_map/ppermute | solution.py:352
  161.1 2.2 %copy-start = (bf16[64,64,512]{2,1,0:T(8,128)(2,1)S(1)}, bf16[64,64,512]{2,1,0:T(8,128)(2,1)}, u32[]{:S(2)}) copy-start(bf16[64,64,512]{2,1,0:T(8,128)(2,1)} %all-gather.3.cloned.1.call-done) | copy-start | bytes 12582916
  166.2 8.0 %collective-permute-start.9 = (bf16[256,1024]{1,0:T(8,128)(2,1)S(1)}, bf16[256,1024]{1,0:T(8,128)(2,1)S(1)}, u32[]{:S(2)}, u32[]{:S(2)}) collective-permute-start(bf16[256,1024]{1,0:T(8,128)(2,1)S(1)} %shard_map.90), channel_id=1, source_target_pairs={{0,4},{4,0},{1,5},{5,1},{2,6},{6,2},{3,7},{7,3},{8,12},{12,8},{9,1... | collective-permute-start | bytes 1572872 | tf_op jit(solution)/shard_map/ppermute | solution.py:19
  (5 other events, 3.7 us)
Sparse Core Ops, SparseCore 0:
  38.8 91.3 all-gather.2

commit v5 on v4

--- a/solution.py
+++ b/solution.py
@@ -9,7 +9,8 @@
 
 BF = jnp.bfloat16
 F32 = jnp.float32
-SEQ = ("y", "a", "b", "c")
+SEQ = ("y", "a", "p", "q", "c")
+NEAR = ("p", "q")
 NT = (((1,), (1,)), ((), ()))
 TN = (((0,), (0,)), ((), ()))
 LOGS = 1024
@@ -55,7 +56,7 @@
 def call(body, outs, args, unread=(), scratch=(), hbm=()):
     specs = [pl.BlockSpec(memory_space=pltpu.SMEM)]
     specs += [
-        pl.BlockSpec(memory_space=pl.ANY if i in hbm else pltpu.VMEM)
+        pl.BlockSpec(memory_space=pltpu.HBM if i in hbm else pltpu.VMEM)
         for i in range(1, len(args))
     ]
     specs += [pl.BlockSpec(memory_space=pl.ANY)] * len(unread)
@@ -195,10 +196,8 @@
     return at, pl.ds(pl.multiple_of(at * 256, 256), 256)
 
 
-def own_body(at, keep, got, first, n0, n1, n2, n3, mixture, coef, near):
+def own_body(at, keep, got, first, mixture, coef):
     core = at[0]
-    for k, n in enumerate((n0, n1, n2, n3)):
-        near[at[1] ^ k] = n[...]
     rows = lax.broadcasted_iota(jnp.int32, (256, 256), 0)
     cols = lax.broadcasted_iota(jnp.int32, (256, 256), 1)
     lower = rows >= cols
@@ -222,13 +221,24 @@
             total = dot(weights, v) * m[0]
             start = jnp.exp(local)
             total += dot(q, first[h]) * jnp.where(second == 1, start * m[1], 0.0)
+            mixture[here, hc] = total
             start = start * jnp.exp(first_log[h : h + 1])
-            read = dot(q, near[h, 0:128, :])
-            total += read[:, 0:128] * (start * m[2]) + read[:, 128:256] * (start * m[3])
-            mixture[here, hc] = total
-            start = start * jnp.exp(untail(near[h, 128:144, 0:128])[:, 0:1])
-            for l in range(4, 8):
-                coef[here, 4 * h + l - 4 : 4 * h + l - 3] = start * m[l]
+            for l in range(2, 8):
+                coef[here, 6 * h + l - 2 : 6 * h + l - 1] = start * m[l]
+
+
+def near_mix_body(at, keep, got, mixture, coef, n0, n1, n2, n3, mixed, later, near):
+    for k, n in enumerate((n0, n1, n2, n3)):
+        near[at[1] ^ k] = n[...]
+    for s, ref in enumerate((keep, got)):
+        _, here = place(s, at[0])
+        for h in range(4):
+            hc = slice(h * 128, h * 128 + 128)
+            read = dot(ref[512:768, hc], near[h, 0:128, :])
+            total = mixture[here, hc] + read[:, 0:128] * coef[here, 6 * h : 6 * h + 1]
+            mixed[here, hc] = total + read[:, 128:256] * coef[here, 6 * h + 1 : 6 * h + 2]
+            before = jnp.exp(untail(near[h, 128:144, 0:128])[:, 0:1])
+            later[here, 4 * h : 4 * h + 4] = coef[here, 6 * h + 2 : 6 * h + 6] * before
 
 
 def norm_body(at, keep, got, gain, mixture, coef, last, normed):
@@ -249,45 +259,39 @@
             normed[here, hc] = (gated * size * gain[:, mine].astype(F32)).astype(BF)
 
 
-def project_body(other, at, b0, b1, b2, b3, right, out, total):
-    step = pl.program_id(0)
+def project_body(other, at, b0, b1, b2, b3, w0, w1, w2, w3, out, left, right, sems):
     row = (1 - at[0]) if other else at[0]
     rows = pl.ds(pl.multiple_of(row * 256, 256), 256)
+    copies = [
+        pltpu.make_async_copy(w, right.at[k], sems.at[k]) for k, w in enumerate((w0, w1, w2, w3))
+    ]
+    for copy in copies:
+        copy.start()
     for j, block in enumerate((b0, b1, b2, b3)):
-
-        @pl.when(step == j)
-        def _():
-            part = dot(block[rows, :], right[...].reshape(1024, 512), NT)
-            if j == 0:
-                total[...] = part
-            elif j < 3:
-                total[...] += part
-            else:
-                out[...] = (total[...] + part).astype(out.dtype)
-
-
-def project(at, blocks, right, other):
-    whole_block = pl.BlockSpec((512, 512), lambda k, at: (0, 0))
-    return pl.pallas_call(
+        left[(at[4] + 4 - j) % 4] = block[rows, :]
+    total = 0.0
+    for k, turn in enumerate((0, 1, 3, 2)):
+        copies[k].wait()
+        total += dot(left[(at[3] + turn) % 4], right[k].reshape(1024, 512), NT)
+    out[...] = total.astype(out.dtype)
+
+
+def project(at, blocks, rights, other):
+    return call(
         functools.partial(project_body, other),
-        out_shape=jax.ShapeDtypeStruct((256, 1024), BF if other else F32),
-        grid_spec=pltpu.PrefetchScalarGridSpec(
-            num_scalar_prefetch=1,
-            grid=(4,),
-            in_specs=[whole_block] * 4
-            + [pl.BlockSpec((16, 1, 64, 512), lambda k, at: (0, (at[4] + 4 - k) % 4, 0, 0))],
-            out_specs=pl.BlockSpec((256, 1024), lambda k, at: (0, 0)),
-            scratch_shapes=[pltpu.VMEM((256, 1024), F32)],
-        ),
-        compiler_params=pltpu.CompilerParams(vmem_limit_bytes=32 * 2**20),
-        cost_estimate=pl.CostEstimate(
-            flops=2**30, bytes_accessed=6 * 2**20, transcendentals=0
-        ),
-    )(at, *blocks, right)
+        [((256, 1024), BF if other else F32)],
+        (at, *blocks, *rights),
+        scratch=[
+            pltpu.VMEM((4, 256, 512), BF),
+            pltpu.VMEM((4, 16, 64, 512), BF),
+            pltpu.SemaphoreType.DMA((4,)),
+        ],
+        hbm=range(5, 9),
+    )[0]
 
 
 def shards(values, keys, queries, gates, log_decay, level_mix, norm_gain, weight):
-    y, a, b, c, x = (lax.axis_index(n) for n in ("y", "a", "b", "c", "x"))
+    y, a, b, q, c, x = (lax.axis_index(n) for n in ("y", "a", NEAR, "q", "c", "x"))
     at = jnp.stack([c, b, a, y, x]).astype(jnp.int32)
     block = ((LOGS + 48, 512), BF)
     keep, send, w_same, w_other = call(
@@ -316,22 +320,24 @@
     first_rows = jnp.where(c == 0, turned[0], turned[1])
     later_rows = jnp.where(c == 0, turned[1], turned[0])
     mine = jnp.concatenate([first_rows, later_rows])
-    mine = jnp.broadcast_to(mine[None], (4, 64, 512))
-    mine = lax.all_to_all(mine, "y", 0, 0, tiled=True)
-    gathered = lax.all_gather(mine, ("a", "b"))
+    next_z = lax.ppermute(mine, "q", [(0, 1), (1, 0)])
+    mine = jnp.stack([jnp.where(q == 0, mine, next_z), jnp.where(q == 0, next_z, mine)])
+    right = lax.all_gather(mine, ("a", "p"), axis=0, tiled=True)
+    rights = [right] + [
+        lax.ppermute(right, "y", [(i, (i - k) % 4) for i in range(4)]) for k in (1, 3, 2)
+    ]
 
     pay, first = call(
         ends_body, [((4, 144, 128), BF), ((4, 128, 128), BF)], (at, keep, got)
     )
-    near = lax.all_to_all(pay, "b", 0, 0, tiled=True)
+    near = lax.all_to_all(pay, NEAR, 0, 0, tiled=True)
     pay, *near = call(near_body, [((4, 144, 128), BF)] + [((144, 256), BF)] * 4, (at, near))
     far = lax.all_to_all(pay, "a", 0, 0, tiled=True)
-    near = near[:1] + [flip(near[k], "b", k) for k in (1, 2, 3)]
+    near = near[:1] + [flip(near[k], NEAR, k) for k in (1, 2, 3)]
     mixture, coef = call(
         own_body,
-        [((512, 512), F32), ((512, 16), F32)],
-        (at, keep, got, first, *near),
-        scratch=[pltpu.VMEM((4, 144, 256), BF)],
+        [((512, 512), F32), ((512, 24), F32)],
+        (at, keep, got, first),
     )
     pay, far, before = call(
         far_body,
@@ -339,9 +345,17 @@
         (at, far),
         unread=(mixture,),
     )
+    mixture, coef = call(
+        near_mix_body,
+        [((512, 512), F32), ((512, 16), F32)],
+        (at, keep, got, mixture, coef, *near),
+        scratch=[pltpu.VMEM((4, 144, 256), BF)],
+    )
     last = lax.all_to_all(pay, "y", 0, 0, tiled=True)
-    (last,) = call(last_body, [((4, 128, 512), BF)], (at, last, far, before))
-    last = lax.all_to_all(last, "b", 0, 0, tiled=True)
+    (last,) = call(
+        last_body, [((4, 128, 512), BF)], (at, last, far, before), unread=(mixture,)
+    )
+    last = lax.all_to_all(last, NEAR, 0, 0, tiled=True)
     (normed,) = call(
         norm_body,
         [((512, 512), BF)],
@@ -351,13 +365,13 @@
     blocks = [normed] + [
         lax.ppermute(normed, "x", [(i, (i + j) % 4) for i in range(4)]) for j in (1, 2, 3)
     ]
-    theirs = swap(project(at, blocks, gathered, True))
-    own = project(at, blocks, gathered, False)
+    theirs = swap(project(at, blocks, rights, True))
+    own = project(at, blocks, rights, False)
     return (own + theirs.astype(F32)).astype(BF)
 
 
 def solution(mesh):
-    fine = Mesh(mesh.devices.reshape(4, 4, 4, 2, 4), SEQ + ("x",))
+    fine = Mesh(mesh.devices.reshape(4, 4, 2, 2, 2, 4), SEQ + ("x",))
     return jax.shard_map(
         shards,
         mesh=fine,

time: 183 us -> 191 us (1.044)
  starting transfers between devices: 52.2 us -> 91.1 us
  blocking collectives: 32.5 us -> 7.87 us
  waiting for transfers between devices: 50.8 us -> 39.2 us
  Pallas kernels: 18.8 us -> 21.9 us
    ppermute x0 -> x4, waiting for transfers between devices: none -> 26.8 us  [the longest x3 23.6 us: shards(): lax.ppermute(right, 'y', [(i, (i - k) % 4) for i in range(4)])]
    all_to_all x3 -> x1, blocking collectives: 32.5 us -> 7.87 us  [shards(): near = lax.all_to_all(pay, NEAR, 0, 0, tiled=True)]
    ppermute x3, waiting for transfers between devices: 19.2 us -> 0.01 us  [shards(): lax.ppermute(normed, 'x', [(i, (i + j) % 4) for i in range(4)])]
    all_to_all x1 -> x2, waiting for transfers between devices: 17.7 us -> 0.01 us  [the longest x1 0.01 us: shards(): last = lax.all_to_all(pay, 'y', 0, 0, tiled=True)]
    all_to_all x1 -> x2, starting transfers between devices: 3.47 us -> 19 us  [the longest x1 14.7 us: shards(): last = lax.all_to_all(pay, 'y', 0, 0, tiled=True)]
    ppermute x0 -> x4, starting transfers between devices: none -> 11.8 us  [the longest x3 9.85 us: shards(): lax.ppermute(right, 'y', [(i, (i - k) % 4) for i in range(4)])]
    pallas_call x7 -> x10, Pallas kernels: 13 us -> 21.9 us  [call(): pl.pallas_call(run, out_shape=[jax.ShapeDtypeStruct(*o) for o in outs], i...]
    ppermute x2, starting transfers between devices: 9.02 us -> 17.8 us  [swap(): return lax.ppermute(value, 'c', [(0, 1), (1, 0)])]
  transfers between devices with their start and end apart: 13 -> 18, of which waited for: 9 -> 6; matrix products, arithmetic and copies ran while one was open for 0% -> 1% of each run, Pallas kernels for 8% -> 9%
where the time goes in v5:
time: 191 us; the launch traced here: 190 us
  starting transfers between devices  91.1 us (48%)
  waiting for transfers between devices  39.2 us (21%)
  Pallas kernels  21.9 us (11%)
  between operations  13.7 us (7%)
  local copies, waits for them, and re-layouts  13.5 us (7%)
  blocking collectives  7.87 us (4%)
  other arithmetic  2.5 us (1%)
    ppermute x3, waiting for transfers between devices, shards(): lax.ppermute(right, 'y', [(i, (i - k) % 4) for i in range(4)])  23.6 us
    pallas_call x10, Pallas kernels, call(): pl.pallas_call(run, out_shape=[jax.ShapeDtypeStruct(*o) for o in outs], i...  21.9 us
    ppermute x2, starting transfers between devices, swap(): return lax.ppermute(value, 'c', [(0, 1), (1, 0)])  17.8 us
    all_to_all x1, starting transfers between devices, shards(): last = lax.all_to_all(pay, 'y', 0, 0, tiled=True)  14.7 us
    unnamed x42, local copies, waits for them, and re-layouts  13.4 us
    ppermute x3, starting transfers between devices, flip(): return lax.ppermute(value, axis, [(i, i ^ mask) for i in range(4)])  12.3 us
    ppermute x3, starting transfers between devices, shards(): lax.ppermute(normed, 'x', [(i, (i + j) % 4) for i in range(4)])  10.9 us
    ppermute x3, starting transfers between devices, shards(): lax.ppermute(right, 'y', [(i, (i - k) % 4) for i in range(4)])  9.85 us
  transfers between devices with their start and end apart: 18, of which 6 were waited for; matrix products, arithmetic and copies ran while one was open for 1% of the time, Pallas kernels for 9%

profile of v5, /device:TPU:1, one launch (start us, length us, event | category | flops | bytes accessed | tf_op | source)
XLA Modules:
  0.0 189.8 jit_solution(2543079263517816915)
XLA Ops:
  14.9 8.8 %collective-permute-start.8 = (bf16[32,512]{1,0:T(8,128)(2,1)S(1)}, bf16[32,512]{1,0:T(8,128)(2,1)S(1)}, u32[]{:S(2)}, u32[]{:S(2)}) collective-permute-start(bf16[32,512]{1,0:T(8,128)(2,1)S(1)} %get-tuple-element.40), channel_id=1, source_target_pairs={{0,4},{4,0},{1,132},{5,128},{2,260},{6,256},{3,388},{7,384},{128,5... | collective-permute-start | bytes 98312 | tf_op jit(solution)/shard_map/ppermute | solution.py:318
  25.6 1.9 %collective-permute-start.9 = (bf16[64,512]{1,0:T(8,128)(2,1)S(1)}, bf16[64,512]{1,0:T(8,128)(2,1)}, u32[]{:S(2)}, u32[]{:S(2)}) collective-permute-start(bf16[64,512]{1,0:T(8,128)(2,1)S(1)} %pad_maximum_fusion.1), channel_id=1, source_target_pairs={{0,8},{8,0},{1,9},{9,1},{2,10},{10,2},{3,11},{11,3},{4,12},{12,4},... | collective-permute-start | bytes 196616 | tf_op jit(solution)/shard_map/ppermute | solution.py:323
  27.6 3.2 %collective-permute-done.9 = bf16[64,512]{1,0:T(8,128)(2,1)} collective-permute-done((bf16[64,512]{1,0:T(8,128)(2,1)S(1)}, bf16[64,512]{1,0:T(8,128)(2,1)}, u32[]{:S(2)}, u32[]{:S(2)}) %collective-permute-start.9) | collective-permute-done | bytes 65568 | tf_op jit(solution)/shard_map/ppermute | solution.py:323
  34.1 7.9 %all_to_all.20.refs_1_ = bf16[4,144,128]{2,1,0:T(8,128)(2,1)S(1)} all-to-all(bf16[4,144,128]{2,1,0:T(8,128)(2,1)S(1)} %get-tuple-element.28), channel_id=1, replica_groups=mesh['y'=4,'a'=4,'p'=2,'q'=2,'c'=2,'x'=4] {'p','q'}, dimensions={0} | all-to-all | bytes 294912 | tf_op jit(solution)/shard_map/all_to_all | solution.py:333
  45.7 9.8 %all-to-all-start.1 = ((bf16[4,144,128]{2,1,0:T(8,128)(2,1)}), bf16[4,144,128]{2,1,0:T(8,128)(2,1)S(1)}, u32[]{:S(2)}, u32[]{:S(2)}) async-start(bf16[4,144,128]{2,1,0:T(8,128)(2,1)} %get-tuple-element.35), calls=%async_computation.1 | async-start | bytes 294912 | tf_op jit(solution)/shard_map/all_to_all | solution.py:335
  55.5 4.3 %shard_map.84 = (f32[512,512]{1,0:T(8,128)S(1)}, f32[512,24]{1,0:T(8,128)S(1)}) custom-call(s32[5]{0:T(128)S(1)} %stack.32.refs_0_, bf16[1072,512]{1,0:T(8,128)(2,1)S(1)} %get-tuple-element.23.refs_1_, bf16[1072,512]{1,0:T(8,128)(2,1)S(1)} %collective-permute-done.refs_2_, bf16[4,128,128]{2,1,0:T(8,128)(2,1)S(1)} %get-tuple-element.25.refs_3_), custom_call_target="tpu_custom_call" | custom-call | flops 1000000 | bytes 1000000 | tf_op jit(solution)/shard_map/pallas_call | solution.py:67
  60.6 7.8 %all-to-all-done.1.refs_1_ = bf16[4,144,128]{2,1,0:T(8,128)(2,1)S(1)} async-done(((bf16[4,144,128]{2,1,0:T(8,128)(2,1)}), bf16[4,144,128]{2,1,0:T(8,128)(2,1)S(1)}, u32[]{:S(2)}, u32[]{:S(2)}) %all-to-all-start.1) | async-done | bytes 147488 | tf_op jit(solution)/shard_map/all_to_all | solution.py:335
  69.7 14.7 %all-to-all-start.2 = ((bf16[4,144,128]{2,1,0:T(8,128)(2,1)}), bf16[4,144,128]{2,1,0:T(8,128)(2,1)S(1)}, u32[]{:S(2)}, u32[]{:S(2)}) async-start(bf16[4,144,128]{2,1,0:T(8,128)(2,1)} %get-tuple-element.36), calls=%async_computation.2 | async-start | bytes 294912 | tf_op jit(solution)/shard_map/all_to_all | solution.py:354
  84.4 3.9 %collective-permute-start.1 = (bf16[144,256]{1,0:T(8,128)(2,1)}, bf16[144,256]{1,0:T(8,128)(2,1)S(1)}, u32[]{:S(2)}, u32[]{:S(2)}) collective-permute-start(bf16[144,256]{1,0:T(8,128)(2,1)} %copy-done.19), channel_id=1, source_target_pairs={{0,8},{8,0},{16,24},{24,16},{1,9},{9,1},{17,25},{25,17},{2,10},{10... | collective-permute-start | bytes 221192 | tf_op jit(solution)/shard_map/ppermute | solution.py:24
  88.3 5.3 %collective-permute-start.2 = (bf16[144,256]{1,0:T(8,128)(2,1)}, bf16[144,256]{1,0:T(8,128)(2,1)S(1)}, u32[]{:S(2)}, u32[]{:S(2)}) collective-permute-start(bf16[144,256]{1,0:T(8,128)(2,1)} %copy-done.18), channel_id=1, source_target_pairs={{0,16},{8,24},{16,0},{24,8},{1,17},{9,25},{17,1},{25,9},{2,18},{10... | collective-permute-start | bytes 221192 | tf_op jit(solution)/shard_map/ppermute | solution.py:24
  93.7 3.1 %collective-permute-start.3 = (bf16[144,256]{1,0:T(8,128)(2,1)}, bf16[144,256]{1,0:T(8,128)(2,1)S(1)}, u32[]{:S(2)}, u32[]{:S(2)}) collective-permute-start(bf16[144,256]{1,0:T(8,128)(2,1)} %copy-done.17), channel_id=1, source_target_pairs={{0,24},{8,16},{16,8},{24,0},{1,25},{9,17},{17,9},{25,1},{2,26},{10... | collective-permute-start | bytes 221192 | tf_op jit(solution)/shard_map/ppermute | solution.py:24
  96.8 4.5 %collective-permute-done.3.refs_8_ = bf16[144,256]{1,0:T(8,128)(2,1)S(1)} collective-permute-done((bf16[144,256]{1,0:T(8,128)(2,1)}, bf16[144,256]{1,0:T(8,128)(2,1)S(1)}, u32[]{:S(2)}, u32[]{:S(2)}) %collective-permute-start.3) | collective-permute-done | bytes 73760 | tf_op jit(solution)/shard_map/ppermute | solution.py:24
  103.5 1.9 %shard_map.86 = (f32[512,512]{1,0:T(8,128)S(1)}, f32[512,16]{1,0:T(8,128)S(1)}) custom-call(s32[5]{0:T(128)S(1)} %stack.32.refs_0_, bf16[1072,512]{1,0:T(8,128)(2,1)S(1)} %get-tuple-element.23.refs_1_, bf16[1072,512]{1,0:T(8,128)(2,1)S(1)} %collective-permute-done.refs_2_, f32[512,512]{1,0:T(8,128)S(1)} %copy-done.1, f32[512,24]{1,0:T(8,128)S(1)} %copy-done.11, ...), custom_call_target="tpu_custom_call" | custom-call | flops 1000000 | bytes 1000000 | tf_op jit(solution)/shard_map/pallas_call | solution.py:67
  107.5 4.3 %all-to-all-start.3 = ((bf16[4,128,512]{2,1,0:T(8,128)(2,1)}), bf16[4,128,512]{2,1,0:T(8,128)(2,1)}, u32[]{:S(2)}, u32[]{:S(2)}) async-start(bf16[4,128,512]{2,1,0:T(8,128)(2,1)} %copy-done.3), calls=%async_computation.3 | async-start | bytes 1048576 | tf_op jit(solution)/shard_map/all_to_all | solution.py:358
  111.9 4.3 %collective-permute-start.10 = (bf16[16,64,512]{2,1,0:T(8,128)(2,1)}, bf16[16,64,512]{2,1,0:T(8,128)(2,1)}, u32[]{:S(2)}, u32[]{:S(2)}) collective-permute-start(bf16[16,64,512]{2,1,0:T(8,128)(2,1)} %all-gather.2.cloned.1.call-done.refs_5_), channel_id=1, source_target_pairs={{0,384},{128,0},{256,128},{384,256},{1,385},{129,1},{257,129},{385... | collective-permute-start | bytes 3145736 | tf_op jit(solution)/shard_map/ppermute | solution.py:327
  118.1 3.7 %collective-permute-start.12 = (bf16[16,64,512]{2,1,0:T(8,128)(2,1)}, bf16[16,64,512]{2,1,0:T(8,128)(2,1)}, u32[]{:S(2)}, u32[]{:S(2)}) collective-permute-start(bf16[16,64,512]{2,1,0:T(8,128)(2,1)} %all-gather.2.cloned.1.call-done.refs_5_), channel_id=1, source_target_pairs={{0,256},{128,384},{256,0},{384,128},{1,257},{129,385},{257,1},{385... | collective-permute-start | bytes 3145736 | tf_op jit(solution)/shard_map/ppermute | solution.py:327
  121.8 3.1 %shard_map.89.refs_1_ = bf16[512,512]{1,0:T(8,128)(2,1)S(1)} custom-call(s32[5]{0:T(128)S(1)} %stack.32.refs_0_, bf16[1072,512]{1,0:T(8,128)(2,1)S(1)} %get-tuple-element.23.refs_1_, bf16[1072,512]{1,0:T(8,128)(2,1)S(1)} %collective-permute-done.refs_2_, bf16[1,1024]{1,0:T(2,128)(2,1)S(1)} %broadcast_in_dim.3.refs_3_, ...), custom_call_target="tpu_custom_call" | custom-call | flops 1000000 | bytes 1000000 | tf_op jit(solution)/shard_map/pallas_call | solution.py:67
  124.8 2.2 %collective-permute-start.4 = (bf16[512,512]{1,0:T(8,128)(2,1)S(1)}, bf16[512,512]{1,0:T(8,128)(2,1)S(1)}, u32[]{:S(2)}, u32[]{:S(2)}) collective-permute-start(bf16[512,512]{1,0:T(8,128)(2,1)S(1)} %shard_map.89.refs_1_), channel_id=1, source_target_pairs={{0,1},{1,2},{2,3},{3,0},{4,5},{5,6},{6,7},{7,4},{8,9},{9,10},{10,1... | collective-permute-start | bytes 1572872 | tf_op jit(solution)/shard_map/ppermute | solution.py:366
  127.1 4.5 %collective-permute-start.5 = (bf16[512,512]{1,0:T(8,128)(2,1)S(1)}, bf16[512,512]{1,0:T(8,128)(2,1)S(1)}, u32[]{:S(2)}, u32[]{:S(2)}) collective-permute-start(bf16[512,512]{1,0:T(8,128)(2,1)S(1)} %shard_map.89.refs_1_), channel_id=1, source_target_pairs={{0,2},{1,3},{2,0},{3,1},{4,6},{5,7},{6,4},{7,5},{8,10},{9,11},{10,... | collective-permute-start | bytes 1572872 | tf_op jit(solution)/shard_map/ppermute | solution.py:366
  133.1 4.2 %collective-permute-start.6 = (bf16[512,512]{1,0:T(8,128)(2,1)S(1)}, bf16[512,512]{1,0:T(8,128)(2,1)S(1)}, u32[]{:S(2)}, u32[]{:S(2)}) collective-permute-start(bf16[512,512]{1,0:T(8,128)(2,1)S(1)} %shard_map.89.refs_1_), channel_id=1, source_target_pairs={{0,3},{1,0},{2,1},{3,2},{4,7},{5,4},{6,5},{7,6},{8,11},{9,8},{10,9... | collective-permute-start | bytes 1572872 | tf_op jit(solution)/shard_map/ppermute | solution.py:366
  138.6 20.7 %collective-permute-done.12.refs_8_ = bf16[16,64,512]{2,1,0:T(8,128)(2,1)} collective-permute-done((bf16[16,64,512]{2,1,0:T(8,128)(2,1)}, bf16[16,64,512]{2,1,0:T(8,128)(2,1)}, u32[]{:S(2)}, u32[]{:S(2)}) %collective-permute-start.12) | collective-permute-done | bytes 1048608 | tf_op jit(solution)/shard_map/ppermute | solution.py:327
  159.4 3.3 %shard_map.91 = bf16[256,1024]{1,0:T(8,128)(2,1)S(1)} custom-call(s32[5]{0:T(128)S(1)} %stack.32.refs_0_, bf16[512,512]{1,0:T(8,128)(2,1)S(1)} %shard_map.89.refs_1_, bf16[512,512]{1,0:T(8,128)(2,1)S(1)} %collective-permute-done.4.refs_2_, bf16[512,512]{1,0:T(8,128)(2,1)S(1)} %collective-permute-done.5.refs_3_, ...), custom_call_target="tpu_custom_call" | custom-call | flops 1000000 | bytes 1000000 | tf_op jit(solution)/shard_map/pallas_call | solution.py:67
  162.7 15.9 %collective-permute-start.13 = (bf16[256,1024]{1,0:T(8,128)(2,1)S(1)}, bf16[256,1024]{1,0:T(8,128)(2,1)S(1)}, u32[]{:S(2)}, u32[]{:S(2)}) collective-permute-start(bf16[256,1024]{1,0:T(8,128)(2,1)S(1)} %shard_map.91), channel_id=1, source_target_pairs={{0,4},{4,0},{1,5},{5,1},{2,6},{6,2},{3,7},{7,3},{8,12},{12,8},{9,1... | collective-permute-start | bytes 1572872 | tf_op jit(solution)/shard_map/ppermute | solution.py:20
  178.6 3.3 %shard_map.90 = f32[256,1024]{1,0:T(8,128)S(1)} custom-call(s32[5]{0:T(128)S(1)} %stack.32.refs_0_, bf16[512,512]{1,0:T(8,128)(2,1)S(1)} %shard_map.89.refs_1_, bf16[512,512]{1,0:T(8,128)(2,1)S(1)} %collective-permute-done.4.refs_2_, bf16[512,512]{1,0:T(8,128)(2,1)S(1)} %collective-permute-done.5.refs_3_, ...), custom_call_target="tpu_custom_call" | custom-call | flops 1000000 | bytes 1000000 | tf_op jit(solution)/shard_map/pallas_call | solution.py:67
  (73 shorter events, 29.4 us)
Async XLA Ops:
  6.5 105.3 %all-gather.2.cloned.1.call-start = ((), (), s32[]{:S(2)}) async-start(), calls=%async_computation.4 | async-start | bytes 1179648 | tf_op jit(solution)/shard_map/all_gather | solution.py:325
  14.2 11.4 %collective-permute-start.7 = (bf16[32,512]{1,0:T(8,128)(2,1)S(1)}, bf16[32,512]{1,0:T(8,128)(2,1)S(1)}, u32[]{:S(2)}, u32[]{:S(2)}) collective-permute-start(bf16[32,512]{1,0:T(8,128)(2,1)S(1)} %get-tuple-element.39), channel_id=1, source_target_pairs={{0,0},{4,4},{1,128},{5,132},{2,256},{6,260},{3,384},{7,388},{128,1... | collective-permute-start | bytes 98312 | tf_op jit(solution)/shard_map/ppermute | solution.py:318
  14.9 10.7 %collective-permute-start.8 = (bf16[32,512]{1,0:T(8,128)(2,1)S(1)}, bf16[32,512]{1,0:T(8,128)(2,1)S(1)}, u32[]{:S(2)}, u32[]{:S(2)}) collective-permute-start(bf16[32,512]{1,0:T(8,128)(2,1)S(1)} %get-tuple-element.40), channel_id=1, source_target_pairs={{0,4},{4,0},{1,132},{5,128},{2,260},{6,256},{3,388},{7,384},{128,5... | collective-permute-start | bytes 98312 | tf_op jit(solution)/shard_map/ppermute | solution.py:318
  23.7 8.7 %collective-permute-start = (bf16[1072,512]{1,0:T(8,128)(2,1)S(1)}, bf16[1072,512]{1,0:T(8,128)(2,1)S(1)}, u32[]{:S(2)}, u32[]{:S(2)}) collective-permute-start(bf16[1072,512]{1,0:T(8,128)(2,1)S(1)} %get-tuple-element.24), channel_id=1, source_target_pairs={{0,4},{4,0},{1,5},{5,1},{2,6},{6,2},{3,7},{7,3},{8,12},{12,8},{9,1... | collective-permute-start | bytes 3293192 | tf_op jit(solution)/shard_map/ppermute | solution.py:20
  25.6 5.1 %collective-permute-start.9 = (bf16[64,512]{1,0:T(8,128)(2,1)S(1)}, bf16[64,512]{1,0:T(8,128)(2,1)}, u32[]{:S(2)}, u32[]{:S(2)}) collective-permute-start(bf16[64,512]{1,0:T(8,128)(2,1)S(1)} %pad_maximum_fusion.1), channel_id=1, source_target_pairs={{0,8},{8,0},{1,9},{9,1},{2,10},{10,2},{3,11},{11,3},{4,12},{12,4},... | collective-permute-start | bytes 196616 | tf_op jit(solution)/shard_map/ppermute | solution.py:323
  45.7 22.7 %all-to-all-start.1 = ((bf16[4,144,128]{2,1,0:T(8,128)(2,1)}), bf16[4,144,128]{2,1,0:T(8,128)(2,1)S(1)}, u32[]{:S(2)}, u32[]{:S(2)}) async-start(bf16[4,144,128]{2,1,0:T(8,128)(2,1)} %get-tuple-element.35), calls=%async_computation.1 | async-start | bytes 294912 | tf_op jit(solution)/shard_map/all_to_all | solution.py:335
  60.6 40.7 %copy-start = (f32[512,512]{1,0:T(8,128)}, f32[512,512]{1,0:T(8,128)S(1)}, u32[]{:S(2)}) copy-start(f32[512,512]{1,0:T(8,128)S(1)} %get-tuple-element.26.refs_3_.refs_2_) | copy-start | bytes 3145732
  60.6 40.7 %copy-start.13 = (bf16[144,256]{1,0:T(8,128)(2,1)S(1)}, bf16[144,256]{1,0:T(8,128)(2,1)}, u32[]{:S(2)}) copy-start(bf16[144,256]{1,0:T(8,128)(2,1)} %copy-done.12) | copy-start | bytes 221188
  69.7 36.5 %all-to-all-start.2 = ((bf16[4,144,128]{2,1,0:T(8,128)(2,1)}), bf16[4,144,128]{2,1,0:T(8,128)(2,1)S(1)}, u32[]{:S(2)}, u32[]{:S(2)}) async-start(bf16[4,144,128]{2,1,0:T(8,128)(2,1)} %get-tuple-element.36), calls=%async_computation.2 | async-start | bytes 294912 | tf_op jit(solution)/shard_map/all_to_all | solution.py:354
  84.4 12.3 %collective-permute-start.1 = (bf16[144,256]{1,0:T(8,128)(2,1)}, bf16[144,256]{1,0:T(8,128)(2,1)S(1)}, u32[]{:S(2)}, u32[]{:S(2)}) collective-permute-start(bf16[144,256]{1,0:T(8,128)(2,1)} %copy-done.19), channel_id=1, source_target_pairs={{0,8},{8,0},{16,24},{24,16},{1,9},{9,1},{17,25},{25,17},{2,10},{10... | collective-permute-start | bytes 221192 | tf_op jit(solution)/shard_map/ppermute | solution.py:24
  88.3 8.5 %collective-permute-start.2 = (bf16[144,256]{1,0:T(8,128)(2,1)}, bf16[144,256]{1,0:T(8,128)(2,1)S(1)}, u32[]{:S(2)}, u32[]{:S(2)}) collective-permute-start(bf16[144,256]{1,0:T(8,128)(2,1)} %copy-done.18), channel_id=1, source_target_pairs={{0,16},{8,24},{16,0},{24,8},{1,17},{9,25},{17,1},{25,9},{2,18},{10... | collective-permute-start | bytes 221192 | tf_op jit(solution)/shard_map/ppermute | solution.py:24
  93.7 7.6 %collective-permute-start.3 = (bf16[144,256]{1,0:T(8,128)(2,1)}, bf16[144,256]{1,0:T(8,128)(2,1)S(1)}, u32[]{:S(2)}, u32[]{:S(2)}) collective-permute-start(bf16[144,256]{1,0:T(8,128)(2,1)} %copy-done.17), channel_id=1, source_target_pairs={{0,24},{8,16},{16,8},{24,0},{1,25},{9,17},{17,9},{25,1},{2,26},{10... | collective-permute-start | bytes 221192 | tf_op jit(solution)/shard_map/ppermute | solution.py:24
  101.3 1.2 copy-start.1
  106.1 15.6 %copy-start.20 = (bf16[1024]{0:T(1024)(128)(2,1)S(1)}, bf16[1024]{0:T(1024)(128)(2,1)}, u32[]{:S(2)}) copy-start(bf16[1024]{0:T(1024)(128)(2,1)} %param.14) | copy-start | bytes 6148
  107.5 14.2 %copy-start.9 = (f32[512,16]{1,0:T(8,128)S(1)}, f32[512,16]{1,0:T(8,128)}, u32[]{:S(2)}) copy-start(f32[512,16]{1,0:T(8,128)} %copy-done.8) | copy-start | bytes 98308
  107.5 14.2 %all-to-all-start.3 = ((bf16[4,128,512]{2,1,0:T(8,128)(2,1)}), bf16[4,128,512]{2,1,0:T(8,128)(2,1)}, u32[]{:S(2)}, u32[]{:S(2)}) async-start(bf16[4,128,512]{2,1,0:T(8,128)(2,1)} %copy-done.3), calls=%async_computation.3 | async-start | bytes 1048576 | tf_op jit(solution)/shard_map/all_to_all | solution.py:358
  111.9 21.3 %collective-permute-start.10 = (bf16[16,64,512]{2,1,0:T(8,128)(2,1)}, bf16[16,64,512]{2,1,0:T(8,128)(2,1)}, u32[]{:S(2)}, u32[]{:S(2)}) collective-permute-start(bf16[16,64,512]{2,1,0:T(8,128)(2,1)} %all-gather.2.cloned.1.call-done.refs_5_), channel_id=1, source_target_pairs={{0,384},{128,0},{256,128},{384,256},{1,385},{129,1},{257,129},{385... | collective-permute-start | bytes 3145736 | tf_op jit(solution)/shard_map/ppermute | solution.py:327
  116.1 22.5 %collective-permute-start.11 = (bf16[16,64,512]{2,1,0:T(8,128)(2,1)}, bf16[16,64,512]{2,1,0:T(8,128)(2,1)}, u32[]{:S(2)}, u32[]{:S(2)}) collective-permute-start(bf16[16,64,512]{2,1,0:T(8,128)(2,1)} %all-gather.2.cloned.1.call-done.refs_5_), channel_id=1, source_target_pairs={{0,128},{128,256},{256,384},{384,0},{1,129},{129,257},{257,385},{3... | collective-permute-start | bytes 3145736 | tf_op jit(solution)/shard_map/ppermute | solution.py:327
  118.1 41.3 %collective-permute-start.12 = (bf16[16,64,512]{2,1,0:T(8,128)(2,1)}, bf16[16,64,512]{2,1,0:T(8,128)(2,1)}, u32[]{:S(2)}, u32[]{:S(2)}) collective-permute-start(bf16[16,64,512]{2,1,0:T(8,128)(2,1)} %all-gather.2.cloned.1.call-done.refs_5_), channel_id=1, source_target_pairs={{0,256},{128,384},{256,0},{384,128},{1,257},{129,385},{257,1},{385... | collective-permute-start | bytes 3145736 | tf_op jit(solution)/shard_map/ppermute | solution.py:327
  121.8 37.6 %copy-start.2 = (bf16[16,64,512]{2,1,0:T(8,128)(2,1)S(1)}, bf16[16,64,512]{2,1,0:T(8,128)(2,1)}, u32[]{:S(2)}) copy-start(bf16[16,64,512]{2,1,0:T(8,128)(2,1)} %all-gather.2.cloned.1.call-done.refs_5_) | copy-start | bytes 3145732
  124.8 34.5 %collective-permute-start.4 = (bf16[512,512]{1,0:T(8,128)(2,1)S(1)}, bf16[512,512]{1,0:T(8,128)(2,1)S(1)}, u32[]{:S(2)}, u32[]{:S(2)}) collective-permute-start(bf16[512,512]{1,0:T(8,128)(2,1)S(1)} %shard_map.89.refs_1_), channel_id=1, source_target_pairs={{0,1},{1,2},{2,3},{3,0},{4,5},{5,6},{6,7},{7,4},{8,9},{9,10},{10,1... | collective-permute-start | bytes 1572872 | tf_op jit(solution)/shard_map/ppermute | solution.py:366
  127.1 32.3 %collective-permute-start.5 = (bf16[512,512]{1,0:T(8,128)(2,1)S(1)}, bf16[512,512]{1,0:T(8,128)(2,1)S(1)}, u32[]{:S(2)}, u32[]{:S(2)}) collective-permute-start(bf16[512,512]{1,0:T(8,128)(2,1)S(1)} %shard_map.89.refs_1_), channel_id=1, source_target_pairs={{0,2},{1,3},{2,0},{3,1},{4,6},{5,7},{6,4},{7,5},{8,10},{9,11},{10,... | collective-permute-start | bytes 1572872 | tf_op jit(solution)/shard_map/ppermute | solution.py:366
  133.1 26.2 %collective-permute-start.6 = (bf16[512,512]{1,0:T(8,128)(2,1)S(1)}, bf16[512,512]{1,0:T(8,128)(2,1)S(1)}, u32[]{:S(2)}, u32[]{:S(2)}) collective-permute-start(bf16[512,512]{1,0:T(8,128)(2,1)S(1)} %shard_map.89.refs_1_), channel_id=1, source_target_pairs={{0,3},{1,0},{2,1},{3,2},{4,7},{5,4},{6,5},{7,6},{8,11},{9,8},{10,9... | collective-permute-start | bytes 1572872 | tf_op jit(solution)/shard_map/ppermute | solution.py:366
  162.7 19.3 %collective-permute-start.13 = (bf16[256,1024]{1,0:T(8,128)(2,1)S(1)}, bf16[256,1024]{1,0:T(8,128)(2,1)S(1)}, u32[]{:S(2)}, u32[]{:S(2)}) collective-permute-start(bf16[256,1024]{1,0:T(8,128)(2,1)S(1)} %shard_map.91), channel_id=1, source_target_pairs={{0,4},{4,0},{1,5},{5,1},{2,6},{6,2},{3,7},{7,3},{8,12},{12,8},{9,1... | collective-permute-start | bytes 1572872 | tf_op jit(solution)/shard_map/ppermute | solution.py:20
  (15 other events, 12.2 us)
Sparse Core Ops, SparseCore 0:
  32.5 60.6 all-gather.1

commit v6 on v5

v6 whole, which is shorter than its diff:
```python
import functools

import jax
import jax.numpy as jnp
from jax import lax
from jax.experimental import pallas as pl
from jax.experimental.pallas import tpu as pltpu
from jax.sharding import Mesh, PartitionSpec as P

BF = jnp.bfloat16
F32 = jnp.float32
SEQ = ("y", "a", "p", "q", "c")
NEAR = ("p", "q")
NT = (((1,), (1,)), ((), ()))
TN = (((0,), (0,)), ((), ()))
LOGS = 1024


def swap(value):
    return lax.ppermute(value, "c", [(0, 1), (1, 0)])


def flat(place):
    y, x, core = place // 8, place // 2 % 4, place % 2
    return (y * 2 + core) * 4 + x


def dot(left, right, dims=(((1,), (0,)), ((), ()))):
    return lax.dot_general(left, right, dims, preferred_element_type=F32)


def exact(left, right, dims):
    return lax.dot_general(
        left, right, dims, precision=lax.Precision.HIGHEST, preferred_element_type=F32
    )


def tails(logs):
    row = lax.broadcasted_iota(jnp.int32, (16, 128), 0)
    tile = jnp.zeros((16, 128), F32)
    for h, log in enumerate(logs):
        high = log.astype(BF).astype(F32)
        middle = (log - high).astype(BF).astype(F32)
        for i, term in enumerate((high, middle, log - high - middle)):
            tile = jnp.where(row == 3 * h + i, term, tile)
    return tile.astype(BF)


def untail(tile, h):
    return jnp.sum(tile[3 * h : 3 * h + 3].astype(F32), axis=0, keepdims=True)


def call(body, outs, args, unread=(), scratch=(), hbm=(), vmem=12):
    specs = [pl.BlockSpec(memory_space=pltpu.SMEM)]
    specs += [
        pl.BlockSpec(memory_space=pltpu.HBM if i in hbm else pltpu.VMEM)
        for i in range(1, len(args))
    ]
    specs += [pl.BlockSpec(memory_space=pl.ANY)] * len(unread)

    def run(*refs):
        body(*refs[: len(args)], *refs[len(args) + len(unread) :])

    return pl.pallas_call(
        run,
        out_shape=[jax.ShapeDtypeStruct(*o) for o in outs],
        in_specs=specs,
        out_specs=[pl.BlockSpec(memory_space=pltpu.VMEM)] * len(outs),
        scratch_shapes=list(scratch),
        compiler_params=pltpu.CompilerParams(vmem_limit_bytes=vmem * 2**20),
        cost_estimate=pl.CostEstimate(flops=10**6, bytes_accessed=10**6, transcendentals=0),
    )(*args, *unread)


def pack_body(
    at, keys, values, queries, gates, decay, mix, weight,
    keep, send, w_same, w_other, small, levels, wide, sems,
):
    core = at[0]
    mine = pl.ds(pl.multiple_of(core * 512, 512), 512)
    theirs = pl.ds(pl.multiple_of((1 - core) * 512, 512), 512)
    copies = [
        pltpu.make_async_copy(decay, small, sems.at[0]),
        pltpu.make_async_copy(mix, levels, sems.at[1]),
        pltpu.make_async_copy(weight, wide, sems.at[2]),
    ]
    for i, ref in enumerate((keys, values, queries, gates)):
        rows = pl.ds(i * 256, 256)
        for out, cols, n in ((send, theirs, 3), (keep, mine, 7)):
            copies.append(pltpu.make_async_copy(ref.at[:, cols], out.at[rows, :], sems.at[n + i]))
    for copy in copies:
        copy.start()
    for copy in copies[:3]:
        copy.wait()
    w_same[...] = wide[:, mine]
    w_other[...] = wide[:, theirs]
    for out, low in ((keep, core == 0), (send, core == 1)):
        logs = [jnp.where(low, small[0:4], small[4:8])]
        logs += [jnp.where(low, levels[l, 0:4], levels[l, 4:8]) for l in range(8)]
        logs = jnp.concatenate(logs + [jnp.zeros((12, 256), F32)], axis=0)
        high = logs.astype(BF)
        out[LOGS:, 0:256] = high
        out[LOGS:, 256:512] = (logs - high.astype(F32)).astype(BF)
    for copy in copies[3:]:
        copy.wait()


def logs_of(block):
    tile = block[LOGS:, :].astype(F32)
    return tile[:, 0:256] + tile[:, 256:512]


def ends_body(at, keep, got, pay, first):
    core = at[0]
    logs = jnp.concatenate([logs_of(keep)[0:4], logs_of(got)[0:4]], axis=0)
    after = (
        lax.broadcasted_iota(jnp.int32, (256, 256), 1)
        > lax.broadcasted_iota(jnp.int32, (256, 256), 0)
    ).astype(F32)
    scale = jnp.exp(exact(after, logs, NT))
    total = jnp.sum(logs, axis=1, keepdims=True)
    for h in range(4):
        cols = slice(h * 128, h * 128 + 128)
        end = []
        for i, ref in enumerate((keep, got)):
            scaled = ref[0:256, cols].astype(F32) * scale[:, 4 * i + h : 4 * i + h + 1]
            end.append(dot(scaled.astype(BF), ref[256:512, cols], TN))
        own_later = jnp.exp(jnp.where(core == 0, total[4 + h : 5 + h], 0.0))
        got_later = jnp.exp(jnp.where(core == 0, 0.0, total[h : h + 1]))
        state = (end[0] * own_later + end[1] * got_later).astype(BF)
        for i in range(4):
            pay[i, h * 128 : h * 128 + 128, :] = state
        first[h, :, :] = jnp.where(core == 0, end[0], end[1]).astype(BF)
    tile = tails([total[h : h + 1] + total[4 + h : 5 + h] for h in range(4)])
    for i in range(4):
        pay[i, 512:528, :] = tile


def lower_states(got, h, at):
    s = [got[i, h * 128 : h * 128 + 128, :].astype(F32) for i in range(4)]
    tiles = [got[i, 512:528, :] for i in range(4)]
    t = [untail(tile, h) for tile in tiles]
    pair = s[0] * jnp.exp(t[1]) + s[1]
    whole = pair * jnp.exp(t[2] + t[3]) + s[2] * jnp.exp(t[3]) + s[3]
    odd, upper = at % 2 == 1, at >= 2
    one = jnp.where(odd, jnp.where(upper, s[2], s[0]), 0.0).astype(BF)
    step = jnp.where(odd, jnp.where(upper, t[2], t[0]), 0.0)
    two = jnp.where(upper, pair * jnp.exp(step), 0.0).astype(BF)
    before = sum(jnp.where(at > i, t[i], 0.0) for i in range(3))
    return whole.astype(BF), t[0] + t[1] + t[2] + t[3], one, two, before


def merge_body(which, at, got, pay, levels, before_out):
    logs = []
    for h in range(4):
        whole, log, one, two, before = lower_states(got, h, at[which])
        logs.append(log)
        for i in range(4):
            pay[i, h * 128 : h * 128 + 128, :] = whole
        levels[h, :, 0:128] = one
        levels[h, :, 128:256] = two
        before_out[h, :, :] = jnp.broadcast_to(before, (8, 128))
    tile = tails(logs)
    for i in range(4):
        pay[i, 512:528, :] = tile


def place(s, core):
    at = core if s == 0 else 1 - core
    return at, pl.ds(pl.multiple_of(at * 256, 256), 256)


def own_body(at, keep, got, first, near, before, mixture, coef):
    core = at[0]
    rows = lax.broadcasted_iota(jnp.int32, (256, 256), 0)
    cols = lax.broadcasted_iota(jnp.int32, (256, 256), 1)
    lower = rows >= cols
    upto = lower.astype(F32)
    both = (logs_of(keep), logs_of(got))
    for s, ref in enumerate((keep, got)):
        second, here = place(s, core)
        logs = both[s]
        at_row = exact(logs[0:8], upto, NT)
        at_col = exact(upto, logs[0:8], NT)
        level = logs.T
        first_log = jnp.sum(both[1 - s][0:4], axis=1, keepdims=True)
        first_log = jnp.where(second == 1, first_log, 0.0)
        for h in range(4):
            hc = slice(h * 128, h * 128 + 128)
            q, kb, v = ref[512:768, hc], ref[0:256, hc], ref[256:512, hc]
            local = at_col[:, h : h + 1]
            gap = jnp.where(lower, local - at_row[h : h + 1, :], -1e30)
            weights = (dot(q, kb, NT) * jnp.exp(gap)).astype(BF)
            m = [level[:, 4 + 4 * l + h : 5 + 4 * l + h] for l in range(8)]
            total = dot(weights, v) * m[0]
            start = jnp.exp(local)
            total += dot(q, first[h]) * jnp.where(second == 1, start * m[1], 0.0)
            start = start * jnp.exp(first_log[h : h + 1])
            read = dot(q, near[h])
            total += read[:, 0:128] * (start * m[2]) + read[:, 128:256] * (start * m[3])
            mixture[here, hc] = total
            start = start * jnp.exp(before[h, 0:1, 0:1])
            for l in range(4, 8):
                coef[here, 4 * h + l - 4 : 4 * h + l - 3] = start * m[l]


def far_mix_body(at, keep, got, mixture, coef, far, mixed):
    for s, ref in enumerate((keep, got)):
        _, here = place(s, at[0])
        for h in range(4):
            hc = slice(h * 128, h * 128 + 128)
            read = dot(ref[512:768, hc], far[h])
            total = mixture[here, hc] + read[:, 0:128] * coef[here, 4 * h : 4 * h + 1]
            mixed[here, hc] = total + read[:, 128:256] * coef[here, 4 * h + 1 : 4 * h + 2]


def norm_body(at, keep, got, gain, mixture, coef, last, before, normed):
    core = at[0]
    for h in range(4):
        _, _, one, two, _ = lower_states(last, h, at[3])
        earlier = jnp.exp(before[h, 0:1, 0:1])
        states = jnp.concatenate([one, two], axis=1)
        mine = pl.ds(pl.multiple_of(core * 512 + h * 128, 128), 128)
        hc = slice(h * 128, h * 128 + 128)
        for s, ref in enumerate((keep, got)):
            _, here = place(s, core)
            z = ref[768:1024, hc].astype(F32)
            read = dot(ref[512:768, hc], states)
            total = mixture[here, hc]
            total += read[:, 0:128] * (coef[here, 4 * h + 2 : 4 * h + 3] * earlier)
            total += read[:, 128:256] * (coef[here, 4 * h + 3 : 4 * h + 4] * earlier)
            gated = total * (z / (1.0 + jnp.exp(-z)))
            size = lax.rsqrt(jnp.mean(gated * gated, axis=1, keepdims=True) + 1e-05)
            normed[here, hc] = (gated * size * gain[:, mine].astype(F32)).astype(BF)


def project_body(other, at, b0, b1, b2, b3, gathered, out, left, right, sems):
    row = (1 - at[0]) if other else at[0]
    rows = pl.ds(pl.multiple_of(row * 256, 256), 256)
    copies = [
        pltpu.make_async_copy(gathered.at[:, k], right.at[k], sems.at[k]) for k in range(4)
    ]
    for copy in copies:
        copy.start()
    for j, block in enumerate((b0, b1, b2, b3)):
        left[(at[4] + 4 - j) % 4] = block[rows, :]
    total = 0.0
    for k, turn in enumerate((0, 1, 3, 2)):
        copies[k].wait()
        total += dot(left[(at[3] + turn) % 4], right[k].reshape(1024, 512), NT)
    out[...] = total.astype(out.dtype)


def project(at, blocks, gathered, other):
    return call(
        functools.partial(project_body, other),
        [((256, 1024), BF if other else F32)],
        (at, *blocks, gathered),
        scratch=[
            pltpu.VMEM((4, 256, 512), BF),
            pltpu.VMEM((4, 16, 64, 512), BF),
            pltpu.SemaphoreType.DMA((4,)),
        ],
        hbm=(5,),
        vmem=56,
    )[0]


def shards(values, keys, queries, gates, log_decay, level_mix, norm_gain, weight):
    y, a, b, c, x = (lax.axis_index(n) for n in ("y", "a", NEAR, "c", "x"))
    at = jnp.stack([c, b, a, y, x]).astype(jnp.int32)
    block = ((LOGS + 48, 512), BF)
    keep, send, w_same, w_other = call(
        pack_body,
        [block, block, ((32, 512), BF), ((32, 512), BF)],
        (at, keys, values, queries, gates, log_decay, level_mix, weight),
        scratch=[
            pltpu.VMEM((8, 256), F32),
            pltpu.VMEM((8, 8, 256), F32),
            pltpu.VMEM((32, 1024), BF),
            pltpu.SemaphoreType.DMA((11,)),
        ],
        hbm=range(1, 8),
        vmem=60,
    )
    turned = []
    for other, part in ((0, w_same), (1, w_other)):
        perm = [
            ((s * 4 + f) * 2 + k, (f * 4 + s) * 2 + (k ^ other))
            for s in range(4)
            for f in range(4)
            for k in range(2)
        ]
        perm = [(flat(p), flat(q)) for p, q in perm]
        turned.append(lax.ppermute(part, ("y", "c", "x"), perm))
    got = swap(send)
    first_rows = jnp.where(c == 0, turned[0], turned[1])
    later_rows = jnp.where(c == 0, turned[1], turned[0])
    mine = jnp.concatenate([first_rows, later_rows])
    mine = jnp.stack(
        [mine]
        + [lax.ppermute(mine, "y", [(i, (i - k) % 4) for i in range(4)]) for k in (1, 3, 2)]
    )
    gathered = lax.all_gather(mine, ("a", "p", "q"))

    pay = ((4, 528, 128), BF)
    merged = [pay, ((4, 128, 256), BF), ((4, 8, 128), F32)]
    pay_b, first = call(ends_body, [pay, ((4, 128, 128), BF)], (at, keep, got))
    near = lax.all_to_all(pay_b, NEAR, 0, 0, tiled=True)
    pay_a, near, before_b = call(functools.partial(merge_body, 1), merged, (at, near))
    far = lax.all_to_all(pay_a, "a", 0, 0, tiled=True)
    mixture, coef = call(
        own_body,
        [((512, 512), F32), ((512, 16), F32)],
        (at, keep, got, first, near, before_b),
    )
    pay_y, far, before_a = call(
        functools.partial(merge_body, 2), merged, (at, far), unread=(mixture,)
    )
    last = lax.all_to_all(pay_y, "y", 0, 0, tiled=True)
    (mixture,) = call(
        far_mix_body, [((512, 512), F32)], (at, keep, got, mixture, coef, far)
    )
    (normed,) = call(
        norm_body,
        [((512, 512), BF)],
        (at, keep, got, norm_gain[None], mixture, coef, last, before_a),
    )

    blocks = [normed] + [
        lax.ppermute(normed, "x", [(i, (i + j) % 4) for i in range(4)]) for j in (1, 2, 3)
    ]
    theirs = swap(project(at, blocks, gathered, True))
    own = project(at, blocks, gathered, False)
    return (own + theirs.astype(F32)).astype(BF)


def solution(mesh):
    fine = Mesh(mesh.devices.reshape(4, 4, 2, 2, 2, 4), SEQ + ("x",))
    return jax.shard_map(
        shards,
        mesh=fine,
        in_specs=(
            P(SEQ, "x"),
            P(SEQ, "x"),
            P(SEQ, "x"),
            P(SEQ, "x"),
            P("x", SEQ),
            P(None, "x", SEQ),
            P("x"),
            P(SEQ, "x"),
        ),
        out_specs=P(SEQ, "x"),
        check_vma=False,
    )
```

time: 191 us -> 196 us (1.026)
  starting transfers between devices: 91.1 us -> 61.7 us
  waiting for transfers between devices: 39.2 us -> 57.2 us
  blocking collectives: 7.87 us -> 21.2 us
  Pallas kernels: 21.9 us -> 29.2 us
  local copies, waits for them, and re-layouts: 13.5 us -> 9.29 us
    ppermute x7 -> x3, waiting for transfers between devices: 31.3 us -> 1.29 us  [shards(): lax.ppermute(mine, 'y', [(i, (i - k) % 4) for i in range(4)])]
    all_to_all x3 -> x2, waiting for transfers between devices: 7.83 us -> 32.5 us  [the longest x1 28.7 us: shards(): far = lax.all_to_all(pay_a, 'a', 0, 0, tiled=True)]
    ppermute x3, waiting for transfers between devices: 0.01 us -> 19.8 us  [shards(): lax.ppermute(normed, 'x', [(i, (i + j) % 4) for i in range(4)])]
    all_to_all x1, blocking collectives: 7.87 us -> 21.2 us  [shards(): near = lax.all_to_all(pay_b, NEAR, 0, 0, tiled=True)]
    all_to_all x3 -> x2, starting transfers between devices: 28.8 us -> 19.1 us  [the longest x1 12.5 us: shards(): far = lax.all_to_all(pay_a, 'a', 0, 0, tiled=True)]
    ppermute x7 -> x3, starting transfers between devices: 24.1 us -> 15.1 us  [shards(): lax.ppermute(mine, 'y', [(i, (i - k) % 4) for i in range(4)])]
    ppermute x2, starting transfers between devices: 17.8 us -> 8.84 us  [swap(): return lax.ppermute(value, 'c', [(0, 1), (1, 0)])]
    pallas_call x10 -> x9, Pallas kernels: 21.9 us -> 29.2 us  [call(): pl.pallas_call(run, out_shape=[jax.ShapeDtypeStruct(*o) for o in outs], i...]
  transfers between devices with their start and end apart: 18 -> 13, of which waited for: 6 -> 8; matrix products, arithmetic and copies ran while one was open for 1% -> 0% of each run, Pallas kernels for 9% -> 10%
where the time goes in v6:
time: 196 us; the launch traced here: 195 us
  starting transfers between devices  61.7 us (31%)
  waiting for transfers between devices  57.2 us (29%)
  Pallas kernels  29.2 us (15%)
  blocking collectives  21.2 us (11%)
  between operations  13.6 us (7%)
  local copies, waits for them, and re-layouts  9.29 us (5%)
  other arithmetic  2.91 us (1%)
    pallas_call x9, Pallas kernels, call(): pl.pallas_call(run, out_shape=[jax.ShapeDtypeStruct(*o) for o in outs], i...  29.2 us
    all_to_all x1, waiting for transfers between devices, shards(): far = lax.all_to_all(pay_a, 'a', 0, 0, tiled=True)  28.7 us
    all_to_all x1, blocking collectives, shards(): near = lax.all_to_all(pay_b, NEAR, 0, 0, tiled=True)  21.2 us
    ppermute x3, waiting for transfers between devices, shards(): lax.ppermute(normed, 'x', [(i, (i + j) % 4) for i in range(4)])  19.8 us
    ppermute x3, starting transfers between devices, shards(): lax.ppermute(mine, 'y', [(i, (i - k) % 4) for i in range(4)])  15.1 us
    all_to_all x1, starting transfers between devices, shards(): far = lax.all_to_all(pay_a, 'a', 0, 0, tiled=True)  12.5 us
    ppermute x2, starting transfers between devices, shards(): turned.append(lax.ppermute(part, ('y', 'c', 'x'), perm))  10.3 us
    ppermute x2, starting transfers between devices, swap(): return lax.ppermute(value, 'c', [(0, 1), (1, 0)])  8.84 us
  transfers between devices with their start and end apart: 13, of which 8 were waited for; matrix products, arithmetic and copies ran while one was open for 0% of the time, Pallas kernels for 10%

profile of v6, /device:TPU:1, one launch (start us, length us, event | category | flops | bytes accessed | tf_op | source)
XLA Modules:
  0.0 195.2 jit_solution(8730392959495405685)
XLA Ops:
  7.1 3.8 %shard_map.82 = (bf16[1072,512]{1,0:T(8,128)(2,1)}, bf16[1072,512]{1,0:T(8,128)(2,1)}, bf16[32,512]{1,0:T(8,128)(2,1)}, bf16[32,512]{1,0:T(8,128)(2,1)}) custom-call(s32[5]{0:T(128)} %stack.38.refs_0_, bf16[256,1024]{1,0:T(8,128)(2,1)} %refs_1_.1, bf16[256,1024]{1,0:T(8,128)(2,1)} %refs_2_.1, bf16[256,1024]{1,0:T(8,128)(2,1)} %refs_3_.1, ...), custom_call_target="tpu_custom_call" | custom-call | flops 1000000 | bytes 1000000 | tf_op jit(solution)/shard_map/pallas_call | solution.py:64
  12.4 8.8 %collective-permute-start.5 = (bf16[32,512]{1,0:T(8,128)(2,1)}, bf16[32,512]{1,0:T(8,128)(2,1)S(1)}, u32[]{:S(2)}, u32[]{:S(2)}) collective-permute-start(bf16[32,512]{1,0:T(8,128)(2,1)} %get-tuple-element.32), channel_id=1, source_target_pairs={{0,4},{4,0},{1,132},{5,128},{2,260},{6,256},{3,388},{7,384},{128,5... | collective-permute-start | bytes 98312 | tf_op jit(solution)/shard_map/ppermute | solution.py:295
  22.3 8.6 %collective-permute-start.8 = (bf16[64,512]{1,0:T(8,128)(2,1)S(1)}, bf16[64,512]{1,0:T(8,128)(2,1)S(1)}, u32[]{:S(2)}, u32[]{:S(2)}) collective-permute-start(bf16[64,512]{1,0:T(8,128)(2,1)S(1)} %get-tuple-element.34), channel_id=1, source_target_pairs={{0,256},{128,384},{256,0},{384,128},{1,257},{129,385},{257,1},{385... | collective-permute-start | bytes 196616 | tf_op jit(solution)/shard_map/ppermute | solution.py:302
  30.9 1.9 collective-permute-start.7
  32.8 4.6 %collective-permute-start.6 = (bf16[64,512]{1,0:T(8,128)(2,1)S(1)}, bf16[64,512]{1,0:T(8,128)(2,1)S(1)}, u32[]{:S(2)}, u32[]{:S(2)}) collective-permute-start(bf16[64,512]{1,0:T(8,128)(2,1)S(1)} %get-tuple-element.34), channel_id=1, source_target_pairs={{0,384},{128,0},{256,128},{384,256},{1,385},{129,1},{257,129},{385... | collective-permute-start | bytes 196616 | tf_op jit(solution)/shard_map/ppermute | solution.py:302
  39.4 4.0 %collective-permute-start = (bf16[1072,512]{1,0:T(8,128)(2,1)}, bf16[1072,512]{1,0:T(8,128)(2,1)S(1)}, u32[]{:S(2)}, u32[]{:S(2)}) collective-permute-start(bf16[1072,512]{1,0:T(8,128)(2,1)} %get-tuple-element.20), channel_id=1, source_target_pairs={{0,4},{4,0},{1,5},{5,1},{2,6},{6,2},{3,7},{7,3},{8,12},{12,8},{9,1... | collective-permute-start | bytes 3293192 | tf_op jit(solution)/shard_map/ppermute | solution.py:20
  43.4 2.5 %collective-permute-done.refs_2_ = bf16[1072,512]{1,0:T(8,128)(2,1)S(1)} collective-permute-done((bf16[1072,512]{1,0:T(8,128)(2,1)}, bf16[1072,512]{1,0:T(8,128)(2,1)S(1)}, u32[]{:S(2)}, u32[]{:S(2)}) %collective-permute-start) | collective-permute-done | bytes 1097760 | tf_op jit(solution)/shard_map/ppermute | solution.py:20
  48.4 21.2 %all_to_all.15.refs_1_ = bf16[4,528,128]{2,1,0:T(8,128)(2,1)S(1)} all-to-all(bf16[4,528,128]{2,1,0:T(8,128)(2,1)S(1)} %get-tuple-element.22), channel_id=1, replica_groups=mesh['y'=4,'a'=4,'p'=2,'q'=2,'c'=2,'x'=4] {'p','q'}, dimensions={0} | all-to-all | bytes 1081344 | tf_op jit(solution)/shard_map/all_to_all | solution.py:309
  71.9 12.5 %all-to-all-start.1 = ((bf16[4,528,128]{2,1,0:T(8,128)(2,1)}), bf16[4,528,128]{2,1,0:T(8,128)(2,1)}, u32[]{:S(2)}, u32[]{:S(2)}) async-start(bf16[4,528,128]{2,1,0:T(8,128)(2,1)} %get-tuple-element.27), calls=%async_computation.1 | async-start | bytes 1081344 | tf_op jit(solution)/shard_map/all_to_all | solution.py:311
  86.2 5.3 %shard_map.85 = (f32[512,512]{1,0:T(8,128)S(1)}, f32[512,16]{1,0:T(8,128)S(1)}) custom-call(s32[5]{0:T(128)S(1)} %copy-done.11, bf16[1072,512]{1,0:T(8,128)(2,1)S(1)} %copy-done, bf16[1072,512]{1,0:T(8,128)(2,1)S(1)} %collective-permute-done.refs_2_, bf16[4,128,128]{2,1,0:T(8,128)(2,1)S(1)} %copy-done.10, bf16[4,128,256]{2,1,0:T(8,128)(2,1)S(1)} %copy-done.8, ...), custom_call_target="tpu_custom_call" | custom-call | flops 1000000 | bytes 1000000 | tf_op jit(solution)/shard_map/pallas_call | solution.py:64
  91.6 28.7 %all-to-all-done.1.refs_1_ = bf16[4,528,128]{2,1,0:T(8,128)(2,1)} async-done(((bf16[4,528,128]{2,1,0:T(8,128)(2,1)}), bf16[4,528,128]{2,1,0:T(8,128)(2,1)}, u32[]{:S(2)}, u32[]{:S(2)}) %all-to-all-start.1) | async-done | bytes 540704 | tf_op jit(solution)/shard_map/all_to_all | solution.py:311
  123.1 6.6 %all-to-all-start.2 = ((bf16[4,528,128]{2,1,0:T(8,128)(2,1)}), bf16[4,528,128]{2,1,0:T(8,128)(2,1)}, u32[]{:S(2)}, u32[]{:S(2)}) async-start(bf16[4,528,128]{2,1,0:T(8,128)(2,1)} %copy-done.4), calls=%async_computation.2 | async-start | bytes 1081344 | tf_op jit(solution)/shard_map/all_to_all | solution.py:320
  132.9 3.9 %all-to-all-done.2.refs_6_ = bf16[4,528,128]{2,1,0:T(8,128)(2,1)} async-done(((bf16[4,528,128]{2,1,0:T(8,128)(2,1)}), bf16[4,528,128]{2,1,0:T(8,128)(2,1)}, u32[]{:S(2)}, u32[]{:S(2)}) %all-to-all-start.2) | async-done | bytes 540704 | tf_op jit(solution)/shard_map/all_to_all | solution.py:320
  138.0 3.3 %shard_map.88.refs_1_ = bf16[512,512]{1,0:T(8,128)(2,1)S(1)} custom-call(s32[5]{0:T(128)S(1)} %copy-done.11, bf16[1072,512]{1,0:T(8,128)(2,1)S(1)} %copy-done, bf16[1072,512]{1,0:T(8,128)(2,1)S(1)} %collective-permute-done.refs_2_, bf16[1,1024]{1,0:T(2,128)(2,1)S(1)} %broadcast_in_dim.3.refs_3_, f32[512,512]{1,0:T(8,128)S(1)} %copy-done.3, ...), custom_call_target="tpu_custom_call" | custom-call | flops 1000000 | bytes 1000000 | tf_op jit(solution)/shard_map/pallas_call | solution.py:64
  141.3 1.9 collective-permute-start.1
  143.2 3.8 %collective-permute-start.2 = (bf16[512,512]{1,0:T(8,128)(2,1)S(1)}, bf16[512,512]{1,0:T(8,128)(2,1)S(1)}, u32[]{:S(2)}, u32[]{:S(2)}) collective-permute-start(bf16[512,512]{1,0:T(8,128)(2,1)S(1)} %shard_map.88.refs_1_), channel_id=1, source_target_pairs={{0,2},{1,3},{2,0},{3,1},{4,6},{5,7},{6,4},{7,5},{8,10},{9,11},{10,... | collective-permute-start | bytes 1572872 | tf_op jit(solution)/shard_map/ppermute | solution.py:331
  147.1 2.7 %collective-permute-start.3 = (bf16[512,512]{1,0:T(8,128)(2,1)S(1)}, bf16[512,512]{1,0:T(8,128)(2,1)S(1)}, u32[]{:S(2)}, u32[]{:S(2)}) collective-permute-start(bf16[512,512]{1,0:T(8,128)(2,1)S(1)} %shard_map.88.refs_1_), channel_id=1, source_target_pairs={{0,3},{1,0},{2,1},{3,2},{4,7},{5,4},{6,5},{7,6},{8,11},{9,8},{10,9... | collective-permute-start | bytes 1572872 | tf_op jit(solution)/shard_map/ppermute | solution.py:331
  149.8 5.0 %collective-permute-done.1.refs_2_ = bf16[512,512]{1,0:T(8,128)(2,1)S(1)} collective-permute-done((bf16[512,512]{1,0:T(8,128)(2,1)S(1)}, bf16[512,512]{1,0:T(8,128)(2,1)S(1)}, u32[]{:S(2)}, u32[]{:S(2)}) %collective-permute-start.1) | collective-permute-done | bytes 524320 | tf_op jit(solution)/shard_map/ppermute | solution.py:331
  154.7 7.8 %collective-permute-done.2.refs_3_ = bf16[512,512]{1,0:T(8,128)(2,1)S(1)} collective-permute-done((bf16[512,512]{1,0:T(8,128)(2,1)S(1)}, bf16[512,512]{1,0:T(8,128)(2,1)S(1)}, u32[]{:S(2)}, u32[]{:S(2)}) %collective-permute-start.2) | collective-permute-done | bytes 524320 | tf_op jit(solution)/shard_map/ppermute | solution.py:331
  162.6 7.0 %collective-permute-done.3.refs_4_ = bf16[512,512]{1,0:T(8,128)(2,1)S(1)} collective-permute-done((bf16[512,512]{1,0:T(8,128)(2,1)S(1)}, bf16[512,512]{1,0:T(8,128)(2,1)S(1)}, u32[]{:S(2)}, u32[]{:S(2)}) %collective-permute-start.3) | collective-permute-done | bytes 524320 | tf_op jit(solution)/shard_map/ppermute | solution.py:331
  170.4 5.3 %shard_map.90 = bf16[256,1024]{1,0:T(8,128)(2,1)} custom-call(s32[5]{0:T(128)} %stack.38.refs_0_, bf16[512,512]{1,0:T(8,128)(2,1)} %copy-done.1, bf16[512,512]{1,0:T(8,128)(2,1)} %copy-done.12, bf16[512,512]{1,0:T(8,128)(2,1)} %copy-done.13, bf16[512,512]{1,0:T(8,128)(2,1)} %copy-done.14, bf16[16,4,64,512]{3,2,1,0:T(8,128)(2,1)} %bitcast.11), custom_call_target="tpu_custom_call" | custom-call | flops 1000000 | bytes 1000000 | tf_op jit(solution)/shard_map/pallas_call | solution.py:64
  175.7 4.9 %collective-permute-start.9 = (bf16[256,1024]{1,0:T(8,128)(2,1)}, bf16[256,1024]{1,0:T(8,128)(2,1)S(1)}, u32[]{:S(2)}, u32[]{:S(2)}) collective-permute-start(bf16[256,1024]{1,0:T(8,128)(2,1)} %shard_map.90), channel_id=1, source_target_pairs={{0,4},{4,0},{1,5},{5,1},{2,6},{6,2},{3,7},{7,3},{8,12},{12,8},{9,1... | collective-permute-start | bytes 1572872 | tf_op jit(solution)/shard_map/ppermute | solution.py:20
  180.6 5.6 %shard_map.89 = f32[256,1024]{1,0:T(8,128)} custom-call(s32[5]{0:T(128)} %stack.38.refs_0_, bf16[512,512]{1,0:T(8,128)(2,1)} %copy-done.1, bf16[512,512]{1,0:T(8,128)(2,1)} %copy-done.12, bf16[512,512]{1,0:T(8,128)(2,1)} %copy-done.13, bf16[512,512]{1,0:T(8,128)(2,1)} %copy-done.14, bf16[16,4,64,512]{3,2,1,0:T(8,128)(2,1)} %bitcast.12), custom_call_target="tpu_custom_call" | custom-call | flops 1000000 | bytes 1000000 | tf_op jit(solution)/shard_map/pallas_call | solution.py:64
  186.2 2.2 %add_convert_fusion = bf16[256,1024]{1,0:T(8,128)(2,1)} fusion(f32[256,1024]{1,0:T(8,128)} %shard_map.89, bf16[256,1024]{1,0:T(8,128)(2,1)S(1)} %collective-permute-done.9), kind=kLoop, calls=%fused_computation | loop fusion | flops 786432 | bytes 2097152 | tf_op jit(solution)/shard_map/convert_element_type | solution.py:335
  (51 shorter events, 19.8 us)
Async XLA Ops:
  6.5 163.1 %all-gather.3.cloned.1.call-start = ((), (), s32[]{:S(2)}) async-start(), calls=%async_computation.3 | async-start | bytes 4456448 | tf_op jit(solution)/shard_map/all_gather | solution.py:304
  10.9 35.1 %copy-start = (bf16[1072,512]{1,0:T(8,128)(2,1)S(1)}, bf16[1072,512]{1,0:T(8,128)(2,1)}, u32[]{:S(2)}) copy-start(bf16[1072,512]{1,0:T(8,128)(2,1)} %get-tuple-element.19.refs_1_) | copy-start | bytes 3293188
  10.9 35.1 %copy-start.11 = (s32[5]{0:T(128)S(1)}, s32[5]{0:T(128)}, u32[]{:S(2)}) copy-start(s32[5]{0:T(128)} %stack.38.refs_0_) | copy-start | bytes 64
  10.9 10.3 %collective-permute-start.4 = (bf16[32,512]{1,0:T(8,128)(2,1)}, bf16[32,512]{1,0:T(8,128)(2,1)S(1)}, u32[]{:S(2)}, u32[]{:S(2)}) collective-permute-start(bf16[32,512]{1,0:T(8,128)(2,1)} %get-tuple-element.31), channel_id=1, source_target_pairs={{0,0},{4,4},{1,128},{5,132},{2,256},{6,260},{3,384},{7,388},{128,1... | collective-permute-start | bytes 98312 | tf_op jit(solution)/shard_map/ppermute | solution.py:295
  12.4 9.8 %collective-permute-start.5 = (bf16[32,512]{1,0:T(8,128)(2,1)}, bf16[32,512]{1,0:T(8,128)(2,1)S(1)}, u32[]{:S(2)}, u32[]{:S(2)}) collective-permute-start(bf16[32,512]{1,0:T(8,128)(2,1)} %get-tuple-element.32), channel_id=1, source_target_pairs={{0,4},{4,0},{1,132},{5,128},{2,260},{6,256},{3,388},{7,384},{128,5... | collective-permute-start | bytes 98312 | tf_op jit(solution)/shard_map/ppermute | solution.py:295
  22.3 15.1 %collective-permute-start.8 = (bf16[64,512]{1,0:T(8,128)(2,1)S(1)}, bf16[64,512]{1,0:T(8,128)(2,1)S(1)}, u32[]{:S(2)}, u32[]{:S(2)}) collective-permute-start(bf16[64,512]{1,0:T(8,128)(2,1)S(1)} %get-tuple-element.34), channel_id=1, source_target_pairs={{0,256},{128,384},{256,0},{384,128},{1,257},{129,385},{257,1},{385... | collective-permute-start | bytes 196616 | tf_op jit(solution)/shard_map/ppermute | solution.py:302
  30.9 6.5 %collective-permute-start.7 = (bf16[64,512]{1,0:T(8,128)(2,1)S(1)}, bf16[64,512]{1,0:T(8,128)(2,1)S(1)}, u32[]{:S(2)}, u32[]{:S(2)}) collective-permute-start(bf16[64,512]{1,0:T(8,128)(2,1)S(1)} %get-tuple-element.34), channel_id=1, source_target_pairs={{0,128},{128,256},{256,384},{384,0},{1,129},{129,257},{257,385},{3... | collective-permute-start | bytes 196616 | tf_op jit(solution)/shard_map/ppermute | solution.py:302
  32.8 5.9 %collective-permute-start.6 = (bf16[64,512]{1,0:T(8,128)(2,1)S(1)}, bf16[64,512]{1,0:T(8,128)(2,1)S(1)}, u32[]{:S(2)}, u32[]{:S(2)}) collective-permute-start(bf16[64,512]{1,0:T(8,128)(2,1)S(1)} %get-tuple-element.34), channel_id=1, source_target_pairs={{0,384},{128,0},{256,128},{384,256},{1,385},{129,1},{257,129},{385... | collective-permute-start | bytes 196616 | tf_op jit(solution)/shard_map/ppermute | solution.py:302
  39.4 6.5 %collective-permute-start = (bf16[1072,512]{1,0:T(8,128)(2,1)}, bf16[1072,512]{1,0:T(8,128)(2,1)S(1)}, u32[]{:S(2)}, u32[]{:S(2)}) collective-permute-start(bf16[1072,512]{1,0:T(8,128)(2,1)} %get-tuple-element.20), channel_id=1, source_target_pairs={{0,4},{4,0},{1,5},{5,1},{2,6},{6,2},{3,7},{7,3},{8,12},{12,8},{9,1... | collective-permute-start | bytes 3293192 | tf_op jit(solution)/shard_map/ppermute | solution.py:20
  71.9 48.4 %all-to-all-start.1 = ((bf16[4,528,128]{2,1,0:T(8,128)(2,1)}), bf16[4,528,128]{2,1,0:T(8,128)(2,1)}, u32[]{:S(2)}, u32[]{:S(2)}) async-start(bf16[4,528,128]{2,1,0:T(8,128)(2,1)} %get-tuple-element.27), calls=%async_computation.1 | async-start | bytes 1081344 | tf_op jit(solution)/shard_map/all_to_all | solution.py:311
  84.4 0.9 copy-start.8
  85.3 0.9 copy-start.10
  120.2 9.4 %copy-start.15 = (bf16[1024]{0:T(1024)(128)(2,1)S(1)}, bf16[1024]{0:T(1024)(128)(2,1)}, u32[]{:S(2)}) copy-start(bf16[1024]{0:T(1024)(128)(2,1)} %param.14) | copy-start | bytes 6148
  123.1 13.7 %all-to-all-start.2 = ((bf16[4,528,128]{2,1,0:T(8,128)(2,1)}), bf16[4,528,128]{2,1,0:T(8,128)(2,1)}, u32[]{:S(2)}, u32[]{:S(2)}) async-start(bf16[4,528,128]{2,1,0:T(8,128)(2,1)} %copy-done.4), calls=%async_computation.2 | async-start | bytes 1081344 | tf_op jit(solution)/shard_map/all_to_all | solution.py:320
  129.7 1.0 copy-start.6
  131.9 1.0 copy-start.2
  136.8 1.2 copy-start.3
  141.3 28.3 %copy-start.1 = (bf16[512,512]{1,0:T(8,128)(2,1)}, bf16[512,512]{1,0:T(8,128)(2,1)S(1)}, u32[]{:S(2)}) copy-start(bf16[512,512]{1,0:T(8,128)(2,1)S(1)} %shard_map.88.refs_1_) | copy-start | bytes 1572868
  141.3 13.4 %collective-permute-start.1 = (bf16[512,512]{1,0:T(8,128)(2,1)S(1)}, bf16[512,512]{1,0:T(8,128)(2,1)S(1)}, u32[]{:S(2)}, u32[]{:S(2)}) collective-permute-start(bf16[512,512]{1,0:T(8,128)(2,1)S(1)} %shard_map.88.refs_1_), channel_id=1, source_target_pairs={{0,1},{1,2},{2,3},{3,0},{4,5},{5,6},{6,7},{7,4},{8,9},{9,10},{10,1... | collective-permute-start | bytes 1572872 | tf_op jit(solution)/shard_map/ppermute | solution.py:331
  143.2 19.3 %collective-permute-start.2 = (bf16[512,512]{1,0:T(8,128)(2,1)S(1)}, bf16[512,512]{1,0:T(8,128)(2,1)S(1)}, u32[]{:S(2)}, u32[]{:S(2)}) collective-permute-start(bf16[512,512]{1,0:T(8,128)(2,1)S(1)} %shard_map.88.refs_1_), channel_id=1, source_target_pairs={{0,2},{1,3},{2,0},{3,1},{4,6},{5,7},{6,4},{7,5},{8,10},{9,11},{10,... | collective-permute-start | bytes 1572872 | tf_op jit(solution)/shard_map/ppermute | solution.py:331
  147.1 22.5 %collective-permute-start.3 = (bf16[512,512]{1,0:T(8,128)(2,1)S(1)}, bf16[512,512]{1,0:T(8,128)(2,1)S(1)}, u32[]{:S(2)}, u32[]{:S(2)}) collective-permute-start(bf16[512,512]{1,0:T(8,128)(2,1)S(1)} %shard_map.88.refs_1_), channel_id=1, source_target_pairs={{0,3},{1,0},{2,1},{3,2},{4,7},{5,4},{6,5},{7,6},{8,11},{9,8},{10,9... | collective-permute-start | bytes 1572872 | tf_op jit(solution)/shard_map/ppermute | solution.py:331
  154.7 14.9 %copy-start.12 = (bf16[512,512]{1,0:T(8,128)(2,1)}, bf16[512,512]{1,0:T(8,128)(2,1)S(1)}, u32[]{:S(2)}) copy-start(bf16[512,512]{1,0:T(8,128)(2,1)S(1)} %collective-permute-done.1.refs_2_) | copy-start | bytes 1572868
  162.6 7.0 %copy-start.13 = (bf16[512,512]{1,0:T(8,128)(2,1)}, bf16[512,512]{1,0:T(8,128)(2,1)S(1)}, u32[]{:S(2)}) copy-start(bf16[512,512]{1,0:T(8,128)(2,1)S(1)} %collective-permute-done.2.refs_3_) | copy-start | bytes 1572868
  175.7 10.4 %collective-permute-start.9 = (bf16[256,1024]{1,0:T(8,128)(2,1)}, bf16[256,1024]{1,0:T(8,128)(2,1)S(1)}, u32[]{:S(2)}, u32[]{:S(2)}) collective-permute-start(bf16[256,1024]{1,0:T(8,128)(2,1)} %shard_map.90), channel_id=1, source_target_pairs={{0,4},{4,0},{1,5},{5,1},{2,6},{6,2},{3,7},{7,3},{8,12},{12,8},{9,1... | collective-permute-start | bytes 1572872 | tf_op jit(solution)/shard_map/ppermute | solution.py:20
  (5 other events, 3.7 us)
Sparse Core Ops, SparseCore 0:
  39.6 103.8 all-gather.2

commit v7 on v5

v7 whole, which is shorter than its diff:
```python
import functools

import jax
import jax.numpy as jnp
from jax import lax
from jax.experimental import pallas as pl
from jax.experimental.pallas import tpu as pltpu
from jax.sharding import Mesh, PartitionSpec as P

BF = jnp.bfloat16
F32 = jnp.float32
SEQ = ("y", "a", "p", "q", "c")
NEAR = ("p", "q")
NT = (((1,), (1,)), ((), ()))
TN = (((0,), (0,)), ((), ()))
LOGS = 1024


def swap(value):
    return lax.ppermute(value, "c", [(0, 1), (1, 0)])


def dot(left, right, dims=(((1,), (0,)), ((), ()))):
    return lax.dot_general(left, right, dims, preferred_element_type=F32)


def exact(left, right, dims):
    return lax.dot_general(
        left, right, dims, precision=lax.Precision.HIGHEST, preferred_element_type=F32
    )


def tail(log):
    high = log.astype(BF).astype(F32)
    middle = (log - high).astype(BF).astype(F32)
    low = log - high - middle
    row = lax.broadcasted_iota(jnp.int32, (16, 128), 0)
    return jnp.where(
        row == 0, high, jnp.where(row == 1, middle, jnp.where(row == 2, low, 0.0))
    ).astype(BF)


def untail(tile):
    return jnp.sum(tile.astype(F32), axis=0, keepdims=True)


def call(body, outs, args, unread=(), scratch=(), hbm=(), vmem=12):
    specs = [pl.BlockSpec(memory_space=pltpu.SMEM)]
    specs += [
        pl.BlockSpec(memory_space=pltpu.HBM if i in hbm else pltpu.VMEM)
        for i in range(1, len(args))
    ]
    specs += [pl.BlockSpec(memory_space=pl.ANY)] * len(unread)

    def run(*refs):
        body(*refs[: len(args)], *refs[len(args) + len(unread) :])

    return pl.pallas_call(
        run,
        out_shape=[jax.ShapeDtypeStruct(*o) for o in outs],
        in_specs=specs,
        out_specs=[pl.BlockSpec(memory_space=pltpu.VMEM)] * len(outs),
        scratch_shapes=list(scratch),
        compiler_params=pltpu.CompilerParams(vmem_limit_bytes=vmem * 2**20),
        cost_estimate=pl.CostEstimate(flops=10**6, bytes_accessed=10**6, transcendentals=0),
    )(*args, *unread)


def pack_body(at, keys, values, queries, gates, decay, mix, keep, send, small, levels, sems):
    core = at[0]
    mine = pl.ds(pl.multiple_of(core * 512, 512), 512)
    theirs = pl.ds(pl.multiple_of((1 - core) * 512, 512), 512)
    copies = [
        pltpu.make_async_copy(decay, small, sems.at[0]),
        pltpu.make_async_copy(mix, levels, sems.at[1]),
    ]
    for i, ref in enumerate((keys, values, queries, gates)):
        rows = pl.ds(i * 256, 256)
        for out, cols, n in ((send, theirs, 2), (keep, mine, 6)):
            copies.append(pltpu.make_async_copy(ref.at[:, cols], out.at[rows, :], sems.at[n + i]))
    for copy in copies:
        copy.start()
    for copy in copies[:2]:
        copy.wait()
    for out, low in ((keep, core == 0), (send, core == 1)):
        logs = [jnp.where(low, small[0:4], small[4:8])]
        logs += [jnp.where(low, levels[l, 0:4], levels[l, 4:8]) for l in range(8)]
        logs = jnp.concatenate(logs + [jnp.zeros((12, 256), F32)], axis=0)
        high = logs.astype(BF)
        out[LOGS:, 0:256] = high
        out[LOGS:, 256:512] = (logs - high.astype(F32)).astype(BF)
    for copy in copies[2:]:
        copy.wait()


def logs_of(block):
    tile = block[LOGS:, :].astype(F32)
    return tile[:, 0:256] + tile[:, 256:512]


def ends_body(at, keep, got, pay, first):
    core = at[0]
    logs = jnp.concatenate([logs_of(keep)[0:4], logs_of(got)[0:4]], axis=0)
    after = (
        lax.broadcasted_iota(jnp.int32, (256, 256), 1)
        > lax.broadcasted_iota(jnp.int32, (256, 256), 0)
    ).astype(F32)
    scale = jnp.exp(exact(after, logs, NT))
    total = jnp.sum(logs, axis=1, keepdims=True)
    for h in range(4):
        cols = slice(h * 128, h * 128 + 128)
        end = []
        for i, ref in enumerate((keep, got)):
            scaled = ref[0:256, cols].astype(F32) * scale[:, 4 * i + h : 4 * i + h + 1]
            end.append(dot(scaled.astype(BF), ref[256:512, cols], TN))
        own_log, got_log = total[h : h + 1], total[4 + h : 5 + h]
        own_later = jnp.exp(jnp.where(core == 0, got_log, 0.0))
        got_later = jnp.exp(jnp.where(core == 0, 0.0, own_log))
        pay[h, 0:128, :] = (end[0] * own_later + end[1] * got_later).astype(BF)
        pay[h, 128:144, :] = tail(own_log + got_log)
        first[h, :, :] = jnp.where(core == 0, end[0], end[1]).astype(BF)


def blocks_of(got):
    s = [got[i, 0:128, :].astype(F32) for i in range(4)]
    t = [untail(got[i, 128:144, :]) for i in range(4)]
    pair = s[0] * jnp.exp(t[1]) + s[1]
    return s, t, pair


def send_whole(s, t, pair, pay):
    state = (pair * jnp.exp(t[2] + t[3]) + s[2] * jnp.exp(t[3]) + s[3]).astype(BF)
    log = tail(t[0] + t[1] + t[2] + t[3])
    for i in range(4):
        pay[i, 0:128, :] = state
        pay[i, 128:144, :] = log


def lower_states(s, t, pair, at):
    odd, upper = at % 2 == 1, at >= 2
    one = jnp.where(odd, jnp.where(upper, s[2], s[0]), 0.0)
    step = jnp.where(odd, jnp.where(upper, t[2], t[0]), 0.0)
    two = jnp.where(upper, pair * jnp.exp(step), 0.0)
    before = sum(jnp.where(at > i, t[i], 0.0) for i in range(3))
    return one, two, before


def near_body(at, near, pay):
    send_whole(*blocks_of(near), pay)


def far_body(at, near, far, pay, m0, m1, m2, m3, before_out):
    s, t, pair = blocks_of(far)
    send_whole(s, t, pair, pay)
    three, four, before = lower_states(s, t, pair, at[2])
    before_out[...] = jnp.broadcast_to(before, (8, 128))
    s, t, pair = blocks_of(near)
    for k, message in enumerate((m0, m1, m2, m3)):
        one, two, before = lower_states(s, t, pair, at[1] ^ k)
        for i, state in enumerate((one, two, three, four)):
            message[0:128, i * 128 : i * 128 + 128] = state.astype(BF)
        message[128:144, 0:128] = tail(before)
        message[128:144, 128:512] = jnp.zeros((16, 384), BF)


def last_body(at, last, before, message):
    one, two, _ = lower_states(*blocks_of(last), at[3])
    earlier = jnp.exp(before[0:1, :])
    one, two = (one * earlier).astype(BF), (two * earlier).astype(BF)
    for i in range(4):
        message[i, :, 0:128] = one
        message[i, :, 128:256] = two


def place(s, core):
    at = core if s == 0 else 1 - core
    return at, pl.ds(pl.multiple_of(at * 256, 256), 256)


def own_body(at, keep, got, first, mixture, coef):
    core = at[0]
    rows = lax.broadcasted_iota(jnp.int32, (256, 256), 0)
    cols = lax.broadcasted_iota(jnp.int32, (256, 256), 1)
    lower = rows >= cols
    upto = lower.astype(F32)
    both = (logs_of(keep), logs_of(got))
    for s, ref in enumerate((keep, got)):
        second, here = place(s, core)
        logs = both[s]
        at_row = exact(logs[0:8], upto, NT)
        at_col = exact(upto, logs[0:8], NT)
        level = logs.T
        first_log = jnp.sum(both[1 - s][0:4], axis=1, keepdims=True)
        first_log = jnp.where(second == 1, first_log, 0.0)
        for h in range(4):
            hc = slice(h * 128, h * 128 + 128)
            q, kb, v = ref[512:768, hc], ref[0:256, hc], ref[256:512, hc]
            local = at_col[:, h : h + 1]
            gap = jnp.where(lower, local - at_row[h : h + 1, :], -1e30)
            weights = (dot(q, kb, NT) * jnp.exp(gap)).astype(BF)
            m = [level[:, 4 + 4 * l + h : 5 + 4 * l + h] for l in range(8)]
            total = dot(weights, v) * m[0]
            start = jnp.exp(local)
            total += dot(q, first[h]) * jnp.where(second == 1, start * m[1], 0.0)
            mixture[here, hc] = total
            start = start * jnp.exp(first_log[h : h + 1])
            for l in range(2, 8):
                coef[here, 6 * h + l - 2 : 6 * h + l - 1] = start * m[l]


def mix_body(at, keep, got, mixture, coef, m0, m1, m2, m3, mixed, later, states):
    for k, message in enumerate((m0, m1, m2, m3)):
        states[at[1] ^ k] = message[...]
    for h in range(4):
        before = jnp.exp(untail(states[h, 128:144, 0:128])[:, 0:1])
        hc = slice(h * 128, h * 128 + 128)
        for s, ref in enumerate((keep, got)):
            _, here = place(s, at[0])
            total = mixture[here, hc]
            for l in range(4):
                if l % 2 == 0:
                    read = dot(ref[512:768, hc], states[h, 0:128, l * 128 : l * 128 + 256])
                scale = coef[here, 6 * h + l : 6 * h + l + 1]
                scale = scale if l < 2 else scale * before
                total += read[:, (l % 2) * 128 : (l % 2) * 128 + 128] * scale
            mixed[here, hc] = total
            later[here, 2 * h : 2 * h + 2] = coef[here, 6 * h + 4 : 6 * h + 6] * before


def norm_body(at, keep, got, gain, mixture, coef, last, normed):
    core = at[0]
    for h in range(4):
        mine = pl.ds(pl.multiple_of(core * 512 + h * 128, 128), 128)
        hc = slice(h * 128, h * 128 + 128)
        for s, ref in enumerate((keep, got)):
            _, here = place(s, core)
            z = ref[768:1024, hc].astype(F32)
            read = dot(ref[512:768, hc], last[h])
            total = mixture[here, hc]
            total += read[:, 0:128] * coef[here, 2 * h : 2 * h + 1]
            total += read[:, 128:256] * coef[here, 2 * h + 1 : 2 * h + 2]
            gated = total * (z / (1.0 + jnp.exp(-z)))
            size = lax.rsqrt(jnp.mean(gated * gated, axis=1, keepdims=True) + 1e-05)
            normed[here, hc] = (gated * size * gain[:, mine].astype(F32)).astype(BF)


def project_body(
    other, at, a0, a1, a2, a3, b0, b1, b2, b3, gathered, w1, w2, w3, out, left, right, sems
):
    row = (1 - at[0]) if other else at[0]
    rows = pl.ds(pl.multiple_of(row * 256, 256), 256)
    pieces = [gathered.at[:, 0:512], gathered.at[:, 512:1024]]
    pieces += [gathered.at[:, 512 + 512 * k : 1024 + 512 * k] for k in (1, 2, 3)] + [w1, w2, w3]
    copies = [
        pltpu.make_async_copy(piece, right.at[i], sems.at[i]) for i, piece in enumerate(pieces)
    ]
    for copy in copies:
        copy.start()
    for j, (own, got) in enumerate(((a0, b0), (a1, b1), (a2, b2), (a3, b3))):
        spot = (at[4] + 4 - j) % 4
        left[at[0], spot] = own[rows, :]
        left[1 - at[0], spot] = got[rows, :]
    total = 0.0
    for i, (half, k) in enumerate(
        ((0, 0), (1, 0), (0, 1), (0, 2), (0, 3), (1, 1), (1, 2), (1, 3))
    ):
        copies[i].wait()
        total += dot(left[half, (at[3] + 4 - k) % 4], right[i], NT)
    out[...] = total.astype(BF)


def project(at, owns, gots, gathered, lates, other):
    return call(
        functools.partial(project_body, other),
        [((256, 512), BF)],
        (at, *owns, *gots, gathered, *lates),
        scratch=[
            pltpu.VMEM((2, 4, 256, 512), BF),
            pltpu.VMEM((8, 512, 512), BF),
            pltpu.SemaphoreType.DMA((8,)),
        ],
        hbm=range(9, 13),
        vmem=20,
    )[0]


def weave_body(at, own, got, out):
    core = at[0]
    i = lax.broadcasted_iota(jnp.int32, (128, 256), 0)
    j = lax.broadcasted_iota(jnp.int32, (128, 256), 1)
    spot = (i >> 5) * 64 + (i & 31)
    mine = (j == spot + core * 32).astype(BF)
    theirs = (j == spot + (1 - core) * 32).astype(BF)
    for m in range(4):
        cols = slice(m * 128, m * 128 + 128)
        both = dot(own[:, cols], mine) + dot(got[:, cols], theirs)
        out[:, m * 256 : m * 256 + 256] = both.astype(BF)


def shift(value, axis, by):
    return lax.ppermute(value, axis, [(i, (i + by) % 4) for i in range(4)])


def shards(values, keys, queries, gates, log_decay, level_mix, norm_gain, weight):
    y, a, b, c, x = (lax.axis_index(n) for n in ("y", "a", NEAR, "c", "x"))
    at = jnp.stack([c, b, a, y, x]).astype(jnp.int32)
    block = ((LOGS + 48, 512), BF)
    keep, send = call(
        pack_body,
        [block, block],
        (at, keys, values, queries, gates, log_decay, level_mix),
        scratch=[
            pltpu.VMEM((8, 256), F32),
            pltpu.VMEM((8, 8, 256), F32),
            pltpu.SemaphoreType.DMA((10,)),
        ],
        hbm=range(1, 7),
        vmem=60,
    )
    got = swap(send)
    mine = []
    for k in range(4):
        perm = [(s * 4 + f, ((f + k) % 4) * 4 + s) for s in range(4) for f in range(4)]
        mine.append(lax.ppermute(weight[:, : 512 if k else 1024], ("y", "x"), perm))
    mine = jnp.concatenate(mine, axis=1)
    gathered = lax.all_gather(mine, ("a", "p", "q"), axis=0, tiled=True)
    late = gathered[:, 512:1024]
    lates = [shift(late, "y", k) for k in (1, 2, 3)]

    pay = ((4, 144, 128), BF)
    pay_b, first = call(ends_body, [pay, ((4, 128, 128), BF)], (at, keep, got))
    near = lax.all_to_all(pay_b, NEAR, 0, 0, tiled=True)
    (pay_a,) = call(near_body, [pay], (at, near))
    far = lax.all_to_all(pay_a, "a", 0, 0, tiled=True)
    mixture, coef = call(
        own_body, [((512, 512), F32), ((512, 24), F32)], (at, keep, got, first)
    )
    pay_y, *messages, before = call(
        far_body,
        [pay] + [((144, 512), BF)] * 4 + [((8, 128), F32)],
        (at, near, far),
        unread=(mixture,),
    )
    last = lax.all_to_all(pay_y, "y", 0, 0, tiled=True)
    messages = messages[:1] + [
        lax.ppermute(messages[k], NEAR, [(i, i ^ k) for i in range(4)]) for k in (1, 2, 3)
    ]
    (last,) = call(last_body, [((4, 128, 256), BF)], (at, last, before))
    last = lax.all_to_all(last, NEAR, 0, 0, tiled=True)
    mixture, coef = call(
        mix_body,
        [((512, 512), F32), ((512, 8), F32)],
        (at, keep, got, mixture, coef, *messages),
        scratch=[pltpu.VMEM((4, 144, 512), BF)],
    )
    (normed,) = call(
        norm_body, [((512, 512), BF)], (at, keep, got, norm_gain[None], mixture, coef, last)
    )

    owns = [normed] + [shift(normed, "x", j) for j in (1, 2, 3)]
    gots = [swap(block) for block in owns]
    theirs = swap(project(at, owns, gots, gathered, lates, True))
    own = project(at, owns, gots, gathered, lates, False)
    return call(weave_body, [((256, 1024), BF)], (at, own, theirs))[0]


def solution(mesh):
    fine = Mesh(mesh.devices.reshape(4, 4, 2, 2, 2, 4), SEQ + ("x",))
    return jax.shard_map(
        shards,
        mesh=fine,
        in_specs=(
            P(SEQ, "x"),
            P(SEQ, "x"),
            P(SEQ, "x"),
            P(SEQ, "x"),
            P("x", SEQ),
            P(None, "x", SEQ),
            P("x"),
            P(SEQ, "x"),
        ),
        out_specs=P(SEQ, "x"),
        check_vma=False,
    )
```

time: 191 us -> 221 us (1.16); the launches traced: 190 us -> 217 us
  blocking collectives: 7.87 us -> 23 us
  waiting for transfers between devices: 39.2 us -> 47.7 us
  Pallas kernels: 21.9 us -> 26.9 us
    all_to_all x1 -> x2, blocking collectives: 7.87 us -> 23 us  [the longest x1 13.5 us: shards(): near = lax.all_to_all(pay_b, NEAR, 0, 0, tiled=True)]
    all_to_all x2 -> x1, starting transfers between devices: 24.5 us -> 11.5 us  [shards(): far = lax.all_to_all(pay_a, 'a', 0, 0, tiled=True)]
    ppermute x2 -> x6, starting transfers between devices: 17.8 us -> 27.3 us  [swap(): return lax.ppermute(value, 'c', [(0, 1), (1, 0)])]
    pallas_call x10 -> x11, Pallas kernels: 21.9 us -> 26.9 us  [call(): pl.pallas_call(run, out_shape=[jax.ShapeDtypeStruct(*o) for o in outs], i...]
    ppermute x12 -> x13, starting transfers between devices: 44.4 us -> 48.8 us  [the longest x6 22.3 us: shift(): return lax.ppermute(value, axis, [(i, (i + by) % 4) for i in range(4)])]
    ppermute x12 -> x13, waiting for transfers between devices: 31.3 us -> 34.3 us  [the longest x6 22.6 us: shift(): return lax.ppermute(value, axis, [(i, (i + by) % 4) for i in range(4)])]
    all_to_all x2 -> x1, waiting for transfers between devices: 7.83 us -> 10.8 us  [shards(): far = lax.all_to_all(pay_a, 'a', 0, 0, tiled=True)]
    ppermute x2 -> x6, waiting for transfers between devices: 0.01 us -> 2.56 us  [swap(): return lax.ppermute(value, 'c', [(0, 1), (1, 0)])]
  transfers between devices with their start and end apart: 18 -> 22, of which waited for: 6 -> 9; matrix products, arithmetic and copies ran while one was open for 1% -> 1% of each run, Pallas kernels for 9% -> 10%
where the time goes in v7:
time: 221 us; the launch traced here: 217 us
  starting transfers between devices  91 us (41%)
  waiting for transfers between devices  47.7 us (22%)
  Pallas kernels  26.9 us (12%)
  blocking collectives  23 us (10%)
  local copies, waits for them, and re-layouts  14.1 us (6%)
  between operations  13.7 us (6%)
    ppermute x6, starting transfers between devices, swap(): return lax.ppermute(value, 'c', [(0, 1), (1, 0)])  27.3 us
    pallas_call x11, Pallas kernels, call(): pl.pallas_call(run, out_shape=[jax.ShapeDtypeStruct(*o) for o in outs], i...  26.9 us
    ppermute x6, waiting for transfers between devices, shift(): return lax.ppermute(value, axis, [(i, (i + by) % 4) for i in range(4)])  22.6 us
    ppermute x6, starting transfers between devices, shift(): return lax.ppermute(value, axis, [(i, (i + by) % 4) for i in range(4)])  22.3 us
    ppermute x4, starting transfers between devices, shards(): mine.append(lax.ppermute(weight[:, :512 if k else 1024], ('y', 'x'), perm))  17.2 us
    all_to_all x1, blocking collectives, shards(): near = lax.all_to_all(pay_b, NEAR, 0, 0, tiled=True)  13.5 us
    unnamed x36, local copies, waits for them, and re-layouts  11.7 us
    all_to_all x1, starting transfers between devices, shards(): far = lax.all_to_all(pay_a, 'a', 0, 0, tiled=True)  11.5 us
  transfers between devices with their start and end apart: 22, of which 9 were waited for; matrix products, arithmetic and copies ran while one was open for 1% of the time, Pallas kernels for 10%

profile of v7, /device:TPU:1, one launch (start us, length us, event | category | flops | bytes accessed | tf_op | source)
XLA Modules:
  0.0 217.2 jit_solution(7335193284743799532)
XLA Ops:
  8.8 5.5 %collective-permute-start.12 = (bf16[32,512]{1,0:T(8,128)(2,1)S(1)}, bf16[32,512]{1,0:T(8,128)(2,1)S(1)}, u32[]{:S(2)}, u32[]{:S(2)}) collective-permute-start(bf16[32,512]{1,0:T(8,128)(2,1)S(1)} %slice.8), channel_id=1, source_target_pairs={{0,128},{1,256},{2,384},{3,0},{128,129},{129,257},{130,385},{131,1... | collective-permute-start | bytes 98312 | tf_op jit(solution)/shard_map/ppermute | solution.py:324
  14.3 6.3 %collective-permute-start.13 = (bf16[32,512]{1,0:T(8,128)(2,1)S(1)}, bf16[32,512]{1,0:T(8,128)(2,1)S(1)}, u32[]{:S(2)}, u32[]{:S(2)}) collective-permute-start(bf16[32,512]{1,0:T(8,128)(2,1)S(1)} %slice.8), channel_id=1, source_target_pairs={{0,256},{1,384},{2,0},{3,128},{128,257},{129,385},{130,1},{131,129... | collective-permute-start | bytes 98312 | tf_op jit(solution)/shard_map/ppermute | solution.py:324
  20.7 3.9 %collective-permute-start.14 = (bf16[32,512]{1,0:T(8,128)(2,1)S(1)}, bf16[32,512]{1,0:T(8,128)(2,1)S(1)}, u32[]{:S(2)}, u32[]{:S(2)}) collective-permute-start(bf16[32,512]{1,0:T(8,128)(2,1)S(1)} %slice.8), channel_id=1, source_target_pairs={{0,384},{1,0},{2,128},{3,256},{128,385},{129,1},{130,129},{131,257... | collective-permute-start | bytes 98312 | tf_op jit(solution)/shard_map/ppermute | solution.py:324
  28.4 3.8 %shard_map.82 = (bf16[1072,512]{1,0:T(8,128)(2,1)}, bf16[1072,512]{1,0:T(8,128)(2,1)}) custom-call(s32[5]{0:T(128)} %stack.23.refs_0_, bf16[256,1024]{1,0:T(8,128)(2,1)} %refs_1_.1, bf16[256,1024]{1,0:T(8,128)(2,1)} %refs_2_.1, bf16[256,1024]{1,0:T(8,128)(2,1)} %refs_3_.1, bf16[256,1024]{1,0:T(8,128)(2,1)} %refs_4_.1, f32[8,256]{1,0:T(8,128)} %refs_5_.1, ...), custom_call_target="tpu_custom_call" | custom-call | flops 1000000 | bytes 1000000 | tf_op jit(solution)/shard_map/pallas_call | solution.py:58
  32.3 4.2 %collective-permute-start = (bf16[1072,512]{1,0:T(8,128)(2,1)}, bf16[1072,512]{1,0:T(8,128)(2,1)S(1)}, u32[]{:S(2)}, u32[]{:S(2)}) collective-permute-start(bf16[1072,512]{1,0:T(8,128)(2,1)} %get-tuple-element.20), channel_id=1, source_target_pairs={{0,4},{4,0},{1,5},{5,1},{2,6},{6,2},{3,7},{7,3},{8,12},{12,8},{9,1... | collective-permute-start | bytes 3293192 | tf_op jit(solution)/shard_map/ppermute | solution.py:20
  42.1 13.5 %all_to_all.20.refs_1_ = bf16[4,144,128]{2,1,0:T(8,128)(2,1)S(1)} all-to-all(bf16[4,144,128]{2,1,0:T(8,128)(2,1)S(1)} %get-tuple-element.24), channel_id=1, replica_groups=mesh['y'=4,'a'=4,'p'=2,'q'=2,'c'=2,'x'=4] {'p','q'}, dimensions={0} | all-to-all | bytes 294912 | tf_op jit(solution)/shard_map/all_to_all | solution.py:332
  56.8 11.5 %all-to-all-start.1 = ((bf16[4,144,128]{2,1,0:T(8,128)(2,1)}), bf16[4,144,128]{2,1,0:T(8,128)(2,1)S(1)}, u32[]{:S(2)}, u32[]{:S(2)}) async-start(bf16[4,144,128]{2,1,0:T(8,128)(2,1)} %shard_map.85), calls=%async_computation.1 | async-start | bytes 294912 | tf_op jit(solution)/shard_map/all_to_all | solution.py:334
  69.2 4.4 %shard_map.84 = (f32[512,512]{1,0:T(8,128)S(1)}, f32[512,24]{1,0:T(8,128)S(1)}) custom-call(s32[5]{0:T(128)S(1)} %copy-done.13, bf16[1072,512]{1,0:T(8,128)(2,1)S(1)} %copy-done.1, bf16[1072,512]{1,0:T(8,128)(2,1)S(1)} %collective-permute-done.refs_2_, bf16[4,128,128]{2,1,0:T(8,128)(2,1)S(1)} %copy-done.12), custom_call_target="tpu_custom_call" | custom-call | flops 1000000 | bytes 1000000 | tf_op jit(solution)/shard_map/pallas_call | solution.py:58
  74.3 10.8 %all-to-all-done.1.refs_2_ = bf16[4,144,128]{2,1,0:T(8,128)(2,1)S(1)} async-done(((bf16[4,144,128]{2,1,0:T(8,128)(2,1)}), bf16[4,144,128]{2,1,0:T(8,128)(2,1)S(1)}, u32[]{:S(2)}, u32[]{:S(2)}) %all-to-all-start.1) | async-done | bytes 147488 | tf_op jit(solution)/shard_map/all_to_all | solution.py:334
  87.1 9.6 %all_to_all.21.refs_1_ = bf16[4,144,128]{2,1,0:T(8,128)(2,1)S(1)} all-to-all(bf16[4,144,128]{2,1,0:T(8,128)(2,1)S(1)} %get-tuple-element.31), channel_id=1, replica_groups=mesh['y'=4,'a'=4,'p'=2,'q'=2,'c'=2,'x'=4] {'y'}, dimensions={0} | all-to-all | bytes 294912 | tf_op jit(solution)/shard_map/all_to_all | solution.py:344
  98.0 3.4 %all-to-all-start.3 = ((bf16[4,128,256]{2,1,0:T(8,128)(2,1)}), bf16[4,128,256]{2,1,0:T(8,128)(2,1)S(1)}, u32[]{:S(2)}, u32[]{:S(2)}) async-start(bf16[4,128,256]{2,1,0:T(8,128)(2,1)} %shard_map.88), calls=%async_computation.3 | async-start | bytes 524288 | tf_op jit(solution)/shard_map/all_to_all | solution.py:349
  104.7 4.0 %collective-permute-start.2 = (bf16[144,512]{1,0:T(8,128)(2,1)}, bf16[144,512]{1,0:T(8,128)(2,1)S(1)}, u32[]{:S(2)}, u32[]{:S(2)}) collective-permute-start(bf16[144,512]{1,0:T(8,128)(2,1)} %copy-done.15), channel_id=1, source_target_pairs={{0,16},{8,24},{16,0},{24,8},{1,17},{9,25},{17,1},{25,9},{2,18},{10... | collective-permute-start | bytes 442376 | tf_op jit(solution)/shard_map/ppermute | solution.py:346
  113.5 6.4 %collective-permute-done.2.refs_7_ = bf16[144,512]{1,0:T(8,128)(2,1)S(1)} collective-permute-done((bf16[144,512]{1,0:T(8,128)(2,1)}, bf16[144,512]{1,0:T(8,128)(2,1)S(1)}, u32[]{:S(2)}, u32[]{:S(2)}) %collective-permute-start.2) | collective-permute-done | bytes 147488 | tf_op jit(solution)/shard_map/ppermute | solution.py:346
  135.7 4.8 %collective-permute-start.5 = (bf16[512,512]{1,0:T(8,128)(2,1)S(1)}, bf16[512,512]{1,0:T(8,128)(2,1)S(1)}, u32[]{:S(2)}, u32[]{:S(2)}) collective-permute-start(bf16[512,512]{1,0:T(8,128)(2,1)S(1)} %shard_map.89.refs_1_), channel_id=1, source_target_pairs={{0,2},{1,3},{2,0},{3,1},{4,6},{5,7},{6,4},{7,5},{8,10},{9,11},{10,... | collective-permute-start | bytes 1572872 | tf_op jit(solution)/shard_map/ppermute | solution.py:301
  140.5 5.4 %collective-permute-start.7 = (bf16[512,512]{1,0:T(8,128)(2,1)S(1)}, bf16[512,512]{1,0:T(8,128)(2,1)S(1)}, u32[]{:S(2)}, u32[]{:S(2)}) collective-permute-start(bf16[512,512]{1,0:T(8,128)(2,1)S(1)} %shard_map.89.refs_1_), channel_id=1, source_target_pairs={{0,4},{4,0},{1,5},{5,1},{2,6},{6,2},{3,7},{7,3},{8,12},{12,8},{9,1... | collective-permute-start | bytes 1572872 | tf_op jit(solution)/shard_map/ppermute | solution.py:20
  145.9 6.8 %collective-permute-start.10 = (bf16[512,512]{1,0:T(8,128)(2,1)S(1)}, bf16[512,512]{1,0:T(8,128)(2,1)S(1)}, u32[]{:S(2)}, u32[]{:S(2)}) collective-permute-start(bf16[512,512]{1,0:T(8,128)(2,1)S(1)} %collective-permute-done.6.refs_4_), channel_id=1, source_target_pairs={{0,4},{4,0},{1,5},{5,1},{2,6},{6,2},{3,7},{7,3},{8,12},{12,8},{9,1... | collective-permute-start | bytes 1572872 | tf_op jit(solution)/shard_map/ppermute | solution.py:20
  154.7 4.2 %collective-permute-done.5.refs_3_ = bf16[512,512]{1,0:T(8,128)(2,1)S(1)} collective-permute-done((bf16[512,512]{1,0:T(8,128)(2,1)S(1)}, bf16[512,512]{1,0:T(8,128)(2,1)S(1)}, u32[]{:S(2)}, u32[]{:S(2)}) %collective-permute-start.5) | collective-permute-done | bytes 524320 | tf_op jit(solution)/shard_map/ppermute | solution.py:301
  158.9 5.7 %collective-permute-start.9 = (bf16[512,512]{1,0:T(8,128)(2,1)S(1)}, bf16[512,512]{1,0:T(8,128)(2,1)}, u32[]{:S(2)}, u32[]{:S(2)}) collective-permute-start(bf16[512,512]{1,0:T(8,128)(2,1)S(1)} %collective-permute-done.5.refs_3_), channel_id=1, source_target_pairs={{0,4},{4,0},{1,5},{5,1},{2,6},{6,2},{3,7},{7,3},{8,12},{12,8},{9,1... | collective-permute-start | bytes 1572872 | tf_op jit(solution)/shard_map/ppermute | solution.py:20
  165.7 5.9 %collective-permute-start.15 = (bf16[512,512]{1,0:T(8,128)(2,1)S(1)}, bf16[512,512]{1,0:T(8,128)(2,1)S(1)}, u32[]{:S(2)}, u32[]{:S(2)}) collective-permute-start(bf16[512,512]{1,0:T(8,128)(2,1)S(1)} %slice.10), channel_id=1, source_target_pairs={{0,128},{128,256},{256,384},{384,0},{1,129},{129,257},{257,385},{3... | collective-permute-start | bytes 1572872 | tf_op jit(solution)/shard_map/ppermute | solution.py:301
  174.3 3.8 %collective-permute-start.17 = (bf16[512,512]{1,0:T(8,128)(2,1)S(1)}, bf16[512,512]{1,0:T(8,128)(2,1)S(1)}, u32[]{:S(2)}, u32[]{:S(2)}) collective-permute-start(bf16[512,512]{1,0:T(8,128)(2,1)S(1)} %slice.10), channel_id=1, source_target_pairs={{0,384},{128,0},{256,128},{384,256},{1,385},{129,1},{257,129},{385... | collective-permute-start | bytes 1572872 | tf_op jit(solution)/shard_map/ppermute | solution.py:301
  178.0 4.9 %collective-permute-done.15.refs_10_ = bf16[512,512]{1,0:T(8,128)(2,1)S(1)} collective-permute-done((bf16[512,512]{1,0:T(8,128)(2,1)S(1)}, bf16[512,512]{1,0:T(8,128)(2,1)S(1)}, u32[]{:S(2)}, u32[]{:S(2)}) %collective-permute-start.15) | collective-permute-done | bytes 524320 | tf_op jit(solution)/shard_map/ppermute | solution.py:301
  183.0 12.1 %collective-permute-done.16.refs_11_ = bf16[512,512]{1,0:T(8,128)(2,1)S(1)} collective-permute-done((bf16[512,512]{1,0:T(8,128)(2,1)S(1)}, bf16[512,512]{1,0:T(8,128)(2,1)S(1)}, u32[]{:S(2)}, u32[]{:S(2)}) %collective-permute-start.16) | collective-permute-done | bytes 524320 | tf_op jit(solution)/shard_map/ppermute | solution.py:301
  198.2 3.6 %shard_map.91 = bf16[256,512]{1,0:T(8,128)(2,1)S(1)} custom-call(s32[5]{0:T(128)S(1)} %copy-done.13, bf16[512,512]{1,0:T(8,128)(2,1)S(1)} %shard_map.89.refs_1_, bf16[512,512]{1,0:T(8,128)(2,1)S(1)} %collective-permute-done.4.refs_2_, bf16[512,512]{1,0:T(8,128)(2,1)S(1)} %collective-permute-done.5.refs_3_, ...), custom_call_target="tpu_custom_call" | custom-call | flops 1000000 | bytes 1000000 | tf_op jit(solution)/shard_map/pallas_call | solution.py:58
  205.0 3.6 %shard_map.90.refs_1_ = bf16[256,512]{1,0:T(8,128)(2,1)S(1)} custom-call(s32[5]{0:T(128)S(1)} %copy-done.13, bf16[512,512]{1,0:T(8,128)(2,1)S(1)} %shard_map.89.refs_1_, bf16[512,512]{1,0:T(8,128)(2,1)S(1)} %collective-permute-done.4.refs_2_, bf16[512,512]{1,0:T(8,128)(2,1)S(1)} %collective-permute-done.5.refs_3_, ...), custom_call_target="tpu_custom_call" | custom-call | flops 1000000 | bytes 1000000 | tf_op jit(solution)/shard_map/pallas_call | solution.py:58
  (75 shorter events, 55.6 us)
Async XLA Ops:
  6.5 158.1 %all-gather.2.cloned.1.call-start = ((), (), s32[]{:S(2)}) async-start(), calls=%async_computation.4 | async-start | bytes 2785280 | tf_op jit(solution)/shard_map/all_gather | solution.py:326
  6.5 20.6 %collective-permute-start.11 = (bf16[32,1024]{1,0:T(8,128)(2,1)}, bf16[32,1024]{1,0:T(8,128)(2,1)S(1)}, u32[]{:S(2)}, u32[]{:S(2)}) collective-permute-start(bf16[32,1024]{1,0:T(8,128)(2,1)} %param.15), channel_id=1, source_target_pairs={{0,0},{1,128},{2,256},{3,384},{128,1},{129,129},{130,257},{131,385... | collective-permute-start | bytes 196616 | tf_op jit(solution)/shard_map/ppermute | solution.py:324
  8.8 15.8 %collective-permute-start.12 = (bf16[32,512]{1,0:T(8,128)(2,1)S(1)}, bf16[32,512]{1,0:T(8,128)(2,1)S(1)}, u32[]{:S(2)}, u32[]{:S(2)}) collective-permute-start(bf16[32,512]{1,0:T(8,128)(2,1)S(1)} %slice.8), channel_id=1, source_target_pairs={{0,128},{1,256},{2,384},{3,0},{128,129},{129,257},{130,385},{131,1... | collective-permute-start | bytes 98312 | tf_op jit(solution)/shard_map/ppermute | solution.py:324
  14.3 10.2 %collective-permute-start.13 = (bf16[32,512]{1,0:T(8,128)(2,1)S(1)}, bf16[32,512]{1,0:T(8,128)(2,1)S(1)}, u32[]{:S(2)}, u32[]{:S(2)}) collective-permute-start(bf16[32,512]{1,0:T(8,128)(2,1)S(1)} %slice.8), channel_id=1, source_target_pairs={{0,256},{1,384},{2,0},{3,128},{128,257},{129,385},{130,1},{131,129... | collective-permute-start | bytes 98312 | tf_op jit(solution)/shard_map/ppermute | solution.py:324
  20.7 6.4 %collective-permute-start.14 = (bf16[32,512]{1,0:T(8,128)(2,1)S(1)}, bf16[32,512]{1,0:T(8,128)(2,1)S(1)}, u32[]{:S(2)}, u32[]{:S(2)}) collective-permute-start(bf16[32,512]{1,0:T(8,128)(2,1)S(1)} %slice.8), channel_id=1, source_target_pairs={{0,384},{1,0},{2,128},{3,256},{128,385},{129,1},{130,129},{131,257... | collective-permute-start | bytes 98312 | tf_op jit(solution)/shard_map/ppermute | solution.py:324
  32.3 6.7 %collective-permute-start = (bf16[1072,512]{1,0:T(8,128)(2,1)}, bf16[1072,512]{1,0:T(8,128)(2,1)S(1)}, u32[]{:S(2)}, u32[]{:S(2)}) collective-permute-start(bf16[1072,512]{1,0:T(8,128)(2,1)} %get-tuple-element.20), channel_id=1, source_target_pairs={{0,4},{4,0},{1,5},{5,1},{2,6},{6,2},{3,7},{7,3},{8,12},{12,8},{9,1... | collective-permute-start | bytes 3293192 | tf_op jit(solution)/shard_map/ppermute | solution.py:20
  40.3 28.0 %copy-start.1 = (bf16[1072,512]{1,0:T(8,128)(2,1)S(1)}, bf16[1072,512]{1,0:T(8,128)(2,1)}, u32[]{:S(2)}) copy-start(bf16[1072,512]{1,0:T(8,128)(2,1)} %get-tuple-element.19.refs_1_) | copy-start | bytes 3293188
  56.8 28.3 %all-to-all-start.1 = ((bf16[4,144,128]{2,1,0:T(8,128)(2,1)}), bf16[4,144,128]{2,1,0:T(8,128)(2,1)S(1)}, u32[]{:S(2)}, u32[]{:S(2)}) async-start(bf16[4,144,128]{2,1,0:T(8,128)(2,1)} %shard_map.85), calls=%async_computation.1 | async-start | bytes 294912 | tf_op jit(solution)/shard_map/all_to_all | solution.py:334
  85.1 25.6 %copy-start.17 = (bf16[1024]{0:T(1024)(128)(2,1)S(1)}, bf16[1024]{0:T(1024)(128)(2,1)}, u32[]{:S(2)}) copy-start(bf16[1024]{0:T(1024)(128)(2,1)} %param.14) | copy-start | bytes 6148
  98.0 28.0 %all-to-all-start.3 = ((bf16[4,128,256]{2,1,0:T(8,128)(2,1)}), bf16[4,128,256]{2,1,0:T(8,128)(2,1)S(1)}, u32[]{:S(2)}, u32[]{:S(2)}) async-start(bf16[4,128,256]{2,1,0:T(8,128)(2,1)} %shard_map.88), calls=%async_computation.3 | async-start | bytes 524288 | tf_op jit(solution)/shard_map/all_to_all | solution.py:349
  101.4 12.1 %collective-permute-start.1 = (bf16[144,512]{1,0:T(8,128)(2,1)}, bf16[144,512]{1,0:T(8,128)(2,1)S(1)}, u32[]{:S(2)}, u32[]{:S(2)}) collective-permute-start(bf16[144,512]{1,0:T(8,128)(2,1)} %copy-done.16), channel_id=1, source_target_pairs={{0,8},{8,0},{16,24},{24,16},{1,9},{9,1},{17,25},{25,17},{2,10},{10... | collective-permute-start | bytes 442376 | tf_op jit(solution)/shard_map/ppermute | solution.py:346
  104.7 15.2 %collective-permute-start.2 = (bf16[144,512]{1,0:T(8,128)(2,1)}, bf16[144,512]{1,0:T(8,128)(2,1)S(1)}, u32[]{:S(2)}, u32[]{:S(2)}) collective-permute-start(bf16[144,512]{1,0:T(8,128)(2,1)} %copy-done.15), channel_id=1, source_target_pairs={{0,16},{8,24},{16,0},{24,8},{1,17},{9,25},{17,1},{25,9},{2,18},{10... | collective-permute-start | bytes 442376 | tf_op jit(solution)/shard_map/ppermute | solution.py:346
  108.7 11.2 %collective-permute-start.3 = (bf16[144,512]{1,0:T(8,128)(2,1)}, bf16[144,512]{1,0:T(8,128)(2,1)S(1)}, u32[]{:S(2)}, u32[]{:S(2)}) collective-permute-start(bf16[144,512]{1,0:T(8,128)(2,1)} %copy-done.14), channel_id=1, source_target_pairs={{0,24},{8,16},{16,8},{24,0},{1,25},{9,17},{17,9},{25,1},{2,26},{10... | collective-permute-start | bytes 442376 | tf_op jit(solution)/shard_map/ppermute | solution.py:346
  130.4 15.5 %collective-permute-start.6 = (bf16[512,512]{1,0:T(8,128)(2,1)S(1)}, bf16[512,512]{1,0:T(8,128)(2,1)S(1)}, u32[]{:S(2)}, u32[]{:S(2)}) collective-permute-start(bf16[512,512]{1,0:T(8,128)(2,1)S(1)} %shard_map.89.refs_1_), channel_id=1, source_target_pairs={{0,3},{1,0},{2,1},{3,2},{4,7},{5,4},{6,5},{7,6},{8,11},{9,8},{10,9... | collective-permute-start | bytes 1572872 | tf_op jit(solution)/shard_map/ppermute | solution.py:301
  132.9 19.8 %collective-permute-start.4 = (bf16[512,512]{1,0:T(8,128)(2,1)S(1)}, bf16[512,512]{1,0:T(8,128)(2,1)S(1)}, u32[]{:S(2)}, u32[]{:S(2)}) collective-permute-start(bf16[512,512]{1,0:T(8,128)(2,1)S(1)} %shard_map.89.refs_1_), channel_id=1, source_target_pairs={{0,1},{1,2},{2,3},{3,0},{4,5},{5,6},{6,7},{7,4},{8,9},{9,10},{10,1... | collective-permute-start | bytes 1572872 | tf_op jit(solution)/shard_map/ppermute | solution.py:301
  135.7 23.1 %collective-permute-start.5 = (bf16[512,512]{1,0:T(8,128)(2,1)S(1)}, bf16[512,512]{1,0:T(8,128)(2,1)S(1)}, u32[]{:S(2)}, u32[]{:S(2)}) collective-permute-start(bf16[512,512]{1,0:T(8,128)(2,1)S(1)} %shard_map.89.refs_1_), channel_id=1, source_target_pairs={{0,2},{1,3},{2,0},{3,1},{4,6},{5,7},{6,4},{7,5},{8,10},{9,11},{10,... | collective-permute-start | bytes 1572872 | tf_op jit(solution)/shard_map/ppermute | solution.py:301
  140.5 31.1 %collective-permute-start.7 = (bf16[512,512]{1,0:T(8,128)(2,1)S(1)}, bf16[512,512]{1,0:T(8,128)(2,1)S(1)}, u32[]{:S(2)}, u32[]{:S(2)}) collective-permute-start(bf16[512,512]{1,0:T(8,128)(2,1)S(1)} %shard_map.89.refs_1_), channel_id=1, source_target_pairs={{0,4},{4,0},{1,5},{5,1},{2,6},{6,2},{3,7},{7,3},{8,12},{12,8},{9,1... | collective-permute-start | bytes 1572872 | tf_op jit(solution)/shard_map/ppermute | solution.py:20
  145.9 28.3 %collective-permute-start.10 = (bf16[512,512]{1,0:T(8,128)(2,1)S(1)}, bf16[512,512]{1,0:T(8,128)(2,1)S(1)}, u32[]{:S(2)}, u32[]{:S(2)}) collective-permute-start(bf16[512,512]{1,0:T(8,128)(2,1)S(1)} %collective-permute-done.6.refs_4_), channel_id=1, source_target_pairs={{0,4},{4,0},{1,5},{5,1},{2,6},{6,2},{3,7},{7,3},{8,12},{12,8},{9,1... | collective-permute-start | bytes 1572872 | tf_op jit(solution)/shard_map/ppermute | solution.py:20
  152.8 25.3 %collective-permute-start.8 = (bf16[512,512]{1,0:T(8,128)(2,1)S(1)}, bf16[512,512]{1,0:T(8,128)(2,1)}, u32[]{:S(2)}, u32[]{:S(2)}) collective-permute-start(bf16[512,512]{1,0:T(8,128)(2,1)S(1)} %collective-permute-done.4.refs_2_), channel_id=1, source_target_pairs={{0,4},{4,0},{1,5},{5,1},{2,6},{6,2},{3,7},{7,3},{8,12},{12,8},{9,1... | collective-permute-start | bytes 1572872 | tf_op jit(solution)/shard_map/ppermute | solution.py:20
  158.9 19.2 %collective-permute-start.9 = (bf16[512,512]{1,0:T(8,128)(2,1)S(1)}, bf16[512,512]{1,0:T(8,128)(2,1)}, u32[]{:S(2)}, u32[]{:S(2)}) collective-permute-start(bf16[512,512]{1,0:T(8,128)(2,1)S(1)} %collective-permute-done.5.refs_3_), channel_id=1, source_target_pairs={{0,4},{4,0},{1,5},{5,1},{2,6},{6,2},{3,7},{7,3},{8,12},{12,8},{9,1... | collective-permute-start | bytes 1572872 | tf_op jit(solution)/shard_map/ppermute | solution.py:20
  165.7 17.3 %collective-permute-start.15 = (bf16[512,512]{1,0:T(8,128)(2,1)S(1)}, bf16[512,512]{1,0:T(8,128)(2,1)S(1)}, u32[]{:S(2)}, u32[]{:S(2)}) collective-permute-start(bf16[512,512]{1,0:T(8,128)(2,1)S(1)} %slice.10), channel_id=1, source_target_pairs={{0,128},{128,256},{256,384},{384,0},{1,129},{129,257},{257,385},{3... | collective-permute-start | bytes 1572872 | tf_op jit(solution)/shard_map/ppermute | solution.py:301
  171.6 23.5 %collective-permute-start.16 = (bf16[512,512]{1,0:T(8,128)(2,1)S(1)}, bf16[512,512]{1,0:T(8,128)(2,1)S(1)}, u32[]{:S(2)}, u32[]{:S(2)}) collective-permute-start(bf16[512,512]{1,0:T(8,128)(2,1)S(1)} %slice.10), channel_id=1, source_target_pairs={{0,256},{128,384},{256,0},{384,128},{1,257},{129,385},{257,1},{385... | collective-permute-start | bytes 1572872 | tf_op jit(solution)/shard_map/ppermute | solution.py:301
  174.3 22.2 %collective-permute-start.17 = (bf16[512,512]{1,0:T(8,128)(2,1)S(1)}, bf16[512,512]{1,0:T(8,128)(2,1)S(1)}, u32[]{:S(2)}, u32[]{:S(2)}) collective-permute-start(bf16[512,512]{1,0:T(8,128)(2,1)S(1)} %slice.10), channel_id=1, source_target_pairs={{0,384},{128,0},{256,128},{384,256},{1,385},{129,1},{257,129},{385... | collective-permute-start | bytes 1572872 | tf_op jit(solution)/shard_map/ppermute | solution.py:301
  201.7 6.8 %collective-permute-start.18 = (bf16[256,512]{1,0:T(8,128)(2,1)S(1)}, bf16[256,512]{1,0:T(8,128)(2,1)S(1)}, u32[]{:S(2)}, u32[]{:S(2)}) collective-permute-start(bf16[256,512]{1,0:T(8,128)(2,1)S(1)} %shard_map.91), channel_id=1, source_target_pairs={{0,4},{4,0},{1,5},{5,1},{2,6},{6,2},{3,7},{7,3},{8,12},{12,8},{9,1... | collective-permute-start | bytes 786440 | tf_op jit(solution)/shard_map/ppermute | solution.py:20
  (16 other events, 54.9 us)
Sparse Core Ops, SparseCore 0:
  27.9 76.7 all-gather.1

commit v8 on v7

--- a/solution.py
+++ b/solution.py
@@ -14,6 +14,7 @@
 NT = (((1,), (1,)), ((), ()))
 TN = (((0,), (0,)), ((), ()))
 LOGS = 1024
+ROWS = 1104
 
 
 def swap(value):
@@ -66,7 +67,9 @@
     )(*args, *unread)
 
 
-def pack_body(at, keys, values, queries, gates, decay, mix, keep, send, small, levels, sems):
+def pack_body(
+    at, keys, values, queries, gates, weight, decay, mix, keep, send, small, levels, sems
+):
     core = at[0]
     mine = pl.ds(pl.multiple_of(core * 512, 512), 512)
     theirs = pl.ds(pl.multiple_of((1 - core) * 512, 512), 512)
@@ -74,9 +77,9 @@
         pltpu.make_async_copy(decay, small, sems.at[0]),
         pltpu.make_async_copy(mix, levels, sems.at[1]),
     ]
-    for i, ref in enumerate((keys, values, queries, gates)):
-        rows = pl.ds(i * 256, 256)
-        for out, cols, n in ((send, theirs, 2), (keep, mine, 6)):
+    for i, ref in enumerate((keys, values, queries, gates, weight)):
+        rows = pl.ds(i * 256, 256) if i < 4 else pl.ds(LOGS + 48, 32)
+        for out, cols, n in ((send, theirs, 2), (keep, mine, 7)):
             copies.append(pltpu.make_async_copy(ref.at[:, cols], out.at[rows, :], sems.at[n + i]))
     for copy in copies:
         copy.start()
@@ -87,14 +90,14 @@
         logs += [jnp.where(low, levels[l, 0:4], levels[l, 4:8]) for l in range(8)]
         logs = jnp.concatenate(logs + [jnp.zeros((12, 256), F32)], axis=0)
         high = logs.astype(BF)
-        out[LOGS:, 0:256] = high
-        out[LOGS:, 256:512] = (logs - high.astype(F32)).astype(BF)
+        out[LOGS : LOGS + 48, 0:256] = high
+        out[LOGS : LOGS + 48, 256:512] = (logs - high.astype(F32)).astype(BF)
     for copy in copies[2:]:
         copy.wait()
 
 
 def logs_of(block):
-    tile = block[LOGS:, :].astype(F32)
+    tile = block[LOGS : LOGS + 48, :].astype(F32)
     return tile[:, 0:256] + tile[:, 256:512]
 
 
@@ -149,27 +152,29 @@
     send_whole(*blocks_of(near), pay)
 
 
-def far_body(at, near, far, pay, m0, m1, m2, m3, before_out):
+def far_body(at, far, pay, states, before_out):
     s, t, pair = blocks_of(far)
     send_whole(s, t, pair, pay)
-    three, four, before = lower_states(s, t, pair, at[2])
+    one, two, before = lower_states(s, t, pair, at[2])
+    states[:, 0:128] = one.astype(BF)
+    states[:, 128:256] = two.astype(BF)
     before_out[...] = jnp.broadcast_to(before, (8, 128))
-    s, t, pair = blocks_of(near)
-    for k, message in enumerate((m0, m1, m2, m3)):
-        one, two, before = lower_states(s, t, pair, at[1] ^ k)
-        for i, state in enumerate((one, two, three, four)):
-            message[0:128, i * 128 : i * 128 + 128] = state.astype(BF)
-        message[128:144, 0:128] = tail(before)
-        message[128:144, 128:512] = jnp.zeros((16, 384), BF)
-
-
-def last_body(at, last, before, message):
+
+
+def last_body(at, last, before, near, far, message):
     one, two, _ = lower_states(*blocks_of(last), at[3])
     earlier = jnp.exp(before[0:1, :])
-    one, two = (one * earlier).astype(BF), (two * earlier).astype(BF)
+    later = [state.astype(BF) for state in (one * earlier, two * earlier)]
+    s, t, pair = blocks_of(near)
     for i in range(4):
-        message[i, :, 0:128] = one
-        message[i, :, 128:256] = two
+        one, two, before_near = lower_states(s, t, pair, jnp.int32(i))
+        message[i, 0:128, 0:128] = one.astype(BF)
+        message[i, 0:128, 128:256] = two.astype(BF)
+        message[i, 0:128, 256:512] = far[...]
+        message[i, 0:128, 512:640] = later[0]
+        message[i, 0:128, 640:768] = later[1]
+        message[i, 128:144, 0:128] = tail(before_near)
+        message[i, 128:144, 128:768] = jnp.zeros((16, 640), BF)
 
 
 def place(s, core):
@@ -208,93 +213,66 @@
                 coef[here, 6 * h + l - 2 : 6 * h + l - 1] = start * m[l]
 
 
-def mix_body(at, keep, got, mixture, coef, m0, m1, m2, m3, mixed, later, states):
-    for k, message in enumerate((m0, m1, m2, m3)):
-        states[at[1] ^ k] = message[...]
+def norm_body(at, keep, got, gain, mixture, coef, states, normed):
+    core = at[0]
     for h in range(4):
+        mine = pl.ds(pl.multiple_of(core * 512 + h * 128, 128), 128)
+        hc = slice(h * 128, h * 128 + 128)
         before = jnp.exp(untail(states[h, 128:144, 0:128])[:, 0:1])
-        hc = slice(h * 128, h * 128 + 128)
         for s, ref in enumerate((keep, got)):
-            _, here = place(s, at[0])
+            _, here = place(s, core)
+            z = ref[768:1024, hc].astype(F32)
             total = mixture[here, hc]
-            for l in range(4):
+            for l in range(6):
                 if l % 2 == 0:
                     read = dot(ref[512:768, hc], states[h, 0:128, l * 128 : l * 128 + 256])
                 scale = coef[here, 6 * h + l : 6 * h + l + 1]
                 scale = scale if l < 2 else scale * before
                 total += read[:, (l % 2) * 128 : (l % 2) * 128 + 128] * scale
-            mixed[here, hc] = total
-            later[here, 2 * h : 2 * h + 2] = coef[here, 6 * h + 4 : 6 * h + 6] * before
-
-
-def norm_body(at, keep, got, gain, mixture, coef, last, normed):
-    core = at[0]
-    for h in range(4):
-        mine = pl.ds(pl.multiple_of(core * 512 + h * 128, 128), 128)
-        hc = slice(h * 128, h * 128 + 128)
-        for s, ref in enumerate((keep, got)):
-            _, here = place(s, core)
-            z = ref[768:1024, hc].astype(F32)
-            read = dot(ref[512:768, hc], last[h])
-            total = mixture[here, hc]
-            total += read[:, 0:128] * coef[here, 2 * h : 2 * h + 1]
-            total += read[:, 128:256] * coef[here, 2 * h + 1 : 2 * h + 2]
             gated = total * (z / (1.0 + jnp.exp(-z)))
             size = lax.rsqrt(jnp.mean(gated * gated, axis=1, keepdims=True) + 1e-05)
             normed[here, hc] = (gated * size * gain[:, mine].astype(F32)).astype(BF)
 
 
-def project_body(
-    other, at, a0, a1, a2, a3, b0, b1, b2, b3, gathered, w1, w2, w3, out, left, right, sems
-):
+def project_body(other, at, b0, b1, b2, b3, right, out, total):
+    step = pl.program_id(0)
     row = (1 - at[0]) if other else at[0]
     rows = pl.ds(pl.multiple_of(row * 256, 256), 256)
-    pieces = [gathered.at[:, 0:512], gathered.at[:, 512:1024]]
-    pieces += [gathered.at[:, 512 + 512 * k : 1024 + 512 * k] for k in (1, 2, 3)] + [w1, w2, w3]
-    copies = [
-        pltpu.make_async_copy(piece, right.at[i], sems.at[i]) for i, piece in enumerate(pieces)
-    ]
-    for copy in copies:
-        copy.start()
-    for j, (own, got) in enumerate(((a0, b0), (a1, b1), (a2, b2), (a3, b3))):
-        spot = (at[4] + 4 - j) % 4
-        left[at[0], spot] = own[rows, :]
-        left[1 - at[0], spot] = got[rows, :]
-    total = 0.0
-    for i, (half, k) in enumerate(
-        ((0, 0), (1, 0), (0, 1), (0, 2), (0, 3), (1, 1), (1, 2), (1, 3))
-    ):
-        copies[i].wait()
-        total += dot(left[half, (at[3] + 4 - k) % 4], right[i], NT)
-    out[...] = total.astype(BF)
-
-
-def project(at, owns, gots, gathered, lates, other):
-    return call(
+    want = (at[4] - at[3] + step + 4) % 4
+
+    @pl.when(step == 0)
+    def _():
+        total[...] = jnp.zeros_like(total)
+
+    for j, block in enumerate((b0, b1, b2, b3)):
+
+        @pl.when(want == j)
+        def _():
+            total[...] += dot(block[rows, :], right[...].reshape(1024, 512), NT)
+
+    @pl.when(step == 3)
+    def _():
+        out[...] = total[...].astype(out.dtype)
+
+
+def project(at, blocks, right, other):
+    whole_block = pl.BlockSpec((512, 512), lambda k, at: (0, 0))
+    return pl.pallas_call(
         functools.partial(project_body, other),
-        [((256, 512), BF)],
-        (at, *owns, *gots, gathered, *lates),
-        scratch=[
-            pltpu.VMEM((2, 4, 256, 512), BF),
-            pltpu.VMEM((8, 512, 512), BF),
-            pltpu.SemaphoreType.DMA((8,)),
-        ],
-        hbm=range(9, 13),
-        vmem=20,
-    )[0]
-
-
-def weave_body(at, own, got, out):
-    core = at[0]
-    i = lax.broadcasted_iota(jnp.int32, (128, 256), 0)
-    j = lax.broadcasted_iota(jnp.int32, (128, 256), 1)
-    spot = (i >> 5) * 64 + (i & 31)
-    mine = (j == spot + core * 32).astype(BF)
-    theirs = (j == spot + (1 - core) * 32).astype(BF)
-    for m in range(4):
-        cols = slice(m * 128, m * 128 + 128)
-        both = dot(own[:, cols], mine) + dot(got[:, cols], theirs)
-        out[:, m * 256 : m * 256 + 256] = both.astype(BF)
+        out_shape=jax.ShapeDtypeStruct((256, 1024), BF if other else F32),
+        grid_spec=pltpu.PrefetchScalarGridSpec(
+            num_scalar_prefetch=1,
+            grid=(4,),
+            in_specs=[whole_block] * 4
+            + [pl.BlockSpec((16, 64, 512), lambda k, at: (0, 0, k))],
+            out_specs=pl.BlockSpec((256, 1024), lambda k, at: (0, 0)),
+            scratch_shapes=[pltpu.VMEM((256, 1024), F32)],
+        ),
+        compiler_params=pltpu.CompilerParams(vmem_limit_bytes=20 * 2**20),
+        cost_estimate=pl.CostEstimate(
+            flops=2**30, bytes_accessed=6 * 2**20, transcendentals=0
+        ),
+    )(at, *blocks, right)
 
 
 def shift(value, axis, by):
@@ -304,64 +282,57 @@
 def shards(values, keys, queries, gates, log_decay, level_mix, norm_gain, weight):
     y, a, b, c, x = (lax.axis_index(n) for n in ("y", "a", NEAR, "c", "x"))
     at = jnp.stack([c, b, a, y, x]).astype(jnp.int32)
-    block = ((LOGS + 48, 512), BF)
+    block = ((ROWS, 512), BF)
     keep, send = call(
         pack_body,
         [block, block],
-        (at, keys, values, queries, gates, log_decay, level_mix),
+        (at, keys, values, queries, gates, weight, log_decay, level_mix),
         scratch=[
             pltpu.VMEM((8, 256), F32),
             pltpu.VMEM((8, 8, 256), F32),
-            pltpu.SemaphoreType.DMA((10,)),
+            pltpu.SemaphoreType.DMA((12,)),
         ],
-        hbm=range(1, 7),
+        hbm=range(1, 8),
         vmem=60,
     )
     got = swap(send)
+    pay = ((4, 144, 128), BF)
+    pay_b, first = call(ends_body, [pay, ((4, 128, 128), BF)], (at, keep, got))
+
+    kept, theirs = keep[LOGS + 48 :], got[LOGS + 48 :]
+    both = jnp.concatenate(
+        [jnp.where(c == 0, kept, theirs), jnp.where(c == 0, theirs, kept)]
+    )
+    both, pay_b = lax.optimization_barrier((both, pay_b))
     mine = []
     for k in range(4):
         perm = [(s * 4 + f, ((f + k) % 4) * 4 + s) for s in range(4) for f in range(4)]
-        mine.append(lax.ppermute(weight[:, : 512 if k else 1024], ("y", "x"), perm))
-    mine = jnp.concatenate(mine, axis=1)
-    gathered = lax.all_gather(mine, ("a", "p", "q"), axis=0, tiled=True)
-    late = gathered[:, 512:1024]
-    lates = [shift(late, "y", k) for k in (1, 2, 3)]
-
-    pay = ((4, 144, 128), BF)
-    pay_b, first = call(ends_body, [pay, ((4, 128, 128), BF)], (at, keep, got))
+        mine.append(lax.ppermute(both, ("y", "x"), perm))
+    gathered = lax.all_gather(jnp.concatenate(mine, axis=1), ("a", "p", "q"))
+
     near = lax.all_to_all(pay_b, NEAR, 0, 0, tiled=True)
     (pay_a,) = call(near_body, [pay], (at, near))
     far = lax.all_to_all(pay_a, "a", 0, 0, tiled=True)
     mixture, coef = call(
         own_body, [((512, 512), F32), ((512, 24), F32)], (at, keep, got, first)
     )
-    pay_y, *messages, before = call(
+    pay_y, far, before = call(
         far_body,
-        [pay] + [((144, 512), BF)] * 4 + [((8, 128), F32)],
-        (at, near, far),
+        [pay, ((128, 256), BF), ((8, 128), F32)],
+        (at, far),
         unread=(mixture,),
     )
     last = lax.all_to_all(pay_y, "y", 0, 0, tiled=True)
-    messages = messages[:1] + [
-        lax.ppermute(messages[k], NEAR, [(i, i ^ k) for i in range(4)]) for k in (1, 2, 3)
-    ]
-    (last,) = call(last_body, [((4, 128, 256), BF)], (at, last, before))
+    (last,) = call(last_body, [((4, 144, 768), BF)], (at, last, before, near, far))
     last = lax.all_to_all(last, NEAR, 0, 0, tiled=True)
-    mixture, coef = call(
-        mix_body,
-        [((512, 512), F32), ((512, 8), F32)],
-        (at, keep, got, mixture, coef, *messages),
-        scratch=[pltpu.VMEM((4, 144, 512), BF)],
-    )
     (normed,) = call(
         norm_body, [((512, 512), BF)], (at, keep, got, norm_gain[None], mixture, coef, last)
     )
 
-    owns = [normed] + [shift(normed, "x", j) for j in (1, 2, 3)]
-    gots = [swap(block) for block in owns]
-    theirs = swap(project(at, owns, gots, gathered, lates, True))
-    own = project(at, owns, gots, gathered, lates, False)
-    return call(weave_body, [((256, 1024), BF)], (at, own, theirs))[0]
+    blocks = [normed] + [shift(normed, "x", j) for j in (1, 2, 3)]
+    theirs = swap(project(at, blocks, gathered, True))
+    own = project(at, blocks, gathered, False)
+    return (own + theirs.astype(F32)).astype(BF)
 
 
 def solution(mesh):

time: 221 us -> 186 us (0.84); the launches traced: 217 us -> 185 us
  starting transfers between devices: 91 us -> 46.8 us
  waiting for transfers between devices: 47.7 us -> 60.8 us
  Pallas kernels: 26.9 us -> 23.1 us
  blocking collectives: 23 us -> 26.6 us
  local copies, waits for them, and re-layouts: 14.1 us -> 11.5 us
    all_to_all x1, waiting for transfers between devices: 0.01 us -> 28.8 us  [shards(): last = lax.all_to_all(last, NEAR, 0, 0, tiled=True)]
    ppermute x7 -> x4, starting transfers between devices: 26.5 us -> 7.52 us  [shards(): mine.append(lax.ppermute(both, ('y', 'x'), perm))]
    ppermute x6 -> x3, starting transfers between devices: 22.3 us -> 9.01 us  [shift(): return lax.ppermute(value, axis, [(i, (i + by) % 4) for i in range(4)])]
    ppermute x6 -> x2, starting transfers between devices: 27.3 us -> 14.5 us  [swap(): return lax.ppermute(value, 'c', [(0, 1), (1, 0)])]
    pallas_call x11 -> x7, Pallas kernels: 26.9 us -> 17 us  [call(): pl.pallas_call(run, out_shape=[jax.ShapeDtypeStruct(*o) for o in outs], i...]
    ppermute x7 -> x4, waiting for transfers between devices: 11.8 us -> 3.94 us  [shards(): mine.append(lax.ppermute(both, ('y', 'x'), perm))]
    all_to_all x1, blocking collectives: 9.56 us -> 15.7 us  [shards(): last = lax.all_to_all(pay_y, 'y', 0, 0, tiled=True)]
    pallas_call x0 -> x2, Pallas kernels: none -> 6.06 us  [project(): pl.pallas_call(functools.partial(project_body, other), out_shape=jax.Shap...]
  transfers between devices with their start and end apart: 22 -> 12, of which waited for: 9 -> 8; matrix products, arithmetic and copies ran while one was open for 1% -> 0% of each run, Pallas kernels for 10% -> 8%
where the time goes in v8:
time: 186 us; the launch traced here: 185 us
  waiting for transfers between devices  60.8 us (33%)
  starting transfers between devices  46.8 us (25%)
  blocking collectives  26.6 us (14%)
  Pallas kernels  23.1 us (12%)
  between operations  13.6 us (7%)
  local copies, waits for them, and re-layouts  11.5 us (6%)
  other arithmetic  2.43 us (1%)
    all_to_all x1, waiting for transfers between devices, shards(): last = lax.all_to_all(last, NEAR, 0, 0, tiled=True)  28.8 us
    ppermute x3, waiting for transfers between devices, shift(): return lax.ppermute(value, axis, [(i, (i + by) % 4) for i in range(4)])  18.3 us
    pallas_call x7, Pallas kernels, call(): pl.pallas_call(run, out_shape=[jax.ShapeDtypeStruct(*o) for o in outs], i...  17 us
    all_to_all x1, blocking collectives, shards(): last = lax.all_to_all(pay_y, 'y', 0, 0, tiled=True)  15.7 us
    ppermute x2, starting transfers between devices, swap(): return lax.ppermute(value, 'c', [(0, 1), (1, 0)])  14.5 us
    all_to_all x1, starting transfers between devices, shards(): far = lax.all_to_all(pay_a, 'a', 0, 0, tiled=True)  12.1 us
    all_to_all x1, blocking collectives, shards(): near = lax.all_to_all(pay_b, NEAR, 0, 0, tiled=True)  11 us
    unnamed x28, local copies, waits for them, and re-layouts  10.9 us
  transfers between devices with their start and end apart: 12, of which 8 were waited for; matrix products, arithmetic and copies ran while one was open for 0% of the time, Pallas kernels for 8%

profile of v8, /device:TPU:1, one launch (start us, length us, event | category | flops | bytes accessed | tf_op | source)
XLA Modules:
  0.0 184.8 jit_solution(571932363216710448)
XLA Ops:
  7.2 3.8 %shard_map.82 = (bf16[1104,512]{1,0:T(8,128)(2,1)}, bf16[1104,512]{1,0:T(8,128)(2,1)}) custom-call(s32[5]{0:T(128)} %stack.23.refs_0_.at, bf16[256,1024]{1,0:T(8,128)(2,1)} %refs_1_.1, bf16[256,1024]{1,0:T(8,128)(2,1)} %refs_2_.1, bf16[256,1024]{1,0:T(8,128)(2,1)} %refs_3_.1, bf16[256,1024]{1,0:T(8,128)(2,1)} %refs_4_.1, bf16[32,1024]{1,0:T(8,128)(2,1)} %refs_5_.1, ...), custom_call_target="tpu_custom_call" | custom-call | flops 1000000 | bytes 1000000 | tf_op jit(solution)/shard_map/pallas_call | solution.py:59
  11.0 8.8 %collective-permute-start = (bf16[1104,512]{1,0:T(8,128)(2,1)}, bf16[1104,512]{1,0:T(8,128)(2,1)S(1)}, u32[]{:S(2)}, u32[]{:S(2)}) collective-permute-start(bf16[1104,512]{1,0:T(8,128)(2,1)} %get-tuple-element.17), channel_id=1, source_target_pairs={{0,4},{4,0},{1,5},{5,1},{2,6},{6,2},{3,7},{7,3},{8,12},{12,8},{9,1... | collective-permute-start | bytes 3391496 | tf_op jit(solution)/shard_map/ppermute | solution.py:21
  19.8 2.6 %collective-permute-done.refs_2_ = bf16[1104,512]{1,0:T(8,128)(2,1)S(1)} collective-permute-done((bf16[1104,512]{1,0:T(8,128)(2,1)}, bf16[1104,512]{1,0:T(8,128)(2,1)S(1)}, u32[]{:S(2)}, u32[]{:S(2)}) %collective-permute-start) | collective-permute-done | bytes 1130528 | tf_op jit(solution)/shard_map/ppermute | solution.py:21
  26.8 2.0 %collective-permute-start.7 = (bf16[64,512]{1,0:T(8,128)(2,1)S(1)}, bf16[64,512]{1,0:T(8,128)(2,1)S(1)}, u32[]{:S(2)}, u32[]{:S(2)}) collective-permute-start(bf16[64,512]{1,0:T(8,128)(2,1)S(1)} %pad_maximum_fusion.1), channel_id=1, source_target_pairs={{0,384},{1,0},{2,128},{3,256},{128,385},{129,1},{130,129},{131,257... | collective-permute-start | bytes 196616 | tf_op jit(solution)/shard_map/ppermute | solution.py:310
  28.9 2.9 %collective-permute-start.6 = (bf16[64,512]{1,0:T(8,128)(2,1)S(1)}, bf16[64,512]{1,0:T(8,128)(2,1)S(1)}, u32[]{:S(2)}, u32[]{:S(2)}) collective-permute-start(bf16[64,512]{1,0:T(8,128)(2,1)S(1)} %pad_maximum_fusion.1), channel_id=1, source_target_pairs={{0,256},{1,384},{2,0},{3,128},{128,257},{129,385},{130,1},{131,129... | collective-permute-start | bytes 196616 | tf_op jit(solution)/shard_map/ppermute | solution.py:310
  31.8 1.9 %collective-permute-start.5 = (bf16[64,512]{1,0:T(8,128)(2,1)S(1)}, bf16[64,512]{1,0:T(8,128)(2,1)S(1)}, u32[]{:S(2)}, u32[]{:S(2)}) collective-permute-start(bf16[64,512]{1,0:T(8,128)(2,1)S(1)} %pad_maximum_fusion.1), channel_id=1, source_target_pairs={{0,128},{1,256},{2,384},{3,0},{128,129},{129,257},{130,385},{131,1... | collective-permute-start | bytes 196616 | tf_op jit(solution)/shard_map/ppermute | solution.py:310
  35.5 2.8 %collective-permute-done.5 = bf16[64,512]{1,0:T(8,128)(2,1)S(1)} collective-permute-done((bf16[64,512]{1,0:T(8,128)(2,1)S(1)}, bf16[64,512]{1,0:T(8,128)(2,1)S(1)}, u32[]{:S(2)}, u32[]{:S(2)}) %collective-permute-start.5) | collective-permute-done | bytes 65568 | tf_op jit(solution)/shard_map/ppermute | solution.py:310
  39.1 11.0 %all_to_all.20.refs_1_.refs_3_ = bf16[4,144,128]{2,1,0:T(8,128)(2,1)S(1)} all-to-all(bf16[4,144,128]{2,1,0:T(8,128)(2,1)S(1)} %get-tuple-element.22), channel_id=1, replica_groups=mesh['y'=4,'a'=4,'p'=2,'q'=2,'c'=2,'x'=4] {'p','q'}, dimensions={0} | all-to-all | bytes 294912 | tf_op jit(solution)/shard_map/all_to_all | solution.py:313
  51.3 12.1 %all-to-all-start.1 = ((bf16[4,144,128]{2,1,0:T(8,128)(2,1)}), bf16[4,144,128]{2,1,0:T(8,128)(2,1)}, u32[]{:S(2)}, u32[]{:S(2)}) async-start(bf16[4,144,128]{2,1,0:T(8,128)(2,1)} %shard_map.85), calls=%async_computation.1 | async-start | bytes 294912 | tf_op jit(solution)/shard_map/all_to_all | solution.py:315
  64.3 4.3 %shard_map.84 = (f32[512,512]{1,0:T(8,128)S(1)}, f32[512,24]{1,0:T(8,128)S(1)}) custom-call(s32[5]{0:T(128)S(1)} %copy-done.12, bf16[1104,512]{1,0:T(8,128)(2,1)S(1)} %copy-done.2, bf16[1104,512]{1,0:T(8,128)(2,1)S(1)} %collective-permute-done.refs_2_, bf16[4,128,128]{2,1,0:T(8,128)(2,1)S(1)} %copy-done.11), custom_call_target="tpu_custom_call" | custom-call | flops 1000000 | bytes 1000000 | tf_op jit(solution)/shard_map/pallas_call | solution.py:59
  69.4 7.1 %all-to-all-done.1.refs_1_ = bf16[4,144,128]{2,1,0:T(8,128)(2,1)} async-done(((bf16[4,144,128]{2,1,0:T(8,128)(2,1)}), bf16[4,144,128]{2,1,0:T(8,128)(2,1)}, u32[]{:S(2)}, u32[]{:S(2)}) %all-to-all-start.1) | async-done | bytes 147488 | tf_op jit(solution)/shard_map/all_to_all | solution.py:315
  77.4 15.7 %all_to_all.21.refs_1_ = bf16[4,144,128]{2,1,0:T(8,128)(2,1)S(1)} all-to-all(bf16[4,144,128]{2,1,0:T(8,128)(2,1)S(1)} %get-tuple-element.23), channel_id=1, replica_groups=mesh['y'=4,'a'=4,'p'=2,'q'=2,'c'=2,'x'=4] {'y'}, dimensions={0} | all-to-all | bytes 294912 | tf_op jit(solution)/shard_map/all_to_all | solution.py:325
  94.7 3.6 %all-to-all-start.3 = ((bf16[4,144,768]{2,1,0:T(8,128)(2,1)}), bf16[4,144,768]{2,1,0:T(8,128)(2,1)S(1)}, u32[]{:S(2)}, u32[]{:S(2)}) async-start(bf16[4,144,768]{2,1,0:T(8,128)(2,1)} %copy-done.5), calls=%async_computation.3 | async-start | bytes 1769472 | tf_op jit(solution)/shard_map/all_to_all | solution.py:327
  98.3 28.8 %all-to-all-done.3.refs_6_ = bf16[4,144,768]{2,1,0:T(8,128)(2,1)S(1)} async-done(((bf16[4,144,768]{2,1,0:T(8,128)(2,1)}), bf16[4,144,768]{2,1,0:T(8,128)(2,1)S(1)}, u32[]{:S(2)}, u32[]{:S(2)}) %all-to-all-start.3) | async-done | bytes 884768 | tf_op jit(solution)/shard_map/all_to_all | solution.py:327
  131.4 4.2 %shard_map.88.b0 = bf16[512,512]{1,0:T(8,128)(2,1)S(1)} custom-call(s32[5]{0:T(128)S(1)} %copy-done.12, bf16[1104,512]{1,0:T(8,128)(2,1)S(1)} %copy-done.2, bf16[1104,512]{1,0:T(8,128)(2,1)S(1)} %collective-permute-done.refs_2_, bf16[1,1024]{1,0:T(2,128)(2,1)S(1)} %broadcast_in_dim.3.refs_3_, f32[512,512]{1,0:T(8,128)S(1)} %copy-done.4, ...), custom_call_target="tpu_custom_call" | custom-call | flops 1000000 | bytes 1000000 | tf_op jit(solution)/shard_map/pallas_call | solution.py:59
  135.6 1.9 %collective-permute-start.1 = (bf16[512,512]{1,0:T(8,128)(2,1)S(1)}, bf16[512,512]{1,0:T(8,128)(2,1)S(1)}, u32[]{:S(2)}, u32[]{:S(2)}) collective-permute-start(bf16[512,512]{1,0:T(8,128)(2,1)S(1)} %shard_map.88.b0), channel_id=1, source_target_pairs={{0,1},{1,2},{2,3},{3,0},{4,5},{5,6},{6,7},{7,4},{8,9},{9,10},{10,1... | collective-permute-start | bytes 1572872 | tf_op jit(solution)/shard_map/ppermute | solution.py:279
  137.5 5.2 %collective-permute-start.2 = (bf16[512,512]{1,0:T(8,128)(2,1)S(1)}, bf16[512,512]{1,0:T(8,128)(2,1)S(1)}, u32[]{:S(2)}, u32[]{:S(2)}) collective-permute-start(bf16[512,512]{1,0:T(8,128)(2,1)S(1)} %shard_map.88.b0), channel_id=1, source_target_pairs={{0,2},{1,3},{2,0},{3,1},{4,6},{5,7},{6,4},{7,5},{8,10},{9,11},{10,... | collective-permute-start | bytes 1572872 | tf_op jit(solution)/shard_map/ppermute | solution.py:279
  144.6 2.1 %collective-permute-done.1.b1 = bf16[512,512]{1,0:T(8,128)(2,1)S(1)} collective-permute-done((bf16[512,512]{1,0:T(8,128)(2,1)S(1)}, bf16[512,512]{1,0:T(8,128)(2,1)S(1)}, u32[]{:S(2)}, u32[]{:S(2)}) %collective-permute-start.1) | collective-permute-done | bytes 524320 | tf_op jit(solution)/shard_map/ppermute | solution.py:279
  146.8 11.5 %collective-permute-done.2.b2 = bf16[512,512]{1,0:T(8,128)(2,1)S(1)} collective-permute-done((bf16[512,512]{1,0:T(8,128)(2,1)S(1)}, bf16[512,512]{1,0:T(8,128)(2,1)S(1)}, u32[]{:S(2)}, u32[]{:S(2)}) %collective-permute-start.2) | collective-permute-done | bytes 524320 | tf_op jit(solution)/shard_map/ppermute | solution.py:279
  158.3 4.7 %collective-permute-done.3.b3 = bf16[512,512]{1,0:T(8,128)(2,1)S(1)} collective-permute-done((bf16[512,512]{1,0:T(8,128)(2,1)S(1)}, bf16[512,512]{1,0:T(8,128)(2,1)S(1)}, u32[]{:S(2)}, u32[]{:S(2)}) %collective-permute-start.3) | collective-permute-done | bytes 524320 | tf_op jit(solution)/shard_map/ppermute | solution.py:279
  163.0 2.2 %copy-done = bf16[1024,2048]{1,0:T(8,128)(2,1)S(1)} copy-done((bf16[1024,2048]{1,0:T(8,128)(2,1)S(1)}, bf16[1024,2048]{1,0:T(8,128)(2,1)}, u32[]{:S(2)}) %copy-start) | copy-done | bytes 4194328
  165.2 3.0 %shard_map.90 = bf16[256,1024]{1,0:T(8,128)(2,1)S(1)} custom-call(s32[5]{0:T(128)S(1)} %copy-done.12, bf16[512,512]{1,0:T(8,128)(2,1)S(1)} %shard_map.88.b0, bf16[512,512]{1,0:T(8,128)(2,1)S(1)} %collective-permute-done.1.b1, bf16[512,512]{1,0:T(8,128)(2,1)S(1)} %collective-permute-done.2.b2, bf16[512,512]{1,0:T(8,128)(2,1)S(1)} %collective-permute-done.3.b3, ...), custom_call_target="tpu_custom_call" | custom-call | flops 1073741824 | bytes 6291456 | tf_op jit(solution)/shard_map/pallas_call | solution.py:260
  168.2 5.8 %collective-permute-start.8 = (bf16[256,1024]{1,0:T(8,128)(2,1)S(1)}, bf16[256,1024]{1,0:T(8,128)(2,1)S(1)}, u32[]{:S(2)}, u32[]{:S(2)}) collective-permute-start(bf16[256,1024]{1,0:T(8,128)(2,1)S(1)} %shard_map.90), channel_id=1, source_target_pairs={{0,4},{4,0},{1,5},{5,1},{2,6},{6,2},{3,7},{7,3},{8,12},{12,8},{9,1... | collective-permute-start | bytes 1572872 | tf_op jit(solution)/shard_map/ppermute | solution.py:21
  174.0 3.0 %shard_map.89 = f32[256,1024]{1,0:T(8,128)S(1)} custom-call(s32[5]{0:T(128)S(1)} %copy-done.12, bf16[512,512]{1,0:T(8,128)(2,1)S(1)} %shard_map.88.b0, bf16[512,512]{1,0:T(8,128)(2,1)S(1)} %collective-permute-done.1.b1, bf16[512,512]{1,0:T(8,128)(2,1)S(1)} %collective-permute-done.2.b2, bf16[512,512]{1,0:T(8,128)(2,1)S(1)} %collective-permute-done.3.b3, ...), custom_call_target="tpu_custom_call" | custom-call | flops 1073741824 | bytes 6291456 | tf_op jit(solution)/shard_map/pallas_call | solution.py:260
  (46 shorter events, 20.1 us)
Async XLA Ops:
  6.5 156.4 %all-gather.3.cloned.1.call-start = ((), (), s32[]{:S(2)}) async-start(), calls=%async_computation.4 | async-start | bytes 4456448 | tf_op jit(solution)/shard_map/all_gather | solution.py:311
  7.2 16.0 %copy-start.12 = (s32[5]{0:T(128)S(1)}, s32[5]{0:T(128)}, u32[]{:S(2)}) copy-start(s32[5]{0:T(128)} %stack.23.refs_0_.at) | copy-start | bytes 64
  11.0 11.4 %collective-permute-start = (bf16[1104,512]{1,0:T(8,128)(2,1)}, bf16[1104,512]{1,0:T(8,128)(2,1)S(1)}, u32[]{:S(2)}, u32[]{:S(2)}) collective-permute-start(bf16[1104,512]{1,0:T(8,128)(2,1)} %get-tuple-element.17), channel_id=1, source_target_pairs={{0,4},{4,0},{1,5},{5,1},{2,6},{6,2},{3,7},{7,3},{8,12},{12,8},{9,1... | collective-permute-start | bytes 3391496 | tf_op jit(solution)/shard_map/ppermute | solution.py:21
  23.1 1.3 copy-start.1
  26.8 36.6 %copy-start.2 = (bf16[1104,512]{1,0:T(8,128)(2,1)S(1)}, bf16[1104,512]{1,0:T(8,128)(2,1)}, u32[]{:S(2)}) copy-start(bf16[1104,512]{1,0:T(8,128)(2,1)} %get-tuple-element.16.refs_1_) | copy-start | bytes 3391492
  26.8 7.6 %collective-permute-start.7 = (bf16[64,512]{1,0:T(8,128)(2,1)S(1)}, bf16[64,512]{1,0:T(8,128)(2,1)S(1)}, u32[]{:S(2)}, u32[]{:S(2)}) collective-permute-start(bf16[64,512]{1,0:T(8,128)(2,1)S(1)} %pad_maximum_fusion.1), channel_id=1, source_target_pairs={{0,384},{1,0},{2,128},{3,256},{128,385},{129,1},{130,129},{131,257... | collective-permute-start | bytes 196616 | tf_op jit(solution)/shard_map/ppermute | solution.py:310
  28.9 6.6 %collective-permute-start.6 = (bf16[64,512]{1,0:T(8,128)(2,1)S(1)}, bf16[64,512]{1,0:T(8,128)(2,1)S(1)}, u32[]{:S(2)}, u32[]{:S(2)}) collective-permute-start(bf16[64,512]{1,0:T(8,128)(2,1)S(1)} %pad_maximum_fusion.1), channel_id=1, source_target_pairs={{0,256},{1,384},{2,0},{3,128},{128,257},{129,385},{130,1},{131,129... | collective-permute-start | bytes 196616 | tf_op jit(solution)/shard_map/ppermute | solution.py:310
  31.8 6.5 %collective-permute-start.5 = (bf16[64,512]{1,0:T(8,128)(2,1)S(1)}, bf16[64,512]{1,0:T(8,128)(2,1)S(1)}, u32[]{:S(2)}, u32[]{:S(2)}) collective-permute-start(bf16[64,512]{1,0:T(8,128)(2,1)S(1)} %pad_maximum_fusion.1), channel_id=1, source_target_pairs={{0,128},{1,256},{2,384},{3,0},{128,129},{129,257},{130,385},{131,1... | collective-permute-start | bytes 196616 | tf_op jit(solution)/shard_map/ppermute | solution.py:310
  33.7 4.6 %collective-permute-start.4 = (bf16[64,512]{1,0:T(8,128)(2,1)S(1)}, bf16[64,512]{1,0:T(8,128)(2,1)S(1)}, u32[]{:S(2)}, u32[]{:S(2)}) collective-permute-start(bf16[64,512]{1,0:T(8,128)(2,1)S(1)} %pad_maximum_fusion.1), channel_id=1, source_target_pairs={{0,0},{1,128},{2,256},{3,384},{128,1},{129,129},{130,257},{131,385... | collective-permute-start | bytes 196616 | tf_op jit(solution)/shard_map/ppermute | solution.py:310
  51.3 25.1 %all-to-all-start.1 = ((bf16[4,144,128]{2,1,0:T(8,128)(2,1)}), bf16[4,144,128]{2,1,0:T(8,128)(2,1)}, u32[]{:S(2)}, u32[]{:S(2)}) async-start(bf16[4,144,128]{2,1,0:T(8,128)(2,1)} %shard_map.85), calls=%async_computation.1 | async-start | bytes 294912 | tf_op jit(solution)/shard_map/all_to_all | solution.py:315
  63.4 0.9 copy-start.11
  69.4 24.4 %copy-start.3 = (f32[512,512]{1,0:T(8,128)}, f32[512,512]{1,0:T(8,128)S(1)}, u32[]{:S(2)}) copy-start(f32[512,512]{1,0:T(8,128)S(1)} %get-tuple-element.19.refs_2_.refs_4_) | copy-start | bytes 3145732
  93.7 0.9 copy-start.5
  94.7 3.6 %copy-start.13 = (bf16[1024]{0:T(1024)(128)(2,1)S(1)}, bf16[1024]{0:T(1024)(128)(2,1)}, u32[]{:S(2)}) copy-start(bf16[1024]{0:T(1024)(128)(2,1)} %param.14) | copy-start | bytes 6148
  94.7 32.5 %all-to-all-start.3 = ((bf16[4,144,768]{2,1,0:T(8,128)(2,1)}), bf16[4,144,768]{2,1,0:T(8,128)(2,1)S(1)}, u32[]{:S(2)}, u32[]{:S(2)}) async-start(bf16[4,144,768]{2,1,0:T(8,128)(2,1)} %copy-done.5), calls=%async_computation.3 | async-start | bytes 1769472 | tf_op jit(solution)/shard_map/all_to_all | solution.py:327
  127.1 0.9 copy-start.6
  128.1 1.2 copy-start.4
  129.3 1.2 copy-start.7
  130.5 1.0 copy-start.9
  135.6 11.1 %collective-permute-start.1 = (bf16[512,512]{1,0:T(8,128)(2,1)S(1)}, bf16[512,512]{1,0:T(8,128)(2,1)S(1)}, u32[]{:S(2)}, u32[]{:S(2)}) collective-permute-start(bf16[512,512]{1,0:T(8,128)(2,1)S(1)} %shard_map.88.b0), channel_id=1, source_target_pairs={{0,1},{1,2},{2,3},{3,0},{4,5},{5,6},{6,7},{7,4},{8,9},{9,10},{10,1... | collective-permute-start | bytes 1572872 | tf_op jit(solution)/shard_map/ppermute | solution.py:279
  137.5 20.7 %collective-permute-start.2 = (bf16[512,512]{1,0:T(8,128)(2,1)S(1)}, bf16[512,512]{1,0:T(8,128)(2,1)S(1)}, u32[]{:S(2)}, u32[]{:S(2)}) collective-permute-start(bf16[512,512]{1,0:T(8,128)(2,1)S(1)} %shard_map.88.b0), channel_id=1, source_target_pairs={{0,2},{1,3},{2,0},{3,1},{4,6},{5,7},{6,4},{7,5},{8,10},{9,11},{10,... | collective-permute-start | bytes 1572872 | tf_op jit(solution)/shard_map/ppermute | solution.py:279
  142.7 20.3 %collective-permute-start.3 = (bf16[512,512]{1,0:T(8,128)(2,1)S(1)}, bf16[512,512]{1,0:T(8,128)(2,1)S(1)}, u32[]{:S(2)}, u32[]{:S(2)}) collective-permute-start(bf16[512,512]{1,0:T(8,128)(2,1)S(1)} %shard_map.88.b0), channel_id=1, source_target_pairs={{0,3},{1,0},{2,1},{3,2},{4,7},{5,4},{6,5},{7,6},{8,11},{9,8},{10,9... | collective-permute-start | bytes 1572872 | tf_op jit(solution)/shard_map/ppermute | solution.py:279
  163.0 2.2 %copy-start = (bf16[1024,2048]{1,0:T(8,128)(2,1)S(1)}, bf16[1024,2048]{1,0:T(8,128)(2,1)}, u32[]{:S(2)}) copy-start(bf16[1024,2048]{1,0:T(8,128)(2,1)} %all-gather.3.cloned.1.call-done) | copy-start | bytes 12582916
  168.2 8.8 %collective-permute-start.8 = (bf16[256,1024]{1,0:T(8,128)(2,1)S(1)}, bf16[256,1024]{1,0:T(8,128)(2,1)S(1)}, u32[]{:S(2)}, u32[]{:S(2)}) collective-permute-start(bf16[256,1024]{1,0:T(8,128)(2,1)S(1)} %shard_map.90), channel_id=1, source_target_pairs={{0,4},{4,0},{1,5},{5,1},{2,6},{6,2},{3,7},{7,3},{8,12},{12,8},{9,1... | collective-permute-start | bytes 1572872 | tf_op jit(solution)/shard_map/ppermute | solution.py:21
  (2 other events, 1.4 us)
Sparse Core Ops, SparseCore 0:
  39.2 101.3 all-gather.2

commit v9 on v8

--- a/solution.py
+++ b/solution.py
@@ -234,29 +234,32 @@
             normed[here, hc] = (gated * size * gain[:, mine].astype(F32)).astype(BF)
 
 
-def project_body(other, at, b0, b1, b2, b3, right, out, total):
+def project_body(other, at, b0, b1, b2, b3, right, next_right, far_right, out, total):
     step = pl.program_id(0)
     row = (1 - at[0]) if other else at[0]
     rows = pl.ds(pl.multiple_of(row * 256, 256), 256)
-    want = (at[4] - at[3] + step + 4) % 4
+    turn = jnp.where(step == 2, 3, jnp.where(step == 3, 2, step))
+    want = (at[4] - at[3] + turn + 4) % 4
 
     @pl.when(step == 0)
     def _():
         total[...] = jnp.zeros_like(total)
 
     for j, block in enumerate((b0, b1, b2, b3)):
-
-        @pl.when(want == j)
-        def _():
-            total[...] += dot(block[rows, :], right[...].reshape(1024, 512), NT)
+        for ref, now in ((right, step < 2), (next_right, step == 2), (far_right, step == 3)):
+
+            @pl.when(jnp.logical_and(want == j, now))
+            def _():
+                total[...] += dot(block[rows, :], ref[...].reshape(1024, 512), NT)
 
     @pl.when(step == 3)
     def _():
         out[...] = total[...].astype(out.dtype)
 
 
-def project(at, blocks, right, other):
+def project(at, blocks, right, next_right, far_right, other):
     whole_block = pl.BlockSpec((512, 512), lambda k, at: (0, 0))
+    whole_right = pl.BlockSpec((16, 64, 512), lambda k, at: (0, 0, 0))
     return pl.pallas_call(
         functools.partial(project_body, other),
         out_shape=jax.ShapeDtypeStruct((256, 1024), BF if other else F32),
@@ -264,15 +267,16 @@
             num_scalar_prefetch=1,
             grid=(4,),
             in_specs=[whole_block] * 4
-            + [pl.BlockSpec((16, 64, 512), lambda k, at: (0, 0, k))],
+            + [pl.BlockSpec((16, 64, 512), lambda k, at: (0, 0, jnp.minimum(k, 1)))]
+            + [whole_right] * 2,
             out_specs=pl.BlockSpec((256, 1024), lambda k, at: (0, 0)),
             scratch_shapes=[pltpu.VMEM((256, 1024), F32)],
         ),
-        compiler_params=pltpu.CompilerParams(vmem_limit_bytes=20 * 2**20),
+        compiler_params=pltpu.CompilerParams(vmem_limit_bytes=24 * 2**20),
         cost_estimate=pl.CostEstimate(
             flops=2**30, bytes_accessed=6 * 2**20, transcendentals=0
         ),
-    )(at, *blocks, right)
+    )(at, *blocks, right, next_right, far_right)
 
 
 def shift(value, axis, by):
@@ -305,13 +309,14 @@
     )
     both, pay_b = lax.optimization_barrier((both, pay_b))
     mine = []
-    for k in range(4):
+    for k in range(2):
         perm = [(s * 4 + f, ((f + k) % 4) * 4 + s) for s in range(4) for f in range(4)]
         mine.append(lax.ppermute(both, ("y", "x"), perm))
-    gathered = lax.all_gather(jnp.concatenate(mine, axis=1), ("a", "p", "q"))
+    mine = jnp.concatenate(mine, axis=1)
+    gathered = lax.all_gather(mine, ("a", "p", "q"))
 
     near = lax.all_to_all(pay_b, NEAR, 0, 0, tiled=True)
-    (pay_a,) = call(near_body, [pay], (at, near))
+    (pay_a,) = call(near_body, [pay], (at, near), unread=(mine,))
     far = lax.all_to_all(pay_a, "a", 0, 0, tiled=True)
     mixture, coef = call(
         own_body, [((512, 512), F32), ((512, 24), F32)], (at, keep, got, first)
@@ -323,15 +328,23 @@
         unread=(mixture,),
     )
     last = lax.all_to_all(pay_y, "y", 0, 0, tiled=True)
-    (last,) = call(last_body, [((4, 144, 768), BF)], (at, last, before, near, far))
+    (last,) = call(
+        last_body, [((4, 144, 768), BF)], (at, last, before, near, far), vmem=60
+    )
     last = lax.all_to_all(last, NEAR, 0, 0, tiled=True)
+    last, gathered = lax.optimization_barrier((last, gathered))
+    next_right = shift(gathered[:, :, :512], "y", 3)
+    far_right = shift(gathered[:, :, 512:], "y", 1)
     (normed,) = call(
-        norm_body, [((512, 512), BF)], (at, keep, got, norm_gain[None], mixture, coef, last)
+        norm_body,
+        [((512, 512), BF)],
+        (at, keep, got, norm_gain[None], mixture, coef, last),
+        vmem=60,
     )
 
     blocks = [normed] + [shift(normed, "x", j) for j in (1, 2, 3)]
-    theirs = swap(project(at, blocks, gathered, True))
-    own = project(at, blocks, gathered, False)
+    theirs = swap(project(at, blocks, gathered, next_right, far_right, True))
+    own = project(at, blocks, gathered, next_right, far_right, False)
     return (own + theirs.astype(F32)).astype(BF)
 
 

time: 186 us -> 190 us (1.022)
  blocking collectives: 26.6 us -> 50.3 us
  waiting for transfers between devices: 60.8 us -> 40.1 us
  Pallas kernels: 23.1 us -> 29.6 us
  starting transfers between devices: 46.8 us -> 43.5 us
    all_to_all x0 -> x1, blocking collectives: none -> 31.5 us  [shards(): last = lax.all_to_all(last, NEAR, 0, 0, tiled=True)]
    all_to_all x1 -> x0, waiting for transfers between devices: 28.8 us -> none  [shards(): last = lax.all_to_all(last, NEAR, 0, 0, tiled=True)]
    all_to_all x1, blocking collectives: 15.7 us -> 8.1 us  [shards(): last = lax.all_to_all(pay_y, 'y', 0, 0, tiled=True)]
    ppermute x3 -> x5, starting transfers between devices: 9.01 us -> 16.4 us  [shift(): return lax.ppermute(value, axis, [(i, (i + by) % 4) for i in range(4)])]
    unnamed x28 -> x37, local copies, waits for them, and re-layouts: 10.9 us -> 5.48 us
    ppermute x4 -> x2, starting transfers between devices: 7.52 us -> 2.72 us  [shards(): mine.append(lax.ppermute(both, ('y', 'x'), perm))]
    ppermute x3 -> x5, waiting for transfers between devices: 18.3 us -> 22.7 us  [shift(): return lax.ppermute(value, axis, [(i, (i + by) % 4) for i in range(4)])]
    pallas_call x7, Pallas kernels: 17 us -> 21.1 us  [call(): pl.pallas_call(run, out_shape=[jax.ShapeDtypeStruct(*o) for o in outs], i...]
  transfers between devices with their start and end apart: 12 -> 11, of which waited for: 8 -> 6; matrix products, arithmetic and copies ran while one was open for 0% -> 0% of each run, Pallas kernels for 8% -> 10%
where the time goes in v9:
time: 190 us; the launch traced here: 189 us
  blocking collectives  50.3 us (26%)
  starting transfers between devices  43.5 us (23%)
  waiting for transfers between devices  40.1 us (21%)
  Pallas kernels  29.6 us (16%)
  between operations  13.7 us (7%)
  local copies, waits for them, and re-layouts  9.88 us (5%)
    all_to_all x1, blocking collectives, shards(): last = lax.all_to_all(last, NEAR, 0, 0, tiled=True)  31.5 us
    ppermute x5, waiting for transfers between devices, shift(): return lax.ppermute(value, axis, [(i, (i + by) % 4) for i in range(4)])  22.7 us
    pallas_call x7, Pallas kernels, call(): pl.pallas_call(run, out_shape=[jax.ShapeDtypeStruct(*o) for o in outs], i...  21.1 us
    ppermute x5, starting transfers between devices, shift(): return lax.ppermute(value, axis, [(i, (i + by) % 4) for i in range(4)])  16.4 us
    ppermute x2, starting transfers between devices, swap(): return lax.ppermute(value, 'c', [(0, 1), (1, 0)])  12.3 us
    all_to_all x1, starting transfers between devices, shards(): far = lax.all_to_all(pay_a, 'a', 0, 0, tiled=True)  12.1 us
    all_to_all x1, blocking collectives, shards(): near = lax.all_to_all(pay_b, NEAR, 0, 0, tiled=True)  10.6 us
    all_to_all x1, waiting for transfers between devices, shards(): far = lax.all_to_all(pay_a, 'a', 0, 0, tiled=True)  10.5 us
  transfers between devices with their start and end apart: 11, of which 6 were waited for; matrix products, arithmetic and copies ran while one was open for 0% of the time, Pallas kernels for 10%

profile of v9, /device:TPU:1, one launch (start us, length us, event | category | flops | bytes accessed | tf_op | source)
XLA Modules:
  0.0 188.7 jit_solution(14246156598951833769)
XLA Ops:
  7.2 3.8 %shard_map.82 = (bf16[1104,512]{1,0:T(8,128)(2,1)}, bf16[1104,512]{1,0:T(8,128)(2,1)}) custom-call(s32[5]{0:T(128)} %stack.23.refs_0_.at, bf16[256,1024]{1,0:T(8,128)(2,1)} %refs_1_.1, bf16[256,1024]{1,0:T(8,128)(2,1)} %refs_2_.1, bf16[256,1024]{1,0:T(8,128)(2,1)} %refs_3_.1, bf16[256,1024]{1,0:T(8,128)(2,1)} %refs_4_.1, bf16[32,1024]{1,0:T(8,128)(2,1)} %refs_5_.1, ...), custom_call_target="tpu_custom_call" | custom-call | flops 1000000 | bytes 1000000 | tf_op jit(solution)/shard_map/pallas_call | solution.py:59
  11.0 8.8 %collective-permute-start = (bf16[1104,512]{1,0:T(8,128)(2,1)}, bf16[1104,512]{1,0:T(8,128)(2,1)S(1)}, u32[]{:S(2)}, u32[]{:S(2)}) collective-permute-start(bf16[1104,512]{1,0:T(8,128)(2,1)} %get-tuple-element.19), channel_id=1, source_target_pairs={{0,4},{4,0},{1,5},{5,1},{2,6},{6,2},{3,7},{7,3},{8,12},{12,8},{9,1... | collective-permute-start | bytes 3391496 | tf_op jit(solution)/shard_map/ppermute | solution.py:21
  19.8 2.6 %collective-permute-done.refs_2_ = bf16[1104,512]{1,0:T(8,128)(2,1)S(1)} collective-permute-done((bf16[1104,512]{1,0:T(8,128)(2,1)}, bf16[1104,512]{1,0:T(8,128)(2,1)S(1)}, u32[]{:S(2)}, u32[]{:S(2)}) %collective-permute-start) | collective-permute-done | bytes 1130528 | tf_op jit(solution)/shard_map/ppermute | solution.py:21
  29.0 4.3 %collective-permute-done.2 = bf16[64,512]{1,0:T(8,128)(2,1)S(1)} collective-permute-done((bf16[64,512]{1,0:T(8,128)(2,1)S(1)}, bf16[64,512]{1,0:T(8,128)(2,1)S(1)}, u32[]{:S(2)}, u32[]{:S(2)}) %collective-permute-start.2) | collective-permute-done | bytes 65568 | tf_op jit(solution)/shard_map/ppermute | solution.py:314
  33.9 10.6 %all_to_all.20.refs_1_.refs_3_ = bf16[4,144,128]{2,1,0:T(8,128)(2,1)S(1)} all-to-all(bf16[4,144,128]{2,1,0:T(8,128)(2,1)S(1)} %get-tuple-element.24), channel_id=1, replica_groups=mesh['y'=4,'a'=4,'p'=2,'q'=2,'c'=2,'x'=4] {'p','q'}, dimensions={0} | all-to-all | bytes 294912 | tf_op jit(solution)/shard_map/all_to_all | solution.py:318
  46.7 12.1 %all-to-all-start.1 = ((bf16[4,144,128]{2,1,0:T(8,128)(2,1)}), bf16[4,144,128]{2,1,0:T(8,128)(2,1)}, u32[]{:S(2)}, u32[]{:S(2)}) async-start(bf16[4,144,128]{2,1,0:T(8,128)(2,1)} %shard_map.85), calls=%async_computation.1 | async-start | bytes 294912 | tf_op jit(solution)/shard_map/all_to_all | solution.py:320
  59.7 4.4 %shard_map.84 = (f32[512,512]{1,0:T(8,128)S(1)}, f32[512,24]{1,0:T(8,128)S(1)}) custom-call(s32[5]{0:T(128)S(1)} %copy-done.14, bf16[1104,512]{1,0:T(8,128)(2,1)S(1)} %copy-done.2, bf16[1104,512]{1,0:T(8,128)(2,1)S(1)} %collective-permute-done.refs_2_, bf16[4,128,128]{2,1,0:T(8,128)(2,1)S(1)} %copy-done.12), custom_call_target="tpu_custom_call" | custom-call | flops 1000000 | bytes 1000000 | tf_op jit(solution)/shard_map/pallas_call | solution.py:59
  64.8 10.5 %all-to-all-done.1.refs_1_ = bf16[4,144,128]{2,1,0:T(8,128)(2,1)} async-done(((bf16[4,144,128]{2,1,0:T(8,128)(2,1)}), bf16[4,144,128]{2,1,0:T(8,128)(2,1)}, u32[]{:S(2)}, u32[]{:S(2)}) %all-to-all-start.1) | async-done | bytes 147488 | tf_op jit(solution)/shard_map/all_to_all | solution.py:320
  76.3 8.1 %all_to_all.21.refs_1_ = bf16[4,144,128]{2,1,0:T(8,128)(2,1)} all-to-all(bf16[4,144,128]{2,1,0:T(8,128)(2,1)S(1)} %get-tuple-element.26), channel_id=1, replica_groups=mesh['y'=4,'a'=4,'p'=2,'q'=2,'c'=2,'x'=4] {'y'}, dimensions={0} | all-to-all | bytes 294912 | tf_op jit(solution)/shard_map/all_to_all | solution.py:330
  84.4 2.0 %shard_map.87 = bf16[4,144,768]{2,1,0:T(8,128)(2,1)} custom-call(s32[5]{0:T(128)} %stack.23.refs_0_.at, bf16[4,144,128]{2,1,0:T(8,128)(2,1)} %all_to_all.21.refs_1_, f32[8,128]{1,0:T(8,128)} %copy-done.16, bf16[4,144,128]{2,1,0:T(8,128)(2,1)} %copy-done.7, bf16[128,256]{1,0:T(8,128)(2,1)} %copy-done.13), custom_call_target="tpu_custom_call" | custom-call | flops 1000000 | bytes 1000000 | tf_op jit(solution)/shard_map/pallas_call | solution.py:59
  86.5 31.5 %all_to_all.22.refs_6_ = bf16[4,144,768]{2,1,0:T(8,128)(2,1)} all-to-all(bf16[4,144,768]{2,1,0:T(8,128)(2,1)} %shard_map.87), channel_id=1, replica_groups=mesh['y'=4,'a'=4,'p'=2,'q'=2,'c'=2,'x'=4] {'p','q'}, dimensions={0} | all-to-all | bytes 1769472 | tf_op jit(solution)/shard_map/all_to_all | solution.py:334
  118.0 3.2 %fusion = (bf16[16,64,512]{2,1,0:T(8,128)(2,1)}, bf16[16,64,512]{2,1,0:T(8,128)(2,1)}) fusion(bf16[16,64,1024]{2,1,0:T(8,128)(2,1)} %bitcast.6), kind=kLoop, calls=%fused_computation.6 | loop fusion | bytes 4194304 | tf_op jit(solution)/shard_map/slice | solution.py:337
  121.2 2.4 %collective-permute-start.7 = (bf16[16,64,512]{2,1,0:T(8,128)(2,1)}, bf16[16,64,512]{2,1,0:T(8,128)(2,1)S(1)}, u32[]{:S(2)}, u32[]{:S(2)}) collective-permute-start(bf16[16,64,512]{2,1,0:T(8,128)(2,1)} %get-tuple-element.33), channel_id=1, source_target_pairs={{0,128},{128,256},{256,384},{384,0},{1,129},{129,257},{257,385},{3... | collective-permute-start | bytes 3145736 | tf_op jit(solution)/shard_map/ppermute | solution.py:283
  123.6 4.0 %collective-permute-start.6 = (bf16[16,64,512]{2,1,0:T(8,128)(2,1)}, bf16[16,64,512]{2,1,0:T(8,128)(2,1)}, u32[]{:S(2)}, u32[]{:S(2)}) collective-permute-start(bf16[16,64,512]{2,1,0:T(8,128)(2,1)} %get-tuple-element.34), channel_id=1, source_target_pairs={{0,384},{128,0},{256,128},{384,256},{1,385},{129,1},{257,129},{385... | collective-permute-start | bytes 3145736 | tf_op jit(solution)/shard_map/ppermute | solution.py:283
  128.3 6.9 %shard_map.88.b0 = bf16[512,512]{1,0:T(8,128)(2,1)} custom-call(s32[5]{0:T(128)} %stack.23.refs_0_.at, bf16[1104,512]{1,0:T(8,128)(2,1)} %get-tuple-element.18.refs_1_, bf16[1104,512]{1,0:T(8,128)(2,1)} %copy-done.3, bf16[1,1024]{1,0:T(2,128)(2,1)} %broadcast_in_dim.3.refs_3_, f32[512,512]{1,0:T(8,128)} %copy-done.6, f32[512,24]{1,0:T(8,128)} %copy-done.10, ...), custom_call_target="tpu_custom_call" | custom-call | flops 1000000 | bytes 1000000 | tf_op jit(solution)/shard_map/pallas_call | solution.py:59
  135.2 5.0 %collective-permute-start.5 = (bf16[512,512]{1,0:T(8,128)(2,1)}, bf16[512,512]{1,0:T(8,128)(2,1)S(1)}, u32[]{:S(2)}, u32[]{:S(2)}) collective-permute-start(bf16[512,512]{1,0:T(8,128)(2,1)} %shard_map.88.b0), channel_id=1, source_target_pairs={{0,3},{1,0},{2,1},{3,2},{4,7},{5,4},{6,5},{7,6},{8,11},{9,8},{10,9... | collective-permute-start | bytes 1572872 | tf_op jit(solution)/shard_map/ppermute | solution.py:283
  140.2 2.4 %collective-permute-start.4 = (bf16[512,512]{1,0:T(8,128)(2,1)}, bf16[512,512]{1,0:T(8,128)(2,1)S(1)}, u32[]{:S(2)}, u32[]{:S(2)}) collective-permute-start(bf16[512,512]{1,0:T(8,128)(2,1)} %shard_map.88.b0), channel_id=1, source_target_pairs={{0,2},{1,3},{2,0},{3,1},{4,6},{5,7},{6,4},{7,5},{8,10},{9,11},{10,... | collective-permute-start | bytes 1572872 | tf_op jit(solution)/shard_map/ppermute | solution.py:283
  142.6 2.5 %collective-permute-start.3 = (bf16[512,512]{1,0:T(8,128)(2,1)}, bf16[512,512]{1,0:T(8,128)(2,1)S(1)}, u32[]{:S(2)}, u32[]{:S(2)}) collective-permute-start(bf16[512,512]{1,0:T(8,128)(2,1)} %shard_map.88.b0), channel_id=1, source_target_pairs={{0,1},{1,2},{2,3},{3,0},{4,5},{5,6},{6,7},{7,4},{8,9},{9,10},{10,1... | collective-permute-start | bytes 1572872 | tf_op jit(solution)/shard_map/ppermute | solution.py:283
  145.1 5.2 %collective-permute-done.5.b3 = bf16[512,512]{1,0:T(8,128)(2,1)S(1)} collective-permute-done((bf16[512,512]{1,0:T(8,128)(2,1)}, bf16[512,512]{1,0:T(8,128)(2,1)S(1)}, u32[]{:S(2)}, u32[]{:S(2)}) %collective-permute-start.5) | collective-permute-done | bytes 524320 | tf_op jit(solution)/shard_map/ppermute | solution.py:283
  150.3 2.1 %collective-permute-done.4.b2 = bf16[512,512]{1,0:T(8,128)(2,1)S(1)} collective-permute-done((bf16[512,512]{1,0:T(8,128)(2,1)}, bf16[512,512]{1,0:T(8,128)(2,1)S(1)}, u32[]{:S(2)}, u32[]{:S(2)}) %collective-permute-start.4) | collective-permute-done | bytes 524320 | tf_op jit(solution)/shard_map/ppermute | solution.py:283
  152.4 15.4 %collective-permute-done.3.b1 = bf16[512,512]{1,0:T(8,128)(2,1)S(1)} collective-permute-done((bf16[512,512]{1,0:T(8,128)(2,1)}, bf16[512,512]{1,0:T(8,128)(2,1)S(1)}, u32[]{:S(2)}, u32[]{:S(2)}) %collective-permute-start.3) | collective-permute-done | bytes 524320 | tf_op jit(solution)/shard_map/ppermute | solution.py:283
  168.9 4.2 %shard_map.90 = bf16[256,1024]{1,0:T(8,128)(2,1)S(1)} custom-call(s32[5]{0:T(128)S(1)} %copy-done.15, bf16[512,512]{1,0:T(8,128)(2,1)S(1)} %copy-done.4, bf16[512,512]{1,0:T(8,128)(2,1)S(1)} %collective-permute-done.3.b1, bf16[512,512]{1,0:T(8,128)(2,1)S(1)} %collective-permute-done.4.b2, bf16[512,512]{1,0:T(8,128)(2,1)S(1)} %collective-permute-done.5.b3, ...), custom_call_target="tpu_custom_call" | custom-call | flops 1073741824 | bytes 6291456 | tf_op jit(solution)/shard_map/pallas_call | solution.py:263
  173.1 3.5 %collective-permute-start.8 = (bf16[256,1024]{1,0:T(8,128)(2,1)S(1)}, bf16[256,1024]{1,0:T(8,128)(2,1)S(1)}, u32[]{:S(2)}, u32[]{:S(2)}) collective-permute-start(bf16[256,1024]{1,0:T(8,128)(2,1)S(1)} %shard_map.90), channel_id=1, source_target_pairs={{0,4},{4,0},{1,5},{5,1},{2,6},{6,2},{3,7},{7,3},{8,12},{12,8},{9,1... | collective-permute-start | bytes 1572872 | tf_op jit(solution)/shard_map/ppermute | solution.py:21
  176.6 4.2 %shard_map.89 = f32[256,1024]{1,0:T(8,128)S(1)} custom-call(s32[5]{0:T(128)S(1)} %copy-done.15, bf16[512,512]{1,0:T(8,128)(2,1)S(1)} %copy-done.5, bf16[512,512]{1,0:T(8,128)(2,1)S(1)} %collective-permute-done.3.b1, bf16[512,512]{1,0:T(8,128)(2,1)S(1)} %collective-permute-done.4.b2, bf16[512,512]{1,0:T(8,128)(2,1)S(1)} %collective-permute-done.5.b3, ...), custom_call_target="tpu_custom_call" | custom-call | flops 1073741824 | bytes 6291456 | tf_op jit(solution)/shard_map/pallas_call | solution.py:263
  (55 shorter events, 15.2 us)
Async XLA Ops:
  6.5 111.5 %all-gather.3.cloned.1.call-start = ((), (), s32[]{:S(2)}) async-start(), calls=%async_computation.4 | async-start | bytes 2228224 | tf_op jit(solution)/shard_map/all_gather | solution.py:316
  7.2 16.0 %copy-start.14 = (s32[5]{0:T(128)S(1)}, s32[5]{0:T(128)}, u32[]{:S(2)}) copy-start(s32[5]{0:T(128)} %stack.23.refs_0_.at) | copy-start | bytes 64
  11.0 11.4 %collective-permute-start = (bf16[1104,512]{1,0:T(8,128)(2,1)}, bf16[1104,512]{1,0:T(8,128)(2,1)S(1)}, u32[]{:S(2)}, u32[]{:S(2)}) collective-permute-start(bf16[1104,512]{1,0:T(8,128)(2,1)} %get-tuple-element.19), channel_id=1, source_target_pairs={{0,4},{4,0},{1,5},{5,1},{2,6},{6,2},{3,7},{7,3},{8,12},{12,8},{9,1... | collective-permute-start | bytes 3391496 | tf_op jit(solution)/shard_map/ppermute | solution.py:21
  22.4 36.5 %copy-start.3 = (bf16[1104,512]{1,0:T(8,128)(2,1)}, bf16[1104,512]{1,0:T(8,128)(2,1)S(1)}, u32[]{:S(2)}) copy-start(bf16[1104,512]{1,0:T(8,128)(2,1)S(1)} %collective-permute-done.refs_2_) | copy-start | bytes 3391492
  23.2 1.3 copy-start.1
  26.2 2.8 %copy-start.11 = (bf16[4,128,128]{2,1,0:T(8,128)(2,1)}, bf16[4,128,128]{2,1,0:T(8,128)(2,1)S(1)}, u32[]{:S(2)}) copy-start(bf16[4,128,128]{2,1,0:T(8,128)(2,1)S(1)} %get-tuple-element.20.refs_3_) | copy-start | bytes 393220
  26.2 32.6 %copy-start.2 = (bf16[1104,512]{1,0:T(8,128)(2,1)S(1)}, bf16[1104,512]{1,0:T(8,128)(2,1)}, u32[]{:S(2)}) copy-start(bf16[1104,512]{1,0:T(8,128)(2,1)} %get-tuple-element.18.refs_1_) | copy-start | bytes 3391492
  26.2 2.7 %collective-permute-start.1 = (bf16[64,512]{1,0:T(8,128)(2,1)S(1)}, bf16[64,512]{1,0:T(8,128)(2,1)S(1)}, u32[]{:S(2)}, u32[]{:S(2)}) collective-permute-start(bf16[64,512]{1,0:T(8,128)(2,1)S(1)} %pad_maximum_fusion), channel_id=1, source_target_pairs={{0,0},{1,128},{2,256},{3,384},{128,1},{129,129},{130,257},{131,385... | collective-permute-start | bytes 196616 | tf_op jit(solution)/shard_map/ppermute | solution.py:314
  27.0 6.2 %collective-permute-start.2 = (bf16[64,512]{1,0:T(8,128)(2,1)S(1)}, bf16[64,512]{1,0:T(8,128)(2,1)S(1)}, u32[]{:S(2)}, u32[]{:S(2)}) collective-permute-start(bf16[64,512]{1,0:T(8,128)(2,1)S(1)} %pad_maximum_fusion), channel_id=1, source_target_pairs={{0,128},{1,256},{2,384},{3,0},{128,129},{129,257},{130,385},{131,1... | collective-permute-start | bytes 196616 | tf_op jit(solution)/shard_map/ppermute | solution.py:314
  45.5 18.7 %copy-start.7 = (bf16[4,144,128]{2,1,0:T(8,128)(2,1)}, bf16[4,144,128]{2,1,0:T(8,128)(2,1)S(1)}, u32[]{:S(2)}) copy-start(bf16[4,144,128]{2,1,0:T(8,128)(2,1)S(1)} %all_to_all.20.refs_1_.refs_3_) | copy-start | bytes 442372
  46.7 28.6 %all-to-all-start.1 = ((bf16[4,144,128]{2,1,0:T(8,128)(2,1)}), bf16[4,144,128]{2,1,0:T(8,128)(2,1)}, u32[]{:S(2)}, u32[]{:S(2)}) async-start(bf16[4,144,128]{2,1,0:T(8,128)(2,1)} %shard_map.85), calls=%async_computation.1 | async-start | bytes 294912 | tf_op jit(solution)/shard_map/all_to_all | solution.py:320
  64.8 21.6 %copy-start.6 = (f32[512,512]{1,0:T(8,128)}, f32[512,512]{1,0:T(8,128)S(1)}, u32[]{:S(2)}) copy-start(f32[512,512]{1,0:T(8,128)S(1)} %get-tuple-element.21.refs_2_.refs_4_) | copy-start | bytes 3145732
  76.3 8.1 %copy-start.13 = (bf16[128,256]{1,0:T(8,128)(2,1)}, bf16[128,256]{1,0:T(8,128)(2,1)S(1)}, u32[]{:S(2)}) copy-start(bf16[128,256]{1,0:T(8,128)(2,1)S(1)} %get-tuple-element.28.refs_4_) | copy-start | bytes 196612
  76.3 8.1 %copy-start.16 = (f32[8,128]{1,0:T(8,128)}, f32[8,128]{1,0:T(8,128)S(1)}, u32[]{:S(2)}) copy-start(f32[8,128]{1,0:T(8,128)S(1)} %get-tuple-element.27.refs_2_) | copy-start | bytes 12292
  118.0 9.7 %copy-start.17 = (bf16[1024]{0:T(1024)(128)(2,1)S(1)}, bf16[1024]{0:T(1024)(128)(2,1)}, u32[]{:S(2)}) copy-start(bf16[1024]{0:T(1024)(128)(2,1)} %param.14) | copy-start | bytes 6148
  121.2 46.7 %collective-permute-start.7 = (bf16[16,64,512]{2,1,0:T(8,128)(2,1)}, bf16[16,64,512]{2,1,0:T(8,128)(2,1)S(1)}, u32[]{:S(2)}, u32[]{:S(2)}) collective-permute-start(bf16[16,64,512]{2,1,0:T(8,128)(2,1)} %get-tuple-element.33), channel_id=1, source_target_pairs={{0,128},{128,256},{256,384},{384,0},{1,129},{129,257},{257,385},{3... | collective-permute-start | bytes 3145736 | tf_op jit(solution)/shard_map/ppermute | solution.py:283
  123.6 44.2 %collective-permute-start.6 = (bf16[16,64,512]{2,1,0:T(8,128)(2,1)}, bf16[16,64,512]{2,1,0:T(8,128)(2,1)}, u32[]{:S(2)}, u32[]{:S(2)}) collective-permute-start(bf16[16,64,512]{2,1,0:T(8,128)(2,1)} %get-tuple-element.34), channel_id=1, source_target_pairs={{0,384},{128,0},{256,128},{384,256},{1,385},{129,1},{257,129},{385... | collective-permute-start | bytes 3145736 | tf_op jit(solution)/shard_map/ppermute | solution.py:283
  128.3 39.6 %copy-start = (bf16[1024,1024]{1,0:T(8,128)(2,1)S(1)}, bf16[1024,1024]{1,0:T(8,128)(2,1)}, u32[]{:S(2)}) copy-start(bf16[1024,1024]{1,0:T(8,128)(2,1)} %all-gather.3.cloned.1.call-done) | copy-start | bytes 6291460
  128.3 39.6 %copy-start.15 = (s32[5]{0:T(128)S(1)}, s32[5]{0:T(128)}, u32[]{:S(2)}) copy-start(s32[5]{0:T(128)} %stack.23.refs_0_.at) | copy-start | bytes 64
  135.2 15.1 %collective-permute-start.5 = (bf16[512,512]{1,0:T(8,128)(2,1)}, bf16[512,512]{1,0:T(8,128)(2,1)S(1)}, u32[]{:S(2)}, u32[]{:S(2)}) collective-permute-start(bf16[512,512]{1,0:T(8,128)(2,1)} %shard_map.88.b0), channel_id=1, source_target_pairs={{0,3},{1,0},{2,1},{3,2},{4,7},{5,4},{6,5},{7,6},{8,11},{9,8},{10,9... | collective-permute-start | bytes 1572872 | tf_op jit(solution)/shard_map/ppermute | solution.py:283
  140.2 12.2 %collective-permute-start.4 = (bf16[512,512]{1,0:T(8,128)(2,1)}, bf16[512,512]{1,0:T(8,128)(2,1)S(1)}, u32[]{:S(2)}, u32[]{:S(2)}) collective-permute-start(bf16[512,512]{1,0:T(8,128)(2,1)} %shard_map.88.b0), channel_id=1, source_target_pairs={{0,2},{1,3},{2,0},{3,1},{4,6},{5,7},{6,4},{7,5},{8,10},{9,11},{10,... | collective-permute-start | bytes 1572872 | tf_op jit(solution)/shard_map/ppermute | solution.py:283
  142.6 25.2 %collective-permute-start.3 = (bf16[512,512]{1,0:T(8,128)(2,1)}, bf16[512,512]{1,0:T(8,128)(2,1)S(1)}, u32[]{:S(2)}, u32[]{:S(2)}) collective-permute-start(bf16[512,512]{1,0:T(8,128)(2,1)} %shard_map.88.b0), channel_id=1, source_target_pairs={{0,1},{1,2},{2,3},{3,0},{4,5},{5,6},{6,7},{7,4},{8,9},{9,10},{10,1... | collective-permute-start | bytes 1572872 | tf_op jit(solution)/shard_map/ppermute | solution.py:283
  168.9 7.7 %copy-start.5 = (bf16[512,512]{1,0:T(8,128)(2,1)S(1)}, bf16[512,512]{1,0:T(8,128)(2,1)}, u32[]{:S(2)}) copy-start(bf16[512,512]{1,0:T(8,128)(2,1)} %shard_map.88.b0) | copy-start | bytes 1572868
  173.1 7.7 %collective-permute-start.8 = (bf16[256,1024]{1,0:T(8,128)(2,1)S(1)}, bf16[256,1024]{1,0:T(8,128)(2,1)S(1)}, u32[]{:S(2)}, u32[]{:S(2)}) collective-permute-start(bf16[256,1024]{1,0:T(8,128)(2,1)S(1)} %shard_map.90), channel_id=1, source_target_pairs={{0,4},{4,0},{1,5},{5,1},{2,6},{6,2},{3,7},{7,3},{8,12},{12,8},{9,1... | collective-permute-start | bytes 1572872 | tf_op jit(solution)/shard_map/ppermute | solution.py:21
  (5 other events, 4.2 us)
Sparse Core Ops, SparseCore 0:
  34.1 79.2 all-gather.2

commit v10 on v7

--- a/solution.py
+++ b/solution.py
@@ -14,6 +14,7 @@
 NT = (((1,), (1,)), ((), ()))
 TN = (((0,), (0,)), ((), ()))
 LOGS = 1024
+ROWS = 1072
 
 
 def swap(value):
@@ -66,7 +67,9 @@
     )(*args, *unread)
 
 
-def pack_body(at, keys, values, queries, gates, decay, mix, keep, send, small, levels, sems):
+def pack_body(
+    at, keys, values, queries, gates, decay, mix, keep, send, small, levels, sems
+):
     core = at[0]
     mine = pl.ds(pl.multiple_of(core * 512, 512), 512)
     theirs = pl.ds(pl.multiple_of((1 - core) * 512, 512), 512)
@@ -87,14 +90,14 @@
         logs += [jnp.where(low, levels[l, 0:4], levels[l, 4:8]) for l in range(8)]
         logs = jnp.concatenate(logs + [jnp.zeros((12, 256), F32)], axis=0)
         high = logs.astype(BF)
-        out[LOGS:, 0:256] = high
-        out[LOGS:, 256:512] = (logs - high.astype(F32)).astype(BF)
+        out[LOGS : LOGS + 48, 0:256] = high
+        out[LOGS : LOGS + 48, 256:512] = (logs - high.astype(F32)).astype(BF)
     for copy in copies[2:]:
         copy.wait()
 
 
 def logs_of(block):
-    tile = block[LOGS:, :].astype(F32)
+    tile = block[LOGS : LOGS + 48, :].astype(F32)
     return tile[:, 0:256] + tile[:, 256:512]
 
 
@@ -149,27 +152,26 @@
     send_whole(*blocks_of(near), pay)
 
 
-def far_body(at, near, far, pay, m0, m1, m2, m3, before_out):
+def far_body(at, near, far, message):
     s, t, pair = blocks_of(far)
-    send_whole(s, t, pair, pay)
-    three, four, before = lower_states(s, t, pair, at[2])
-    before_out[...] = jnp.broadcast_to(before, (8, 128))
+    row = (pair * jnp.exp(t[2] + t[3]) + s[2] * jnp.exp(t[3]) + s[3]).astype(BF)
+    row_log = tail(t[0] + t[1] + t[2] + t[3])
+    three, four, before_far = lower_states(s, t, pair, at[2])
+    three, four, before_far = three.astype(BF), four.astype(BF), tail(before_far)
     s, t, pair = blocks_of(near)
-    for k, message in enumerate((m0, m1, m2, m3)):
-        one, two, before = lower_states(s, t, pair, at[1] ^ k)
-        for i, state in enumerate((one, two, three, four)):
-            message[0:128, i * 128 : i * 128 + 128] = state.astype(BF)
-        message[128:144, 0:128] = tail(before)
-        message[128:144, 128:512] = jnp.zeros((16, 384), BF)
-
-
-def last_body(at, last, before, message):
-    one, two, _ = lower_states(*blocks_of(last), at[3])
-    earlier = jnp.exp(before[0:1, :])
-    one, two = (one * earlier).astype(BF), (two * earlier).astype(BF)
     for i in range(4):
-        message[i, :, 0:128] = one
-        message[i, :, 128:256] = two
+        one, two, before = lower_states(s, t, pair, jnp.int32(i))
+        for l, state in enumerate((one.astype(BF), two.astype(BF), three, four, row)):
+            message[i, 0:128, l * 128 : l * 128 + 128] = state
+        message[i, 128:144, 0:128] = tail(before)
+        message[i, 128:144, 128:256] = before_far
+        message[i, 128:144, 256:512] = jnp.zeros((16, 256), BF)
+        message[i, 128:144, 512:640] = row_log
+
+
+def spread_body(at, message, pay):
+    for i in range(4):
+        pay[i] = message[:, :, 512:640]
 
 
 def place(s, core):
@@ -208,11 +210,10 @@
                 coef[here, 6 * h + l - 2 : 6 * h + l - 1] = start * m[l]
 
 
-def mix_body(at, keep, got, mixture, coef, m0, m1, m2, m3, mixed, later, states):
-    for k, message in enumerate((m0, m1, m2, m3)):
-        states[at[1] ^ k] = message[...]
+def mix_body(at, keep, got, mixture, coef, states, mixed, later):
     for h in range(4):
-        before = jnp.exp(untail(states[h, 128:144, 0:128])[:, 0:1])
+        near = untail(states[h, 128:144, 0:128])[:, 0:1]
+        far = untail(states[h, 128:144, 128:256])[:, 0:1]
         hc = slice(h * 128, h * 128 + 128)
         for s, ref in enumerate((keep, got)):
             _, here = place(s, at[0])
@@ -221,21 +222,23 @@
                 if l % 2 == 0:
                     read = dot(ref[512:768, hc], states[h, 0:128, l * 128 : l * 128 + 256])
                 scale = coef[here, 6 * h + l : 6 * h + l + 1]
-                scale = scale if l < 2 else scale * before
+                scale = scale if l < 2 else scale * jnp.exp(near)
                 total += read[:, (l % 2) * 128 : (l % 2) * 128 + 128] * scale
             mixed[here, hc] = total
-            later[here, 2 * h : 2 * h + 2] = coef[here, 6 * h + 4 : 6 * h + 6] * before
-
-
-def norm_body(at, keep, got, gain, mixture, coef, last, normed):
+            later[here, 2 * h : 2 * h + 2] = coef[here, 6 * h + 4 : 6 * h + 6] * jnp.exp(near + far)
+
+
+def norm_body(at, keep, got, gain, mixture, coef, rows, normed):
     core = at[0]
     for h in range(4):
+        one, two, _ = lower_states(*blocks_of(rows.at[:, h]), at[3])
+        states = jnp.concatenate([one.astype(BF), two.astype(BF)], axis=1)
         mine = pl.ds(pl.multiple_of(core * 512 + h * 128, 128), 128)
         hc = slice(h * 128, h * 128 + 128)
         for s, ref in enumerate((keep, got)):
             _, here = place(s, core)
             z = ref[768:1024, hc].astype(F32)
-            read = dot(ref[512:768, hc], last[h])
+            read = dot(ref[512:768, hc], states)
             total = mixture[here, hc]
             total += read[:, 0:128] * coef[here, 2 * h : 2 * h + 1]
             total += read[:, 128:256] * coef[here, 2 * h + 1 : 2 * h + 2]
@@ -244,57 +247,37 @@
             normed[here, hc] = (gated * size * gain[:, mine].astype(F32)).astype(BF)
 
 
-def project_body(
-    other, at, a0, a1, a2, a3, b0, b1, b2, b3, gathered, w1, w2, w3, out, left, right, sems
-):
+def project_body(other, at, b0, b1, b2, b3, gathered, next_right, far_right, out, left, right, sems):
     row = (1 - at[0]) if other else at[0]
     rows = pl.ds(pl.multiple_of(row * 256, 256), 256)
-    pieces = [gathered.at[:, 0:512], gathered.at[:, 512:1024]]
-    pieces += [gathered.at[:, 512 + 512 * k : 1024 + 512 * k] for k in (1, 2, 3)] + [w1, w2, w3]
+    pieces = (gathered.at[:, :, 0:512], gathered.at[:, :, 512:1024], next_right, far_right)
     copies = [
-        pltpu.make_async_copy(piece, right.at[i], sems.at[i]) for i, piece in enumerate(pieces)
+        pltpu.make_async_copy(piece, right.at[k], sems.at[k]) for k, piece in enumerate(pieces)
     ]
     for copy in copies:
         copy.start()
-    for j, (own, got) in enumerate(((a0, b0), (a1, b1), (a2, b2), (a3, b3))):
-        spot = (at[4] + 4 - j) % 4
-        left[at[0], spot] = own[rows, :]
-        left[1 - at[0], spot] = got[rows, :]
+    for j, block in enumerate((b0, b1, b2, b3)):
+        left[(at[4] + 4 - j) % 4] = block[rows, :]
     total = 0.0
-    for i, (half, k) in enumerate(
-        ((0, 0), (1, 0), (0, 1), (0, 2), (0, 3), (1, 1), (1, 2), (1, 3))
-    ):
-        copies[i].wait()
-        total += dot(left[half, (at[3] + 4 - k) % 4], right[i], NT)
-    out[...] = total.astype(BF)
-
-
-def project(at, owns, gots, gathered, lates, other):
+    for k, turn in enumerate((0, 3, 1, 2)):
+        copies[k].wait()
+        total += dot(left[(at[3] + turn) % 4], right[k].reshape(1024, 512), NT)
+    out[...] = total.astype(out.dtype)
+
+
+def project(at, blocks, gathered, next_right, far_right, other):
     return call(
         functools.partial(project_body, other),
-        [((256, 512), BF)],
-        (at, *owns, *gots, gathered, *lates),
+        [((256, 1024), BF if other else F32)],
+        (at, *blocks, gathered, next_right, far_right),
         scratch=[
-            pltpu.VMEM((2, 4, 256, 512), BF),
-            pltpu.VMEM((8, 512, 512), BF),
-            pltpu.SemaphoreType.DMA((8,)),
+            pltpu.VMEM((4, 256, 512), BF),
+            pltpu.VMEM((4, 16, 64, 512), BF),
+            pltpu.SemaphoreType.DMA((4,)),
         ],
-        hbm=range(9, 13),
+        hbm=(5, 6, 7),
         vmem=20,
     )[0]
-
-
-def weave_body(at, own, got, out):
-    core = at[0]
-    i = lax.broadcasted_iota(jnp.int32, (128, 256), 0)
-    j = lax.broadcasted_iota(jnp.int32, (128, 256), 1)
-    spot = (i >> 5) * 64 + (i & 31)
-    mine = (j == spot + core * 32).astype(BF)
-    theirs = (j == spot + (1 - core) * 32).astype(BF)
-    for m in range(4):
-        cols = slice(m * 128, m * 128 + 128)
-        both = dot(own[:, cols], mine) + dot(got[:, cols], theirs)
-        out[:, m * 256 : m * 256 + 256] = both.astype(BF)
 
 
 def shift(value, axis, by):
@@ -304,7 +287,16 @@
 def shards(values, keys, queries, gates, log_decay, level_mix, norm_gain, weight):
     y, a, b, c, x = (lax.axis_index(n) for n in ("y", "a", NEAR, "c", "x"))
     at = jnp.stack([c, b, a, y, x]).astype(jnp.int32)
-    block = ((LOGS + 48, 512), BF)
+    kept = lax.dynamic_slice_in_dim(weight, c * 512, 512, 1)
+    theirs = swap(lax.dynamic_slice_in_dim(weight, (1 - c) * 512, 512, 1))
+    both = jnp.concatenate(
+        [jnp.where(c == 0, kept, theirs), jnp.where(c == 0, theirs, kept)]
+    )
+    mine = []
+    for k in range(2):
+        perm = [(s * 4 + f, ((f + k) % 4) * 4 + s) for s in range(4) for f in range(4)]
+        mine.append(lax.ppermute(both, ("y", "x"), perm))
+    block = ((ROWS, 512), BF)
     keep, send = call(
         pack_body,
         [block, block],
@@ -317,16 +309,11 @@
         hbm=range(1, 7),
         vmem=60,
     )
+    mine, send = lax.optimization_barrier((mine, send))
+    mine = jnp.concatenate(mine, axis=1)
+    gathered = lax.all_gather(mine, ("a", "p", "q"))
+
     got = swap(send)
-    mine = []
-    for k in range(4):
-        perm = [(s * 4 + f, ((f + k) % 4) * 4 + s) for s in range(4) for f in range(4)]
-        mine.append(lax.ppermute(weight[:, : 512 if k else 1024], ("y", "x"), perm))
-    mine = jnp.concatenate(mine, axis=1)
-    gathered = lax.all_gather(mine, ("a", "p", "q"), axis=0, tiled=True)
-    late = gathered[:, 512:1024]
-    lates = [shift(late, "y", k) for k in (1, 2, 3)]
-
     pay = ((4, 144, 128), BF)
     pay_b, first = call(ends_body, [pay, ((4, 128, 128), BF)], (at, keep, got))
     near = lax.all_to_all(pay_b, NEAR, 0, 0, tiled=True)
@@ -335,33 +322,26 @@
     mixture, coef = call(
         own_body, [((512, 512), F32), ((512, 24), F32)], (at, keep, got, first)
     )
-    pay_y, *messages, before = call(
-        far_body,
-        [pay] + [((144, 512), BF)] * 4 + [((8, 128), F32)],
-        (at, near, far),
-        unread=(mixture,),
-    )
-    last = lax.all_to_all(pay_y, "y", 0, 0, tiled=True)
-    messages = messages[:1] + [
-        lax.ppermute(messages[k], NEAR, [(i, i ^ k) for i in range(4)]) for k in (1, 2, 3)
-    ]
-    (last,) = call(last_body, [((4, 128, 256), BF)], (at, last, before))
-    last = lax.all_to_all(last, NEAR, 0, 0, tiled=True)
+    (message,) = call(far_body, [((4, 144, 640), BF)], (at, near, far), unread=(mixture,))
+    states = lax.all_to_all(message, NEAR, 0, 0, tiled=True)
+    (pay_y,) = call(spread_body, [((4, 4, 144, 128), BF)], (at, states))
+    rows = lax.all_to_all(pay_y, "y", 0, 0, tiled=True)
     mixture, coef = call(
         mix_body,
         [((512, 512), F32), ((512, 8), F32)],
-        (at, keep, got, mixture, coef, *messages),
-        scratch=[pltpu.VMEM((4, 144, 512), BF)],
+        (at, keep, got, mixture, coef, states),
     )
     (normed,) = call(
-        norm_body, [((512, 512), BF)], (at, keep, got, norm_gain[None], mixture, coef, last)
-    )
-
-    owns = [normed] + [shift(normed, "x", j) for j in (1, 2, 3)]
-    gots = [swap(block) for block in owns]
-    theirs = swap(project(at, owns, gots, gathered, lates, True))
-    own = project(at, owns, gots, gathered, lates, False)
-    return call(weave_body, [((256, 1024), BF)], (at, own, theirs))[0]
+        norm_body, [((512, 512), BF)], (at, keep, got, norm_gain[None], mixture, coef, rows)
+    )
+
+    normed, gathered = lax.optimization_barrier((normed, gathered))
+    next_right = shift(gathered[:, :, :512], "y", 3)
+    far_right = shift(gathered[:, :, 512:], "y", 1)
+    blocks = [normed] + [shift(normed, "x", j) for j in (1, 2, 3)]
+    theirs = swap(project(at, blocks, gathered, next_right, far_right, True))
+    own = project(at, blocks, gathered, next_right, far_right, False)
+    return (own + theirs.astype(F32)).astype(BF)
 
 
 def solution(mesh):

time: 221 us -> 181 us (0.82); the launches traced: 217 us -> 180 us
  starting transfers between devices: 91 us -> 54.1 us
  blocking collectives: 23 us -> 37.3 us
  waiting for transfers between devices: 47.7 us -> 36.9 us
  Pallas kernels: 26.9 us -> 23 us
    ppermute x7 -> x2, starting transfers between devices: 26.5 us -> 2.59 us  [shards(): mine.append(lax.ppermute(both, ('y', 'x'), perm))]
    all_to_all x1, blocking collectives: 9.56 us -> 28.8 us  [shards(): states = lax.all_to_all(message, NEAR, 0, 0, tiled=True)]
    ppermute x6 -> x3, starting transfers between devices: 27.3 us -> 13.7 us  [swap(): return lax.ppermute(value, 'c', [(0, 1), (1, 0)])]
    ppermute x7 -> x2, waiting for transfers between devices: 11.8 us -> 0.01 us  [shards(): mine.append(lax.ppermute(both, ('y', 'x'), perm))]
    all_to_all x1, starting transfers between devices: 3.4 us -> 13.6 us  [shards(): rows = lax.all_to_all(pay_y, 'y', 0, 0, tiled=True)]
    ppermute x6 -> x5, starting transfers between devices: 22.3 us -> 13.7 us  [shift(): return lax.ppermute(value, axis, [(i, (i + by) % 4) for i in range(4)])]
    all_to_all x1, blocking collectives: 13.5 us -> 8.45 us  [shards(): near = lax.all_to_all(pay_b, NEAR, 0, 0, tiled=True)]
    pallas_call x11 -> x10, Pallas kernels: 26.9 us -> 23 us  [call(): pl.pallas_call(run, out_shape=[jax.ShapeDtypeStruct(*o) for o in outs], i...]
  transfers between devices with their start and end apart: 22 -> 13, of which waited for: 9 -> 7; matrix products, arithmetic and copies ran while one was open for 1% -> 1% of each run, Pallas kernels for 10% -> 11%
where the time goes in v10:
time: 181 us; the launch traced here: 180 us
  starting transfers between devices  54.1 us (30%)
  blocking collectives  37.3 us (21%)
  waiting for transfers between devices  36.9 us (20%)
  Pallas kernels  23 us (13%)
  between operations  13.6 us (8%)
  local copies, waits for them, and re-layouts  13.2 us (7%)
  other arithmetic  2.39 us (1%)
    all_to_all x1, blocking collectives, shards(): states = lax.all_to_all(message, NEAR, 0, 0, tiled=True)  28.8 us
    ppermute x5, waiting for transfers between devices, shift(): return lax.ppermute(value, axis, [(i, (i + by) % 4) for i in range(4)])  23.2 us
    pallas_call x10, Pallas kernels, call(): pl.pallas_call(run, out_shape=[jax.ShapeDtypeStruct(*o) for o in outs], i...  23 us
    ppermute x5, starting transfers between devices, shift(): return lax.ppermute(value, axis, [(i, (i + by) % 4) for i in range(4)])  13.7 us
    ppermute x3, starting transfers between devices, swap(): return lax.ppermute(value, 'c', [(0, 1), (1, 0)])  13.7 us
    all_to_all x1, starting transfers between devices, shards(): rows = lax.all_to_all(pay_y, 'y', 0, 0, tiled=True)  13.6 us
    all_to_all x1, starting transfers between devices, shards(): far = lax.all_to_all(pay_a, 'a', 0, 0, tiled=True)  10.5 us
    unnamed x30, local copies, waits for them, and re-layouts  9.89 us
  transfers between devices with their start and end apart: 13, of which 7 were waited for; matrix products, arithmetic and copies ran while one was open for 1% of the time, Pallas kernels for 11%

profile of v10, /device:TPU:1, one launch (start us, length us, event | category | flops | bytes accessed | tf_op | source)
XLA Modules:
  0.0 180.4 jit_solution(7690623596697306786)
XLA Ops:
  7.3 8.8 %collective-permute-start = (bf16[32,512]{1,0:T(8,128)(2,1)S(1)}, bf16[32,512]{1,0:T(8,128)(2,1)S(1)}, u32[]{:S(2)}, u32[]{:S(2)}) collective-permute-start(bf16[32,512]{1,0:T(8,128)(2,1)S(1)} %constant_dynamic-slice_fusion), channel_id=1, source_target_pairs={{0,4},{4,0},{1,5},{5,1},{2,6},{6,2},{3,7},{7,3},{8,12},{12,8},{9,1... | collective-permute-start | bytes 98312 | tf_op jit(solution)/shard_map/ppermute | solution.py:21
  17.7 1.9 %collective-permute-start.2 = (bf16[64,512]{1,0:T(8,128)(2,1)S(1)}, bf16[64,512]{1,0:T(8,128)(2,1)S(1)}, u32[]{:S(2)}, u32[]{:S(2)}) collective-permute-start(bf16[64,512]{1,0:T(8,128)(2,1)S(1)} %pad_maximum_fusion.1), channel_id=1, source_target_pairs={{0,128},{1,256},{2,384},{3,0},{128,129},{129,257},{130,385},{131,1... | collective-permute-start | bytes 196616 | tf_op jit(solution)/shard_map/ppermute | solution.py:298
  21.0 3.8 %shard_map.82 = (bf16[1072,512]{1,0:T(8,128)(2,1)}, bf16[1072,512]{1,0:T(8,128)(2,1)}) custom-call(s32[5]{0:T(128)} %stack.23.refs_0_, bf16[256,1024]{1,0:T(8,128)(2,1)} %refs_1_.1, bf16[256,1024]{1,0:T(8,128)(2,1)} %refs_2_.1, bf16[256,1024]{1,0:T(8,128)(2,1)} %refs_3_.1, bf16[256,1024]{1,0:T(8,128)(2,1)} %refs_4_.1, f32[8,256]{1,0:T(8,128)} %refs_5_.1, ...), custom_call_target="tpu_custom_call" | custom-call | flops 1000000 | bytes 1000000 | tf_op jit(solution)/shard_map/pallas_call | solution.py:59
  24.8 2.5 %collective-permute-start.3 = (bf16[1072,512]{1,0:T(8,128)(2,1)}, bf16[1072,512]{1,0:T(8,128)(2,1)S(1)}, u32[]{:S(2)}, u32[]{:S(2)}) collective-permute-start(bf16[1072,512]{1,0:T(8,128)(2,1)} %get-tuple-element.20), channel_id=1, source_target_pairs={{0,4},{4,0},{1,5},{5,1},{2,6},{6,2},{3,7},{7,3},{8,12},{12,8},{9,1... | collective-permute-start | bytes 3293192 | tf_op jit(solution)/shard_map/ppermute | solution.py:21
  32.9 8.5 %all_to_all.20.refs_1_ = bf16[4,144,128]{2,1,0:T(8,128)(2,1)S(1)} all-to-all(bf16[4,144,128]{2,1,0:T(8,128)(2,1)S(1)} %get-tuple-element.24), channel_id=1, replica_groups=mesh['y'=4,'a'=4,'p'=2,'q'=2,'c'=2,'x'=4] {'p','q'}, dimensions={0} | all-to-all | bytes 294912 | tf_op jit(solution)/shard_map/all_to_all | solution.py:319
  42.6 10.5 %all-to-all-start.1 = ((bf16[4,144,128]{2,1,0:T(8,128)(2,1)}), bf16[4,144,128]{2,1,0:T(8,128)(2,1)S(1)}, u32[]{:S(2)}, u32[]{:S(2)}) async-start(bf16[4,144,128]{2,1,0:T(8,128)(2,1)} %shard_map.85), calls=%async_computation.1 | async-start | bytes 294912 | tf_op jit(solution)/shard_map/all_to_all | solution.py:321
  54.1 4.3 %shard_map.84 = (f32[512,512]{1,0:T(8,128)S(1)}, f32[512,24]{1,0:T(8,128)S(1)}) custom-call(s32[5]{0:T(128)S(1)} %copy-done.13, bf16[1072,512]{1,0:T(8,128)(2,1)S(1)} %copy-done.2, bf16[1072,512]{1,0:T(8,128)(2,1)S(1)} %collective-permute-done.3.refs_2_, bf16[4,128,128]{2,1,0:T(8,128)(2,1)S(1)} %copy-done.12), custom_call_target="tpu_custom_call" | custom-call | flops 1000000 | bytes 1000000 | tf_op jit(solution)/shard_map/pallas_call | solution.py:59
  59.1 8.8 %all-to-all-done.1.refs_2_ = bf16[4,144,128]{2,1,0:T(8,128)(2,1)S(1)} async-done(((bf16[4,144,128]{2,1,0:T(8,128)(2,1)}), bf16[4,144,128]{2,1,0:T(8,128)(2,1)S(1)}, u32[]{:S(2)}, u32[]{:S(2)}) %all-to-all-start.1) | async-done | bytes 147488 | tf_op jit(solution)/shard_map/all_to_all | solution.py:321
  69.5 28.8 %all_to_all.21.refs_5_.refs_1_ = bf16[4,144,640]{2,1,0:T(8,128)(2,1)S(1)} all-to-all(bf16[4,144,640]{2,1,0:T(8,128)(2,1)S(1)} %shard_map.86), channel_id=1, replica_groups=mesh['y'=4,'a'=4,'p'=2,'q'=2,'c'=2,'x'=4] {'p','q'}, dimensions={0} | all-to-all | bytes 1474560 | tf_op jit(solution)/shard_map/all_to_all | solution.py:326
  99.8 13.6 %all-to-all-start.3 = ((bf16[4,4,144,128]{3,2,1,0:T(8,128)(2,1)}), bf16[4,4,144,128]{3,2,1,0:T(8,128)(2,1)S(1)}, u32[]{:S(2)}, u32[]{:S(2)}) async-start(bf16[4,4,144,128]{3,2,1,0:T(8,128)(2,1)} %shard_map.88), calls=%async_computation.3 | async-start | bytes 1179648 | tf_op jit(solution)/shard_map/all_to_all | solution.py:328
  115.5 2.5 %shard_map.87 = (f32[512,512]{1,0:T(8,128)S(1)}, f32[512,8]{1,0:T(8,128)S(1)}) custom-call(s32[5]{0:T(128)S(1)} %copy-done.13, bf16[1072,512]{1,0:T(8,128)(2,1)S(1)} %copy-done.2, bf16[1072,512]{1,0:T(8,128)(2,1)S(1)} %collective-permute-done.3.refs_2_, f32[512,512]{1,0:T(8,128)S(1)} %copy-done.4, f32[512,24]{1,0:T(8,128)S(1)} %copy-done.8, ...), custom_call_target="tpu_custom_call" | custom-call | flops 1000000 | bytes 1000000 | tf_op jit(solution)/shard_map/pallas_call | solution.py:59
  119.7 2.2 %all-to-all-done.3.refs_6_ = bf16[4,4,144,128]{3,2,1,0:T(8,128)(2,1)S(1)} async-done(((bf16[4,4,144,128]{3,2,1,0:T(8,128)(2,1)}), bf16[4,4,144,128]{3,2,1,0:T(8,128)(2,1)S(1)}, u32[]{:S(2)}, u32[]{:S(2)}) %all-to-all-start.3) | async-done | bytes 589856 | tf_op jit(solution)/shard_map/all_to_all | solution.py:328
  124.1 2.0 %shard_map.89.refs_1_ = bf16[512,512]{1,0:T(8,128)(2,1)S(1)} custom-call(s32[5]{0:T(128)S(1)} %copy-done.13, bf16[1072,512]{1,0:T(8,128)(2,1)S(1)} %copy-done.2, bf16[1072,512]{1,0:T(8,128)(2,1)S(1)} %collective-permute-done.3.refs_2_, bf16[1,1024]{1,0:T(2,128)(2,1)S(1)} %broadcast_in_dim.3.refs_3_, f32[512,512]{1,0:T(8,128)S(1)} %copy-done.6, ...), custom_call_target="tpu_custom_call" | custom-call | flops 1000000 | bytes 1000000 | tf_op jit(solution)/shard_map/pallas_call | solution.py:59
  128.0 2.2 %collective-permute-start.8 = (bf16[16,64,512]{2,1,0:T(8,128)(2,1)S(1)}, bf16[16,64,512]{2,1,0:T(8,128)(2,1)S(1)}, u32[]{:S(2)}, u32[]{:S(2)}) collective-permute-start(bf16[16,64,512]{2,1,0:T(8,128)(2,1)S(1)} %get-tuple-element.31), channel_id=1, source_target_pairs={{0,128},{128,256},{256,384},{384,0},{1,129},{129,257},{257,385},{3... | collective-permute-start | bytes 3145736 | tf_op jit(solution)/shard_map/ppermute | solution.py:284
  130.2 4.3 %collective-permute-start.7 = (bf16[16,64,512]{2,1,0:T(8,128)(2,1)S(1)}, bf16[16,64,512]{2,1,0:T(8,128)(2,1)S(1)}, u32[]{:S(2)}, u32[]{:S(2)}) collective-permute-start(bf16[16,64,512]{2,1,0:T(8,128)(2,1)S(1)} %get-tuple-element.32), channel_id=1, source_target_pairs={{0,384},{128,0},{256,128},{384,256},{1,385},{129,1},{257,129},{385... | collective-permute-start | bytes 3145736 | tf_op jit(solution)/shard_map/ppermute | solution.py:284
  134.5 1.9 %collective-permute-start.6 = (bf16[512,512]{1,0:T(8,128)(2,1)S(1)}, bf16[512,512]{1,0:T(8,128)(2,1)S(1)}, u32[]{:S(2)}, u32[]{:S(2)}) collective-permute-start(bf16[512,512]{1,0:T(8,128)(2,1)S(1)} %shard_map.89.refs_1_), channel_id=1, source_target_pairs={{0,3},{1,0},{2,1},{3,2},{4,7},{5,4},{6,5},{7,6},{8,11},{9,8},{10,9... | collective-permute-start | bytes 1572872 | tf_op jit(solution)/shard_map/ppermute | solution.py:284
  136.4 2.4 %collective-permute-start.5 = (bf16[512,512]{1,0:T(8,128)(2,1)S(1)}, bf16[512,512]{1,0:T(8,128)(2,1)S(1)}, u32[]{:S(2)}, u32[]{:S(2)}) collective-permute-start(bf16[512,512]{1,0:T(8,128)(2,1)S(1)} %shard_map.89.refs_1_), channel_id=1, source_target_pairs={{0,2},{1,3},{2,0},{3,1},{4,6},{5,7},{6,4},{7,5},{8,10},{9,11},{10,... | collective-permute-start | bytes 1572872 | tf_op jit(solution)/shard_map/ppermute | solution.py:284
  138.9 2.8 %collective-permute-start.4 = (bf16[512,512]{1,0:T(8,128)(2,1)S(1)}, bf16[512,512]{1,0:T(8,128)(2,1)S(1)}, u32[]{:S(2)}, u32[]{:S(2)}) collective-permute-start(bf16[512,512]{1,0:T(8,128)(2,1)S(1)} %shard_map.89.refs_1_), channel_id=1, source_target_pairs={{0,1},{1,2},{2,3},{3,0},{4,5},{5,6},{6,7},{7,4},{8,9},{9,10},{10,1... | collective-permute-start | bytes 1572872 | tf_op jit(solution)/shard_map/ppermute | solution.py:284
  141.7 4.9 %collective-permute-done.6.refs_4_ = bf16[512,512]{1,0:T(8,128)(2,1)S(1)} collective-permute-done((bf16[512,512]{1,0:T(8,128)(2,1)S(1)}, bf16[512,512]{1,0:T(8,128)(2,1)S(1)}, u32[]{:S(2)}, u32[]{:S(2)}) %collective-permute-start.6) | collective-permute-done | bytes 524320 | tf_op jit(solution)/shard_map/ppermute | solution.py:284
  146.7 3.5 %collective-permute-done.5.refs_3_ = bf16[512,512]{1,0:T(8,128)(2,1)S(1)} collective-permute-done((bf16[512,512]{1,0:T(8,128)(2,1)S(1)}, bf16[512,512]{1,0:T(8,128)(2,1)S(1)}, u32[]{:S(2)}, u32[]{:S(2)}) %collective-permute-start.5) | collective-permute-done | bytes 524320 | tf_op jit(solution)/shard_map/ppermute | solution.py:284
  150.2 14.8 %collective-permute-done.4.refs_2_ = bf16[512,512]{1,0:T(8,128)(2,1)S(1)} collective-permute-done((bf16[512,512]{1,0:T(8,128)(2,1)S(1)}, bf16[512,512]{1,0:T(8,128)(2,1)S(1)}, u32[]{:S(2)}, u32[]{:S(2)}) %collective-permute-start.4) | collective-permute-done | bytes 524320 | tf_op jit(solution)/shard_map/ppermute | solution.py:284
  164.9 2.6 %shard_map.91 = bf16[256,1024]{1,0:T(8,128)(2,1)S(1)} custom-call(s32[5]{0:T(128)S(1)} %copy-done.13, bf16[512,512]{1,0:T(8,128)(2,1)S(1)} %shard_map.89.refs_1_, bf16[512,512]{1,0:T(8,128)(2,1)S(1)} %collective-permute-done.4.refs_2_, bf16[512,512]{1,0:T(8,128)(2,1)S(1)} %collective-permute-done.5.refs_3_, ...), custom_call_target="tpu_custom_call" | custom-call | flops 1000000 | bytes 1000000 | tf_op jit(solution)/shard_map/pallas_call | solution.py:59
  167.6 2.4 %collective-permute-start.9 = (bf16[256,1024]{1,0:T(8,128)(2,1)S(1)}, bf16[256,1024]{1,0:T(8,128)(2,1)S(1)}, u32[]{:S(2)}, u32[]{:S(2)}) collective-permute-start(bf16[256,1024]{1,0:T(8,128)(2,1)S(1)} %shard_map.91), channel_id=1, source_target_pairs={{0,4},{4,0},{1,5},{5,1},{2,6},{6,2},{3,7},{7,3},{8,12},{12,8},{9,1... | collective-permute-start | bytes 1572872 | tf_op jit(solution)/shard_map/ppermute | solution.py:21
  170.0 2.6 %shard_map.90 = f32[256,1024]{1,0:T(8,128)S(1)} custom-call(s32[5]{0:T(128)S(1)} %copy-done.13, bf16[512,512]{1,0:T(8,128)(2,1)S(1)} %shard_map.89.refs_1_, bf16[512,512]{1,0:T(8,128)(2,1)S(1)} %collective-permute-done.4.refs_2_, bf16[512,512]{1,0:T(8,128)(2,1)S(1)} %collective-permute-done.5.refs_3_, bf16[512,512]{1,0:T(8,128)(2,1)S(1)} %collective-permute-done.6.refs_4_, ...), custom_call_target="tpu_custom_call" | custom-call | flops 1000000 | bytes 1000000 | tf_op jit(solution)/shard_map/pallas_call | solution.py:59
  (53 shorter events, 24.1 us)
Async XLA Ops:
  6.5 119.6 %all-gather.3.cloned.1.call-start = ((), (), s32[]{:S(2)}) async-start(), calls=%async_computation.4 | async-start | bytes 2228224 | tf_op jit(solution)/shard_map/all_gather | solution.py:314
  7.3 9.6 %collective-permute-start = (bf16[32,512]{1,0:T(8,128)(2,1)S(1)}, bf16[32,512]{1,0:T(8,128)(2,1)S(1)}, u32[]{:S(2)}, u32[]{:S(2)}) collective-permute-start(bf16[32,512]{1,0:T(8,128)(2,1)S(1)} %constant_dynamic-slice_fusion), channel_id=1, source_target_pairs={{0,4},{4,0},{1,5},{5,1},{2,6},{6,2},{3,7},{7,3},{8,12},{12,8},{9,1... | collective-permute-start | bytes 98312 | tf_op jit(solution)/shard_map/ppermute | solution.py:21
  17.7 7.1 %collective-permute-start.2 = (bf16[64,512]{1,0:T(8,128)(2,1)S(1)}, bf16[64,512]{1,0:T(8,128)(2,1)S(1)}, u32[]{:S(2)}, u32[]{:S(2)}) collective-permute-start(bf16[64,512]{1,0:T(8,128)(2,1)S(1)} %pad_maximum_fusion.1), channel_id=1, source_target_pairs={{0,128},{1,256},{2,384},{3,0},{128,129},{129,257},{130,385},{131,1... | collective-permute-start | bytes 196616 | tf_op jit(solution)/shard_map/ppermute | solution.py:298
  19.6 5.2 %collective-permute-start.1 = (bf16[64,512]{1,0:T(8,128)(2,1)S(1)}, bf16[64,512]{1,0:T(8,128)(2,1)S(1)}, u32[]{:S(2)}, u32[]{:S(2)}) collective-permute-start(bf16[64,512]{1,0:T(8,128)(2,1)S(1)} %pad_maximum_fusion.1), channel_id=1, source_target_pairs={{0,0},{1,128},{2,256},{3,384},{128,1},{129,129},{130,257},{131,385... | collective-permute-start | bytes 196616 | tf_op jit(solution)/shard_map/ppermute | solution.py:298
  21.0 8.9 %copy-start.13 = (s32[5]{0:T(128)S(1)}, s32[5]{0:T(128)}, u32[]{:S(2)}) copy-start(s32[5]{0:T(128)} %stack.23.refs_0_) | copy-start | bytes 64
  24.8 5.1 %collective-permute-start.3 = (bf16[1072,512]{1,0:T(8,128)(2,1)}, bf16[1072,512]{1,0:T(8,128)(2,1)S(1)}, u32[]{:S(2)}, u32[]{:S(2)}) collective-permute-start(bf16[1072,512]{1,0:T(8,128)(2,1)} %get-tuple-element.20), channel_id=1, source_target_pairs={{0,4},{4,0},{1,5},{5,1},{2,6},{6,2},{3,7},{7,3},{8,12},{12,8},{9,1... | collective-permute-start | bytes 3293192 | tf_op jit(solution)/shard_map/ppermute | solution.py:21
  29.9 1.2 copy-start.1
  31.1 22.0 %copy-start.2 = (bf16[1072,512]{1,0:T(8,128)(2,1)S(1)}, bf16[1072,512]{1,0:T(8,128)(2,1)}, u32[]{:S(2)}) copy-start(bf16[1072,512]{1,0:T(8,128)(2,1)} %get-tuple-element.18.refs_1_) | copy-start | bytes 3293188
  32.9 8.5 %copy-start.11 = (bf16[4,128,128]{2,1,0:T(8,128)(2,1)}, bf16[4,128,128]{2,1,0:T(8,128)(2,1)S(1)}, u32[]{:S(2)}) copy-start(bf16[4,128,128]{2,1,0:T(8,128)(2,1)S(1)} %get-tuple-element.21.refs_3_) | copy-start | bytes 393220
  42.6 25.3 %all-to-all-start.1 = ((bf16[4,144,128]{2,1,0:T(8,128)(2,1)}), bf16[4,144,128]{2,1,0:T(8,128)(2,1)S(1)}, u32[]{:S(2)}, u32[]{:S(2)}) async-start(bf16[4,144,128]{2,1,0:T(8,128)(2,1)} %shard_map.85), calls=%async_computation.1 | async-start | bytes 294912 | tf_op jit(solution)/shard_map/all_to_all | solution.py:321
  68.6 1.0 copy-start.3
  98.3 15.0 %copy-start.14 = (bf16[1024]{0:T(1024)(128)(2,1)S(1)}, bf16[1024]{0:T(1024)(128)(2,1)}, u32[]{:S(2)}) copy-start(bf16[1024]{0:T(1024)(128)(2,1)} %param.14) | copy-start | bytes 6148
  99.8 22.1 %all-to-all-start.3 = ((bf16[4,4,144,128]{3,2,1,0:T(8,128)(2,1)}), bf16[4,4,144,128]{3,2,1,0:T(8,128)(2,1)S(1)}, u32[]{:S(2)}, u32[]{:S(2)}) async-start(bf16[4,4,144,128]{3,2,1,0:T(8,128)(2,1)} %shard_map.88), calls=%async_computation.3 | async-start | bytes 1179648 | tf_op jit(solution)/shard_map/all_to_all | solution.py:328
  113.4 1.2 copy-start.4
  114.6 0.9 copy-start.8
  118.0 1.0 copy-start.5
  121.9 1.2 copy-start.6
  126.2 38.8 %copy-start = (bf16[1024,1024]{1,0:T(8,128)(2,1)S(1)}, bf16[1024,1024]{1,0:T(8,128)(2,1)}, u32[]{:S(2)}) copy-start(bf16[1024,1024]{1,0:T(8,128)(2,1)} %all-gather.3.cloned.1.call-done) | copy-start | bytes 6291460
  128.0 36.9 %collective-permute-start.8 = (bf16[16,64,512]{2,1,0:T(8,128)(2,1)S(1)}, bf16[16,64,512]{2,1,0:T(8,128)(2,1)S(1)}, u32[]{:S(2)}, u32[]{:S(2)}) collective-permute-start(bf16[16,64,512]{2,1,0:T(8,128)(2,1)S(1)} %get-tuple-element.31), channel_id=1, source_target_pairs={{0,128},{128,256},{256,384},{384,0},{1,129},{129,257},{257,385},{3... | collective-permute-start | bytes 3145736 | tf_op jit(solution)/shard_map/ppermute | solution.py:284
  130.2 34.7 %collective-permute-start.7 = (bf16[16,64,512]{2,1,0:T(8,128)(2,1)S(1)}, bf16[16,64,512]{2,1,0:T(8,128)(2,1)S(1)}, u32[]{:S(2)}, u32[]{:S(2)}) collective-permute-start(bf16[16,64,512]{2,1,0:T(8,128)(2,1)S(1)} %get-tuple-element.32), channel_id=1, source_target_pairs={{0,384},{128,0},{256,128},{384,256},{1,385},{129,1},{257,129},{385... | collective-permute-start | bytes 3145736 | tf_op jit(solution)/shard_map/ppermute | solution.py:284
  134.5 12.2 %collective-permute-start.6 = (bf16[512,512]{1,0:T(8,128)(2,1)S(1)}, bf16[512,512]{1,0:T(8,128)(2,1)S(1)}, u32[]{:S(2)}, u32[]{:S(2)}) collective-permute-start(bf16[512,512]{1,0:T(8,128)(2,1)S(1)} %shard_map.89.refs_1_), channel_id=1, source_target_pairs={{0,3},{1,0},{2,1},{3,2},{4,7},{5,4},{6,5},{7,6},{8,11},{9,8},{10,9... | collective-permute-start | bytes 1572872 | tf_op jit(solution)/shard_map/ppermute | solution.py:284
  136.4 13.7 %collective-permute-start.5 = (bf16[512,512]{1,0:T(8,128)(2,1)S(1)}, bf16[512,512]{1,0:T(8,128)(2,1)S(1)}, u32[]{:S(2)}, u32[]{:S(2)}) collective-permute-start(bf16[512,512]{1,0:T(8,128)(2,1)S(1)} %shard_map.89.refs_1_), channel_id=1, source_target_pairs={{0,2},{1,3},{2,0},{3,1},{4,6},{5,7},{6,4},{7,5},{8,10},{9,11},{10,... | collective-permute-start | bytes 1572872 | tf_op jit(solution)/shard_map/ppermute | solution.py:284
  138.9 26.0 %collective-permute-start.4 = (bf16[512,512]{1,0:T(8,128)(2,1)S(1)}, bf16[512,512]{1,0:T(8,128)(2,1)S(1)}, u32[]{:S(2)}, u32[]{:S(2)}) collective-permute-start(bf16[512,512]{1,0:T(8,128)(2,1)S(1)} %shard_map.89.refs_1_), channel_id=1, source_target_pairs={{0,1},{1,2},{2,3},{3,0},{4,5},{5,6},{6,7},{7,4},{8,9},{9,10},{10,1... | collective-permute-start | bytes 1572872 | tf_op jit(solution)/shard_map/ppermute | solution.py:284
  167.6 5.0 %collective-permute-start.9 = (bf16[256,1024]{1,0:T(8,128)(2,1)S(1)}, bf16[256,1024]{1,0:T(8,128)(2,1)S(1)}, u32[]{:S(2)}, u32[]{:S(2)}) collective-permute-start(bf16[256,1024]{1,0:T(8,128)(2,1)S(1)} %shard_map.91), channel_id=1, source_target_pairs={{0,4},{4,0},{1,5},{5,1},{2,6},{6,2},{3,7},{7,3},{8,12},{12,8},{9,1... | collective-permute-start | bytes 1572872 | tf_op jit(solution)/shard_map/ppermute | solution.py:21
  (4 other events, 3.3 us)
Sparse Core Ops, SparseCore 0:
  28.1 81.5 all-gather.2

commit v11 on v10

--- a/solution.py
+++ b/solution.py
@@ -148,30 +148,34 @@
     return one, two, before
 
 
-def near_body(at, near, pay):
-    send_whole(*blocks_of(near), pay)
-
-
-def far_body(at, near, far, message):
+def near_body(at, near, pay, *messages):
+    s, t, pair = blocks_of(near)
+    send_whole(s, t, pair, pay)
+    for k, message in enumerate(messages):
+        one, two, before = lower_states(s, t, pair, at[1] ^ k)
+        message[0:128, 0:128] = one.astype(BF)
+        message[0:128, 128:256] = two.astype(BF)
+        message[128:144, 0:128] = tail(before)
+        message[128:144, 128:256] = jnp.zeros((16, 128), BF)
+
+
+def far_body(at, far, pay, states, before_out):
     s, t, pair = blocks_of(far)
-    row = (pair * jnp.exp(t[2] + t[3]) + s[2] * jnp.exp(t[3]) + s[3]).astype(BF)
-    row_log = tail(t[0] + t[1] + t[2] + t[3])
-    three, four, before_far = lower_states(s, t, pair, at[2])
-    three, four, before_far = three.astype(BF), four.astype(BF), tail(before_far)
-    s, t, pair = blocks_of(near)
+    send_whole(s, t, pair, pay)
+    one, two, before = lower_states(s, t, pair, at[2])
+    states[:, 0:128] = one.astype(BF)
+    states[:, 128:256] = two.astype(BF)
+    before_out[...] = jnp.broadcast_to(before, (8, 128))
+
+
+def last_body(at, rows, before, far, message):
+    one, two, _ = lower_states(*blocks_of(rows), at[3])
+    earlier = jnp.exp(before[0:1, :])
+    one, two = (one * earlier).astype(BF), (two * earlier).astype(BF)
     for i in range(4):
-        one, two, before = lower_states(s, t, pair, jnp.int32(i))
-        for l, state in enumerate((one.astype(BF), two.astype(BF), three, four, row)):
-            message[i, 0:128, l * 128 : l * 128 + 128] = state
-        message[i, 128:144, 0:128] = tail(before)
-        message[i, 128:144, 128:256] = before_far
-        message[i, 128:144, 256:512] = jnp.zeros((16, 256), BF)
-        message[i, 128:144, 512:640] = row_log
-
-
-def spread_body(at, message, pay):
-    for i in range(4):
-        pay[i] = message[:, :, 512:640]
+        message[i, :, 0:256] = far[...]
+        message[i, :, 256:384] = one
+        message[i, :, 384:512] = two
 
 
 def place(s, core):
@@ -210,38 +214,33 @@
                 coef[here, 6 * h + l - 2 : 6 * h + l - 1] = start * m[l]
 
 
-def mix_body(at, keep, got, mixture, coef, states, mixed, later):
+def mix_body(at, keep, got, mixture, coef, n0, n1, n2, n3, mixed, later, near):
+    for k, n in enumerate((n0, n1, n2, n3)):
+        near[at[1] ^ k] = n[...]
     for h in range(4):
-        near = untail(states[h, 128:144, 0:128])[:, 0:1]
-        far = untail(states[h, 128:144, 128:256])[:, 0:1]
+        before = jnp.exp(untail(near[h, 128:144, 0:128])[:, 0:1])
         hc = slice(h * 128, h * 128 + 128)
         for s, ref in enumerate((keep, got)):
             _, here = place(s, at[0])
-            total = mixture[here, hc]
-            for l in range(4):
-                if l % 2 == 0:
-                    read = dot(ref[512:768, hc], states[h, 0:128, l * 128 : l * 128 + 256])
-                scale = coef[here, 6 * h + l : 6 * h + l + 1]
-                scale = scale if l < 2 else scale * jnp.exp(near)
-                total += read[:, (l % 2) * 128 : (l % 2) * 128 + 128] * scale
-            mixed[here, hc] = total
-            later[here, 2 * h : 2 * h + 2] = coef[here, 6 * h + 4 : 6 * h + 6] * jnp.exp(near + far)
-
-
-def norm_body(at, keep, got, gain, mixture, coef, rows, normed):
+            read = dot(ref[512:768, hc], near[h, 0:128, :])
+            total = mixture[here, hc] + read[:, 0:128] * coef[here, 6 * h : 6 * h + 1]
+            mixed[here, hc] = total + read[:, 128:256] * coef[here, 6 * h + 1 : 6 * h + 2]
+            later[here, 4 * h : 4 * h + 4] = coef[here, 6 * h + 2 : 6 * h + 6] * before
+
+
+def norm_body(at, keep, got, gain, mixture, coef, states, normed):
     core = at[0]
     for h in range(4):
-        one, two, _ = lower_states(*blocks_of(rows.at[:, h]), at[3])
-        states = jnp.concatenate([one.astype(BF), two.astype(BF)], axis=1)
         mine = pl.ds(pl.multiple_of(core * 512 + h * 128, 128), 128)
         hc = slice(h * 128, h * 128 + 128)
         for s, ref in enumerate((keep, got)):
             _, here = place(s, core)
             z = ref[768:1024, hc].astype(F32)
-            read = dot(ref[512:768, hc], states)
             total = mixture[here, hc]
-            total += read[:, 0:128] * coef[here, 2 * h : 2 * h + 1]
-            total += read[:, 128:256] * coef[here, 2 * h + 1 : 2 * h + 2]
+            for l in range(0, 4, 2):
+                read = dot(ref[512:768, hc], states[h, :, l * 128 : l * 128 + 256])
+                total += read[:, 0:128] * coef[here, 4 * h + l : 4 * h + l + 1]
+                total += read[:, 128:256] * coef[here, 4 * h + l + 1 : 4 * h + l + 2]
             gated = total * (z / (1.0 + jnp.exp(-z)))
             size = lax.rsqrt(jnp.mean(gated * gated, axis=1, keepdims=True) + 1e-05)
             normed[here, hc] = (gated * size * gain[:, mine].astype(F32)).astype(BF)
@@ -317,25 +316,34 @@
     pay = ((4, 144, 128), BF)
     pay_b, first = call(ends_body, [pay, ((4, 128, 128), BF)], (at, keep, got))
     near = lax.all_to_all(pay_b, NEAR, 0, 0, tiled=True)
-    (pay_a,) = call(near_body, [pay], (at, near))
+    pay_a, *near = call(near_body, [pay] + [((144, 256), BF)] * 4, (at, near))
     far = lax.all_to_all(pay_a, "a", 0, 0, tiled=True)
+    near = near[:1] + [
+        lax.ppermute(near[k], NEAR, [(i, i ^ k) for i in range(4)]) for k in (1, 2, 3)
+    ]
     mixture, coef = call(
         own_body, [((512, 512), F32), ((512, 24), F32)], (at, keep, got, first)
     )
-    (message,) = call(far_body, [((4, 144, 640), BF)], (at, near, far), unread=(mixture,))
-    states = lax.all_to_all(message, NEAR, 0, 0, tiled=True)
-    (pay_y,) = call(spread_body, [((4, 4, 144, 128), BF)], (at, states))
+    pay_y, far, before = call(
+        far_body,
+        [pay, ((128, 256), BF), ((8, 128), F32)],
+        (at, far),
+        unread=(mixture, *near[1:]),
+    )
     rows = lax.all_to_all(pay_y, "y", 0, 0, tiled=True)
+    (states,) = call(last_body, [((4, 128, 512), BF)], (at, rows, before, far))
+    states = lax.all_to_all(states, NEAR, 0, 0, tiled=True)
     mixture, coef = call(
         mix_body,
-        [((512, 512), F32), ((512, 8), F32)],
-        (at, keep, got, mixture, coef, states),
+        [((512, 512), F32), ((512, 16), F32)],
+        (at, keep, got, mixture, coef, *near),
+        scratch=[pltpu.VMEM((4, 144, 256), BF)],
     )
     (normed,) = call(
-        norm_body, [((512, 512), BF)], (at, keep, got, norm_gain[None], mixture, coef, rows)
-    )
-
-    normed, gathered = lax.optimization_barrier((normed, gathered))
+        norm_body, [((512, 512), BF)], (at, keep, got, norm_gain[None], mixture, coef, states)
+    )
+
+    _, gathered = lax.optimization_barrier((normed, gathered))
     next_right = shift(gathered[:, :, :512], "y", 3)
     far_right = shift(gathered[:, :, 512:], "y", 1)
     blocks = [normed] + [shift(normed, "x", j) for j in (1, 2, 3)]

time: 181 us -> 175 us (0.967)
  blocking collectives: 37.3 us -> 24.8 us
  waiting for transfers between devices: 36.9 us -> 41.9 us
    all_to_all x1, blocking collectives: 28.8 us -> 16.3 us  [shards(): rows = lax.all_to_all(pay_y, 'y', 0, 0, tiled=True)]
    all_to_all x1, starting transfers between devices: 13.6 us -> 4.14 us  [shards(): states = lax.all_to_all(states, NEAR, 0, 0, tiled=True)]
    ppermute x0 -> x3, starting transfers between devices: none -> 9.26 us  [shards(): lax.ppermute(near[k], NEAR, [(i, i ^ k) for i in range(4)])]
    all_to_all x1, waiting for transfers between devices: 2.17 us -> 11 us  [shards(): states = lax.all_to_all(states, NEAR, 0, 0, tiled=True)]
    all_to_all x1, waiting for transfers between devices: 8.78 us -> 0.01 us  [shards(): far = lax.all_to_all(pay_a, 'a', 0, 0, tiled=True)]
    ppermute x0 -> x3, waiting for transfers between devices: none -> 3.44 us  [shards(): lax.ppermute(near[k], NEAR, [(i, i ^ k) for i in range(4)])]
    unnamed x30 -> x38, local copies, waits for them, and re-layouts: 9.89 us -> 10.6 us
  transfers between devices with their start and end apart: 13 -> 16, of which waited for: 7 -> 7; matrix products, arithmetic and copies ran while one was open for 1% -> 0% of each run, Pallas kernels for 11% -> 11%
where the time goes in v11:
time: 175 us; the launch traced here: 174 us
  starting transfers between devices  55.1 us (31%)
  waiting for transfers between devices  41.9 us (24%)
  blocking collectives  24.8 us (14%)
  Pallas kernels  22.3 us (13%)
  local copies, waits for them, and re-layouts  13.9 us (8%)
  between operations  13.8 us (8%)
  other arithmetic  2.4 us (1%)
    ppermute x5, waiting for transfers between devices, shift(): return lax.ppermute(value, axis, [(i, (i + by) % 4) for i in range(4)])  24.1 us
    pallas_call x10, Pallas kernels, call(): pl.pallas_call(run, out_shape=[jax.ShapeDtypeStruct(*o) for o in outs], i...  22.3 us
    all_to_all x1, blocking collectives, shards(): rows = lax.all_to_all(pay_y, 'y', 0, 0, tiled=True)  16.3 us
    ppermute x5, starting transfers between devices, shift(): return lax.ppermute(value, axis, [(i, (i + by) % 4) for i in range(4)])  14.9 us
    ppermute x3, starting transfers between devices, swap(): return lax.ppermute(value, 'c', [(0, 1), (1, 0)])  13.7 us
    all_to_all x1, waiting for transfers between devices, shards(): states = lax.all_to_all(states, NEAR, 0, 0, tiled=True)  11 us
    unnamed x38, local copies, waits for them, and re-layouts  10.6 us
    all_to_all x1, starting transfers between devices, shards(): far = lax.all_to_all(pay_a, 'a', 0, 0, tiled=True)  10.5 us
  transfers between devices with their start and end apart: 16, of which 7 were waited for; matrix products, arithmetic and copies ran while one was open for 0% of the time, Pallas kernels for 11%

profile of v11, /device:TPU:1, one launch (start us, length us, event | category | flops | bytes accessed | tf_op | source)
XLA Modules:
  0.0 174.2 jit_solution(2719636935957498168)
XLA Ops:
  7.3 8.8 %collective-permute-start = (bf16[32,512]{1,0:T(8,128)(2,1)S(1)}, bf16[32,512]{1,0:T(8,128)(2,1)S(1)}, u32[]{:S(2)}, u32[]{:S(2)}) collective-permute-start(bf16[32,512]{1,0:T(8,128)(2,1)S(1)} %constant_dynamic-slice_fusion), channel_id=1, source_target_pairs={{0,4},{4,0},{1,5},{5,1},{2,6},{6,2},{3,7},{7,3},{8,12},{12,8},{9,1... | collective-permute-start | bytes 98312 | tf_op jit(solution)/shard_map/ppermute | solution.py:21
  21.0 3.8 %shard_map.82 = (bf16[1072,512]{1,0:T(8,128)(2,1)}, bf16[1072,512]{1,0:T(8,128)(2,1)}) custom-call(s32[5]{0:T(128)} %stack.23.refs_0_, bf16[256,1024]{1,0:T(8,128)(2,1)} %refs_1_.1, bf16[256,1024]{1,0:T(8,128)(2,1)} %refs_2_.1, bf16[256,1024]{1,0:T(8,128)(2,1)} %refs_3_.1, bf16[256,1024]{1,0:T(8,128)(2,1)} %refs_4_.1, f32[8,256]{1,0:T(8,128)} %refs_5_.1, ...), custom_call_target="tpu_custom_call" | custom-call | flops 1000000 | bytes 1000000 | tf_op jit(solution)/shard_map/pallas_call | solution.py:59
  25.5 2.5 %collective-permute-start.3 = (bf16[1072,512]{1,0:T(8,128)(2,1)}, bf16[1072,512]{1,0:T(8,128)(2,1)S(1)}, u32[]{:S(2)}, u32[]{:S(2)}) collective-permute-start(bf16[1072,512]{1,0:T(8,128)(2,1)} %get-tuple-element.27), channel_id=1, source_target_pairs={{0,4},{4,0},{1,5},{5,1},{2,6},{6,2},{3,7},{7,3},{8,12},{12,8},{9,1... | collective-permute-start | bytes 3293192 | tf_op jit(solution)/shard_map/ppermute | solution.py:21
  28.0 2.5 %collective-permute-done.3.refs_2_ = bf16[1072,512]{1,0:T(8,128)(2,1)S(1)} collective-permute-done((bf16[1072,512]{1,0:T(8,128)(2,1)}, bf16[1072,512]{1,0:T(8,128)(2,1)S(1)}, u32[]{:S(2)}, u32[]{:S(2)}) %collective-permute-start.3) | collective-permute-done | bytes 1097760 | tf_op jit(solution)/shard_map/ppermute | solution.py:21
  33.6 8.4 %all_to_all.20.refs_1_ = bf16[4,144,128]{2,1,0:T(8,128)(2,1)S(1)} all-to-all(bf16[4,144,128]{2,1,0:T(8,128)(2,1)S(1)} %get-tuple-element.31), channel_id=1, replica_groups=mesh['y'=4,'a'=4,'p'=2,'q'=2,'c'=2,'x'=4] {'p','q'}, dimensions={0} | all-to-all | bytes 294912 | tf_op jit(solution)/shard_map/all_to_all | solution.py:318
  44.0 10.5 %all-to-all-start.1 = ((bf16[4,144,128]{2,1,0:T(8,128)(2,1)}), bf16[4,144,128]{2,1,0:T(8,128)(2,1)S(1)}, u32[]{:S(2)}, u32[]{:S(2)}) async-start(bf16[4,144,128]{2,1,0:T(8,128)(2,1)} %get-tuple-element.38), calls=%async_computation.1 | async-start | bytes 294912 | tf_op jit(solution)/shard_map/all_to_all | solution.py:320
  56.9 4.0 %collective-permute-start.5 = (bf16[144,256]{1,0:T(8,128)(2,1)}, bf16[144,256]{1,0:T(8,128)(2,1)S(1)}, u32[]{:S(2)}, u32[]{:S(2)}) collective-permute-start(bf16[144,256]{1,0:T(8,128)(2,1)} %get-tuple-element.34), channel_id=1, source_target_pairs={{0,16},{8,24},{16,0},{24,8},{1,17},{9,25},{17,1},{25,9},{2,18},{10... | collective-permute-start | bytes 221192 | tf_op jit(solution)/shard_map/ppermute | solution.py:322
  60.9 3.0 %collective-permute-start.6 = (bf16[144,256]{1,0:T(8,128)(2,1)}, bf16[144,256]{1,0:T(8,128)(2,1)S(1)}, u32[]{:S(2)}, u32[]{:S(2)}) collective-permute-start(bf16[144,256]{1,0:T(8,128)(2,1)} %get-tuple-element.35), channel_id=1, source_target_pairs={{0,24},{8,16},{16,8},{24,0},{1,25},{9,17},{17,9},{25,1},{2,26},{10... | collective-permute-start | bytes 221192 | tf_op jit(solution)/shard_map/ppermute | solution.py:322
  64.7 4.3 %shard_map.84 = (f32[512,512]{1,0:T(8,128)S(1)}, f32[512,24]{1,0:T(8,128)S(1)}) custom-call(s32[5]{0:T(128)S(1)} %copy-done.17, bf16[1072,512]{1,0:T(8,128)(2,1)S(1)} %copy-done.2, bf16[1072,512]{1,0:T(8,128)(2,1)S(1)} %collective-permute-done.3.refs_2_, bf16[4,128,128]{2,1,0:T(8,128)(2,1)S(1)} %copy-done.14), custom_call_target="tpu_custom_call" | custom-call | flops 1000000 | bytes 1000000 | tf_op jit(solution)/shard_map/pallas_call | solution.py:59
  69.8 3.4 %collective-permute-done.6.refs_8_.refs_5_ = bf16[144,256]{1,0:T(8,128)(2,1)S(1)} collective-permute-done((bf16[144,256]{1,0:T(8,128)(2,1)}, bf16[144,256]{1,0:T(8,128)(2,1)S(1)}, u32[]{:S(2)}, u32[]{:S(2)}) %collective-permute-start.6) | collective-permute-done | bytes 73760 | tf_op jit(solution)/shard_map/ppermute | solution.py:322
  75.4 16.3 %all_to_all.21.refs_1_ = bf16[4,144,128]{2,1,0:T(8,128)(2,1)S(1)} all-to-all(bf16[4,144,128]{2,1,0:T(8,128)(2,1)S(1)} %get-tuple-element.39), channel_id=1, replica_groups=mesh['y'=4,'a'=4,'p'=2,'q'=2,'c'=2,'x'=4] {'y'}, dimensions={0} | all-to-all | bytes 294912 | tf_op jit(solution)/shard_map/all_to_all | solution.py:333
  93.1 4.1 %all-to-all-start.3 = ((bf16[4,128,512]{2,1,0:T(8,128)(2,1)}), bf16[4,128,512]{2,1,0:T(8,128)(2,1)}, u32[]{:S(2)}, u32[]{:S(2)}) async-start(bf16[4,128,512]{2,1,0:T(8,128)(2,1)} %copy-done.3), calls=%async_computation.3 | async-start | bytes 1048576 | tf_op jit(solution)/shard_map/all_to_all | solution.py:335
  101.6 11.0 %all-to-all-done.3.refs_6_ = bf16[4,128,512]{2,1,0:T(8,128)(2,1)} async-done(((bf16[4,128,512]{2,1,0:T(8,128)(2,1)}), bf16[4,128,512]{2,1,0:T(8,128)(2,1)}, u32[]{:S(2)}, u32[]{:S(2)}) %all-to-all-start.3) | async-done | bytes 524320 | tf_op jit(solution)/shard_map/all_to_all | solution.py:335
  114.8 3.0 %shard_map.89.refs_1_ = bf16[512,512]{1,0:T(8,128)(2,1)S(1)} custom-call(s32[5]{0:T(128)S(1)} %copy-done.17, bf16[1072,512]{1,0:T(8,128)(2,1)S(1)} %copy-done.2, bf16[1072,512]{1,0:T(8,128)(2,1)S(1)} %collective-permute-done.3.refs_2_, bf16[1,1024]{1,0:T(2,128)(2,1)S(1)} %broadcast_in_dim.3.refs_3_, f32[512,512]{1,0:T(8,128)S(1)} %copy-done.5, ...), custom_call_target="tpu_custom_call" | custom-call | flops 1000000 | bytes 1000000 | tf_op jit(solution)/shard_map/pallas_call | solution.py:59
  119.8 3.0 %collective-permute-start.11 = (bf16[16,64,512]{2,1,0:T(8,128)(2,1)S(1)}, bf16[16,64,512]{2,1,0:T(8,128)(2,1)S(1)}, u32[]{:S(2)}, u32[]{:S(2)}) collective-permute-start(bf16[16,64,512]{2,1,0:T(8,128)(2,1)S(1)} %get-tuple-element.45), channel_id=1, source_target_pairs={{0,128},{128,256},{256,384},{384,0},{1,129},{129,257},{257,385},{3... | collective-permute-start | bytes 3145736 | tf_op jit(solution)/shard_map/ppermute | solution.py:283
  122.8 3.5 %collective-permute-start.10 = (bf16[16,64,512]{2,1,0:T(8,128)(2,1)S(1)}, bf16[16,64,512]{2,1,0:T(8,128)(2,1)S(1)}, u32[]{:S(2)}, u32[]{:S(2)}) collective-permute-start(bf16[16,64,512]{2,1,0:T(8,128)(2,1)S(1)} %get-tuple-element.46), channel_id=1, source_target_pairs={{0,384},{128,0},{256,128},{384,256},{1,385},{129,1},{257,129},{385... | collective-permute-start | bytes 3145736 | tf_op jit(solution)/shard_map/ppermute | solution.py:283
  126.3 4.0 %collective-permute-start.9 = (bf16[512,512]{1,0:T(8,128)(2,1)S(1)}, bf16[512,512]{1,0:T(8,128)(2,1)S(1)}, u32[]{:S(2)}, u32[]{:S(2)}) collective-permute-start(bf16[512,512]{1,0:T(8,128)(2,1)S(1)} %shard_map.89.refs_1_), channel_id=1, source_target_pairs={{0,3},{1,0},{2,1},{3,2},{4,7},{5,4},{6,5},{7,6},{8,11},{9,8},{10,9... | collective-permute-start | bytes 1572872 | tf_op jit(solution)/shard_map/ppermute | solution.py:283
  132.2 2.5 %collective-permute-start.7 = (bf16[512,512]{1,0:T(8,128)(2,1)S(1)}, bf16[512,512]{1,0:T(8,128)(2,1)S(1)}, u32[]{:S(2)}, u32[]{:S(2)}) collective-permute-start(bf16[512,512]{1,0:T(8,128)(2,1)S(1)} %shard_map.89.refs_1_), channel_id=1, source_target_pairs={{0,1},{1,2},{2,3},{3,0},{4,5},{5,6},{6,7},{7,4},{8,9},{9,10},{10,1... | collective-permute-start | bytes 1572872 | tf_op jit(solution)/shard_map/ppermute | solution.py:283
  134.7 6.7 %collective-permute-done.9.refs_4_ = bf16[512,512]{1,0:T(8,128)(2,1)S(1)} collective-permute-done((bf16[512,512]{1,0:T(8,128)(2,1)S(1)}, bf16[512,512]{1,0:T(8,128)(2,1)S(1)}, u32[]{:S(2)}, u32[]{:S(2)}) %collective-permute-start.9) | collective-permute-done | bytes 524320 | tf_op jit(solution)/shard_map/ppermute | solution.py:283
  141.4 3.9 %collective-permute-done.8.refs_3_ = bf16[512,512]{1,0:T(8,128)(2,1)S(1)} collective-permute-done((bf16[512,512]{1,0:T(8,128)(2,1)S(1)}, bf16[512,512]{1,0:T(8,128)(2,1)S(1)}, u32[]{:S(2)}, u32[]{:S(2)}) %collective-permute-start.8) | collective-permute-done | bytes 524320 | tf_op jit(solution)/shard_map/ppermute | solution.py:283
  145.3 13.5 %collective-permute-done.7.refs_2_ = bf16[512,512]{1,0:T(8,128)(2,1)S(1)} collective-permute-done((bf16[512,512]{1,0:T(8,128)(2,1)S(1)}, bf16[512,512]{1,0:T(8,128)(2,1)S(1)}, u32[]{:S(2)}, u32[]{:S(2)}) %collective-permute-start.7) | collective-permute-done | bytes 524320 | tf_op jit(solution)/shard_map/ppermute | solution.py:283
  158.8 2.6 %shard_map.91 = bf16[256,1024]{1,0:T(8,128)(2,1)S(1)} custom-call(s32[5]{0:T(128)S(1)} %copy-done.17, bf16[512,512]{1,0:T(8,128)(2,1)S(1)} %shard_map.89.refs_1_, bf16[512,512]{1,0:T(8,128)(2,1)S(1)} %collective-permute-done.7.refs_2_, bf16[512,512]{1,0:T(8,128)(2,1)S(1)} %collective-permute-done.8.refs_3_, ...), custom_call_target="tpu_custom_call" | custom-call | flops 1000000 | bytes 1000000 | tf_op jit(solution)/shard_map/pallas_call | solution.py:59
  161.4 2.4 %collective-permute-start.12 = (bf16[256,1024]{1,0:T(8,128)(2,1)S(1)}, bf16[256,1024]{1,0:T(8,128)(2,1)S(1)}, u32[]{:S(2)}, u32[]{:S(2)}) collective-permute-start(bf16[256,1024]{1,0:T(8,128)(2,1)S(1)} %shard_map.91), channel_id=1, source_target_pairs={{0,4},{4,0},{1,5},{5,1},{2,6},{6,2},{3,7},{7,3},{8,12},{12,8},{9,1... | collective-permute-start | bytes 1572872 | tf_op jit(solution)/shard_map/ppermute | solution.py:21
  163.8 2.6 %shard_map.90 = f32[256,1024]{1,0:T(8,128)S(1)} custom-call(s32[5]{0:T(128)S(1)} %copy-done.17, bf16[512,512]{1,0:T(8,128)(2,1)S(1)} %shard_map.89.refs_1_, bf16[512,512]{1,0:T(8,128)(2,1)S(1)} %collective-permute-done.7.refs_2_, bf16[512,512]{1,0:T(8,128)(2,1)S(1)} %collective-permute-done.8.refs_3_, bf16[512,512]{1,0:T(8,128)(2,1)S(1)} %collective-permute-done.9.refs_4_, ...), custom_call_target="tpu_custom_call" | custom-call | flops 1000000 | bytes 1000000 | tf_op jit(solution)/shard_map/pallas_call | solution.py:59
  (67 shorter events, 30.0 us)
Async XLA Ops:
  6.5 111.3 %all-gather.3.cloned.1.call-start = ((), (), s32[]{:S(2)}) async-start(), calls=%async_computation.4 | async-start | bytes 2228224 | tf_op jit(solution)/shard_map/all_gather | solution.py:313
  7.3 9.6 %collective-permute-start = (bf16[32,512]{1,0:T(8,128)(2,1)S(1)}, bf16[32,512]{1,0:T(8,128)(2,1)S(1)}, u32[]{:S(2)}, u32[]{:S(2)}) collective-permute-start(bf16[32,512]{1,0:T(8,128)(2,1)S(1)} %constant_dynamic-slice_fusion), channel_id=1, source_target_pairs={{0,4},{4,0},{1,5},{5,1},{2,6},{6,2},{3,7},{7,3},{8,12},{12,8},{9,1... | collective-permute-start | bytes 98312 | tf_op jit(solution)/shard_map/ppermute | solution.py:21
  17.7 7.1 %collective-permute-start.2 = (bf16[64,512]{1,0:T(8,128)(2,1)S(1)}, bf16[64,512]{1,0:T(8,128)(2,1)S(1)}, u32[]{:S(2)}, u32[]{:S(2)}) collective-permute-start(bf16[64,512]{1,0:T(8,128)(2,1)S(1)} %pad_maximum_fusion.1), channel_id=1, source_target_pairs={{0,128},{1,256},{2,384},{3,0},{128,129},{129,257},{130,385},{131,1... | collective-permute-start | bytes 196616 | tf_op jit(solution)/shard_map/ppermute | solution.py:297
  19.6 5.2 %collective-permute-start.1 = (bf16[64,512]{1,0:T(8,128)(2,1)S(1)}, bf16[64,512]{1,0:T(8,128)(2,1)S(1)}, u32[]{:S(2)}, u32[]{:S(2)}) collective-permute-start(bf16[64,512]{1,0:T(8,128)(2,1)S(1)} %pad_maximum_fusion.1), channel_id=1, source_target_pairs={{0,0},{1,128},{2,256},{3,384},{128,1},{129,129},{130,257},{131,385... | collective-permute-start | bytes 196616 | tf_op jit(solution)/shard_map/ppermute | solution.py:297
  21.0 9.6 %copy-start.17 = (s32[5]{0:T(128)S(1)}, s32[5]{0:T(128)}, u32[]{:S(2)}) copy-start(s32[5]{0:T(128)} %stack.23.refs_0_) | copy-start | bytes 64
  25.5 5.1 %collective-permute-start.3 = (bf16[1072,512]{1,0:T(8,128)(2,1)}, bf16[1072,512]{1,0:T(8,128)(2,1)S(1)}, u32[]{:S(2)}, u32[]{:S(2)}) collective-permute-start(bf16[1072,512]{1,0:T(8,128)(2,1)} %get-tuple-element.27), channel_id=1, source_target_pairs={{0,4},{4,0},{1,5},{5,1},{2,6},{6,2},{3,7},{7,3},{8,12},{12,8},{9,1... | collective-permute-start | bytes 3293192 | tf_op jit(solution)/shard_map/ppermute | solution.py:21
  30.6 1.2 copy-start.1
  31.8 32.0 %copy-start.2 = (bf16[1072,512]{1,0:T(8,128)(2,1)S(1)}, bf16[1072,512]{1,0:T(8,128)(2,1)}, u32[]{:S(2)}) copy-start(bf16[1072,512]{1,0:T(8,128)(2,1)} %get-tuple-element.25.refs_1_) | copy-start | bytes 3293188
  33.6 9.8 %copy-start.13 = (bf16[4,128,128]{2,1,0:T(8,128)(2,1)}, bf16[4,128,128]{2,1,0:T(8,128)(2,1)S(1)}, u32[]{:S(2)}) copy-start(bf16[4,128,128]{2,1,0:T(8,128)(2,1)S(1)} %get-tuple-element.28.refs_3_) | copy-start | bytes 393220
  44.0 29.8 %all-to-all-start.1 = ((bf16[4,144,128]{2,1,0:T(8,128)(2,1)}), bf16[4,144,128]{2,1,0:T(8,128)(2,1)S(1)}, u32[]{:S(2)}, u32[]{:S(2)}) async-start(bf16[4,144,128]{2,1,0:T(8,128)(2,1)} %get-tuple-element.38), calls=%async_computation.1 | async-start | bytes 294912 | tf_op jit(solution)/shard_map/all_to_all | solution.py:320
  54.5 15.3 %collective-permute-start.4 = (bf16[144,256]{1,0:T(8,128)(2,1)}, bf16[144,256]{1,0:T(8,128)(2,1)S(1)}, u32[]{:S(2)}, u32[]{:S(2)}) collective-permute-start(bf16[144,256]{1,0:T(8,128)(2,1)} %get-tuple-element.33), channel_id=1, source_target_pairs={{0,8},{8,0},{16,24},{24,16},{1,9},{9,1},{17,25},{25,17},{2,10},{10... | collective-permute-start | bytes 221192 | tf_op jit(solution)/shard_map/ppermute | solution.py:322
  56.9 12.9 %collective-permute-start.5 = (bf16[144,256]{1,0:T(8,128)(2,1)}, bf16[144,256]{1,0:T(8,128)(2,1)S(1)}, u32[]{:S(2)}, u32[]{:S(2)}) collective-permute-start(bf16[144,256]{1,0:T(8,128)(2,1)} %get-tuple-element.34), channel_id=1, source_target_pairs={{0,16},{8,24},{16,0},{24,8},{1,17},{9,25},{17,1},{25,9},{2,18},{10... | collective-permute-start | bytes 221192 | tf_op jit(solution)/shard_map/ppermute | solution.py:322
  60.9 12.4 %collective-permute-start.6 = (bf16[144,256]{1,0:T(8,128)(2,1)}, bf16[144,256]{1,0:T(8,128)(2,1)S(1)}, u32[]{:S(2)}, u32[]{:S(2)}) collective-permute-start(bf16[144,256]{1,0:T(8,128)(2,1)} %get-tuple-element.35), channel_id=1, source_target_pairs={{0,24},{8,16},{16,8},{24,0},{1,25},{9,17},{17,9},{25,1},{2,26},{10... | collective-permute-start | bytes 221192 | tf_op jit(solution)/shard_map/ppermute | solution.py:322
  75.4 21.9 %copy-start.18 = (bf16[1024]{0:T(1024)(128)(2,1)S(1)}, bf16[1024]{0:T(1024)(128)(2,1)}, u32[]{:S(2)}) copy-start(bf16[1024]{0:T(1024)(128)(2,1)} %param.14) | copy-start | bytes 6148
  75.4 21.9 %copy-start.8 = (bf16[144,256]{1,0:T(8,128)(2,1)S(1)}, bf16[144,256]{1,0:T(8,128)(2,1)}, u32[]{:S(2)}) copy-start(bf16[144,256]{1,0:T(8,128)(2,1)} %copy-done.6) | copy-start | bytes 221188
  75.4 21.9 %copy-start.16 = (bf16[144,256]{1,0:T(8,128)(2,1)S(1)}, bf16[144,256]{1,0:T(8,128)(2,1)}, u32[]{:S(2)}) copy-start(bf16[144,256]{1,0:T(8,128)(2,1)} %copy-done.15) | copy-start | bytes 221188
  93.1 19.5 %all-to-all-start.3 = ((bf16[4,128,512]{2,1,0:T(8,128)(2,1)}), bf16[4,128,512]{2,1,0:T(8,128)(2,1)}, u32[]{:S(2)}, u32[]{:S(2)}) async-start(bf16[4,128,512]{2,1,0:T(8,128)(2,1)} %copy-done.3), calls=%async_computation.3 | async-start | bytes 1048576 | tf_op jit(solution)/shard_map/all_to_all | solution.py:335
  117.9 40.9 %copy-start = (bf16[1024,1024]{1,0:T(8,128)(2,1)S(1)}, bf16[1024,1024]{1,0:T(8,128)(2,1)}, u32[]{:S(2)}) copy-start(bf16[1024,1024]{1,0:T(8,128)(2,1)} %all-gather.3.cloned.1.call-done) | copy-start | bytes 6291460
  119.8 39.0 %collective-permute-start.11 = (bf16[16,64,512]{2,1,0:T(8,128)(2,1)S(1)}, bf16[16,64,512]{2,1,0:T(8,128)(2,1)S(1)}, u32[]{:S(2)}, u32[]{:S(2)}) collective-permute-start(bf16[16,64,512]{2,1,0:T(8,128)(2,1)S(1)} %get-tuple-element.45), channel_id=1, source_target_pairs={{0,128},{128,256},{256,384},{384,0},{1,129},{129,257},{257,385},{3... | collective-permute-start | bytes 3145736 | tf_op jit(solution)/shard_map/ppermute | solution.py:283
  122.8 36.0 %collective-permute-start.10 = (bf16[16,64,512]{2,1,0:T(8,128)(2,1)S(1)}, bf16[16,64,512]{2,1,0:T(8,128)(2,1)S(1)}, u32[]{:S(2)}, u32[]{:S(2)}) collective-permute-start(bf16[16,64,512]{2,1,0:T(8,128)(2,1)S(1)} %get-tuple-element.46), channel_id=1, source_target_pairs={{0,384},{128,0},{256,128},{384,256},{1,385},{129,1},{257,129},{385... | collective-permute-start | bytes 3145736 | tf_op jit(solution)/shard_map/ppermute | solution.py:283
  126.3 15.1 %collective-permute-start.9 = (bf16[512,512]{1,0:T(8,128)(2,1)S(1)}, bf16[512,512]{1,0:T(8,128)(2,1)S(1)}, u32[]{:S(2)}, u32[]{:S(2)}) collective-permute-start(bf16[512,512]{1,0:T(8,128)(2,1)S(1)} %shard_map.89.refs_1_), channel_id=1, source_target_pairs={{0,3},{1,0},{2,1},{3,2},{4,7},{5,4},{6,5},{7,6},{8,11},{9,8},{10,9... | collective-permute-start | bytes 1572872 | tf_op jit(solution)/shard_map/ppermute | solution.py:283
  130.3 15.0 %collective-permute-start.8 = (bf16[512,512]{1,0:T(8,128)(2,1)S(1)}, bf16[512,512]{1,0:T(8,128)(2,1)S(1)}, u32[]{:S(2)}, u32[]{:S(2)}) collective-permute-start(bf16[512,512]{1,0:T(8,128)(2,1)S(1)} %shard_map.89.refs_1_), channel_id=1, source_target_pairs={{0,2},{1,3},{2,0},{3,1},{4,6},{5,7},{6,4},{7,5},{8,10},{9,11},{10,... | collective-permute-start | bytes 1572872 | tf_op jit(solution)/shard_map/ppermute | solution.py:283
  132.2 26.6 %collective-permute-start.7 = (bf16[512,512]{1,0:T(8,128)(2,1)S(1)}, bf16[512,512]{1,0:T(8,128)(2,1)S(1)}, u32[]{:S(2)}, u32[]{:S(2)}) collective-permute-start(bf16[512,512]{1,0:T(8,128)(2,1)S(1)} %shard_map.89.refs_1_), channel_id=1, source_target_pairs={{0,1},{1,2},{2,3},{3,0},{4,5},{5,6},{6,7},{7,4},{8,9},{9,10},{10,1... | collective-permute-start | bytes 1572872 | tf_op jit(solution)/shard_map/ppermute | solution.py:283
  161.4 5.0 %collective-permute-start.12 = (bf16[256,1024]{1,0:T(8,128)(2,1)S(1)}, bf16[256,1024]{1,0:T(8,128)(2,1)S(1)}, u32[]{:S(2)}, u32[]{:S(2)}) collective-permute-start(bf16[256,1024]{1,0:T(8,128)(2,1)S(1)} %shard_map.91), channel_id=1, source_target_pairs={{0,4},{4,0},{1,5},{5,1},{2,6},{6,2},{3,7},{7,3},{8,12},{12,8},{9,1... | collective-permute-start | bytes 1572872 | tf_op jit(solution)/shard_map/ppermute | solution.py:21
  (11 other events, 9.4 us)
Sparse Core Ops, SparseCore 0:
  25.6 76.5 all-gather.2

commit v12 on v11

--- a/solution.py
+++ b/solution.py
@@ -96,14 +96,29 @@
         copy.wait()
 
 
-def logs_of(block):
-    tile = block[LOGS : LOGS + 48, :].astype(F32)
+def logs_of(block, start=LOGS):
+    tile = block[start : start + 48, :].astype(F32)
     return tile[:, 0:256] + tile[:, 256:512]
 
 
-def ends_body(at, keep, got, pay, first):
+def ends_body(at, keep, got, pay, first, blocks, logs_in, sems):
     core = at[0]
-    logs = jnp.concatenate([logs_of(keep)[0:4], logs_of(got)[0:4]], axis=0)
+    copies = []
+    for i, ref in enumerate((keep, got)):
+        copy = pltpu.make_async_copy(ref.at[LOGS : LOGS + 48], logs_in.at[i], sems.at[i, 4])
+        copy.start()
+        copies.append([copy])
+    for h in range(4):
+        cols = pl.ds(h * 128, 128)
+        for i, ref in enumerate((keep, got)):
+            copy = pltpu.make_async_copy(
+                ref.at[0:512, cols], blocks.at[i, :, cols], sems.at[i, h]
+            )
+            copy.start()
+            copies[i].append(copy)
+    for i in range(2):
+        copies[i][0].wait()
+    logs = jnp.concatenate([logs_of(logs_in.at[i], 0)[0:4] for i in range(2)], axis=0)
     after = (
         lax.broadcasted_iota(jnp.int32, (256, 256), 1)
         > lax.broadcasted_iota(jnp.int32, (256, 256), 0)
@@ -113,9 +128,10 @@
     for h in range(4):
         cols = slice(h * 128, h * 128 + 128)
         end = []
-        for i, ref in enumerate((keep, got)):
-            scaled = ref[0:256, cols].astype(F32) * scale[:, 4 * i + h : 4 * i + h + 1]
-            end.append(dot(scaled.astype(BF), ref[256:512, cols], TN))
+        for i in range(2):
+            copies[i][1 + h].wait()
+            scaled = blocks[i, 0:256, cols].astype(F32) * scale[:, 4 * i + h : 4 * i + h + 1]
+            end.append(dot(scaled.astype(BF), blocks[i, 256:512, cols], TN))
         own_log, got_log = total[h : h + 1], total[4 + h : 5 + h]
         own_later = jnp.exp(jnp.where(core == 0, got_log, 0.0))
         got_later = jnp.exp(jnp.where(core == 0, 0.0, own_log))
@@ -228,17 +244,38 @@
             later[here, 4 * h : 4 * h + 4] = coef[here, 6 * h + 2 : 6 * h + 6] * before
 
 
-def norm_body(at, keep, got, gain, mixture, coef, states, normed):
+def norm_body(
+    at, keep, got, gain, mixture_in, coef_in, states_in, normed, blocks, mixture, coef, states, sems
+):
     core = at[0]
+    copies = [[pltpu.make_async_copy(coef_in, coef, sems.at[0, 4])]]
+    copies[0][0].start()
+    for h in range(4):
+        cols = pl.ds(h * 128, 128)
+        copies.append(
+            [
+                pltpu.make_async_copy(ref.at[512:1024, cols], blocks.at[i, :, cols], sems.at[i, h])
+                for i, ref in enumerate((keep, got))
+            ]
+            + [
+                pltpu.make_async_copy(mixture_in.at[:, cols], mixture.at[:, cols], sems.at[2, h]),
+                pltpu.make_async_copy(states_in.at[h], states.at[h], sems.at[3, h]),
+            ]
+        )
+        for copy in copies[-1]:
+            copy.start()
+    copies[0][0].wait()
     for h in range(4):
         mine = pl.ds(pl.multiple_of(core * 512 + h * 128, 128), 128)
         hc = slice(h * 128, h * 128 + 128)
-        for s, ref in enumerate((keep, got)):
+        for copy in copies[1 + h]:
+            copy.wait()
+        for s in range(2):
             _, here = place(s, core)
-            z = ref[768:1024, hc].astype(F32)
+            q, z = blocks[s, 0:256, hc], blocks[s, 256:512, hc].astype(F32)
             total = mixture[here, hc]
             for l in range(0, 4, 2):
-                read = dot(ref[512:768, hc], states[h, :, l * 128 : l * 128 + 256])
+                read = dot(q, states[h, :, l * 128 : l * 128 + 256])
                 total += read[:, 0:128] * coef[here, 4 * h + l : 4 * h + l + 1]
                 total += read[:, 128:256] * coef[here, 4 * h + l + 1 : 4 * h + l + 2]
             gated = total * (z / (1.0 + jnp.exp(-z)))
@@ -246,35 +283,34 @@
             normed[here, hc] = (gated * size * gain[:, mine].astype(F32)).astype(BF)
 
 
-def project_body(other, at, b0, b1, b2, b3, gathered, next_right, far_right, out, left, right, sems):
+def project_body(other, at, b0, b1, b2, b3, w0, w1, w2, w3, out, left, right, sems):
     row = (1 - at[0]) if other else at[0]
     rows = pl.ds(pl.multiple_of(row * 256, 256), 256)
-    pieces = (gathered.at[:, :, 0:512], gathered.at[:, :, 512:1024], next_right, far_right)
     copies = [
-        pltpu.make_async_copy(piece, right.at[k], sems.at[k]) for k, piece in enumerate(pieces)
+        pltpu.make_async_copy(w, right.at[k], sems.at[k]) for k, w in enumerate((w0, w1, w2, w3))
     ]
     for copy in copies:
         copy.start()
     for j, block in enumerate((b0, b1, b2, b3)):
         left[(at[4] + 4 - j) % 4] = block[rows, :]
     total = 0.0
-    for k, turn in enumerate((0, 3, 1, 2)):
+    for k, turn in enumerate((0, 1, 3, 2)):
         copies[k].wait()
         total += dot(left[(at[3] + turn) % 4], right[k].reshape(1024, 512), NT)
     out[...] = total.astype(out.dtype)
 
 
-def project(at, blocks, gathered, next_right, far_right, other):
+def project(at, blocks, rights, other):
     return call(
         functools.partial(project_body, other),
         [((256, 1024), BF if other else F32)],
-        (at, *blocks, gathered, next_right, far_right),
+        (at, *blocks, *rights),
         scratch=[
             pltpu.VMEM((4, 256, 512), BF),
             pltpu.VMEM((4, 16, 64, 512), BF),
             pltpu.SemaphoreType.DMA((4,)),
         ],
-        hbm=(5, 6, 7),
+        hbm=range(5, 9),
         vmem=20,
     )[0]
 
@@ -291,10 +327,8 @@
     both = jnp.concatenate(
         [jnp.where(c == 0, kept, theirs), jnp.where(c == 0, theirs, kept)]
     )
-    mine = []
-    for k in range(2):
-        perm = [(s * 4 + f, ((f + k) % 4) * 4 + s) for s in range(4) for f in range(4)]
-        mine.append(lax.ppermute(both, ("y", "x"), perm))
+    perm = [(s * 4 + f, f * 4 + s) for s in range(4) for f in range(4)]
+    mine = lax.ppermute(both, ("y", "x"), perm)
     block = ((ROWS, 512), BF)
     keep, send = call(
         pack_body,
@@ -309,12 +343,22 @@
         vmem=60,
     )
     mine, send = lax.optimization_barrier((mine, send))
-    mine = jnp.concatenate(mine, axis=1)
     gathered = lax.all_gather(mine, ("a", "p", "q"))
 
     got = swap(send)
     pay = ((4, 144, 128), BF)
-    pay_b, first = call(ends_body, [pay, ((4, 128, 128), BF)], (at, keep, got))
+    pay_b, first = call(
+        ends_body,
+        [pay, ((4, 128, 128), BF)],
+        (at, keep, got),
+        scratch=[
+            pltpu.VMEM((2, 512, 512), BF),
+            pltpu.VMEM((2, 48, 512), BF),
+            pltpu.SemaphoreType.DMA((2, 5)),
+        ],
+        hbm=(1, 2),
+        vmem=60,
+    )
     near = lax.all_to_all(pay_b, NEAR, 0, 0, tiled=True)
     pay_a, *near = call(near_body, [pay] + [((144, 256), BF)] * 4, (at, near))
     far = lax.all_to_all(pay_a, "a", 0, 0, tiled=True)
@@ -322,33 +366,46 @@
         lax.ppermute(near[k], NEAR, [(i, i ^ k) for i in range(4)]) for k in (1, 2, 3)
     ]
     mixture, coef = call(
-        own_body, [((512, 512), F32), ((512, 24), F32)], (at, keep, got, first)
+        own_body, [((512, 512), F32), ((512, 24), F32)], (at, keep, got, first), vmem=60
     )
     pay_y, far, before = call(
         far_body,
         [pay, ((128, 256), BF), ((8, 128), F32)],
         (at, far),
-        unread=(mixture, *near[1:]),
+        unread=near[1:],
     )
     rows = lax.all_to_all(pay_y, "y", 0, 0, tiled=True)
-    (states,) = call(last_body, [((4, 128, 512), BF)], (at, rows, before, far))
+    (states,) = call(
+        last_body, [((4, 128, 512), BF)], (at, rows, before, far), unread=(mixture,)
+    )
+    states, gathered = lax.optimization_barrier((states, gathered))
+    rights = [gathered] + [shift(gathered, "y", 4 - k) for k in (1, 3, 2)]
     states = lax.all_to_all(states, NEAR, 0, 0, tiled=True)
     mixture, coef = call(
         mix_body,
         [((512, 512), F32), ((512, 16), F32)],
         (at, keep, got, mixture, coef, *near),
         scratch=[pltpu.VMEM((4, 144, 256), BF)],
+        vmem=60,
     )
     (normed,) = call(
-        norm_body, [((512, 512), BF)], (at, keep, got, norm_gain[None], mixture, coef, states)
-    )
-
-    _, gathered = lax.optimization_barrier((normed, gathered))
-    next_right = shift(gathered[:, :, :512], "y", 3)
-    far_right = shift(gathered[:, :, 512:], "y", 1)
+        norm_body,
+        [((512, 512), BF)],
+        (at, keep, got, norm_gain[None], mixture, coef, states),
+        scratch=[
+            pltpu.VMEM((2, 512, 512), BF),
+            pltpu.VMEM((512, 512), F32),
+            pltpu.VMEM((512, 16), F32),
+            pltpu.VMEM((4, 128, 512), BF),
+            pltpu.SemaphoreType.DMA((4, 5)),
+        ],
+        hbm=(1, 2, 4, 5, 6),
+        vmem=60,
+    )
+
     blocks = [normed] + [shift(normed, "x", j) for j in (1, 2, 3)]
-    theirs = swap(project(at, blocks, gathered, next_right, far_right, True))
-    own = project(at, blocks, gathered, next_right, far_right, False)
+    theirs = swap(project(at, blocks, rights, True))
+    own = project(at, blocks, rights, False)
     return (own + theirs.astype(F32)).astype(BF)
 
 

time: 175 us -> 172 us (0.983)
  starting transfers between devices: 55.1 us -> 74.5 us
  blocking collectives: 24.8 us -> 9.44 us
  Pallas kernels: 22.3 us -> 35.4 us
  waiting for transfers between devices: 41.9 us -> 29.1 us
  local copies, waits for them, and re-layouts: 13.9 us -> 6.74 us
    all_to_all x1 -> x0, blocking collectives: 16.3 us -> none  [shards(): rows = lax.all_to_all(pay_y, 'y', 0, 0, tiled=True)]
    pallas_call x10, Pallas kernels: 22.3 us -> 35.4 us  [call(): pl.pallas_call(run, out_shape=[jax.ShapeDtypeStruct(*o) for o in outs], i...]
    all_to_all x1, waiting for transfers between devices: 11 us -> 0.01 us  [shards(): states = lax.all_to_all(states, NEAR, 0, 0, tiled=True)]
    all_to_all x0 -> x1, starting transfers between devices: none -> 10.9 us  [shards(): rows = lax.all_to_all(pay_y, 'y', 0, 0, tiled=True)]
    ppermute x5 -> x6, waiting for transfers between devices: 24.1 us -> 17.8 us  [shift(): return lax.ppermute(value, axis, [(i, (i + by) % 4) for i in range(4)])]
    ppermute x3, starting transfers between devices: 13.7 us -> 19.9 us  [swap(): return lax.ppermute(value, 'c', [(0, 1), (1, 0)])]
    ppermute x5 -> x6, starting transfers between devices: 14.9 us -> 20.8 us  [shift(): return lax.ppermute(value, axis, [(i, (i + by) % 4) for i in range(4)])]
    unnamed x38 -> x30, local copies, waits for them, and re-layouts: 10.6 us -> 4.73 us
  transfers between devices with their start and end apart: 16 -> 17, of which waited for: 7 -> 6; matrix products, arithmetic and copies ran while one was open for 0% -> 1% of each run, Pallas kernels for 11% -> 19%
where the time goes in v12:
time: 172 us; the launch traced here: 171 us
  starting transfers between devices  74.5 us (43%)
  Pallas kernels  35.4 us (21%)
  waiting for transfers between devices  29.1 us (17%)
  between operations  13.7 us (8%)
  blocking collectives  9.44 us (5%)
  local copies, waits for them, and re-layouts  6.74 us (4%)
  other arithmetic  1.72 us (1%)
    pallas_call x10, Pallas kernels, call(): pl.pallas_call(run, out_shape=[jax.ShapeDtypeStruct(*o) for o in outs], i...  35.4 us
    ppermute x6, starting transfers between devices, shift(): return lax.ppermute(value, axis, [(i, (i + by) % 4) for i in range(4)])  20.8 us
    ppermute x3, starting transfers between devices, swap(): return lax.ppermute(value, 'c', [(0, 1), (1, 0)])  19.9 us
    ppermute x6, waiting for transfers between devices, shift(): return lax.ppermute(value, axis, [(i, (i + by) % 4) for i in range(4)])  17.8 us
    all_to_all x1, starting transfers between devices, shards(): rows = lax.all_to_all(pay_y, 'y', 0, 0, tiled=True)  10.9 us
    all_to_all x1, blocking collectives, shards(): near = lax.all_to_all(pay_b, NEAR, 0, 0, tiled=True)  9.44 us
    all_to_all x1, starting transfers between devices, shards(): far = lax.all_to_all(pay_a, 'a', 0, 0, tiled=True)  9.41 us
    ppermute x3, starting transfers between devices, shards(): lax.ppermute(near[k], NEAR, [(i, i ^ k) for i in range(4)])  9.26 us
  transfers between devices with their start and end apart: 17, of which 6 were waited for; matrix products, arithmetic and copies ran while one was open for 1% of the time, Pallas kernels for 19%

profile of v12, /device:TPU:1, one launch (start us, length us, event | category | flops | bytes accessed | tf_op | source)
XLA Modules:
  0.0 170.6 jit_solution(3749516049084665034)
XLA Ops:
  7.3 8.8 %collective-permute-start = (bf16[32,512]{1,0:T(8,128)(2,1)S(1)}, bf16[32,512]{1,0:T(8,128)(2,1)S(1)}, u32[]{:S(2)}, u32[]{:S(2)}) collective-permute-start(bf16[32,512]{1,0:T(8,128)(2,1)S(1)} %constant_dynamic-slice_fusion), channel_id=1, source_target_pairs={{0,4},{4,0},{1,5},{5,1},{2,6},{6,2},{3,7},{7,3},{8,12},{12,8},{9,1... | collective-permute-start | bytes 98312 | tf_op jit(solution)/shard_map/ppermute | solution.py:21
  19.1 3.7 %shard_map.82 = (bf16[1072,512]{1,0:T(8,128)(2,1)}, bf16[1072,512]{1,0:T(8,128)(2,1)}) custom-call(s32[5]{0:T(128)} %stack.23.refs_0_, bf16[256,1024]{1,0:T(8,128)(2,1)} %refs_1_.1, bf16[256,1024]{1,0:T(8,128)(2,1)} %refs_2_.1, bf16[256,1024]{1,0:T(8,128)(2,1)} %refs_3_.1, bf16[256,1024]{1,0:T(8,128)(2,1)} %refs_4_.1, f32[8,256]{1,0:T(8,128)} %refs_5_.1, ...), custom_call_target="tpu_custom_call" | custom-call | flops 1000000 | bytes 1000000 | tf_op jit(solution)/shard_map/pallas_call | solution.py:59
  22.7 2.3 %collective-permute-start.2 = (bf16[1072,512]{1,0:T(8,128)(2,1)}, bf16[1072,512]{1,0:T(8,128)(2,1)S(1)}, u32[]{:S(2)}, u32[]{:S(2)}) collective-permute-start(bf16[1072,512]{1,0:T(8,128)(2,1)} %get-tuple-element.27), channel_id=1, source_target_pairs={{0,4},{4,0},{1,5},{5,1},{2,6},{6,2},{3,7},{7,3},{8,12},{12,8},{9,1... | collective-permute-start | bytes 3293192 | tf_op jit(solution)/shard_map/ppermute | solution.py:21
  25.0 2.5 %collective-permute-done.2.refs_2_ = bf16[1072,512]{1,0:T(8,128)(2,1)S(1)} collective-permute-done((bf16[1072,512]{1,0:T(8,128)(2,1)}, bf16[1072,512]{1,0:T(8,128)(2,1)S(1)}, u32[]{:S(2)}, u32[]{:S(2)}) %collective-permute-start.2) | collective-permute-done | bytes 1097760 | tf_op jit(solution)/shard_map/ppermute | solution.py:21
  28.6 5.2 %shard_map.83 = (bf16[4,144,128]{2,1,0:T(8,128)(2,1)}, bf16[4,128,128]{2,1,0:T(8,128)(2,1)}) custom-call(s32[5]{0:T(128)} %stack.23.refs_0_, bf16[1072,512]{1,0:T(8,128)(2,1)} %get-tuple-element.25.refs_1_, bf16[1072,512]{1,0:T(8,128)(2,1)} %copy-done.11), custom_call_target="tpu_custom_call" | custom-call | flops 1000000 | bytes 1000000 | tf_op jit(solution)/shard_map/pallas_call | solution.py:59
  33.8 9.4 %all_to_all.20.refs_1_ = bf16[4,144,128]{2,1,0:T(8,128)(2,1)S(1)} all-to-all(bf16[4,144,128]{2,1,0:T(8,128)(2,1)} %get-tuple-element.31), channel_id=1, replica_groups=mesh['y'=4,'a'=4,'p'=2,'q'=2,'c'=2,'x'=4] {'p','q'}, dimensions={0} | all-to-all | bytes 294912 | tf_op jit(solution)/shard_map/all_to_all | solution.py:362
  45.1 9.4 %all-to-all-start.1 = ((bf16[4,144,128]{2,1,0:T(8,128)(2,1)}), bf16[4,144,128]{2,1,0:T(8,128)(2,1)S(1)}, u32[]{:S(2)}, u32[]{:S(2)}) async-start(bf16[4,144,128]{2,1,0:T(8,128)(2,1)} %get-tuple-element.38), calls=%async_computation.1 | async-start | bytes 294912 | tf_op jit(solution)/shard_map/all_to_all | solution.py:364
  56.6 3.7 %collective-permute-start.4 = (bf16[144,256]{1,0:T(8,128)(2,1)S(1)}, bf16[144,256]{1,0:T(8,128)(2,1)S(1)}, u32[]{:S(2)}, u32[]{:S(2)}) collective-permute-start(bf16[144,256]{1,0:T(8,128)(2,1)S(1)} %get-tuple-element.34), channel_id=1, source_target_pairs={{0,16},{8,24},{16,0},{24,8},{1,17},{9,25},{17,1},{25,9},{2,18},{10... | collective-permute-start | bytes 221192 | tf_op jit(solution)/shard_map/ppermute | solution.py:366
  60.3 3.5 %collective-permute-start.5 = (bf16[144,256]{1,0:T(8,128)(2,1)S(1)}, bf16[144,256]{1,0:T(8,128)(2,1)S(1)}, u32[]{:S(2)}, u32[]{:S(2)}) collective-permute-start(bf16[144,256]{1,0:T(8,128)(2,1)S(1)} %get-tuple-element.35), channel_id=1, source_target_pairs={{0,24},{8,16},{16,8},{24,0},{1,25},{9,17},{17,9},{25,1},{2,26},{10... | collective-permute-start | bytes 221192 | tf_op jit(solution)/shard_map/ppermute | solution.py:366
  65.7 5.0 %collective-permute-done.5.refs_8_.refs_4_ = bf16[144,256]{1,0:T(8,128)(2,1)S(1)} collective-permute-done((bf16[144,256]{1,0:T(8,128)(2,1)S(1)}, bf16[144,256]{1,0:T(8,128)(2,1)S(1)}, u32[]{:S(2)}, u32[]{:S(2)}) %collective-permute-start.5) | collective-permute-done | bytes 73760 | tf_op jit(solution)/shard_map/ppermute | solution.py:366
  72.0 10.9 %all-to-all-start.2 = ((bf16[4,144,128]{2,1,0:T(8,128)(2,1)}), bf16[4,144,128]{2,1,0:T(8,128)(2,1)S(1)}, u32[]{:S(2)}, u32[]{:S(2)}) async-start(bf16[4,144,128]{2,1,0:T(8,128)(2,1)} %get-tuple-element.39), calls=%async_computation.2 | async-start | bytes 294912 | tf_op jit(solution)/shard_map/all_to_all | solution.py:377
  83.0 6.4 %shard_map.84 = (f32[512,512]{1,0:T(8,128)}, f32[512,24]{1,0:T(8,128)}) custom-call(s32[5]{0:T(128)} %stack.23.refs_0_, bf16[1072,512]{1,0:T(8,128)(2,1)} %get-tuple-element.25.refs_1_, bf16[1072,512]{1,0:T(8,128)(2,1)} %copy-done.11, bf16[4,128,128]{2,1,0:T(8,128)(2,1)} %get-tuple-element.28.refs_3_), custom_call_target="tpu_custom_call" | custom-call | flops 1000000 | bytes 1000000 | tf_op jit(solution)/shard_map/pallas_call | solution.py:59
  93.0 3.6 %all-to-all-start.3 = ((bf16[4,128,512]{2,1,0:T(8,128)(2,1)}), bf16[4,128,512]{2,1,0:T(8,128)(2,1)S(1)}, u32[]{:S(2)}, u32[]{:S(2)}) async-start(bf16[4,128,512]{2,1,0:T(8,128)(2,1)} %shard_map.88), calls=%async_computation.3 | async-start | bytes 1048576 | tf_op jit(solution)/shard_map/all_to_all | solution.py:383
  96.6 5.2 %collective-permute-start.11 = (bf16[16,64,512]{2,1,0:T(8,128)(2,1)}, bf16[16,64,512]{2,1,0:T(8,128)(2,1)S(1)}, u32[]{:S(2)}, u32[]{:S(2)}) collective-permute-start(bf16[16,64,512]{2,1,0:T(8,128)(2,1)} %bitcast.6), channel_id=1, source_target_pairs={{0,256},{128,384},{256,0},{384,128},{1,257},{129,385},{257,1},{385... | collective-permute-start | bytes 3145736 | tf_op jit(solution)/shard_map/ppermute | solution.py:319
  101.8 2.6 %collective-permute-start.10 = (bf16[16,64,512]{2,1,0:T(8,128)(2,1)}, bf16[16,64,512]{2,1,0:T(8,128)(2,1)S(1)}, u32[]{:S(2)}, u32[]{:S(2)}) collective-permute-start(bf16[16,64,512]{2,1,0:T(8,128)(2,1)} %bitcast.7), channel_id=1, source_target_pairs={{0,128},{128,256},{256,384},{384,0},{1,129},{129,257},{257,385},{3... | collective-permute-start | bytes 3145736 | tf_op jit(solution)/shard_map/ppermute | solution.py:319
  104.5 3.9 %collective-permute-start.9 = (bf16[16,64,512]{2,1,0:T(8,128)(2,1)}, bf16[16,64,512]{2,1,0:T(8,128)(2,1)}, u32[]{:S(2)}, u32[]{:S(2)}) collective-permute-start(bf16[16,64,512]{2,1,0:T(8,128)(2,1)} %bitcast.8), channel_id=1, source_target_pairs={{0,384},{128,0},{256,128},{384,256},{1,385},{129,1},{257,129},{385... | collective-permute-start | bytes 3145736 | tf_op jit(solution)/shard_map/ppermute | solution.py:319
  108.9 4.2 %shard_map.86 = (f32[512,512]{1,0:T(8,128)}, f32[512,16]{1,0:T(8,128)}) custom-call(s32[5]{0:T(128)} %stack.23.refs_0_, bf16[1072,512]{1,0:T(8,128)(2,1)} %get-tuple-element.25.refs_1_, bf16[1072,512]{1,0:T(8,128)(2,1)} %copy-done.11, f32[512,512]{1,0:T(8,128)} %get-tuple-element.29.refs_3_.refs_4_, f32[512,24]{1,0:T(8,128)} %get-tuple-element.30.refs_4_, ...), custom_call_target="tpu_custom_call" | custom-call | flops 1000000 | bytes 1000000 | tf_op jit(solution)/shard_map/pallas_call | solution.py:59
  113.9 5.3 %shard_map.89.refs_1_ = bf16[512,512]{1,0:T(8,128)(2,1)} custom-call(s32[5]{0:T(128)} %stack.23.refs_0_, bf16[1072,512]{1,0:T(8,128)(2,1)} %get-tuple-element.25.refs_1_, bf16[1072,512]{1,0:T(8,128)(2,1)} %copy-done.11, bf16[1,1024]{1,0:T(2,128)(2,1)} %broadcast_in_dim.3.refs_3_, f32[512,512]{1,0:T(8,128)} %get-tuple-element.36.refs_4_, ...), custom_call_target="tpu_custom_call" | custom-call | flops 1000000 | bytes 1000000 | tf_op jit(solution)/shard_map/pallas_call | solution.py:59
  119.2 4.7 %collective-permute-start.8 = (bf16[512,512]{1,0:T(8,128)(2,1)}, bf16[512,512]{1,0:T(8,128)(2,1)S(1)}, u32[]{:S(2)}, u32[]{:S(2)}) collective-permute-start(bf16[512,512]{1,0:T(8,128)(2,1)} %shard_map.89.refs_1_), channel_id=1, source_target_pairs={{0,3},{1,0},{2,1},{3,2},{4,7},{5,4},{6,5},{7,6},{8,11},{9,8},{10,9... | collective-permute-start | bytes 1572872 | tf_op jit(solution)/shard_map/ppermute | solution.py:319
  123.9 2.3 %collective-permute-start.7 = (bf16[512,512]{1,0:T(8,128)(2,1)}, bf16[512,512]{1,0:T(8,128)(2,1)S(1)}, u32[]{:S(2)}, u32[]{:S(2)}) collective-permute-start(bf16[512,512]{1,0:T(8,128)(2,1)} %shard_map.89.refs_1_), channel_id=1, source_target_pairs={{0,2},{1,3},{2,0},{3,1},{4,6},{5,7},{6,4},{7,5},{8,10},{9,11},{10,... | collective-permute-start | bytes 1572872 | tf_op jit(solution)/shard_map/ppermute | solution.py:319
  128.4 17.8 %collective-permute-done.10.refs_7_ = bf16[16,64,512]{2,1,0:T(8,128)(2,1)S(1)} collective-permute-done((bf16[16,64,512]{2,1,0:T(8,128)(2,1)}, bf16[16,64,512]{2,1,0:T(8,128)(2,1)S(1)}, u32[]{:S(2)}, u32[]{:S(2)}) %collective-permute-start.10) | collective-permute-done | bytes 1048608 | tf_op jit(solution)/shard_map/ppermute | solution.py:319
  147.3 3.3 %shard_map.91 = bf16[256,1024]{1,0:T(8,128)(2,1)S(1)} custom-call(s32[5]{0:T(128)S(1)} %copy-done.10, bf16[512,512]{1,0:T(8,128)(2,1)S(1)} %copy-done, bf16[512,512]{1,0:T(8,128)(2,1)S(1)} %collective-permute-done.6.refs_2_, bf16[512,512]{1,0:T(8,128)(2,1)S(1)} %collective-permute-done.7.refs_3_, bf16[512,512]{1,0:T(8,128)(2,1)S(1)} %collective-permute-done.8.refs_4_, ...), custom_call_target="tpu_custom_call" | custom-call | flops 1000000 | bytes 1000000 | tf_op jit(solution)/shard_map/pallas_call | solution.py:59
  150.6 8.9 %collective-permute-start.12 = (bf16[256,1024]{1,0:T(8,128)(2,1)S(1)}, bf16[256,1024]{1,0:T(8,128)(2,1)S(1)}, u32[]{:S(2)}, u32[]{:S(2)}) collective-permute-start(bf16[256,1024]{1,0:T(8,128)(2,1)S(1)} %shard_map.91), channel_id=1, source_target_pairs={{0,4},{4,0},{1,5},{5,1},{2,6},{6,2},{3,7},{7,3},{8,12},{12,8},{9,1... | collective-permute-start | bytes 1572872 | tf_op jit(solution)/shard_map/ppermute | solution.py:21
  159.5 3.3 %shard_map.90 = f32[256,1024]{1,0:T(8,128)S(1)} custom-call(s32[5]{0:T(128)S(1)} %copy-done.10, bf16[512,512]{1,0:T(8,128)(2,1)S(1)} %copy-done.1, bf16[512,512]{1,0:T(8,128)(2,1)S(1)} %collective-permute-done.6.refs_2_, bf16[512,512]{1,0:T(8,128)(2,1)S(1)} %collective-permute-done.7.refs_3_, bf16[512,512]{1,0:T(8,128)(2,1)S(1)} %collective-permute-done.8.refs_4_, ...), custom_call_target="tpu_custom_call" | custom-call | flops 1000000 | bytes 1000000 | tf_op jit(solution)/shard_map/pallas_call | solution.py:59
  (58 shorter events, 21.0 us)
Async XLA Ops:
  6.5 86.5 %all-gather.3.cloned.1.call-start = ((), (), s32[]{:S(2)}) async-start(), calls=%async_computation.4 | async-start | bytes 1114112 | tf_op jit(solution)/shard_map/all_gather | solution.py:346
  7.3 9.6 %collective-permute-start = (bf16[32,512]{1,0:T(8,128)(2,1)S(1)}, bf16[32,512]{1,0:T(8,128)(2,1)S(1)}, u32[]{:S(2)}, u32[]{:S(2)}) collective-permute-start(bf16[32,512]{1,0:T(8,128)(2,1)S(1)} %constant_dynamic-slice_fusion), channel_id=1, source_target_pairs={{0,4},{4,0},{1,5},{5,1},{2,6},{6,2},{3,7},{7,3},{8,12},{12,8},{9,1... | collective-permute-start | bytes 98312 | tf_op jit(solution)/shard_map/ppermute | solution.py:21
  17.7 5.0 %collective-permute-start.1 = (bf16[64,512]{1,0:T(8,128)(2,1)S(1)}, bf16[64,512]{1,0:T(8,128)(2,1)S(1)}, u32[]{:S(2)}, u32[]{:S(2)}) collective-permute-start(bf16[64,512]{1,0:T(8,128)(2,1)S(1)} %pad_maximum_fusion), channel_id=1, source_target_pairs={{0,0},{1,128},{2,256},{3,384},{128,1},{129,129},{130,257},{131,385... | collective-permute-start | bytes 196616 | tf_op jit(solution)/shard_map/ppermute | solution.py:331
  22.7 4.8 %collective-permute-start.2 = (bf16[1072,512]{1,0:T(8,128)(2,1)}, bf16[1072,512]{1,0:T(8,128)(2,1)S(1)}, u32[]{:S(2)}, u32[]{:S(2)}) collective-permute-start(bf16[1072,512]{1,0:T(8,128)(2,1)} %get-tuple-element.27), channel_id=1, source_target_pairs={{0,4},{4,0},{1,5},{5,1},{2,6},{6,2},{3,7},{7,3},{8,12},{12,8},{9,1... | collective-permute-start | bytes 3293192 | tf_op jit(solution)/shard_map/ppermute | solution.py:21
  28.6 14.7 %copy-start.8 = (s32[5]{0:T(128)S(1)}, s32[5]{0:T(128)}, u32[]{:S(2)}) copy-start(s32[5]{0:T(128)} %stack.23.refs_0_) | copy-start | bytes 64
  45.1 25.6 %all-to-all-start.1 = ((bf16[4,144,128]{2,1,0:T(8,128)(2,1)}), bf16[4,144,128]{2,1,0:T(8,128)(2,1)S(1)}, u32[]{:S(2)}, u32[]{:S(2)}) async-start(bf16[4,144,128]{2,1,0:T(8,128)(2,1)} %get-tuple-element.38), calls=%async_computation.1 | async-start | bytes 294912 | tf_op jit(solution)/shard_map/all_to_all | solution.py:364
  54.6 9.3 %collective-permute-start.3 = (bf16[144,256]{1,0:T(8,128)(2,1)S(1)}, bf16[144,256]{1,0:T(8,128)(2,1)S(1)}, u32[]{:S(2)}, u32[]{:S(2)}) collective-permute-start(bf16[144,256]{1,0:T(8,128)(2,1)S(1)} %get-tuple-element.33), channel_id=1, source_target_pairs={{0,8},{8,0},{16,24},{24,16},{1,9},{9,1},{17,25},{25,17},{2,10},{10... | collective-permute-start | bytes 221192 | tf_op jit(solution)/shard_map/ppermute | solution.py:366
  56.6 9.1 %collective-permute-start.4 = (bf16[144,256]{1,0:T(8,128)(2,1)S(1)}, bf16[144,256]{1,0:T(8,128)(2,1)S(1)}, u32[]{:S(2)}, u32[]{:S(2)}) collective-permute-start(bf16[144,256]{1,0:T(8,128)(2,1)S(1)} %get-tuple-element.34), channel_id=1, source_target_pairs={{0,16},{8,24},{16,0},{24,8},{1,17},{9,25},{17,1},{25,9},{2,18},{10... | collective-permute-start | bytes 221192 | tf_op jit(solution)/shard_map/ppermute | solution.py:366
  60.3 10.4 %collective-permute-start.5 = (bf16[144,256]{1,0:T(8,128)(2,1)S(1)}, bf16[144,256]{1,0:T(8,128)(2,1)S(1)}, u32[]{:S(2)}, u32[]{:S(2)}) collective-permute-start(bf16[144,256]{1,0:T(8,128)(2,1)S(1)} %get-tuple-element.35), channel_id=1, source_target_pairs={{0,24},{8,16},{16,8},{24,0},{1,25},{9,17},{17,9},{25,1},{2,26},{10... | collective-permute-start | bytes 221192 | tf_op jit(solution)/shard_map/ppermute | solution.py:366
  63.9 25.5 %copy-start.4 = (bf16[144,256]{1,0:T(8,128)(2,1)}, bf16[144,256]{1,0:T(8,128)(2,1)S(1)}, u32[]{:S(2)}) copy-start(bf16[144,256]{1,0:T(8,128)(2,1)S(1)} %collective-permute-done.3.refs_6_.refs_2_) | copy-start | bytes 221188
  65.7 23.7 %copy-start.5 = (bf16[144,256]{1,0:T(8,128)(2,1)}, bf16[144,256]{1,0:T(8,128)(2,1)S(1)}, u32[]{:S(2)}) copy-start(bf16[144,256]{1,0:T(8,128)(2,1)S(1)} %collective-permute-done.4.refs_7_.refs_3_) | copy-start | bytes 221188
  70.8 18.6 %copy-start.6 = (bf16[144,256]{1,0:T(8,128)(2,1)}, bf16[144,256]{1,0:T(8,128)(2,1)S(1)}, u32[]{:S(2)}) copy-start(bf16[144,256]{1,0:T(8,128)(2,1)S(1)} %collective-permute-done.5.refs_8_.refs_4_) | copy-start | bytes 221188
  72.0 17.4 %all-to-all-start.2 = ((bf16[4,144,128]{2,1,0:T(8,128)(2,1)}), bf16[4,144,128]{2,1,0:T(8,128)(2,1)S(1)}, u32[]{:S(2)}, u32[]{:S(2)}) async-start(bf16[4,144,128]{2,1,0:T(8,128)(2,1)} %get-tuple-element.39), calls=%async_computation.2 | async-start | bytes 294912 | tf_op jit(solution)/shard_map/all_to_all | solution.py:377
  90.7 17.7 %copy-start.14 = (bf16[1024]{0:T(1024)(128)(2,1)S(1)}, bf16[1024]{0:T(1024)(128)(2,1)}, u32[]{:S(2)}) copy-start(bf16[1024]{0:T(1024)(128)(2,1)} %param.14) | copy-start | bytes 6148
  93.0 20.1 %all-to-all-start.3 = ((bf16[4,128,512]{2,1,0:T(8,128)(2,1)}), bf16[4,128,512]{2,1,0:T(8,128)(2,1)S(1)}, u32[]{:S(2)}, u32[]{:S(2)}) async-start(bf16[4,128,512]{2,1,0:T(8,128)(2,1)} %shard_map.88), calls=%async_computation.3 | async-start | bytes 1048576 | tf_op jit(solution)/shard_map/all_to_all | solution.py:383
  96.6 29.6 %collective-permute-start.11 = (bf16[16,64,512]{2,1,0:T(8,128)(2,1)}, bf16[16,64,512]{2,1,0:T(8,128)(2,1)S(1)}, u32[]{:S(2)}, u32[]{:S(2)}) collective-permute-start(bf16[16,64,512]{2,1,0:T(8,128)(2,1)} %bitcast.6), channel_id=1, source_target_pairs={{0,256},{128,384},{256,0},{384,128},{1,257},{129,385},{257,1},{385... | collective-permute-start | bytes 3145736 | tf_op jit(solution)/shard_map/ppermute | solution.py:319
  101.8 44.3 %collective-permute-start.10 = (bf16[16,64,512]{2,1,0:T(8,128)(2,1)}, bf16[16,64,512]{2,1,0:T(8,128)(2,1)S(1)}, u32[]{:S(2)}, u32[]{:S(2)}) collective-permute-start(bf16[16,64,512]{2,1,0:T(8,128)(2,1)} %bitcast.7), channel_id=1, source_target_pairs={{0,128},{128,256},{256,384},{384,0},{1,129},{129,257},{257,385},{3... | collective-permute-start | bytes 3145736 | tf_op jit(solution)/shard_map/ppermute | solution.py:319
  104.5 41.7 %collective-permute-start.9 = (bf16[16,64,512]{2,1,0:T(8,128)(2,1)}, bf16[16,64,512]{2,1,0:T(8,128)(2,1)}, u32[]{:S(2)}, u32[]{:S(2)}) collective-permute-start(bf16[16,64,512]{2,1,0:T(8,128)(2,1)} %bitcast.8), channel_id=1, source_target_pairs={{0,384},{128,0},{256,128},{384,256},{1,385},{129,1},{257,129},{385... | collective-permute-start | bytes 3145736 | tf_op jit(solution)/shard_map/ppermute | solution.py:319
  113.9 32.3 %copy-start.3 = (bf16[1024,512]{1,0:T(8,128)(2,1)S(1)}, bf16[1024,512]{1,0:T(8,128)(2,1)}, u32[]{:S(2)}) copy-start(bf16[1024,512]{1,0:T(8,128)(2,1)} %all-gather.3.cloned.1.call-done) | copy-start | bytes 3145732
  113.9 32.3 %copy-start.10 = (s32[5]{0:T(128)S(1)}, s32[5]{0:T(128)}, u32[]{:S(2)}) copy-start(s32[5]{0:T(128)} %stack.23.refs_0_) | copy-start | bytes 64
  119.2 26.9 %collective-permute-start.8 = (bf16[512,512]{1,0:T(8,128)(2,1)}, bf16[512,512]{1,0:T(8,128)(2,1)S(1)}, u32[]{:S(2)}, u32[]{:S(2)}) collective-permute-start(bf16[512,512]{1,0:T(8,128)(2,1)} %shard_map.89.refs_1_), channel_id=1, source_target_pairs={{0,3},{1,0},{2,1},{3,2},{4,7},{5,4},{6,5},{7,6},{8,11},{9,8},{10,9... | collective-permute-start | bytes 1572872 | tf_op jit(solution)/shard_map/ppermute | solution.py:319
  123.9 22.2 %collective-permute-start.7 = (bf16[512,512]{1,0:T(8,128)(2,1)}, bf16[512,512]{1,0:T(8,128)(2,1)S(1)}, u32[]{:S(2)}, u32[]{:S(2)}) collective-permute-start(bf16[512,512]{1,0:T(8,128)(2,1)} %shard_map.89.refs_1_), channel_id=1, source_target_pairs={{0,2},{1,3},{2,0},{3,1},{4,6},{5,7},{6,4},{7,5},{8,10},{9,11},{10,... | collective-permute-start | bytes 1572872 | tf_op jit(solution)/shard_map/ppermute | solution.py:319
  126.2 20.0 %collective-permute-start.6 = (bf16[512,512]{1,0:T(8,128)(2,1)}, bf16[512,512]{1,0:T(8,128)(2,1)S(1)}, u32[]{:S(2)}, u32[]{:S(2)}) collective-permute-start(bf16[512,512]{1,0:T(8,128)(2,1)} %shard_map.89.refs_1_), channel_id=1, source_target_pairs={{0,1},{1,2},{2,3},{3,0},{4,5},{5,6},{6,7},{7,4},{8,9},{9,10},{10,1... | collective-permute-start | bytes 1572872 | tf_op jit(solution)/shard_map/ppermute | solution.py:319
  150.6 12.2 %collective-permute-start.12 = (bf16[256,1024]{1,0:T(8,128)(2,1)S(1)}, bf16[256,1024]{1,0:T(8,128)(2,1)S(1)}, u32[]{:S(2)}, u32[]{:S(2)}) collective-permute-start(bf16[256,1024]{1,0:T(8,128)(2,1)S(1)} %shard_map.91), channel_id=1, source_target_pairs={{0,4},{4,0},{1,5},{5,1},{2,6},{6,2},{3,7},{7,3},{8,12},{12,8},{9,1... | collective-permute-start | bytes 1572872 | tf_op jit(solution)/shard_map/ppermute | solution.py:21
  (8 other events, 25.6 us)
Sparse Core Ops, SparseCore 0:
  25.2 67.8 all-gather.2

commit v13 on v11

--- a/solution.py
+++ b/solution.py
@@ -246,35 +246,34 @@
             normed[here, hc] = (gated * size * gain[:, mine].astype(F32)).astype(BF)
 
 
-def project_body(other, at, b0, b1, b2, b3, gathered, next_right, far_right, out, left, right, sems):
+def project_body(other, at, b0, b1, b2, b3, w0, w1, w2, w3, out, left, right, sems):
     row = (1 - at[0]) if other else at[0]
     rows = pl.ds(pl.multiple_of(row * 256, 256), 256)
-    pieces = (gathered.at[:, :, 0:512], gathered.at[:, :, 512:1024], next_right, far_right)
     copies = [
-        pltpu.make_async_copy(piece, right.at[k], sems.at[k]) for k, piece in enumerate(pieces)
+        pltpu.make_async_copy(w, right.at[k], sems.at[k]) for k, w in enumerate((w0, w1, w2, w3))
     ]
     for copy in copies:
         copy.start()
     for j, block in enumerate((b0, b1, b2, b3)):
         left[(at[4] + 4 - j) % 4] = block[rows, :]
     total = 0.0
-    for k, turn in enumerate((0, 3, 1, 2)):
+    for k, turn in enumerate((0, 1, 3, 2)):
         copies[k].wait()
         total += dot(left[(at[3] + turn) % 4], right[k].reshape(1024, 512), NT)
     out[...] = total.astype(out.dtype)
 
 
-def project(at, blocks, gathered, next_right, far_right, other):
+def project(at, blocks, rights, other):
     return call(
         functools.partial(project_body, other),
         [((256, 1024), BF if other else F32)],
-        (at, *blocks, gathered, next_right, far_right),
+        (at, *blocks, *rights),
         scratch=[
             pltpu.VMEM((4, 256, 512), BF),
             pltpu.VMEM((4, 16, 64, 512), BF),
             pltpu.SemaphoreType.DMA((4,)),
         ],
-        hbm=(5, 6, 7),
+        hbm=range(5, 9),
         vmem=20,
     )[0]
 
@@ -284,17 +283,15 @@
 
 
 def shards(values, keys, queries, gates, log_decay, level_mix, norm_gain, weight):
-    y, a, b, c, x = (lax.axis_index(n) for n in ("y", "a", NEAR, "c", "x"))
+    y, a, b, q, c, x = (lax.axis_index(n) for n in ("y", "a", NEAR, "q", "c", "x"))
     at = jnp.stack([c, b, a, y, x]).astype(jnp.int32)
     kept = lax.dynamic_slice_in_dim(weight, c * 512, 512, 1)
     theirs = swap(lax.dynamic_slice_in_dim(weight, (1 - c) * 512, 512, 1))
     both = jnp.concatenate(
         [jnp.where(c == 0, kept, theirs), jnp.where(c == 0, theirs, kept)]
     )
-    mine = []
-    for k in range(2):
-        perm = [(s * 4 + f, ((f + k) % 4) * 4 + s) for s in range(4) for f in range(4)]
-        mine.append(lax.ppermute(both, ("y", "x"), perm))
+    perm = [(s * 4 + f, f * 4 + s) for s in range(4) for f in range(4)]
+    mine = lax.ppermute(both, ("y", "x"), perm)
     block = ((ROWS, 512), BF)
     keep, send = call(
         pack_body,
@@ -309,8 +306,9 @@
         vmem=60,
     )
     mine, send = lax.optimization_barrier((mine, send))
-    mine = jnp.concatenate(mine, axis=1)
-    gathered = lax.all_gather(mine, ("a", "p", "q"))
+    theirs = lax.ppermute(mine, "q", [(0, 1), (1, 0)])
+    mine = jnp.stack([jnp.where(q == 0, mine, theirs), jnp.where(q == 0, theirs, mine)])
+    gathered = lax.all_gather(mine, ("a", "p"), axis=0, tiled=True)
 
     got = swap(send)
     pay = ((4, 144, 128), BF)
@@ -328,10 +326,12 @@
         far_body,
         [pay, ((128, 256), BF), ((8, 128), F32)],
         (at, far),
-        unread=(mixture, *near[1:]),
+        unread=near[1:],
     )
     rows = lax.all_to_all(pay_y, "y", 0, 0, tiled=True)
-    (states,) = call(last_body, [((4, 128, 512), BF)], (at, rows, before, far))
+    (states,) = call(
+        last_body, [((4, 128, 512), BF)], (at, rows, before, far), unread=(mixture,)
+    )
     states = lax.all_to_all(states, NEAR, 0, 0, tiled=True)
     mixture, coef = call(
         mix_body,
@@ -339,16 +339,15 @@
         (at, keep, got, mixture, coef, *near),
         scratch=[pltpu.VMEM((4, 144, 256), BF)],
     )
+    _, gathered = lax.optimization_barrier((coef, gathered))
+    rights = [gathered] + [shift(gathered, "y", 4 - k) for k in (1, 3, 2)]
     (normed,) = call(
         norm_body, [((512, 512), BF)], (at, keep, got, norm_gain[None], mixture, coef, states)
     )
 
-    _, gathered = lax.optimization_barrier((normed, gathered))
-    next_right = shift(gathered[:, :, :512], "y", 3)
-    far_right = shift(gathered[:, :, 512:], "y", 1)
     blocks = [normed] + [shift(normed, "x", j) for j in (1, 2, 3)]
-    theirs = swap(project(at, blocks, gathered, next_right, far_right, True))
-    own = project(at, blocks, gathered, next_right, far_right, False)
+    theirs = swap(project(at, blocks, rights, True))
+    own = project(at, blocks, rights, False)
     return (own + theirs.astype(F32)).astype(BF)
 
 

time: 175 us -> 174 us (level)
  blocking collectives: 24.8 us -> 8.1 us
  starting transfers between devices: 55.1 us -> 69.1 us
  Pallas kernels: 22.3 us -> 24.4 us
  local copies, waits for them, and re-layouts: 13.9 us -> 12 us
    all_to_all x1 -> x0, blocking collectives: 16.3 us -> none  [shards(): rows = lax.all_to_all(pay_y, 'y', 0, 0, tiled=True)]
    all_to_all x1, waiting for transfers between devices: 11 us -> 0.01 us  [shards(): states = lax.all_to_all(states, NEAR, 0, 0, tiled=True)]
    all_to_all x0 -> x1, starting transfers between devices: none -> 10.3 us  [shards(): rows = lax.all_to_all(pay_y, 'y', 0, 0, tiled=True)]
    ppermute x3, waiting for transfers between devices: 3.44 us -> 11.6 us  [shards(): lax.ppermute(near[k], NEAR, [(i, i ^ k) for i in range(4)])]
    ppermute x5 -> x6, starting transfers between devices: 14.9 us -> 19.2 us  [shift(): return lax.ppermute(value, axis, [(i, (i + by) % 4) for i in range(4)])]
    ppermute x2, waiting for transfers between devices: 0.01 us -> 3.51 us  [the longest x1 3.5 us: shards(): theirs = lax.ppermute(mine, 'q', [(0, 1), (1, 0)])]
    ppermute x5 -> x6, waiting for transfers between devices: 24.1 us -> 26.7 us  [shift(): return lax.ppermute(value, axis, [(i, (i + by) % 4) for i in range(4)])]
    ppermute x3, waiting for transfers between devices: 3.38 us -> 0.84 us  [swap(): return lax.ppermute(value, 'c', [(0, 1), (1, 0)])]
  transfers between devices with their start and end apart: 16 -> 18, of which waited for: 7 -> 7; matrix products, arithmetic and copies ran while one was open for 0% -> 1% of each run, Pallas kernels for 11% -> 12%
where the time goes in v13:
time: 174 us; the launch traced here: 172 us
  starting transfers between devices  69.1 us (40%)
  waiting for transfers between devices  42.7 us (25%)
  Pallas kernels  24.4 us (14%)
  between operations  13.8 us (8%)
  local copies, waits for them, and re-layouts  12 us (7%)
  blocking collectives  8.1 us (5%)
  other arithmetic  2.4 us (1%)
    ppermute x6, waiting for transfers between devices, shift(): return lax.ppermute(value, axis, [(i, (i + by) % 4) for i in range(4)])  26.7 us
    pallas_call x10, Pallas kernels, call(): pl.pallas_call(run, out_shape=[jax.ShapeDtypeStruct(*o) for o in outs], i...  24.4 us
    ppermute x6, starting transfers between devices, shift(): return lax.ppermute(value, axis, [(i, (i + by) % 4) for i in range(4)])  19.2 us
    ppermute x3, starting transfers between devices, swap(): return lax.ppermute(value, 'c', [(0, 1), (1, 0)])  13.7 us
    ppermute x3, waiting for transfers between devices, shards(): lax.ppermute(near[k], NEAR, [(i, i ^ k) for i in range(4)])  11.6 us
    unnamed x40, local copies, waits for them, and re-layouts  10.6 us
    all_to_all x1, starting transfers between devices, shards(): rows = lax.all_to_all(pay_y, 'y', 0, 0, tiled=True)  10.3 us
    all_to_all x1, starting transfers between devices, shards(): far = lax.all_to_all(pay_a, 'a', 0, 0, tiled=True)  9.72 us
  transfers between devices with their start and end apart: 18, of which 7 were waited for; matrix products, arithmetic and copies ran while one was open for 1% of the time, Pallas kernels for 12%

profile of v13, /device:TPU:1, one launch (start us, length us, event | category | flops | bytes accessed | tf_op | source)
XLA Modules:
  0.0 172.4 jit_solution(8381068206429363027)
XLA Ops:
  7.3 8.8 %collective-permute-start = (bf16[32,512]{1,0:T(8,128)(2,1)S(1)}, bf16[32,512]{1,0:T(8,128)(2,1)S(1)}, u32[]{:S(2)}, u32[]{:S(2)}) collective-permute-start(bf16[32,512]{1,0:T(8,128)(2,1)S(1)} %constant_dynamic-slice_fusion), channel_id=1, source_target_pairs={{0,4},{4,0},{1,5},{5,1},{2,6},{6,2},{3,7},{7,3},{8,12},{12,8},{9,1... | collective-permute-start | bytes 98312 | tf_op jit(solution)/shard_map/ppermute | solution.py:21
  19.1 3.8 %shard_map.82 = (bf16[1072,512]{1,0:T(8,128)(2,1)}, bf16[1072,512]{1,0:T(8,128)(2,1)}) custom-call(s32[5]{0:T(128)} %stack.32.refs_0_, bf16[256,1024]{1,0:T(8,128)(2,1)} %refs_1_.1, bf16[256,1024]{1,0:T(8,128)(2,1)} %refs_2_.1, bf16[256,1024]{1,0:T(8,128)(2,1)} %refs_3_.1, bf16[256,1024]{1,0:T(8,128)(2,1)} %refs_4_.1, f32[8,256]{1,0:T(8,128)} %refs_5_.1, ...), custom_call_target="tpu_custom_call" | custom-call | flops 1000000 | bytes 1000000 | tf_op jit(solution)/shard_map/pallas_call | solution.py:59
  22.8 2.3 %collective-permute-start.2 = (bf16[1072,512]{1,0:T(8,128)(2,1)}, bf16[1072,512]{1,0:T(8,128)(2,1)S(1)}, u32[]{:S(2)}, u32[]{:S(2)}) collective-permute-start(bf16[1072,512]{1,0:T(8,128)(2,1)} %get-tuple-element.26), channel_id=1, source_target_pairs={{0,4},{4,0},{1,5},{5,1},{2,6},{6,2},{3,7},{7,3},{8,12},{12,8},{9,1... | collective-permute-start | bytes 3293192 | tf_op jit(solution)/shard_map/ppermute | solution.py:21
  27.0 3.5 %collective-permute-done.9 = bf16[64,512]{1,0:T(8,128)(2,1)S(1)} collective-permute-done((bf16[64,512]{1,0:T(8,128)(2,1)S(1)}, bf16[64,512]{1,0:T(8,128)(2,1)S(1)}, u32[]{:S(2)}, u32[]{:S(2)}) %collective-permute-start.9) | collective-permute-done | bytes 65568 | tf_op jit(solution)/shard_map/ppermute | solution.py:309
  34.3 8.1 %all_to_all.20.refs_1_ = bf16[4,144,128]{2,1,0:T(8,128)(2,1)S(1)} all-to-all(bf16[4,144,128]{2,1,0:T(8,128)(2,1)S(1)} %get-tuple-element.30), channel_id=1, replica_groups=mesh['y'=4,'a'=4,'p'=2,'q'=2,'c'=2,'x'=4] {'p','q'}, dimensions={0} | all-to-all | bytes 294912 | tf_op jit(solution)/shard_map/all_to_all | solution.py:316
  44.3 9.7 %all-to-all-start.1 = ((bf16[4,144,128]{2,1,0:T(8,128)(2,1)}), bf16[4,144,128]{2,1,0:T(8,128)(2,1)S(1)}, u32[]{:S(2)}, u32[]{:S(2)}) async-start(bf16[4,144,128]{2,1,0:T(8,128)(2,1)} %get-tuple-element.37), calls=%async_computation.1 | async-start | bytes 294912 | tf_op jit(solution)/shard_map/all_to_all | solution.py:318
  54.0 2.2 %collective-permute-start.3 = (bf16[144,256]{1,0:T(8,128)(2,1)S(1)}, bf16[144,256]{1,0:T(8,128)(2,1)S(1)}, u32[]{:S(2)}, u32[]{:S(2)}) collective-permute-start(bf16[144,256]{1,0:T(8,128)(2,1)S(1)} %get-tuple-element.32), channel_id=1, source_target_pairs={{0,8},{8,0},{16,24},{24,16},{1,9},{9,1},{17,25},{25,17},{2,10},{10... | collective-permute-start | bytes 221192 | tf_op jit(solution)/shard_map/ppermute | solution.py:320
  56.3 2.9 %collective-permute-start.4 = (bf16[144,256]{1,0:T(8,128)(2,1)S(1)}, bf16[144,256]{1,0:T(8,128)(2,1)S(1)}, u32[]{:S(2)}, u32[]{:S(2)}) collective-permute-start(bf16[144,256]{1,0:T(8,128)(2,1)S(1)} %get-tuple-element.33), channel_id=1, source_target_pairs={{0,16},{8,24},{16,0},{24,8},{1,17},{9,25},{17,1},{25,9},{2,18},{10... | collective-permute-start | bytes 221192 | tf_op jit(solution)/shard_map/ppermute | solution.py:320
  59.2 4.1 %collective-permute-start.5 = (bf16[144,256]{1,0:T(8,128)(2,1)S(1)}, bf16[144,256]{1,0:T(8,128)(2,1)S(1)}, u32[]{:S(2)}, u32[]{:S(2)}) collective-permute-start(bf16[144,256]{1,0:T(8,128)(2,1)S(1)} %get-tuple-element.34), channel_id=1, source_target_pairs={{0,24},{8,16},{16,8},{24,0},{1,25},{9,17},{17,9},{25,1},{2,26},{10... | collective-permute-start | bytes 221192 | tf_op jit(solution)/shard_map/ppermute | solution.py:320
  63.3 3.8 %collective-permute-done.3.refs_6_.refs_2_ = bf16[144,256]{1,0:T(8,128)(2,1)S(1)} collective-permute-done((bf16[144,256]{1,0:T(8,128)(2,1)S(1)}, bf16[144,256]{1,0:T(8,128)(2,1)S(1)}, u32[]{:S(2)}, u32[]{:S(2)}) %collective-permute-start.3) | collective-permute-done | bytes 73760 | tf_op jit(solution)/shard_map/ppermute | solution.py:320
  67.4 7.5 %collective-permute-done.5.refs_8_.refs_4_ = bf16[144,256]{1,0:T(8,128)(2,1)S(1)} collective-permute-done((bf16[144,256]{1,0:T(8,128)(2,1)S(1)}, bf16[144,256]{1,0:T(8,128)(2,1)S(1)}, u32[]{:S(2)}, u32[]{:S(2)}) %collective-permute-start.5) | collective-permute-done | bytes 73760 | tf_op jit(solution)/shard_map/ppermute | solution.py:320
  76.8 10.3 %all-to-all-start.2 = ((bf16[4,144,128]{2,1,0:T(8,128)(2,1)}), bf16[4,144,128]{2,1,0:T(8,128)(2,1)S(1)}, u32[]{:S(2)}, u32[]{:S(2)}) async-start(bf16[4,144,128]{2,1,0:T(8,128)(2,1)} %get-tuple-element.38), calls=%async_computation.2 | async-start | bytes 294912 | tf_op jit(solution)/shard_map/all_to_all | solution.py:331
  88.0 4.3 %shard_map.84 = (f32[512,512]{1,0:T(8,128)S(1)}, f32[512,24]{1,0:T(8,128)S(1)}) custom-call(s32[5]{0:T(128)S(1)} %copy-done.18, bf16[1072,512]{1,0:T(8,128)(2,1)S(1)} %copy-done.1, bf16[1072,512]{1,0:T(8,128)(2,1)S(1)} %collective-permute-done.2.refs_2_, bf16[4,128,128]{2,1,0:T(8,128)(2,1)S(1)} %copy-done.13), custom_call_target="tpu_custom_call" | custom-call | flops 1000000 | bytes 1000000 | tf_op jit(solution)/shard_map/pallas_call | solution.py:59
  95.3 4.3 %all-to-all-start.3 = ((bf16[4,128,512]{2,1,0:T(8,128)(2,1)}), bf16[4,128,512]{2,1,0:T(8,128)(2,1)}, u32[]{:S(2)}, u32[]{:S(2)}) async-start(bf16[4,128,512]{2,1,0:T(8,128)(2,1)} %copy-done.3), calls=%async_computation.3 | async-start | bytes 1048576 | tf_op jit(solution)/shard_map/all_to_all | solution.py:335
  103.9 4.9 %collective-permute-start.12 = (bf16[16,64,512]{2,1,0:T(8,128)(2,1)}, bf16[16,64,512]{2,1,0:T(8,128)(2,1)S(1)}, u32[]{:S(2)}, u32[]{:S(2)}) collective-permute-start(bf16[16,64,512]{2,1,0:T(8,128)(2,1)} %all-gather.2.cloned.1.call-done.refs_5_), channel_id=1, source_target_pairs={{0,256},{128,384},{256,0},{384,128},{1,257},{129,385},{257,1},{385... | collective-permute-start | bytes 3145736 | tf_op jit(solution)/shard_map/ppermute | solution.py:282
  108.8 2.2 %collective-permute-start.11 = (bf16[16,64,512]{2,1,0:T(8,128)(2,1)}, bf16[16,64,512]{2,1,0:T(8,128)(2,1)}, u32[]{:S(2)}, u32[]{:S(2)}) collective-permute-start(bf16[16,64,512]{2,1,0:T(8,128)(2,1)} %all-gather.2.cloned.1.call-done.refs_5_), channel_id=1, source_target_pairs={{0,128},{128,256},{256,384},{384,0},{1,129},{129,257},{257,385},{3... | collective-permute-start | bytes 3145736 | tf_op jit(solution)/shard_map/ppermute | solution.py:282
  111.0 4.3 %collective-permute-start.10 = (bf16[16,64,512]{2,1,0:T(8,128)(2,1)}, bf16[16,64,512]{2,1,0:T(8,128)(2,1)}, u32[]{:S(2)}, u32[]{:S(2)}) collective-permute-start(bf16[16,64,512]{2,1,0:T(8,128)(2,1)} %all-gather.2.cloned.1.call-done.refs_5_), channel_id=1, source_target_pairs={{0,384},{128,0},{256,128},{384,256},{1,385},{129,1},{257,129},{385... | collective-permute-start | bytes 3145736 | tf_op jit(solution)/shard_map/ppermute | solution.py:282
  117.5 3.1 %shard_map.89.refs_1_ = bf16[512,512]{1,0:T(8,128)(2,1)S(1)} custom-call(s32[5]{0:T(128)S(1)} %copy-done.18, bf16[1072,512]{1,0:T(8,128)(2,1)S(1)} %copy-done.1, bf16[1072,512]{1,0:T(8,128)(2,1)S(1)} %collective-permute-done.2.refs_2_, bf16[1,1024]{1,0:T(2,128)(2,1)S(1)} %broadcast_in_dim.3.refs_3_, f32[512,512]{1,0:T(8,128)S(1)} %copy-done.5, ...), custom_call_target="tpu_custom_call" | custom-call | flops 1000000 | bytes 1000000 | tf_op jit(solution)/shard_map/pallas_call | solution.py:59
  120.6 4.0 %collective-permute-start.8 = (bf16[512,512]{1,0:T(8,128)(2,1)S(1)}, bf16[512,512]{1,0:T(8,128)(2,1)S(1)}, u32[]{:S(2)}, u32[]{:S(2)}) collective-permute-start(bf16[512,512]{1,0:T(8,128)(2,1)S(1)} %shard_map.89.refs_1_), channel_id=1, source_target_pairs={{0,3},{1,0},{2,1},{3,2},{4,7},{5,4},{6,5},{7,6},{8,11},{9,8},{10,9... | collective-permute-start | bytes 1572872 | tf_op jit(solution)/shard_map/ppermute | solution.py:282
  126.6 3.3 %collective-permute-done.12.refs_8_ = bf16[16,64,512]{2,1,0:T(8,128)(2,1)S(1)} collective-permute-done((bf16[16,64,512]{2,1,0:T(8,128)(2,1)}, bf16[16,64,512]{2,1,0:T(8,128)(2,1)S(1)}, u32[]{:S(2)}, u32[]{:S(2)}) %collective-permute-start.12) | collective-permute-done | bytes 1048608 | tf_op jit(solution)/shard_map/ppermute | solution.py:282
  131.8 23.4 %collective-permute-done.11.refs_7_ = bf16[16,64,512]{2,1,0:T(8,128)(2,1)} collective-permute-done((bf16[16,64,512]{2,1,0:T(8,128)(2,1)}, bf16[16,64,512]{2,1,0:T(8,128)(2,1)}, u32[]{:S(2)}, u32[]{:S(2)}) %collective-permute-start.11) | collective-permute-done | bytes 1048608 | tf_op jit(solution)/shard_map/ppermute | solution.py:282
  155.2 3.3 %shard_map.91 = bf16[256,1024]{1,0:T(8,128)(2,1)S(1)} custom-call(s32[5]{0:T(128)S(1)} %copy-done.18, bf16[512,512]{1,0:T(8,128)(2,1)S(1)} %shard_map.89.refs_1_, bf16[512,512]{1,0:T(8,128)(2,1)S(1)} %collective-permute-done.6.refs_2_, bf16[512,512]{1,0:T(8,128)(2,1)S(1)} %collective-permute-done.7.refs_3_, ...), custom_call_target="tpu_custom_call" | custom-call | flops 1000000 | bytes 1000000 | tf_op jit(solution)/shard_map/pallas_call | solution.py:59
  158.6 2.7 %collective-permute-start.13 = (bf16[256,1024]{1,0:T(8,128)(2,1)S(1)}, bf16[256,1024]{1,0:T(8,128)(2,1)S(1)}, u32[]{:S(2)}, u32[]{:S(2)}) collective-permute-start(bf16[256,1024]{1,0:T(8,128)(2,1)S(1)} %shard_map.91), channel_id=1, source_target_pairs={{0,4},{4,0},{1,5},{5,1},{2,6},{6,2},{3,7},{7,3},{8,12},{12,8},{9,1... | collective-permute-start | bytes 1572872 | tf_op jit(solution)/shard_map/ppermute | solution.py:21
  161.3 3.3 %shard_map.90 = f32[256,1024]{1,0:T(8,128)S(1)} custom-call(s32[5]{0:T(128)S(1)} %copy-done.18, bf16[512,512]{1,0:T(8,128)(2,1)S(1)} %shard_map.89.refs_1_, bf16[512,512]{1,0:T(8,128)(2,1)S(1)} %collective-permute-done.6.refs_2_, bf16[512,512]{1,0:T(8,128)(2,1)S(1)} %collective-permute-done.7.refs_3_, bf16[512,512]{1,0:T(8,128)(2,1)S(1)} %collective-permute-done.8.refs_4_, ...), custom_call_target="tpu_custom_call" | custom-call | flops 1000000 | bytes 1000000 | tf_op jit(solution)/shard_map/pallas_call | solution.py:59
  (72 shorter events, 28.6 us)
Async XLA Ops:
  6.5 97.4 %all-gather.2.cloned.1.call-start = ((), (), s32[]{:S(2)}) async-start(), calls=%async_computation.4 | async-start | bytes 1179648 | tf_op jit(solution)/shard_map/all_gather | solution.py:311
  7.3 9.6 %collective-permute-start = (bf16[32,512]{1,0:T(8,128)(2,1)S(1)}, bf16[32,512]{1,0:T(8,128)(2,1)S(1)}, u32[]{:S(2)}, u32[]{:S(2)}) collective-permute-start(bf16[32,512]{1,0:T(8,128)(2,1)S(1)} %constant_dynamic-slice_fusion), channel_id=1, source_target_pairs={{0,4},{4,0},{1,5},{5,1},{2,6},{6,2},{3,7},{7,3},{8,12},{12,8},{9,1... | collective-permute-start | bytes 98312 | tf_op jit(solution)/shard_map/ppermute | solution.py:21
  17.7 5.1 %collective-permute-start.1 = (bf16[64,512]{1,0:T(8,128)(2,1)S(1)}, bf16[64,512]{1,0:T(8,128)(2,1)S(1)}, u32[]{:S(2)}, u32[]{:S(2)}) collective-permute-start(bf16[64,512]{1,0:T(8,128)(2,1)S(1)} %pad_maximum_fusion.1), channel_id=1, source_target_pairs={{0,0},{1,128},{2,256},{3,384},{128,1},{129,129},{130,257},{131,385... | collective-permute-start | bytes 196616 | tf_op jit(solution)/shard_map/ppermute | solution.py:294
  19.1 12.2 %copy-start.18 = (s32[5]{0:T(128)S(1)}, s32[5]{0:T(128)}, u32[]{:S(2)}) copy-start(s32[5]{0:T(128)} %stack.32.refs_0_) | copy-start | bytes 64
  22.8 8.4 %collective-permute-start.2 = (bf16[1072,512]{1,0:T(8,128)(2,1)}, bf16[1072,512]{1,0:T(8,128)(2,1)S(1)}, u32[]{:S(2)}, u32[]{:S(2)}) collective-permute-start(bf16[1072,512]{1,0:T(8,128)(2,1)} %get-tuple-element.26), channel_id=1, source_target_pairs={{0,4},{4,0},{1,5},{5,1},{2,6},{6,2},{3,7},{7,3},{8,12},{12,8},{9,1... | collective-permute-start | bytes 3293192 | tf_op jit(solution)/shard_map/ppermute | solution.py:21
  25.1 5.4 %collective-permute-start.9 = (bf16[64,512]{1,0:T(8,128)(2,1)S(1)}, bf16[64,512]{1,0:T(8,128)(2,1)S(1)}, u32[]{:S(2)}, u32[]{:S(2)}) collective-permute-start(bf16[64,512]{1,0:T(8,128)(2,1)S(1)} %collective-permute-done.1), channel_id=1, source_target_pairs={{0,8},{8,0},{1,9},{9,1},{2,10},{10,2},{3,11},{11,3},{4,12},{12,4},... | collective-permute-start | bytes 196616 | tf_op jit(solution)/shard_map/ppermute | solution.py:309
  34.3 9.4 %copy-start.12 = (bf16[4,128,128]{2,1,0:T(8,128)(2,1)}, bf16[4,128,128]{2,1,0:T(8,128)(2,1)S(1)}, u32[]{:S(2)}) copy-start(bf16[4,128,128]{2,1,0:T(8,128)(2,1)S(1)} %get-tuple-element.27.refs_3_) | copy-start | bytes 393220
  34.3 52.8 %copy-start.1 = (bf16[1072,512]{1,0:T(8,128)(2,1)S(1)}, bf16[1072,512]{1,0:T(8,128)(2,1)}, u32[]{:S(2)}) copy-start(bf16[1072,512]{1,0:T(8,128)(2,1)} %get-tuple-element.24.refs_1_) | copy-start | bytes 3293188
  44.3 30.6 %all-to-all-start.1 = ((bf16[4,144,128]{2,1,0:T(8,128)(2,1)}), bf16[4,144,128]{2,1,0:T(8,128)(2,1)S(1)}, u32[]{:S(2)}, u32[]{:S(2)}) async-start(bf16[4,144,128]{2,1,0:T(8,128)(2,1)} %get-tuple-element.37), calls=%async_computation.1 | async-start | bytes 294912 | tf_op jit(solution)/shard_map/all_to_all | solution.py:318
  54.0 13.1 %collective-permute-start.3 = (bf16[144,256]{1,0:T(8,128)(2,1)S(1)}, bf16[144,256]{1,0:T(8,128)(2,1)S(1)}, u32[]{:S(2)}, u32[]{:S(2)}) collective-permute-start(bf16[144,256]{1,0:T(8,128)(2,1)S(1)} %get-tuple-element.32), channel_id=1, source_target_pairs={{0,8},{8,0},{16,24},{24,16},{1,9},{9,1},{17,25},{25,17},{2,10},{10... | collective-permute-start | bytes 221192 | tf_op jit(solution)/shard_map/ppermute | solution.py:320
  56.3 11.1 %collective-permute-start.4 = (bf16[144,256]{1,0:T(8,128)(2,1)S(1)}, bf16[144,256]{1,0:T(8,128)(2,1)S(1)}, u32[]{:S(2)}, u32[]{:S(2)}) collective-permute-start(bf16[144,256]{1,0:T(8,128)(2,1)S(1)} %get-tuple-element.33), channel_id=1, source_target_pairs={{0,16},{8,24},{16,0},{24,8},{1,17},{9,25},{17,1},{25,9},{2,18},{10... | collective-permute-start | bytes 221192 | tf_op jit(solution)/shard_map/ppermute | solution.py:320
  59.2 15.7 %collective-permute-start.5 = (bf16[144,256]{1,0:T(8,128)(2,1)S(1)}, bf16[144,256]{1,0:T(8,128)(2,1)S(1)}, u32[]{:S(2)}, u32[]{:S(2)}) collective-permute-start(bf16[144,256]{1,0:T(8,128)(2,1)S(1)} %get-tuple-element.34), channel_id=1, source_target_pairs={{0,24},{8,16},{16,8},{24,0},{1,25},{9,17},{17,9},{25,1},{2,26},{10... | collective-permute-start | bytes 221192 | tf_op jit(solution)/shard_map/ppermute | solution.py:320
  74.9 12.2 %copy-start.6 = (bf16[144,256]{1,0:T(8,128)(2,1)}, bf16[144,256]{1,0:T(8,128)(2,1)S(1)}, u32[]{:S(2)}) copy-start(bf16[144,256]{1,0:T(8,128)(2,1)S(1)} %collective-permute-done.5.refs_8_.refs_4_) | copy-start | bytes 221188
  76.8 16.3 %all-to-all-start.2 = ((bf16[4,144,128]{2,1,0:T(8,128)(2,1)}), bf16[4,144,128]{2,1,0:T(8,128)(2,1)S(1)}, u32[]{:S(2)}, u32[]{:S(2)}) async-start(bf16[4,144,128]{2,1,0:T(8,128)(2,1)} %get-tuple-element.38), calls=%async_computation.2 | async-start | bytes 294912 | tf_op jit(solution)/shard_map/all_to_all | solution.py:331
  95.3 20.1 %all-to-all-start.3 = ((bf16[4,128,512]{2,1,0:T(8,128)(2,1)}), bf16[4,128,512]{2,1,0:T(8,128)(2,1)}, u32[]{:S(2)}, u32[]{:S(2)}) async-start(bf16[4,128,512]{2,1,0:T(8,128)(2,1)} %copy-done.3), calls=%async_computation.3 | async-start | bytes 1048576 | tf_op jit(solution)/shard_map/all_to_all | solution.py:335
  100.5 14.8 %copy-start.19 = (bf16[1024]{0:T(1024)(128)(2,1)S(1)}, bf16[1024]{0:T(1024)(128)(2,1)}, u32[]{:S(2)}) copy-start(bf16[1024]{0:T(1024)(128)(2,1)} %param.14) | copy-start | bytes 6148
  103.9 26.0 %collective-permute-start.12 = (bf16[16,64,512]{2,1,0:T(8,128)(2,1)}, bf16[16,64,512]{2,1,0:T(8,128)(2,1)S(1)}, u32[]{:S(2)}, u32[]{:S(2)}) collective-permute-start(bf16[16,64,512]{2,1,0:T(8,128)(2,1)} %all-gather.2.cloned.1.call-done.refs_5_), channel_id=1, source_target_pairs={{0,256},{128,384},{256,0},{384,128},{1,257},{129,385},{257,1},{385... | collective-permute-start | bytes 3145736 | tf_op jit(solution)/shard_map/ppermute | solution.py:282
  108.8 46.4 %collective-permute-start.11 = (bf16[16,64,512]{2,1,0:T(8,128)(2,1)}, bf16[16,64,512]{2,1,0:T(8,128)(2,1)}, u32[]{:S(2)}, u32[]{:S(2)}) collective-permute-start(bf16[16,64,512]{2,1,0:T(8,128)(2,1)} %all-gather.2.cloned.1.call-done.refs_5_), channel_id=1, source_target_pairs={{0,128},{128,256},{256,384},{384,0},{1,129},{129,257},{257,385},{3... | collective-permute-start | bytes 3145736 | tf_op jit(solution)/shard_map/ppermute | solution.py:282
  111.0 44.2 %collective-permute-start.10 = (bf16[16,64,512]{2,1,0:T(8,128)(2,1)}, bf16[16,64,512]{2,1,0:T(8,128)(2,1)}, u32[]{:S(2)}, u32[]{:S(2)}) collective-permute-start(bf16[16,64,512]{2,1,0:T(8,128)(2,1)} %all-gather.2.cloned.1.call-done.refs_5_), channel_id=1, source_target_pairs={{0,384},{128,0},{256,128},{384,256},{1,385},{129,1},{257,129},{385... | collective-permute-start | bytes 3145736 | tf_op jit(solution)/shard_map/ppermute | solution.py:282
  117.5 37.7 %copy-start.2 = (bf16[16,64,512]{2,1,0:T(8,128)(2,1)S(1)}, bf16[16,64,512]{2,1,0:T(8,128)(2,1)}, u32[]{:S(2)}) copy-start(bf16[16,64,512]{2,1,0:T(8,128)(2,1)} %all-gather.2.cloned.1.call-done.refs_5_) | copy-start | bytes 3145732
  120.6 34.6 %collective-permute-start.8 = (bf16[512,512]{1,0:T(8,128)(2,1)S(1)}, bf16[512,512]{1,0:T(8,128)(2,1)S(1)}, u32[]{:S(2)}, u32[]{:S(2)}) collective-permute-start(bf16[512,512]{1,0:T(8,128)(2,1)S(1)} %shard_map.89.refs_1_), channel_id=1, source_target_pairs={{0,3},{1,0},{2,1},{3,2},{4,7},{5,4},{6,5},{7,6},{8,11},{9,8},{10,9... | collective-permute-start | bytes 1572872 | tf_op jit(solution)/shard_map/ppermute | solution.py:282
  124.6 30.6 %collective-permute-start.7 = (bf16[512,512]{1,0:T(8,128)(2,1)S(1)}, bf16[512,512]{1,0:T(8,128)(2,1)S(1)}, u32[]{:S(2)}, u32[]{:S(2)}) collective-permute-start(bf16[512,512]{1,0:T(8,128)(2,1)S(1)} %shard_map.89.refs_1_), channel_id=1, source_target_pairs={{0,2},{1,3},{2,0},{3,1},{4,6},{5,7},{6,4},{7,5},{8,10},{9,11},{10,... | collective-permute-start | bytes 1572872 | tf_op jit(solution)/shard_map/ppermute | solution.py:282
  129.9 25.3 %collective-permute-start.6 = (bf16[512,512]{1,0:T(8,128)(2,1)S(1)}, bf16[512,512]{1,0:T(8,128)(2,1)S(1)}, u32[]{:S(2)}, u32[]{:S(2)}) collective-permute-start(bf16[512,512]{1,0:T(8,128)(2,1)S(1)} %shard_map.89.refs_1_), channel_id=1, source_target_pairs={{0,1},{1,2},{2,3},{3,0},{4,5},{5,6},{6,7},{7,4},{8,9},{9,10},{10,1... | collective-permute-start | bytes 1572872 | tf_op jit(solution)/shard_map/ppermute | solution.py:282
  158.6 6.0 %collective-permute-start.13 = (bf16[256,1024]{1,0:T(8,128)(2,1)S(1)}, bf16[256,1024]{1,0:T(8,128)(2,1)S(1)}, u32[]{:S(2)}, u32[]{:S(2)}) collective-permute-start(bf16[256,1024]{1,0:T(8,128)(2,1)S(1)} %shard_map.91), channel_id=1, source_target_pairs={{0,4},{4,0},{1,5},{5,1},{2,6},{6,2},{3,7},{7,3},{8,12},{12,8},{9,1... | collective-permute-start | bytes 1572872 | tf_op jit(solution)/shard_map/ppermute | solution.py:21
  (14 other events, 19.2 us)
Sparse Core Ops, SparseCore 0:
  31.4 60.7 all-gather.1

commit v14 on v8

--- a/solution.py
+++ b/solution.py
@@ -14,7 +14,7 @@
 NT = (((1,), (1,)), ((), ()))
 TN = (((0,), (0,)), ((), ()))
 LOGS = 1024
-ROWS = 1104
+ROWS = 1072
 
 
 def swap(value):
@@ -68,7 +68,7 @@
 
 
 def pack_body(
-    at, keys, values, queries, gates, weight, decay, mix, keep, send, small, levels, sems
+    at, keys, values, queries, gates, decay, mix, keep, send, small, levels, sems
 ):
     core = at[0]
     mine = pl.ds(pl.multiple_of(core * 512, 512), 512)
@@ -77,9 +77,9 @@
         pltpu.make_async_copy(decay, small, sems.at[0]),
         pltpu.make_async_copy(mix, levels, sems.at[1]),
     ]
-    for i, ref in enumerate((keys, values, queries, gates, weight)):
-        rows = pl.ds(i * 256, 256) if i < 4 else pl.ds(LOGS + 48, 32)
-        for out, cols, n in ((send, theirs, 2), (keep, mine, 7)):
+    for i, ref in enumerate((keys, values, queries, gates)):
+        rows = pl.ds(i * 256, 256)
+        for out, cols, n in ((send, theirs, 2), (keep, mine, 6)):
             copies.append(pltpu.make_async_copy(ref.at[:, cols], out.at[rows, :], sems.at[n + i]))
     for copy in copies:
         copy.start()
@@ -152,6 +152,16 @@
     send_whole(*blocks_of(near), pay)
 
 
+def pair_body(at, own, other, pay):
+    odd = at[1] % 2 == 1
+    for h in range(4):
+        s = [ref[h, 0:128, :].astype(F32) for ref in (own, other)]
+        t = [untail(ref[h, 128:144, :]) for ref in (own, other)]
+        scales = (jnp.where(odd, 0.0, t[1]), jnp.where(odd, t[0], 0.0))
+        pay[h, 0:128, :] = (s[0] * jnp.exp(scales[0]) + s[1] * jnp.exp(scales[1])).astype(BF)
+        pay[h, 128:144, :] = tail(t[0] + t[1])
+
+
 def far_body(at, far, pay, states, before_out):
     s, t, pair = blocks_of(far)
     send_whole(s, t, pair, pay)
@@ -161,20 +171,14 @@
     before_out[...] = jnp.broadcast_to(before, (8, 128))
 
 
-def last_body(at, last, before, near, far, message):
-    one, two, _ = lower_states(*blocks_of(last), at[3])
+def last_body(at, rows, before, far, message):
+    one, two, _ = lower_states(*blocks_of(rows), at[3])
     earlier = jnp.exp(before[0:1, :])
-    later = [state.astype(BF) for state in (one * earlier, two * earlier)]
-    s, t, pair = blocks_of(near)
+    one, two = (one * earlier).astype(BF), (two * earlier).astype(BF)
     for i in range(4):
-        one, two, before_near = lower_states(s, t, pair, jnp.int32(i))
-        message[i, 0:128, 0:128] = one.astype(BF)
-        message[i, 0:128, 128:256] = two.astype(BF)
-        message[i, 0:128, 256:512] = far[...]
-        message[i, 0:128, 512:640] = later[0]
-        message[i, 0:128, 640:768] = later[1]
-        message[i, 128:144, 0:128] = tail(before_near)
-        message[i, 128:144, 128:768] = jnp.zeros((16, 640), BF)
+        message[i, :, 0:256] = far[...]
+        message[i, :, 256:384] = one
+        message[i, :, 384:512] = two
 
 
 def place(s, core):
@@ -213,22 +217,36 @@
                 coef[here, 6 * h + l - 2 : 6 * h + l - 1] = start * m[l]
 
 
+def mix_body(at, keep, got, mixture, coef, other, pair, mixed, later):
+    odd, upper = at[1] % 2 == 1, at[1] >= 2
+    for h in range(4):
+        step = jnp.where(odd, untail(other[h, 128:144, :]), 0.0)
+        one = jnp.where(odd, other[h, 0:128, :].astype(F32), 0.0).astype(BF)
+        two = jnp.where(upper, pair[h, 0:128, :].astype(F32) * jnp.exp(step), 0.0).astype(BF)
+        before = jnp.exp(step + jnp.where(upper, untail(pair[h, 128:144, :]), 0.0))[:, 0:1]
+        states = jnp.concatenate([one, two], axis=1)
+        hc = slice(h * 128, h * 128 + 128)
+        for s, ref in enumerate((keep, got)):
+            _, here = place(s, at[0])
+            read = dot(ref[512:768, hc], states)
+            total = mixture[here, hc] + read[:, 0:128] * coef[here, 6 * h : 6 * h + 1]
+            mixed[here, hc] = total + read[:, 128:256] * coef[here, 6 * h + 1 : 6 * h + 2]
+            later[here, 4 * h : 4 * h + 4] = coef[here, 6 * h + 2 : 6 * h + 6] * before
+
+
 def norm_body(at, keep, got, gain, mixture, coef, states, normed):
     core = at[0]
     for h in range(4):
         mine = pl.ds(pl.multiple_of(core * 512 + h * 128, 128), 128)
         hc = slice(h * 128, h * 128 + 128)
-        before = jnp.exp(untail(states[h, 128:144, 0:128])[:, 0:1])
         for s, ref in enumerate((keep, got)):
             _, here = place(s, core)
             z = ref[768:1024, hc].astype(F32)
             total = mixture[here, hc]
-            for l in range(6):
-                if l % 2 == 0:
-                    read = dot(ref[512:768, hc], states[h, 0:128, l * 128 : l * 128 + 256])
-                scale = coef[here, 6 * h + l : 6 * h + l + 1]
-                scale = scale if l < 2 else scale * before
-                total += read[:, (l % 2) * 128 : (l % 2) * 128 + 128] * scale
+            for l in range(0, 4, 2):
+                read = dot(ref[512:768, hc], states[h, :, l * 128 : l * 128 + 256])
+                total += read[:, 0:128] * coef[here, 4 * h + l : 4 * h + l + 1]
+                total += read[:, 128:256] * coef[here, 4 * h + l + 1 : 4 * h + l + 2]
             gated = total * (z / (1.0 + jnp.exp(-z)))
             size = lax.rsqrt(jnp.mean(gated * gated, axis=1, keepdims=True) + 1e-05)
             normed[here, hc] = (gated * size * gain[:, mine].astype(F32)).astype(BF)
@@ -282,51 +300,59 @@
 def shards(values, keys, queries, gates, log_decay, level_mix, norm_gain, weight):
     y, a, b, c, x = (lax.axis_index(n) for n in ("y", "a", NEAR, "c", "x"))
     at = jnp.stack([c, b, a, y, x]).astype(jnp.int32)
+    kept = lax.dynamic_slice_in_dim(weight, c * 512, 512, 1)
+    theirs = swap(lax.dynamic_slice_in_dim(weight, (1 - c) * 512, 512, 1))
+    both = jnp.concatenate(
+        [jnp.where(c == 0, kept, theirs), jnp.where(c == 0, theirs, kept)]
+    )
+    mine = []
+    for k in range(4):
+        perm = [(s * 4 + f, ((f + k) % 4) * 4 + s) for s in range(4) for f in range(4)]
+        mine.append(lax.ppermute(both, ("y", "x"), perm))
     block = ((ROWS, 512), BF)
     keep, send = call(
         pack_body,
         [block, block],
-        (at, keys, values, queries, gates, weight, log_decay, level_mix),
+        (at, keys, values, queries, gates, log_decay, level_mix),
         scratch=[
             pltpu.VMEM((8, 256), F32),
             pltpu.VMEM((8, 8, 256), F32),
-            pltpu.SemaphoreType.DMA((12,)),
+            pltpu.SemaphoreType.DMA((10,)),
         ],
-        hbm=range(1, 8),
+        hbm=range(1, 7),
         vmem=60,
     )
+    mine, send = lax.optimization_barrier((mine, send))
+    gathered = lax.all_gather(jnp.concatenate(mine, axis=1), ("a", "p", "q"))
+
     got = swap(send)
     pay = ((4, 144, 128), BF)
     pay_b, first = call(ends_body, [pay, ((4, 128, 128), BF)], (at, keep, got))
-
-    kept, theirs = keep[LOGS + 48 :], got[LOGS + 48 :]
-    both = jnp.concatenate(
-        [jnp.where(c == 0, kept, theirs), jnp.where(c == 0, theirs, kept)]
-    )
-    both, pay_b = lax.optimization_barrier((both, pay_b))
-    mine = []
-    for k in range(4):
-        perm = [(s * 4 + f, ((f + k) % 4) * 4 + s) for s in range(4) for f in range(4)]
-        mine.append(lax.ppermute(both, ("y", "x"), perm))
-    gathered = lax.all_gather(jnp.concatenate(mine, axis=1), ("a", "p", "q"))
-
     near = lax.all_to_all(pay_b, NEAR, 0, 0, tiled=True)
-    (pay_a,) = call(near_body, [pay], (at, near))
+    other = lax.ppermute(pay_b, NEAR, [(i, i ^ 1) for i in range(4)])
+    (pay_a,) = call(near_body, [pay], (at, near), unread=(other,))
     far = lax.all_to_all(pay_a, "a", 0, 0, tiled=True)
-    mixture, coef = call(
-        own_body, [((512, 512), F32), ((512, 24), F32)], (at, keep, got, first)
-    )
+    (pair,) = call(pair_body, [pay], (at, pay_b, other))
+    pair = lax.ppermute(pair, NEAR, [(i, i ^ 2) for i in range(4)])
     pay_y, far, before = call(
         far_body,
         [pay, ((128, 256), BF), ((8, 128), F32)],
         (at, far),
-        unread=(mixture,),
-    )
-    last = lax.all_to_all(pay_y, "y", 0, 0, tiled=True)
-    (last,) = call(last_body, [((4, 144, 768), BF)], (at, last, before, near, far))
-    last = lax.all_to_all(last, NEAR, 0, 0, tiled=True)
+        unread=(pair,),
+    )
+    rows = lax.all_to_all(pay_y, "y", 0, 0, tiled=True)
+    (states,) = call(last_body, [((4, 128, 512), BF)], (at, rows, before, far))
+    states = lax.all_to_all(states, NEAR, 0, 0, tiled=True)
+    mixture, coef = call(
+        own_body, [((512, 512), F32), ((512, 24), F32)], (at, keep, got, first)
+    )
+    mixture, coef = call(
+        mix_body,
+        [((512, 512), F32), ((512, 16), F32)],
+        (at, keep, got, mixture, coef, other, pair),
+    )
     (normed,) = call(
-        norm_body, [((512, 512), BF)], (at, keep, got, norm_gain[None], mixture, coef, last)
+        norm_body, [((512, 512), BF)], (at, keep, got, norm_gain[None], mixture, coef, states)
     )
 
     blocks = [normed] + [shift(normed, "x", j) for j in (1, 2, 3)]

time: 186 us -> 181 us (0.973)
  starting transfers between devices: 46.8 us -> 69.4 us
  blocking collectives: 26.6 us -> 7.87 us
  waiting for transfers between devices: 60.8 us -> 53.6 us
  local copies, waits for them, and re-layouts: 11.5 us -> 7.03 us
  Pallas kernels: 23.1 us -> 25.2 us
    ppermute x0 -> x2, waiting for transfers between devices: none -> 21.3 us  [the longest x1 14.3 us: shards(): pair = lax.ppermute(pair, NEAR, [(i, i ^ 2) for i in range(4)])]
    all_to_all x1 -> x2, waiting for transfers between devices: 28.8 us -> 9.82 us  [the longest x1 9.82 us: shards(): states = lax.all_to_all(states, NEAR, 0, 0, tiled=True)]
    all_to_all x2 -> x1, blocking collectives: 26.6 us -> 7.87 us  [shards(): rows = lax.all_to_all(pay_y, 'y', 0, 0, tiled=True)]
    ppermute x0 -> x2, starting transfers between devices: none -> 9.05 us  [the longest x1 5.69 us: shards(): pair = lax.ppermute(pair, NEAR, [(i, i ^ 2) for i in range(4)])]
    all_to_all x1, waiting for transfers between devices: 7.08 us -> 0.01 us  [shards(): far = lax.all_to_all(pay_a, 'a', 0, 0, tiled=True)]
    all_to_all x1 -> x2, starting transfers between devices: 3.63 us -> 9.08 us  [the longest x1 5.61 us: shards(): near = lax.all_to_all(pay_b, NEAR, 0, 0, tiled=True)]
    unnamed x28 -> x14, local copies, waits for them, and re-layouts: 10.9 us -> 5.69 us
    ppermute x4, waiting for transfers between devices: 3.94 us -> 0.01 us  [shards(): mine.append(lax.ppermute(both, ('y', 'x'), perm))]
  transfers between devices with their start and end apart: 12 -> 16, of which waited for: 8 -> 8; matrix products, arithmetic and copies ran while one was open for 0% -> 0% of each run, Pallas kernels for 8% -> 12%
where the time goes in v14:
time: 181 us; the launch traced here: 179 us
  starting transfers between devices  69.4 us (38%)
  waiting for transfers between devices  53.6 us (30%)
  Pallas kernels  25.2 us (14%)
  between operations  13.7 us (8%)
  blocking collectives  7.87 us (4%)
  local copies, waits for them, and re-layouts  7.03 us (4%)
  other arithmetic  2.46 us (1%)
    pallas_call x9, Pallas kernels, call(): pl.pallas_call(run, out_shape=[jax.ShapeDtypeStruct(*o) for o in outs], i...  19.1 us
    ppermute x3, waiting for transfers between devices, shift(): return lax.ppermute(value, axis, [(i, (i + by) % 4) for i in range(4)])  19.1 us
    ppermute x3, starting transfers between devices, swap(): return lax.ppermute(value, 'c', [(0, 1), (1, 0)])  17 us
    all_to_all x1, starting transfers between devices, shards(): far = lax.all_to_all(pay_a, 'a', 0, 0, tiled=True)  14.3 us
    ppermute x1, waiting for transfers between devices, shards(): pair = lax.ppermute(pair, NEAR, [(i, i ^ 2) for i in range(4)])  14.3 us
    ppermute x4, starting transfers between devices, shards(): mine.append(lax.ppermute(both, ('y', 'x'), perm))  11 us
    all_to_all x1, waiting for transfers between devices, shards(): states = lax.all_to_all(states, NEAR, 0, 0, tiled=True)  9.82 us
    ppermute x3, starting transfers between devices, shift(): return lax.ppermute(value, axis, [(i, (i + by) % 4) for i in range(4)])  8.99 us
  transfers between devices with their start and end apart: 16, of which 8 were waited for; matrix products, arithmetic and copies ran while one was open for 0% of the time, Pallas kernels for 12%

profile of v14, /device:TPU:1, one launch (start us, length us, event | category | flops | bytes accessed | tf_op | source)
XLA Modules:
  0.0 179.2 jit_solution(17375267977448236244)
XLA Ops:
  7.3 8.8 %collective-permute-start = (bf16[32,512]{1,0:T(8,128)(2,1)S(1)}, bf16[32,512]{1,0:T(8,128)(2,1)S(1)}, u32[]{:S(2)}, u32[]{:S(2)}) collective-permute-start(bf16[32,512]{1,0:T(8,128)(2,1)S(1)} %constant_dynamic-slice_fusion), channel_id=1, source_target_pairs={{0,4},{4,0},{1,5},{5,1},{2,6},{6,2},{3,7},{7,3},{8,12},{12,8},{9,1... | collective-permute-start | bytes 98312 | tf_op jit(solution)/shard_map/ppermute | solution.py:21
  20.3 4.6 %collective-permute-start.3 = (bf16[64,512]{1,0:T(8,128)(2,1)S(1)}, bf16[64,512]{1,0:T(8,128)(2,1)S(1)}, u32[]{:S(2)}, u32[]{:S(2)}) collective-permute-start(bf16[64,512]{1,0:T(8,128)(2,1)S(1)} %pad_maximum_fusion.1), channel_id=1, source_target_pairs={{0,256},{1,384},{2,0},{3,128},{128,257},{129,385},{130,1},{131,129... | collective-permute-start | bytes 196616 | tf_op jit(solution)/shard_map/ppermute | solution.py:311
  24.9 3.9 %collective-permute-start.4 = (bf16[64,512]{1,0:T(8,128)(2,1)S(1)}, bf16[64,512]{1,0:T(8,128)(2,1)S(1)}, u32[]{:S(2)}, u32[]{:S(2)}) collective-permute-start(bf16[64,512]{1,0:T(8,128)(2,1)S(1)} %pad_maximum_fusion.1), channel_id=1, source_target_pairs={{0,384},{1,0},{2,128},{3,256},{128,385},{129,1},{130,129},{131,257... | collective-permute-start | bytes 196616 | tf_op jit(solution)/shard_map/ppermute | solution.py:311
  29.3 3.9 %shard_map.82 = (bf16[1072,512]{1,0:T(8,128)(2,1)}, bf16[1072,512]{1,0:T(8,128)(2,1)}) custom-call(s32[5]{0:T(128)} %stack.23.refs_0_.at, bf16[256,1024]{1,0:T(8,128)(2,1)} %refs_1_.1, bf16[256,1024]{1,0:T(8,128)(2,1)} %refs_2_.1, bf16[256,1024]{1,0:T(8,128)(2,1)} %refs_3_.1, bf16[256,1024]{1,0:T(8,128)(2,1)} %refs_4_.1, f32[8,256]{1,0:T(8,128)} %refs_5_.1, ...), custom_call_target="tpu_custom_call" | custom-call | flops 1000000 | bytes 1000000 | tf_op jit(solution)/shard_map/pallas_call | solution.py:59
  34.0 3.2 %collective-permute-start.5 = (bf16[1072,512]{1,0:T(8,128)(2,1)}, bf16[1072,512]{1,0:T(8,128)(2,1)S(1)}, u32[]{:S(2)}, u32[]{:S(2)}) collective-permute-start(bf16[1072,512]{1,0:T(8,128)(2,1)} %get-tuple-element.23), channel_id=1, source_target_pairs={{0,4},{4,0},{1,5},{5,1},{2,6},{6,2},{3,7},{7,3},{8,12},{12,8},{9,1... | collective-permute-start | bytes 3293192 | tf_op jit(solution)/shard_map/ppermute | solution.py:21
  37.2 2.5 %collective-permute-done.5.refs_2_ = bf16[1072,512]{1,0:T(8,128)(2,1)S(1)} collective-permute-done((bf16[1072,512]{1,0:T(8,128)(2,1)}, bf16[1072,512]{1,0:T(8,128)(2,1)S(1)}, u32[]{:S(2)}, u32[]{:S(2)}) %collective-permute-start.5) | collective-permute-done | bytes 1097760 | tf_op jit(solution)/shard_map/ppermute | solution.py:21
  43.4 5.6 %all-to-all-start = ((bf16[4,144,128]{2,1,0:T(8,128)(2,1)}), bf16[4,144,128]{2,1,0:T(8,128)(2,1)S(1)}, u32[]{:S(2)}, u32[]{:S(2)}) async-start(bf16[4,144,128]{2,1,0:T(8,128)(2,1)} %get-tuple-element.27.refs_1_), calls=%async_computation | async-start | bytes 294912 | tf_op jit(solution)/shard_map/all_to_all | solution.py:331
  49.0 3.4 %collective-permute-start.6 = (bf16[4,144,128]{2,1,0:T(8,128)(2,1)}, bf16[4,144,128]{2,1,0:T(8,128)(2,1)S(1)}, u32[]{:S(2)}, u32[]{:S(2)}) collective-permute-start(bf16[4,144,128]{2,1,0:T(8,128)(2,1)} %get-tuple-element.27.refs_1_), channel_id=1, source_target_pairs={{0,8},{8,0},{16,24},{24,16},{1,9},{9,1},{17,25},{25,17},{2,10},{10... | collective-permute-start | bytes 442376 | tf_op jit(solution)/shard_map/ppermute | solution.py:332
  52.4 7.0 %collective-permute-done.6.refs_2_.refs_5_ = bf16[4,144,128]{2,1,0:T(8,128)(2,1)S(1)} collective-permute-done((bf16[4,144,128]{2,1,0:T(8,128)(2,1)}, bf16[4,144,128]{2,1,0:T(8,128)(2,1)S(1)}, u32[]{:S(2)}, u32[]{:S(2)}) %collective-permute-start.6) | collective-permute-done | bytes 147488 | tf_op jit(solution)/shard_map/ppermute | solution.py:332
  60.7 14.3 %all-to-all-start.1 = ((bf16[4,144,128]{2,1,0:T(8,128)(2,1)}), bf16[4,144,128]{2,1,0:T(8,128)(2,1)S(1)}, u32[]{:S(2)}, u32[]{:S(2)}) async-start(bf16[4,144,128]{2,1,0:T(8,128)(2,1)} %shard_map.87), calls=%async_computation.1 | async-start | bytes 294912 | tf_op jit(solution)/shard_map/all_to_all | solution.py:334
  76.0 5.7 %collective-permute-start.7 = (bf16[4,144,128]{2,1,0:T(8,128)(2,1)S(1)}, bf16[4,144,128]{2,1,0:T(8,128)(2,1)S(1)}, u32[]{:S(2)}, u32[]{:S(2)}) collective-permute-start(bf16[4,144,128]{2,1,0:T(8,128)(2,1)S(1)} %shard_map.85), channel_id=1, source_target_pairs={{0,16},{8,24},{16,0},{24,8},{1,17},{9,25},{17,1},{25,9},{2,18},{10... | collective-permute-start | bytes 442376 | tf_op jit(solution)/shard_map/ppermute | solution.py:336
  81.7 14.3 %collective-permute-done.7.refs_6_.refs_2_ = bf16[4,144,128]{2,1,0:T(8,128)(2,1)S(1)} collective-permute-done((bf16[4,144,128]{2,1,0:T(8,128)(2,1)S(1)}, bf16[4,144,128]{2,1,0:T(8,128)(2,1)S(1)}, u32[]{:S(2)}, u32[]{:S(2)}) %collective-permute-start.7) | collective-permute-done | bytes 147488 | tf_op jit(solution)/shard_map/ppermute | solution.py:336
  96.6 7.9 %all_to_all.20.refs_1_ = bf16[4,144,128]{2,1,0:T(8,128)(2,1)S(1)} all-to-all(bf16[4,144,128]{2,1,0:T(8,128)(2,1)S(1)} %get-tuple-element.30), channel_id=1, replica_groups=mesh['y'=4,'a'=4,'p'=2,'q'=2,'c'=2,'x'=4] {'y'}, dimensions={0} | all-to-all | bytes 294912 | tf_op jit(solution)/shard_map/all_to_all | solution.py:343
  105.8 3.5 %all-to-all-start.3 = ((bf16[4,128,512]{2,1,0:T(8,128)(2,1)}), bf16[4,128,512]{2,1,0:T(8,128)(2,1)S(1)}, u32[]{:S(2)}, u32[]{:S(2)}) async-start(bf16[4,128,512]{2,1,0:T(8,128)(2,1)} %shard_map.89), calls=%async_computation.3 | async-start | bytes 1048576 | tf_op jit(solution)/shard_map/all_to_all | solution.py:345
  109.4 4.3 %shard_map.84 = (f32[512,512]{1,0:T(8,128)S(1)}, f32[512,24]{1,0:T(8,128)S(1)}) custom-call(s32[5]{0:T(128)S(1)} %copy-done.5, bf16[1072,512]{1,0:T(8,128)(2,1)S(1)} %copy-done.1, bf16[1072,512]{1,0:T(8,128)(2,1)S(1)} %collective-permute-done.5.refs_2_, bf16[4,128,128]{2,1,0:T(8,128)(2,1)S(1)} %get-tuple-element.24.refs_3_), custom_call_target="tpu_custom_call" | custom-call | flops 1000000 | bytes 1000000 | tf_op jit(solution)/shard_map/pallas_call | solution.py:59
  116.4 9.8 %all-to-all-done.3.refs_6_ = bf16[4,128,512]{2,1,0:T(8,128)(2,1)S(1)} async-done(((bf16[4,128,512]{2,1,0:T(8,128)(2,1)}), bf16[4,128,512]{2,1,0:T(8,128)(2,1)S(1)}, u32[]{:S(2)}, u32[]{:S(2)}) %all-to-all-start.3) | async-done | bytes 524320 | tf_op jit(solution)/shard_map/all_to_all | solution.py:345
  130.0 2.8 %collective-permute-start.8 = (bf16[512,512]{1,0:T(8,128)(2,1)S(1)}, bf16[512,512]{1,0:T(8,128)(2,1)S(1)}, u32[]{:S(2)}, u32[]{:S(2)}) collective-permute-start(bf16[512,512]{1,0:T(8,128)(2,1)S(1)} %shard_map.90.b0), channel_id=1, source_target_pairs={{0,1},{1,2},{2,3},{3,0},{4,5},{5,6},{6,7},{7,4},{8,9},{9,10},{10,1... | collective-permute-start | bytes 1572872 | tf_op jit(solution)/shard_map/ppermute | solution.py:297
  132.8 2.7 %collective-permute-start.9 = (bf16[512,512]{1,0:T(8,128)(2,1)S(1)}, bf16[512,512]{1,0:T(8,128)(2,1)S(1)}, u32[]{:S(2)}, u32[]{:S(2)}) collective-permute-start(bf16[512,512]{1,0:T(8,128)(2,1)S(1)} %shard_map.90.b0), channel_id=1, source_target_pairs={{0,2},{1,3},{2,0},{3,1},{4,6},{5,7},{6,4},{7,5},{8,10},{9,11},{10,... | collective-permute-start | bytes 1572872 | tf_op jit(solution)/shard_map/ppermute | solution.py:297
  135.5 3.5 %collective-permute-start.10 = (bf16[512,512]{1,0:T(8,128)(2,1)S(1)}, bf16[512,512]{1,0:T(8,128)(2,1)S(1)}, u32[]{:S(2)}, u32[]{:S(2)}) collective-permute-start(bf16[512,512]{1,0:T(8,128)(2,1)S(1)} %shard_map.90.b0), channel_id=1, source_target_pairs={{0,3},{1,0},{2,1},{3,2},{4,7},{5,4},{6,5},{7,6},{8,11},{9,8},{10,9... | collective-permute-start | bytes 1572872 | tf_op jit(solution)/shard_map/ppermute | solution.py:297
  141.4 11.1 %collective-permute-done.9.b2 = bf16[512,512]{1,0:T(8,128)(2,1)S(1)} collective-permute-done((bf16[512,512]{1,0:T(8,128)(2,1)S(1)}, bf16[512,512]{1,0:T(8,128)(2,1)S(1)}, u32[]{:S(2)}, u32[]{:S(2)}) %collective-permute-start.9) | collective-permute-done | bytes 524320 | tf_op jit(solution)/shard_map/ppermute | solution.py:297
  152.5 5.6 %collective-permute-done.10.b3 = bf16[512,512]{1,0:T(8,128)(2,1)S(1)} collective-permute-done((bf16[512,512]{1,0:T(8,128)(2,1)S(1)}, bf16[512,512]{1,0:T(8,128)(2,1)S(1)}, u32[]{:S(2)}, u32[]{:S(2)}) %collective-permute-start.10) | collective-permute-done | bytes 524320 | tf_op jit(solution)/shard_map/ppermute | solution.py:297
  160.3 3.0 %shard_map.92 = bf16[256,1024]{1,0:T(8,128)(2,1)S(1)} custom-call(s32[5]{0:T(128)S(1)} %copy-done.5, bf16[512,512]{1,0:T(8,128)(2,1)S(1)} %shard_map.90.b0, bf16[512,512]{1,0:T(8,128)(2,1)S(1)} %collective-permute-done.8.b1, bf16[512,512]{1,0:T(8,128)(2,1)S(1)} %collective-permute-done.9.b2, bf16[512,512]{1,0:T(8,128)(2,1)S(1)} %collective-permute-done.10.b3, ...), custom_call_target="tpu_custom_call" | custom-call | flops 1073741824 | bytes 6291456 | tf_op jit(solution)/shard_map/pallas_call | solution.py:278
  163.3 5.0 %collective-permute-start.11 = (bf16[256,1024]{1,0:T(8,128)(2,1)S(1)}, bf16[256,1024]{1,0:T(8,128)(2,1)S(1)}, u32[]{:S(2)}, u32[]{:S(2)}) collective-permute-start(bf16[256,1024]{1,0:T(8,128)(2,1)S(1)} %shard_map.92), channel_id=1, source_target_pairs={{0,4},{4,0},{1,5},{5,1},{2,6},{6,2},{3,7},{7,3},{8,12},{12,8},{9,1... | collective-permute-start | bytes 1572872 | tf_op jit(solution)/shard_map/ppermute | solution.py:21
  168.4 3.0 %shard_map.91 = f32[256,1024]{1,0:T(8,128)S(1)} custom-call(s32[5]{0:T(128)S(1)} %copy-done.5, bf16[512,512]{1,0:T(8,128)(2,1)S(1)} %shard_map.90.b0, bf16[512,512]{1,0:T(8,128)(2,1)S(1)} %collective-permute-done.8.b1, bf16[512,512]{1,0:T(8,128)(2,1)S(1)} %collective-permute-done.9.b2, bf16[512,512]{1,0:T(8,128)(2,1)S(1)} %collective-permute-done.10.b3, ...), custom_call_target="tpu_custom_call" | custom-call | flops 1073741824 | bytes 6291456 | tf_op jit(solution)/shard_map/pallas_call | solution.py:278
  (42 shorter events, 26.2 us)
Async XLA Ops:
  6.5 151.6 %all-gather.3.cloned.1.call-start = ((), (), s32[]{:S(2)}) async-start(), calls=%async_computation.4 | async-start | bytes 4456448 | tf_op jit(solution)/shard_map/all_gather | solution.py:326
  7.3 9.6 %collective-permute-start = (bf16[32,512]{1,0:T(8,128)(2,1)S(1)}, bf16[32,512]{1,0:T(8,128)(2,1)S(1)}, u32[]{:S(2)}, u32[]{:S(2)}) collective-permute-start(bf16[32,512]{1,0:T(8,128)(2,1)S(1)} %constant_dynamic-slice_fusion), channel_id=1, source_target_pairs={{0,4},{4,0},{1,5},{5,1},{2,6},{6,2},{3,7},{7,3},{8,12},{12,8},{9,1... | collective-permute-start | bytes 98312 | tf_op jit(solution)/shard_map/ppermute | solution.py:21
  17.7 15.5 %collective-permute-start.1 = (bf16[64,512]{1,0:T(8,128)(2,1)S(1)}, bf16[64,512]{1,0:T(8,128)(2,1)S(1)}, u32[]{:S(2)}, u32[]{:S(2)}) collective-permute-start(bf16[64,512]{1,0:T(8,128)(2,1)S(1)} %pad_maximum_fusion.1), channel_id=1, source_target_pairs={{0,0},{1,128},{2,256},{3,384},{128,1},{129,129},{130,257},{131,385... | collective-permute-start | bytes 196616 | tf_op jit(solution)/shard_map/ppermute | solution.py:311
  18.4 14.8 %collective-permute-start.2 = (bf16[64,512]{1,0:T(8,128)(2,1)S(1)}, bf16[64,512]{1,0:T(8,128)(2,1)S(1)}, u32[]{:S(2)}, u32[]{:S(2)}) collective-permute-start(bf16[64,512]{1,0:T(8,128)(2,1)S(1)} %pad_maximum_fusion.1), channel_id=1, source_target_pairs={{0,128},{1,256},{2,384},{3,0},{128,129},{129,257},{130,385},{131,1... | collective-permute-start | bytes 196616 | tf_op jit(solution)/shard_map/ppermute | solution.py:311
  20.3 12.9 %collective-permute-start.3 = (bf16[64,512]{1,0:T(8,128)(2,1)S(1)}, bf16[64,512]{1,0:T(8,128)(2,1)S(1)}, u32[]{:S(2)}, u32[]{:S(2)}) collective-permute-start(bf16[64,512]{1,0:T(8,128)(2,1)S(1)} %pad_maximum_fusion.1), channel_id=1, source_target_pairs={{0,256},{1,384},{2,0},{3,128},{128,257},{129,385},{130,1},{131,129... | collective-permute-start | bytes 196616 | tf_op jit(solution)/shard_map/ppermute | solution.py:311
  24.9 8.3 %collective-permute-start.4 = (bf16[64,512]{1,0:T(8,128)(2,1)S(1)}, bf16[64,512]{1,0:T(8,128)(2,1)S(1)}, u32[]{:S(2)}, u32[]{:S(2)}) collective-permute-start(bf16[64,512]{1,0:T(8,128)(2,1)S(1)} %pad_maximum_fusion.1), channel_id=1, source_target_pairs={{0,384},{1,0},{2,128},{3,256},{128,385},{129,1},{130,129},{131,257... | collective-permute-start | bytes 196616 | tf_op jit(solution)/shard_map/ppermute | solution.py:311
  29.3 10.4 %copy-start.5 = (s32[5]{0:T(128)S(1)}, s32[5]{0:T(128)}, u32[]{:S(2)}) copy-start(s32[5]{0:T(128)} %stack.23.refs_0_.at) | copy-start | bytes 64
  34.0 5.7 %collective-permute-start.5 = (bf16[1072,512]{1,0:T(8,128)(2,1)}, bf16[1072,512]{1,0:T(8,128)(2,1)S(1)}, u32[]{:S(2)}, u32[]{:S(2)}) collective-permute-start(bf16[1072,512]{1,0:T(8,128)(2,1)} %get-tuple-element.23), channel_id=1, source_target_pairs={{0,4},{4,0},{1,5},{5,1},{2,6},{6,2},{3,7},{7,3},{8,12},{12,8},{9,1... | collective-permute-start | bytes 3293192 | tf_op jit(solution)/shard_map/ppermute | solution.py:21
  39.7 1.2 copy-start
  43.4 16.0 %all-to-all-start = ((bf16[4,144,128]{2,1,0:T(8,128)(2,1)}), bf16[4,144,128]{2,1,0:T(8,128)(2,1)S(1)}, u32[]{:S(2)}, u32[]{:S(2)}) async-start(bf16[4,144,128]{2,1,0:T(8,128)(2,1)} %get-tuple-element.27.refs_1_), calls=%async_computation | async-start | bytes 294912 | tf_op jit(solution)/shard_map/all_to_all | solution.py:331
  49.0 10.4 %collective-permute-start.6 = (bf16[4,144,128]{2,1,0:T(8,128)(2,1)}, bf16[4,144,128]{2,1,0:T(8,128)(2,1)S(1)}, u32[]{:S(2)}, u32[]{:S(2)}) collective-permute-start(bf16[4,144,128]{2,1,0:T(8,128)(2,1)} %get-tuple-element.27.refs_1_), channel_id=1, source_target_pairs={{0,8},{8,0},{16,24},{24,16},{1,9},{9,1},{17,25},{25,17},{2,10},{10... | collective-permute-start | bytes 442376 | tf_op jit(solution)/shard_map/ppermute | solution.py:332
  60.7 35.3 %all-to-all-start.1 = ((bf16[4,144,128]{2,1,0:T(8,128)(2,1)}), bf16[4,144,128]{2,1,0:T(8,128)(2,1)S(1)}, u32[]{:S(2)}, u32[]{:S(2)}) async-start(bf16[4,144,128]{2,1,0:T(8,128)(2,1)} %shard_map.87), calls=%async_computation.1 | async-start | bytes 294912 | tf_op jit(solution)/shard_map/all_to_all | solution.py:334
  76.0 20.0 %collective-permute-start.7 = (bf16[4,144,128]{2,1,0:T(8,128)(2,1)S(1)}, bf16[4,144,128]{2,1,0:T(8,128)(2,1)S(1)}, u32[]{:S(2)}, u32[]{:S(2)}) collective-permute-start(bf16[4,144,128]{2,1,0:T(8,128)(2,1)S(1)} %shard_map.85), channel_id=1, source_target_pairs={{0,16},{8,24},{16,0},{24,8},{1,17},{9,25},{17,1},{25,9},{2,18},{10... | collective-permute-start | bytes 442376 | tf_op jit(solution)/shard_map/ppermute | solution.py:336
  96.6 12.8 %copy-start.6 = (bf16[1024]{0:T(1024)(128)(2,1)S(1)}, bf16[1024]{0:T(1024)(128)(2,1)}, u32[]{:S(2)}) copy-start(bf16[1024]{0:T(1024)(128)(2,1)} %param.14) | copy-start | bytes 6148
  96.6 12.8 %copy-start.1 = (bf16[1072,512]{1,0:T(8,128)(2,1)S(1)}, bf16[1072,512]{1,0:T(8,128)(2,1)}, u32[]{:S(2)}) copy-start(bf16[1072,512]{1,0:T(8,128)(2,1)} %get-tuple-element.21.refs_1_) | copy-start | bytes 3293188
  105.8 20.4 %all-to-all-start.3 = ((bf16[4,128,512]{2,1,0:T(8,128)(2,1)}), bf16[4,128,512]{2,1,0:T(8,128)(2,1)S(1)}, u32[]{:S(2)}, u32[]{:S(2)}) async-start(bf16[4,128,512]{2,1,0:T(8,128)(2,1)} %shard_map.89), calls=%async_computation.3 | async-start | bytes 1048576 | tf_op jit(solution)/shard_map/all_to_all | solution.py:345
  115.4 1.0 copy-start.3
  126.3 1.2 copy-start.4
  130.0 11.4 %collective-permute-start.8 = (bf16[512,512]{1,0:T(8,128)(2,1)S(1)}, bf16[512,512]{1,0:T(8,128)(2,1)S(1)}, u32[]{:S(2)}, u32[]{:S(2)}) collective-permute-start(bf16[512,512]{1,0:T(8,128)(2,1)S(1)} %shard_map.90.b0), channel_id=1, source_target_pairs={{0,1},{1,2},{2,3},{3,0},{4,5},{5,6},{6,7},{7,4},{8,9},{9,10},{10,1... | collective-permute-start | bytes 1572872 | tf_op jit(solution)/shard_map/ppermute | solution.py:297
  132.8 19.7 %collective-permute-start.9 = (bf16[512,512]{1,0:T(8,128)(2,1)S(1)}, bf16[512,512]{1,0:T(8,128)(2,1)S(1)}, u32[]{:S(2)}, u32[]{:S(2)}) collective-permute-start(bf16[512,512]{1,0:T(8,128)(2,1)S(1)} %shard_map.90.b0), channel_id=1, source_target_pairs={{0,2},{1,3},{2,0},{3,1},{4,6},{5,7},{6,4},{7,5},{8,10},{9,11},{10,... | collective-permute-start | bytes 1572872 | tf_op jit(solution)/shard_map/ppermute | solution.py:297
  135.5 22.6 %collective-permute-start.10 = (bf16[512,512]{1,0:T(8,128)(2,1)S(1)}, bf16[512,512]{1,0:T(8,128)(2,1)S(1)}, u32[]{:S(2)}, u32[]{:S(2)}) collective-permute-start(bf16[512,512]{1,0:T(8,128)(2,1)S(1)} %shard_map.90.b0), channel_id=1, source_target_pairs={{0,3},{1,0},{2,1},{3,2},{4,7},{5,4},{6,5},{7,6},{8,11},{9,8},{10,9... | collective-permute-start | bytes 1572872 | tf_op jit(solution)/shard_map/ppermute | solution.py:297
  158.1 2.2 %copy-start.2 = (bf16[1024,2048]{1,0:T(8,128)(2,1)S(1)}, bf16[1024,2048]{1,0:T(8,128)(2,1)}, u32[]{:S(2)}) copy-start(bf16[1024,2048]{1,0:T(8,128)(2,1)} %all-gather.3.cloned.1.call-done) | copy-start | bytes 12582916
  163.3 8.1 %collective-permute-start.11 = (bf16[256,1024]{1,0:T(8,128)(2,1)S(1)}, bf16[256,1024]{1,0:T(8,128)(2,1)S(1)}, u32[]{:S(2)}, u32[]{:S(2)}) collective-permute-start(bf16[256,1024]{1,0:T(8,128)(2,1)S(1)} %shard_map.92), channel_id=1, source_target_pairs={{0,4},{4,0},{1,5},{5,1},{2,6},{6,2},{3,7},{7,3},{8,12},{12,8},{9,1... | collective-permute-start | bytes 1572872 | tf_op jit(solution)/shard_map/ppermute | solution.py:21
Sparse Core Ops, SparseCore 0:
  34.1 95.1 all-gather.2

commit v15 on v13

--- a/solution.py
+++ b/solution.py
@@ -148,15 +148,18 @@
     return one, two, before
 
 
-def near_body(at, near, pay, *messages):
-    s, t, pair = blocks_of(near)
-    send_whole(s, t, pair, pay)
-    for k, message in enumerate(messages):
-        one, two, before = lower_states(s, t, pair, at[1] ^ k)
-        message[0:128, 0:128] = one.astype(BF)
-        message[0:128, 128:256] = two.astype(BF)
-        message[128:144, 0:128] = tail(before)
-        message[128:144, 128:256] = jnp.zeros((16, 128), BF)
+def near_body(at, near, pay):
+    send_whole(*blocks_of(near), pay)
+
+
+def pair_body(at, own, other, pay):
+    odd = at[1] % 2 == 1
+    for h in range(4):
+        s = [ref[h, 0:128, :].astype(F32) for ref in (own, other)]
+        t = [untail(ref[h, 128:144, :]) for ref in (own, other)]
+        scales = (jnp.where(odd, 0.0, t[1]), jnp.where(odd, t[0], 0.0))
+        pay[h, 0:128, :] = (s[0] * jnp.exp(scales[0]) + s[1] * jnp.exp(scales[1])).astype(BF)
+        pay[h, 128:144, :] = tail(t[0] + t[1])
 
 
 def far_body(at, far, pay, states, before_out):
@@ -214,15 +217,18 @@
                 coef[here, 6 * h + l - 2 : 6 * h + l - 1] = start * m[l]
 
 
-def mix_body(at, keep, got, mixture, coef, n0, n1, n2, n3, mixed, later, near):
-    for k, n in enumerate((n0, n1, n2, n3)):
-        near[at[1] ^ k] = n[...]
+def mix_body(at, keep, got, mixture, coef, other, pair, mixed, later):
+    odd, upper = at[1] % 2 == 1, at[1] >= 2
     for h in range(4):
-        before = jnp.exp(untail(near[h, 128:144, 0:128])[:, 0:1])
+        step = jnp.where(odd, untail(other[h, 128:144, :]), 0.0)
+        one = jnp.where(odd, other[h, 0:128, :].astype(F32), 0.0).astype(BF)
+        two = jnp.where(upper, pair[h, 0:128, :].astype(F32) * jnp.exp(step), 0.0).astype(BF)
+        before = jnp.exp(step + jnp.where(upper, untail(pair[h, 128:144, :]), 0.0))[:, 0:1]
+        states = jnp.concatenate([one, two], axis=1)
         hc = slice(h * 128, h * 128 + 128)
         for s, ref in enumerate((keep, got)):
             _, here = place(s, at[0])
-            read = dot(ref[512:768, hc], near[h, 0:128, :])
+            read = dot(ref[512:768, hc], states)
             total = mixture[here, hc] + read[:, 0:128] * coef[here, 6 * h : 6 * h + 1]
             mixed[here, hc] = total + read[:, 128:256] * coef[here, 6 * h + 1 : 6 * h + 2]
             later[here, 4 * h : 4 * h + 4] = coef[here, 6 * h + 2 : 6 * h + 6] * before
@@ -292,6 +298,7 @@
     )
     perm = [(s * 4 + f, f * 4 + s) for s in range(4) for f in range(4)]
     mine = lax.ppermute(both, ("y", "x"), perm)
+    theirs = lax.ppermute(mine, "q", [(0, 1), (1, 0)])
     block = ((ROWS, 512), BF)
     keep, send = call(
         pack_body,
@@ -305,8 +312,7 @@
         hbm=range(1, 7),
         vmem=60,
     )
-    mine, send = lax.optimization_barrier((mine, send))
-    theirs = lax.ppermute(mine, "q", [(0, 1), (1, 0)])
+    theirs, send = lax.optimization_barrier((theirs, send))
     mine = jnp.stack([jnp.where(q == 0, mine, theirs), jnp.where(q == 0, theirs, mine)])
     gathered = lax.all_gather(mine, ("a", "p"), axis=0, tiled=True)
 
@@ -314,30 +320,27 @@
     pay = ((4, 144, 128), BF)
     pay_b, first = call(ends_body, [pay, ((4, 128, 128), BF)], (at, keep, got))
     near = lax.all_to_all(pay_b, NEAR, 0, 0, tiled=True)
-    pay_a, *near = call(near_body, [pay] + [((144, 256), BF)] * 4, (at, near))
+    other = lax.ppermute(pay_b, NEAR, [(i, i ^ 1) for i in range(4)])
+    (pay_a,) = call(near_body, [pay], (at, near), unread=(other,))
     far = lax.all_to_all(pay_a, "a", 0, 0, tiled=True)
-    near = near[:1] + [
-        lax.ppermute(near[k], NEAR, [(i, i ^ k) for i in range(4)]) for k in (1, 2, 3)
-    ]
-    mixture, coef = call(
-        own_body, [((512, 512), F32), ((512, 24), F32)], (at, keep, got, first)
-    )
+    (pair,) = call(pair_body, [pay], (at, pay_b, other))
+    pair = lax.ppermute(pair, NEAR, [(i, i ^ 2) for i in range(4)])
     pay_y, far, before = call(
         far_body,
         [pay, ((128, 256), BF), ((8, 128), F32)],
         (at, far),
-        unread=near[1:],
+        unread=(pair,),
     )
     rows = lax.all_to_all(pay_y, "y", 0, 0, tiled=True)
-    (states,) = call(
-        last_body, [((4, 128, 512), BF)], (at, rows, before, far), unread=(mixture,)
-    )
+    (states,) = call(last_body, [((4, 128, 512), BF)], (at, rows, before, far))
     states = lax.all_to_all(states, NEAR, 0, 0, tiled=True)
+    mixture, coef = call(
+        own_body, [((512, 512), F32), ((512, 24), F32)], (at, keep, got, first)
+    )
     mixture, coef = call(
         mix_body,
         [((512, 512), F32), ((512, 16), F32)],
-        (at, keep, got, mixture, coef, *near),
-        scratch=[pltpu.VMEM((4, 144, 256), BF)],
+        (at, keep, got, mixture, coef, other, pair),
     )
     _, gathered = lax.optimization_barrier((coef, gathered))
     rights = [gathered] + [shift(gathered, "y", 4 - k) for k in (1, 3, 2)]

time: 174 us -> 186 us (1.069)
  blocking collectives: 8.1 us -> 23.3 us
  waiting for transfers between devices: 42.7 us -> 56.9 us
  starting transfers between devices: 69.1 us -> 57.3 us
  local copies, waits for them, and re-layouts: 12 us -> 4.78 us
  Pallas kernels: 24.4 us -> 26.3 us
    all_to_all x1, blocking collectives: 8.1 us -> 23.3 us  [shards(): rows = lax.all_to_all(pay_y, 'y', 0, 0, tiled=True)]
    ppermute x3 -> x2, waiting for transfers between devices: 11.6 us -> 24.5 us  [the longest x1 19.2 us: shards(): pair = lax.ppermute(pair, NEAR, [(i, i ^ 2) for i in range(4)])]
    unnamed x40 -> x14, local copies, waits for them, and re-layouts: 10.6 us -> 3.45 us
    all_to_all x1, starting transfers between devices: 10.3 us -> 3.34 us  [shards(): near = lax.all_to_all(pay_b, NEAR, 0, 0, tiled=True)]
    ppermute x1, waiting for transfers between devices: 3.5 us -> 0.01 us  [shards(): theirs = lax.ppermute(mine, 'q', [(0, 1), (1, 0)])]
    ppermute x3 -> x2, starting transfers between devices: 9.26 us -> 6.28 us  [the longest x1 3.6 us: shards(): other = lax.ppermute(pay_b, NEAR, [(i, i ^ 1) for i in range(4)])]
    ppermute x6, waiting for transfers between devices: 26.7 us -> 29.7 us  [shift(): return lax.ppermute(value, axis, [(i, (i + by) % 4) for i in range(4)])]
    ppermute x6, starting transfers between devices: 19.2 us -> 17.1 us  [shift(): return lax.ppermute(value, axis, [(i, (i + by) % 4) for i in range(4)])]
  transfers between devices with their start and end apart: 18 -> 17, of which waited for: 7 -> 6; matrix products, arithmetic and copies ran while one was open for 1% -> 1% of each run, Pallas kernels for 12% -> 12%
where the time goes in v15:
time: 186 us; the launch traced here: 185 us
  starting transfers between devices  57.3 us (31%)
  waiting for transfers between devices  56.9 us (31%)
  Pallas kernels  26.3 us (14%)
  blocking collectives  23.3 us (13%)
  between operations  13.7 us (7%)
  local copies, waits for them, and re-layouts  4.78 us (3%)
  other arithmetic  2.41 us (1%)
    ppermute x6, waiting for transfers between devices, shift(): return lax.ppermute(value, axis, [(i, (i + by) % 4) for i in range(4)])  29.7 us
    pallas_call x11, Pallas kernels, call(): pl.pallas_call(run, out_shape=[jax.ShapeDtypeStruct(*o) for o in outs], i...  26.3 us
    all_to_all x1, blocking collectives, shards(): rows = lax.all_to_all(pay_y, 'y', 0, 0, tiled=True)  23.3 us
    ppermute x1, waiting for transfers between devices, shards(): pair = lax.ppermute(pair, NEAR, [(i, i ^ 2) for i in range(4)])  19.2 us
    ppermute x6, starting transfers between devices, shift(): return lax.ppermute(value, axis, [(i, (i + by) % 4) for i in range(4)])  17.1 us
    ppermute x3, starting transfers between devices, swap(): return lax.ppermute(value, 'c', [(0, 1), (1, 0)])  13.4 us
    all_to_all x1, starting transfers between devices, shards(): far = lax.all_to_all(pay_a, 'a', 0, 0, tiled=True)  10.4 us
    ppermute x1, waiting for transfers between devices, shards(): other = lax.ppermute(pay_b, NEAR, [(i, i ^ 1) for i in range(4)])  5.25 us
  transfers between devices with their start and end apart: 17, of which 6 were waited for; matrix products, arithmetic and copies ran while one was open for 1% of the time, Pallas kernels for 12%

profile of v15, /device:TPU:1, one launch (start us, length us, event | category | flops | bytes accessed | tf_op | source)
XLA Modules:
  0.0 184.6 jit_solution(5835655327380211390)
XLA Ops:
  7.3 8.8 %collective-permute-start = (bf16[32,512]{1,0:T(8,128)(2,1)S(1)}, bf16[32,512]{1,0:T(8,128)(2,1)S(1)}, u32[]{:S(2)}, u32[]{:S(2)}) collective-permute-start(bf16[32,512]{1,0:T(8,128)(2,1)S(1)} %constant_dynamic-slice_fusion), channel_id=1, source_target_pairs={{0,4},{4,0},{1,5},{5,1},{2,6},{6,2},{3,7},{7,3},{8,12},{12,8},{9,1... | collective-permute-start | bytes 98312 | tf_op jit(solution)/shard_map/ppermute | solution.py:21
  20.9 3.8 %shard_map.82 = (bf16[1072,512]{1,0:T(8,128)(2,1)}, bf16[1072,512]{1,0:T(8,128)(2,1)}) custom-call(s32[5]{0:T(128)} %stack.32.refs_0_, bf16[256,1024]{1,0:T(8,128)(2,1)} %refs_1_.1, bf16[256,1024]{1,0:T(8,128)(2,1)} %refs_2_.1, bf16[256,1024]{1,0:T(8,128)(2,1)} %refs_3_.1, bf16[256,1024]{1,0:T(8,128)(2,1)} %refs_4_.1, f32[8,256]{1,0:T(8,128)} %refs_5_.1, ...), custom_call_target="tpu_custom_call" | custom-call | flops 1000000 | bytes 1000000 | tf_op jit(solution)/shard_map/pallas_call | solution.py:59
  24.7 2.3 %collective-permute-start.3 = (bf16[1072,512]{1,0:T(8,128)(2,1)}, bf16[1072,512]{1,0:T(8,128)(2,1)S(1)}, u32[]{:S(2)}, u32[]{:S(2)}) collective-permute-start(bf16[1072,512]{1,0:T(8,128)(2,1)} %get-tuple-element.21), channel_id=1, source_target_pairs={{0,4},{4,0},{1,5},{5,1},{2,6},{6,2},{3,7},{7,3},{8,12},{12,8},{9,1... | collective-permute-start | bytes 3293192 | tf_op jit(solution)/shard_map/ppermute | solution.py:21
  30.8 2.4 %shard_map.83 = (bf16[4,144,128]{2,1,0:T(8,128)(2,1)}, bf16[4,128,128]{2,1,0:T(8,128)(2,1)S(1)}) custom-call(s32[5]{0:T(128)S(1)} %copy-done.5, bf16[1072,512]{1,0:T(8,128)(2,1)S(1)} %copy-done, bf16[1072,512]{1,0:T(8,128)(2,1)S(1)} %collective-permute-done.3.refs_2_), custom_call_target="tpu_custom_call" | custom-call | flops 1000000 | bytes 1000000 | tf_op jit(solution)/shard_map/pallas_call | solution.py:59
  33.2 3.3 %all-to-all-start = ((bf16[4,144,128]{2,1,0:T(8,128)(2,1)}), bf16[4,144,128]{2,1,0:T(8,128)(2,1)S(1)}, u32[]{:S(2)}, u32[]{:S(2)}) async-start(bf16[4,144,128]{2,1,0:T(8,128)(2,1)} %get-tuple-element.25.refs_1_), calls=%async_computation | async-start | bytes 294912 | tf_op jit(solution)/shard_map/all_to_all | solution.py:322
  36.6 3.6 %collective-permute-start.4 = (bf16[4,144,128]{2,1,0:T(8,128)(2,1)}, bf16[4,144,128]{2,1,0:T(8,128)(2,1)S(1)}, u32[]{:S(2)}, u32[]{:S(2)}) collective-permute-start(bf16[4,144,128]{2,1,0:T(8,128)(2,1)} %get-tuple-element.25.refs_1_), channel_id=1, source_target_pairs={{0,8},{8,0},{16,24},{24,16},{1,9},{9,1},{17,25},{25,17},{2,10},{10... | collective-permute-start | bytes 442376 | tf_op jit(solution)/shard_map/ppermute | solution.py:323
  40.2 5.2 %collective-permute-done.4.refs_2_.refs_5_ = bf16[4,144,128]{2,1,0:T(8,128)(2,1)S(1)} collective-permute-done((bf16[4,144,128]{2,1,0:T(8,128)(2,1)}, bf16[4,144,128]{2,1,0:T(8,128)(2,1)S(1)}, u32[]{:S(2)}, u32[]{:S(2)}) %collective-permute-start.4) | collective-permute-done | bytes 147488 | tf_op jit(solution)/shard_map/ppermute | solution.py:323
  46.7 10.4 %all-to-all-start.1 = ((bf16[4,144,128]{2,1,0:T(8,128)(2,1)}), bf16[4,144,128]{2,1,0:T(8,128)(2,1)S(1)}, u32[]{:S(2)}, u32[]{:S(2)}) async-start(bf16[4,144,128]{2,1,0:T(8,128)(2,1)} %shard_map.87), calls=%async_computation.1 | async-start | bytes 294912 | tf_op jit(solution)/shard_map/all_to_all | solution.py:325
  58.0 2.7 %collective-permute-start.5 = (bf16[4,144,128]{2,1,0:T(8,128)(2,1)S(1)}, bf16[4,144,128]{2,1,0:T(8,128)(2,1)S(1)}, u32[]{:S(2)}, u32[]{:S(2)}) collective-permute-start(bf16[4,144,128]{2,1,0:T(8,128)(2,1)S(1)} %shard_map.85), channel_id=1, source_target_pairs={{0,16},{8,24},{16,0},{24,8},{1,17},{9,25},{17,1},{25,9},{2,18},{10... | collective-permute-start | bytes 442376 | tf_op jit(solution)/shard_map/ppermute | solution.py:327
  60.7 19.2 %collective-permute-done.5.refs_6_.refs_2_ = bf16[4,144,128]{2,1,0:T(8,128)(2,1)S(1)} collective-permute-done((bf16[4,144,128]{2,1,0:T(8,128)(2,1)S(1)}, bf16[4,144,128]{2,1,0:T(8,128)(2,1)S(1)}, u32[]{:S(2)}, u32[]{:S(2)}) %collective-permute-start.5) | collective-permute-done | bytes 147488 | tf_op jit(solution)/shard_map/ppermute | solution.py:327
  80.5 23.3 %all_to_all.20.refs_1_ = bf16[4,144,128]{2,1,0:T(8,128)(2,1)S(1)} all-to-all(bf16[4,144,128]{2,1,0:T(8,128)(2,1)S(1)} %get-tuple-element.28), channel_id=1, replica_groups=mesh['y'=4,'a'=4,'p'=2,'q'=2,'c'=2,'x'=4] {'y'}, dimensions={0} | all-to-all | bytes 294912 | tf_op jit(solution)/shard_map/all_to_all | solution.py:334
  105.2 4.1 %all-to-all-start.3 = ((bf16[4,128,512]{2,1,0:T(8,128)(2,1)}), bf16[4,128,512]{2,1,0:T(8,128)(2,1)}, u32[]{:S(2)}, u32[]{:S(2)}) async-start(bf16[4,128,512]{2,1,0:T(8,128)(2,1)} %shard_map.89), calls=%async_computation.3 | async-start | bytes 1048576 | tf_op jit(solution)/shard_map/all_to_all | solution.py:336
  109.4 4.3 %shard_map.84 = (f32[512,512]{1,0:T(8,128)S(1)}, f32[512,24]{1,0:T(8,128)S(1)}) custom-call(s32[5]{0:T(128)S(1)} %copy-done.5, bf16[1072,512]{1,0:T(8,128)(2,1)S(1)} %copy-done.1, bf16[1072,512]{1,0:T(8,128)(2,1)S(1)} %collective-permute-done.3.refs_2_, bf16[4,128,128]{2,1,0:T(8,128)(2,1)S(1)} %get-tuple-element.22.refs_3_), custom_call_target="tpu_custom_call" | custom-call | flops 1000000 | bytes 1000000 | tf_op jit(solution)/shard_map/pallas_call | solution.py:59
  116.4 3.0 %collective-permute-start.11 = (bf16[16,64,512]{2,1,0:T(8,128)(2,1)}, bf16[16,64,512]{2,1,0:T(8,128)(2,1)S(1)}, u32[]{:S(2)}, u32[]{:S(2)}) collective-permute-start(bf16[16,64,512]{2,1,0:T(8,128)(2,1)} %all-gather.2.cloned.1.call-done.refs_5_), channel_id=1, source_target_pairs={{0,256},{128,384},{256,0},{384,128},{1,257},{129,385},{257,1},{385... | collective-permute-start | bytes 3145736 | tf_op jit(solution)/shard_map/ppermute | solution.py:288
  119.5 2.2 %collective-permute-start.10 = (bf16[16,64,512]{2,1,0:T(8,128)(2,1)}, bf16[16,64,512]{2,1,0:T(8,128)(2,1)}, u32[]{:S(2)}, u32[]{:S(2)}) collective-permute-start(bf16[16,64,512]{2,1,0:T(8,128)(2,1)} %all-gather.2.cloned.1.call-done.refs_5_), channel_id=1, source_target_pairs={{0,128},{128,256},{256,384},{384,0},{1,129},{129,257},{257,385},{3... | collective-permute-start | bytes 3145736 | tf_op jit(solution)/shard_map/ppermute | solution.py:288
  121.7 4.3 %collective-permute-start.9 = (bf16[16,64,512]{2,1,0:T(8,128)(2,1)}, bf16[16,64,512]{2,1,0:T(8,128)(2,1)}, u32[]{:S(2)}, u32[]{:S(2)}) collective-permute-start(bf16[16,64,512]{2,1,0:T(8,128)(2,1)} %all-gather.2.cloned.1.call-done.refs_5_), channel_id=1, source_target_pairs={{0,384},{128,0},{256,128},{384,256},{1,385},{129,1},{257,129},{385... | collective-permute-start | bytes 3145736 | tf_op jit(solution)/shard_map/ppermute | solution.py:288
  127.2 3.1 %shard_map.90.refs_1_ = bf16[512,512]{1,0:T(8,128)(2,1)S(1)} custom-call(s32[5]{0:T(128)S(1)} %copy-done.5, bf16[1072,512]{1,0:T(8,128)(2,1)S(1)} %copy-done.1, bf16[1072,512]{1,0:T(8,128)(2,1)S(1)} %collective-permute-done.3.refs_2_, bf16[1,1024]{1,0:T(2,128)(2,1)S(1)} %broadcast_in_dim.3.refs_3_, f32[512,512]{1,0:T(8,128)S(1)} %copy-done.4, ...), custom_call_target="tpu_custom_call" | custom-call | flops 1000000 | bytes 1000000 | tf_op jit(solution)/shard_map/pallas_call | solution.py:59
  130.4 2.4 %collective-permute-start.8 = (bf16[512,512]{1,0:T(8,128)(2,1)S(1)}, bf16[512,512]{1,0:T(8,128)(2,1)S(1)}, u32[]{:S(2)}, u32[]{:S(2)}) collective-permute-start(bf16[512,512]{1,0:T(8,128)(2,1)S(1)} %shard_map.90.refs_1_), channel_id=1, source_target_pairs={{0,3},{1,0},{2,1},{3,2},{4,7},{5,4},{6,5},{7,6},{8,11},{9,8},{10,9... | collective-permute-start | bytes 1572872 | tf_op jit(solution)/shard_map/ppermute | solution.py:288
  132.8 3.2 %collective-permute-start.7 = (bf16[512,512]{1,0:T(8,128)(2,1)S(1)}, bf16[512,512]{1,0:T(8,128)(2,1)S(1)}, u32[]{:S(2)}, u32[]{:S(2)}) collective-permute-start(bf16[512,512]{1,0:T(8,128)(2,1)S(1)} %shard_map.90.refs_1_), channel_id=1, source_target_pairs={{0,2},{1,3},{2,0},{3,1},{4,6},{5,7},{6,4},{7,5},{8,10},{9,11},{10,... | collective-permute-start | bytes 1572872 | tf_op jit(solution)/shard_map/ppermute | solution.py:288
  136.0 6.6 %collective-permute-done.11.refs_8_ = bf16[16,64,512]{2,1,0:T(8,128)(2,1)S(1)} collective-permute-done((bf16[16,64,512]{2,1,0:T(8,128)(2,1)}, bf16[16,64,512]{2,1,0:T(8,128)(2,1)S(1)}, u32[]{:S(2)}, u32[]{:S(2)}) %collective-permute-start.11) | collective-permute-done | bytes 1048608 | tf_op jit(solution)/shard_map/ppermute | solution.py:288
  144.6 23.1 %collective-permute-done.10.refs_7_ = bf16[16,64,512]{2,1,0:T(8,128)(2,1)} collective-permute-done((bf16[16,64,512]{2,1,0:T(8,128)(2,1)}, bf16[16,64,512]{2,1,0:T(8,128)(2,1)}, u32[]{:S(2)}, u32[]{:S(2)}) %collective-permute-start.10) | collective-permute-done | bytes 1048608 | tf_op jit(solution)/shard_map/ppermute | solution.py:288
  167.7 3.3 %shard_map.92 = bf16[256,1024]{1,0:T(8,128)(2,1)S(1)} custom-call(s32[5]{0:T(128)S(1)} %copy-done.5, bf16[512,512]{1,0:T(8,128)(2,1)S(1)} %shard_map.90.refs_1_, bf16[512,512]{1,0:T(8,128)(2,1)S(1)} %collective-permute-done.6.refs_2_, bf16[512,512]{1,0:T(8,128)(2,1)S(1)} %collective-permute-done.7.refs_3_, ...), custom_call_target="tpu_custom_call" | custom-call | flops 1000000 | bytes 1000000 | tf_op jit(solution)/shard_map/pallas_call | solution.py:59
  171.0 2.4 %collective-permute-start.12 = (bf16[256,1024]{1,0:T(8,128)(2,1)S(1)}, bf16[256,1024]{1,0:T(8,128)(2,1)S(1)}, u32[]{:S(2)}, u32[]{:S(2)}) collective-permute-start(bf16[256,1024]{1,0:T(8,128)(2,1)S(1)} %shard_map.92), channel_id=1, source_target_pairs={{0,4},{4,0},{1,5},{5,1},{2,6},{6,2},{3,7},{7,3},{8,12},{12,8},{9,1... | collective-permute-start | bytes 1572872 | tf_op jit(solution)/shard_map/ppermute | solution.py:21
  173.5 3.3 %shard_map.91 = f32[256,1024]{1,0:T(8,128)S(1)} custom-call(s32[5]{0:T(128)S(1)} %copy-done.5, bf16[512,512]{1,0:T(8,128)(2,1)S(1)} %shard_map.90.refs_1_, bf16[512,512]{1,0:T(8,128)(2,1)S(1)} %collective-permute-done.6.refs_2_, bf16[512,512]{1,0:T(8,128)(2,1)S(1)} %collective-permute-done.7.refs_3_, bf16[512,512]{1,0:T(8,128)(2,1)S(1)} %collective-permute-done.8.refs_4_, ...), custom_call_target="tpu_custom_call" | custom-call | flops 1000000 | bytes 1000000 | tf_op jit(solution)/shard_map/pallas_call | solution.py:59
  (45 shorter events, 20.4 us)
Async XLA Ops:
  6.5 109.9 %all-gather.2.cloned.1.call-start = ((), (), s32[]{:S(2)}) async-start(), calls=%async_computation.4 | async-start | bytes 1179648 | tf_op jit(solution)/shard_map/all_gather | solution.py:317
  7.3 9.6 %collective-permute-start = (bf16[32,512]{1,0:T(8,128)(2,1)S(1)}, bf16[32,512]{1,0:T(8,128)(2,1)S(1)}, u32[]{:S(2)}, u32[]{:S(2)}) collective-permute-start(bf16[32,512]{1,0:T(8,128)(2,1)S(1)} %constant_dynamic-slice_fusion), channel_id=1, source_target_pairs={{0,4},{4,0},{1,5},{5,1},{2,6},{6,2},{3,7},{7,3},{8,12},{12,8},{9,1... | collective-permute-start | bytes 98312 | tf_op jit(solution)/shard_map/ppermute | solution.py:21
  17.7 0.7 collective-permute-start.1
  18.4 6.3 %collective-permute-start.2 = (bf16[64,512]{1,0:T(8,128)(2,1)S(1)}, bf16[64,512]{1,0:T(8,128)(2,1)S(1)}, u32[]{:S(2)}, u32[]{:S(2)}) collective-permute-start(bf16[64,512]{1,0:T(8,128)(2,1)S(1)} %collective-permute-done.1), channel_id=1, source_target_pairs={{0,8},{8,0},{1,9},{9,1},{2,10},{10,2},{3,11},{11,3},{4,12},{12,4},... | collective-permute-start | bytes 196616 | tf_op jit(solution)/shard_map/ppermute | solution.py:301
  20.9 8.6 %copy-start.5 = (s32[5]{0:T(128)S(1)}, s32[5]{0:T(128)}, u32[]{:S(2)}) copy-start(s32[5]{0:T(128)} %stack.32.refs_0_) | copy-start | bytes 64
  24.7 4.8 %collective-permute-start.3 = (bf16[1072,512]{1,0:T(8,128)(2,1)}, bf16[1072,512]{1,0:T(8,128)(2,1)S(1)}, u32[]{:S(2)}, u32[]{:S(2)}) collective-permute-start(bf16[1072,512]{1,0:T(8,128)(2,1)} %get-tuple-element.21), channel_id=1, source_target_pairs={{0,4},{4,0},{1,5},{5,1},{2,6},{6,2},{3,7},{7,3},{8,12},{12,8},{9,1... | collective-permute-start | bytes 3293192 | tf_op jit(solution)/shard_map/ppermute | solution.py:21
  29.5 1.2 copy-start
  33.2 12.2 %all-to-all-start = ((bf16[4,144,128]{2,1,0:T(8,128)(2,1)}), bf16[4,144,128]{2,1,0:T(8,128)(2,1)S(1)}, u32[]{:S(2)}, u32[]{:S(2)}) async-start(bf16[4,144,128]{2,1,0:T(8,128)(2,1)} %get-tuple-element.25.refs_1_), calls=%async_computation | async-start | bytes 294912 | tf_op jit(solution)/shard_map/all_to_all | solution.py:322
  36.6 8.9 %collective-permute-start.4 = (bf16[4,144,128]{2,1,0:T(8,128)(2,1)}, bf16[4,144,128]{2,1,0:T(8,128)(2,1)S(1)}, u32[]{:S(2)}, u32[]{:S(2)}) collective-permute-start(bf16[4,144,128]{2,1,0:T(8,128)(2,1)} %get-tuple-element.25.refs_1_), channel_id=1, source_target_pairs={{0,8},{8,0},{16,24},{24,16},{1,9},{9,1},{17,25},{25,17},{2,10},{10... | collective-permute-start | bytes 442376 | tf_op jit(solution)/shard_map/ppermute | solution.py:323
  46.7 33.3 %all-to-all-start.1 = ((bf16[4,144,128]{2,1,0:T(8,128)(2,1)}), bf16[4,144,128]{2,1,0:T(8,128)(2,1)S(1)}, u32[]{:S(2)}, u32[]{:S(2)}) async-start(bf16[4,144,128]{2,1,0:T(8,128)(2,1)} %shard_map.87), calls=%async_computation.1 | async-start | bytes 294912 | tf_op jit(solution)/shard_map/all_to_all | solution.py:325
  58.0 21.9 %collective-permute-start.5 = (bf16[4,144,128]{2,1,0:T(8,128)(2,1)S(1)}, bf16[4,144,128]{2,1,0:T(8,128)(2,1)S(1)}, u32[]{:S(2)}, u32[]{:S(2)}) collective-permute-start(bf16[4,144,128]{2,1,0:T(8,128)(2,1)S(1)} %shard_map.85), channel_id=1, source_target_pairs={{0,16},{8,24},{16,0},{24,8},{1,17},{9,25},{17,1},{25,9},{2,18},{10... | collective-permute-start | bytes 442376 | tf_op jit(solution)/shard_map/ppermute | solution.py:327
  80.5 28.9 %copy-start.1 = (bf16[1072,512]{1,0:T(8,128)(2,1)S(1)}, bf16[1072,512]{1,0:T(8,128)(2,1)}, u32[]{:S(2)}) copy-start(bf16[1072,512]{1,0:T(8,128)(2,1)} %get-tuple-element.19.refs_1_) | copy-start | bytes 3293188
  105.2 20.8 %all-to-all-start.3 = ((bf16[4,128,512]{2,1,0:T(8,128)(2,1)}), bf16[4,128,512]{2,1,0:T(8,128)(2,1)}, u32[]{:S(2)}, u32[]{:S(2)}) async-start(bf16[4,128,512]{2,1,0:T(8,128)(2,1)} %shard_map.89), calls=%async_computation.3 | async-start | bytes 1048576 | tf_op jit(solution)/shard_map/all_to_all | solution.py:336
  113.7 12.2 %copy-start.6 = (bf16[1024]{0:T(1024)(128)(2,1)S(1)}, bf16[1024]{0:T(1024)(128)(2,1)}, u32[]{:S(2)}) copy-start(bf16[1024]{0:T(1024)(128)(2,1)} %param.14) | copy-start | bytes 6148
  115.4 1.0 copy-start.3
  116.4 26.1 %collective-permute-start.11 = (bf16[16,64,512]{2,1,0:T(8,128)(2,1)}, bf16[16,64,512]{2,1,0:T(8,128)(2,1)S(1)}, u32[]{:S(2)}, u32[]{:S(2)}) collective-permute-start(bf16[16,64,512]{2,1,0:T(8,128)(2,1)} %all-gather.2.cloned.1.call-done.refs_5_), channel_id=1, source_target_pairs={{0,256},{128,384},{256,0},{384,128},{1,257},{129,385},{257,1},{385... | collective-permute-start | bytes 3145736 | tf_op jit(solution)/shard_map/ppermute | solution.py:288
  119.5 48.2 %collective-permute-start.10 = (bf16[16,64,512]{2,1,0:T(8,128)(2,1)}, bf16[16,64,512]{2,1,0:T(8,128)(2,1)}, u32[]{:S(2)}, u32[]{:S(2)}) collective-permute-start(bf16[16,64,512]{2,1,0:T(8,128)(2,1)} %all-gather.2.cloned.1.call-done.refs_5_), channel_id=1, source_target_pairs={{0,128},{128,256},{256,384},{384,0},{1,129},{129,257},{257,385},{3... | collective-permute-start | bytes 3145736 | tf_op jit(solution)/shard_map/ppermute | solution.py:288
  121.7 46.0 %collective-permute-start.9 = (bf16[16,64,512]{2,1,0:T(8,128)(2,1)}, bf16[16,64,512]{2,1,0:T(8,128)(2,1)}, u32[]{:S(2)}, u32[]{:S(2)}) collective-permute-start(bf16[16,64,512]{2,1,0:T(8,128)(2,1)} %all-gather.2.cloned.1.call-done.refs_5_), channel_id=1, source_target_pairs={{0,384},{128,0},{256,128},{384,256},{1,385},{129,1},{257,129},{385... | collective-permute-start | bytes 3145736 | tf_op jit(solution)/shard_map/ppermute | solution.py:288
  126.0 1.2 copy-start.4
  127.2 40.5 %copy-start.2 = (bf16[16,64,512]{2,1,0:T(8,128)(2,1)S(1)}, bf16[16,64,512]{2,1,0:T(8,128)(2,1)}, u32[]{:S(2)}) copy-start(bf16[16,64,512]{2,1,0:T(8,128)(2,1)} %all-gather.2.cloned.1.call-done.refs_5_) | copy-start | bytes 3145732
  130.4 37.3 %collective-permute-start.8 = (bf16[512,512]{1,0:T(8,128)(2,1)S(1)}, bf16[512,512]{1,0:T(8,128)(2,1)S(1)}, u32[]{:S(2)}, u32[]{:S(2)}) collective-permute-start(bf16[512,512]{1,0:T(8,128)(2,1)S(1)} %shard_map.90.refs_1_), channel_id=1, source_target_pairs={{0,3},{1,0},{2,1},{3,2},{4,7},{5,4},{6,5},{7,6},{8,11},{9,8},{10,9... | collective-permute-start | bytes 1572872 | tf_op jit(solution)/shard_map/ppermute | solution.py:288
  132.8 34.9 %collective-permute-start.7 = (bf16[512,512]{1,0:T(8,128)(2,1)S(1)}, bf16[512,512]{1,0:T(8,128)(2,1)S(1)}, u32[]{:S(2)}, u32[]{:S(2)}) collective-permute-start(bf16[512,512]{1,0:T(8,128)(2,1)S(1)} %shard_map.90.refs_1_), channel_id=1, source_target_pairs={{0,2},{1,3},{2,0},{3,1},{4,6},{5,7},{6,4},{7,5},{8,10},{9,11},{10,... | collective-permute-start | bytes 1572872 | tf_op jit(solution)/shard_map/ppermute | solution.py:288
  142.6 25.1 %collective-permute-start.6 = (bf16[512,512]{1,0:T(8,128)(2,1)S(1)}, bf16[512,512]{1,0:T(8,128)(2,1)S(1)}, u32[]{:S(2)}, u32[]{:S(2)}) collective-permute-start(bf16[512,512]{1,0:T(8,128)(2,1)S(1)} %shard_map.90.refs_1_), channel_id=1, source_target_pairs={{0,1},{1,2},{2,3},{3,0},{4,5},{5,6},{6,7},{7,4},{8,9},{9,10},{10,1... | collective-permute-start | bytes 1572872 | tf_op jit(solution)/shard_map/ppermute | solution.py:288
  171.0 5.7 %collective-permute-start.12 = (bf16[256,1024]{1,0:T(8,128)(2,1)S(1)}, bf16[256,1024]{1,0:T(8,128)(2,1)S(1)}, u32[]{:S(2)}, u32[]{:S(2)}) collective-permute-start(bf16[256,1024]{1,0:T(8,128)(2,1)S(1)} %shard_map.92), channel_id=1, source_target_pairs={{0,4},{4,0},{1,5},{5,1},{2,6},{6,2},{3,7},{7,3},{8,12},{12,8},{9,1... | collective-permute-start | bytes 1572872 | tf_op jit(solution)/shard_map/ppermute | solution.py:21
Sparse Core Ops, SparseCore 0:
  27.8 67.2 all-gather.1

commit v16 on v13

--- a/solution.py
+++ b/solution.py
@@ -283,7 +283,7 @@
 
 
 def shards(values, keys, queries, gates, log_decay, level_mix, norm_gain, weight):
-    y, a, b, q, c, x = (lax.axis_index(n) for n in ("y", "a", NEAR, "q", "c", "x"))
+    y, a, b, c, x = (lax.axis_index(n) for n in ("y", "a", NEAR, "c", "x"))
     at = jnp.stack([c, b, a, y, x]).astype(jnp.int32)
     kept = lax.dynamic_slice_in_dim(weight, c * 512, 512, 1)
     theirs = swap(lax.dynamic_slice_in_dim(weight, (1 - c) * 512, 512, 1))
@@ -306,9 +306,7 @@
         vmem=60,
     )
     mine, send = lax.optimization_barrier((mine, send))
-    theirs = lax.ppermute(mine, "q", [(0, 1), (1, 0)])
-    mine = jnp.stack([jnp.where(q == 0, mine, theirs), jnp.where(q == 0, theirs, mine)])
-    gathered = lax.all_gather(mine, ("a", "p"), axis=0, tiled=True)
+    gathered = lax.all_gather(mine, ("a", "p", "q"))
 
     got = swap(send)
     pay = ((4, 144, 128), BF)

time: 174 us -> 166 us (0.954)
  waiting for transfers between devices: 42.7 us -> 36.1 us
    ppermute x3, waiting for transfers between devices: 11.6 us -> 7.12 us  [shards(): lax.ppermute(near[k], NEAR, [(i, i ^ k) for i in range(4)])]
    ppermute x1 -> x0, waiting for transfers between devices: 3.5 us -> none  [shards(): theirs = lax.ppermute(mine, 'q', [(0, 1), (1, 0)])]
    ppermute x3, waiting for transfers between devices: 0.84 us -> 3.37 us  [swap(): return lax.ppermute(value, 'c', [(0, 1), (1, 0)])]
    ppermute x1 -> x0, starting transfers between devices: 1.92 us -> none  [shards(): theirs = lax.ppermute(mine, 'q', [(0, 1), (1, 0)])]
    unnamed x40 -> x42, local copies, waits for them, and re-layouts: 10.6 us -> 10.5 us
  transfers between devices with their start and end apart: 18 -> 17, of which waited for: 7 -> 6; matrix products, arithmetic and copies ran while one was open for 1% -> 0% of each run, Pallas kernels for 12% -> 13%
where the time goes in v16:
time: 166 us; the launch traced here: 165 us
  starting transfers between devices  68.2 us (41%)
  waiting for transfers between devices  36.1 us (22%)
  Pallas kernels  24.4 us (15%)
  between operations  13.7 us (8%)
  local copies, waits for them, and re-layouts  11.9 us (7%)
  blocking collectives  8.61 us (5%)
  other arithmetic  1.72 us (1%)
    ppermute x6, waiting for transfers between devices, shift(): return lax.ppermute(value, axis, [(i, (i + by) % 4) for i in range(4)])  25.6 us
    pallas_call x10, Pallas kernels, call(): pl.pallas_call(run, out_shape=[jax.ShapeDtypeStruct(*o) for o in outs], i...  24.4 us
    ppermute x6, starting transfers between devices, shift(): return lax.ppermute(value, axis, [(i, (i + by) % 4) for i in range(4)])  20.3 us
    ppermute x3, starting transfers between devices, swap(): return lax.ppermute(value, 'c', [(0, 1), (1, 0)])  13.7 us
    unnamed x42, local copies, waits for them, and re-layouts  10.5 us
    all_to_all x1, starting transfers between devices, shards(): rows = lax.all_to_all(pay_y, 'y', 0, 0, tiled=True)  9.43 us
    ppermute x3, starting transfers between devices, shards(): lax.ppermute(near[k], NEAR, [(i, i ^ k) for i in range(4)])  9.26 us
    all_to_all x1, starting transfers between devices, shards(): far = lax.all_to_all(pay_a, 'a', 0, 0, tiled=True)  9.19 us
  transfers between devices with their start and end apart: 17, of which 6 were waited for; matrix products, arithmetic and copies ran while one was open for 0% of the time, Pallas kernels for 13%

profile of v16, /device:TPU:1, one launch (start us, length us, event | category | flops | bytes accessed | tf_op | source)
XLA Modules:
  0.0 164.7 jit_solution(13093173084816768836)
XLA Ops:
  7.3 8.8 %collective-permute-start = (bf16[32,512]{1,0:T(8,128)(2,1)S(1)}, bf16[32,512]{1,0:T(8,128)(2,1)S(1)}, u32[]{:S(2)}, u32[]{:S(2)}) collective-permute-start(bf16[32,512]{1,0:T(8,128)(2,1)S(1)} %constant_dynamic-slice_fusion), channel_id=1, source_target_pairs={{0,4},{4,0},{1,5},{5,1},{2,6},{6,2},{3,7},{7,3},{8,12},{12,8},{9,1... | collective-permute-start | bytes 98312 | tf_op jit(solution)/shard_map/ppermute | solution.py:21
  19.0 3.8 %shard_map.82 = (bf16[1072,512]{1,0:T(8,128)(2,1)}, bf16[1072,512]{1,0:T(8,128)(2,1)}) custom-call(s32[5]{0:T(128)} %stack.23.refs_0_, bf16[256,1024]{1,0:T(8,128)(2,1)} %refs_1_.1, bf16[256,1024]{1,0:T(8,128)(2,1)} %refs_2_.1, bf16[256,1024]{1,0:T(8,128)(2,1)} %refs_3_.1, bf16[256,1024]{1,0:T(8,128)(2,1)} %refs_4_.1, f32[8,256]{1,0:T(8,128)} %refs_5_.1, ...), custom_call_target="tpu_custom_call" | custom-call | flops 1000000 | bytes 1000000 | tf_op jit(solution)/shard_map/pallas_call | solution.py:59
  22.8 2.3 %collective-permute-start.2 = (bf16[1072,512]{1,0:T(8,128)(2,1)}, bf16[1072,512]{1,0:T(8,128)(2,1)S(1)}, u32[]{:S(2)}, u32[]{:S(2)}) collective-permute-start(bf16[1072,512]{1,0:T(8,128)(2,1)} %get-tuple-element.26), channel_id=1, source_target_pairs={{0,4},{4,0},{1,5},{5,1},{2,6},{6,2},{3,7},{7,3},{8,12},{12,8},{9,1... | collective-permute-start | bytes 3293192 | tf_op jit(solution)/shard_map/ppermute | solution.py:21
  25.1 2.5 %collective-permute-done.2.refs_2_ = bf16[1072,512]{1,0:T(8,128)(2,1)S(1)} collective-permute-done((bf16[1072,512]{1,0:T(8,128)(2,1)}, bf16[1072,512]{1,0:T(8,128)(2,1)S(1)}, u32[]{:S(2)}, u32[]{:S(2)}) %collective-permute-start.2) | collective-permute-done | bytes 1097760 | tf_op jit(solution)/shard_map/ppermute | solution.py:21
  30.7 8.6 %all_to_all.20.refs_1_ = bf16[4,144,128]{2,1,0:T(8,128)(2,1)S(1)} all-to-all(bf16[4,144,128]{2,1,0:T(8,128)(2,1)S(1)} %get-tuple-element.30), channel_id=1, replica_groups=mesh['y'=4,'a'=4,'p'=2,'q'=2,'c'=2,'x'=4] {'p','q'}, dimensions={0} | all-to-all | bytes 294912 | tf_op jit(solution)/shard_map/all_to_all | solution.py:314
  41.2 9.2 %all-to-all-start.1 = ((bf16[4,144,128]{2,1,0:T(8,128)(2,1)}), bf16[4,144,128]{2,1,0:T(8,128)(2,1)S(1)}, u32[]{:S(2)}, u32[]{:S(2)}) async-start(bf16[4,144,128]{2,1,0:T(8,128)(2,1)} %get-tuple-element.37), calls=%async_computation.1 | async-start | bytes 294912 | tf_op jit(solution)/shard_map/all_to_all | solution.py:316
  50.3 2.4 %collective-permute-start.3 = (bf16[144,256]{1,0:T(8,128)(2,1)S(1)}, bf16[144,256]{1,0:T(8,128)(2,1)S(1)}, u32[]{:S(2)}, u32[]{:S(2)}) collective-permute-start(bf16[144,256]{1,0:T(8,128)(2,1)S(1)} %get-tuple-element.32), channel_id=1, source_target_pairs={{0,8},{8,0},{16,24},{24,16},{1,9},{9,1},{17,25},{25,17},{2,10},{10... | collective-permute-start | bytes 221192 | tf_op jit(solution)/shard_map/ppermute | solution.py:318
  52.7 4.0 %collective-permute-start.4 = (bf16[144,256]{1,0:T(8,128)(2,1)S(1)}, bf16[144,256]{1,0:T(8,128)(2,1)S(1)}, u32[]{:S(2)}, u32[]{:S(2)}) collective-permute-start(bf16[144,256]{1,0:T(8,128)(2,1)S(1)} %get-tuple-element.33), channel_id=1, source_target_pairs={{0,16},{8,24},{16,0},{24,8},{1,17},{9,25},{17,1},{25,9},{2,18},{10... | collective-permute-start | bytes 221192 | tf_op jit(solution)/shard_map/ppermute | solution.py:318
  56.7 2.9 %collective-permute-start.5 = (bf16[144,256]{1,0:T(8,128)(2,1)S(1)}, bf16[144,256]{1,0:T(8,128)(2,1)S(1)}, u32[]{:S(2)}, u32[]{:S(2)}) collective-permute-start(bf16[144,256]{1,0:T(8,128)(2,1)S(1)} %get-tuple-element.34), channel_id=1, source_target_pairs={{0,24},{8,16},{16,8},{24,0},{1,25},{9,17},{17,9},{25,1},{2,26},{10... | collective-permute-start | bytes 221192 | tf_op jit(solution)/shard_map/ppermute | solution.py:318
  62.1 4.6 %collective-permute-done.5.refs_8_.refs_4_ = bf16[144,256]{1,0:T(8,128)(2,1)S(1)} collective-permute-done((bf16[144,256]{1,0:T(8,128)(2,1)S(1)}, bf16[144,256]{1,0:T(8,128)(2,1)S(1)}, u32[]{:S(2)}, u32[]{:S(2)}) %collective-permute-start.5) | collective-permute-done | bytes 73760 | tf_op jit(solution)/shard_map/ppermute | solution.py:318
  68.6 9.4 %all-to-all-start.2 = ((bf16[4,144,128]{2,1,0:T(8,128)(2,1)}), bf16[4,144,128]{2,1,0:T(8,128)(2,1)S(1)}, u32[]{:S(2)}, u32[]{:S(2)}) async-start(bf16[4,144,128]{2,1,0:T(8,128)(2,1)} %get-tuple-element.38), calls=%async_computation.2 | async-start | bytes 294912 | tf_op jit(solution)/shard_map/all_to_all | solution.py:329
  79.0 4.3 %shard_map.84 = (f32[512,512]{1,0:T(8,128)S(1)}, f32[512,24]{1,0:T(8,128)S(1)}) custom-call(s32[5]{0:T(128)S(1)} %copy-done.18, bf16[1072,512]{1,0:T(8,128)(2,1)S(1)} %copy-done.1, bf16[1072,512]{1,0:T(8,128)(2,1)S(1)} %collective-permute-done.2.refs_2_, bf16[4,128,128]{2,1,0:T(8,128)(2,1)S(1)} %copy-done.13), custom_call_target="tpu_custom_call" | custom-call | flops 1000000 | bytes 1000000 | tf_op jit(solution)/shard_map/pallas_call | solution.py:59
  86.3 5.6 %all-to-all-start.3 = ((bf16[4,128,512]{2,1,0:T(8,128)(2,1)}), bf16[4,128,512]{2,1,0:T(8,128)(2,1)}, u32[]{:S(2)}, u32[]{:S(2)}) async-start(bf16[4,128,512]{2,1,0:T(8,128)(2,1)} %copy-done.3), calls=%async_computation.3 | async-start | bytes 1048576 | tf_op jit(solution)/shard_map/all_to_all | solution.py:333
  96.2 4.9 %collective-permute-start.11 = (bf16[16,64,512]{2,1,0:T(8,128)(2,1)}, bf16[16,64,512]{2,1,0:T(8,128)(2,1)S(1)}, u32[]{:S(2)}, u32[]{:S(2)}) collective-permute-start(bf16[16,64,512]{2,1,0:T(8,128)(2,1)} %bitcast.6), channel_id=1, source_target_pairs={{0,256},{128,384},{256,0},{384,128},{1,257},{129,385},{257,1},{385... | collective-permute-start | bytes 3145736 | tf_op jit(solution)/shard_map/ppermute | solution.py:282
  101.1 2.2 %collective-permute-start.10 = (bf16[16,64,512]{2,1,0:T(8,128)(2,1)}, bf16[16,64,512]{2,1,0:T(8,128)(2,1)}, u32[]{:S(2)}, u32[]{:S(2)}) collective-permute-start(bf16[16,64,512]{2,1,0:T(8,128)(2,1)} %bitcast.7), channel_id=1, source_target_pairs={{0,128},{128,256},{256,384},{384,0},{1,129},{129,257},{257,385},{3... | collective-permute-start | bytes 3145736 | tf_op jit(solution)/shard_map/ppermute | solution.py:282
  103.3 4.3 %collective-permute-start.9 = (bf16[16,64,512]{2,1,0:T(8,128)(2,1)}, bf16[16,64,512]{2,1,0:T(8,128)(2,1)}, u32[]{:S(2)}, u32[]{:S(2)}) collective-permute-start(bf16[16,64,512]{2,1,0:T(8,128)(2,1)} %bitcast.8), channel_id=1, source_target_pairs={{0,384},{128,0},{256,128},{384,256},{1,385},{129,1},{257,129},{385... | collective-permute-start | bytes 3145736 | tf_op jit(solution)/shard_map/ppermute | solution.py:282
  109.8 3.1 %shard_map.89.refs_1_ = bf16[512,512]{1,0:T(8,128)(2,1)S(1)} custom-call(s32[5]{0:T(128)S(1)} %copy-done.18, bf16[1072,512]{1,0:T(8,128)(2,1)S(1)} %copy-done.1, bf16[1072,512]{1,0:T(8,128)(2,1)S(1)} %collective-permute-done.2.refs_2_, bf16[1,1024]{1,0:T(2,128)(2,1)S(1)} %broadcast_in_dim.3.refs_3_, f32[512,512]{1,0:T(8,128)S(1)} %copy-done.5, ...), custom_call_target="tpu_custom_call" | custom-call | flops 1000000 | bytes 1000000 | tf_op jit(solution)/shard_map/pallas_call | solution.py:59
  112.9 4.1 %collective-permute-start.8 = (bf16[512,512]{1,0:T(8,128)(2,1)S(1)}, bf16[512,512]{1,0:T(8,128)(2,1)S(1)}, u32[]{:S(2)}, u32[]{:S(2)}) collective-permute-start(bf16[512,512]{1,0:T(8,128)(2,1)S(1)} %shard_map.89.refs_1_), channel_id=1, source_target_pairs={{0,3},{1,0},{2,1},{3,2},{4,7},{5,4},{6,5},{7,6},{8,11},{9,8},{10,9... | collective-permute-start | bytes 1572872 | tf_op jit(solution)/shard_map/ppermute | solution.py:282
  117.0 2.1 %collective-permute-start.7 = (bf16[512,512]{1,0:T(8,128)(2,1)S(1)}, bf16[512,512]{1,0:T(8,128)(2,1)S(1)}, u32[]{:S(2)}, u32[]{:S(2)}) collective-permute-start(bf16[512,512]{1,0:T(8,128)(2,1)S(1)} %shard_map.89.refs_1_), channel_id=1, source_target_pairs={{0,2},{1,3},{2,0},{3,1},{4,6},{5,7},{6,4},{7,5},{8,10},{9,11},{10,... | collective-permute-start | bytes 1572872 | tf_op jit(solution)/shard_map/ppermute | solution.py:282
  119.1 2.8 %collective-permute-start.6 = (bf16[512,512]{1,0:T(8,128)(2,1)S(1)}, bf16[512,512]{1,0:T(8,128)(2,1)S(1)}, u32[]{:S(2)}, u32[]{:S(2)}) collective-permute-start(bf16[512,512]{1,0:T(8,128)(2,1)S(1)} %shard_map.89.refs_1_), channel_id=1, source_target_pairs={{0,1},{1,2},{2,3},{3,0},{4,5},{5,6},{6,7},{7,4},{8,9},{9,10},{10,1... | collective-permute-start | bytes 1572872 | tf_op jit(solution)/shard_map/ppermute | solution.py:282
  121.9 25.6 %collective-permute-done.10.refs_7_ = bf16[16,64,512]{2,1,0:T(8,128)(2,1)} collective-permute-done((bf16[16,64,512]{2,1,0:T(8,128)(2,1)}, bf16[16,64,512]{2,1,0:T(8,128)(2,1)}, u32[]{:S(2)}, u32[]{:S(2)}) %collective-permute-start.10) | collective-permute-done | bytes 1048608 | tf_op jit(solution)/shard_map/ppermute | solution.py:282
  147.5 3.3 %shard_map.91 = bf16[256,1024]{1,0:T(8,128)(2,1)S(1)} custom-call(s32[5]{0:T(128)S(1)} %copy-done.18, bf16[512,512]{1,0:T(8,128)(2,1)S(1)} %shard_map.89.refs_1_, bf16[512,512]{1,0:T(8,128)(2,1)S(1)} %collective-permute-done.6.refs_2_, bf16[512,512]{1,0:T(8,128)(2,1)S(1)} %collective-permute-done.7.refs_3_, ...), custom_call_target="tpu_custom_call" | custom-call | flops 1000000 | bytes 1000000 | tf_op jit(solution)/shard_map/pallas_call | solution.py:59
  150.8 2.7 %collective-permute-start.12 = (bf16[256,1024]{1,0:T(8,128)(2,1)S(1)}, bf16[256,1024]{1,0:T(8,128)(2,1)S(1)}, u32[]{:S(2)}, u32[]{:S(2)}) collective-permute-start(bf16[256,1024]{1,0:T(8,128)(2,1)S(1)} %shard_map.91), channel_id=1, source_target_pairs={{0,4},{4,0},{1,5},{5,1},{2,6},{6,2},{3,7},{7,3},{8,12},{12,8},{9,1... | collective-permute-start | bytes 1572872 | tf_op jit(solution)/shard_map/ppermute | solution.py:21
  153.5 3.3 %shard_map.90 = f32[256,1024]{1,0:T(8,128)S(1)} custom-call(s32[5]{0:T(128)S(1)} %copy-done.18, bf16[512,512]{1,0:T(8,128)(2,1)S(1)} %shard_map.89.refs_1_, bf16[512,512]{1,0:T(8,128)(2,1)S(1)} %collective-permute-done.6.refs_2_, bf16[512,512]{1,0:T(8,128)(2,1)S(1)} %collective-permute-done.7.refs_3_, bf16[512,512]{1,0:T(8,128)(2,1)S(1)} %collective-permute-done.8.refs_4_, ...), custom_call_target="tpu_custom_call" | custom-call | flops 1000000 | bytes 1000000 | tf_op jit(solution)/shard_map/pallas_call | solution.py:59
  (70 shorter events, 24.2 us)
Async XLA Ops:
  6.5 89.7 %all-gather.3.cloned.1.call-start = ((), (), s32[]{:S(2)}) async-start(), calls=%async_computation.4 | async-start | bytes 1114112 | tf_op jit(solution)/shard_map/all_gather | solution.py:309
  7.3 9.6 %collective-permute-start = (bf16[32,512]{1,0:T(8,128)(2,1)S(1)}, bf16[32,512]{1,0:T(8,128)(2,1)S(1)}, u32[]{:S(2)}, u32[]{:S(2)}) collective-permute-start(bf16[32,512]{1,0:T(8,128)(2,1)S(1)} %constant_dynamic-slice_fusion), channel_id=1, source_target_pairs={{0,4},{4,0},{1,5},{5,1},{2,6},{6,2},{3,7},{7,3},{8,12},{12,8},{9,1... | collective-permute-start | bytes 98312 | tf_op jit(solution)/shard_map/ppermute | solution.py:21
  17.7 5.1 %collective-permute-start.1 = (bf16[64,512]{1,0:T(8,128)(2,1)S(1)}, bf16[64,512]{1,0:T(8,128)(2,1)S(1)}, u32[]{:S(2)}, u32[]{:S(2)}) collective-permute-start(bf16[64,512]{1,0:T(8,128)(2,1)S(1)} %pad_maximum_fusion), channel_id=1, source_target_pairs={{0,0},{1,128},{2,256},{3,384},{128,1},{129,129},{130,257},{131,385... | collective-permute-start | bytes 196616 | tf_op jit(solution)/shard_map/ppermute | solution.py:294
  19.0 8.6 %copy-start.18 = (s32[5]{0:T(128)S(1)}, s32[5]{0:T(128)}, u32[]{:S(2)}) copy-start(s32[5]{0:T(128)} %stack.23.refs_0_) | copy-start | bytes 64
  22.8 4.8 %collective-permute-start.2 = (bf16[1072,512]{1,0:T(8,128)(2,1)}, bf16[1072,512]{1,0:T(8,128)(2,1)S(1)}, u32[]{:S(2)}, u32[]{:S(2)}) collective-permute-start(bf16[1072,512]{1,0:T(8,128)(2,1)} %get-tuple-element.26), channel_id=1, source_target_pairs={{0,4},{4,0},{1,5},{5,1},{2,6},{6,2},{3,7},{7,3},{8,12},{12,8},{9,1... | collective-permute-start | bytes 3293192 | tf_op jit(solution)/shard_map/ppermute | solution.py:21
  30.6 9.9 %copy-start.12 = (bf16[4,128,128]{2,1,0:T(8,128)(2,1)}, bf16[4,128,128]{2,1,0:T(8,128)(2,1)S(1)}, u32[]{:S(2)}) copy-start(bf16[4,128,128]{2,1,0:T(8,128)(2,1)S(1)} %get-tuple-element.27.refs_3_) | copy-start | bytes 393220
  30.7 47.4 %copy-start.1 = (bf16[1072,512]{1,0:T(8,128)(2,1)S(1)}, bf16[1072,512]{1,0:T(8,128)(2,1)}, u32[]{:S(2)}) copy-start(bf16[1072,512]{1,0:T(8,128)(2,1)} %get-tuple-element.24.refs_1_) | copy-start | bytes 3293188
  41.2 25.6 %all-to-all-start.1 = ((bf16[4,144,128]{2,1,0:T(8,128)(2,1)}), bf16[4,144,128]{2,1,0:T(8,128)(2,1)S(1)}, u32[]{:S(2)}, u32[]{:S(2)}) async-start(bf16[4,144,128]{2,1,0:T(8,128)(2,1)} %get-tuple-element.37), calls=%async_computation.1 | async-start | bytes 294912 | tf_op jit(solution)/shard_map/all_to_all | solution.py:316
  50.3 11.0 %collective-permute-start.3 = (bf16[144,256]{1,0:T(8,128)(2,1)S(1)}, bf16[144,256]{1,0:T(8,128)(2,1)S(1)}, u32[]{:S(2)}, u32[]{:S(2)}) collective-permute-start(bf16[144,256]{1,0:T(8,128)(2,1)S(1)} %get-tuple-element.32), channel_id=1, source_target_pairs={{0,8},{8,0},{16,24},{24,16},{1,9},{9,1},{17,25},{25,17},{2,10},{10... | collective-permute-start | bytes 221192 | tf_op jit(solution)/shard_map/ppermute | solution.py:318
  52.7 9.4 %collective-permute-start.4 = (bf16[144,256]{1,0:T(8,128)(2,1)S(1)}, bf16[144,256]{1,0:T(8,128)(2,1)S(1)}, u32[]{:S(2)}, u32[]{:S(2)}) collective-permute-start(bf16[144,256]{1,0:T(8,128)(2,1)S(1)} %get-tuple-element.33), channel_id=1, source_target_pairs={{0,16},{8,24},{16,0},{24,8},{1,17},{9,25},{17,1},{25,9},{2,18},{10... | collective-permute-start | bytes 221192 | tf_op jit(solution)/shard_map/ppermute | solution.py:318
  56.7 10.1 %collective-permute-start.5 = (bf16[144,256]{1,0:T(8,128)(2,1)S(1)}, bf16[144,256]{1,0:T(8,128)(2,1)S(1)}, u32[]{:S(2)}, u32[]{:S(2)}) collective-permute-start(bf16[144,256]{1,0:T(8,128)(2,1)S(1)} %get-tuple-element.34), channel_id=1, source_target_pairs={{0,24},{8,16},{16,8},{24,0},{1,25},{9,17},{17,9},{25,1},{2,26},{10... | collective-permute-start | bytes 221192 | tf_op jit(solution)/shard_map/ppermute | solution.py:318
  66.7 11.3 %copy-start.6 = (bf16[144,256]{1,0:T(8,128)(2,1)}, bf16[144,256]{1,0:T(8,128)(2,1)S(1)}, u32[]{:S(2)}) copy-start(bf16[144,256]{1,0:T(8,128)(2,1)S(1)} %collective-permute-done.5.refs_8_.refs_4_) | copy-start | bytes 221188
  68.6 15.4 %all-to-all-start.2 = ((bf16[4,144,128]{2,1,0:T(8,128)(2,1)}), bf16[4,144,128]{2,1,0:T(8,128)(2,1)S(1)}, u32[]{:S(2)}, u32[]{:S(2)}) async-start(bf16[4,144,128]{2,1,0:T(8,128)(2,1)} %get-tuple-element.38), calls=%async_computation.2 | async-start | bytes 294912 | tf_op jit(solution)/shard_map/all_to_all | solution.py:329
  86.3 5.6 %copy-start.15 = (bf16[144,256]{1,0:T(8,128)(2,1)S(1)}, bf16[144,256]{1,0:T(8,128)(2,1)}, u32[]{:S(2)}) copy-start(bf16[144,256]{1,0:T(8,128)(2,1)} %copy-done.14) | copy-start | bytes 221188
  86.3 21.3 %all-to-all-start.3 = ((bf16[4,128,512]{2,1,0:T(8,128)(2,1)}), bf16[4,128,512]{2,1,0:T(8,128)(2,1)}, u32[]{:S(2)}, u32[]{:S(2)}) async-start(bf16[4,128,512]{2,1,0:T(8,128)(2,1)} %copy-done.3), calls=%async_computation.3 | async-start | bytes 1048576 | tf_op jit(solution)/shard_map/all_to_all | solution.py:333
  92.8 14.8 %copy-start.20 = (bf16[1024]{0:T(1024)(128)(2,1)S(1)}, bf16[1024]{0:T(1024)(128)(2,1)}, u32[]{:S(2)}) copy-start(bf16[1024]{0:T(1024)(128)(2,1)} %param.14) | copy-start | bytes 6148
  96.2 22.9 %collective-permute-start.11 = (bf16[16,64,512]{2,1,0:T(8,128)(2,1)}, bf16[16,64,512]{2,1,0:T(8,128)(2,1)S(1)}, u32[]{:S(2)}, u32[]{:S(2)}) collective-permute-start(bf16[16,64,512]{2,1,0:T(8,128)(2,1)} %bitcast.6), channel_id=1, source_target_pairs={{0,256},{128,384},{256,0},{384,128},{1,257},{129,385},{257,1},{385... | collective-permute-start | bytes 3145736 | tf_op jit(solution)/shard_map/ppermute | solution.py:282
  101.1 46.4 %collective-permute-start.10 = (bf16[16,64,512]{2,1,0:T(8,128)(2,1)}, bf16[16,64,512]{2,1,0:T(8,128)(2,1)}, u32[]{:S(2)}, u32[]{:S(2)}) collective-permute-start(bf16[16,64,512]{2,1,0:T(8,128)(2,1)} %bitcast.7), channel_id=1, source_target_pairs={{0,128},{128,256},{256,384},{384,0},{1,129},{129,257},{257,385},{3... | collective-permute-start | bytes 3145736 | tf_op jit(solution)/shard_map/ppermute | solution.py:282
  103.3 44.2 %collective-permute-start.9 = (bf16[16,64,512]{2,1,0:T(8,128)(2,1)}, bf16[16,64,512]{2,1,0:T(8,128)(2,1)}, u32[]{:S(2)}, u32[]{:S(2)}) collective-permute-start(bf16[16,64,512]{2,1,0:T(8,128)(2,1)} %bitcast.8), channel_id=1, source_target_pairs={{0,384},{128,0},{256,128},{384,256},{1,385},{129,1},{257,129},{385... | collective-permute-start | bytes 3145736 | tf_op jit(solution)/shard_map/ppermute | solution.py:282
  109.8 37.7 %copy-start.2 = (bf16[1024,512]{1,0:T(8,128)(2,1)S(1)}, bf16[1024,512]{1,0:T(8,128)(2,1)}, u32[]{:S(2)}) copy-start(bf16[1024,512]{1,0:T(8,128)(2,1)} %all-gather.3.cloned.1.call-done) | copy-start | bytes 3145732
  112.9 34.6 %collective-permute-start.8 = (bf16[512,512]{1,0:T(8,128)(2,1)S(1)}, bf16[512,512]{1,0:T(8,128)(2,1)S(1)}, u32[]{:S(2)}, u32[]{:S(2)}) collective-permute-start(bf16[512,512]{1,0:T(8,128)(2,1)S(1)} %shard_map.89.refs_1_), channel_id=1, source_target_pairs={{0,3},{1,0},{2,1},{3,2},{4,7},{5,4},{6,5},{7,6},{8,11},{9,8},{10,9... | collective-permute-start | bytes 1572872 | tf_op jit(solution)/shard_map/ppermute | solution.py:282
  117.0 30.5 %collective-permute-start.7 = (bf16[512,512]{1,0:T(8,128)(2,1)S(1)}, bf16[512,512]{1,0:T(8,128)(2,1)S(1)}, u32[]{:S(2)}, u32[]{:S(2)}) collective-permute-start(bf16[512,512]{1,0:T(8,128)(2,1)S(1)} %shard_map.89.refs_1_), channel_id=1, source_target_pairs={{0,2},{1,3},{2,0},{3,1},{4,6},{5,7},{6,4},{7,5},{8,10},{9,11},{10,... | collective-permute-start | bytes 1572872 | tf_op jit(solution)/shard_map/ppermute | solution.py:282
  119.1 28.4 %collective-permute-start.6 = (bf16[512,512]{1,0:T(8,128)(2,1)S(1)}, bf16[512,512]{1,0:T(8,128)(2,1)S(1)}, u32[]{:S(2)}, u32[]{:S(2)}) collective-permute-start(bf16[512,512]{1,0:T(8,128)(2,1)S(1)} %shard_map.89.refs_1_), channel_id=1, source_target_pairs={{0,1},{1,2},{2,3},{3,0},{4,5},{5,6},{6,7},{7,4},{8,9},{9,10},{10,1... | collective-permute-start | bytes 1572872 | tf_op jit(solution)/shard_map/ppermute | solution.py:282
  150.8 6.0 %collective-permute-start.12 = (bf16[256,1024]{1,0:T(8,128)(2,1)S(1)}, bf16[256,1024]{1,0:T(8,128)(2,1)S(1)}, u32[]{:S(2)}, u32[]{:S(2)}) collective-permute-start(bf16[256,1024]{1,0:T(8,128)(2,1)S(1)} %shard_map.91), channel_id=1, source_target_pairs={{0,4},{4,0},{1,5},{5,1},{2,6},{6,2},{3,7},{7,3},{8,12},{12,8},{9,1... | collective-permute-start | bytes 1572872 | tf_op jit(solution)/shard_map/ppermute | solution.py:21
  (14 other events, 18.4 us)
Sparse Core Ops, SparseCore 0:
  25.2 67.8 all-gather.2

commit v17 on v16

--- a/solution.py
+++ b/solution.py
@@ -246,34 +246,32 @@
             normed[here, hc] = (gated * size * gain[:, mine].astype(F32)).astype(BF)
 
 
-def project_body(other, at, b0, b1, b2, b3, w0, w1, w2, w3, out, left, right, sems):
+def project_body(other, at, b0, b1, b2, b3, weights, out, left, right, sems):
     row = (1 - at[0]) if other else at[0]
     rows = pl.ds(pl.multiple_of(row * 256, 256), 256)
-    copies = [
-        pltpu.make_async_copy(w, right.at[k], sems.at[k]) for k, w in enumerate((w0, w1, w2, w3))
-    ]
+    copies = [pltpu.make_async_copy(weights.at[f], right.at[f], sems.at[f]) for f in range(4)]
     for copy in copies:
         copy.start()
     for j, block in enumerate((b0, b1, b2, b3)):
         left[(at[4] + 4 - j) % 4] = block[rows, :]
     total = 0.0
-    for k, turn in enumerate((0, 1, 3, 2)):
-        copies[k].wait()
-        total += dot(left[(at[3] + turn) % 4], right[k].reshape(1024, 512), NT)
+    for f in range(4):
+        copies[f].wait()
+        total += dot(left[f], right[f].reshape(1024, 512), NT)
     out[...] = total.astype(out.dtype)
 
 
-def project(at, blocks, rights, other):
+def project(at, blocks, weights, other):
     return call(
         functools.partial(project_body, other),
         [((256, 1024), BF if other else F32)],
-        (at, *blocks, *rights),
+        (at, *blocks, weights),
         scratch=[
             pltpu.VMEM((4, 256, 512), BF),
             pltpu.VMEM((4, 16, 64, 512), BF),
             pltpu.SemaphoreType.DMA((4,)),
         ],
-        hbm=range(5, 9),
+        hbm=(5,),
         vmem=20,
     )[0]
 
@@ -305,7 +303,6 @@
         hbm=range(1, 7),
         vmem=60,
     )
-    mine, send = lax.optimization_barrier((mine, send))
     gathered = lax.all_gather(mine, ("a", "p", "q"))
 
     got = swap(send)
@@ -327,9 +324,7 @@
         unread=near[1:],
     )
     rows = lax.all_to_all(pay_y, "y", 0, 0, tiled=True)
-    (states,) = call(
-        last_body, [((4, 128, 512), BF)], (at, rows, before, far), unread=(mixture,)
-    )
+    (states,) = call(last_body, [((4, 128, 512), BF)], (at, rows, before, far))
     states = lax.all_to_all(states, NEAR, 0, 0, tiled=True)
     mixture, coef = call(
         mix_body,
@@ -338,14 +333,15 @@
         scratch=[pltpu.VMEM((4, 144, 256), BF)],
     )
     _, gathered = lax.optimization_barrier((coef, gathered))
-    rights = [gathered] + [shift(gathered, "y", 4 - k) for k in (1, 3, 2)]
+    gathered = jnp.broadcast_to(gathered[None], (4, 16, 64, 512))
+    weights = lax.all_to_all(gathered, "y", 0, 0, tiled=True)
     (normed,) = call(
         norm_body, [((512, 512), BF)], (at, keep, got, norm_gain[None], mixture, coef, states)
     )
 
     blocks = [normed] + [shift(normed, "x", j) for j in (1, 2, 3)]
-    theirs = swap(project(at, blocks, rights, True))
-    own = project(at, blocks, rights, False)
+    theirs = swap(project(at, blocks, weights, True))
+    own = project(at, blocks, weights, False)
     return (own + theirs.astype(F32)).astype(BF)
 
 

time: 166 us -> 199 us (1.20)
  waiting for transfers between devices: 36.1 us -> 67.7 us
  blocking collectives: 8.61 us -> 17.6 us
  starting transfers between devices: 68.2 us -> 63.6 us
  local copies, waits for them, and re-layouts: 11.9 us -> 9.09 us
    all_gather x1, waiting for transfers between devices: 0.01 us -> 31.3 us  [shards(): gathered = lax.all_gather(mine, ('a', 'p', 'q'))]
    all_to_all x1 -> x2, waiting for transfers between devices: 0.01 us -> 15.6 us  [the longest x1 13.9 us: shards(): weights = lax.all_to_all(gathered, 'y', 0, 0, tiled=True)]
    ppermute x6 -> x3, waiting for transfers between devices: 25.6 us -> 12.6 us  [shift(): return lax.ppermute(value, axis, [(i, (i + by) % 4) for i in range(4)])]
    ppermute x6 -> x3, starting transfers between devices: 20.3 us -> 9.11 us  [shift(): return lax.ppermute(value, axis, [(i, (i + by) % 4) for i in range(4)])]
    ppermute x3, starting transfers between devices: 13.7 us -> 23.3 us  [swap(): return lax.ppermute(value, 'c', [(0, 1), (1, 0)])]
    all_to_all x1, blocking collectives: 8.61 us -> 17.6 us  [shards(): rows = lax.all_to_all(pay_y, 'y', 0, 0, tiled=True)]
    unnamed x42 -> x20, local copies, waits for them, and re-layouts: 10.5 us -> 4.72 us
    broadcast_in_dim x0 -> x1, local copies, waits for them, and re-layouts: none -> 3.76 us  [shards(): gathered = jnp.broadcast_to(gathered[None], (4, 16, 64, 512))]
  transfers between devices with their start and end apart: 17 -> 15, of which waited for: 6 -> 9; matrix products, arithmetic and copies ran while one was open for 0% -> 0% of each run, Pallas kernels for 13% -> 7%
where the time goes in v17:
time: 199 us; the launch traced here: 198 us
  waiting for transfers between devices  67.7 us (34%)
  starting transfers between devices  63.6 us (32%)
  Pallas kernels  25.2 us (13%)
  blocking collectives  17.6 us (9%)
  between operations  13.7 us (7%)
  local copies, waits for them, and re-layouts  9.09 us (5%)
    all_gather x1, waiting for transfers between devices, shards(): gathered = lax.all_gather(mine, ('a', 'p', 'q'))  31.3 us
    pallas_call x10, Pallas kernels, call(): pl.pallas_call(run, out_shape=[jax.ShapeDtypeStruct(*o) for o in outs], i...  25.2 us
    ppermute x3, starting transfers between devices, swap(): return lax.ppermute(value, 'c', [(0, 1), (1, 0)])  23.3 us
    all_to_all x1, blocking collectives, shards(): rows = lax.all_to_all(pay_y, 'y', 0, 0, tiled=True)  17.6 us
    all_to_all x1, waiting for transfers between devices, shards(): weights = lax.all_to_all(gathered, 'y', 0, 0, tiled=True)  13.9 us
    ppermute x3, waiting for transfers between devices, shift(): return lax.ppermute(value, axis, [(i, (i + by) % 4) for i in range(4)])  12.6 us
    all_to_all x1, starting transfers between devices, shards(): far = lax.all_to_all(pay_a, 'a', 0, 0, tiled=True)  9.43 us
    ppermute x3, starting transfers between devices, shards(): lax.ppermute(near[k], NEAR, [(i, i ^ k) for i in range(4)])  9.27 us
  transfers between devices with their start and end apart: 15, of which 9 were waited for; matrix products, arithmetic and copies ran while one was open for 0% of the time, Pallas kernels for 7%

profile of v17, /device:TPU:1, one launch (start us, length us, event | category | flops | bytes accessed | tf_op | source)
XLA Modules:
  0.0 197.9 jit_solution(17631938687155143091)
XLA Ops:
  7.1 3.8 %shard_map.82 = (bf16[1072,512]{1,0:T(8,128)(2,1)}, bf16[1072,512]{1,0:T(8,128)(2,1)}) custom-call(s32[5]{0:T(128)} %stack.23.refs_0_, bf16[256,1024]{1,0:T(8,128)(2,1)} %refs_1_.1, bf16[256,1024]{1,0:T(8,128)(2,1)} %refs_2_.1, bf16[256,1024]{1,0:T(8,128)(2,1)} %refs_3_.1, bf16[256,1024]{1,0:T(8,128)(2,1)} %refs_4_.1, f32[8,256]{1,0:T(8,128)} %refs_5_.1, ...), custom_call_target="tpu_custom_call" | custom-call | flops 1000000 | bytes 1000000 | tf_op jit(solution)/shard_map/pallas_call | solution.py:59
  11.0 8.8 %collective-permute-start = (bf16[1072,512]{1,0:T(8,128)(2,1)}, bf16[1072,512]{1,0:T(8,128)(2,1)S(1)}, u32[]{:S(2)}, u32[]{:S(2)}) collective-permute-start(bf16[1072,512]{1,0:T(8,128)(2,1)} %get-tuple-element.23), channel_id=1, source_target_pairs={{0,4},{4,0},{1,5},{5,1},{2,6},{6,2},{3,7},{7,3},{8,12},{12,8},{9,1... | collective-permute-start | bytes 3293192 | tf_op jit(solution)/shard_map/ppermute | solution.py:21
  19.8 2.5 %collective-permute-done.refs_2_ = bf16[1072,512]{1,0:T(8,128)(2,1)S(1)} collective-permute-done((bf16[1072,512]{1,0:T(8,128)(2,1)}, bf16[1072,512]{1,0:T(8,128)(2,1)S(1)}, u32[]{:S(2)}, u32[]{:S(2)}) %collective-permute-start) | collective-permute-done | bytes 1097760 | tf_op jit(solution)/shard_map/ppermute | solution.py:21
  26.0 3.3 %all-to-all-start = ((bf16[4,144,128]{2,1,0:T(8,128)(2,1)}), bf16[4,144,128]{2,1,0:T(8,128)(2,1)S(1)}, u32[]{:S(2)}, u32[]{:S(2)}) async-start(bf16[4,144,128]{2,1,0:T(8,128)(2,1)} %get-tuple-element.27), calls=%async_computation | async-start | bytes 294912 | tf_op jit(solution)/shard_map/all_to_all | solution.py:311
  36.1 9.4 %all-to-all-start.1 = ((bf16[4,144,128]{2,1,0:T(8,128)(2,1)}), bf16[4,144,128]{2,1,0:T(8,128)(2,1)S(1)}, u32[]{:S(2)}, u32[]{:S(2)}) async-start(bf16[4,144,128]{2,1,0:T(8,128)(2,1)} %get-tuple-element.34), calls=%async_computation.1 | async-start | bytes 294912 | tf_op jit(solution)/shard_map/all_to_all | solution.py:313
  46.9 3.3 %collective-permute-start.1 = (bf16[144,256]{1,0:T(8,128)(2,1)S(1)}, bf16[144,256]{1,0:T(8,128)(2,1)S(1)}, u32[]{:S(2)}, u32[]{:S(2)}) collective-permute-start(bf16[144,256]{1,0:T(8,128)(2,1)S(1)} %get-tuple-element.29), channel_id=1, source_target_pairs={{0,8},{8,0},{16,24},{24,16},{1,9},{9,1},{17,25},{25,17},{2,10},{10... | collective-permute-start | bytes 221192 | tf_op jit(solution)/shard_map/ppermute | solution.py:315
  50.1 3.4 %collective-permute-start.2 = (bf16[144,256]{1,0:T(8,128)(2,1)S(1)}, bf16[144,256]{1,0:T(8,128)(2,1)S(1)}, u32[]{:S(2)}, u32[]{:S(2)}) collective-permute-start(bf16[144,256]{1,0:T(8,128)(2,1)S(1)} %get-tuple-element.30), channel_id=1, source_target_pairs={{0,16},{8,24},{16,0},{24,8},{1,17},{9,25},{17,1},{25,9},{2,18},{10... | collective-permute-start | bytes 221192 | tf_op jit(solution)/shard_map/ppermute | solution.py:315
  53.5 2.6 %collective-permute-start.3 = (bf16[144,256]{1,0:T(8,128)(2,1)S(1)}, bf16[144,256]{1,0:T(8,128)(2,1)S(1)}, u32[]{:S(2)}, u32[]{:S(2)}) collective-permute-start(bf16[144,256]{1,0:T(8,128)(2,1)S(1)} %get-tuple-element.31), channel_id=1, source_target_pairs={{0,24},{8,16},{16,8},{24,0},{1,25},{9,17},{17,9},{25,1},{2,26},{10... | collective-permute-start | bytes 221192 | tf_op jit(solution)/shard_map/ppermute | solution.py:315
  56.2 4.7 %collective-permute-done.2.refs_7_.refs_3_ = bf16[144,256]{1,0:T(8,128)(2,1)S(1)} collective-permute-done((bf16[144,256]{1,0:T(8,128)(2,1)S(1)}, bf16[144,256]{1,0:T(8,128)(2,1)S(1)}, u32[]{:S(2)}, u32[]{:S(2)}) %collective-permute-start.2) | collective-permute-done | bytes 73760 | tf_op jit(solution)/shard_map/ppermute | solution.py:315
  61.5 17.6 %all_to_all.25.refs_1_ = bf16[4,144,128]{2,1,0:T(8,128)(2,1)S(1)} all-to-all(bf16[4,144,128]{2,1,0:T(8,128)(2,1)S(1)} %get-tuple-element.35), channel_id=1, replica_groups=mesh['y'=4,'a'=4,'p'=2,'q'=2,'c'=2,'x'=4] {'y'}, dimensions={0} | all-to-all | bytes 294912 | tf_op jit(solution)/shard_map/all_to_all | solution.py:326
  80.5 3.5 %all-to-all-start.3 = ((bf16[4,128,512]{2,1,0:T(8,128)(2,1)}), bf16[4,128,512]{2,1,0:T(8,128)(2,1)S(1)}, u32[]{:S(2)}, u32[]{:S(2)}) async-start(bf16[4,128,512]{2,1,0:T(8,128)(2,1)} %shard_map.88), calls=%async_computation.3 | async-start | bytes 1048576 | tf_op jit(solution)/shard_map/all_to_all | solution.py:328
  84.0 4.3 %shard_map.84 = (f32[512,512]{1,0:T(8,128)S(1)}, f32[512,24]{1,0:T(8,128)S(1)}) custom-call(s32[5]{0:T(128)S(1)} %copy-done.6, bf16[1072,512]{1,0:T(8,128)(2,1)S(1)} %copy-done.1, bf16[1072,512]{1,0:T(8,128)(2,1)S(1)} %collective-permute-done.refs_2_, bf16[4,128,128]{2,1,0:T(8,128)(2,1)S(1)} %get-tuple-element.24.refs_3_), custom_call_target="tpu_custom_call" | custom-call | flops 1000000 | bytes 1000000 | tf_op jit(solution)/shard_map/pallas_call | solution.py:59
  91.1 31.3 %all-gather.3.cloned.1.call-done = bf16[1024,512]{1,0:T(8,128)(2,1)} async-done(((bf16[64,512]{1,0:T(8,128)(2,1)}), bf16[1024,512]{1,0:T(8,128)(2,1)}) %all-gather.3.cloned.1.call-update) | async-done | bytes 1048592 | tf_op jit(solution)/shard_map/all_gather | solution.py:306
  122.4 3.8 %broadcast_in_dim.10 = bf16[4,16,64,512]{3,2,1,0:T(8,128)(2,1)} broadcast(bf16[16,64,512]{2,1,0:T(8,128)(2,1)} %bitcast.6), dimensions={1,2,3} | broadcast | bytes 5242880 | tf_op jit(solution)/shard_map/broadcast_in_dim | solution.py:336
  126.2 5.0 %all-to-all-start.4 = ((bf16[4,16,64,512]{3,2,1,0:T(8,128)(2,1)}), bf16[4,16,64,512]{3,2,1,0:T(8,128)(2,1)}, u32[]{:S(2)}, u32[]{:S(2)}) async-start(bf16[4,16,64,512]{3,2,1,0:T(8,128)(2,1)} %broadcast_in_dim.10), calls=%async_computation.4 | async-start | bytes 8388608 | tf_op jit(solution)/shard_map/all_to_all | solution.py:337
  132.5 2.5 %shard_map.89.refs_1_ = bf16[512,512]{1,0:T(8,128)(2,1)S(1)} custom-call(s32[5]{0:T(128)S(1)} %copy-done.6, bf16[1072,512]{1,0:T(8,128)(2,1)S(1)} %copy-done.1, bf16[1072,512]{1,0:T(8,128)(2,1)S(1)} %collective-permute-done.refs_2_, bf16[1,1024]{1,0:T(2,128)(2,1)S(1)} %broadcast_in_dim.4.refs_3_, f32[512,512]{1,0:T(8,128)S(1)} %copy-done.3, ...), custom_call_target="tpu_custom_call" | custom-call | flops 1000000 | bytes 1000000 | tf_op jit(solution)/shard_map/pallas_call | solution.py:59
  135.0 4.0 %collective-permute-start.6 = (bf16[512,512]{1,0:T(8,128)(2,1)S(1)}, bf16[512,512]{1,0:T(8,128)(2,1)S(1)}, u32[]{:S(2)}, u32[]{:S(2)}) collective-permute-start(bf16[512,512]{1,0:T(8,128)(2,1)S(1)} %shard_map.89.refs_1_), channel_id=1, source_target_pairs={{0,3},{1,0},{2,1},{3,2},{4,7},{5,4},{6,5},{7,6},{8,11},{9,8},{10,9... | collective-permute-start | bytes 1572872 | tf_op jit(solution)/shard_map/ppermute | solution.py:280
  141.4 2.8 %collective-permute-start.4 = (bf16[512,512]{1,0:T(8,128)(2,1)S(1)}, bf16[512,512]{1,0:T(8,128)(2,1)S(1)}, u32[]{:S(2)}, u32[]{:S(2)}) collective-permute-start(bf16[512,512]{1,0:T(8,128)(2,1)S(1)} %shard_map.89.refs_1_), channel_id=1, source_target_pairs={{0,1},{1,2},{2,3},{3,0},{4,5},{5,6},{6,7},{7,4},{8,9},{9,10},{10,1... | collective-permute-start | bytes 1572872 | tf_op jit(solution)/shard_map/ppermute | solution.py:280
  144.1 5.9 %collective-permute-done.6.refs_4_ = bf16[512,512]{1,0:T(8,128)(2,1)S(1)} collective-permute-done((bf16[512,512]{1,0:T(8,128)(2,1)S(1)}, bf16[512,512]{1,0:T(8,128)(2,1)S(1)}, u32[]{:S(2)}, u32[]{:S(2)}) %collective-permute-start.6) | collective-permute-done | bytes 524320 | tf_op jit(solution)/shard_map/ppermute | solution.py:280
  150.5 6.2 %collective-permute-done.4.refs_2_ = bf16[512,512]{1,0:T(8,128)(2,1)S(1)} collective-permute-done((bf16[512,512]{1,0:T(8,128)(2,1)S(1)}, bf16[512,512]{1,0:T(8,128)(2,1)S(1)}, u32[]{:S(2)}, u32[]{:S(2)}) %collective-permute-start.4) | collective-permute-done | bytes 524320 | tf_op jit(solution)/shard_map/ppermute | solution.py:280
  156.8 13.9 %all-to-all-done.4.refs_5_ = bf16[4,16,64,512]{3,2,1,0:T(8,128)(2,1)} async-done(((bf16[4,16,64,512]{3,2,1,0:T(8,128)(2,1)}), bf16[4,16,64,512]{3,2,1,0:T(8,128)(2,1)}, u32[]{:S(2)}, u32[]{:S(2)}) %all-to-all-start.4) | async-done | bytes 4194336 | tf_op jit(solution)/shard_map/all_to_all | solution.py:337
  170.7 3.6 %shard_map.91 = bf16[256,1024]{1,0:T(8,128)(2,1)S(1)} custom-call(s32[5]{0:T(128)S(1)} %copy-done.6, bf16[512,512]{1,0:T(8,128)(2,1)S(1)} %shard_map.89.refs_1_, bf16[512,512]{1,0:T(8,128)(2,1)S(1)} %collective-permute-done.4.refs_2_, bf16[512,512]{1,0:T(8,128)(2,1)S(1)} %collective-permute-done.5.refs_3_, ...), custom_call_target="tpu_custom_call" | custom-call | flops 1000000 | bytes 1000000 | tf_op jit(solution)/shard_map/pallas_call | solution.py:59
  174.3 12.2 %collective-permute-start.9 = (bf16[256,1024]{1,0:T(8,128)(2,1)S(1)}, bf16[256,1024]{1,0:T(8,128)(2,1)S(1)}, u32[]{:S(2)}, u32[]{:S(2)}) collective-permute-start(bf16[256,1024]{1,0:T(8,128)(2,1)S(1)} %shard_map.91), channel_id=1, source_target_pairs={{0,4},{4,0},{1,5},{5,1},{2,6},{6,2},{3,7},{7,3},{8,12},{12,8},{9,1... | collective-permute-start | bytes 1572872 | tf_op jit(solution)/shard_map/ppermute | solution.py:21
  186.5 3.6 %shard_map.90 = f32[256,1024]{1,0:T(8,128)S(1)} custom-call(s32[5]{0:T(128)S(1)} %copy-done.6, bf16[512,512]{1,0:T(8,128)(2,1)S(1)} %shard_map.89.refs_1_, bf16[512,512]{1,0:T(8,128)(2,1)S(1)} %collective-permute-done.4.refs_2_, bf16[512,512]{1,0:T(8,128)(2,1)S(1)} %collective-permute-done.5.refs_3_, bf16[512,512]{1,0:T(8,128)(2,1)S(1)} %collective-permute-done.6.refs_4_, ...), custom_call_target="tpu_custom_call" | custom-call | flops 1000000 | bytes 1000000 | tf_op jit(solution)/shard_map/pallas_call | solution.py:59
  (45 shorter events, 22.1 us)
Async XLA Ops:
  7.1 15.2 %copy-start.6 = (s32[5]{0:T(128)S(1)}, s32[5]{0:T(128)}, u32[]{:S(2)}) copy-start(s32[5]{0:T(128)} %stack.23.refs_0_) | copy-start | bytes 64
  11.0 11.3 %collective-permute-start = (bf16[1072,512]{1,0:T(8,128)(2,1)}, bf16[1072,512]{1,0:T(8,128)(2,1)S(1)}, u32[]{:S(2)}, u32[]{:S(2)}) collective-permute-start(bf16[1072,512]{1,0:T(8,128)(2,1)} %get-tuple-element.23), channel_id=1, source_target_pairs={{0,4},{4,0},{1,5},{5,1},{2,6},{6,2},{3,7},{7,3},{8,12},{12,8},{9,1... | collective-permute-start | bytes 3293192 | tf_op jit(solution)/shard_map/ppermute | solution.py:21
  22.3 1.2 copy-start
  23.5 5.8 %copy-start.8 = (bf16[32,1024]{1,0:T(8,128)(2,1)S(1)}, bf16[32,1024]{1,0:T(8,128)(2,1)}, u32[]{:S(2)}) copy-start(bf16[32,1024]{1,0:T(8,128)(2,1)} %param.15) | copy-start | bytes 196612
  26.0 8.2 %all-to-all-start = ((bf16[4,144,128]{2,1,0:T(8,128)(2,1)}), bf16[4,144,128]{2,1,0:T(8,128)(2,1)S(1)}, u32[]{:S(2)}, u32[]{:S(2)}) async-start(bf16[4,144,128]{2,1,0:T(8,128)(2,1)} %get-tuple-element.27), calls=%async_computation | async-start | bytes 294912 | tf_op jit(solution)/shard_map/all_to_all | solution.py:311
  29.4 3.1 %collective-permute-start.7 = (bf16[32,512]{1,0:T(8,128)(2,1)S(1)}, bf16[32,512]{1,0:T(8,128)(2,1)S(1)}, u32[]{:S(2)}, u32[]{:S(2)}) collective-permute-start(bf16[32,512]{1,0:T(8,128)(2,1)S(1)} %constant_dynamic-slice_fusion), channel_id=1, source_target_pairs={{0,4},{4,0},{1,5},{5,1},{2,6},{6,2},{3,7},{7,3},{8,12},{12,8},{9,1... | collective-permute-start | bytes 98312 | tf_op jit(solution)/shard_map/ppermute | solution.py:21
  36.1 24.7 %all-to-all-start.1 = ((bf16[4,144,128]{2,1,0:T(8,128)(2,1)}), bf16[4,144,128]{2,1,0:T(8,128)(2,1)S(1)}, u32[]{:S(2)}, u32[]{:S(2)}) async-start(bf16[4,144,128]{2,1,0:T(8,128)(2,1)} %get-tuple-element.34), calls=%async_computation.1 | async-start | bytes 294912 | tf_op jit(solution)/shard_map/all_to_all | solution.py:313
  45.5 76.9 %all-gather.3.cloned.1.call-start = ((), (), s32[]{:S(2)}) async-start(), calls=%async_computation.5 | async-start | bytes 1114112 | tf_op jit(solution)/shard_map/all_gather | solution.py:306
  45.5 0.7 collective-permute-start.8
  46.2 0.6 copy-start.7
  46.9 9.3 %collective-permute-start.1 = (bf16[144,256]{1,0:T(8,128)(2,1)S(1)}, bf16[144,256]{1,0:T(8,128)(2,1)S(1)}, u32[]{:S(2)}, u32[]{:S(2)}) collective-permute-start(bf16[144,256]{1,0:T(8,128)(2,1)S(1)} %get-tuple-element.29), channel_id=1, source_target_pairs={{0,8},{8,0},{16,24},{24,16},{1,9},{9,1},{17,25},{25,17},{2,10},{10... | collective-permute-start | bytes 221192 | tf_op jit(solution)/shard_map/ppermute | solution.py:315
  50.1 10.7 %collective-permute-start.2 = (bf16[144,256]{1,0:T(8,128)(2,1)S(1)}, bf16[144,256]{1,0:T(8,128)(2,1)S(1)}, u32[]{:S(2)}, u32[]{:S(2)}) collective-permute-start(bf16[144,256]{1,0:T(8,128)(2,1)S(1)} %get-tuple-element.30), channel_id=1, source_target_pairs={{0,16},{8,24},{16,0},{24,8},{1,17},{9,25},{17,1},{25,9},{2,18},{10... | collective-permute-start | bytes 221192 | tf_op jit(solution)/shard_map/ppermute | solution.py:315
  53.5 7.3 %collective-permute-start.3 = (bf16[144,256]{1,0:T(8,128)(2,1)S(1)}, bf16[144,256]{1,0:T(8,128)(2,1)S(1)}, u32[]{:S(2)}, u32[]{:S(2)}) collective-permute-start(bf16[144,256]{1,0:T(8,128)(2,1)S(1)} %get-tuple-element.31), channel_id=1, source_target_pairs={{0,24},{8,16},{16,8},{24,0},{1,25},{9,17},{17,9},{25,1},{2,26},{10... | collective-permute-start | bytes 221192 | tf_op jit(solution)/shard_map/ppermute | solution.py:315
  61.5 22.5 %copy-start.1 = (bf16[1072,512]{1,0:T(8,128)(2,1)S(1)}, bf16[1072,512]{1,0:T(8,128)(2,1)}, u32[]{:S(2)}) copy-start(bf16[1072,512]{1,0:T(8,128)(2,1)} %get-tuple-element.22.refs_1_) | copy-start | bytes 3293188
  80.5 41.9 %all-to-all-start.3 = ((bf16[4,128,512]{2,1,0:T(8,128)(2,1)}), bf16[4,128,512]{2,1,0:T(8,128)(2,1)S(1)}, u32[]{:S(2)}, u32[]{:S(2)}) async-start(bf16[4,128,512]{2,1,0:T(8,128)(2,1)} %shard_map.88), calls=%async_computation.3 | async-start | bytes 1048576 | tf_op jit(solution)/shard_map/all_to_all | solution.py:328
  84.0 4.4 %copy-start.5 = (bf16[144,256]{1,0:T(8,128)(2,1)S(1)}, bf16[144,256]{1,0:T(8,128)(2,1)}, u32[]{:S(2)}) copy-start(bf16[144,256]{1,0:T(8,128)(2,1)} %copy-done.4) | copy-start | bytes 221188
  90.1 1.0 copy-start.2
  126.2 5.0 %copy-start.9 = (bf16[1024]{0:T(1024)(128)(2,1)S(1)}, bf16[1024]{0:T(1024)(128)(2,1)}, u32[]{:S(2)}) copy-start(bf16[1024]{0:T(1024)(128)(2,1)} %param.14) | copy-start | bytes 6148
  126.2 44.5 %all-to-all-start.4 = ((bf16[4,16,64,512]{3,2,1,0:T(8,128)(2,1)}), bf16[4,16,64,512]{3,2,1,0:T(8,128)(2,1)}, u32[]{:S(2)}, u32[]{:S(2)}) async-start(bf16[4,16,64,512]{3,2,1,0:T(8,128)(2,1)} %broadcast_in_dim.10), calls=%async_computation.4 | async-start | bytes 8388608 | tf_op jit(solution)/shard_map/all_to_all | solution.py:337
  131.2 1.2 copy-start.3
  135.0 15.1 %collective-permute-start.6 = (bf16[512,512]{1,0:T(8,128)(2,1)S(1)}, bf16[512,512]{1,0:T(8,128)(2,1)S(1)}, u32[]{:S(2)}, u32[]{:S(2)}) collective-permute-start(bf16[512,512]{1,0:T(8,128)(2,1)S(1)} %shard_map.89.refs_1_), channel_id=1, source_target_pairs={{0,3},{1,0},{2,1},{3,2},{4,7},{5,4},{6,5},{7,6},{8,11},{9,8},{10,9... | collective-permute-start | bytes 1572872 | tf_op jit(solution)/shard_map/ppermute | solution.py:280
  139.0 11.5 %collective-permute-start.5 = (bf16[512,512]{1,0:T(8,128)(2,1)S(1)}, bf16[512,512]{1,0:T(8,128)(2,1)S(1)}, u32[]{:S(2)}, u32[]{:S(2)}) collective-permute-start(bf16[512,512]{1,0:T(8,128)(2,1)S(1)} %shard_map.89.refs_1_), channel_id=1, source_target_pairs={{0,2},{1,3},{2,0},{3,1},{4,6},{5,7},{6,4},{7,5},{8,10},{9,11},{10,... | collective-permute-start | bytes 1572872 | tf_op jit(solution)/shard_map/ppermute | solution.py:280
  141.4 15.4 %collective-permute-start.4 = (bf16[512,512]{1,0:T(8,128)(2,1)S(1)}, bf16[512,512]{1,0:T(8,128)(2,1)S(1)}, u32[]{:S(2)}, u32[]{:S(2)}) collective-permute-start(bf16[512,512]{1,0:T(8,128)(2,1)S(1)} %shard_map.89.refs_1_), channel_id=1, source_target_pairs={{0,1},{1,2},{2,3},{3,0},{4,5},{5,6},{6,7},{7,4},{8,9},{9,10},{10,1... | collective-permute-start | bytes 1572872 | tf_op jit(solution)/shard_map/ppermute | solution.py:280
  174.3 15.8 %collective-permute-start.9 = (bf16[256,1024]{1,0:T(8,128)(2,1)S(1)}, bf16[256,1024]{1,0:T(8,128)(2,1)S(1)}, u32[]{:S(2)}, u32[]{:S(2)}) collective-permute-start(bf16[256,1024]{1,0:T(8,128)(2,1)S(1)} %shard_map.91), channel_id=1, source_target_pairs={{0,4},{4,0},{1,5},{5,1},{2,6},{6,2},{3,7},{7,3},{8,12},{12,8},{9,1... | collective-permute-start | bytes 1572872 | tf_op jit(solution)/shard_map/ppermute | solution.py:21
  (1 other events, 0.6 us)
Sparse Core Ops, SparseCore 0:
  48.4 73.9 all-gather.2

commit v18 on v16

--- a/solution.py
+++ b/solution.py
@@ -292,6 +292,9 @@
     )
     perm = [(s * 4 + f, f * 4 + s) for s in range(4) for f in range(4)]
     mine = lax.ppermute(both, ("y", "x"), perm)
+    mine, log_decay = lax.optimization_barrier((mine, log_decay))
+    gathered = lax.all_gather(mine, ("a", "p", "q"))
+
     block = ((ROWS, 512), BF)
     keep, send = call(
         pack_body,
@@ -305,9 +308,6 @@
         hbm=range(1, 7),
         vmem=60,
     )
-    mine, send = lax.optimization_barrier((mine, send))
-    gathered = lax.all_gather(mine, ("a", "p", "q"))
-
     got = swap(send)
     pay = ((4, 144, 128), BF)
     pay_b, first = call(ends_body, [pay, ((4, 128, 128), BF)], (at, keep, got))
@@ -327,9 +327,7 @@
         unread=near[1:],
     )
     rows = lax.all_to_all(pay_y, "y", 0, 0, tiled=True)
-    (states,) = call(
-        last_body, [((4, 128, 512), BF)], (at, rows, before, far), unread=(mixture,)
-    )
+    (states,) = call(last_body, [((4, 128, 512), BF)], (at, rows, before, far))
     states = lax.all_to_all(states, NEAR, 0, 0, tiled=True)
     mixture, coef = call(
         mix_body,

time: 166 us -> 169 us (1.018)
  blocking collectives: 8.61 us -> 26.6 us
  starting transfers between devices: 68.2 us -> 60.9 us
  local copies, waits for them, and re-layouts: 11.9 us -> 4.87 us
    all_to_all x0 -> x1, blocking collectives: none -> 18.1 us  [shards(): rows = lax.all_to_all(pay_y, 'y', 0, 0, tiled=True)]
    all_to_all x1 -> x0, starting transfers between devices: 9.43 us -> none  [shards(): rows = lax.all_to_all(pay_y, 'y', 0, 0, tiled=True)]
    unnamed x42 -> x16, local copies, waits for them, and re-layouts: 10.5 us -> 3.44 us
    ppermute x3, starting transfers between devices: 13.7 us -> 16.7 us  [swap(): return lax.ppermute(value, 'c', [(0, 1), (1, 0)])]
  transfers between devices with their start and end apart: 17 -> 16, of which waited for: 6 -> 7; matrix products, arithmetic and copies ran while one was open for 0% -> 0% of each run, Pallas kernels for 13% -> 10%
where the time goes in v18:
time: 169 us; the launch traced here: 167 us
  starting transfers between devices  60.9 us (36%)
  waiting for transfers between devices  34.8 us (21%)
  blocking collectives  26.6 us (16%)
  Pallas kernels  24.6 us (15%)
  between operations  13.7 us (8%)
  local copies, waits for them, and re-layouts  4.87 us (3%)
  other arithmetic  1.72 us (1%)
    pallas_call x10, Pallas kernels, call(): pl.pallas_call(run, out_shape=[jax.ShapeDtypeStruct(*o) for o in outs], i...  24.6 us
    ppermute x6, waiting for transfers between devices, shift(): return lax.ppermute(value, axis, [(i, (i + by) % 4) for i in range(4)])  24.3 us
    ppermute x6, starting transfers between devices, shift(): return lax.ppermute(value, axis, [(i, (i + by) % 4) for i in range(4)])  20.3 us
    all_to_all x1, blocking collectives, shards(): rows = lax.all_to_all(pay_y, 'y', 0, 0, tiled=True)  18.1 us
    ppermute x3, starting transfers between devices, swap(): return lax.ppermute(value, 'c', [(0, 1), (1, 0)])  16.7 us
    ppermute x3, starting transfers between devices, shards(): lax.ppermute(near[k], NEAR, [(i, i ^ k) for i in range(4)])  9.26 us
    all_to_all x1, starting transfers between devices, shards(): far = lax.all_to_all(pay_a, 'a', 0, 0, tiled=True)  9.19 us
    all_to_all x1, blocking collectives, shards(): near = lax.all_to_all(pay_b, NEAR, 0, 0, tiled=True)  8.48 us
  transfers between devices with their start and end apart: 16, of which 7 were waited for; matrix products, arithmetic and copies ran while one was open for 0% of the time, Pallas kernels for 10%

profile of v18, /device:TPU:1, one launch (start us, length us, event | category | flops | bytes accessed | tf_op | source)
XLA Modules:
  0.0 167.2 jit_solution(18047304556400988878)
XLA Ops:
  7.3 8.8 %collective-permute-start = (bf16[32,512]{1,0:T(8,128)(2,1)S(1)}, bf16[32,512]{1,0:T(8,128)(2,1)S(1)}, u32[]{:S(2)}, u32[]{:S(2)}) collective-permute-start(bf16[32,512]{1,0:T(8,128)(2,1)S(1)} %constant_dynamic-slice_fusion), channel_id=1, source_target_pairs={{0,4},{4,0},{1,5},{5,1},{2,6},{6,2},{3,7},{7,3},{8,12},{12,8},{9,1... | collective-permute-start | bytes 98312 | tf_op jit(solution)/shard_map/ppermute | solution.py:21
  19.1 3.8 %shard_map.82 = (bf16[1072,512]{1,0:T(8,128)(2,1)}, bf16[1072,512]{1,0:T(8,128)(2,1)}) custom-call(s32[5]{0:T(128)} %stack.23.refs_0_, bf16[256,1024]{1,0:T(8,128)(2,1)} %refs_1_.1, bf16[256,1024]{1,0:T(8,128)(2,1)} %refs_2_.1, bf16[256,1024]{1,0:T(8,128)(2,1)} %refs_3_.1, bf16[256,1024]{1,0:T(8,128)(2,1)} %refs_4_.1, f32[8,256]{1,0:T(8,128)} %refs_5_, ...), custom_call_target="tpu_custom_call" | custom-call | flops 1000000 | bytes 1000000 | tf_op jit(solution)/shard_map/pallas_call | solution.py:59
  22.9 2.3 %collective-permute-start.2 = (bf16[1072,512]{1,0:T(8,128)(2,1)}, bf16[1072,512]{1,0:T(8,128)(2,1)S(1)}, u32[]{:S(2)}, u32[]{:S(2)}) collective-permute-start(bf16[1072,512]{1,0:T(8,128)(2,1)} %get-tuple-element.26), channel_id=1, source_target_pairs={{0,4},{4,0},{1,5},{5,1},{2,6},{6,2},{3,7},{7,3},{8,12},{12,8},{9,1... | collective-permute-start | bytes 3293192 | tf_op jit(solution)/shard_map/ppermute | solution.py:21
  25.2 2.5 %collective-permute-done.2.refs_2_ = bf16[1072,512]{1,0:T(8,128)(2,1)S(1)} collective-permute-done((bf16[1072,512]{1,0:T(8,128)(2,1)}, bf16[1072,512]{1,0:T(8,128)(2,1)S(1)}, u32[]{:S(2)}, u32[]{:S(2)}) %collective-permute-start.2) | collective-permute-done | bytes 1097760 | tf_op jit(solution)/shard_map/ppermute | solution.py:21
  30.7 8.5 %all_to_all.20.refs_1_ = bf16[4,144,128]{2,1,0:T(8,128)(2,1)S(1)} all-to-all(bf16[4,144,128]{2,1,0:T(8,128)(2,1)S(1)} %get-tuple-element.30), channel_id=1, replica_groups=mesh['y'=4,'a'=4,'p'=2,'q'=2,'c'=2,'x'=4] {'p','q'}, dimensions={0} | all-to-all | bytes 294912 | tf_op jit(solution)/shard_map/all_to_all | solution.py:314
  40.4 9.2 %all-to-all-start.1 = ((bf16[4,144,128]{2,1,0:T(8,128)(2,1)}), bf16[4,144,128]{2,1,0:T(8,128)(2,1)S(1)}, u32[]{:S(2)}, u32[]{:S(2)}) async-start(bf16[4,144,128]{2,1,0:T(8,128)(2,1)} %get-tuple-element.37), calls=%async_computation.1 | async-start | bytes 294912 | tf_op jit(solution)/shard_map/all_to_all | solution.py:316
  49.6 2.4 %collective-permute-start.3 = (bf16[144,256]{1,0:T(8,128)(2,1)S(1)}, bf16[144,256]{1,0:T(8,128)(2,1)S(1)}, u32[]{:S(2)}, u32[]{:S(2)}) collective-permute-start(bf16[144,256]{1,0:T(8,128)(2,1)S(1)} %get-tuple-element.32), channel_id=1, source_target_pairs={{0,8},{8,0},{16,24},{24,16},{1,9},{9,1},{17,25},{25,17},{2,10},{10... | collective-permute-start | bytes 221192 | tf_op jit(solution)/shard_map/ppermute | solution.py:318
  52.0 4.0 %collective-permute-start.4 = (bf16[144,256]{1,0:T(8,128)(2,1)S(1)}, bf16[144,256]{1,0:T(8,128)(2,1)S(1)}, u32[]{:S(2)}, u32[]{:S(2)}) collective-permute-start(bf16[144,256]{1,0:T(8,128)(2,1)S(1)} %get-tuple-element.33), channel_id=1, source_target_pairs={{0,16},{8,24},{16,0},{24,8},{1,17},{9,25},{17,1},{25,9},{2,18},{10... | collective-permute-start | bytes 221192 | tf_op jit(solution)/shard_map/ppermute | solution.py:318
  56.0 2.9 %collective-permute-start.5 = (bf16[144,256]{1,0:T(8,128)(2,1)S(1)}, bf16[144,256]{1,0:T(8,128)(2,1)S(1)}, u32[]{:S(2)}, u32[]{:S(2)}) collective-permute-start(bf16[144,256]{1,0:T(8,128)(2,1)S(1)} %get-tuple-element.34), channel_id=1, source_target_pairs={{0,24},{8,16},{16,8},{24,0},{1,25},{9,17},{17,9},{25,1},{2,26},{10... | collective-permute-start | bytes 221192 | tf_op jit(solution)/shard_map/ppermute | solution.py:318
  61.3 4.5 %collective-permute-done.5.refs_8_.refs_4_ = bf16[144,256]{1,0:T(8,128)(2,1)S(1)} collective-permute-done((bf16[144,256]{1,0:T(8,128)(2,1)S(1)}, bf16[144,256]{1,0:T(8,128)(2,1)S(1)}, u32[]{:S(2)}, u32[]{:S(2)}) %collective-permute-start.5) | collective-permute-done | bytes 73760 | tf_op jit(solution)/shard_map/ppermute | solution.py:318
  66.6 18.1 %all_to_all.21.refs_1_ = bf16[4,144,128]{2,1,0:T(8,128)(2,1)S(1)} all-to-all(bf16[4,144,128]{2,1,0:T(8,128)(2,1)S(1)} %get-tuple-element.38), channel_id=1, replica_groups=mesh['y'=4,'a'=4,'p'=2,'q'=2,'c'=2,'x'=4] {'y'}, dimensions={0} | all-to-all | bytes 294912 | tf_op jit(solution)/shard_map/all_to_all | solution.py:329
  86.2 4.9 %all-to-all-start.3 = ((bf16[4,128,512]{2,1,0:T(8,128)(2,1)}), bf16[4,128,512]{2,1,0:T(8,128)(2,1)}, u32[]{:S(2)}, u32[]{:S(2)}) async-start(bf16[4,128,512]{2,1,0:T(8,128)(2,1)} %shard_map.88), calls=%async_computation.3 | async-start | bytes 1048576 | tf_op jit(solution)/shard_map/all_to_all | solution.py:331
  91.0 4.3 %shard_map.84 = (f32[512,512]{1,0:T(8,128)S(1)}, f32[512,24]{1,0:T(8,128)S(1)}) custom-call(s32[5]{0:T(128)S(1)} %copy-done.5, bf16[1072,512]{1,0:T(8,128)(2,1)S(1)} %copy-done.1, bf16[1072,512]{1,0:T(8,128)(2,1)S(1)} %collective-permute-done.2.refs_2_, bf16[4,128,128]{2,1,0:T(8,128)(2,1)S(1)} %get-tuple-element.27.refs_3_), custom_call_target="tpu_custom_call" | custom-call | flops 1000000 | bytes 1000000 | tf_op jit(solution)/shard_map/pallas_call | solution.py:59
  98.1 3.8 %collective-permute-start.11 = (bf16[16,64,512]{2,1,0:T(8,128)(2,1)}, bf16[16,64,512]{2,1,0:T(8,128)(2,1)S(1)}, u32[]{:S(2)}, u32[]{:S(2)}) collective-permute-start(bf16[16,64,512]{2,1,0:T(8,128)(2,1)} %bitcast.6), channel_id=1, source_target_pairs={{0,256},{128,384},{256,0},{384,128},{1,257},{129,385},{257,1},{385... | collective-permute-start | bytes 3145736 | tf_op jit(solution)/shard_map/ppermute | solution.py:282
  101.8 2.9 %collective-permute-start.10 = (bf16[16,64,512]{2,1,0:T(8,128)(2,1)}, bf16[16,64,512]{2,1,0:T(8,128)(2,1)}, u32[]{:S(2)}, u32[]{:S(2)}) collective-permute-start(bf16[16,64,512]{2,1,0:T(8,128)(2,1)} %bitcast.7), channel_id=1, source_target_pairs={{0,128},{128,256},{256,384},{384,0},{1,129},{129,257},{257,385},{3... | collective-permute-start | bytes 3145736 | tf_op jit(solution)/shard_map/ppermute | solution.py:282
  104.7 3.6 %collective-permute-start.9 = (bf16[16,64,512]{2,1,0:T(8,128)(2,1)}, bf16[16,64,512]{2,1,0:T(8,128)(2,1)}, u32[]{:S(2)}, u32[]{:S(2)}) collective-permute-start(bf16[16,64,512]{2,1,0:T(8,128)(2,1)} %bitcast.8), channel_id=1, source_target_pairs={{0,384},{128,0},{256,128},{384,256},{1,385},{129,1},{257,129},{385... | collective-permute-start | bytes 3145736 | tf_op jit(solution)/shard_map/ppermute | solution.py:282
  109.6 3.1 %shard_map.89.refs_1_ = bf16[512,512]{1,0:T(8,128)(2,1)S(1)} custom-call(s32[5]{0:T(128)S(1)} %copy-done.5, bf16[1072,512]{1,0:T(8,128)(2,1)S(1)} %copy-done.1, bf16[1072,512]{1,0:T(8,128)(2,1)S(1)} %collective-permute-done.2.refs_2_, bf16[1,1024]{1,0:T(2,128)(2,1)S(1)} %broadcast_in_dim.3.refs_3_, f32[512,512]{1,0:T(8,128)S(1)} %copy-done.4, ...), custom_call_target="tpu_custom_call" | custom-call | flops 1000000 | bytes 1000000 | tf_op jit(solution)/shard_map/pallas_call | solution.py:59
  112.7 4.9 %collective-permute-start.8 = (bf16[512,512]{1,0:T(8,128)(2,1)S(1)}, bf16[512,512]{1,0:T(8,128)(2,1)S(1)}, u32[]{:S(2)}, u32[]{:S(2)}) collective-permute-start(bf16[512,512]{1,0:T(8,128)(2,1)S(1)} %shard_map.89.refs_1_), channel_id=1, source_target_pairs={{0,3},{1,0},{2,1},{3,2},{4,7},{5,4},{6,5},{7,6},{8,11},{9,8},{10,9... | collective-permute-start | bytes 1572872 | tf_op jit(solution)/shard_map/ppermute | solution.py:282
  117.6 2.4 %collective-permute-start.7 = (bf16[512,512]{1,0:T(8,128)(2,1)S(1)}, bf16[512,512]{1,0:T(8,128)(2,1)S(1)}, u32[]{:S(2)}, u32[]{:S(2)}) collective-permute-start(bf16[512,512]{1,0:T(8,128)(2,1)S(1)} %shard_map.89.refs_1_), channel_id=1, source_target_pairs={{0,2},{1,3},{2,0},{3,1},{4,6},{5,7},{6,4},{7,5},{8,10},{9,11},{10,... | collective-permute-start | bytes 1572872 | tf_op jit(solution)/shard_map/ppermute | solution.py:282
  120.0 2.8 %collective-permute-start.6 = (bf16[512,512]{1,0:T(8,128)(2,1)S(1)}, bf16[512,512]{1,0:T(8,128)(2,1)S(1)}, u32[]{:S(2)}, u32[]{:S(2)}) collective-permute-start(bf16[512,512]{1,0:T(8,128)(2,1)S(1)} %shard_map.89.refs_1_), channel_id=1, source_target_pairs={{0,1},{1,2},{2,3},{3,0},{4,5},{5,6},{6,7},{7,4},{8,9},{9,10},{10,1... | collective-permute-start | bytes 1572872 | tf_op jit(solution)/shard_map/ppermute | solution.py:282
  122.8 24.3 %collective-permute-done.10.refs_7_ = bf16[16,64,512]{2,1,0:T(8,128)(2,1)} collective-permute-done((bf16[16,64,512]{2,1,0:T(8,128)(2,1)}, bf16[16,64,512]{2,1,0:T(8,128)(2,1)}, u32[]{:S(2)}, u32[]{:S(2)}) %collective-permute-start.10) | collective-permute-done | bytes 1048608 | tf_op jit(solution)/shard_map/ppermute | solution.py:282
  147.1 3.3 %shard_map.91 = bf16[256,1024]{1,0:T(8,128)(2,1)S(1)} custom-call(s32[5]{0:T(128)S(1)} %copy-done.5, bf16[512,512]{1,0:T(8,128)(2,1)S(1)} %shard_map.89.refs_1_, bf16[512,512]{1,0:T(8,128)(2,1)S(1)} %collective-permute-done.6.refs_2_, bf16[512,512]{1,0:T(8,128)(2,1)S(1)} %collective-permute-done.7.refs_3_, ...), custom_call_target="tpu_custom_call" | custom-call | flops 1000000 | bytes 1000000 | tf_op jit(solution)/shard_map/pallas_call | solution.py:59
  150.5 5.6 %collective-permute-start.12 = (bf16[256,1024]{1,0:T(8,128)(2,1)S(1)}, bf16[256,1024]{1,0:T(8,128)(2,1)S(1)}, u32[]{:S(2)}, u32[]{:S(2)}) collective-permute-start(bf16[256,1024]{1,0:T(8,128)(2,1)S(1)} %shard_map.91), channel_id=1, source_target_pairs={{0,4},{4,0},{1,5},{5,1},{2,6},{6,2},{3,7},{7,3},{8,12},{12,8},{9,1... | collective-permute-start | bytes 1572872 | tf_op jit(solution)/shard_map/ppermute | solution.py:21
  156.1 3.3 %shard_map.90 = f32[256,1024]{1,0:T(8,128)S(1)} custom-call(s32[5]{0:T(128)S(1)} %copy-done.5, bf16[512,512]{1,0:T(8,128)(2,1)S(1)} %shard_map.89.refs_1_, bf16[512,512]{1,0:T(8,128)(2,1)S(1)} %collective-permute-done.6.refs_2_, bf16[512,512]{1,0:T(8,128)(2,1)S(1)} %collective-permute-done.7.refs_3_, bf16[512,512]{1,0:T(8,128)(2,1)S(1)} %collective-permute-done.8.refs_4_, ...), custom_call_target="tpu_custom_call" | custom-call | flops 1000000 | bytes 1000000 | tf_op jit(solution)/shard_map/pallas_call | solution.py:59
  (43 shorter events, 17.5 us)
Async XLA Ops:
  6.5 91.5 %all-gather.3.cloned.1.call-start = ((), (), s32[]{:S(2)}) async-start(), calls=%async_computation.4 | async-start | bytes 1114112 | tf_op jit(solution)/shard_map/all_gather | solution.py:296
  7.3 9.6 %collective-permute-start = (bf16[32,512]{1,0:T(8,128)(2,1)S(1)}, bf16[32,512]{1,0:T(8,128)(2,1)S(1)}, u32[]{:S(2)}, u32[]{:S(2)}) collective-permute-start(bf16[32,512]{1,0:T(8,128)(2,1)S(1)} %constant_dynamic-slice_fusion), channel_id=1, source_target_pairs={{0,4},{4,0},{1,5},{5,1},{2,6},{6,2},{3,7},{7,3},{8,12},{12,8},{9,1... | collective-permute-start | bytes 98312 | tf_op jit(solution)/shard_map/ppermute | solution.py:21
  17.7 1.4 collective-permute-start.1
  19.1 6.1 %copy-start.6 = (bf16[64,512]{1,0:T(8,128)(2,1)}, bf16[64,512]{1,0:T(8,128)(2,1)S(1)}, u32[]{:S(2)}) copy-start(bf16[64,512]{1,0:T(8,128)(2,1)S(1)} %collective-permute-done.1) | copy-start | bytes 196612
  19.1 8.6 %copy-start.5 = (s32[5]{0:T(128)S(1)}, s32[5]{0:T(128)}, u32[]{:S(2)}) copy-start(s32[5]{0:T(128)} %stack.23.refs_0_) | copy-start | bytes 64
  22.9 4.8 %collective-permute-start.2 = (bf16[1072,512]{1,0:T(8,128)(2,1)}, bf16[1072,512]{1,0:T(8,128)(2,1)S(1)}, u32[]{:S(2)}, u32[]{:S(2)}) collective-permute-start(bf16[1072,512]{1,0:T(8,128)(2,1)} %get-tuple-element.26), channel_id=1, source_target_pairs={{0,4},{4,0},{1,5},{5,1},{2,6},{6,2},{3,7},{7,3},{8,12},{12,8},{9,1... | collective-permute-start | bytes 3293192 | tf_op jit(solution)/shard_map/ppermute | solution.py:21
  27.7 1.2 copy-start
  40.4 25.6 %all-to-all-start.1 = ((bf16[4,144,128]{2,1,0:T(8,128)(2,1)}), bf16[4,144,128]{2,1,0:T(8,128)(2,1)S(1)}, u32[]{:S(2)}, u32[]{:S(2)}) async-start(bf16[4,144,128]{2,1,0:T(8,128)(2,1)} %get-tuple-element.37), calls=%async_computation.1 | async-start | bytes 294912 | tf_op jit(solution)/shard_map/all_to_all | solution.py:316
  49.6 9.9 %collective-permute-start.3 = (bf16[144,256]{1,0:T(8,128)(2,1)S(1)}, bf16[144,256]{1,0:T(8,128)(2,1)S(1)}, u32[]{:S(2)}, u32[]{:S(2)}) collective-permute-start(bf16[144,256]{1,0:T(8,128)(2,1)S(1)} %get-tuple-element.32), channel_id=1, source_target_pairs={{0,8},{8,0},{16,24},{24,16},{1,9},{9,1},{17,25},{25,17},{2,10},{10... | collective-permute-start | bytes 221192 | tf_op jit(solution)/shard_map/ppermute | solution.py:318
  52.0 9.3 %collective-permute-start.4 = (bf16[144,256]{1,0:T(8,128)(2,1)S(1)}, bf16[144,256]{1,0:T(8,128)(2,1)S(1)}, u32[]{:S(2)}, u32[]{:S(2)}) collective-permute-start(bf16[144,256]{1,0:T(8,128)(2,1)S(1)} %get-tuple-element.33), channel_id=1, source_target_pairs={{0,16},{8,24},{16,0},{24,8},{1,17},{9,25},{17,1},{25,9},{2,18},{10... | collective-permute-start | bytes 221192 | tf_op jit(solution)/shard_map/ppermute | solution.py:318
  56.0 9.8 %collective-permute-start.5 = (bf16[144,256]{1,0:T(8,128)(2,1)S(1)}, bf16[144,256]{1,0:T(8,128)(2,1)S(1)}, u32[]{:S(2)}, u32[]{:S(2)}) collective-permute-start(bf16[144,256]{1,0:T(8,128)(2,1)S(1)} %get-tuple-element.34), channel_id=1, source_target_pairs={{0,24},{8,16},{16,8},{24,0},{1,25},{9,17},{17,9},{25,1},{2,26},{10... | collective-permute-start | bytes 221192 | tf_op jit(solution)/shard_map/ppermute | solution.py:318
  66.6 24.4 %copy-start.1 = (bf16[1072,512]{1,0:T(8,128)(2,1)S(1)}, bf16[1072,512]{1,0:T(8,128)(2,1)}, u32[]{:S(2)}) copy-start(bf16[1072,512]{1,0:T(8,128)(2,1)} %get-tuple-element.25.refs_1_) | copy-start | bytes 3293188
  86.2 22.2 %all-to-all-start.3 = ((bf16[4,128,512]{2,1,0:T(8,128)(2,1)}), bf16[4,128,512]{2,1,0:T(8,128)(2,1)}, u32[]{:S(2)}, u32[]{:S(2)}) async-start(bf16[4,128,512]{2,1,0:T(8,128)(2,1)} %shard_map.88), calls=%async_computation.3 | async-start | bytes 1048576 | tf_op jit(solution)/shard_map/all_to_all | solution.py:331
  95.4 13.0 %copy-start.7 = (bf16[1024]{0:T(1024)(128)(2,1)S(1)}, bf16[1024]{0:T(1024)(128)(2,1)}, u32[]{:S(2)}) copy-start(bf16[1024]{0:T(1024)(128)(2,1)} %param.14) | copy-start | bytes 6148
  97.1 1.0 copy-start.3
  98.1 21.9 %collective-permute-start.11 = (bf16[16,64,512]{2,1,0:T(8,128)(2,1)}, bf16[16,64,512]{2,1,0:T(8,128)(2,1)S(1)}, u32[]{:S(2)}, u32[]{:S(2)}) collective-permute-start(bf16[16,64,512]{2,1,0:T(8,128)(2,1)} %bitcast.6), channel_id=1, source_target_pairs={{0,256},{128,384},{256,0},{384,128},{1,257},{129,385},{257,1},{385... | collective-permute-start | bytes 3145736 | tf_op jit(solution)/shard_map/ppermute | solution.py:282
  101.8 45.3 %collective-permute-start.10 = (bf16[16,64,512]{2,1,0:T(8,128)(2,1)}, bf16[16,64,512]{2,1,0:T(8,128)(2,1)}, u32[]{:S(2)}, u32[]{:S(2)}) collective-permute-start(bf16[16,64,512]{2,1,0:T(8,128)(2,1)} %bitcast.7), channel_id=1, source_target_pairs={{0,128},{128,256},{256,384},{384,0},{1,129},{129,257},{257,385},{3... | collective-permute-start | bytes 3145736 | tf_op jit(solution)/shard_map/ppermute | solution.py:282
  104.7 42.4 %collective-permute-start.9 = (bf16[16,64,512]{2,1,0:T(8,128)(2,1)}, bf16[16,64,512]{2,1,0:T(8,128)(2,1)}, u32[]{:S(2)}, u32[]{:S(2)}) collective-permute-start(bf16[16,64,512]{2,1,0:T(8,128)(2,1)} %bitcast.8), channel_id=1, source_target_pairs={{0,384},{128,0},{256,128},{384,256},{1,385},{129,1},{257,129},{385... | collective-permute-start | bytes 3145736 | tf_op jit(solution)/shard_map/ppermute | solution.py:282
  108.4 1.2 copy-start.4
  109.6 37.5 %copy-start.2 = (bf16[1024,512]{1,0:T(8,128)(2,1)S(1)}, bf16[1024,512]{1,0:T(8,128)(2,1)}, u32[]{:S(2)}) copy-start(bf16[1024,512]{1,0:T(8,128)(2,1)} %all-gather.3.cloned.1.call-done) | copy-start | bytes 3145732
  112.7 34.4 %collective-permute-start.8 = (bf16[512,512]{1,0:T(8,128)(2,1)S(1)}, bf16[512,512]{1,0:T(8,128)(2,1)S(1)}, u32[]{:S(2)}, u32[]{:S(2)}) collective-permute-start(bf16[512,512]{1,0:T(8,128)(2,1)S(1)} %shard_map.89.refs_1_), channel_id=1, source_target_pairs={{0,3},{1,0},{2,1},{3,2},{4,7},{5,4},{6,5},{7,6},{8,11},{9,8},{10,9... | collective-permute-start | bytes 1572872 | tf_op jit(solution)/shard_map/ppermute | solution.py:282
  117.6 29.5 %collective-permute-start.7 = (bf16[512,512]{1,0:T(8,128)(2,1)S(1)}, bf16[512,512]{1,0:T(8,128)(2,1)S(1)}, u32[]{:S(2)}, u32[]{:S(2)}) collective-permute-start(bf16[512,512]{1,0:T(8,128)(2,1)S(1)} %shard_map.89.refs_1_), channel_id=1, source_target_pairs={{0,2},{1,3},{2,0},{3,1},{4,6},{5,7},{6,4},{7,5},{8,10},{9,11},{10,... | collective-permute-start | bytes 1572872 | tf_op jit(solution)/shard_map/ppermute | solution.py:282
  120.0 27.1 %collective-permute-start.6 = (bf16[512,512]{1,0:T(8,128)(2,1)S(1)}, bf16[512,512]{1,0:T(8,128)(2,1)S(1)}, u32[]{:S(2)}, u32[]{:S(2)}) collective-permute-start(bf16[512,512]{1,0:T(8,128)(2,1)S(1)} %shard_map.89.refs_1_), channel_id=1, source_target_pairs={{0,1},{1,2},{2,3},{3,0},{4,5},{5,6},{6,7},{7,4},{8,9},{9,10},{10,1... | collective-permute-start | bytes 1572872 | tf_op jit(solution)/shard_map/ppermute | solution.py:282
  150.5 9.0 %collective-permute-start.12 = (bf16[256,1024]{1,0:T(8,128)(2,1)S(1)}, bf16[256,1024]{1,0:T(8,128)(2,1)S(1)}, u32[]{:S(2)}, u32[]{:S(2)}) collective-permute-start(bf16[256,1024]{1,0:T(8,128)(2,1)S(1)} %shard_map.91), channel_id=1, source_target_pairs={{0,4},{4,0},{1,5},{5,1},{2,6},{6,2},{3,7},{7,3},{8,12},{12,8},{9,1... | collective-permute-start | bytes 1572872 | tf_op jit(solution)/shard_map/ppermute | solution.py:21
Sparse Core Ops, SparseCore 0:
  25.3 72.6 all-gather.2

commit v19 on v18

--- a/solution.py
+++ b/solution.py
@@ -285,16 +285,16 @@
 def shards(values, keys, queries, gates, log_decay, level_mix, norm_gain, weight):
     y, a, b, c, x = (lax.axis_index(n) for n in ("y", "a", NEAR, "c", "x"))
     at = jnp.stack([c, b, a, y, x]).astype(jnp.int32)
-    kept = lax.dynamic_slice_in_dim(weight, c * 512, 512, 1)
-    theirs = swap(lax.dynamic_slice_in_dim(weight, (1 - c) * 512, 512, 1))
-    both = jnp.concatenate(
-        [jnp.where(c == 0, kept, theirs), jnp.where(c == 0, theirs, kept)]
-    )
-    perm = [(s * 4 + f, f * 4 + s) for s in range(4) for f in range(4)]
-    mine = lax.ppermute(both, ("y", "x"), perm)
-    mine, log_decay = lax.optimization_barrier((mine, log_decay))
-    gathered = lax.all_gather(mine, ("a", "p", "q"))
-
+    turned = []
+    for other in range(2):
+        half = lax.dynamic_slice_in_dim(weight, (c ^ other) * 512, 512, 1)
+        perm = [
+            ((s * 2 + k) * 4 + f, (f * 2 + (k ^ other)) * 4 + s)
+            for s in range(4)
+            for f in range(4)
+            for k in range(2)
+        ]
+        turned.append(lax.ppermute(half, ("y", "c", "x"), perm))
     block = ((ROWS, 512), BF)
     keep, send = call(
         pack_body,
@@ -308,6 +308,10 @@
         hbm=range(1, 7),
         vmem=60,
     )
+    turned, send = lax.optimization_barrier((turned, send))
+    mine = jnp.where(c == 0, jnp.concatenate(turned), jnp.concatenate(turned[::-1]))
+    gathered = lax.all_gather(mine, ("a", "p", "q"))
+
     got = swap(send)
     pay = ((4, 144, 128), BF)
     pay_b, first = call(ends_body, [pay, ((4, 128, 128), BF)], (at, keep, got))
@@ -336,11 +340,13 @@
         scratch=[pltpu.VMEM((4, 144, 256), BF)],
     )
     _, gathered = lax.optimization_barrier((coef, gathered))
-    rights = [gathered] + [shift(gathered, "y", 4 - k) for k in (1, 3, 2)]
+    rights = [gathered] + [shift(gathered, "y", 4 - k) for k in (1, 3)]
     (normed,) = call(
         norm_body, [((512, 512), BF)], (at, keep, got, norm_gain[None], mixture, coef, states)
     )
 
+    _, gathered = lax.optimization_barrier((normed, gathered))
+    rights.append(shift(gathered, "y", 2))
     blocks = [normed] + [shift(normed, "x", j) for j in (1, 2, 3)]
     theirs = swap(project(at, blocks, rights, True))
     own = project(at, blocks, rights, False)

time: 169 us -> 188 us (1.11)
  the two profiles are of different devices: /device:TPU:1 before, /device:TPU:33 now
where the time goes in v19:
time: 188 us; the launch traced here: 187 us
  starting transfers between devices  79.8 us (42%)
  waiting for transfers between devices  46.1 us (25%)
  Pallas kernels  25.3 us (13%)
  blocking collectives  15.7 us (8%)
  between operations  13.7 us (7%)
  local copies, waits for them, and re-layouts  4.93 us (3%)
    pallas_call x10, Pallas kernels, call(): pl.pallas_call(run, out_shape=[jax.ShapeDtypeStruct(*o) for o in outs], i...  25.3 us
    ppermute x2, starting transfers between devices, swap(): return lax.ppermute(value, 'c', [(0, 1), (1, 0)])  23.5 us
    ppermute x6, starting transfers between devices, shift(): return lax.ppermute(value, axis, [(i, (i + by) % 4) for i in range(4)])  22.7 us
    ppermute x6, waiting for transfers between devices, shift(): return lax.ppermute(value, axis, [(i, (i + by) % 4) for i in range(4)])  19.8 us
    all_to_all x1, blocking collectives, shards(): rows = lax.all_to_all(pay_y, 'y', 0, 0, tiled=True)  15.7 us
    all_gather x1, waiting for transfers between devices, shards(): gathered = lax.all_gather(mine, ('a', 'p', 'q'))  10.3 us
    all_to_all x1, starting transfers between devices, shards(): far = lax.all_to_all(pay_a, 'a', 0, 0, tiled=True)  9.43 us
    ppermute x3, waiting for transfers between devices, shards(): lax.ppermute(near[k], NEAR, [(i, i ^ k) for i in range(4)])  8.79 us
  transfers between devices with their start and end apart: 17, of which 8 were waited for; matrix products, arithmetic and copies ran while one was open for 1% of the time, Pallas kernels for 10%

profile of v19, /device:TPU:33, one launch (start us, length us, event | category | flops | bytes accessed | tf_op | source)
XLA Modules:
  0.0 187.2 jit_solution(4233957287117981092)
XLA Ops:
  11.3 3.8 %shard_map.82 = (bf16[1072,512]{1,0:T(8,128)(2,1)}, bf16[1072,512]{1,0:T(8,128)(2,1)}) custom-call(s32[5]{0:T(128)} %stack.23.refs_0_, bf16[256,1024]{1,0:T(8,128)(2,1)} %refs_1_.1, bf16[256,1024]{1,0:T(8,128)(2,1)} %refs_2_.1, bf16[256,1024]{1,0:T(8,128)(2,1)} %refs_3_.1, bf16[256,1024]{1,0:T(8,128)(2,1)} %refs_4_.1, f32[8,256]{1,0:T(8,128)} %refs_5_.1, ...), custom_call_target="tpu_custom_call" | custom-call | flops 1000000 | bytes 1000000 | tf_op jit(solution)/shard_map/pallas_call | solution.py:59
  17.0 2.9 %collective-permute-done.2.refs_2_ = bf16[1072,512]{1,0:T(8,128)(2,1)S(1)} collective-permute-done((bf16[1072,512]{1,0:T(8,128)(2,1)}, bf16[1072,512]{1,0:T(8,128)(2,1)S(1)}, u32[]{:S(2)}, u32[]{:S(2)}) %collective-permute-start.2) | collective-permute-done | bytes 1097760 | tf_op jit(solution)/shard_map/ppermute | solution.py:21
  23.6 8.5 %all-to-all-start = ((bf16[4,144,128]{2,1,0:T(8,128)(2,1)}), bf16[4,144,128]{2,1,0:T(8,128)(2,1)S(1)}, u32[]{:S(2)}, u32[]{:S(2)}) async-start(bf16[4,144,128]{2,1,0:T(8,128)(2,1)} %get-tuple-element.32), calls=%async_computation | async-start | bytes 294912 | tf_op jit(solution)/shard_map/all_to_all | solution.py:318
  32.9 4.3 %all-to-all-done.refs_1_ = bf16[4,144,128]{2,1,0:T(8,128)(2,1)S(1)} async-done(((bf16[4,144,128]{2,1,0:T(8,128)(2,1)}), bf16[4,144,128]{2,1,0:T(8,128)(2,1)S(1)}, u32[]{:S(2)}, u32[]{:S(2)}) %all-to-all-start) | async-done | bytes 147488 | tf_op jit(solution)/shard_map/all_to_all | solution.py:318
  38.4 9.4 %all-to-all-start.1 = ((bf16[4,144,128]{2,1,0:T(8,128)(2,1)}), bf16[4,144,128]{2,1,0:T(8,128)(2,1)S(1)}, u32[]{:S(2)}, u32[]{:S(2)}) async-start(bf16[4,144,128]{2,1,0:T(8,128)(2,1)} %get-tuple-element.39), calls=%async_computation.1 | async-start | bytes 294912 | tf_op jit(solution)/shard_map/all_to_all | solution.py:320
  49.8 3.5 %collective-permute-start.4 = (bf16[144,256]{1,0:T(8,128)(2,1)S(1)}, bf16[144,256]{1,0:T(8,128)(2,1)S(1)}, u32[]{:S(2)}, u32[]{:S(2)}) collective-permute-start(bf16[144,256]{1,0:T(8,128)(2,1)S(1)} %get-tuple-element.35), channel_id=1, source_target_pairs={{0,16},{8,24},{16,0},{24,8},{1,17},{9,25},{17,1},{25,9},{2,18},{10... | collective-permute-start | bytes 221192 | tf_op jit(solution)/shard_map/ppermute | solution.py:322
  53.3 3.0 %collective-permute-start.5 = (bf16[144,256]{1,0:T(8,128)(2,1)S(1)}, bf16[144,256]{1,0:T(8,128)(2,1)S(1)}, u32[]{:S(2)}, u32[]{:S(2)}) collective-permute-start(bf16[144,256]{1,0:T(8,128)(2,1)S(1)} %get-tuple-element.36), channel_id=1, source_target_pairs={{0,24},{8,16},{16,8},{24,0},{1,25},{9,17},{17,9},{25,1},{2,26},{10... | collective-permute-start | bytes 221192 | tf_op jit(solution)/shard_map/ppermute | solution.py:322
  58.5 6.6 %collective-permute-done.5.refs_8_.refs_4_ = bf16[144,256]{1,0:T(8,128)(2,1)S(1)} collective-permute-done((bf16[144,256]{1,0:T(8,128)(2,1)S(1)}, bf16[144,256]{1,0:T(8,128)(2,1)S(1)}, u32[]{:S(2)}, u32[]{:S(2)}) %collective-permute-start.5) | collective-permute-done | bytes 73760 | tf_op jit(solution)/shard_map/ppermute | solution.py:322
  65.7 15.7 %all_to_all.20.refs_1_ = bf16[4,144,128]{2,1,0:T(8,128)(2,1)S(1)} all-to-all(bf16[4,144,128]{2,1,0:T(8,128)(2,1)S(1)} %get-tuple-element.40), channel_id=1, replica_groups=mesh['y'=4,'a'=4,'p'=2,'q'=2,'c'=2,'x'=4] {'y'}, dimensions={0} | all-to-all | bytes 294912 | tf_op jit(solution)/shard_map/all_to_all | solution.py:333
  82.8 4.1 %all-to-all-start.3 = ((bf16[4,128,512]{2,1,0:T(8,128)(2,1)}), bf16[4,128,512]{2,1,0:T(8,128)(2,1)}, u32[]{:S(2)}, u32[]{:S(2)}) async-start(bf16[4,128,512]{2,1,0:T(8,128)(2,1)} %shard_map.88), calls=%async_computation.3 | async-start | bytes 1048576 | tf_op jit(solution)/shard_map/all_to_all | solution.py:335
  86.9 4.3 %shard_map.84 = (f32[512,512]{1,0:T(8,128)S(1)}, f32[512,24]{1,0:T(8,128)S(1)}) custom-call(s32[5]{0:T(128)S(1)} %copy-done.5, bf16[1072,512]{1,0:T(8,128)(2,1)S(1)} %copy-done.1, bf16[1072,512]{1,0:T(8,128)(2,1)S(1)} %collective-permute-done.2.refs_2_, bf16[4,128,128]{2,1,0:T(8,128)(2,1)S(1)} %get-tuple-element.29.refs_3_), custom_call_target="tpu_custom_call" | custom-call | flops 1000000 | bytes 1000000 | tf_op jit(solution)/shard_map/pallas_call | solution.py:59
  94.0 10.3 %all-gather.2.cloned.1.call-done.refs_5_ = bf16[16,64,512]{2,1,0:T(8,128)(2,1)} async-done(((bf16[1,64,512]{2,1,0:T(8,128)(2,1)}), bf16[16,64,512]{2,1,0:T(8,128)(2,1)}) %all-gather.2.cloned.1.call-update) | async-done | bytes 1048592 | tf_op jit(solution)/shard_map/all_gather | solution.py:313
  104.3 4.5 %collective-permute-start.10 = (bf16[16,64,512]{2,1,0:T(8,128)(2,1)}, bf16[16,64,512]{2,1,0:T(8,128)(2,1)S(1)}, u32[]{:S(2)}, u32[]{:S(2)}) collective-permute-start(bf16[16,64,512]{2,1,0:T(8,128)(2,1)} %all-gather.2.cloned.1.call-done.refs_5_), channel_id=1, source_target_pairs={{0,128},{128,256},{256,384},{384,0},{1,129},{129,257},{257,385},{3... | collective-permute-start | bytes 3145736 | tf_op jit(solution)/shard_map/ppermute | solution.py:282
  108.8 5.1 %collective-permute-start.9 = (bf16[16,64,512]{2,1,0:T(8,128)(2,1)}, bf16[16,64,512]{2,1,0:T(8,128)(2,1)}, u32[]{:S(2)}, u32[]{:S(2)}) collective-permute-start(bf16[16,64,512]{2,1,0:T(8,128)(2,1)} %all-gather.2.cloned.1.call-done.refs_5_), channel_id=1, source_target_pairs={{0,384},{128,0},{256,128},{384,256},{1,385},{129,1},{257,129},{385... | collective-permute-start | bytes 3145736 | tf_op jit(solution)/shard_map/ppermute | solution.py:282
  115.1 3.1 %shard_map.89.refs_1_ = bf16[512,512]{1,0:T(8,128)(2,1)S(1)} custom-call(s32[5]{0:T(128)S(1)} %copy-done.5, bf16[1072,512]{1,0:T(8,128)(2,1)S(1)} %copy-done.1, bf16[1072,512]{1,0:T(8,128)(2,1)S(1)} %collective-permute-done.2.refs_2_, bf16[1,1024]{1,0:T(2,128)(2,1)S(1)} %broadcast_in_dim.3.refs_3_, f32[512,512]{1,0:T(8,128)S(1)} %copy-done.4, ...), custom_call_target="tpu_custom_call" | custom-call | flops 1000000 | bytes 1000000 | tf_op jit(solution)/shard_map/pallas_call | solution.py:59
  118.3 3.3 %collective-permute-start.11 = (bf16[16,64,512]{2,1,0:T(8,128)(2,1)S(1)}, bf16[16,64,512]{2,1,0:T(8,128)(2,1)S(1)}, u32[]{:S(2)}, u32[]{:S(2)}) collective-permute-start(bf16[16,64,512]{2,1,0:T(8,128)(2,1)S(1)} %copy-done.2), channel_id=1, source_target_pairs={{0,256},{128,384},{256,0},{384,128},{1,257},{129,385},{257,1},{385... | collective-permute-start | bytes 3145736 | tf_op jit(solution)/shard_map/ppermute | solution.py:282
  121.6 4.1 %collective-permute-start.8 = (bf16[512,512]{1,0:T(8,128)(2,1)S(1)}, bf16[512,512]{1,0:T(8,128)(2,1)S(1)}, u32[]{:S(2)}, u32[]{:S(2)}) collective-permute-start(bf16[512,512]{1,0:T(8,128)(2,1)S(1)} %shard_map.89.refs_1_), channel_id=1, source_target_pairs={{0,3},{1,0},{2,1},{3,2},{4,7},{5,4},{6,5},{7,6},{8,11},{9,8},{10,9... | collective-permute-start | bytes 1572872 | tf_op jit(solution)/shard_map/ppermute | solution.py:282
  128.2 3.2 %collective-permute-start.6 = (bf16[512,512]{1,0:T(8,128)(2,1)S(1)}, bf16[512,512]{1,0:T(8,128)(2,1)S(1)}, u32[]{:S(2)}, u32[]{:S(2)}) collective-permute-start(bf16[512,512]{1,0:T(8,128)(2,1)S(1)} %shard_map.89.refs_1_), channel_id=1, source_target_pairs={{0,1},{1,2},{2,3},{3,0},{4,5},{5,6},{6,7},{7,4},{8,9},{9,10},{10,1... | collective-permute-start | bytes 1572872 | tf_op jit(solution)/shard_map/ppermute | solution.py:282
  131.4 5.8 %collective-permute-done.8.refs_4_ = bf16[512,512]{1,0:T(8,128)(2,1)S(1)} collective-permute-done((bf16[512,512]{1,0:T(8,128)(2,1)S(1)}, bf16[512,512]{1,0:T(8,128)(2,1)S(1)}, u32[]{:S(2)}, u32[]{:S(2)}) %collective-permute-start.8) | collective-permute-done | bytes 524320 | tf_op jit(solution)/shard_map/ppermute | solution.py:282
  137.2 7.6 %collective-permute-done.6.refs_2_ = bf16[512,512]{1,0:T(8,128)(2,1)S(1)} collective-permute-done((bf16[512,512]{1,0:T(8,128)(2,1)S(1)}, bf16[512,512]{1,0:T(8,128)(2,1)S(1)}, u32[]{:S(2)}, u32[]{:S(2)}) %collective-permute-start.6) | collective-permute-done | bytes 524320 | tf_op jit(solution)/shard_map/ppermute | solution.py:282
  144.8 6.3 %collective-permute-done.11.refs_8_ = bf16[16,64,512]{2,1,0:T(8,128)(2,1)S(1)} collective-permute-done((bf16[16,64,512]{2,1,0:T(8,128)(2,1)S(1)}, bf16[16,64,512]{2,1,0:T(8,128)(2,1)S(1)}, u32[]{:S(2)}, u32[]{:S(2)}) %collective-permute-start.11) | collective-permute-done | bytes 1048608 | tf_op jit(solution)/shard_map/ppermute | solution.py:282
  151.1 3.3 %shard_map.91 = bf16[256,1024]{1,0:T(8,128)(2,1)S(1)} custom-call(s32[5]{0:T(128)S(1)} %copy-done.5, bf16[512,512]{1,0:T(8,128)(2,1)S(1)} %shard_map.89.refs_1_, bf16[512,512]{1,0:T(8,128)(2,1)S(1)} %collective-permute-done.6.refs_2_, bf16[512,512]{1,0:T(8,128)(2,1)S(1)} %collective-permute-done.7.refs_3_, ...), custom_call_target="tpu_custom_call" | custom-call | flops 1000000 | bytes 1000000 | tf_op jit(solution)/shard_map/pallas_call | solution.py:59
  154.5 21.6 %collective-permute-start.12 = (bf16[256,1024]{1,0:T(8,128)(2,1)S(1)}, bf16[256,1024]{1,0:T(8,128)(2,1)S(1)}, u32[]{:S(2)}, u32[]{:S(2)}) collective-permute-start(bf16[256,1024]{1,0:T(8,128)(2,1)S(1)} %shard_map.91), channel_id=1, source_target_pairs={{0,4},{4,0},{1,5},{5,1},{2,6},{6,2},{3,7},{7,3},{8,12},{12,8},{9,1... | collective-permute-start | bytes 1572872 | tf_op jit(solution)/shard_map/ppermute | solution.py:21
  176.1 3.3 %shard_map.90 = f32[256,1024]{1,0:T(8,128)S(1)} custom-call(s32[5]{0:T(128)S(1)} %copy-done.5, bf16[512,512]{1,0:T(8,128)(2,1)S(1)} %shard_map.89.refs_1_, bf16[512,512]{1,0:T(8,128)(2,1)S(1)} %collective-permute-done.6.refs_2_, bf16[512,512]{1,0:T(8,128)(2,1)S(1)} %collective-permute-done.7.refs_3_, bf16[512,512]{1,0:T(8,128)(2,1)S(1)} %collective-permute-done.8.refs_4_, ...), custom_call_target="tpu_custom_call" | custom-call | flops 1000000 | bytes 1000000 | tf_op jit(solution)/shard_map/pallas_call | solution.py:59
  (41 shorter events, 25.8 us)
Async XLA Ops:
  7.3 7.8 %collective-permute-start.1 = (bf16[32,512]{1,0:T(8,128)(2,1)S(1)}, bf16[32,512]{1,0:T(8,128)(2,1)S(1)}, u32[]{:S(2)}, u32[]{:S(2)}) collective-permute-start(bf16[32,512]{1,0:T(8,128)(2,1)S(1)} %get-tuple-element.47), channel_id=1, source_target_pairs={{0,4},{4,0},{1,132},{5,128},{2,260},{6,256},{3,388},{7,384},{128,5... | collective-permute-start | bytes 98312 | tf_op jit(solution)/shard_map/ppermute | solution.py:297
  9.9 5.2 %collective-permute-start = (bf16[32,512]{1,0:T(8,128)(2,1)S(1)}, bf16[32,512]{1,0:T(8,128)(2,1)S(1)}, u32[]{:S(2)}, u32[]{:S(2)}) collective-permute-start(bf16[32,512]{1,0:T(8,128)(2,1)S(1)} %get-tuple-element.48), channel_id=1, source_target_pairs={{0,0},{4,4},{1,128},{5,132},{2,256},{6,260},{3,384},{7,388},{128,1... | collective-permute-start | bytes 98312 | tf_op jit(solution)/shard_map/ppermute | solution.py:297
  11.3 8.7 %copy-start.5 = (s32[5]{0:T(128)S(1)}, s32[5]{0:T(128)}, u32[]{:S(2)}) copy-start(s32[5]{0:T(128)} %stack.23.refs_0_) | copy-start | bytes 64
  15.1 4.8 %collective-permute-start.2 = (bf16[1072,512]{1,0:T(8,128)(2,1)}, bf16[1072,512]{1,0:T(8,128)(2,1)S(1)}, u32[]{:S(2)}, u32[]{:S(2)}) collective-permute-start(bf16[1072,512]{1,0:T(8,128)(2,1)} %get-tuple-element.28), channel_id=1, source_target_pairs={{0,4},{4,0},{1,5},{5,1},{2,6},{6,2},{3,7},{7,3},{8,12},{12,8},{9,1... | collective-permute-start | bytes 3293192 | tf_op jit(solution)/shard_map/ppermute | solution.py:21
  19.9 1.2 copy-start
  23.6 13.6 %all-to-all-start = ((bf16[4,144,128]{2,1,0:T(8,128)(2,1)}), bf16[4,144,128]{2,1,0:T(8,128)(2,1)S(1)}, u32[]{:S(2)}, u32[]{:S(2)}) async-start(bf16[4,144,128]{2,1,0:T(8,128)(2,1)} %get-tuple-element.32), calls=%async_computation | async-start | bytes 294912 | tf_op jit(solution)/shard_map/all_to_all | solution.py:318
  32.1 72.1 %all-gather.2.cloned.1.call-start = ((), (), s32[]{:S(2)}) async-start(), calls=%async_computation.4 | async-start | bytes 1114112 | tf_op jit(solution)/shard_map/all_gather | solution.py:313
  38.4 26.6 %all-to-all-start.1 = ((bf16[4,144,128]{2,1,0:T(8,128)(2,1)}), bf16[4,144,128]{2,1,0:T(8,128)(2,1)S(1)}, u32[]{:S(2)}, u32[]{:S(2)}) async-start(bf16[4,144,128]{2,1,0:T(8,128)(2,1)} %get-tuple-element.39), calls=%async_computation.1 | async-start | bytes 294912 | tf_op jit(solution)/shard_map/all_to_all | solution.py:320
  47.9 8.4 %collective-permute-start.3 = (bf16[144,256]{1,0:T(8,128)(2,1)S(1)}, bf16[144,256]{1,0:T(8,128)(2,1)S(1)}, u32[]{:S(2)}, u32[]{:S(2)}) collective-permute-start(bf16[144,256]{1,0:T(8,128)(2,1)S(1)} %get-tuple-element.34), channel_id=1, source_target_pairs={{0,8},{8,0},{16,24},{24,16},{1,9},{9,1},{17,25},{25,17},{2,10},{10... | collective-permute-start | bytes 221192 | tf_op jit(solution)/shard_map/ppermute | solution.py:322
  49.8 8.7 %collective-permute-start.4 = (bf16[144,256]{1,0:T(8,128)(2,1)S(1)}, bf16[144,256]{1,0:T(8,128)(2,1)S(1)}, u32[]{:S(2)}, u32[]{:S(2)}) collective-permute-start(bf16[144,256]{1,0:T(8,128)(2,1)S(1)} %get-tuple-element.35), channel_id=1, source_target_pairs={{0,16},{8,24},{16,0},{24,8},{1,17},{9,25},{17,1},{25,9},{2,18},{10... | collective-permute-start | bytes 221192 | tf_op jit(solution)/shard_map/ppermute | solution.py:322
  53.3 11.8 %collective-permute-start.5 = (bf16[144,256]{1,0:T(8,128)(2,1)S(1)}, bf16[144,256]{1,0:T(8,128)(2,1)S(1)}, u32[]{:S(2)}, u32[]{:S(2)}) collective-permute-start(bf16[144,256]{1,0:T(8,128)(2,1)S(1)} %get-tuple-element.36), channel_id=1, source_target_pairs={{0,24},{8,16},{16,8},{24,0},{1,25},{9,17},{17,9},{25,1},{2,26},{10... | collective-permute-start | bytes 221192 | tf_op jit(solution)/shard_map/ppermute | solution.py:322
  65.7 21.2 %copy-start.1 = (bf16[1072,512]{1,0:T(8,128)(2,1)S(1)}, bf16[1072,512]{1,0:T(8,128)(2,1)}, u32[]{:S(2)}) copy-start(bf16[1072,512]{1,0:T(8,128)(2,1)} %get-tuple-element.26.refs_1_) | copy-start | bytes 3293188
  82.8 31.1 %all-to-all-start.3 = ((bf16[4,128,512]{2,1,0:T(8,128)(2,1)}), bf16[4,128,512]{2,1,0:T(8,128)(2,1)}, u32[]{:S(2)}, u32[]{:S(2)}) async-start(bf16[4,128,512]{2,1,0:T(8,128)(2,1)} %shard_map.88), calls=%async_computation.3 | async-start | bytes 1048576 | tf_op jit(solution)/shard_map/all_to_all | solution.py:335
  91.3 17.5 %copy-start.6 = (bf16[1024]{0:T(1024)(128)(2,1)S(1)}, bf16[1024]{0:T(1024)(128)(2,1)}, u32[]{:S(2)}) copy-start(bf16[1024]{0:T(1024)(128)(2,1)} %param.14) | copy-start | bytes 6148
  93.0 1.0 copy-start.3
  104.3 23.9 %collective-permute-start.10 = (bf16[16,64,512]{2,1,0:T(8,128)(2,1)}, bf16[16,64,512]{2,1,0:T(8,128)(2,1)S(1)}, u32[]{:S(2)}, u32[]{:S(2)}) collective-permute-start(bf16[16,64,512]{2,1,0:T(8,128)(2,1)} %all-gather.2.cloned.1.call-done.refs_5_), channel_id=1, source_target_pairs={{0,128},{128,256},{256,384},{384,0},{1,129},{129,257},{257,385},{3... | collective-permute-start | bytes 3145736 | tf_op jit(solution)/shard_map/ppermute | solution.py:282
  108.8 22.6 %collective-permute-start.9 = (bf16[16,64,512]{2,1,0:T(8,128)(2,1)}, bf16[16,64,512]{2,1,0:T(8,128)(2,1)}, u32[]{:S(2)}, u32[]{:S(2)}) collective-permute-start(bf16[16,64,512]{2,1,0:T(8,128)(2,1)} %all-gather.2.cloned.1.call-done.refs_5_), channel_id=1, source_target_pairs={{0,384},{128,0},{256,128},{384,256},{1,385},{129,1},{257,129},{385... | collective-permute-start | bytes 3145736 | tf_op jit(solution)/shard_map/ppermute | solution.py:282
  113.9 1.2 copy-start.4
  115.1 3.1 %copy-start.2 = (bf16[16,64,512]{2,1,0:T(8,128)(2,1)S(1)}, bf16[16,64,512]{2,1,0:T(8,128)(2,1)}, u32[]{:S(2)}) copy-start(bf16[16,64,512]{2,1,0:T(8,128)(2,1)} %all-gather.2.cloned.1.call-done.refs_5_) | copy-start | bytes 3145732
  118.3 32.9 %collective-permute-start.11 = (bf16[16,64,512]{2,1,0:T(8,128)(2,1)S(1)}, bf16[16,64,512]{2,1,0:T(8,128)(2,1)S(1)}, u32[]{:S(2)}, u32[]{:S(2)}) collective-permute-start(bf16[16,64,512]{2,1,0:T(8,128)(2,1)S(1)} %copy-done.2), channel_id=1, source_target_pairs={{0,256},{128,384},{256,0},{384,128},{1,257},{129,385},{257,1},{385... | collective-permute-start | bytes 3145736 | tf_op jit(solution)/shard_map/ppermute | solution.py:282
  121.6 15.7 %collective-permute-start.8 = (bf16[512,512]{1,0:T(8,128)(2,1)S(1)}, bf16[512,512]{1,0:T(8,128)(2,1)S(1)}, u32[]{:S(2)}, u32[]{:S(2)}) collective-permute-start(bf16[512,512]{1,0:T(8,128)(2,1)S(1)} %shard_map.89.refs_1_), channel_id=1, source_target_pairs={{0,3},{1,0},{2,1},{3,2},{4,7},{5,4},{6,5},{7,6},{8,11},{9,8},{10,9... | collective-permute-start | bytes 1572872 | tf_op jit(solution)/shard_map/ppermute | solution.py:282
  125.7 11.5 %collective-permute-start.7 = (bf16[512,512]{1,0:T(8,128)(2,1)S(1)}, bf16[512,512]{1,0:T(8,128)(2,1)S(1)}, u32[]{:S(2)}, u32[]{:S(2)}) collective-permute-start(bf16[512,512]{1,0:T(8,128)(2,1)S(1)} %shard_map.89.refs_1_), channel_id=1, source_target_pairs={{0,2},{1,3},{2,0},{3,1},{4,6},{5,7},{6,4},{7,5},{8,10},{9,11},{10,... | collective-permute-start | bytes 1572872 | tf_op jit(solution)/shard_map/ppermute | solution.py:282
  128.2 16.6 %collective-permute-start.6 = (bf16[512,512]{1,0:T(8,128)(2,1)S(1)}, bf16[512,512]{1,0:T(8,128)(2,1)S(1)}, u32[]{:S(2)}, u32[]{:S(2)}) collective-permute-start(bf16[512,512]{1,0:T(8,128)(2,1)S(1)} %shard_map.89.refs_1_), channel_id=1, source_target_pairs={{0,1},{1,2},{2,3},{3,0},{4,5},{5,6},{6,7},{7,4},{8,9},{9,10},{10,1... | collective-permute-start | bytes 1572872 | tf_op jit(solution)/shard_map/ppermute | solution.py:282
  154.5 24.9 %collective-permute-start.12 = (bf16[256,1024]{1,0:T(8,128)(2,1)S(1)}, bf16[256,1024]{1,0:T(8,128)(2,1)S(1)}, u32[]{:S(2)}, u32[]{:S(2)}) collective-permute-start(bf16[256,1024]{1,0:T(8,128)(2,1)S(1)} %shard_map.91), channel_id=1, source_target_pairs={{0,4},{4,0},{1,5},{5,1},{2,6},{6,2},{3,7},{7,3},{8,12},{12,8},{9,1... | collective-permute-start | bytes 1572872 | tf_op jit(solution)/shard_map/ppermute | solution.py:21
Sparse Core Ops, SparseCore 0:
  35.0 69.1 all-gather.1

commit v20 on v19

--- a/solution.py
+++ b/solution.py
@@ -249,16 +249,19 @@
 def project_body(other, at, b0, b1, b2, b3, w0, w1, w2, w3, out, left, right, sems):
     row = (1 - at[0]) if other else at[0]
     rows = pl.ds(pl.multiple_of(row * 256, 256), 256)
-    copies = [
-        pltpu.make_async_copy(w, right.at[k], sems.at[k]) for k, w in enumerate((w0, w1, w2, w3))
-    ]
+    copies = []
+    for j, block in enumerate((b0, b1, b2, b3)):
+        spot = (at[4] + 4 - j) % 4
+        copies.append(pltpu.make_async_copy(block.at[rows], left.at[spot], sems.at[0, j]))
+    for k, w in enumerate((w0, w1, w2, w3)):
+        copies.append(pltpu.make_async_copy(w, right.at[k], sems.at[1, k]))
     for copy in copies:
         copy.start()
-    for j, block in enumerate((b0, b1, b2, b3)):
-        left[(at[4] + 4 - j) % 4] = block[rows, :]
+    for copy in copies[:4]:
+        copy.wait()
     total = 0.0
     for k, turn in enumerate((0, 1, 3, 2)):
-        copies[k].wait()
+        copies[4 + k].wait()
         total += dot(left[(at[3] + turn) % 4], right[k].reshape(1024, 512), NT)
     out[...] = total.astype(out.dtype)
 
@@ -271,9 +274,9 @@
         scratch=[
             pltpu.VMEM((4, 256, 512), BF),
             pltpu.VMEM((4, 16, 64, 512), BF),
-            pltpu.SemaphoreType.DMA((4,)),
+            pltpu.SemaphoreType.DMA((2, 4)),
         ],
-        hbm=range(5, 9),
+        hbm=range(1, 9),
         vmem=20,
     )[0]
 
@@ -295,6 +298,7 @@
             for k in range(2)
         ]
         turned.append(lax.ppermute(half, ("y", "c", "x"), perm))
+    mine = jnp.where(c == 0, jnp.concatenate(turned), jnp.concatenate(turned[::-1]))
     block = ((ROWS, 512), BF)
     keep, send = call(
         pack_body,
@@ -308,8 +312,7 @@
         hbm=range(1, 7),
         vmem=60,
     )
-    turned, send = lax.optimization_barrier((turned, send))
-    mine = jnp.where(c == 0, jnp.concatenate(turned), jnp.concatenate(turned[::-1]))
+    mine, send = lax.optimization_barrier((mine, send))
     gathered = lax.all_gather(mine, ("a", "p", "q"))
 
     got = swap(send)
@@ -340,13 +343,11 @@
         scratch=[pltpu.VMEM((4, 144, 256), BF)],
     )
     _, gathered = lax.optimization_barrier((coef, gathered))
-    rights = [gathered] + [shift(gathered, "y", 4 - k) for k in (1, 3)]
+    rights = [gathered] + [shift(gathered, "y", 4 - k) for k in (1, 3, 2)]
     (normed,) = call(
         norm_body, [((512, 512), BF)], (at, keep, got, norm_gain[None], mixture, coef, states)
     )
 
-    _, gathered = lax.optimization_barrier((normed, gathered))
-    rights.append(shift(gathered, "y", 2))
     blocks = [normed] + [shift(normed, "x", j) for j in (1, 2, 3)]
     theirs = swap(project(at, blocks, rights, True))
     own = project(at, blocks, rights, False)

time: 188 us -> 166 us (0.88)
  the two profiles are of different devices: /device:TPU:33 before, /device:TPU:1 now
where the time goes in v20:
time: 166 us; the launch traced here: 165 us
  starting transfers between devices  60.6 us (37%)
  waiting for transfers between devices  35 us (21%)
  Pallas kernels  24.9 us (15%)
  blocking collectives  24.5 us (15%)
  between operations  13.7 us (8%)
  local copies, waits for them, and re-layouts  4.84 us (3%)
    ppermute x6, waiting for transfers between devices, shift(): return lax.ppermute(value, axis, [(i, (i + by) % 4) for i in range(4)])  25.1 us
    pallas_call x10, Pallas kernels, call(): pl.pallas_call(run, out_shape=[jax.ShapeDtypeStruct(*o) for o in outs], i...  24.9 us
    ppermute x6, starting transfers between devices, shift(): return lax.ppermute(value, axis, [(i, (i + by) % 4) for i in range(4)])  20 us
    all_to_all x1, blocking collectives, shards(): rows = lax.all_to_all(pay_y, 'y', 0, 0, tiled=True)  16.1 us
    all_to_all x1, starting transfers between devices, shards(): far = lax.all_to_all(pay_a, 'a', 0, 0, tiled=True)  9.77 us
    ppermute x2, starting transfers between devices, shards(): turned.append(lax.ppermute(half, ('y', 'c', 'x'), perm))  9.44 us
    ppermute x3, starting transfers between devices, shards(): lax.ppermute(near[k], NEAR, [(i, i ^ k) for i in range(4)])  9.26 us
    all_to_all x1, blocking collectives, shards(): near = lax.all_to_all(pay_b, NEAR, 0, 0, tiled=True)  8.41 us
  transfers between devices with their start and end apart: 16, of which 5 were waited for; matrix products, arithmetic and copies ran while one was open for 0% of the time, Pallas kernels for 13%

profile of v20, /device:TPU:1, one launch (start us, length us, event | category | flops | bytes accessed | tf_op | source)
XLA Modules:
  0.0 165.1 jit_solution(6280184977037746597)
XLA Ops:
  8.0 8.8 %collective-permute-start.1 = (bf16[32,512]{1,0:T(8,128)(2,1)S(1)}, bf16[32,512]{1,0:T(8,128)(2,1)S(1)}, u32[]{:S(2)}, u32[]{:S(2)}) collective-permute-start(bf16[32,512]{1,0:T(8,128)(2,1)S(1)} %get-tuple-element.44), channel_id=1, source_target_pairs={{0,4},{4,0},{1,132},{5,128},{2,260},{6,256},{3,388},{7,384},{128,5... | collective-permute-start | bytes 98312 | tf_op jit(solution)/shard_map/ppermute | solution.py:300
  17.4 3.8 %shard_map.82 = (bf16[1072,512]{1,0:T(8,128)(2,1)}, bf16[1072,512]{1,0:T(8,128)(2,1)}) custom-call(s32[5]{0:T(128)} %stack.23.refs_0_, bf16[256,1024]{1,0:T(8,128)(2,1)} %refs_1_.1, bf16[256,1024]{1,0:T(8,128)(2,1)} %refs_2_.1, bf16[256,1024]{1,0:T(8,128)(2,1)} %refs_3_.1, bf16[256,1024]{1,0:T(8,128)(2,1)} %refs_4_.1, f32[8,256]{1,0:T(8,128)} %refs_5_.1, ...), custom_call_target="tpu_custom_call" | custom-call | flops 1000000 | bytes 1000000 | tf_op jit(solution)/shard_map/pallas_call | solution.py:59
  23.8 2.9 %collective-permute-done.2.refs_2_ = bf16[1072,512]{1,0:T(8,128)(2,1)S(1)} collective-permute-done((bf16[1072,512]{1,0:T(8,128)(2,1)}, bf16[1072,512]{1,0:T(8,128)(2,1)S(1)}, u32[]{:S(2)}, u32[]{:S(2)}) %collective-permute-start.2) | collective-permute-done | bytes 1097760 | tf_op jit(solution)/shard_map/ppermute | solution.py:21
  29.7 8.4 %all_to_all.20.refs_1_ = bf16[4,144,128]{2,1,0:T(8,128)(2,1)S(1)} all-to-all(bf16[4,144,128]{2,1,0:T(8,128)(2,1)S(1)} %get-tuple-element.30), channel_id=1, replica_groups=mesh['y'=4,'a'=4,'p'=2,'q'=2,'c'=2,'x'=4] {'p','q'}, dimensions={0} | all-to-all | bytes 294912 | tf_op jit(solution)/shard_map/all_to_all | solution.py:321
  39.4 9.8 %all-to-all-start.1 = ((bf16[4,144,128]{2,1,0:T(8,128)(2,1)}), bf16[4,144,128]{2,1,0:T(8,128)(2,1)S(1)}, u32[]{:S(2)}, u32[]{:S(2)}) async-start(bf16[4,144,128]{2,1,0:T(8,128)(2,1)} %get-tuple-element.37), calls=%async_computation.1 | async-start | bytes 294912 | tf_op jit(solution)/shard_map/all_to_all | solution.py:323
  49.2 2.1 %collective-permute-start.3 = (bf16[144,256]{1,0:T(8,128)(2,1)S(1)}, bf16[144,256]{1,0:T(8,128)(2,1)S(1)}, u32[]{:S(2)}, u32[]{:S(2)}) collective-permute-start(bf16[144,256]{1,0:T(8,128)(2,1)S(1)} %get-tuple-element.32), channel_id=1, source_target_pairs={{0,8},{8,0},{16,24},{24,16},{1,9},{9,1},{17,25},{25,17},{2,10},{10... | collective-permute-start | bytes 221192 | tf_op jit(solution)/shard_map/ppermute | solution.py:325
  51.2 3.8 %collective-permute-start.4 = (bf16[144,256]{1,0:T(8,128)(2,1)S(1)}, bf16[144,256]{1,0:T(8,128)(2,1)S(1)}, u32[]{:S(2)}, u32[]{:S(2)}) collective-permute-start(bf16[144,256]{1,0:T(8,128)(2,1)S(1)} %get-tuple-element.33), channel_id=1, source_target_pairs={{0,16},{8,24},{16,0},{24,8},{1,17},{9,25},{17,1},{25,9},{2,18},{10... | collective-permute-start | bytes 221192 | tf_op jit(solution)/shard_map/ppermute | solution.py:325
  55.0 3.4 %collective-permute-start.5 = (bf16[144,256]{1,0:T(8,128)(2,1)S(1)}, bf16[144,256]{1,0:T(8,128)(2,1)S(1)}, u32[]{:S(2)}, u32[]{:S(2)}) collective-permute-start(bf16[144,256]{1,0:T(8,128)(2,1)S(1)} %get-tuple-element.34), channel_id=1, source_target_pairs={{0,24},{8,16},{16,8},{24,0},{1,25},{9,17},{17,9},{25,1},{2,26},{10... | collective-permute-start | bytes 221192 | tf_op jit(solution)/shard_map/ppermute | solution.py:325
  58.4 2.1 %collective-permute-done.4.refs_7_.refs_3_ = bf16[144,256]{1,0:T(8,128)(2,1)S(1)} collective-permute-done((bf16[144,256]{1,0:T(8,128)(2,1)S(1)}, bf16[144,256]{1,0:T(8,128)(2,1)S(1)}, u32[]{:S(2)}, u32[]{:S(2)}) %collective-permute-start.4) | collective-permute-done | bytes 73760 | tf_op jit(solution)/shard_map/ppermute | solution.py:325
  60.5 4.3 %collective-permute-done.5.refs_8_.refs_4_ = bf16[144,256]{1,0:T(8,128)(2,1)S(1)} collective-permute-done((bf16[144,256]{1,0:T(8,128)(2,1)S(1)}, bf16[144,256]{1,0:T(8,128)(2,1)S(1)}, u32[]{:S(2)}, u32[]{:S(2)}) %collective-permute-start.5) | collective-permute-done | bytes 73760 | tf_op jit(solution)/shard_map/ppermute | solution.py:325
  65.4 16.1 %all_to_all.21.refs_1_ = bf16[4,144,128]{2,1,0:T(8,128)(2,1)S(1)} all-to-all(bf16[4,144,128]{2,1,0:T(8,128)(2,1)S(1)} %get-tuple-element.38), channel_id=1, replica_groups=mesh['y'=4,'a'=4,'p'=2,'q'=2,'c'=2,'x'=4] {'y'}, dimensions={0} | all-to-all | bytes 294912 | tf_op jit(solution)/shard_map/all_to_all | solution.py:336
  82.9 5.0 %all-to-all-start.3 = ((bf16[4,128,512]{2,1,0:T(8,128)(2,1)}), bf16[4,128,512]{2,1,0:T(8,128)(2,1)}, u32[]{:S(2)}, u32[]{:S(2)}) async-start(bf16[4,128,512]{2,1,0:T(8,128)(2,1)} %shard_map.88), calls=%async_computation.3 | async-start | bytes 1048576 | tf_op jit(solution)/shard_map/all_to_all | solution.py:338
  88.0 4.3 %shard_map.84 = (f32[512,512]{1,0:T(8,128)S(1)}, f32[512,24]{1,0:T(8,128)S(1)}) custom-call(s32[5]{0:T(128)S(1)} %copy-done.5, bf16[1072,512]{1,0:T(8,128)(2,1)S(1)} %copy-done.1, bf16[1072,512]{1,0:T(8,128)(2,1)S(1)} %collective-permute-done.2.refs_2_, bf16[4,128,128]{2,1,0:T(8,128)(2,1)S(1)} %get-tuple-element.27.refs_3_), custom_call_target="tpu_custom_call" | custom-call | flops 1000000 | bytes 1000000 | tf_op jit(solution)/shard_map/pallas_call | solution.py:59
  95.7 5.0 %collective-permute-start.11 = (bf16[16,64,512]{2,1,0:T(8,128)(2,1)}, bf16[16,64,512]{2,1,0:T(8,128)(2,1)S(1)}, u32[]{:S(2)}, u32[]{:S(2)}) collective-permute-start(bf16[16,64,512]{2,1,0:T(8,128)(2,1)} %bitcast.6), channel_id=1, source_target_pairs={{0,256},{128,384},{256,0},{384,128},{1,257},{129,385},{257,1},{385... | collective-permute-start | bytes 3145736 | tf_op jit(solution)/shard_map/ppermute | solution.py:285
  100.6 2.1 %collective-permute-start.10 = (bf16[16,64,512]{2,1,0:T(8,128)(2,1)}, bf16[16,64,512]{2,1,0:T(8,128)(2,1)}, u32[]{:S(2)}, u32[]{:S(2)}) collective-permute-start(bf16[16,64,512]{2,1,0:T(8,128)(2,1)} %bitcast.7), channel_id=1, source_target_pairs={{0,128},{128,256},{256,384},{384,0},{1,129},{129,257},{257,385},{3... | collective-permute-start | bytes 3145736 | tf_op jit(solution)/shard_map/ppermute | solution.py:285
  102.8 4.4 %collective-permute-start.9 = (bf16[16,64,512]{2,1,0:T(8,128)(2,1)}, bf16[16,64,512]{2,1,0:T(8,128)(2,1)}, u32[]{:S(2)}, u32[]{:S(2)}) collective-permute-start(bf16[16,64,512]{2,1,0:T(8,128)(2,1)} %bitcast.8), channel_id=1, source_target_pairs={{0,384},{128,0},{256,128},{384,256},{1,385},{129,1},{257,129},{385... | collective-permute-start | bytes 3145736 | tf_op jit(solution)/shard_map/ppermute | solution.py:285
  108.4 3.1 %shard_map.89.refs_1_ = bf16[512,512]{1,0:T(8,128)(2,1)S(1)} custom-call(s32[5]{0:T(128)S(1)} %copy-done.5, bf16[1072,512]{1,0:T(8,128)(2,1)S(1)} %copy-done.1, bf16[1072,512]{1,0:T(8,128)(2,1)S(1)} %collective-permute-done.2.refs_2_, bf16[1,1024]{1,0:T(2,128)(2,1)S(1)} %broadcast_in_dim.3.refs_3_, f32[512,512]{1,0:T(8,128)S(1)} %copy-done.4, ...), custom_call_target="tpu_custom_call" | custom-call | flops 1000000 | bytes 1000000 | tf_op jit(solution)/shard_map/pallas_call | solution.py:59
  111.5 3.7 %collective-permute-start.8 = (bf16[512,512]{1,0:T(8,128)(2,1)S(1)}, bf16[512,512]{1,0:T(8,128)(2,1)S(1)}, u32[]{:S(2)}, u32[]{:S(2)}) collective-permute-start(bf16[512,512]{1,0:T(8,128)(2,1)S(1)} %shard_map.89.refs_1_), channel_id=1, source_target_pairs={{0,3},{1,0},{2,1},{3,2},{4,7},{5,4},{6,5},{7,6},{8,11},{9,8},{10,9... | collective-permute-start | bytes 1572872 | tf_op jit(solution)/shard_map/ppermute | solution.py:285
  115.3 2.1 %collective-permute-start.7 = (bf16[512,512]{1,0:T(8,128)(2,1)S(1)}, bf16[512,512]{1,0:T(8,128)(2,1)S(1)}, u32[]{:S(2)}, u32[]{:S(2)}) collective-permute-start(bf16[512,512]{1,0:T(8,128)(2,1)S(1)} %shard_map.89.refs_1_), channel_id=1, source_target_pairs={{0,2},{1,3},{2,0},{3,1},{4,6},{5,7},{6,4},{7,5},{8,10},{9,11},{10,... | collective-permute-start | bytes 1572872 | tf_op jit(solution)/shard_map/ppermute | solution.py:285
  117.4 2.8 %collective-permute-start.6 = (bf16[512,512]{1,0:T(8,128)(2,1)S(1)}, bf16[512,512]{1,0:T(8,128)(2,1)S(1)}, u32[]{:S(2)}, u32[]{:S(2)}) collective-permute-start(bf16[512,512]{1,0:T(8,128)(2,1)S(1)} %shard_map.89.refs_1_), channel_id=1, source_target_pairs={{0,1},{1,2},{2,3},{3,0},{4,5},{5,6},{6,7},{7,4},{8,9},{9,10},{10,1... | collective-permute-start | bytes 1572872 | tf_op jit(solution)/shard_map/ppermute | solution.py:285
  120.2 25.1 %collective-permute-done.10.refs_7_ = bf16[16,64,512]{2,1,0:T(8,128)(2,1)} collective-permute-done((bf16[16,64,512]{2,1,0:T(8,128)(2,1)}, bf16[16,64,512]{2,1,0:T(8,128)(2,1)}, u32[]{:S(2)}, u32[]{:S(2)}) %collective-permute-start.10) | collective-permute-done | bytes 1048608 | tf_op jit(solution)/shard_map/ppermute | solution.py:285
  145.3 3.4 %shard_map.91 = bf16[256,1024]{1,0:T(8,128)(2,1)S(1)} custom-call(s32[5]{0:T(128)S(1)} %copy-done.5, bf16[512,512]{1,0:T(8,128)(2,1)S(1)} %shard_map.89.refs_1_, bf16[512,512]{1,0:T(8,128)(2,1)S(1)} %collective-permute-done.6.refs_2_, bf16[512,512]{1,0:T(8,128)(2,1)S(1)} %collective-permute-done.7.refs_3_, ...), custom_call_target="tpu_custom_call" | custom-call | flops 1000000 | bytes 1000000 | tf_op jit(solution)/shard_map/pallas_call | solution.py:59
  148.8 5.1 %collective-permute-start.12 = (bf16[256,1024]{1,0:T(8,128)(2,1)S(1)}, bf16[256,1024]{1,0:T(8,128)(2,1)S(1)}, u32[]{:S(2)}, u32[]{:S(2)}) collective-permute-start(bf16[256,1024]{1,0:T(8,128)(2,1)S(1)} %shard_map.91), channel_id=1, source_target_pairs={{0,4},{4,0},{1,5},{5,1},{2,6},{6,2},{3,7},{7,3},{8,12},{12,8},{9,1... | collective-permute-start | bytes 1572872 | tf_op jit(solution)/shard_map/ppermute | solution.py:21
  153.9 3.4 %shard_map.90 = f32[256,1024]{1,0:T(8,128)S(1)} custom-call(s32[5]{0:T(128)S(1)} %copy-done.5, bf16[512,512]{1,0:T(8,128)(2,1)S(1)} %shard_map.89.refs_1_, bf16[512,512]{1,0:T(8,128)(2,1)S(1)} %collective-permute-done.6.refs_2_, bf16[512,512]{1,0:T(8,128)(2,1)S(1)} %collective-permute-done.7.refs_3_, bf16[512,512]{1,0:T(8,128)(2,1)S(1)} %collective-permute-done.8.refs_4_, ...), custom_call_target="tpu_custom_call" | custom-call | flops 1000000 | bytes 1000000 | tf_op jit(solution)/shard_map/pallas_call | solution.py:59
  (40 shorter events, 16.4 us)
Async XLA Ops:
  6.5 89.1 %all-gather.3.cloned.1.call-start = ((), (), s32[]{:S(2)}) async-start(), calls=%async_computation.4 | async-start | bytes 1114112 | tf_op jit(solution)/shard_map/all_gather | solution.py:316
  7.3 13.9 %collective-permute-start = (bf16[32,512]{1,0:T(8,128)(2,1)S(1)}, bf16[32,512]{1,0:T(8,128)(2,1)S(1)}, u32[]{:S(2)}, u32[]{:S(2)}) collective-permute-start(bf16[32,512]{1,0:T(8,128)(2,1)S(1)} %get-tuple-element.43), channel_id=1, source_target_pairs={{0,0},{4,4},{1,128},{5,132},{2,256},{6,260},{3,384},{7,388},{128,1... | collective-permute-start | bytes 98312 | tf_op jit(solution)/shard_map/ppermute | solution.py:300
  8.0 13.2 %collective-permute-start.1 = (bf16[32,512]{1,0:T(8,128)(2,1)S(1)}, bf16[32,512]{1,0:T(8,128)(2,1)S(1)}, u32[]{:S(2)}, u32[]{:S(2)}) collective-permute-start(bf16[32,512]{1,0:T(8,128)(2,1)S(1)} %get-tuple-element.44), channel_id=1, source_target_pairs={{0,4},{4,0},{1,132},{5,128},{2,260},{6,256},{3,388},{7,384},{128,5... | collective-permute-start | bytes 98312 | tf_op jit(solution)/shard_map/ppermute | solution.py:300
  17.4 9.3 %copy-start.5 = (s32[5]{0:T(128)S(1)}, s32[5]{0:T(128)}, u32[]{:S(2)}) copy-start(s32[5]{0:T(128)} %stack.23.refs_0_) | copy-start | bytes 64
  21.9 4.8 %collective-permute-start.2 = (bf16[1072,512]{1,0:T(8,128)(2,1)}, bf16[1072,512]{1,0:T(8,128)(2,1)S(1)}, u32[]{:S(2)}, u32[]{:S(2)}) collective-permute-start(bf16[1072,512]{1,0:T(8,128)(2,1)} %get-tuple-element.26), channel_id=1, source_target_pairs={{0,4},{4,0},{1,5},{5,1},{2,6},{6,2},{3,7},{7,3},{8,12},{12,8},{9,1... | collective-permute-start | bytes 3293192 | tf_op jit(solution)/shard_map/ppermute | solution.py:21
  26.7 1.2 copy-start
  39.4 25.4 %all-to-all-start.1 = ((bf16[4,144,128]{2,1,0:T(8,128)(2,1)}), bf16[4,144,128]{2,1,0:T(8,128)(2,1)S(1)}, u32[]{:S(2)}, u32[]{:S(2)}) async-start(bf16[4,144,128]{2,1,0:T(8,128)(2,1)} %get-tuple-element.37), calls=%async_computation.1 | async-start | bytes 294912 | tf_op jit(solution)/shard_map/all_to_all | solution.py:323
  49.2 9.3 %collective-permute-start.3 = (bf16[144,256]{1,0:T(8,128)(2,1)S(1)}, bf16[144,256]{1,0:T(8,128)(2,1)S(1)}, u32[]{:S(2)}, u32[]{:S(2)}) collective-permute-start(bf16[144,256]{1,0:T(8,128)(2,1)S(1)} %get-tuple-element.32), channel_id=1, source_target_pairs={{0,8},{8,0},{16,24},{24,16},{1,9},{9,1},{17,25},{25,17},{2,10},{10... | collective-permute-start | bytes 221192 | tf_op jit(solution)/shard_map/ppermute | solution.py:325
  51.2 9.3 %collective-permute-start.4 = (bf16[144,256]{1,0:T(8,128)(2,1)S(1)}, bf16[144,256]{1,0:T(8,128)(2,1)S(1)}, u32[]{:S(2)}, u32[]{:S(2)}) collective-permute-start(bf16[144,256]{1,0:T(8,128)(2,1)S(1)} %get-tuple-element.33), channel_id=1, source_target_pairs={{0,16},{8,24},{16,0},{24,8},{1,17},{9,25},{17,1},{25,9},{2,18},{10... | collective-permute-start | bytes 221192 | tf_op jit(solution)/shard_map/ppermute | solution.py:325
  55.0 9.7 %collective-permute-start.5 = (bf16[144,256]{1,0:T(8,128)(2,1)S(1)}, bf16[144,256]{1,0:T(8,128)(2,1)S(1)}, u32[]{:S(2)}, u32[]{:S(2)}) collective-permute-start(bf16[144,256]{1,0:T(8,128)(2,1)S(1)} %get-tuple-element.34), channel_id=1, source_target_pairs={{0,24},{8,16},{16,8},{24,0},{1,25},{9,17},{17,9},{25,1},{2,26},{10... | collective-permute-start | bytes 221192 | tf_op jit(solution)/shard_map/ppermute | solution.py:325
  65.4 22.6 %copy-start.1 = (bf16[1072,512]{1,0:T(8,128)(2,1)S(1)}, bf16[1072,512]{1,0:T(8,128)(2,1)}, u32[]{:S(2)}) copy-start(bf16[1072,512]{1,0:T(8,128)(2,1)} %get-tuple-element.24.refs_1_) | copy-start | bytes 3293188
  82.9 24.3 %all-to-all-start.3 = ((bf16[4,128,512]{2,1,0:T(8,128)(2,1)}), bf16[4,128,512]{2,1,0:T(8,128)(2,1)}, u32[]{:S(2)}, u32[]{:S(2)}) async-start(bf16[4,128,512]{2,1,0:T(8,128)(2,1)} %shard_map.88), calls=%async_computation.3 | async-start | bytes 1048576 | tf_op jit(solution)/shard_map/all_to_all | solution.py:338
  92.3 14.8 %copy-start.6 = (bf16[1024]{0:T(1024)(128)(2,1)S(1)}, bf16[1024]{0:T(1024)(128)(2,1)}, u32[]{:S(2)}) copy-start(bf16[1024]{0:T(1024)(128)(2,1)} %param.14) | copy-start | bytes 6148
  94.0 1.0 copy-start.3
  95.7 21.7 %collective-permute-start.11 = (bf16[16,64,512]{2,1,0:T(8,128)(2,1)}, bf16[16,64,512]{2,1,0:T(8,128)(2,1)S(1)}, u32[]{:S(2)}, u32[]{:S(2)}) collective-permute-start(bf16[16,64,512]{2,1,0:T(8,128)(2,1)} %bitcast.6), channel_id=1, source_target_pairs={{0,256},{128,384},{256,0},{384,128},{1,257},{129,385},{257,1},{385... | collective-permute-start | bytes 3145736 | tf_op jit(solution)/shard_map/ppermute | solution.py:285
  100.6 44.6 %collective-permute-start.10 = (bf16[16,64,512]{2,1,0:T(8,128)(2,1)}, bf16[16,64,512]{2,1,0:T(8,128)(2,1)}, u32[]{:S(2)}, u32[]{:S(2)}) collective-permute-start(bf16[16,64,512]{2,1,0:T(8,128)(2,1)} %bitcast.7), channel_id=1, source_target_pairs={{0,128},{128,256},{256,384},{384,0},{1,129},{129,257},{257,385},{3... | collective-permute-start | bytes 3145736 | tf_op jit(solution)/shard_map/ppermute | solution.py:285
  102.8 42.5 %collective-permute-start.9 = (bf16[16,64,512]{2,1,0:T(8,128)(2,1)}, bf16[16,64,512]{2,1,0:T(8,128)(2,1)}, u32[]{:S(2)}, u32[]{:S(2)}) collective-permute-start(bf16[16,64,512]{2,1,0:T(8,128)(2,1)} %bitcast.8), channel_id=1, source_target_pairs={{0,384},{128,0},{256,128},{384,256},{1,385},{129,1},{257,129},{385... | collective-permute-start | bytes 3145736 | tf_op jit(solution)/shard_map/ppermute | solution.py:285
  107.2 1.2 copy-start.4
  108.4 36.9 %copy-start.2 = (bf16[1024,512]{1,0:T(8,128)(2,1)S(1)}, bf16[1024,512]{1,0:T(8,128)(2,1)}, u32[]{:S(2)}) copy-start(bf16[1024,512]{1,0:T(8,128)(2,1)} %all-gather.3.cloned.1.call-done) | copy-start | bytes 3145732
  111.5 33.7 %collective-permute-start.8 = (bf16[512,512]{1,0:T(8,128)(2,1)S(1)}, bf16[512,512]{1,0:T(8,128)(2,1)S(1)}, u32[]{:S(2)}, u32[]{:S(2)}) collective-permute-start(bf16[512,512]{1,0:T(8,128)(2,1)S(1)} %shard_map.89.refs_1_), channel_id=1, source_target_pairs={{0,3},{1,0},{2,1},{3,2},{4,7},{5,4},{6,5},{7,6},{8,11},{9,8},{10,9... | collective-permute-start | bytes 1572872 | tf_op jit(solution)/shard_map/ppermute | solution.py:285
  115.3 30.0 %collective-permute-start.7 = (bf16[512,512]{1,0:T(8,128)(2,1)S(1)}, bf16[512,512]{1,0:T(8,128)(2,1)S(1)}, u32[]{:S(2)}, u32[]{:S(2)}) collective-permute-start(bf16[512,512]{1,0:T(8,128)(2,1)S(1)} %shard_map.89.refs_1_), channel_id=1, source_target_pairs={{0,2},{1,3},{2,0},{3,1},{4,6},{5,7},{6,4},{7,5},{8,10},{9,11},{10,... | collective-permute-start | bytes 1572872 | tf_op jit(solution)/shard_map/ppermute | solution.py:285
  117.4 27.9 %collective-permute-start.6 = (bf16[512,512]{1,0:T(8,128)(2,1)S(1)}, bf16[512,512]{1,0:T(8,128)(2,1)S(1)}, u32[]{:S(2)}, u32[]{:S(2)}) collective-permute-start(bf16[512,512]{1,0:T(8,128)(2,1)S(1)} %shard_map.89.refs_1_), channel_id=1, source_target_pairs={{0,1},{1,2},{2,3},{3,0},{4,5},{5,6},{6,7},{7,4},{8,9},{9,10},{10,1... | collective-permute-start | bytes 1572872 | tf_op jit(solution)/shard_map/ppermute | solution.py:285
  148.8 8.6 %collective-permute-start.12 = (bf16[256,1024]{1,0:T(8,128)(2,1)S(1)}, bf16[256,1024]{1,0:T(8,128)(2,1)S(1)}, u32[]{:S(2)}, u32[]{:S(2)}) collective-permute-start(bf16[256,1024]{1,0:T(8,128)(2,1)S(1)} %shard_map.91), channel_id=1, source_target_pairs={{0,4},{4,0},{1,5},{5,1},{2,6},{6,2},{3,7},{7,3},{8,12},{12,8},{9,1... | collective-permute-start | bytes 1572872 | tf_op jit(solution)/shard_map/ppermute | solution.py:21
Sparse Core Ops, SparseCore 0:
  23.9 71.6 all-gather.2

commit v21 on v20

--- a/solution.py
+++ b/solution.py
@@ -286,7 +286,7 @@
 
 
 def shards(values, keys, queries, gates, log_decay, level_mix, norm_gain, weight):
-    y, a, b, c, x = (lax.axis_index(n) for n in ("y", "a", NEAR, "c", "x"))
+    y, a, b, q, c, x = (lax.axis_index(n) for n in ("y", "a", NEAR, "q", "c", "x"))
     at = jnp.stack([c, b, a, y, x]).astype(jnp.int32)
     turned = []
     for other in range(2):
@@ -313,11 +313,15 @@
         vmem=60,
     )
     mine, send = lax.optimization_barrier((mine, send))
-    gathered = lax.all_gather(mine, ("a", "p", "q"))
+    theirs = lax.ppermute(mine, "q", [(0, 1), (1, 0)])
 
     got = swap(send)
     pay = ((4, 144, 128), BF)
     pay_b, first = call(ends_body, [pay, ((4, 128, 128), BF)], (at, keep, got))
+    theirs, pay_b = lax.optimization_barrier((theirs, pay_b))
+    mine = jnp.stack([jnp.where(q == 0, mine, theirs), jnp.where(q == 0, theirs, mine)])
+    gathered = lax.all_gather(mine, ("a", "p"), axis=0, tiled=True)
+
     near = lax.all_to_all(pay_b, NEAR, 0, 0, tiled=True)
     pay_a, *near = call(near_body, [pay] + [((144, 256), BF)] * 4, (at, near))
     far = lax.all_to_all(pay_a, "a", 0, 0, tiled=True)

time: 166 us -> 169 us (1.018)
  waiting for transfers between devices: 35 us -> 39.1 us
  starting transfers between devices: 60.6 us -> 58.6 us
    ppermute x3, waiting for transfers between devices: 6.32 us -> 10.9 us  [shards(): lax.ppermute(near[k], NEAR, [(i, i ^ k) for i in range(4)])]
    ppermute x2, starting transfers between devices: 7.02 us -> 4.32 us  [swap(): return lax.ppermute(value, 'c', [(0, 1), (1, 0)])]
    ppermute x6, waiting for transfers between devices: 25.1 us -> 27.2 us  [shift(): return lax.ppermute(value, axis, [(i, (i + by) % 4) for i in range(4)])]
    ppermute x0 -> x1, starting transfers between devices: none -> 1.92 us  [shards(): theirs = lax.ppermute(mine, 'q', [(0, 1), (1, 0)])]
    ppermute x2, waiting for transfers between devices: 2.88 us -> 0.98 us  [swap(): return lax.ppermute(value, 'c', [(0, 1), (1, 0)])]
  transfers between devices with their start and end apart: 16 -> 17, of which waited for: 5 -> 5; matrix products, arithmetic and copies ran while one was open for 0% -> 0% of each run, Pallas kernels for 13% -> 13%
where the time goes in v21:
time: 169 us; the launch traced here: 167 us
  starting transfers between devices  58.6 us (35%)
  waiting for transfers between devices  39.1 us (23%)
  Pallas kernels  24.9 us (15%)
  blocking collectives  24.4 us (14%)
  between operations  13.7 us (8%)
  local copies, waits for them, and re-layouts  4.82 us (3%)
    ppermute x6, waiting for transfers between devices, shift(): return lax.ppermute(value, axis, [(i, (i + by) % 4) for i in range(4)])  27.2 us
    pallas_call x10, Pallas kernels, call(): pl.pallas_call(run, out_shape=[jax.ShapeDtypeStruct(*o) for o in outs], i...  24.9 us
    ppermute x6, starting transfers between devices, shift(): return lax.ppermute(value, axis, [(i, (i + by) % 4) for i in range(4)])  19.6 us
    all_to_all x1, blocking collectives, shards(): rows = lax.all_to_all(pay_y, 'y', 0, 0, tiled=True)  16.5 us
    ppermute x3, waiting for transfers between devices, shards(): lax.ppermute(near[k], NEAR, [(i, i ^ k) for i in range(4)])  10.9 us
    all_to_all x1, starting transfers between devices, shards(): far = lax.all_to_all(pay_a, 'a', 0, 0, tiled=True)  9.9 us
    ppermute x2, starting transfers between devices, shards(): turned.append(lax.ppermute(half, ('y', 'c', 'x'), perm))  9.44 us
    ppermute x3, starting transfers between devices, shards(): lax.ppermute(near[k], NEAR, [(i, i ^ k) for i in range(4)])  9.26 us
  transfers between devices with their start and end apart: 17, of which 5 were waited for; matrix products, arithmetic and copies ran while one was open for 0% of the time, Pallas kernels for 13%

profile of v21, /device:TPU:1, one launch (start us, length us, event | category | flops | bytes accessed | tf_op | source)
XLA Modules:
  0.0 167.3 jit_solution(12125344362914772392)
XLA Ops:
  8.0 8.8 %collective-permute-start.1 = (bf16[32,512]{1,0:T(8,128)(2,1)S(1)}, bf16[32,512]{1,0:T(8,128)(2,1)S(1)}, u32[]{:S(2)}, u32[]{:S(2)}) collective-permute-start(bf16[32,512]{1,0:T(8,128)(2,1)S(1)} %get-tuple-element.50), channel_id=1, source_target_pairs={{0,4},{4,0},{1,132},{5,128},{2,260},{6,256},{3,388},{7,384},{128,5... | collective-permute-start | bytes 98312 | tf_op jit(solution)/shard_map/ppermute | solution.py:300
  17.4 3.8 %shard_map.82 = (bf16[1072,512]{1,0:T(8,128)(2,1)}, bf16[1072,512]{1,0:T(8,128)(2,1)}) custom-call(s32[5]{0:T(128)} %stack.32.refs_0_, bf16[256,1024]{1,0:T(8,128)(2,1)} %refs_1_.1, bf16[256,1024]{1,0:T(8,128)(2,1)} %refs_2_.1, bf16[256,1024]{1,0:T(8,128)(2,1)} %refs_3_.1, bf16[256,1024]{1,0:T(8,128)(2,1)} %refs_4_.1, f32[8,256]{1,0:T(8,128)} %refs_5_.1, ...), custom_call_target="tpu_custom_call" | custom-call | flops 1000000 | bytes 1000000 | tf_op jit(solution)/shard_map/pallas_call | solution.py:59
  29.8 7.9 %all_to_all.20.refs_1_ = bf16[4,144,128]{2,1,0:T(8,128)(2,1)S(1)} all-to-all(bf16[4,144,128]{2,1,0:T(8,128)(2,1)S(1)} %get-tuple-element.34), channel_id=1, replica_groups=mesh['y'=4,'a'=4,'p'=2,'q'=2,'c'=2,'x'=4] {'p','q'}, dimensions={0} | all-to-all | bytes 294912 | tf_op jit(solution)/shard_map/all_to_all | solution.py:325
  39.0 9.9 %all-to-all-start.1 = ((bf16[4,144,128]{2,1,0:T(8,128)(2,1)}), bf16[4,144,128]{2,1,0:T(8,128)(2,1)S(1)}, u32[]{:S(2)}, u32[]{:S(2)}) async-start(bf16[4,144,128]{2,1,0:T(8,128)(2,1)} %get-tuple-element.41), calls=%async_computation.1 | async-start | bytes 294912 | tf_op jit(solution)/shard_map/all_to_all | solution.py:327
  48.8 2.2 %collective-permute-start.4 = (bf16[144,256]{1,0:T(8,128)(2,1)S(1)}, bf16[144,256]{1,0:T(8,128)(2,1)S(1)}, u32[]{:S(2)}, u32[]{:S(2)}) collective-permute-start(bf16[144,256]{1,0:T(8,128)(2,1)S(1)} %get-tuple-element.36), channel_id=1, source_target_pairs={{0,8},{8,0},{16,24},{24,16},{1,9},{9,1},{17,25},{25,17},{2,10},{10... | collective-permute-start | bytes 221192 | tf_op jit(solution)/shard_map/ppermute | solution.py:329
  51.1 3.6 %collective-permute-start.5 = (bf16[144,256]{1,0:T(8,128)(2,1)S(1)}, bf16[144,256]{1,0:T(8,128)(2,1)S(1)}, u32[]{:S(2)}, u32[]{:S(2)}) collective-permute-start(bf16[144,256]{1,0:T(8,128)(2,1)S(1)} %get-tuple-element.37), channel_id=1, source_target_pairs={{0,16},{8,24},{16,0},{24,8},{1,17},{9,25},{17,1},{25,9},{2,18},{10... | collective-permute-start | bytes 221192 | tf_op jit(solution)/shard_map/ppermute | solution.py:329
  54.7 3.5 %collective-permute-start.6 = (bf16[144,256]{1,0:T(8,128)(2,1)S(1)}, bf16[144,256]{1,0:T(8,128)(2,1)S(1)}, u32[]{:S(2)}, u32[]{:S(2)}) collective-permute-start(bf16[144,256]{1,0:T(8,128)(2,1)S(1)} %get-tuple-element.38), channel_id=1, source_target_pairs={{0,24},{8,16},{16,8},{24,0},{1,25},{9,17},{17,9},{25,1},{2,26},{10... | collective-permute-start | bytes 221192 | tf_op jit(solution)/shard_map/ppermute | solution.py:329
  58.1 3.3 %collective-permute-done.4.refs_6_.refs_2_ = bf16[144,256]{1,0:T(8,128)(2,1)S(1)} collective-permute-done((bf16[144,256]{1,0:T(8,128)(2,1)S(1)}, bf16[144,256]{1,0:T(8,128)(2,1)S(1)}, u32[]{:S(2)}, u32[]{:S(2)}) %collective-permute-start.4) | collective-permute-done | bytes 73760 | tf_op jit(solution)/shard_map/ppermute | solution.py:329
  61.5 7.6 %collective-permute-done.6.refs_8_.refs_4_ = bf16[144,256]{1,0:T(8,128)(2,1)S(1)} collective-permute-done((bf16[144,256]{1,0:T(8,128)(2,1)S(1)}, bf16[144,256]{1,0:T(8,128)(2,1)S(1)}, u32[]{:S(2)}, u32[]{:S(2)}) %collective-permute-start.6) | collective-permute-done | bytes 73760 | tf_op jit(solution)/shard_map/ppermute | solution.py:329
  69.7 16.5 %all_to_all.21.refs_1_ = bf16[4,144,128]{2,1,0:T(8,128)(2,1)S(1)} all-to-all(bf16[4,144,128]{2,1,0:T(8,128)(2,1)S(1)} %get-tuple-element.42), channel_id=1, replica_groups=mesh['y'=4,'a'=4,'p'=2,'q'=2,'c'=2,'x'=4] {'y'}, dimensions={0} | all-to-all | bytes 294912 | tf_op jit(solution)/shard_map/all_to_all | solution.py:340
  87.6 4.1 %all-to-all-start.3 = ((bf16[4,128,512]{2,1,0:T(8,128)(2,1)}), bf16[4,128,512]{2,1,0:T(8,128)(2,1)}, u32[]{:S(2)}, u32[]{:S(2)}) async-start(bf16[4,128,512]{2,1,0:T(8,128)(2,1)} %shard_map.88), calls=%async_computation.3 | async-start | bytes 1048576 | tf_op jit(solution)/shard_map/all_to_all | solution.py:342
  91.8 4.3 %shard_map.84 = (f32[512,512]{1,0:T(8,128)S(1)}, f32[512,24]{1,0:T(8,128)S(1)}) custom-call(s32[5]{0:T(128)S(1)} %copy-done.5, bf16[1072,512]{1,0:T(8,128)(2,1)S(1)} %copy-done.1, bf16[1072,512]{1,0:T(8,128)(2,1)S(1)} %collective-permute-done.2.refs_2_, bf16[4,128,128]{2,1,0:T(8,128)(2,1)S(1)} %get-tuple-element.29.refs_3_), custom_call_target="tpu_custom_call" | custom-call | flops 1000000 | bytes 1000000 | tf_op jit(solution)/shard_map/pallas_call | solution.py:59
  98.8 3.0 %collective-permute-start.12 = (bf16[16,64,512]{2,1,0:T(8,128)(2,1)}, bf16[16,64,512]{2,1,0:T(8,128)(2,1)S(1)}, u32[]{:S(2)}, u32[]{:S(2)}) collective-permute-start(bf16[16,64,512]{2,1,0:T(8,128)(2,1)} %all-gather.2.cloned.1.call-done.refs_5_), channel_id=1, source_target_pairs={{0,256},{128,384},{256,0},{384,128},{1,257},{129,385},{257,1},{385... | collective-permute-start | bytes 3145736 | tf_op jit(solution)/shard_map/ppermute | solution.py:285
  101.9 2.1 %collective-permute-start.11 = (bf16[16,64,512]{2,1,0:T(8,128)(2,1)}, bf16[16,64,512]{2,1,0:T(8,128)(2,1)}, u32[]{:S(2)}, u32[]{:S(2)}) collective-permute-start(bf16[16,64,512]{2,1,0:T(8,128)(2,1)} %all-gather.2.cloned.1.call-done.refs_5_), channel_id=1, source_target_pairs={{0,128},{128,256},{256,384},{384,0},{1,129},{129,257},{257,385},{3... | collective-permute-start | bytes 3145736 | tf_op jit(solution)/shard_map/ppermute | solution.py:285
  104.0 4.4 %collective-permute-start.10 = (bf16[16,64,512]{2,1,0:T(8,128)(2,1)}, bf16[16,64,512]{2,1,0:T(8,128)(2,1)}, u32[]{:S(2)}, u32[]{:S(2)}) collective-permute-start(bf16[16,64,512]{2,1,0:T(8,128)(2,1)} %all-gather.2.cloned.1.call-done.refs_5_), channel_id=1, source_target_pairs={{0,384},{128,0},{256,128},{384,256},{1,385},{129,1},{257,129},{385... | collective-permute-start | bytes 3145736 | tf_op jit(solution)/shard_map/ppermute | solution.py:285
  109.7 3.1 %shard_map.89.refs_1_ = bf16[512,512]{1,0:T(8,128)(2,1)S(1)} custom-call(s32[5]{0:T(128)S(1)} %copy-done.5, bf16[1072,512]{1,0:T(8,128)(2,1)S(1)} %copy-done.1, bf16[1072,512]{1,0:T(8,128)(2,1)S(1)} %collective-permute-done.2.refs_2_, bf16[1,1024]{1,0:T(2,128)(2,1)S(1)} %broadcast_in_dim.3.refs_3_, f32[512,512]{1,0:T(8,128)S(1)} %copy-done.4, ...), custom_call_target="tpu_custom_call" | custom-call | flops 1000000 | bytes 1000000 | tf_op jit(solution)/shard_map/pallas_call | solution.py:59
  112.8 2.8 %collective-permute-start.9 = (bf16[512,512]{1,0:T(8,128)(2,1)S(1)}, bf16[512,512]{1,0:T(8,128)(2,1)S(1)}, u32[]{:S(2)}, u32[]{:S(2)}) collective-permute-start(bf16[512,512]{1,0:T(8,128)(2,1)S(1)} %shard_map.89.refs_1_), channel_id=1, source_target_pairs={{0,3},{1,0},{2,1},{3,2},{4,7},{5,4},{6,5},{7,6},{8,11},{9,8},{10,9... | collective-permute-start | bytes 1572872 | tf_op jit(solution)/shard_map/ppermute | solution.py:285
  115.6 3.7 %collective-permute-start.8 = (bf16[512,512]{1,0:T(8,128)(2,1)S(1)}, bf16[512,512]{1,0:T(8,128)(2,1)S(1)}, u32[]{:S(2)}, u32[]{:S(2)}) collective-permute-start(bf16[512,512]{1,0:T(8,128)(2,1)S(1)} %shard_map.89.refs_1_), channel_id=1, source_target_pairs={{0,2},{1,3},{2,0},{3,1},{4,6},{5,7},{6,4},{7,5},{8,10},{9,11},{10,... | collective-permute-start | bytes 1572872 | tf_op jit(solution)/shard_map/ppermute | solution.py:285
  119.3 3.6 %collective-permute-done.12.refs_8_ = bf16[16,64,512]{2,1,0:T(8,128)(2,1)S(1)} collective-permute-done((bf16[16,64,512]{2,1,0:T(8,128)(2,1)}, bf16[16,64,512]{2,1,0:T(8,128)(2,1)S(1)}, u32[]{:S(2)}, u32[]{:S(2)}) %collective-permute-start.12) | collective-permute-done | bytes 1048608 | tf_op jit(solution)/shard_map/ppermute | solution.py:285
  122.8 3.7 %collective-permute-start.7 = (bf16[512,512]{1,0:T(8,128)(2,1)S(1)}, bf16[512,512]{1,0:T(8,128)(2,1)S(1)}, u32[]{:S(2)}, u32[]{:S(2)}) collective-permute-start(bf16[512,512]{1,0:T(8,128)(2,1)S(1)} %shard_map.89.refs_1_), channel_id=1, source_target_pairs={{0,1},{1,2},{2,3},{3,0},{4,5},{5,6},{6,7},{7,4},{8,9},{9,10},{10,1... | collective-permute-start | bytes 1572872 | tf_op jit(solution)/shard_map/ppermute | solution.py:285
  126.5 23.6 %collective-permute-done.11.refs_7_ = bf16[16,64,512]{2,1,0:T(8,128)(2,1)} collective-permute-done((bf16[16,64,512]{2,1,0:T(8,128)(2,1)}, bf16[16,64,512]{2,1,0:T(8,128)(2,1)}, u32[]{:S(2)}, u32[]{:S(2)}) %collective-permute-start.11) | collective-permute-done | bytes 1048608 | tf_op jit(solution)/shard_map/ppermute | solution.py:285
  150.1 3.4 %shard_map.91 = bf16[256,1024]{1,0:T(8,128)(2,1)S(1)} custom-call(s32[5]{0:T(128)S(1)} %copy-done.5, bf16[512,512]{1,0:T(8,128)(2,1)S(1)} %shard_map.89.refs_1_, bf16[512,512]{1,0:T(8,128)(2,1)S(1)} %collective-permute-done.7.refs_2_, bf16[512,512]{1,0:T(8,128)(2,1)S(1)} %collective-permute-done.8.refs_3_, ...), custom_call_target="tpu_custom_call" | custom-call | flops 1000000 | bytes 1000000 | tf_op jit(solution)/shard_map/pallas_call | solution.py:59
  153.6 2.4 %collective-permute-start.13 = (bf16[256,1024]{1,0:T(8,128)(2,1)S(1)}, bf16[256,1024]{1,0:T(8,128)(2,1)S(1)}, u32[]{:S(2)}, u32[]{:S(2)}) collective-permute-start(bf16[256,1024]{1,0:T(8,128)(2,1)S(1)} %shard_map.91), channel_id=1, source_target_pairs={{0,4},{4,0},{1,5},{5,1},{2,6},{6,2},{3,7},{7,3},{8,12},{12,8},{9,1... | collective-permute-start | bytes 1572872 | tf_op jit(solution)/shard_map/ppermute | solution.py:21
  156.0 3.4 %shard_map.90 = f32[256,1024]{1,0:T(8,128)S(1)} custom-call(s32[5]{0:T(128)S(1)} %copy-done.5, bf16[512,512]{1,0:T(8,128)(2,1)S(1)} %shard_map.89.refs_1_, bf16[512,512]{1,0:T(8,128)(2,1)S(1)} %collective-permute-done.7.refs_2_, bf16[512,512]{1,0:T(8,128)(2,1)S(1)} %collective-permute-done.8.refs_3_, bf16[512,512]{1,0:T(8,128)(2,1)S(1)} %collective-permute-done.9.refs_4_, ...), custom_call_target="tpu_custom_call" | custom-call | flops 1000000 | bytes 1000000 | tf_op jit(solution)/shard_map/pallas_call | solution.py:59
  (44 shorter events, 18.7 us)
Async XLA Ops:
  6.5 92.3 %all-gather.2.cloned.1.call-start = ((), (), s32[]{:S(2)}) async-start(), calls=%async_computation.4 | async-start | bytes 1179648 | tf_op jit(solution)/shard_map/all_gather | solution.py:323
  7.3 13.9 %collective-permute-start = (bf16[32,512]{1,0:T(8,128)(2,1)S(1)}, bf16[32,512]{1,0:T(8,128)(2,1)S(1)}, u32[]{:S(2)}, u32[]{:S(2)}) collective-permute-start(bf16[32,512]{1,0:T(8,128)(2,1)S(1)} %get-tuple-element.49), channel_id=1, source_target_pairs={{0,0},{4,4},{1,128},{5,132},{2,256},{6,260},{3,384},{7,388},{128,1... | collective-permute-start | bytes 98312 | tf_op jit(solution)/shard_map/ppermute | solution.py:300
  8.0 13.2 %collective-permute-start.1 = (bf16[32,512]{1,0:T(8,128)(2,1)S(1)}, bf16[32,512]{1,0:T(8,128)(2,1)S(1)}, u32[]{:S(2)}, u32[]{:S(2)}) collective-permute-start(bf16[32,512]{1,0:T(8,128)(2,1)S(1)} %get-tuple-element.50), channel_id=1, source_target_pairs={{0,4},{4,0},{1,132},{5,128},{2,260},{6,256},{3,388},{7,384},{128,5... | collective-permute-start | bytes 98312 | tf_op jit(solution)/shard_map/ppermute | solution.py:300
  17.4 8.7 %copy-start.5 = (s32[5]{0:T(128)S(1)}, s32[5]{0:T(128)}, u32[]{:S(2)}) copy-start(s32[5]{0:T(128)} %stack.32.refs_0_) | copy-start | bytes 64
  21.2 4.8 %collective-permute-start.2 = (bf16[1072,512]{1,0:T(8,128)(2,1)}, bf16[1072,512]{1,0:T(8,128)(2,1)S(1)}, u32[]{:S(2)}, u32[]{:S(2)}) collective-permute-start(bf16[1072,512]{1,0:T(8,128)(2,1)} %get-tuple-element.28), channel_id=1, source_target_pairs={{0,4},{4,0},{1,5},{5,1},{2,6},{6,2},{3,7},{7,3},{8,12},{12,8},{9,1... | collective-permute-start | bytes 3293192 | tf_op jit(solution)/shard_map/ppermute | solution.py:21
  23.2 5.9 %collective-permute-start.3 = (bf16[64,512]{1,0:T(8,128)(2,1)S(1)}, bf16[64,512]{1,0:T(8,128)(2,1)S(1)}, u32[]{:S(2)}, u32[]{:S(2)}) collective-permute-start(bf16[64,512]{1,0:T(8,128)(2,1)S(1)} %maximum_select_fusion), channel_id=1, source_target_pairs={{0,8},{8,0},{1,9},{9,1},{2,10},{10,2},{3,11},{11,3},{4,12},{12,4},... | collective-permute-start | bytes 196616 | tf_op jit(solution)/shard_map/ppermute | solution.py:316
  26.1 1.2 copy-start
  39.0 30.1 %all-to-all-start.1 = ((bf16[4,144,128]{2,1,0:T(8,128)(2,1)}), bf16[4,144,128]{2,1,0:T(8,128)(2,1)S(1)}, u32[]{:S(2)}, u32[]{:S(2)}) async-start(bf16[4,144,128]{2,1,0:T(8,128)(2,1)} %get-tuple-element.41), calls=%async_computation.1 | async-start | bytes 294912 | tf_op jit(solution)/shard_map/all_to_all | solution.py:327
  48.8 12.6 %collective-permute-start.4 = (bf16[144,256]{1,0:T(8,128)(2,1)S(1)}, bf16[144,256]{1,0:T(8,128)(2,1)S(1)}, u32[]{:S(2)}, u32[]{:S(2)}) collective-permute-start(bf16[144,256]{1,0:T(8,128)(2,1)S(1)} %get-tuple-element.36), channel_id=1, source_target_pairs={{0,8},{8,0},{16,24},{24,16},{1,9},{9,1},{17,25},{25,17},{2,10},{10... | collective-permute-start | bytes 221192 | tf_op jit(solution)/shard_map/ppermute | solution.py:329
  51.1 10.4 %collective-permute-start.5 = (bf16[144,256]{1,0:T(8,128)(2,1)S(1)}, bf16[144,256]{1,0:T(8,128)(2,1)S(1)}, u32[]{:S(2)}, u32[]{:S(2)}) collective-permute-start(bf16[144,256]{1,0:T(8,128)(2,1)S(1)} %get-tuple-element.37), channel_id=1, source_target_pairs={{0,16},{8,24},{16,0},{24,8},{1,17},{9,25},{17,1},{25,9},{2,18},{10... | collective-permute-start | bytes 221192 | tf_op jit(solution)/shard_map/ppermute | solution.py:329
  54.7 14.4 %collective-permute-start.6 = (bf16[144,256]{1,0:T(8,128)(2,1)S(1)}, bf16[144,256]{1,0:T(8,128)(2,1)S(1)}, u32[]{:S(2)}, u32[]{:S(2)}) collective-permute-start(bf16[144,256]{1,0:T(8,128)(2,1)S(1)} %get-tuple-element.38), channel_id=1, source_target_pairs={{0,24},{8,16},{16,8},{24,0},{1,25},{9,17},{17,9},{25,1},{2,26},{10... | collective-permute-start | bytes 221192 | tf_op jit(solution)/shard_map/ppermute | solution.py:329
  69.7 22.1 %copy-start.1 = (bf16[1072,512]{1,0:T(8,128)(2,1)S(1)}, bf16[1072,512]{1,0:T(8,128)(2,1)}, u32[]{:S(2)}) copy-start(bf16[1072,512]{1,0:T(8,128)(2,1)} %get-tuple-element.26.refs_1_) | copy-start | bytes 3293188
  87.6 20.8 %all-to-all-start.3 = ((bf16[4,128,512]{2,1,0:T(8,128)(2,1)}), bf16[4,128,512]{2,1,0:T(8,128)(2,1)}, u32[]{:S(2)}, u32[]{:S(2)}) async-start(bf16[4,128,512]{2,1,0:T(8,128)(2,1)} %shard_map.88), calls=%async_computation.3 | async-start | bytes 1048576 | tf_op jit(solution)/shard_map/all_to_all | solution.py:342
  96.1 12.3 %copy-start.6 = (bf16[1024]{0:T(1024)(128)(2,1)S(1)}, bf16[1024]{0:T(1024)(128)(2,1)}, u32[]{:S(2)}) copy-start(bf16[1024]{0:T(1024)(128)(2,1)} %param.14) | copy-start | bytes 6148
  97.9 1.0 copy-start.3
  98.8 24.0 %collective-permute-start.12 = (bf16[16,64,512]{2,1,0:T(8,128)(2,1)}, bf16[16,64,512]{2,1,0:T(8,128)(2,1)S(1)}, u32[]{:S(2)}, u32[]{:S(2)}) collective-permute-start(bf16[16,64,512]{2,1,0:T(8,128)(2,1)} %all-gather.2.cloned.1.call-done.refs_5_), channel_id=1, source_target_pairs={{0,256},{128,384},{256,0},{384,128},{1,257},{129,385},{257,1},{385... | collective-permute-start | bytes 3145736 | tf_op jit(solution)/shard_map/ppermute | solution.py:285
  101.9 48.2 %collective-permute-start.11 = (bf16[16,64,512]{2,1,0:T(8,128)(2,1)}, bf16[16,64,512]{2,1,0:T(8,128)(2,1)}, u32[]{:S(2)}, u32[]{:S(2)}) collective-permute-start(bf16[16,64,512]{2,1,0:T(8,128)(2,1)} %all-gather.2.cloned.1.call-done.refs_5_), channel_id=1, source_target_pairs={{0,128},{128,256},{256,384},{384,0},{1,129},{129,257},{257,385},{3... | collective-permute-start | bytes 3145736 | tf_op jit(solution)/shard_map/ppermute | solution.py:285
  104.0 46.1 %collective-permute-start.10 = (bf16[16,64,512]{2,1,0:T(8,128)(2,1)}, bf16[16,64,512]{2,1,0:T(8,128)(2,1)}, u32[]{:S(2)}, u32[]{:S(2)}) collective-permute-start(bf16[16,64,512]{2,1,0:T(8,128)(2,1)} %all-gather.2.cloned.1.call-done.refs_5_), channel_id=1, source_target_pairs={{0,384},{128,0},{256,128},{384,256},{1,385},{129,1},{257,129},{385... | collective-permute-start | bytes 3145736 | tf_op jit(solution)/shard_map/ppermute | solution.py:285
  108.4 1.2 copy-start.4
  109.7 40.5 %copy-start.2 = (bf16[16,64,512]{2,1,0:T(8,128)(2,1)S(1)}, bf16[16,64,512]{2,1,0:T(8,128)(2,1)}, u32[]{:S(2)}) copy-start(bf16[16,64,512]{2,1,0:T(8,128)(2,1)} %all-gather.2.cloned.1.call-done.refs_5_) | copy-start | bytes 3145732
  112.8 37.3 %collective-permute-start.9 = (bf16[512,512]{1,0:T(8,128)(2,1)S(1)}, bf16[512,512]{1,0:T(8,128)(2,1)S(1)}, u32[]{:S(2)}, u32[]{:S(2)}) collective-permute-start(bf16[512,512]{1,0:T(8,128)(2,1)S(1)} %shard_map.89.refs_1_), channel_id=1, source_target_pairs={{0,3},{1,0},{2,1},{3,2},{4,7},{5,4},{6,5},{7,6},{8,11},{9,8},{10,9... | collective-permute-start | bytes 1572872 | tf_op jit(solution)/shard_map/ppermute | solution.py:285
  115.6 34.5 %collective-permute-start.8 = (bf16[512,512]{1,0:T(8,128)(2,1)S(1)}, bf16[512,512]{1,0:T(8,128)(2,1)S(1)}, u32[]{:S(2)}, u32[]{:S(2)}) collective-permute-start(bf16[512,512]{1,0:T(8,128)(2,1)S(1)} %shard_map.89.refs_1_), channel_id=1, source_target_pairs={{0,2},{1,3},{2,0},{3,1},{4,6},{5,7},{6,4},{7,5},{8,10},{9,11},{10,... | collective-permute-start | bytes 1572872 | tf_op jit(solution)/shard_map/ppermute | solution.py:285
  122.8 27.3 %collective-permute-start.7 = (bf16[512,512]{1,0:T(8,128)(2,1)S(1)}, bf16[512,512]{1,0:T(8,128)(2,1)S(1)}, u32[]{:S(2)}, u32[]{:S(2)}) collective-permute-start(bf16[512,512]{1,0:T(8,128)(2,1)S(1)} %shard_map.89.refs_1_), channel_id=1, source_target_pairs={{0,1},{1,2},{2,3},{3,0},{4,5},{5,6},{6,7},{7,4},{8,9},{9,10},{10,1... | collective-permute-start | bytes 1572872 | tf_op jit(solution)/shard_map/ppermute | solution.py:285
  153.6 5.9 %collective-permute-start.13 = (bf16[256,1024]{1,0:T(8,128)(2,1)S(1)}, bf16[256,1024]{1,0:T(8,128)(2,1)S(1)}, u32[]{:S(2)}, u32[]{:S(2)}) collective-permute-start(bf16[256,1024]{1,0:T(8,128)(2,1)S(1)} %shard_map.91), channel_id=1, source_target_pairs={{0,4},{4,0},{1,5},{5,1},{2,6},{6,2},{3,7},{7,3},{8,12},{12,8},{9,1... | collective-permute-start | bytes 1572872 | tf_op jit(solution)/shard_map/ppermute | solution.py:21
Sparse Core Ops, SparseCore 0:
  29.9 61.2 all-gather.1

commit v22 on v21

--- a/solution.py
+++ b/solution.py
@@ -338,7 +338,9 @@
         unread=near[1:],
     )
     rows = lax.all_to_all(pay_y, "y", 0, 0, tiled=True)
-    (states,) = call(last_body, [((4, 128, 512), BF)], (at, rows, before, far))
+    (states,) = call(
+        last_body, [((4, 128, 512), BF)], (at, rows, before, far), unread=(mixture,)
+    )
     states = lax.all_to_all(states, NEAR, 0, 0, tiled=True)
     mixture, coef = call(
         mix_body,

time: 169 us -> 171 us (1.012)
  blocking collectives: 24.4 us -> 8.46 us
  starting transfers between devices: 58.6 us -> 73.7 us
  local copies, waits for them, and re-layouts: 4.82 us -> 12.6 us
  waiting for transfers between devices: 39.1 us -> 34.4 us
    all_to_all x1 -> x0, blocking collectives: 16.5 us -> none  [shards(): rows = lax.all_to_all(pay_y, 'y', 0, 0, tiled=True)]
    all_to_all x0 -> x1, starting transfers between devices: none -> 11.4 us  [shards(): rows = lax.all_to_all(pay_y, 'y', 0, 0, tiled=True)]
    unnamed x14 -> x40, local copies, waits for them, and re-layouts: 3.45 us -> 11.2 us
    ppermute x6, waiting for transfers between devices: 27.2 us -> 22.6 us  [shift(): return lax.ppermute(value, axis, [(i, (i + by) % 4) for i in range(4)])]
    ppermute x6, starting transfers between devices: 19.6 us -> 23.4 us  [shift(): return lax.ppermute(value, axis, [(i, (i + by) % 4) for i in range(4)])]
  transfers between devices with their start and end apart: 17 -> 18, of which waited for: 5 -> 5; matrix products, arithmetic and copies ran while one was open for 0% -> 0% of each run, Pallas kernels for 13% -> 13%
where the time goes in v22:
time: 171 us; the launch traced here: 169 us
  starting transfers between devices  73.7 us (43%)
  waiting for transfers between devices  34.4 us (20%)
  Pallas kernels  24.7 us (14%)
  between operations  13.7 us (8%)
  local copies, waits for them, and re-layouts  12.6 us (7%)
  blocking collectives  8.46 us (5%)
    pallas_call x10, Pallas kernels, call(): pl.pallas_call(run, out_shape=[jax.ShapeDtypeStruct(*o) for o in outs], i...  24.7 us
    ppermute x6, starting transfers between devices, shift(): return lax.ppermute(value, axis, [(i, (i + by) % 4) for i in range(4)])  23.4 us
    ppermute x6, waiting for transfers between devices, shift(): return lax.ppermute(value, axis, [(i, (i + by) % 4) for i in range(4)])  22.6 us
    all_to_all x1, starting transfers between devices, shards(): rows = lax.all_to_all(pay_y, 'y', 0, 0, tiled=True)  11.4 us
    unnamed x40, local copies, waits for them, and re-layouts  11.2 us
    ppermute x3, waiting for transfers between devices, shards(): lax.ppermute(near[k], NEAR, [(i, i ^ k) for i in range(4)])  10.8 us
    ppermute x2, starting transfers between devices, shards(): turned.append(lax.ppermute(half, ('y', 'c', 'x'), perm))  9.44 us
    all_to_all x1, starting transfers between devices, shards(): far = lax.all_to_all(pay_a, 'a', 0, 0, tiled=True)  9.3 us
  transfers between devices with their start and end apart: 18, of which 5 were waited for; matrix products, arithmetic and copies ran while one was open for 0% of the time, Pallas kernels for 13%

profile of v22, /device:TPU:1, one launch (start us, length us, event | category | flops | bytes accessed | tf_op | source)
XLA Modules:
  0.0 169.2 jit_solution(7042820251291038476)
XLA Ops:
  8.0 8.8 %collective-permute-start.1 = (bf16[32,512]{1,0:T(8,128)(2,1)S(1)}, bf16[32,512]{1,0:T(8,128)(2,1)S(1)}, u32[]{:S(2)}, u32[]{:S(2)}) collective-permute-start(bf16[32,512]{1,0:T(8,128)(2,1)S(1)} %get-tuple-element.50), channel_id=1, source_target_pairs={{0,4},{4,0},{1,132},{5,128},{2,260},{6,256},{3,388},{7,384},{128,5... | collective-permute-start | bytes 98312 | tf_op jit(solution)/shard_map/ppermute | solution.py:300
  17.4 3.8 %shard_map.82 = (bf16[1072,512]{1,0:T(8,128)(2,1)}, bf16[1072,512]{1,0:T(8,128)(2,1)}) custom-call(s32[5]{0:T(128)} %stack.32.refs_0_, bf16[256,1024]{1,0:T(8,128)(2,1)} %refs_1_.1, bf16[256,1024]{1,0:T(8,128)(2,1)} %refs_2_.1, bf16[256,1024]{1,0:T(8,128)(2,1)} %refs_3_.1, bf16[256,1024]{1,0:T(8,128)(2,1)} %refs_4_.1, f32[8,256]{1,0:T(8,128)} %refs_5_.1, ...), custom_call_target="tpu_custom_call" | custom-call | flops 1000000 | bytes 1000000 | tf_op jit(solution)/shard_map/pallas_call | solution.py:59
  23.2 1.9 %collective-permute-start.3 = (bf16[64,512]{1,0:T(8,128)(2,1)S(1)}, bf16[64,512]{1,0:T(8,128)(2,1)S(1)}, u32[]{:S(2)}, u32[]{:S(2)}) collective-permute-start(bf16[64,512]{1,0:T(8,128)(2,1)S(1)} %maximum_select_fusion), channel_id=1, source_target_pairs={{0,8},{8,0},{1,9},{9,1},{2,10},{10,2},{3,11},{11,3},{4,12},{12,4},... | collective-permute-start | bytes 196616 | tf_op jit(solution)/shard_map/ppermute | solution.py:316
  30.5 8.5 %all_to_all.20.refs_1_ = bf16[4,144,128]{2,1,0:T(8,128)(2,1)S(1)} all-to-all(bf16[4,144,128]{2,1,0:T(8,128)(2,1)S(1)} %get-tuple-element.34), channel_id=1, replica_groups=mesh['y'=4,'a'=4,'p'=2,'q'=2,'c'=2,'x'=4] {'p','q'}, dimensions={0} | all-to-all | bytes 294912 | tf_op jit(solution)/shard_map/all_to_all | solution.py:325
  40.8 9.3 %all-to-all-start.1 = ((bf16[4,144,128]{2,1,0:T(8,128)(2,1)}), bf16[4,144,128]{2,1,0:T(8,128)(2,1)S(1)}, u32[]{:S(2)}, u32[]{:S(2)}) async-start(bf16[4,144,128]{2,1,0:T(8,128)(2,1)} %get-tuple-element.41), calls=%async_computation.1 | async-start | bytes 294912 | tf_op jit(solution)/shard_map/all_to_all | solution.py:327
  50.1 2.2 %collective-permute-start.4 = (bf16[144,256]{1,0:T(8,128)(2,1)S(1)}, bf16[144,256]{1,0:T(8,128)(2,1)S(1)}, u32[]{:S(2)}, u32[]{:S(2)}) collective-permute-start(bf16[144,256]{1,0:T(8,128)(2,1)S(1)} %get-tuple-element.36), channel_id=1, source_target_pairs={{0,8},{8,0},{16,24},{24,16},{1,9},{9,1},{17,25},{25,17},{2,10},{10... | collective-permute-start | bytes 221192 | tf_op jit(solution)/shard_map/ppermute | solution.py:329
  52.4 3.6 %collective-permute-start.5 = (bf16[144,256]{1,0:T(8,128)(2,1)S(1)}, bf16[144,256]{1,0:T(8,128)(2,1)S(1)}, u32[]{:S(2)}, u32[]{:S(2)}) collective-permute-start(bf16[144,256]{1,0:T(8,128)(2,1)S(1)} %get-tuple-element.37), channel_id=1, source_target_pairs={{0,16},{8,24},{16,0},{24,8},{1,17},{9,25},{17,1},{25,9},{2,18},{10... | collective-permute-start | bytes 221192 | tf_op jit(solution)/shard_map/ppermute | solution.py:329
  56.0 3.4 %collective-permute-start.6 = (bf16[144,256]{1,0:T(8,128)(2,1)S(1)}, bf16[144,256]{1,0:T(8,128)(2,1)S(1)}, u32[]{:S(2)}, u32[]{:S(2)}) collective-permute-start(bf16[144,256]{1,0:T(8,128)(2,1)S(1)} %get-tuple-element.38), channel_id=1, source_target_pairs={{0,24},{8,16},{16,8},{24,0},{1,25},{9,17},{17,9},{25,1},{2,26},{10... | collective-permute-start | bytes 221192 | tf_op jit(solution)/shard_map/ppermute | solution.py:329
  59.4 3.1 %collective-permute-done.4.refs_6_.refs_2_ = bf16[144,256]{1,0:T(8,128)(2,1)S(1)} collective-permute-done((bf16[144,256]{1,0:T(8,128)(2,1)S(1)}, bf16[144,256]{1,0:T(8,128)(2,1)S(1)}, u32[]{:S(2)}, u32[]{:S(2)}) %collective-permute-start.4) | collective-permute-done | bytes 73760 | tf_op jit(solution)/shard_map/ppermute | solution.py:329
  62.6 7.6 %collective-permute-done.6.refs_8_.refs_4_ = bf16[144,256]{1,0:T(8,128)(2,1)S(1)} collective-permute-done((bf16[144,256]{1,0:T(8,128)(2,1)S(1)}, bf16[144,256]{1,0:T(8,128)(2,1)S(1)}, u32[]{:S(2)}, u32[]{:S(2)}) %collective-permute-start.6) | collective-permute-done | bytes 73760 | tf_op jit(solution)/shard_map/ppermute | solution.py:329
  72.1 11.4 %all-to-all-start.2 = ((bf16[4,144,128]{2,1,0:T(8,128)(2,1)}), bf16[4,144,128]{2,1,0:T(8,128)(2,1)S(1)}, u32[]{:S(2)}, u32[]{:S(2)}) async-start(bf16[4,144,128]{2,1,0:T(8,128)(2,1)} %get-tuple-element.42), calls=%async_computation.2 | async-start | bytes 294912 | tf_op jit(solution)/shard_map/all_to_all | solution.py:340
  84.4 4.3 %shard_map.84 = (f32[512,512]{1,0:T(8,128)S(1)}, f32[512,24]{1,0:T(8,128)S(1)}) custom-call(s32[5]{0:T(128)S(1)} %copy-done.18, bf16[1072,512]{1,0:T(8,128)(2,1)S(1)} %copy-done.1, bf16[1072,512]{1,0:T(8,128)(2,1)S(1)} %collective-permute-done.2.refs_2_, bf16[4,128,128]{2,1,0:T(8,128)(2,1)S(1)} %copy-done.13), custom_call_target="tpu_custom_call" | custom-call | flops 1000000 | bytes 1000000 | tf_op jit(solution)/shard_map/pallas_call | solution.py:59
  91.7 4.4 %all-to-all-start.3 = ((bf16[4,128,512]{2,1,0:T(8,128)(2,1)}), bf16[4,128,512]{2,1,0:T(8,128)(2,1)}, u32[]{:S(2)}, u32[]{:S(2)}) async-start(bf16[4,128,512]{2,1,0:T(8,128)(2,1)} %copy-done.3), calls=%async_computation.3 | async-start | bytes 1048576 | tf_op jit(solution)/shard_map/all_to_all | solution.py:344
  100.5 4.9 %collective-permute-start.12 = (bf16[16,64,512]{2,1,0:T(8,128)(2,1)}, bf16[16,64,512]{2,1,0:T(8,128)(2,1)S(1)}, u32[]{:S(2)}, u32[]{:S(2)}) collective-permute-start(bf16[16,64,512]{2,1,0:T(8,128)(2,1)} %all-gather.2.cloned.1.call-done.refs_5_), channel_id=1, source_target_pairs={{0,256},{128,384},{256,0},{384,128},{1,257},{129,385},{257,1},{385... | collective-permute-start | bytes 3145736 | tf_op jit(solution)/shard_map/ppermute | solution.py:285
  105.3 2.2 %collective-permute-start.11 = (bf16[16,64,512]{2,1,0:T(8,128)(2,1)}, bf16[16,64,512]{2,1,0:T(8,128)(2,1)}, u32[]{:S(2)}, u32[]{:S(2)}) collective-permute-start(bf16[16,64,512]{2,1,0:T(8,128)(2,1)} %all-gather.2.cloned.1.call-done.refs_5_), channel_id=1, source_target_pairs={{0,128},{128,256},{256,384},{384,0},{1,129},{129,257},{257,385},{3... | collective-permute-start | bytes 3145736 | tf_op jit(solution)/shard_map/ppermute | solution.py:285
  107.5 4.3 %collective-permute-start.10 = (bf16[16,64,512]{2,1,0:T(8,128)(2,1)}, bf16[16,64,512]{2,1,0:T(8,128)(2,1)}, u32[]{:S(2)}, u32[]{:S(2)}) collective-permute-start(bf16[16,64,512]{2,1,0:T(8,128)(2,1)} %all-gather.2.cloned.1.call-done.refs_5_), channel_id=1, source_target_pairs={{0,384},{128,0},{256,128},{384,256},{1,385},{129,1},{257,129},{385... | collective-permute-start | bytes 3145736 | tf_op jit(solution)/shard_map/ppermute | solution.py:285
  114.1 3.1 %shard_map.89.refs_1_ = bf16[512,512]{1,0:T(8,128)(2,1)S(1)} custom-call(s32[5]{0:T(128)S(1)} %copy-done.18, bf16[1072,512]{1,0:T(8,128)(2,1)S(1)} %copy-done.1, bf16[1072,512]{1,0:T(8,128)(2,1)S(1)} %collective-permute-done.2.refs_2_, bf16[1,1024]{1,0:T(2,128)(2,1)S(1)} %broadcast_in_dim.3.refs_3_, f32[512,512]{1,0:T(8,128)S(1)} %copy-done.5, ...), custom_call_target="tpu_custom_call" | custom-call | flops 1000000 | bytes 1000000 | tf_op jit(solution)/shard_map/pallas_call | solution.py:59
  117.1 4.1 %collective-permute-start.9 = (bf16[512,512]{1,0:T(8,128)(2,1)S(1)}, bf16[512,512]{1,0:T(8,128)(2,1)S(1)}, u32[]{:S(2)}, u32[]{:S(2)}) collective-permute-start(bf16[512,512]{1,0:T(8,128)(2,1)S(1)} %shard_map.89.refs_1_), channel_id=1, source_target_pairs={{0,3},{1,0},{2,1},{3,2},{4,7},{5,4},{6,5},{7,6},{8,11},{9,8},{10,9... | collective-permute-start | bytes 1572872 | tf_op jit(solution)/shard_map/ppermute | solution.py:285
  121.3 3.3 %collective-permute-start.8 = (bf16[512,512]{1,0:T(8,128)(2,1)S(1)}, bf16[512,512]{1,0:T(8,128)(2,1)S(1)}, u32[]{:S(2)}, u32[]{:S(2)}) collective-permute-start(bf16[512,512]{1,0:T(8,128)(2,1)S(1)} %shard_map.89.refs_1_), channel_id=1, source_target_pairs={{0,2},{1,3},{2,0},{3,1},{4,6},{5,7},{6,4},{7,5},{8,10},{9,11},{10,... | collective-permute-start | bytes 1572872 | tf_op jit(solution)/shard_map/ppermute | solution.py:285
  125.1 4.6 %collective-permute-start.7 = (bf16[512,512]{1,0:T(8,128)(2,1)S(1)}, bf16[512,512]{1,0:T(8,128)(2,1)S(1)}, u32[]{:S(2)}, u32[]{:S(2)}) collective-permute-start(bf16[512,512]{1,0:T(8,128)(2,1)S(1)} %shard_map.89.refs_1_), channel_id=1, source_target_pairs={{0,1},{1,2},{2,3},{3,0},{4,5},{5,6},{6,7},{7,4},{8,9},{9,10},{10,1... | collective-permute-start | bytes 1572872 | tf_op jit(solution)/shard_map/ppermute | solution.py:285
  129.7 22.0 %collective-permute-done.11.refs_7_ = bf16[16,64,512]{2,1,0:T(8,128)(2,1)} collective-permute-done((bf16[16,64,512]{2,1,0:T(8,128)(2,1)}, bf16[16,64,512]{2,1,0:T(8,128)(2,1)}, u32[]{:S(2)}, u32[]{:S(2)}) %collective-permute-start.11) | collective-permute-done | bytes 1048608 | tf_op jit(solution)/shard_map/ppermute | solution.py:285
  151.8 3.4 %shard_map.91 = bf16[256,1024]{1,0:T(8,128)(2,1)S(1)} custom-call(s32[5]{0:T(128)S(1)} %copy-done.18, bf16[512,512]{1,0:T(8,128)(2,1)S(1)} %shard_map.89.refs_1_, bf16[512,512]{1,0:T(8,128)(2,1)S(1)} %collective-permute-done.7.refs_2_, bf16[512,512]{1,0:T(8,128)(2,1)S(1)} %collective-permute-done.8.refs_3_, ...), custom_call_target="tpu_custom_call" | custom-call | flops 1000000 | bytes 1000000 | tf_op jit(solution)/shard_map/pallas_call | solution.py:59
  155.2 2.7 %collective-permute-start.13 = (bf16[256,1024]{1,0:T(8,128)(2,1)S(1)}, bf16[256,1024]{1,0:T(8,128)(2,1)S(1)}, u32[]{:S(2)}, u32[]{:S(2)}) collective-permute-start(bf16[256,1024]{1,0:T(8,128)(2,1)S(1)} %shard_map.91), channel_id=1, source_target_pairs={{0,4},{4,0},{1,5},{5,1},{2,6},{6,2},{3,7},{7,3},{8,12},{12,8},{9,1... | collective-permute-start | bytes 1572872 | tf_op jit(solution)/shard_map/ppermute | solution.py:21
  157.9 3.4 %shard_map.90 = f32[256,1024]{1,0:T(8,128)S(1)} custom-call(s32[5]{0:T(128)S(1)} %copy-done.18, bf16[512,512]{1,0:T(8,128)(2,1)S(1)} %shard_map.89.refs_1_, bf16[512,512]{1,0:T(8,128)(2,1)S(1)} %collective-permute-done.7.refs_2_, bf16[512,512]{1,0:T(8,128)(2,1)S(1)} %collective-permute-done.8.refs_3_, bf16[512,512]{1,0:T(8,128)(2,1)S(1)} %collective-permute-done.9.refs_4_, ...), custom_call_target="tpu_custom_call" | custom-call | flops 1000000 | bytes 1000000 | tf_op jit(solution)/shard_map/pallas_call | solution.py:59
  (71 shorter events, 24.9 us)
Async XLA Ops:
  6.5 93.9 %all-gather.2.cloned.1.call-start = ((), (), s32[]{:S(2)}) async-start(), calls=%async_computation.4 | async-start | bytes 1179648 | tf_op jit(solution)/shard_map/all_gather | solution.py:323
  7.3 13.9 %collective-permute-start = (bf16[32,512]{1,0:T(8,128)(2,1)S(1)}, bf16[32,512]{1,0:T(8,128)(2,1)S(1)}, u32[]{:S(2)}, u32[]{:S(2)}) collective-permute-start(bf16[32,512]{1,0:T(8,128)(2,1)S(1)} %get-tuple-element.49), channel_id=1, source_target_pairs={{0,0},{4,4},{1,128},{5,132},{2,256},{6,260},{3,384},{7,388},{128,1... | collective-permute-start | bytes 98312 | tf_op jit(solution)/shard_map/ppermute | solution.py:300
  8.0 13.3 %collective-permute-start.1 = (bf16[32,512]{1,0:T(8,128)(2,1)S(1)}, bf16[32,512]{1,0:T(8,128)(2,1)S(1)}, u32[]{:S(2)}, u32[]{:S(2)}) collective-permute-start(bf16[32,512]{1,0:T(8,128)(2,1)S(1)} %get-tuple-element.50), channel_id=1, source_target_pairs={{0,4},{4,0},{1,132},{5,128},{2,260},{6,256},{3,388},{7,384},{128,5... | collective-permute-start | bytes 98312 | tf_op jit(solution)/shard_map/ppermute | solution.py:300
  17.4 8.7 %copy-start.18 = (s32[5]{0:T(128)S(1)}, s32[5]{0:T(128)}, u32[]{:S(2)}) copy-start(s32[5]{0:T(128)} %stack.32.refs_0_) | copy-start | bytes 64
  21.3 4.8 %collective-permute-start.2 = (bf16[1072,512]{1,0:T(8,128)(2,1)}, bf16[1072,512]{1,0:T(8,128)(2,1)S(1)}, u32[]{:S(2)}, u32[]{:S(2)}) collective-permute-start(bf16[1072,512]{1,0:T(8,128)(2,1)} %get-tuple-element.28), channel_id=1, source_target_pairs={{0,4},{4,0},{1,5},{5,1},{2,6},{6,2},{3,7},{7,3},{8,12},{12,8},{9,1... | collective-permute-start | bytes 3293192 | tf_op jit(solution)/shard_map/ppermute | solution.py:21
  23.2 6.6 %collective-permute-start.3 = (bf16[64,512]{1,0:T(8,128)(2,1)S(1)}, bf16[64,512]{1,0:T(8,128)(2,1)S(1)}, u32[]{:S(2)}, u32[]{:S(2)}) collective-permute-start(bf16[64,512]{1,0:T(8,128)(2,1)S(1)} %maximum_select_fusion), channel_id=1, source_target_pairs={{0,8},{8,0},{1,9},{9,1},{2,10},{10,2},{3,11},{11,3},{4,12},{12,4},... | collective-permute-start | bytes 196616 | tf_op jit(solution)/shard_map/ppermute | solution.py:316
  29.8 53.7 %copy-start.1 = (bf16[1072,512]{1,0:T(8,128)(2,1)S(1)}, bf16[1072,512]{1,0:T(8,128)(2,1)}, u32[]{:S(2)}) copy-start(bf16[1072,512]{1,0:T(8,128)(2,1)} %get-tuple-element.26.refs_1_) | copy-start | bytes 3293188
  40.8 29.4 %all-to-all-start.1 = ((bf16[4,144,128]{2,1,0:T(8,128)(2,1)}), bf16[4,144,128]{2,1,0:T(8,128)(2,1)S(1)}, u32[]{:S(2)}, u32[]{:S(2)}) async-start(bf16[4,144,128]{2,1,0:T(8,128)(2,1)} %get-tuple-element.41), calls=%async_computation.1 | async-start | bytes 294912 | tf_op jit(solution)/shard_map/all_to_all | solution.py:327
  50.1 12.4 %collective-permute-start.4 = (bf16[144,256]{1,0:T(8,128)(2,1)S(1)}, bf16[144,256]{1,0:T(8,128)(2,1)S(1)}, u32[]{:S(2)}, u32[]{:S(2)}) collective-permute-start(bf16[144,256]{1,0:T(8,128)(2,1)S(1)} %get-tuple-element.36), channel_id=1, source_target_pairs={{0,8},{8,0},{16,24},{24,16},{1,9},{9,1},{17,25},{25,17},{2,10},{10... | collective-permute-start | bytes 221192 | tf_op jit(solution)/shard_map/ppermute | solution.py:329
  52.4 10.2 %collective-permute-start.5 = (bf16[144,256]{1,0:T(8,128)(2,1)S(1)}, bf16[144,256]{1,0:T(8,128)(2,1)S(1)}, u32[]{:S(2)}, u32[]{:S(2)}) collective-permute-start(bf16[144,256]{1,0:T(8,128)(2,1)S(1)} %get-tuple-element.37), channel_id=1, source_target_pairs={{0,16},{8,24},{16,0},{24,8},{1,17},{9,25},{17,1},{25,9},{2,18},{10... | collective-permute-start | bytes 221192 | tf_op jit(solution)/shard_map/ppermute | solution.py:329
  56.0 14.2 %collective-permute-start.6 = (bf16[144,256]{1,0:T(8,128)(2,1)S(1)}, bf16[144,256]{1,0:T(8,128)(2,1)S(1)}, u32[]{:S(2)}, u32[]{:S(2)}) collective-permute-start(bf16[144,256]{1,0:T(8,128)(2,1)S(1)} %get-tuple-element.38), channel_id=1, source_target_pairs={{0,24},{8,16},{16,8},{24,0},{1,25},{9,17},{17,9},{25,1},{2,26},{10... | collective-permute-start | bytes 221192 | tf_op jit(solution)/shard_map/ppermute | solution.py:329
  70.2 13.3 %copy-start.6 = (bf16[144,256]{1,0:T(8,128)(2,1)}, bf16[144,256]{1,0:T(8,128)(2,1)S(1)}, u32[]{:S(2)}) copy-start(bf16[144,256]{1,0:T(8,128)(2,1)S(1)} %collective-permute-done.6.refs_8_.refs_4_) | copy-start | bytes 221188
  72.1 17.3 %all-to-all-start.2 = ((bf16[4,144,128]{2,1,0:T(8,128)(2,1)}), bf16[4,144,128]{2,1,0:T(8,128)(2,1)S(1)}, u32[]{:S(2)}, u32[]{:S(2)}) async-start(bf16[4,144,128]{2,1,0:T(8,128)(2,1)} %get-tuple-element.42), calls=%async_computation.2 | async-start | bytes 294912 | tf_op jit(solution)/shard_map/all_to_all | solution.py:340
  91.7 4.4 %copy-start.15 = (bf16[144,256]{1,0:T(8,128)(2,1)S(1)}, bf16[144,256]{1,0:T(8,128)(2,1)}, u32[]{:S(2)}) copy-start(bf16[144,256]{1,0:T(8,128)(2,1)} %copy-done.14) | copy-start | bytes 221188
  91.7 20.2 %all-to-all-start.3 = ((bf16[4,128,512]{2,1,0:T(8,128)(2,1)}), bf16[4,128,512]{2,1,0:T(8,128)(2,1)}, u32[]{:S(2)}, u32[]{:S(2)}) async-start(bf16[4,128,512]{2,1,0:T(8,128)(2,1)} %copy-done.3), calls=%async_computation.3 | async-start | bytes 1048576 | tf_op jit(solution)/shard_map/all_to_all | solution.py:344
  97.1 14.8 %copy-start.19 = (bf16[1024]{0:T(1024)(128)(2,1)S(1)}, bf16[1024]{0:T(1024)(128)(2,1)}, u32[]{:S(2)}) copy-start(bf16[1024]{0:T(1024)(128)(2,1)} %param.14) | copy-start | bytes 6148
  100.5 24.7 %collective-permute-start.12 = (bf16[16,64,512]{2,1,0:T(8,128)(2,1)}, bf16[16,64,512]{2,1,0:T(8,128)(2,1)S(1)}, u32[]{:S(2)}, u32[]{:S(2)}) collective-permute-start(bf16[16,64,512]{2,1,0:T(8,128)(2,1)} %all-gather.2.cloned.1.call-done.refs_5_), channel_id=1, source_target_pairs={{0,256},{128,384},{256,0},{384,128},{1,257},{129,385},{257,1},{385... | collective-permute-start | bytes 3145736 | tf_op jit(solution)/shard_map/ppermute | solution.py:285
  105.3 46.4 %collective-permute-start.11 = (bf16[16,64,512]{2,1,0:T(8,128)(2,1)}, bf16[16,64,512]{2,1,0:T(8,128)(2,1)}, u32[]{:S(2)}, u32[]{:S(2)}) collective-permute-start(bf16[16,64,512]{2,1,0:T(8,128)(2,1)} %all-gather.2.cloned.1.call-done.refs_5_), channel_id=1, source_target_pairs={{0,128},{128,256},{256,384},{384,0},{1,129},{129,257},{257,385},{3... | collective-permute-start | bytes 3145736 | tf_op jit(solution)/shard_map/ppermute | solution.py:285
  107.5 44.2 %collective-permute-start.10 = (bf16[16,64,512]{2,1,0:T(8,128)(2,1)}, bf16[16,64,512]{2,1,0:T(8,128)(2,1)}, u32[]{:S(2)}, u32[]{:S(2)}) collective-permute-start(bf16[16,64,512]{2,1,0:T(8,128)(2,1)} %all-gather.2.cloned.1.call-done.refs_5_), channel_id=1, source_target_pairs={{0,384},{128,0},{256,128},{384,256},{1,385},{129,1},{257,129},{385... | collective-permute-start | bytes 3145736 | tf_op jit(solution)/shard_map/ppermute | solution.py:285
  114.1 37.7 %copy-start.2 = (bf16[16,64,512]{2,1,0:T(8,128)(2,1)S(1)}, bf16[16,64,512]{2,1,0:T(8,128)(2,1)}, u32[]{:S(2)}) copy-start(bf16[16,64,512]{2,1,0:T(8,128)(2,1)} %all-gather.2.cloned.1.call-done.refs_5_) | copy-start | bytes 3145732
  117.1 34.6 %collective-permute-start.9 = (bf16[512,512]{1,0:T(8,128)(2,1)S(1)}, bf16[512,512]{1,0:T(8,128)(2,1)S(1)}, u32[]{:S(2)}, u32[]{:S(2)}) collective-permute-start(bf16[512,512]{1,0:T(8,128)(2,1)S(1)} %shard_map.89.refs_1_), channel_id=1, source_target_pairs={{0,3},{1,0},{2,1},{3,2},{4,7},{5,4},{6,5},{7,6},{8,11},{9,8},{10,9... | collective-permute-start | bytes 1572872 | tf_op jit(solution)/shard_map/ppermute | solution.py:285
  121.3 30.5 %collective-permute-start.8 = (bf16[512,512]{1,0:T(8,128)(2,1)S(1)}, bf16[512,512]{1,0:T(8,128)(2,1)S(1)}, u32[]{:S(2)}, u32[]{:S(2)}) collective-permute-start(bf16[512,512]{1,0:T(8,128)(2,1)S(1)} %shard_map.89.refs_1_), channel_id=1, source_target_pairs={{0,2},{1,3},{2,0},{3,1},{4,6},{5,7},{6,4},{7,5},{8,10},{9,11},{10,... | collective-permute-start | bytes 1572872 | tf_op jit(solution)/shard_map/ppermute | solution.py:285
  125.1 26.6 %collective-permute-start.7 = (bf16[512,512]{1,0:T(8,128)(2,1)S(1)}, bf16[512,512]{1,0:T(8,128)(2,1)S(1)}, u32[]{:S(2)}, u32[]{:S(2)}) collective-permute-start(bf16[512,512]{1,0:T(8,128)(2,1)S(1)} %shard_map.89.refs_1_), channel_id=1, source_target_pairs={{0,1},{1,2},{2,3},{3,0},{4,5},{5,6},{6,7},{7,4},{8,9},{9,10},{10,1... | collective-permute-start | bytes 1572872 | tf_op jit(solution)/shard_map/ppermute | solution.py:285
  155.2 6.2 %collective-permute-start.13 = (bf16[256,1024]{1,0:T(8,128)(2,1)S(1)}, bf16[256,1024]{1,0:T(8,128)(2,1)S(1)}, u32[]{:S(2)}, u32[]{:S(2)}) collective-permute-start(bf16[256,1024]{1,0:T(8,128)(2,1)S(1)} %shard_map.91), channel_id=1, source_target_pairs={{0,4},{4,0},{1,5},{5,1},{2,6},{6,2},{3,7},{7,3},{8,12},{12,8},{9,1... | collective-permute-start | bytes 1572872 | tf_op jit(solution)/shard_map/ppermute | solution.py:21
  (14 other events, 15.6 us)
Sparse Core Ops, SparseCore 0:
  30.6 60.8 all-gather.1

commit v23 on v19

--- a/solution.py
+++ b/solution.py
@@ -295,6 +295,7 @@
             for k in range(2)
         ]
         turned.append(lax.ppermute(half, ("y", "c", "x"), perm))
+    mine = jnp.where(c == 0, jnp.concatenate(turned), jnp.concatenate(turned[::-1]))
     block = ((ROWS, 512), BF)
     keep, send = call(
         pack_body,
@@ -308,8 +309,7 @@
         hbm=range(1, 7),
         vmem=60,
     )
-    turned, send = lax.optimization_barrier((turned, send))
-    mine = jnp.where(c == 0, jnp.concatenate(turned), jnp.concatenate(turned[::-1]))
+    mine, send = lax.optimization_barrier((mine, send))
     gathered = lax.all_gather(mine, ("a", "p", "q"))
 
     got = swap(send)
@@ -331,7 +331,9 @@
         unread=near[1:],
     )
     rows = lax.all_to_all(pay_y, "y", 0, 0, tiled=True)
-    (states,) = call(last_body, [((4, 128, 512), BF)], (at, rows, before, far))
+    (states,) = call(
+        last_body, [((4, 128, 512), BF)], (at, rows, before, far), unread=(mixture,)
+    )
     states = lax.all_to_all(states, NEAR, 0, 0, tiled=True)
     mixture, coef = call(
         mix_body,
@@ -340,13 +342,11 @@
         scratch=[pltpu.VMEM((4, 144, 256), BF)],
     )
     _, gathered = lax.optimization_barrier((coef, gathered))
-    rights = [gathered] + [shift(gathered, "y", 4 - k) for k in (1, 3)]
+    rights = [gathered] + [shift(gathered, "y", 4 - k) for k in (1, 3, 2)]
     (normed,) = call(
         norm_body, [((512, 512), BF)], (at, keep, got, norm_gain[None], mixture, coef, states)
     )
 
-    _, gathered = lax.optimization_barrier((normed, gathered))
-    rights.append(shift(gathered, "y", 2))
     blocks = [normed] + [shift(normed, "x", j) for j in (1, 2, 3)]
     theirs = swap(project(at, blocks, rights, True))
     own = project(at, blocks, rights, False)

time: 188 us -> 166 us (0.88)
  the two profiles are of different devices: /device:TPU:33 before, /device:TPU:1 now
where the time goes in v23:
time: 166 us; the launch traced here: 165 us
  starting transfers between devices  69.3 us (42%)
  waiting for transfers between devices  35.4 us (21%)
  Pallas kernels  24.4 us (15%)
  between operations  13.7 us (8%)
  local copies, waits for them, and re-layouts  11.9 us (7%)
  blocking collectives  8.54 us (5%)
    ppermute x6, waiting for transfers between devices, shift(): return lax.ppermute(value, axis, [(i, (i + by) % 4) for i in range(4)])  25.8 us
    pallas_call x10, Pallas kernels, call(): pl.pallas_call(run, out_shape=[jax.ShapeDtypeStruct(*o) for o in outs], i...  24.4 us
    ppermute x6, starting transfers between devices, shift(): return lax.ppermute(value, axis, [(i, (i + by) % 4) for i in range(4)])  20.1 us
    all_to_all x1, starting transfers between devices, shards(): rows = lax.all_to_all(pay_y, 'y', 0, 0, tiled=True)  11.2 us
    unnamed x40, local copies, waits for them, and re-layouts  10.5 us
    all_to_all x1, starting transfers between devices, shards(): far = lax.all_to_all(pay_a, 'a', 0, 0, tiled=True)  9.77 us
    ppermute x2, starting transfers between devices, shards(): turned.append(lax.ppermute(half, ('y', 'c', 'x'), perm))  9.44 us
    ppermute x3, starting transfers between devices, shards(): lax.ppermute(near[k], NEAR, [(i, i ^ k) for i in range(4)])  9.26 us
  transfers between devices with their start and end apart: 17, of which 5 were waited for; matrix products, arithmetic and copies ran while one was open for 0% of the time, Pallas kernels for 13%

profile of v23, /device:TPU:1, one launch (start us, length us, event | category | flops | bytes accessed | tf_op | source)
XLA Modules:
  0.0 164.7 jit_solution(16492860490915179054)
XLA Ops:
  8.0 8.8 %collective-permute-start.1 = (bf16[32,512]{1,0:T(8,128)(2,1)S(1)}, bf16[32,512]{1,0:T(8,128)(2,1)S(1)}, u32[]{:S(2)}, u32[]{:S(2)}) collective-permute-start(bf16[32,512]{1,0:T(8,128)(2,1)S(1)} %get-tuple-element.44), channel_id=1, source_target_pairs={{0,4},{4,0},{1,132},{5,128},{2,260},{6,256},{3,388},{7,384},{128,5... | collective-permute-start | bytes 98312 | tf_op jit(solution)/shard_map/ppermute | solution.py:297
  17.4 3.8 %shard_map.82 = (bf16[1072,512]{1,0:T(8,128)(2,1)}, bf16[1072,512]{1,0:T(8,128)(2,1)}) custom-call(s32[5]{0:T(128)} %stack.23.refs_0_, bf16[256,1024]{1,0:T(8,128)(2,1)} %refs_1_.1, bf16[256,1024]{1,0:T(8,128)(2,1)} %refs_2_.1, bf16[256,1024]{1,0:T(8,128)(2,1)} %refs_3_.1, bf16[256,1024]{1,0:T(8,128)(2,1)} %refs_4_.1, f32[8,256]{1,0:T(8,128)} %refs_5_.1, ...), custom_call_target="tpu_custom_call" | custom-call | flops 1000000 | bytes 1000000 | tf_op jit(solution)/shard_map/pallas_call | solution.py:59
  21.8 1.9 %collective-permute-start.2 = (bf16[1072,512]{1,0:T(8,128)(2,1)}, bf16[1072,512]{1,0:T(8,128)(2,1)S(1)}, u32[]{:S(2)}, u32[]{:S(2)}) collective-permute-start(bf16[1072,512]{1,0:T(8,128)(2,1)} %get-tuple-element.26), channel_id=1, source_target_pairs={{0,4},{4,0},{1,5},{5,1},{2,6},{6,2},{3,7},{7,3},{8,12},{12,8},{9,1... | collective-permute-start | bytes 3293192 | tf_op jit(solution)/shard_map/ppermute | solution.py:21
  23.7 2.9 %collective-permute-done.2.refs_2_ = bf16[1072,512]{1,0:T(8,128)(2,1)S(1)} collective-permute-done((bf16[1072,512]{1,0:T(8,128)(2,1)}, bf16[1072,512]{1,0:T(8,128)(2,1)S(1)}, u32[]{:S(2)}, u32[]{:S(2)}) %collective-permute-start.2) | collective-permute-done | bytes 1097760 | tf_op jit(solution)/shard_map/ppermute | solution.py:21
  29.6 8.5 %all_to_all.20.refs_1_ = bf16[4,144,128]{2,1,0:T(8,128)(2,1)S(1)} all-to-all(bf16[4,144,128]{2,1,0:T(8,128)(2,1)S(1)} %get-tuple-element.30), channel_id=1, replica_groups=mesh['y'=4,'a'=4,'p'=2,'q'=2,'c'=2,'x'=4] {'p','q'}, dimensions={0} | all-to-all | bytes 294912 | tf_op jit(solution)/shard_map/all_to_all | solution.py:318
  40.1 9.8 %all-to-all-start.1 = ((bf16[4,144,128]{2,1,0:T(8,128)(2,1)}), bf16[4,144,128]{2,1,0:T(8,128)(2,1)S(1)}, u32[]{:S(2)}, u32[]{:S(2)}) async-start(bf16[4,144,128]{2,1,0:T(8,128)(2,1)} %get-tuple-element.37), calls=%async_computation.1 | async-start | bytes 294912 | tf_op jit(solution)/shard_map/all_to_all | solution.py:320
  49.8 2.1 %collective-permute-start.3 = (bf16[144,256]{1,0:T(8,128)(2,1)S(1)}, bf16[144,256]{1,0:T(8,128)(2,1)S(1)}, u32[]{:S(2)}, u32[]{:S(2)}) collective-permute-start(bf16[144,256]{1,0:T(8,128)(2,1)S(1)} %get-tuple-element.32), channel_id=1, source_target_pairs={{0,8},{8,0},{16,24},{24,16},{1,9},{9,1},{17,25},{25,17},{2,10},{10... | collective-permute-start | bytes 221192 | tf_op jit(solution)/shard_map/ppermute | solution.py:322
  51.9 3.8 %collective-permute-start.4 = (bf16[144,256]{1,0:T(8,128)(2,1)S(1)}, bf16[144,256]{1,0:T(8,128)(2,1)S(1)}, u32[]{:S(2)}, u32[]{:S(2)}) collective-permute-start(bf16[144,256]{1,0:T(8,128)(2,1)S(1)} %get-tuple-element.33), channel_id=1, source_target_pairs={{0,16},{8,24},{16,0},{24,8},{1,17},{9,25},{17,1},{25,9},{2,18},{10... | collective-permute-start | bytes 221192 | tf_op jit(solution)/shard_map/ppermute | solution.py:322
  55.7 3.4 %collective-permute-start.5 = (bf16[144,256]{1,0:T(8,128)(2,1)S(1)}, bf16[144,256]{1,0:T(8,128)(2,1)S(1)}, u32[]{:S(2)}, u32[]{:S(2)}) collective-permute-start(bf16[144,256]{1,0:T(8,128)(2,1)S(1)} %get-tuple-element.34), channel_id=1, source_target_pairs={{0,24},{8,16},{16,8},{24,0},{1,25},{9,17},{17,9},{25,1},{2,26},{10... | collective-permute-start | bytes 221192 | tf_op jit(solution)/shard_map/ppermute | solution.py:322
  60.5 5.2 %collective-permute-done.5.refs_8_.refs_4_ = bf16[144,256]{1,0:T(8,128)(2,1)S(1)} collective-permute-done((bf16[144,256]{1,0:T(8,128)(2,1)S(1)}, bf16[144,256]{1,0:T(8,128)(2,1)S(1)}, u32[]{:S(2)}, u32[]{:S(2)}) %collective-permute-start.5) | collective-permute-done | bytes 73760 | tf_op jit(solution)/shard_map/ppermute | solution.py:322
  67.6 11.2 %all-to-all-start.2 = ((bf16[4,144,128]{2,1,0:T(8,128)(2,1)}), bf16[4,144,128]{2,1,0:T(8,128)(2,1)S(1)}, u32[]{:S(2)}, u32[]{:S(2)}) async-start(bf16[4,144,128]{2,1,0:T(8,128)(2,1)} %get-tuple-element.38), calls=%async_computation.2 | async-start | bytes 294912 | tf_op jit(solution)/shard_map/all_to_all | solution.py:333
  79.8 4.3 %shard_map.84 = (f32[512,512]{1,0:T(8,128)S(1)}, f32[512,24]{1,0:T(8,128)S(1)}) custom-call(s32[5]{0:T(128)S(1)} %copy-done.18, bf16[1072,512]{1,0:T(8,128)(2,1)S(1)} %copy-done.1, bf16[1072,512]{1,0:T(8,128)(2,1)S(1)} %collective-permute-done.2.refs_2_, bf16[4,128,128]{2,1,0:T(8,128)(2,1)S(1)} %copy-done.13), custom_call_target="tpu_custom_call" | custom-call | flops 1000000 | bytes 1000000 | tf_op jit(solution)/shard_map/pallas_call | solution.py:59
  87.1 4.9 %all-to-all-start.3 = ((bf16[4,128,512]{2,1,0:T(8,128)(2,1)}), bf16[4,128,512]{2,1,0:T(8,128)(2,1)}, u32[]{:S(2)}, u32[]{:S(2)}) async-start(bf16[4,128,512]{2,1,0:T(8,128)(2,1)} %copy-done.3), calls=%async_computation.3 | async-start | bytes 1048576 | tf_op jit(solution)/shard_map/all_to_all | solution.py:337
  96.3 4.9 %collective-permute-start.11 = (bf16[16,64,512]{2,1,0:T(8,128)(2,1)}, bf16[16,64,512]{2,1,0:T(8,128)(2,1)S(1)}, u32[]{:S(2)}, u32[]{:S(2)}) collective-permute-start(bf16[16,64,512]{2,1,0:T(8,128)(2,1)} %bitcast.6), channel_id=1, source_target_pairs={{0,256},{128,384},{256,0},{384,128},{1,257},{129,385},{257,1},{385... | collective-permute-start | bytes 3145736 | tf_op jit(solution)/shard_map/ppermute | solution.py:282
  101.2 2.2 %collective-permute-start.10 = (bf16[16,64,512]{2,1,0:T(8,128)(2,1)}, bf16[16,64,512]{2,1,0:T(8,128)(2,1)}, u32[]{:S(2)}, u32[]{:S(2)}) collective-permute-start(bf16[16,64,512]{2,1,0:T(8,128)(2,1)} %bitcast.7), channel_id=1, source_target_pairs={{0,128},{128,256},{256,384},{384,0},{1,129},{129,257},{257,385},{3... | collective-permute-start | bytes 3145736 | tf_op jit(solution)/shard_map/ppermute | solution.py:282
  103.4 4.3 %collective-permute-start.9 = (bf16[16,64,512]{2,1,0:T(8,128)(2,1)}, bf16[16,64,512]{2,1,0:T(8,128)(2,1)}, u32[]{:S(2)}, u32[]{:S(2)}) collective-permute-start(bf16[16,64,512]{2,1,0:T(8,128)(2,1)} %bitcast.8), channel_id=1, source_target_pairs={{0,384},{128,0},{256,128},{384,256},{1,385},{129,1},{257,129},{385... | collective-permute-start | bytes 3145736 | tf_op jit(solution)/shard_map/ppermute | solution.py:282
  109.9 3.1 %shard_map.89.refs_1_ = bf16[512,512]{1,0:T(8,128)(2,1)S(1)} custom-call(s32[5]{0:T(128)S(1)} %copy-done.18, bf16[1072,512]{1,0:T(8,128)(2,1)S(1)} %copy-done.1, bf16[1072,512]{1,0:T(8,128)(2,1)S(1)} %collective-permute-done.2.refs_2_, bf16[1,1024]{1,0:T(2,128)(2,1)S(1)} %broadcast_in_dim.3.refs_3_, f32[512,512]{1,0:T(8,128)S(1)} %copy-done.5, ...), custom_call_target="tpu_custom_call" | custom-call | flops 1000000 | bytes 1000000 | tf_op jit(solution)/shard_map/pallas_call | solution.py:59
  113.0 3.2 %collective-permute-start.8 = (bf16[512,512]{1,0:T(8,128)(2,1)S(1)}, bf16[512,512]{1,0:T(8,128)(2,1)S(1)}, u32[]{:S(2)}, u32[]{:S(2)}) collective-permute-start(bf16[512,512]{1,0:T(8,128)(2,1)S(1)} %shard_map.89.refs_1_), channel_id=1, source_target_pairs={{0,3},{1,0},{2,1},{3,2},{4,7},{5,4},{6,5},{7,6},{8,11},{9,8},{10,9... | collective-permute-start | bytes 1572872 | tf_op jit(solution)/shard_map/ppermute | solution.py:282
  116.2 3.0 %collective-permute-start.7 = (bf16[512,512]{1,0:T(8,128)(2,1)S(1)}, bf16[512,512]{1,0:T(8,128)(2,1)S(1)}, u32[]{:S(2)}, u32[]{:S(2)}) collective-permute-start(bf16[512,512]{1,0:T(8,128)(2,1)S(1)} %shard_map.89.refs_1_), channel_id=1, source_target_pairs={{0,2},{1,3},{2,0},{3,1},{4,6},{5,7},{6,4},{7,5},{8,10},{9,11},{10,... | collective-permute-start | bytes 1572872 | tf_op jit(solution)/shard_map/ppermute | solution.py:282
  119.3 2.5 %collective-permute-start.6 = (bf16[512,512]{1,0:T(8,128)(2,1)S(1)}, bf16[512,512]{1,0:T(8,128)(2,1)S(1)}, u32[]{:S(2)}, u32[]{:S(2)}) collective-permute-start(bf16[512,512]{1,0:T(8,128)(2,1)S(1)} %shard_map.89.refs_1_), channel_id=1, source_target_pairs={{0,1},{1,2},{2,3},{3,0},{4,5},{5,6},{6,7},{7,4},{8,9},{9,10},{10,1... | collective-permute-start | bytes 1572872 | tf_op jit(solution)/shard_map/ppermute | solution.py:282
  121.7 25.8 %collective-permute-done.10.refs_7_ = bf16[16,64,512]{2,1,0:T(8,128)(2,1)} collective-permute-done((bf16[16,64,512]{2,1,0:T(8,128)(2,1)}, bf16[16,64,512]{2,1,0:T(8,128)(2,1)}, u32[]{:S(2)}, u32[]{:S(2)}) %collective-permute-start.10) | collective-permute-done | bytes 1048608 | tf_op jit(solution)/shard_map/ppermute | solution.py:282
  147.6 3.3 %shard_map.91 = bf16[256,1024]{1,0:T(8,128)(2,1)S(1)} custom-call(s32[5]{0:T(128)S(1)} %copy-done.18, bf16[512,512]{1,0:T(8,128)(2,1)S(1)} %shard_map.89.refs_1_, bf16[512,512]{1,0:T(8,128)(2,1)S(1)} %collective-permute-done.6.refs_2_, bf16[512,512]{1,0:T(8,128)(2,1)S(1)} %collective-permute-done.7.refs_3_, ...), custom_call_target="tpu_custom_call" | custom-call | flops 1000000 | bytes 1000000 | tf_op jit(solution)/shard_map/pallas_call | solution.py:59
  150.9 2.7 %collective-permute-start.12 = (bf16[256,1024]{1,0:T(8,128)(2,1)S(1)}, bf16[256,1024]{1,0:T(8,128)(2,1)S(1)}, u32[]{:S(2)}, u32[]{:S(2)}) collective-permute-start(bf16[256,1024]{1,0:T(8,128)(2,1)S(1)} %shard_map.91), channel_id=1, source_target_pairs={{0,4},{4,0},{1,5},{5,1},{2,6},{6,2},{3,7},{7,3},{8,12},{12,8},{9,1... | collective-permute-start | bytes 1572872 | tf_op jit(solution)/shard_map/ppermute | solution.py:21
  153.6 3.3 %shard_map.90 = f32[256,1024]{1,0:T(8,128)S(1)} custom-call(s32[5]{0:T(128)S(1)} %copy-done.18, bf16[512,512]{1,0:T(8,128)(2,1)S(1)} %shard_map.89.refs_1_, bf16[512,512]{1,0:T(8,128)(2,1)S(1)} %collective-permute-done.6.refs_2_, bf16[512,512]{1,0:T(8,128)(2,1)S(1)} %collective-permute-done.7.refs_3_, bf16[512,512]{1,0:T(8,128)(2,1)S(1)} %collective-permute-done.8.refs_4_, ...), custom_call_target="tpu_custom_call" | custom-call | flops 1000000 | bytes 1000000 | tf_op jit(solution)/shard_map/pallas_call | solution.py:59
  (67 shorter events, 22.1 us)
Async XLA Ops:
  6.5 89.7 %all-gather.3.cloned.1.call-start = ((), (), s32[]{:S(2)}) async-start(), calls=%async_computation.4 | async-start | bytes 1114112 | tf_op jit(solution)/shard_map/all_gather | solution.py:313
  7.3 13.8 %collective-permute-start = (bf16[32,512]{1,0:T(8,128)(2,1)S(1)}, bf16[32,512]{1,0:T(8,128)(2,1)S(1)}, u32[]{:S(2)}, u32[]{:S(2)}) collective-permute-start(bf16[32,512]{1,0:T(8,128)(2,1)S(1)} %get-tuple-element.43), channel_id=1, source_target_pairs={{0,0},{4,4},{1,128},{5,132},{2,256},{6,260},{3,384},{7,388},{128,1... | collective-permute-start | bytes 98312 | tf_op jit(solution)/shard_map/ppermute | solution.py:297
  8.0 13.2 %collective-permute-start.1 = (bf16[32,512]{1,0:T(8,128)(2,1)S(1)}, bf16[32,512]{1,0:T(8,128)(2,1)S(1)}, u32[]{:S(2)}, u32[]{:S(2)}) collective-permute-start(bf16[32,512]{1,0:T(8,128)(2,1)S(1)} %get-tuple-element.44), channel_id=1, source_target_pairs={{0,4},{4,0},{1,132},{5,128},{2,260},{6,256},{3,388},{7,384},{128,5... | collective-permute-start | bytes 98312 | tf_op jit(solution)/shard_map/ppermute | solution.py:297
  17.4 9.3 %copy-start.18 = (s32[5]{0:T(128)S(1)}, s32[5]{0:T(128)}, u32[]{:S(2)}) copy-start(s32[5]{0:T(128)} %stack.23.refs_0_) | copy-start | bytes 64
  21.8 4.8 %collective-permute-start.2 = (bf16[1072,512]{1,0:T(8,128)(2,1)}, bf16[1072,512]{1,0:T(8,128)(2,1)S(1)}, u32[]{:S(2)}, u32[]{:S(2)}) collective-permute-start(bf16[1072,512]{1,0:T(8,128)(2,1)} %get-tuple-element.26), channel_id=1, source_target_pairs={{0,4},{4,0},{1,5},{5,1},{2,6},{6,2},{3,7},{7,3},{8,12},{12,8},{9,1... | collective-permute-start | bytes 3293192 | tf_op jit(solution)/shard_map/ppermute | solution.py:21
  29.6 9.8 %copy-start.12 = (bf16[4,128,128]{2,1,0:T(8,128)(2,1)}, bf16[4,128,128]{2,1,0:T(8,128)(2,1)S(1)}, u32[]{:S(2)}) copy-start(bf16[4,128,128]{2,1,0:T(8,128)(2,1)S(1)} %get-tuple-element.27.refs_3_) | copy-start | bytes 393220
  29.6 49.2 %copy-start.1 = (bf16[1072,512]{1,0:T(8,128)(2,1)S(1)}, bf16[1072,512]{1,0:T(8,128)(2,1)}, u32[]{:S(2)}) copy-start(bf16[1072,512]{1,0:T(8,128)(2,1)} %get-tuple-element.24.refs_1_) | copy-start | bytes 3293188
  40.1 25.7 %all-to-all-start.1 = ((bf16[4,144,128]{2,1,0:T(8,128)(2,1)}), bf16[4,144,128]{2,1,0:T(8,128)(2,1)S(1)}, u32[]{:S(2)}, u32[]{:S(2)}) async-start(bf16[4,144,128]{2,1,0:T(8,128)(2,1)} %get-tuple-element.37), calls=%async_computation.1 | async-start | bytes 294912 | tf_op jit(solution)/shard_map/all_to_all | solution.py:320
  49.8 10.2 %collective-permute-start.3 = (bf16[144,256]{1,0:T(8,128)(2,1)S(1)}, bf16[144,256]{1,0:T(8,128)(2,1)S(1)}, u32[]{:S(2)}, u32[]{:S(2)}) collective-permute-start(bf16[144,256]{1,0:T(8,128)(2,1)S(1)} %get-tuple-element.32), channel_id=1, source_target_pairs={{0,8},{8,0},{16,24},{24,16},{1,9},{9,1},{17,25},{25,17},{2,10},{10... | collective-permute-start | bytes 221192 | tf_op jit(solution)/shard_map/ppermute | solution.py:322
  51.9 8.6 %collective-permute-start.4 = (bf16[144,256]{1,0:T(8,128)(2,1)S(1)}, bf16[144,256]{1,0:T(8,128)(2,1)S(1)}, u32[]{:S(2)}, u32[]{:S(2)}) collective-permute-start(bf16[144,256]{1,0:T(8,128)(2,1)S(1)} %get-tuple-element.33), channel_id=1, source_target_pairs={{0,16},{8,24},{16,0},{24,8},{1,17},{9,25},{17,1},{25,9},{2,18},{10... | collective-permute-start | bytes 221192 | tf_op jit(solution)/shard_map/ppermute | solution.py:322
  55.7 10.0 %collective-permute-start.5 = (bf16[144,256]{1,0:T(8,128)(2,1)S(1)}, bf16[144,256]{1,0:T(8,128)(2,1)S(1)}, u32[]{:S(2)}, u32[]{:S(2)}) collective-permute-start(bf16[144,256]{1,0:T(8,128)(2,1)S(1)} %get-tuple-element.34), channel_id=1, source_target_pairs={{0,24},{8,16},{16,8},{24,0},{1,25},{9,17},{17,9},{25,1},{2,26},{10... | collective-permute-start | bytes 221192 | tf_op jit(solution)/shard_map/ppermute | solution.py:322
  65.7 13.1 %copy-start.6 = (bf16[144,256]{1,0:T(8,128)(2,1)}, bf16[144,256]{1,0:T(8,128)(2,1)S(1)}, u32[]{:S(2)}) copy-start(bf16[144,256]{1,0:T(8,128)(2,1)S(1)} %collective-permute-done.5.refs_8_.refs_4_) | copy-start | bytes 221188
  67.6 17.2 %all-to-all-start.2 = ((bf16[4,144,128]{2,1,0:T(8,128)(2,1)}), bf16[4,144,128]{2,1,0:T(8,128)(2,1)S(1)}, u32[]{:S(2)}, u32[]{:S(2)}) async-start(bf16[4,144,128]{2,1,0:T(8,128)(2,1)} %get-tuple-element.38), calls=%async_computation.2 | async-start | bytes 294912 | tf_op jit(solution)/shard_map/all_to_all | solution.py:333
  87.1 4.9 %copy-start.15 = (bf16[144,256]{1,0:T(8,128)(2,1)S(1)}, bf16[144,256]{1,0:T(8,128)(2,1)}, u32[]{:S(2)}) copy-start(bf16[144,256]{1,0:T(8,128)(2,1)} %copy-done.14) | copy-start | bytes 221188
  87.1 20.6 %all-to-all-start.3 = ((bf16[4,128,512]{2,1,0:T(8,128)(2,1)}), bf16[4,128,512]{2,1,0:T(8,128)(2,1)}, u32[]{:S(2)}, u32[]{:S(2)}) async-start(bf16[4,128,512]{2,1,0:T(8,128)(2,1)} %copy-done.3), calls=%async_computation.3 | async-start | bytes 1048576 | tf_op jit(solution)/shard_map/all_to_all | solution.py:337
  92.9 14.8 %copy-start.19 = (bf16[1024]{0:T(1024)(128)(2,1)S(1)}, bf16[1024]{0:T(1024)(128)(2,1)}, u32[]{:S(2)}) copy-start(bf16[1024]{0:T(1024)(128)(2,1)} %param.14) | copy-start | bytes 6148
  96.3 23.0 %collective-permute-start.11 = (bf16[16,64,512]{2,1,0:T(8,128)(2,1)}, bf16[16,64,512]{2,1,0:T(8,128)(2,1)S(1)}, u32[]{:S(2)}, u32[]{:S(2)}) collective-permute-start(bf16[16,64,512]{2,1,0:T(8,128)(2,1)} %bitcast.6), channel_id=1, source_target_pairs={{0,256},{128,384},{256,0},{384,128},{1,257},{129,385},{257,1},{385... | collective-permute-start | bytes 3145736 | tf_op jit(solution)/shard_map/ppermute | solution.py:282
  101.2 46.4 %collective-permute-start.10 = (bf16[16,64,512]{2,1,0:T(8,128)(2,1)}, bf16[16,64,512]{2,1,0:T(8,128)(2,1)}, u32[]{:S(2)}, u32[]{:S(2)}) collective-permute-start(bf16[16,64,512]{2,1,0:T(8,128)(2,1)} %bitcast.7), channel_id=1, source_target_pairs={{0,128},{128,256},{256,384},{384,0},{1,129},{129,257},{257,385},{3... | collective-permute-start | bytes 3145736 | tf_op jit(solution)/shard_map/ppermute | solution.py:282
  103.4 44.2 %collective-permute-start.9 = (bf16[16,64,512]{2,1,0:T(8,128)(2,1)}, bf16[16,64,512]{2,1,0:T(8,128)(2,1)}, u32[]{:S(2)}, u32[]{:S(2)}) collective-permute-start(bf16[16,64,512]{2,1,0:T(8,128)(2,1)} %bitcast.8), channel_id=1, source_target_pairs={{0,384},{128,0},{256,128},{384,256},{1,385},{129,1},{257,129},{385... | collective-permute-start | bytes 3145736 | tf_op jit(solution)/shard_map/ppermute | solution.py:282
  109.9 37.7 %copy-start.2 = (bf16[1024,512]{1,0:T(8,128)(2,1)S(1)}, bf16[1024,512]{1,0:T(8,128)(2,1)}, u32[]{:S(2)}) copy-start(bf16[1024,512]{1,0:T(8,128)(2,1)} %all-gather.3.cloned.1.call-done) | copy-start | bytes 3145732
  113.0 34.6 %collective-permute-start.8 = (bf16[512,512]{1,0:T(8,128)(2,1)S(1)}, bf16[512,512]{1,0:T(8,128)(2,1)S(1)}, u32[]{:S(2)}, u32[]{:S(2)}) collective-permute-start(bf16[512,512]{1,0:T(8,128)(2,1)S(1)} %shard_map.89.refs_1_), channel_id=1, source_target_pairs={{0,3},{1,0},{2,1},{3,2},{4,7},{5,4},{6,5},{7,6},{8,11},{9,8},{10,9... | collective-permute-start | bytes 1572872 | tf_op jit(solution)/shard_map/ppermute | solution.py:282
  116.2 31.3 %collective-permute-start.7 = (bf16[512,512]{1,0:T(8,128)(2,1)S(1)}, bf16[512,512]{1,0:T(8,128)(2,1)S(1)}, u32[]{:S(2)}, u32[]{:S(2)}) collective-permute-start(bf16[512,512]{1,0:T(8,128)(2,1)S(1)} %shard_map.89.refs_1_), channel_id=1, source_target_pairs={{0,2},{1,3},{2,0},{3,1},{4,6},{5,7},{6,4},{7,5},{8,10},{9,11},{10,... | collective-permute-start | bytes 1572872 | tf_op jit(solution)/shard_map/ppermute | solution.py:282
  119.3 28.3 %collective-permute-start.6 = (bf16[512,512]{1,0:T(8,128)(2,1)S(1)}, bf16[512,512]{1,0:T(8,128)(2,1)S(1)}, u32[]{:S(2)}, u32[]{:S(2)}) collective-permute-start(bf16[512,512]{1,0:T(8,128)(2,1)S(1)} %shard_map.89.refs_1_), channel_id=1, source_target_pairs={{0,1},{1,2},{2,3},{3,0},{4,5},{5,6},{6,7},{7,4},{8,9},{9,10},{10,1... | collective-permute-start | bytes 1572872 | tf_op jit(solution)/shard_map/ppermute | solution.py:282
  150.9 6.0 %collective-permute-start.12 = (bf16[256,1024]{1,0:T(8,128)(2,1)S(1)}, bf16[256,1024]{1,0:T(8,128)(2,1)S(1)}, u32[]{:S(2)}, u32[]{:S(2)}) collective-permute-start(bf16[256,1024]{1,0:T(8,128)(2,1)S(1)} %shard_map.91), channel_id=1, source_target_pairs={{0,4},{4,0},{1,5},{5,1},{2,6},{6,2},{3,7},{7,3},{8,12},{12,8},{9,1... | collective-permute-start | bytes 1572872 | tf_op jit(solution)/shard_map/ppermute | solution.py:21
  (13 other events, 15.4 us)
Sparse Core Ops, SparseCore 0:
  23.8 69.7 all-gather.2

commit v24 on v23

--- a/solution.py
+++ b/solution.py
@@ -13,8 +13,8 @@
 NEAR = ("p", "q")
 NT = (((1,), (1,)), ((), ()))
 TN = (((0,), (0,)), ((), ()))
-LOGS = 1024
-ROWS = 1072
+LOGS = 512
+ROWS = 560
 
 
 def swap(value):
@@ -68,7 +68,7 @@
 
 
 def pack_body(
-    at, keys, values, queries, gates, decay, mix, keep, send, small, levels, sems
+    at, keys, values, decay, mix, keep, send, small, levels, sems
 ):
     core = at[0]
     mine = pl.ds(pl.multiple_of(core * 512, 512), 512)
@@ -77,9 +77,9 @@
         pltpu.make_async_copy(decay, small, sems.at[0]),
         pltpu.make_async_copy(mix, levels, sems.at[1]),
     ]
-    for i, ref in enumerate((keys, values, queries, gates)):
+    for i, ref in enumerate((keys, values)):
         rows = pl.ds(i * 256, 256)
-        for out, cols, n in ((send, theirs, 2), (keep, mine, 6)):
+        for out, cols, n in ((send, theirs, 2), (keep, mine, 4)):
             copies.append(pltpu.make_async_copy(ref.at[:, cols], out.at[rows, :], sems.at[n + i]))
     for copy in copies:
         copy.start()
@@ -93,6 +93,20 @@
         out[LOGS : LOGS + 48, 0:256] = high
         out[LOGS : LOGS + 48, 256:512] = (logs - high.astype(F32)).astype(BF)
     for copy in copies[2:]:
+        copy.wait()
+
+
+def late_body(at, queries, gates, keep, send, sems):
+    core = at[0]
+    copies = []
+    for i, ref in enumerate((queries, gates)):
+        for n, (out, half) in enumerate(((send, 1 - core), (keep, core))):
+            cols = pl.ds(pl.multiple_of(half * 512, 512), 512)
+            rows = pl.ds(i * 256, 256)
+            copies.append(pltpu.make_async_copy(ref.at[:, cols], out.at[rows, :], sems.at[i, n]))
+    for copy in copies:
+        copy.start()
+    for copy in copies:
         copy.wait()
 
 
@@ -183,7 +197,7 @@
     return at, pl.ds(pl.multiple_of(at * 256, 256), 256)
 
 
-def own_body(at, keep, got, first, mixture, coef):
+def own_body(at, keep, got, keep_q, got_q, first, mixture, coef):
     core = at[0]
     rows = lax.broadcasted_iota(jnp.int32, (256, 256), 0)
     cols = lax.broadcasted_iota(jnp.int32, (256, 256), 1)
@@ -200,7 +214,7 @@
         first_log = jnp.where(second == 1, first_log, 0.0)
         for h in range(4):
             hc = slice(h * 128, h * 128 + 128)
-            q, kb, v = ref[512:768, hc], ref[0:256, hc], ref[256:512, hc]
+            q, kb, v = (keep_q, got_q)[s][0:256, hc], ref[0:256, hc], ref[256:512, hc]
             local = at_col[:, h : h + 1]
             gap = jnp.where(lower, local - at_row[h : h + 1, :], -1e30)
             weights = (dot(q, kb, NT) * jnp.exp(gap)).astype(BF)
@@ -222,7 +236,7 @@
         hc = slice(h * 128, h * 128 + 128)
         for s, ref in enumerate((keep, got)):
             _, here = place(s, at[0])
-            read = dot(ref[512:768, hc], near[h, 0:128, :])
+            read = dot(ref[0:256, hc], near[h, 0:128, :])
             total = mixture[here, hc] + read[:, 0:128] * coef[here, 6 * h : 6 * h + 1]
             mixed[here, hc] = total + read[:, 128:256] * coef[here, 6 * h + 1 : 6 * h + 2]
             later[here, 4 * h : 4 * h + 4] = coef[here, 6 * h + 2 : 6 * h + 6] * before
@@ -235,10 +249,10 @@
         hc = slice(h * 128, h * 128 + 128)
         for s, ref in enumerate((keep, got)):
             _, here = place(s, core)
-            z = ref[768:1024, hc].astype(F32)
+            z = ref[256:512, hc].astype(F32)
             total = mixture[here, hc]
             for l in range(0, 4, 2):
-                read = dot(ref[512:768, hc], states[h, :, l * 128 : l * 128 + 256])
+                read = dot(ref[0:256, hc], states[h, :, l * 128 : l * 128 + 256])
                 total += read[:, 0:128] * coef[here, 4 * h + l : 4 * h + l + 1]
                 total += read[:, 128:256] * coef[here, 4 * h + l + 1 : 4 * h + l + 2]
             gated = total * (z / (1.0 + jnp.exp(-z)))
@@ -300,13 +314,13 @@
     keep, send = call(
         pack_body,
         [block, block],
-        (at, keys, values, queries, gates, log_decay, level_mix),
+        (at, keys, values, log_decay, level_mix),
         scratch=[
             pltpu.VMEM((8, 256), F32),
             pltpu.VMEM((8, 8, 256), F32),
-            pltpu.SemaphoreType.DMA((10,)),
+            pltpu.SemaphoreType.DMA((6,)),
         ],
-        hbm=range(1, 7),
+        hbm=range(1, 5),
         vmem=60,
     )
     mine, send = lax.optimization_barrier((mine, send))
@@ -315,6 +329,16 @@
     got = swap(send)
     pay = ((4, 144, 128), BF)
     pay_b, first = call(ends_body, [pay, ((4, 128, 128), BF)], (at, keep, got))
+    queries, pay_b = lax.optimization_barrier((queries, pay_b))
+    keep_q, send_q = call(
+        late_body,
+        [((512, 512), BF)] * 2,
+        (at, queries, gates),
+        scratch=[pltpu.SemaphoreType.DMA((2, 2))],
+        hbm=(1, 2),
+        vmem=60,
+    )
+    got_q = swap(send_q)
     near = lax.all_to_all(pay_b, NEAR, 0, 0, tiled=True)
     pay_a, *near = call(near_body, [pay] + [((144, 256), BF)] * 4, (at, near))
     far = lax.all_to_all(pay_a, "a", 0, 0, tiled=True)
@@ -322,7 +346,7 @@
         lax.ppermute(near[k], NEAR, [(i, i ^ k) for i in range(4)]) for k in (1, 2, 3)
     ]
     mixture, coef = call(
-        own_body, [((512, 512), F32), ((512, 24), F32)], (at, keep, got, first)
+        own_body, [((512, 512), F32), ((512, 24), F32)], (at, keep, got, keep_q, got_q, first)
     )
     pay_y, far, before = call(
         far_body,
@@ -338,13 +362,13 @@
     mixture, coef = call(
         mix_body,
         [((512, 512), F32), ((512, 16), F32)],
-        (at, keep, got, mixture, coef, *near),
+        (at, keep_q, got_q, mixture, coef, *near),
         scratch=[pltpu.VMEM((4, 144, 256), BF)],
     )
     _, gathered = lax.optimization_barrier((coef, gathered))
     rights = [gathered] + [shift(gathered, "y", 4 - k) for k in (1, 3, 2)]
     (normed,) = call(
-        norm_body, [((512, 512), BF)], (at, keep, got, norm_gain[None], mixture, coef, states)
+        norm_body, [((512, 512), BF)], (at, keep_q, got_q, norm_gain[None], mixture, coef, states)
     )
 
     blocks = [normed] + [shift(normed, "x", j) for j in (1, 2, 3)]

time: 166 us -> 167 us (level)
  waiting for transfers between devices: 35.4 us -> 31.3 us
  starting transfers between devices: 69.3 us -> 72.9 us
  Pallas kernels: 24.4 us -> 27.5 us
  local copies, waits for them, and re-layouts: 11.9 us -> 10.1 us
    ppermute x2 -> x3, starting transfers between devices: 4.61 us -> 8.42 us  [swap(): return lax.ppermute(value, 'c', [(0, 1), (1, 0)])]
    pallas_call x10 -> x11, Pallas kernels: 24.4 us -> 27.5 us  [call(): pl.pallas_call(run, out_shape=[jax.ShapeDtypeStruct(*o) for o in outs], i...]
    ppermute x3, waiting for transfers between devices: 6.62 us -> 3.54 us  [shards(): lax.ppermute(near[k], NEAR, [(i, i ^ k) for i in range(4)])]
    unnamed x40 -> x42, local copies, waits for them, and re-layouts: 10.5 us -> 8.63 us
  transfers between devices with their start and end apart: 17 -> 18, of which waited for: 5 -> 3; matrix products, arithmetic and copies ran while one was open for 0% -> 0% of each run, Pallas kernels for 13% -> 15%
where the time goes in v24:
time: 167 us; the launch traced here: 166 us
  starting transfers between devices  72.9 us (44%)
  waiting for transfers between devices  31.3 us (19%)
  Pallas kernels  27.5 us (16%)
  between operations  13.7 us (8%)
  local copies, waits for them, and re-layouts  10.1 us (6%)
  blocking collectives  8.41 us (5%)
    pallas_call x11, Pallas kernels, call(): pl.pallas_call(run, out_shape=[jax.ShapeDtypeStruct(*o) for o in outs], i...  27.5 us
    ppermute x6, waiting for transfers between devices, shift(): return lax.ppermute(value, axis, [(i, (i + by) % 4) for i in range(4)])  25.6 us
    ppermute x6, starting transfers between devices, shift(): return lax.ppermute(value, axis, [(i, (i + by) % 4) for i in range(4)])  20.3 us
    all_to_all x1, starting transfers between devices, shards(): rows = lax.all_to_all(pay_y, 'y', 0, 0, tiled=True)  11 us
    all_to_all x1, starting transfers between devices, shards(): far = lax.all_to_all(pay_a, 'a', 0, 0, tiled=True)  9.77 us
    ppermute x2, starting transfers between devices, shards(): turned.append(lax.ppermute(half, ('y', 'c', 'x'), perm))  9.44 us
    ppermute x3, starting transfers between devices, shards(): lax.ppermute(near[k], NEAR, [(i, i ^ k) for i in range(4)])  9.27 us
    unnamed x42, local copies, waits for them, and re-layouts  8.63 us
  transfers between devices with their start and end apart: 18, of which 3 were waited for; matrix products, arithmetic and copies ran while one was open for 0% of the time, Pallas kernels for 15%

profile of v24, /device:TPU:1, one launch (start us, length us, event | category | flops | bytes accessed | tf_op | source)
XLA Modules:
  0.0 165.5 jit_solution(14685851103322529576)
XLA Ops:
  8.0 8.8 %collective-permute-start.1 = (bf16[32,512]{1,0:T(8,128)(2,1)S(1)}, bf16[32,512]{1,0:T(8,128)(2,1)S(1)}, u32[]{:S(2)}, u32[]{:S(2)}) collective-permute-start(bf16[32,512]{1,0:T(8,128)(2,1)S(1)} %get-tuple-element.52), channel_id=1, source_target_pairs={{0,4},{4,0},{1,132},{5,128},{2,260},{6,256},{3,388},{7,384},{128,5... | collective-permute-start | bytes 98312 | tf_op jit(solution)/shard_map/ppermute | solution.py:311
  17.5 3.0 %shard_map.82 = (bf16[560,512]{1,0:T(8,128)(2,1)}, bf16[560,512]{1,0:T(8,128)(2,1)}) custom-call(s32[5]{0:T(128)} %stack.23.refs_0_, bf16[256,1024]{1,0:T(8,128)(2,1)} %refs_1_.1, bf16[256,1024]{1,0:T(8,128)(2,1)} %refs_2_.2, f32[8,256]{1,0:T(8,128)} %refs_3_.1, f32[8,8,256]{2,1,0:T(8,128)} %refs_4_.1), custom_call_target="tpu_custom_call" | custom-call | flops 1000000 | bytes 1000000 | tf_op jit(solution)/shard_map/pallas_call | solution.py:59
  28.0 8.4 %all_to_all.20.refs_1_ = bf16[4,144,128]{2,1,0:T(8,128)(2,1)S(1)} all-to-all(bf16[4,144,128]{2,1,0:T(8,128)(2,1)S(1)} %get-tuple-element.38), channel_id=1, replica_groups=mesh['y'=4,'a'=4,'p'=2,'q'=2,'c'=2,'x'=4] {'p','q'}, dimensions={0} | all-to-all | bytes 294912 | tf_op jit(solution)/shard_map/all_to_all | solution.py:342
  38.3 9.8 %all-to-all-start.1 = ((bf16[4,144,128]{2,1,0:T(8,128)(2,1)}), bf16[4,144,128]{2,1,0:T(8,128)(2,1)S(1)}, u32[]{:S(2)}, u32[]{:S(2)}) async-start(bf16[4,144,128]{2,1,0:T(8,128)(2,1)} %get-tuple-element.45), calls=%async_computation.1 | async-start | bytes 294912 | tf_op jit(solution)/shard_map/all_to_all | solution.py:344
  48.1 3.0 %shard_map.84 = (bf16[512,512]{1,0:T(8,128)(2,1)}, bf16[512,512]{1,0:T(8,128)(2,1)}) custom-call(s32[5]{0:T(128)} %stack.23.refs_0_, bf16[256,1024]{1,0:T(8,128)(2,1)} %refs_1_.2, bf16[256,1024]{1,0:T(8,128)(2,1)} %refs_2_.3), custom_call_target="tpu_custom_call" | custom-call | flops 1000000 | bytes 1000000 | tf_op jit(solution)/shard_map/pallas_call | solution.py:59
  51.1 3.7 %collective-permute-start.3 = (bf16[512,512]{1,0:T(8,128)(2,1)}, bf16[512,512]{1,0:T(8,128)(2,1)S(1)}, u32[]{:S(2)}, u32[]{:S(2)}) collective-permute-start(bf16[512,512]{1,0:T(8,128)(2,1)} %get-tuple-element.34), channel_id=1, source_target_pairs={{0,4},{4,0},{1,5},{5,1},{2,6},{6,2},{3,7},{7,3},{8,12},{12,8},{9,1... | collective-permute-start | bytes 1572872 | tf_op jit(solution)/shard_map/ppermute | solution.py:21
  54.8 2.2 %collective-permute-start.4 = (bf16[144,256]{1,0:T(8,128)(2,1)S(1)}, bf16[144,256]{1,0:T(8,128)(2,1)S(1)}, u32[]{:S(2)}, u32[]{:S(2)}) collective-permute-start(bf16[144,256]{1,0:T(8,128)(2,1)S(1)} %get-tuple-element.40), channel_id=1, source_target_pairs={{0,8},{8,0},{16,24},{24,16},{1,9},{9,1},{17,25},{25,17},{2,10},{10... | collective-permute-start | bytes 221192 | tf_op jit(solution)/shard_map/ppermute | solution.py:346
  57.1 3.0 %collective-permute-start.5 = (bf16[144,256]{1,0:T(8,128)(2,1)S(1)}, bf16[144,256]{1,0:T(8,128)(2,1)S(1)}, u32[]{:S(2)}, u32[]{:S(2)}) collective-permute-start(bf16[144,256]{1,0:T(8,128)(2,1)S(1)} %get-tuple-element.41), channel_id=1, source_target_pairs={{0,16},{8,24},{16,0},{24,8},{1,17},{9,25},{17,1},{25,9},{2,18},{10... | collective-permute-start | bytes 221192 | tf_op jit(solution)/shard_map/ppermute | solution.py:346
  60.1 4.0 %collective-permute-start.6 = (bf16[144,256]{1,0:T(8,128)(2,1)S(1)}, bf16[144,256]{1,0:T(8,128)(2,1)S(1)}, u32[]{:S(2)}, u32[]{:S(2)}) collective-permute-start(bf16[144,256]{1,0:T(8,128)(2,1)S(1)} %get-tuple-element.42), channel_id=1, source_target_pairs={{0,24},{8,16},{16,8},{24,0},{1,25},{9,17},{17,9},{25,1},{2,26},{10... | collective-permute-start | bytes 221192 | tf_op jit(solution)/shard_map/ppermute | solution.py:346
  64.1 3.5 %collective-permute-done.6.refs_8_.refs_4_ = bf16[144,256]{1,0:T(8,128)(2,1)S(1)} collective-permute-done((bf16[144,256]{1,0:T(8,128)(2,1)S(1)}, bf16[144,256]{1,0:T(8,128)(2,1)S(1)}, u32[]{:S(2)}, u32[]{:S(2)}) %collective-permute-start.6) | collective-permute-done | bytes 73760 | tf_op jit(solution)/shard_map/ppermute | solution.py:346
  69.6 11.0 %all-to-all-start.2 = ((bf16[4,144,128]{2,1,0:T(8,128)(2,1)}), bf16[4,144,128]{2,1,0:T(8,128)(2,1)S(1)}, u32[]{:S(2)}, u32[]{:S(2)}) async-start(bf16[4,144,128]{2,1,0:T(8,128)(2,1)} %get-tuple-element.46), calls=%async_computation.2 | async-start | bytes 294912 | tf_op jit(solution)/shard_map/all_to_all | solution.py:357
  81.5 4.3 %shard_map.85 = (f32[512,512]{1,0:T(8,128)S(1)}, f32[512,24]{1,0:T(8,128)S(1)}) custom-call(s32[5]{0:T(128)S(1)} %copy-done.17, bf16[560,512]{1,0:T(8,128)(2,1)S(1)} %copy-done.3, bf16[560,512]{1,0:T(8,128)(2,1)S(1)} %collective-permute-done.2.refs_2_, bf16[512,512]{1,0:T(8,128)(2,1)S(1)} %copy-done, ...), custom_call_target="tpu_custom_call" | custom-call | flops 1000000 | bytes 1000000 | tf_op jit(solution)/shard_map/pallas_call | solution.py:59
  88.8 4.7 %all-to-all-start.3 = ((bf16[4,128,512]{2,1,0:T(8,128)(2,1)}), bf16[4,128,512]{2,1,0:T(8,128)(2,1)}, u32[]{:S(2)}, u32[]{:S(2)}) async-start(bf16[4,128,512]{2,1,0:T(8,128)(2,1)} %shard_map.89), calls=%async_computation.3 | async-start | bytes 1048576 | tf_op jit(solution)/shard_map/all_to_all | solution.py:361
  96.9 5.0 %collective-permute-start.12 = (bf16[16,64,512]{2,1,0:T(8,128)(2,1)}, bf16[16,64,512]{2,1,0:T(8,128)(2,1)S(1)}, u32[]{:S(2)}, u32[]{:S(2)}) collective-permute-start(bf16[16,64,512]{2,1,0:T(8,128)(2,1)} %bitcast.6), channel_id=1, source_target_pairs={{0,256},{128,384},{256,0},{384,128},{1,257},{129,385},{257,1},{385... | collective-permute-start | bytes 3145736 | tf_op jit(solution)/shard_map/ppermute | solution.py:296
  101.9 2.2 %collective-permute-start.11 = (bf16[16,64,512]{2,1,0:T(8,128)(2,1)}, bf16[16,64,512]{2,1,0:T(8,128)(2,1)S(1)}, u32[]{:S(2)}, u32[]{:S(2)}) collective-permute-start(bf16[16,64,512]{2,1,0:T(8,128)(2,1)} %bitcast.7), channel_id=1, source_target_pairs={{0,128},{128,256},{256,384},{384,0},{1,129},{129,257},{257,385},{3... | collective-permute-start | bytes 3145736 | tf_op jit(solution)/shard_map/ppermute | solution.py:296
  104.1 4.3 %collective-permute-start.10 = (bf16[16,64,512]{2,1,0:T(8,128)(2,1)}, bf16[16,64,512]{2,1,0:T(8,128)(2,1)}, u32[]{:S(2)}, u32[]{:S(2)}) collective-permute-start(bf16[16,64,512]{2,1,0:T(8,128)(2,1)} %bitcast.8), channel_id=1, source_target_pairs={{0,384},{128,0},{256,128},{384,256},{1,385},{129,1},{257,129},{385... | collective-permute-start | bytes 3145736 | tf_op jit(solution)/shard_map/ppermute | solution.py:296
  110.6 3.1 %shard_map.90.refs_1_ = bf16[512,512]{1,0:T(8,128)(2,1)S(1)} custom-call(s32[5]{0:T(128)S(1)} %copy-done.17, bf16[512,512]{1,0:T(8,128)(2,1)S(1)} %copy-done, bf16[512,512]{1,0:T(8,128)(2,1)S(1)} %collective-permute-done.3.refs_4_.refs_2_, bf16[1,1024]{1,0:T(2,128)(2,1)S(1)} %broadcast_in_dim.3.refs_3_, f32[512,512]{1,0:T(8,128)S(1)} %copy-done.5, ...), custom_call_target="tpu_custom_call" | custom-call | flops 1000000 | bytes 1000000 | tf_op jit(solution)/shard_map/pallas_call | solution.py:59
  113.8 3.4 %collective-permute-start.9 = (bf16[512,512]{1,0:T(8,128)(2,1)S(1)}, bf16[512,512]{1,0:T(8,128)(2,1)S(1)}, u32[]{:S(2)}, u32[]{:S(2)}) collective-permute-start(bf16[512,512]{1,0:T(8,128)(2,1)S(1)} %shard_map.90.refs_1_), channel_id=1, source_target_pairs={{0,3},{1,0},{2,1},{3,2},{4,7},{5,4},{6,5},{7,6},{8,11},{9,8},{10,9... | collective-permute-start | bytes 1572872 | tf_op jit(solution)/shard_map/ppermute | solution.py:296
  117.2 3.2 %collective-permute-start.8 = (bf16[512,512]{1,0:T(8,128)(2,1)S(1)}, bf16[512,512]{1,0:T(8,128)(2,1)S(1)}, u32[]{:S(2)}, u32[]{:S(2)}) collective-permute-start(bf16[512,512]{1,0:T(8,128)(2,1)S(1)} %shard_map.90.refs_1_), channel_id=1, source_target_pairs={{0,2},{1,3},{2,0},{3,1},{4,6},{5,7},{6,4},{7,5},{8,10},{9,11},{10,... | collective-permute-start | bytes 1572872 | tf_op jit(solution)/shard_map/ppermute | solution.py:296
  120.5 2.2 %collective-permute-start.7 = (bf16[512,512]{1,0:T(8,128)(2,1)S(1)}, bf16[512,512]{1,0:T(8,128)(2,1)S(1)}, u32[]{:S(2)}, u32[]{:S(2)}) collective-permute-start(bf16[512,512]{1,0:T(8,128)(2,1)S(1)} %shard_map.90.refs_1_), channel_id=1, source_target_pairs={{0,1},{1,2},{2,3},{3,0},{4,5},{5,6},{6,7},{7,4},{8,9},{9,10},{10,1... | collective-permute-start | bytes 1572872 | tf_op jit(solution)/shard_map/ppermute | solution.py:296
  122.7 25.5 %collective-permute-done.11.refs_7_ = bf16[16,64,512]{2,1,0:T(8,128)(2,1)S(1)} collective-permute-done((bf16[16,64,512]{2,1,0:T(8,128)(2,1)}, bf16[16,64,512]{2,1,0:T(8,128)(2,1)S(1)}, u32[]{:S(2)}, u32[]{:S(2)}) %collective-permute-start.11) | collective-permute-done | bytes 1048608 | tf_op jit(solution)/shard_map/ppermute | solution.py:296
  148.2 3.3 %shard_map.92 = bf16[256,1024]{1,0:T(8,128)(2,1)S(1)} custom-call(s32[5]{0:T(128)S(1)} %copy-done.17, bf16[512,512]{1,0:T(8,128)(2,1)S(1)} %shard_map.90.refs_1_, bf16[512,512]{1,0:T(8,128)(2,1)S(1)} %collective-permute-done.7.refs_2_, bf16[512,512]{1,0:T(8,128)(2,1)S(1)} %collective-permute-done.8.refs_3_, ...), custom_call_target="tpu_custom_call" | custom-call | flops 1000000 | bytes 1000000 | tf_op jit(solution)/shard_map/pallas_call | solution.py:59
  151.6 2.8 %collective-permute-start.13 = (bf16[256,1024]{1,0:T(8,128)(2,1)S(1)}, bf16[256,1024]{1,0:T(8,128)(2,1)S(1)}, u32[]{:S(2)}, u32[]{:S(2)}) collective-permute-start(bf16[256,1024]{1,0:T(8,128)(2,1)S(1)} %shard_map.92), channel_id=1, source_target_pairs={{0,4},{4,0},{1,5},{5,1},{2,6},{6,2},{3,7},{7,3},{8,12},{12,8},{9,1... | collective-permute-start | bytes 1572872 | tf_op jit(solution)/shard_map/ppermute | solution.py:21
  154.4 3.3 %shard_map.91 = f32[256,1024]{1,0:T(8,128)S(1)} custom-call(s32[5]{0:T(128)S(1)} %copy-done.17, bf16[512,512]{1,0:T(8,128)(2,1)S(1)} %shard_map.90.refs_1_, bf16[512,512]{1,0:T(8,128)(2,1)S(1)} %collective-permute-done.7.refs_2_, bf16[512,512]{1,0:T(8,128)(2,1)S(1)} %collective-permute-done.8.refs_3_, bf16[512,512]{1,0:T(8,128)(2,1)S(1)} %collective-permute-done.9.refs_4_, ...), custom_call_target="tpu_custom_call" | custom-call | flops 1000000 | bytes 1000000 | tf_op jit(solution)/shard_map/pallas_call | solution.py:59
  (72 shorter events, 23.8 us)
Async XLA Ops:
  6.5 90.4 %all-gather.3.cloned.1.call-start = ((), (), s32[]{:S(2)}) async-start(), calls=%async_computation.4 | async-start | bytes 1114112 | tf_op jit(solution)/shard_map/all_gather | solution.py:327
  7.3 13.1 %collective-permute-start = (bf16[32,512]{1,0:T(8,128)(2,1)S(1)}, bf16[32,512]{1,0:T(8,128)(2,1)S(1)}, u32[]{:S(2)}, u32[]{:S(2)}) collective-permute-start(bf16[32,512]{1,0:T(8,128)(2,1)S(1)} %get-tuple-element.51), channel_id=1, source_target_pairs={{0,0},{4,4},{1,128},{5,132},{2,256},{6,260},{3,384},{7,388},{128,1... | collective-permute-start | bytes 98312 | tf_op jit(solution)/shard_map/ppermute | solution.py:311
  8.0 12.5 %collective-permute-start.1 = (bf16[32,512]{1,0:T(8,128)(2,1)S(1)}, bf16[32,512]{1,0:T(8,128)(2,1)S(1)}, u32[]{:S(2)}, u32[]{:S(2)}) collective-permute-start(bf16[32,512]{1,0:T(8,128)(2,1)S(1)} %get-tuple-element.52), channel_id=1, source_target_pairs={{0,4},{4,0},{1,132},{5,128},{2,260},{6,256},{3,388},{7,384},{128,5... | collective-permute-start | bytes 98312 | tf_op jit(solution)/shard_map/ppermute | solution.py:311
  21.1 4.1 %collective-permute-start.2 = (bf16[560,512]{1,0:T(8,128)(2,1)}, bf16[560,512]{1,0:T(8,128)(2,1)S(1)}, u32[]{:S(2)}, u32[]{:S(2)}) collective-permute-start(bf16[560,512]{1,0:T(8,128)(2,1)} %get-tuple-element.30), channel_id=1, source_target_pairs={{0,4},{4,0},{1,5},{5,1},{2,6},{6,2},{3,7},{7,3},{8,12},{12,8},{9,1... | collective-permute-start | bytes 1720328 | tf_op jit(solution)/shard_map/ppermute | solution.py:21
  28.0 8.4 %copy-start.12 = (bf16[4,128,128]{2,1,0:T(8,128)(2,1)}, bf16[4,128,128]{2,1,0:T(8,128)(2,1)S(1)}, u32[]{:S(2)}) copy-start(bf16[4,128,128]{2,1,0:T(8,128)(2,1)S(1)} %get-tuple-element.35.refs_5_) | copy-start | bytes 393220
  38.3 29.3 %all-to-all-start.1 = ((bf16[4,144,128]{2,1,0:T(8,128)(2,1)}), bf16[4,144,128]{2,1,0:T(8,128)(2,1)S(1)}, u32[]{:S(2)}, u32[]{:S(2)}) async-start(bf16[4,144,128]{2,1,0:T(8,128)(2,1)} %get-tuple-element.45), calls=%async_computation.1 | async-start | bytes 294912 | tf_op jit(solution)/shard_map/all_to_all | solution.py:344
  48.1 19.6 %copy-start.17 = (s32[5]{0:T(128)S(1)}, s32[5]{0:T(128)}, u32[]{:S(2)}) copy-start(s32[5]{0:T(128)} %stack.23.refs_0_) | copy-start | bytes 64
  48.1 32.5 %copy-start.3 = (bf16[560,512]{1,0:T(8,128)(2,1)S(1)}, bf16[560,512]{1,0:T(8,128)(2,1)}, u32[]{:S(2)}) copy-start(bf16[560,512]{1,0:T(8,128)(2,1)} %get-tuple-element.28.refs_1_) | copy-start | bytes 1720324
  51.1 29.5 %copy-start = (bf16[512,512]{1,0:T(8,128)(2,1)S(1)}, bf16[512,512]{1,0:T(8,128)(2,1)}, u32[]{:S(2)}) copy-start(bf16[512,512]{1,0:T(8,128)(2,1)} %get-tuple-element.33.refs_3_.refs_1_) | copy-start | bytes 1572868
  51.1 29.5 %collective-permute-start.3 = (bf16[512,512]{1,0:T(8,128)(2,1)}, bf16[512,512]{1,0:T(8,128)(2,1)S(1)}, u32[]{:S(2)}, u32[]{:S(2)}) collective-permute-start(bf16[512,512]{1,0:T(8,128)(2,1)} %get-tuple-element.34), channel_id=1, source_target_pairs={{0,4},{4,0},{1,5},{5,1},{2,6},{6,2},{3,7},{7,3},{8,12},{12,8},{9,1... | collective-permute-start | bytes 1572872 | tf_op jit(solution)/shard_map/ppermute | solution.py:21
  54.8 9.3 %collective-permute-start.4 = (bf16[144,256]{1,0:T(8,128)(2,1)S(1)}, bf16[144,256]{1,0:T(8,128)(2,1)S(1)}, u32[]{:S(2)}, u32[]{:S(2)}) collective-permute-start(bf16[144,256]{1,0:T(8,128)(2,1)S(1)} %get-tuple-element.40), channel_id=1, source_target_pairs={{0,8},{8,0},{16,24},{24,16},{1,9},{9,1},{17,25},{25,17},{2,10},{10... | collective-permute-start | bytes 221192 | tf_op jit(solution)/shard_map/ppermute | solution.py:346
  57.1 7.1 %collective-permute-start.5 = (bf16[144,256]{1,0:T(8,128)(2,1)S(1)}, bf16[144,256]{1,0:T(8,128)(2,1)S(1)}, u32[]{:S(2)}, u32[]{:S(2)}) collective-permute-start(bf16[144,256]{1,0:T(8,128)(2,1)S(1)} %get-tuple-element.41), channel_id=1, source_target_pairs={{0,16},{8,24},{16,0},{24,8},{1,17},{9,25},{17,1},{25,9},{2,18},{10... | collective-permute-start | bytes 221192 | tf_op jit(solution)/shard_map/ppermute | solution.py:346
  60.1 7.6 %collective-permute-start.6 = (bf16[144,256]{1,0:T(8,128)(2,1)S(1)}, bf16[144,256]{1,0:T(8,128)(2,1)S(1)}, u32[]{:S(2)}, u32[]{:S(2)}) collective-permute-start(bf16[144,256]{1,0:T(8,128)(2,1)S(1)} %get-tuple-element.42), channel_id=1, source_target_pairs={{0,24},{8,16},{16,8},{24,0},{1,25},{9,17},{17,9},{25,1},{2,26},{10... | collective-permute-start | bytes 221192 | tf_op jit(solution)/shard_map/ppermute | solution.py:346
  69.6 17.0 %all-to-all-start.2 = ((bf16[4,144,128]{2,1,0:T(8,128)(2,1)}), bf16[4,144,128]{2,1,0:T(8,128)(2,1)S(1)}, u32[]{:S(2)}, u32[]{:S(2)}) async-start(bf16[4,144,128]{2,1,0:T(8,128)(2,1)} %get-tuple-element.46), calls=%async_computation.2 | async-start | bytes 294912 | tf_op jit(solution)/shard_map/all_to_all | solution.py:357
  88.8 19.6 %all-to-all-start.3 = ((bf16[4,128,512]{2,1,0:T(8,128)(2,1)}), bf16[4,128,512]{2,1,0:T(8,128)(2,1)}, u32[]{:S(2)}, u32[]{:S(2)}) async-start(bf16[4,128,512]{2,1,0:T(8,128)(2,1)} %shard_map.89), calls=%async_computation.3 | async-start | bytes 1048576 | tf_op jit(solution)/shard_map/all_to_all | solution.py:361
  96.9 11.5 %copy-start.20 = (bf16[1024]{0:T(1024)(128)(2,1)S(1)}, bf16[1024]{0:T(1024)(128)(2,1)}, u32[]{:S(2)}) copy-start(bf16[1024]{0:T(1024)(128)(2,1)} %param.14) | copy-start | bytes 6148
  96.9 23.5 %collective-permute-start.12 = (bf16[16,64,512]{2,1,0:T(8,128)(2,1)}, bf16[16,64,512]{2,1,0:T(8,128)(2,1)S(1)}, u32[]{:S(2)}, u32[]{:S(2)}) collective-permute-start(bf16[16,64,512]{2,1,0:T(8,128)(2,1)} %bitcast.6), channel_id=1, source_target_pairs={{0,256},{128,384},{256,0},{384,128},{1,257},{129,385},{257,1},{385... | collective-permute-start | bytes 3145736 | tf_op jit(solution)/shard_map/ppermute | solution.py:296
  101.9 46.3 %collective-permute-start.11 = (bf16[16,64,512]{2,1,0:T(8,128)(2,1)}, bf16[16,64,512]{2,1,0:T(8,128)(2,1)S(1)}, u32[]{:S(2)}, u32[]{:S(2)}) collective-permute-start(bf16[16,64,512]{2,1,0:T(8,128)(2,1)} %bitcast.7), channel_id=1, source_target_pairs={{0,128},{128,256},{256,384},{384,0},{1,129},{129,257},{257,385},{3... | collective-permute-start | bytes 3145736 | tf_op jit(solution)/shard_map/ppermute | solution.py:296
  104.1 44.1 %collective-permute-start.10 = (bf16[16,64,512]{2,1,0:T(8,128)(2,1)}, bf16[16,64,512]{2,1,0:T(8,128)(2,1)}, u32[]{:S(2)}, u32[]{:S(2)}) collective-permute-start(bf16[16,64,512]{2,1,0:T(8,128)(2,1)} %bitcast.8), channel_id=1, source_target_pairs={{0,384},{128,0},{256,128},{384,256},{1,385},{129,1},{257,129},{385... | collective-permute-start | bytes 3145736 | tf_op jit(solution)/shard_map/ppermute | solution.py:296
  110.6 37.6 %copy-start.1 = (bf16[1024,512]{1,0:T(8,128)(2,1)S(1)}, bf16[1024,512]{1,0:T(8,128)(2,1)}, u32[]{:S(2)}) copy-start(bf16[1024,512]{1,0:T(8,128)(2,1)} %all-gather.3.cloned.1.call-done) | copy-start | bytes 3145732
  113.8 34.4 %collective-permute-start.9 = (bf16[512,512]{1,0:T(8,128)(2,1)S(1)}, bf16[512,512]{1,0:T(8,128)(2,1)S(1)}, u32[]{:S(2)}, u32[]{:S(2)}) collective-permute-start(bf16[512,512]{1,0:T(8,128)(2,1)S(1)} %shard_map.90.refs_1_), channel_id=1, source_target_pairs={{0,3},{1,0},{2,1},{3,2},{4,7},{5,4},{6,5},{7,6},{8,11},{9,8},{10,9... | collective-permute-start | bytes 1572872 | tf_op jit(solution)/shard_map/ppermute | solution.py:296
  117.2 31.0 %collective-permute-start.8 = (bf16[512,512]{1,0:T(8,128)(2,1)S(1)}, bf16[512,512]{1,0:T(8,128)(2,1)S(1)}, u32[]{:S(2)}, u32[]{:S(2)}) collective-permute-start(bf16[512,512]{1,0:T(8,128)(2,1)S(1)} %shard_map.90.refs_1_), channel_id=1, source_target_pairs={{0,2},{1,3},{2,0},{3,1},{4,6},{5,7},{6,4},{7,5},{8,10},{9,11},{10,... | collective-permute-start | bytes 1572872 | tf_op jit(solution)/shard_map/ppermute | solution.py:296
  120.5 27.8 %collective-permute-start.7 = (bf16[512,512]{1,0:T(8,128)(2,1)S(1)}, bf16[512,512]{1,0:T(8,128)(2,1)S(1)}, u32[]{:S(2)}, u32[]{:S(2)}) collective-permute-start(bf16[512,512]{1,0:T(8,128)(2,1)S(1)} %shard_map.90.refs_1_), channel_id=1, source_target_pairs={{0,1},{1,2},{2,3},{3,0},{4,5},{5,6},{6,7},{7,4},{8,9},{9,10},{10,1... | collective-permute-start | bytes 1572872 | tf_op jit(solution)/shard_map/ppermute | solution.py:296
  151.6 6.1 %collective-permute-start.13 = (bf16[256,1024]{1,0:T(8,128)(2,1)S(1)}, bf16[256,1024]{1,0:T(8,128)(2,1)S(1)}, u32[]{:S(2)}, u32[]{:S(2)}) collective-permute-start(bf16[256,1024]{1,0:T(8,128)(2,1)S(1)} %shard_map.92), channel_id=1, source_target_pairs={{0,4},{4,0},{1,5},{5,1},{2,6},{6,2},{3,7},{7,3},{8,12},{12,8},{9,1... | collective-permute-start | bytes 1572872 | tf_op jit(solution)/shard_map/ppermute | solution.py:21
  (15 other events, 26.2 us)
Sparse Core Ops, SparseCore 0:
  23.2 71.3 all-gather.2
